TPU v7x, 32 devices: a whole 2x2x4 slice. The times are simulated.
32 devices in a mesh: blk: 8 (over y, x, core), sub: 4 (over z).
Axes of the slice: x: 2, y: 2, z: 4, core: 2. Of those that a mesh axis runs over, the one named last changes fastest.
Arguments:
- left_emb: float32 [2, 200, 16384], P(None, None, ('blk', 'sub')), may hold values from -1.8 to 1.8
- left_state: float32 [16384], P(('blk', 'sub')), may hold values from 0.003 to 0.1
- right_emb: float32 [2, 200, 16384], P(None, None, ('blk', 'sub')), may hold values from -1.8 to 1.8
- right_state: float32 [16384], P(('blk', 'sub')), may hold values from 0.003 to 0.1
- relation_emb: float32 [2, 200, 1280], replicated, may hold values from -4.2 to 4.2
- relation_state: float32 [1280], replicated, may hold values from 0.003 to 0.1
- hub_emb: float32 [2, 200, 4096], replicated, may hold values from -1.8 to 1.8
- hub_state: float32 [4096], replicated, may hold values from 0.003 to 0.1
- heads: int32 [2, 16384], P(None, ('blk', 'sub')), may hold values from 0 to 511
- relations: int32 [2, 16384], P(None, ('blk', 'sub')), may hold values from 0 to 1279
- tails: int32 [2, 16384], P(None, ('blk', 'sub')), may hold values from 0 to 511
- negatives: int32 [2, 32768], P(None, ('blk', 'sub')), may hold values from 0 to 511
- hub_ids: int32 [2, 8192], P(None, ('blk', 'sub')), may hold values from 0 to 4095
Outputs:
- left_out: float32 [2, 200, 16384], P(None, None, ('blk', 'sub'))
- right_out: float32 [2, 200, 16384], P(None, None, ('blk', 'sub'))
- relation_out: float32 [2, 200, 1280], replicated
- hub_out: float32 [2, 200, 4096], replicated
Inputs may be any that keep to these rules, and one draw needn't show every extreme that they name: `heads`: local row indices of the head-side block. `relations`: relation types. `tails`: local row indices of the tail-side block held in that bucket. `negatives`: local row indices of the tail-side block held in that bucket; indices may repeat. `hub_ids`: hub rows; indices may repeat.
All inputs are finite; a program needn't handle non-finite values.
Results may differ from a plain program's by a relative error of at most 0.0001.
Values sent between devices are 32-bit elements; how exact they have to be, the bound alone decides.
No kernel may reach another device: no remote copies, remote signals or barrier semaphores. Data moves between devices by JAX's collectives and lax.ppermute only.
A program may use at most 128 MiB of HBM per device.

v0:
```python
import functools
import jax
import jax.numpy as jnp
from jax import lax
from jax.experimental import pallas as pl
from jax.experimental.pallas import tpu as pltpu
from jax.sharding import PartitionSpec as P

step_rate = 0.25
F32, BF16 = jnp.float32, jnp.bfloat16
NN = (((1,), (0,)), ((), ()))
NT = (((1,), (1,)), ((), ()))
TN = (((0,), (0,)), ((), ()))
VMEM = pl.BlockSpec(memory_space=pltpu.VMEM)
PARAMS = pltpu.CompilerParams(vmem_limit_bytes=48 * 1024 * 1024)


def split(x):
    hi = x.astype(BF16)
    return hi, (x - hi.astype(F32)).astype(BF16)


def dot(a, b, dims):
    return lax.dot_general(a, b, dims, preferred_element_type=F32)


def dot3(a, b, dims):
    return dot(a[0], b[0], dims) + (dot(a[0], b[1], dims) + dot(a[1], b[0], dims))


def dot2(a, onehot, dims):
    return dot(a[0], onehot, dims) + dot(a[1], onehot, dims)


def onehot(first, rows, idx):
    place = lax.broadcasted_iota(jnp.int32, (rows, idx.shape[1]), 0) + first
    return jnp.where(place == idx, 1.0, 0.0).astype(BF16)


def gather_kernel(tile, idx_ref, table_ref, out_ref):
    step = pl.program_id(0)
    part = dot2(split(table_ref[...]), onehot(step * tile, tile, idx_ref[...]), NN)

    @pl.when(step == 0)
    def _():
        out_ref[...] = part

    @pl.when(step > 0)
    def _():
        out_ref[...] += part


def gather_columns(table, idx, steps):
    features, rows = table.shape
    count = idx.shape[1]
    tile = rows // steps
    return pl.pallas_call(
        functools.partial(gather_kernel, tile),
        grid=(steps,),
        in_specs=[
            pl.BlockSpec((1, count), lambda k: (0, 0)),
            pl.BlockSpec((features, tile), lambda k: (0, k)),
        ],
        out_specs=pl.BlockSpec((features, count), lambda k: (0, 0)),
        out_shape=jax.ShapeDtypeStruct((features, count), F32),
        compiler_params=PARAMS,
        cost_estimate=pl.CostEstimate(
            flops=4 * features * rows * count, bytes_accessed=4 * features * rows, transcendentals=0
        ),
    )(idx, table)


def scatter_kernel(tile, idx_ref, grads_ref, out_ref):
    step = pl.program_id(0)
    out_ref[...] = dot2(split(grads_ref[...]), onehot(step * tile, tile, idx_ref[...]), NT)


def scatter_columns(grads, idx, rows, steps):
    features, count = grads.shape
    tile = rows // steps
    return pl.pallas_call(
        functools.partial(scatter_kernel, tile),
        grid=(steps,),
        in_specs=[
            pl.BlockSpec((1, count), lambda k: (0, 0)),
            pl.BlockSpec((features, count), lambda k: (0, 0)),
        ],
        out_specs=pl.BlockSpec((features, tile), lambda k: (0, k)),
        out_shape=jax.ShapeDtypeStruct((features, rows), F32),
        compiler_params=PARAMS,
        cost_estimate=pl.CostEstimate(
            flops=4 * features * rows * count, bytes_accessed=4 * features * rows, transcendentals=0
        ),
    )(idx, grads)


def adagrad(table, state, grads):
    new_state = state + jnp.sum(grads * grads, axis=0, keepdims=True) * (1.0 / grads.shape[0])
    return table - grads * (step_rate / jnp.sqrt(new_state)), new_state


def bucket_kernel(
    heads_ref, tails_ref, negs_ref, left_ref, left_sums_ref, right_ref, right_sums_ref, rel_ref, hub_ref,
    left_out, left_sums_out, right_out, right_sums_out, rel_out, hub_out,
    left_hi, left_lo, both_hi, both_lo, left_grad, both_grad,
):
    features, rows = left_ref.shape
    half = features // 2
    edges = heads_ref.shape[1]
    hubs = hub_ref.shape[1]
    weight = 1.0 / (negs_ref.shape[1] + hubs)
    place = lax.broadcasted_iota(jnp.int32, (rows, negs_ref.shape[1]), 0)
    counts = jnp.sum(jnp.where(place == negs_ref[...], weight, 0.0), axis=1, keepdims=True)
    left_hi[...], left_lo[...] = split(left_ref[...])
    both_hi[:, :rows], both_lo[:, :rows] = split(right_ref[...])
    both_hi[:, rows:], both_lo[:, rows:] = split(hub_ref[...])
    left_grad[...] = jnp.zeros_like(left_grad)
    both_grad[...] = jnp.zeros_like(both_grad)
    tile = 256

    @pl.loop(0, edges // tile)
    def _(step):
        span = pl.ds(pl.multiple_of(step * tile, tile), tile)
        head_hot = onehot(0, rows, heads_ref[:, span])
        tail_here = lax.broadcasted_iota(jnp.int32, (rows, tile), 0) == tails_ref[:, span]
        h = dot2((left_hi[...], left_lo[...]), head_hot, NN)
        h0, h1 = h[:half], h[half:]
        r0, r1 = rel_ref[:half, span], rel_ref[half:, span]
        q = split(jnp.concatenate([h0 * r0 - h1 * r1, h0 * r1 + h1 * r0], axis=0))
        both = (both_hi[...], both_lo[...])
        scores = dot3(both, q, TN)
        chance = jax.nn.sigmoid(scores[:rows])
        coef = jnp.concatenate(
            [
                counts * chance + jnp.where(tail_here, chance - 1.0, 0.0),
                weight * jax.nn.sigmoid(scores[rows:]),
            ],
            axis=0,
        )
        coef = split(coef)
        dq = dot3(both, coef, NN)
        both_grad[...] += dot3(q, coef, NT)
        d0, d1 = dq[:half], dq[half:]
        dh = jnp.concatenate([d0 * r0 + d1 * r1, d1 * r0 - d0 * r1], axis=0)
        left_grad[...] += dot2(split(dh), head_hot, NT)
        rel_out[:half, span] = d0 * h0 + d1 * h1
        rel_out[half:, span] = d1 * h0 - d0 * h1

    left_out[...], left_sums_out[...] = adagrad(left_ref[...], left_sums_ref[...], left_grad[...])
    right_out[...], right_sums_out[...] = adagrad(right_ref[...], right_sums_ref[...], both_grad[:, :rows])
    hub_out[...] = both_grad[:, rows:]


def bucket_step(heads, tails, negs, left, left_sums, right, right_sums, rel_rows, hub_rows):
    features, rows = left.shape
    edges, hubs = heads.shape[1], hub_rows.shape[1]
    width = rows + hubs
    like = lambda x: jax.ShapeDtypeStruct(x.shape, x.dtype)
    return pl.pallas_call(
        bucket_kernel,
        in_specs=[VMEM] * 9,
        out_specs=[VMEM] * 6,
        out_shape=[like(left), like(left_sums), like(right), like(right_sums), like(rel_rows), like(hub_rows)],
        scratch_shapes=[
            pltpu.VMEM((features, rows), BF16),
            pltpu.VMEM((features, rows), BF16),
            pltpu.VMEM((features, width), BF16),
            pltpu.VMEM((features, width), BF16),
            pltpu.VMEM((features, rows), F32),
            pltpu.VMEM((features, width), F32),
        ],
        compiler_params=PARAMS,
        cost_estimate=pl.CostEstimate(
            flops=18 * features * edges * width, bytes_accessed=24 * features * rows, transcendentals=edges * width
        ),
    )(heads, tails, negs, left, left_sums, right, right_sums, rel_rows, hub_rows)


def from_behind(x, axis, by):
    size = lax.axis_size(axis)
    return lax.ppermute(x, axis, [(i, (i + by) % size) for i in range(size)])


def shards(
    left_emb, left_state, right_emb, right_state, relation_emb, relation_state, hub_emb, hub_state,
    heads, relations, tails, negatives, hub_ids,
):
    components, half_width, row_count = left_emb.shape
    features = components * half_width
    left = left_emb.reshape(features, row_count)
    right = right_emb.reshape(features, row_count)
    rel_table = relation_emb.reshape(features, relation_emb.shape[2])
    hub_table = hub_emb.reshape(features, hub_emb.shape[2])
    left_sums = left_state.reshape(1, row_count)
    right_sums = right_state.reshape(1, row_count)
    buckets, edges = heads.shape
    hubs = hub_ids.shape[1]
    all_rel = relations.reshape(1, buckets * edges)
    all_hub = hub_ids.reshape(1, buckets * hubs)
    rel_rows = gather_columns(rel_table, all_rel, 1)
    hub_rows = gather_columns(hub_table, all_hub, 4)
    rel_parts, hub_parts = [], []
    for b in range(buckets):
        left, left_sums, right, right_sums, rel_part, hub_part = bucket_step(
            heads[b : b + 1], tails[b : b + 1], negatives[b : b + 1],
            left, left_sums, right, right_sums,
            rel_rows[:, b * edges : (b + 1) * edges], hub_rows[:, b * hubs : (b + 1) * hubs],
        )
        rel_parts.append(rel_part)
        hub_parts.append(hub_part)
        if b < buckets - 1:
            right, right_sums = from_behind((right, right_sums), "blk", 1)
    rel_total = scatter_columns(jnp.concatenate(rel_parts, axis=1), all_rel, rel_table.shape[1], 1)
    hub_total = scatter_columns(jnp.concatenate(hub_parts, axis=1), all_hub, hub_table.shape[1], 4)
    rel_total, hub_total = lax.psum((rel_total, hub_total), ("blk", "sub"))
    rel_new, unused_rel = adagrad(rel_table, relation_state[None], rel_total)
    hub_new, unused_hub = adagrad(hub_table, hub_state[None], hub_total)
    return (
        left.reshape(components, half_width, row_count),
        right.reshape(components, half_width, row_count),
        rel_new.reshape(relation_emb.shape),
        hub_new.reshape(hub_emb.shape),
    )


def solution(mesh):
    both = ("blk", "sub")
    block, table, whole = P(None, None, both), P(None, both), P()
    return jax.shard_map(
        shards,
        mesh=mesh,
        in_specs=(block, P(both), block, P(both), whole, whole, whole, whole, table, table, table, table, table),
        out_specs=(block, block, whole, whole),
        check_vma=False,
    )
```

profile of v0, /device:TPU:0, one launch (start us, length us, event | category | flops | bytes accessed | tf_op | source)
XLA Modules:
  0.0 264.4 jit_solution(1472792341920979603)
XLA Ops:
  7.2 0.0 all-reduce.3.cloned.1.call-start
  7.2 0.7 copy.18
  7.9 0.7 copy.17
  8.6 0.8 fusion.2
  9.4 0.0 copy-start
  9.4 6.5 %shard_map.157 = f32[400,512]{1,0:T(8,128)S(1)} custom-call(s32[1,512]{1,0:T(1,128)S(1)} %bitcast.21, f32[400,4096]{1,0:T(8,128)} %bitcast.27), custom_call_target="tpu_custom_call" | custom-call | flops 3355443200 | bytes 6553600 | tf_op jit(solution)/shard_map/pallas_call | solution.py:57
  15.9 0.1 fusion.1
  16.0 2.7 %shard_map.156 = f32[400,1024]{1,0:T(8,128)S(1)} custom-call(s32[1,1024]{1,0:T(1,128)S(1)} %bitcast.19, f32[400,1280]{1,0:T(8,128)S(1)} %bitcast.18), custom_call_target="tpu_custom_call" | custom-call | flops 2097152000 | bytes 2048000 | tf_op jit(solution)/shard_map/pallas_call | solution.py:57
  18.6 0.0 copy-start.10
  18.7 0.0 copy-start.2
  18.7 0.1 fusion
  18.8 0.5 copy-done.9
  19.3 0.0 copy-done.10
  19.4 0.5 copy-done.2
  19.8 0.2 copy-done.3
  20.1 8.4 %shard_map.158 = (f32[400,512]{1,0:T(8,128)S(1)}, f32[1,512]{1,0:T(1,128)S(1)}, f32[400,512]{1,0:T(8,128)S(1)}, f32[1,512]{1,0:T(1,128)S(1)}, f32[400,512]{1,0:T(8,128)S(1)}, /*index=5*/f32[400,256]{1,0:T(8,128)S(1)}) custom-call(s32[1,512]{1,0:T(1,128)S(1)} %get-tuple-element.37.heads_ref, s32[1,512]{1,0:T(1,128)S(1)} %get-tuple-element.32.tails_ref, ...), custom_call_target="tpu_custom_call" | custom-call | flops 2831155200 | bytes 4915200 | tf_op jit(solution)/shard_map/pallas_call | solution.py:159
  28.4 0.5 collective-permute-start
  28.9 2.6 collective-permute-start.1
  31.5 10.3 %collective-permute-done.1.right_sums_ref = f32[1,512]{1,0:T(1,128)S(1)} collective-permute-done((f32[1,512]{1,0:T(1,128)S(1)}, f32[1,512]{1,0:T(1,128)S(1)}, u32[]{:S(2)}, u32[]{:S(2)}) %collective-permute-start.1) | collective-permute-done | bytes 2080 | tf_op jit(solution)/shard_map/ppermute | solution.py:181
  41.9 9.4 %shard_map.159 = (f32[400,512]{1,0:T(8,128)}, f32[1,512]{1,0:T(1,128)}, f32[400,512]{1,0:T(8,128)}, f32[1,512]{1,0:T(1,128)}, f32[400,512]{1,0:T(8,128)S(1)}, /*index=5*/f32[400,256]{1,0:T(8,128)S(1)}) custom-call(s32[1,512]{1,0:T(1,128)S(1)} %get-tuple-element.36.heads_ref, s32[1,512]{1,0:T(1,128)S(1)} %get-tuple-element.33.tails_ref, ...), custom_call_target="tpu_custom_call" | custom-call | flops 2831155200 | bytes 4915200 | tf_op jit(solution)/shard_map/pallas_call | solution.py:159
  51.3 0.1 pad_maximum_fusion.grads_ref
  51.4 2.4 shard_map.160
  53.8 1.3 copy-done.1
  55.1 0.1 pad_maximum_fusion.1.grads_ref
  55.2 5.5 %shard_map.161 = f32[400,4096]{1,0:T(8,128)} custom-call(s32[1,512]{1,0:T(1,128)S(1)} %bitcast.22, f32[400,512]{1,0:T(8,128)S(1)} %pad_maximum_fusion.1.grads_ref), custom_call_target="tpu_custom_call" | custom-call | flops 3355443200 | bytes 6553600 | tf_op jit(solution)/shard_map/pallas_call | solution.py:81
  60.8 0.0 all-reduce.3.cloned.1.call-update
  60.8 183.6 %all-reduce.3.cloned.1.call-done = (f32[400,1280]{1,0:T(8,128)}, f32[400,4096]{1,0:T(8,128)}) async-done(((f32[400,1280]{1,0:T(8,128)}, f32[400,4096]{1,0:T(8,128)}), (f32[400,1280]{1,0:T(8,128)}, f32[400,4096]{1,0:T(8,128)})) %all-reduce.3.cloned.1.call-update) | async-done | bytes 8601616 | tf_op jit(solution)/shard_map/psum | solution.py:215
  244.4 1.9 multiply_reduce_fusion.1
  246.3 3.4 %multiply_subtract_fusion.1 = f32[400,1280]{1,0:T(8,128)} fusion(f32[400,1280]{1,0:T(8,128)} %get-tuple-element.24, f32[1280]{0:T(1024)S(1)} %rsqrt_multiply_fusion.1, f32[2,200,1280]{2,1,0:T(8,128)S(1)} %copy-done), kind=kLoop, calls=%fused_computation.2 | loop fusion | flops 1024000 | bytes 6149120 | tf_op jit(solution)/shard_map/sub | solution.py:99
  249.7 0.7 multiply_reduce_fusion
  250.4 0.0 copy-done.7
  250.5 7.0 %multiply_subtract_fusion = f32[400,4096]{1,0:T(8,128)} fusion(f32[400,4096]{1,0:T(8,128)S(1)} %copy-done.6, f32[4096]{0:T(1024)S(1)} %rsqrt_multiply_fusion, f32[2,200,4096]{2,1,0:T(8,128)} %param.19), kind=kLoop, calls=%fused_computation | loop fusion | flops 3276800 | bytes 19677184 | tf_op jit(solution)/shard_map/sub | solution.py:99
  (17 shorter events, 0.1 us)
Async XLA Ops:
  7.2 237.2 %all-reduce.3.cloned.1.call-start = ((), (), s32[]{:S(2)}) async-start(), calls=%async_computation | async-start | bytes 17203200 | tf_op jit(solution)/shard_map/psum | solution.py:215
  9.4 6.6 %copy-start = (f32[2,200,1280]{2,1,0:T(8,128)S(1)}, f32[2,200,1280]{2,1,0:T(8,128)}, u32[]{:S(2)}) copy-start(f32[2,200,1280]{2,1,0:T(8,128)} %param.17) | copy-start | bytes 6144004
  18.6 0.7 copy-start.9
  18.6 0.7 copy-start.10
  18.7 1.2 copy-start.2
  18.7 1.4 copy-start.3
  18.7 1.4 copy-start.4
  18.7 1.4 copy-start.5
  28.4 13.4 %collective-permute-start = (f32[400,512]{1,0:T(8,128)S(1)}, f32[400,512]{1,0:T(8,128)S(1)}, u32[]{:S(2)}, u32[]{:S(2)}) collective-permute-start(f32[400,512]{1,0:T(8,128)S(1)} %get-tuple-element.16), channel_id=1, source_target_pairs={{0,4},{4,8},{8,12},{12,16},{16,20},{20,24},{24,28},{28,0},{1,5},{5... | collective-permute-start | bytes 2457608 | tf_op jit(solution)/shard_map/ppermute | solution.py:181
  28.9 12.9 %collective-permute-start.1 = (f32[1,512]{1,0:T(1,128)S(1)}, f32[1,512]{1,0:T(1,128)S(1)}, u32[]{:S(2)}, u32[]{:S(2)}) collective-permute-start(f32[1,512]{1,0:T(1,128)S(1)} %get-tuple-element.17), channel_id=1, source_target_pairs={{0,4},{4,8},{8,12},{12,16},{16,20},{20,24},{24,28},{28,0},{1,5},{5... | collective-permute-start | bytes 6152 | tf_op jit(solution)/shard_map/ppermute | solution.py:181
  53.8 1.3 copy-start.1
  60.8 185.5 %copy-start.8 = (f32[1280]{0:T(1024)S(1)}, f32[1280]{0:T(1024)}, u32[]{:S(2)}) copy-start(f32[1280]{0:T(1024)} %param.18) | copy-start | bytes 15364
  244.4 5.3 %copy-start.6 = (f32[400,4096]{1,0:T(8,128)S(1)}, f32[400,4096]{1,0:T(8,128)}, u32[]{:S(2)}) copy-start(f32[400,4096]{1,0:T(8,128)} %get-tuple-element.25) | copy-start | bytes 19660804
  249.7 0.7 copy-start.7
Sparse Core Ops, SparseCore 0:
  60.9 183.4 all-reduce.2
where the time goes:
time: 265 us; the launch traced here: 264 us
  waiting for transfers between devices  194 us (73%)
  Pallas kernels  34.9 us (13%)
  between operations  14.2 us (5%)
  other arithmetic  13.3 us (5%)
  local copies, waits for them, and re-layouts  4.93 us (2%)
  starting transfers between devices  3.14 us (1%)
    psum x1, waiting for transfers between devices, shards(): rel_total, hub_total = lax.psum((rel_total, hub_total), ('blk', 'sub'))  184 us
    pallas_call x2, Pallas kernels, bucket_step(): pl.pallas_call(bucket_kernel, in_specs=[VMEM] * 9, out_specs=[VMEM] * 6,...  17.8 us
    sub x2, other arithmetic, adagrad(): return (table - grads * (step_rate / jnp.sqrt(new_state)), new_state)  10.5 us
    ppermute x2, waiting for transfers between devices, from_behind(): return lax.ppermute(x, axis, [(i, (i + by) % size) for i in range(size)])  10.3 us
    pallas_call x2, Pallas kernels, gather_columns(): pl.pallas_call(functools.partial(gather_kernel, tile), grid=(steps,), in_...  9.16 us
    pallas_call x2, Pallas kernels, scatter_columns(): pl.pallas_call(functools.partial(scatter_kernel, tile), grid=(steps,), in...  7.94 us
  transfers between devices with their start and end apart: 3, of which 2 were waited for; matrix products, arithmetic and copies ran while one was open for 0% of the time, Pallas kernels for 0%

commit v1 on v0

v1 whole, which is shorter than its diff:
```python
import functools
import jax
import jax.numpy as jnp
from jax import lax
from jax.experimental import pallas as pl
from jax.experimental.pallas import tpu as pltpu
from jax.sharding import PartitionSpec as P

step_rate = 0.25
F32, BF16 = jnp.float32, jnp.bfloat16
NN = (((1,), (0,)), ((), ()))
NT = (((1,), (1,)), ((), ()))
TN = (((0,), (0,)), ((), ()))
VMEM = pl.BlockSpec(memory_space=pltpu.VMEM)
PARAMS = pltpu.CompilerParams(vmem_limit_bytes=48 * 1024 * 1024)


def split(x):
    hi = x.astype(BF16)
    return hi, (x - hi.astype(F32)).astype(BF16)


def dot(a, b, dims):
    return lax.dot_general(a, b, dims, preferred_element_type=F32)


def dot3(a, b, dims):
    return dot(a[0], b[0], dims) + (dot(a[0], b[1], dims) + dot(a[1], b[0], dims))


def dot2(a, onehot, dims):
    return dot(a[0], onehot, dims) + dot(a[1], onehot, dims)


def onehot(first, rows, idx):
    place = lax.broadcasted_iota(jnp.int32, (rows, idx.shape[1]), 0) + first
    return jnp.where(place == idx, 1.0, 0.0).astype(BF16)


def gather_kernel(tile, idx_ref, table_ref, out_ref):
    step = pl.program_id(0)
    part = dot2(split(table_ref[...]), onehot(step * tile, tile, idx_ref[...]), NN)

    @pl.when(step == 0)
    def _():
        out_ref[...] = part

    @pl.when(step > 0)
    def _():
        out_ref[...] += part


def gather_columns(table, idx, steps):
    features, rows = table.shape
    count = idx.shape[1]
    tile = rows // steps
    return pl.pallas_call(
        functools.partial(gather_kernel, tile),
        grid=(steps,),
        in_specs=[
            pl.BlockSpec((1, count), lambda k: (0, 0)),
            pl.BlockSpec((features, tile), lambda k: (0, k)),
        ],
        out_specs=pl.BlockSpec((features, count), lambda k: (0, 0)),
        out_shape=jax.ShapeDtypeStruct((features, count), F32),
        compiler_params=PARAMS,
        cost_estimate=pl.CostEstimate(
            flops=4 * features * rows * count, bytes_accessed=4 * features * rows, transcendentals=0
        ),
    )(idx, table)


def spread_bits(place, order):
    bits = len(order)
    return sum((((place >> p) & 1) << (bits - 1 - i)) for i, p in enumerate(order))


def put_chunk(index, value, send_ref, keep_ref):
    half = keep_ref.shape[0]
    spot = index & (half - 1)

    @pl.when(index >= half)
    def _():
        send_ref[spot] = value

    @pl.when(index < half)
    def _():
        keep_ref[spot] = value


def load_columns(idx_refs, grad_refs, idx_all, hi_all, lo_all):
    at = 0
    for ref in idx_refs:
        idx_all[:, at : at + ref.shape[1]] = ref[...]
        at += ref.shape[1]
    at = 0
    for ref in grad_refs:
        width = ref.shape[1]
        hi_all[:, at : at + width], lo_all[:, at : at + width] = split(ref[...])
        at += width


def hub_chunks_kernel(orders, spans, grads, chip_ref, *refs):
    idx_refs, grad_refs, refs = refs[:2], refs[2 : 2 + grads], refs[2 + grads :]
    streams = len(orders)
    sends, keeps = refs[:streams], refs[streams : 2 * streams]
    idx_all, hi_all, lo_all = refs[2 * streams :]
    load_columns(idx_refs, grad_refs, idx_all, hi_all, lo_all)
    chunks, width = 2 * keeps[0].shape[0], keeps[0].shape[2]

    @pl.loop(0, chunks)
    def _(place):
        hot = onehot((chip_ref[0] ^ place) * width, width, idx_all[...])
        chunk = dot2((hi_all[...], lo_all[...]), hot, NT)
        for order, (low, high), send_ref, keep_ref in zip(orders, spans, sends, keeps):
            put_chunk(spread_bits(place, order), chunk[low:high], send_ref, keep_ref)


def rel_chunks_kernel(orders, spans, grads, chip_ref, *refs):
    idx_refs, grad_refs, refs = refs[:2], refs[2 : 2 + grads], refs[2 + grads :]
    streams = len(orders)
    sends, keeps = refs[:streams], refs[streams : 2 * streams]
    idx_all, hi_all, lo_all, dense = refs[2 * streams :]
    load_columns(idx_refs, grad_refs, idx_all, hi_all, lo_all)
    chunks, width = 2 * keeps[0].shape[0], keeps[0].shape[2]
    tile = 256

    @pl.loop(0, dense.shape[1] // tile)
    def _(step):
        hot = onehot(step * tile, tile, idx_all[...])
        dense[:, pl.ds(pl.multiple_of(step * tile, tile), tile)] = dot2((hi_all[...], lo_all[...]), hot, NT)

    for chunk in range(chunks):
        place = chip_ref[0] ^ chunk
        for order, (low, high), send_ref, keep_ref in zip(orders, spans, sends, keeps):
            value = dense[low:high, chunk * width : (chunk + 1) * width]
            put_chunk(spread_bits(place, order), value, send_ref, keep_ref)


SMEM = pl.BlockSpec(memory_space=pltpu.SMEM)


def chunk_columns(kernel, rows, chip, idx, grads, orders, spans):
    chunks = 1 << len(orders[0])
    width = rows // chunks
    half_width = grads[0].shape[0]
    count = sum(g.shape[1] for g in grads)
    shapes = [jax.ShapeDtypeStruct((chunks // 2, high - low, width), F32) for low, high in spans] * 2
    dense = [pltpu.VMEM((half_width, rows), F32)] if kernel is rel_chunks_kernel else []
    out = pl.pallas_call(
        functools.partial(kernel, orders, spans, len(grads)),
        in_specs=[SMEM] + [VMEM] * (2 + len(grads)),
        out_specs=[VMEM] * len(shapes),
        out_shape=shapes,
        scratch_shapes=[
            pltpu.VMEM((1, count), jnp.int32),
            pltpu.VMEM((half_width, count), BF16),
            pltpu.VMEM((half_width, count), BF16),
        ]
        + dense,
        compiler_params=PARAMS,
        cost_estimate=pl.CostEstimate(
            flops=4 * half_width * rows * count, bytes_accessed=4 * half_width * rows, transcendentals=0
        ),
    )(chip, *idx, *grads)
    return out[: len(spans)], out[len(spans) :]


def place_kernel(orders, spans, spot_ref, *refs):
    streams = len(orders)
    lows, highs = refs[:streams], refs[streams : 2 * streams]
    hub_ref, rel_ref = refs[-2:]
    half = lows[0].shape[0]
    hub_width, rel_width = hub_ref.shape[2] // (2 * half), rel_ref.shape[2] // (2 * half)
    for chunk in range(2 * half):
        place = spot_ref[0] ^ chunk
        for order, (low, high), near, far in zip(orders, spans, lows, highs):
            index = spread_bits(place, order)
            spot = index & (half - 1)
            value = jnp.where(index >= half, far[spot], near[spot])
            hub_ref[0, low:high, chunk * hub_width : (chunk + 1) * hub_width] = value[:, :hub_width]
            rel_ref[0, low:high, chunk * rel_width : (chunk + 1) * rel_width] = value[:, hub_width:]


def place_chunks(spot, near, far, orders, spans, hub_shape, rel_shape, earlier):
    whole = [pl.BlockSpec(memory_space=pltpu.VMEM)] * (2 * len(spans))
    kept = [pl.BlockSpec(memory_space=pl.ANY)] * len(earlier)
    mine = lambda shape: pl.BlockSpec((1,) + shape[1:], lambda i, spot: (spot[1], 0, 0))
    return pl.pallas_call(
        functools.partial(place_kernel, orders, spans),
        grid_spec=pltpu.PrefetchScalarGridSpec(
            num_scalar_prefetch=1,
            grid=(1,),
            in_specs=whole + kept,
            out_specs=[mine(hub_shape), mine(rel_shape)],
        ),
        out_shape=[jax.ShapeDtypeStruct(hub_shape, F32), jax.ShapeDtypeStruct(rel_shape, F32)],
        input_output_aliases={1 + len(whole) + i: i for i in range(len(earlier))},
        compiler_params=PARAMS,
        cost_estimate=pl.CostEstimate(flops=0, bytes_accessed=2 * 4 * (hub_shape[1] * (hub_shape[2] + rel_shape[2])), transcendentals=0),
    )(spot, *near, *far, *earlier)


def adagrad(table, state, grads):
    new_state = state + jnp.sum(grads * grads, axis=0, keepdims=True) * (1.0 / grads.shape[0])
    return table - grads * (step_rate / jnp.sqrt(new_state)), new_state


def keep_and_send(core, first, second):
    return jnp.where(core == 0, first, second), jnp.where(core == 0, second, first)


def table_counts(rows, negs, weight):
    place = lax.broadcasted_iota(jnp.int32, (rows, negs.shape[1]), 0)
    return jnp.sum(jnp.where(place == negs, weight, 0.0), axis=1, keepdims=True)


def turned(x, r, half):
    x0, x1, r0, r1 = x[:half], x[half:], r[:half], r[half:]
    return jnp.concatenate([x0 * r0 - x1 * r1, x0 * r1 + x1 * r0], axis=0)


def turned_back(x, r, half):
    x0, x1, r0, r1 = x[:half], x[half:], r[:half], r[half:]
    return x0 * r0 + x1 * r1, x1 * r0 - x0 * r1


EDGE_TILE = 256


def bucket_kernel(
    core_ref, heads_ref, tails_ref, negs_ref, left_ref, left_sums_ref, right_ref, right_sums_ref, rel_ref, hub_ref,
    left_out, left_sums_out, right_out, right_sums_out, rel_keep, rel_send, hub_keep, hub_send,
    left_hi, left_lo, both_hi, both_lo, left_grad, both_grad,
):
    features, rows = left_ref.shape
    half = features // 2
    core = core_ref[0]
    weight = 1.0 / (negs_ref.shape[1] + hub_ref.shape[1])
    counts = table_counts(rows, negs_ref[...], weight)
    left_hi[...], left_lo[...] = split(left_ref[...])
    both_hi[:, :rows], both_lo[:, :rows] = split(right_ref[...])
    both_hi[:, rows:], both_lo[:, rows:] = split(hub_ref[...])
    left_grad[...] = jnp.zeros_like(left_grad)
    both_grad[...] = jnp.zeros_like(both_grad)
    tile = EDGE_TILE

    @pl.loop(0, heads_ref.shape[1] // tile)
    def _(step):
        span = pl.ds(pl.multiple_of(step * tile, tile), tile)
        head_hot = onehot(0, rows, heads_ref[:, span])
        tail_here = lax.broadcasted_iota(jnp.int32, (rows, tile), 0) == tails_ref[:, span]
        h = dot2((left_hi[...], left_lo[...]), head_hot, NN)
        r = rel_ref[:, span]
        q = split(turned(h, r, half))
        both = (both_hi[...], both_lo[...])
        scores = dot3(both, q, TN)
        chance = jax.nn.sigmoid(scores[:rows])
        coef = jnp.concatenate(
            [
                counts * chance + jnp.where(tail_here, chance - 1.0, 0.0),
                weight * jax.nn.sigmoid(scores[rows:]),
            ],
            axis=0,
        )
        coef = split(coef)
        dq = dot3(both, coef, NN)
        both_grad[...] += dot3(q, coef, NT)
        dh = jnp.concatenate(turned_back(dq, r, half), axis=0)
        left_grad[...] += dot2(split(dh), head_hot, NT)
        rel_keep[:, span], rel_send[:, span] = keep_and_send(core, *turned_back(dq, h, half))

    left_out[...], left_sums_out[...] = adagrad(left_ref[...], left_sums_ref[...], left_grad[...])
    right_out[...], right_sums_out[...] = adagrad(right_ref[...], right_sums_ref[...], both_grad[:, :rows])
    hub_keep[...], hub_send[...] = keep_and_send(core, both_grad[:half, rows:], both_grad[half:, rows:])


def like(x, rows=None):
    return jax.ShapeDtypeStruct((rows or x.shape[0], x.shape[1]), x.dtype)


def bucket_step(core, heads, tails, negs, left, left_sums, right, right_sums, rel_rows, hub_rows):
    features, rows = left.shape
    half = features // 2
    edges, hubs = heads.shape[1], hub_rows.shape[1]
    width = rows + hubs
    return pl.pallas_call(
        bucket_kernel,
        in_specs=[SMEM] + [VMEM] * 9,
        out_specs=[VMEM] * 8,
        out_shape=[like(left), like(left_sums), like(right), like(right_sums)]
        + [like(rel_rows, half)] * 2
        + [like(hub_rows, half)] * 2,
        scratch_shapes=[
            pltpu.VMEM((features, rows), BF16),
            pltpu.VMEM((features, rows), BF16),
            pltpu.VMEM((features, width), BF16),
            pltpu.VMEM((features, width), BF16),
            pltpu.VMEM((features, rows), F32),
            pltpu.VMEM((features, width), F32),
        ],
        compiler_params=PARAMS,
        cost_estimate=pl.CostEstimate(
            flops=18 * features * edges * width, bytes_accessed=24 * features * rows, transcendentals=edges * width
        ),
    )(core, heads, tails, negs, left, left_sums, right, right_sums, rel_rows, hub_rows)


def hub_kernel(
    negatives, core_ref, heads_ref, left_ref, rel_ref, hub_ref,
    head_out, query_grad, hub_keep, hub_send,
    left_hi, left_lo, hub_hi, hub_lo, hub_grad,
):
    features, rows = left_ref.shape
    half = features // 2
    weight = 1.0 / (negatives + hub_ref.shape[1])
    left_hi[...], left_lo[...] = split(left_ref[...])
    hub_hi[...], hub_lo[...] = split(hub_ref[...])
    hub_grad[...] = jnp.zeros_like(hub_grad)
    tile = EDGE_TILE

    @pl.loop(0, heads_ref.shape[1] // tile)
    def _(step):
        span = pl.ds(pl.multiple_of(step * tile, tile), tile)
        h = dot2((left_hi[...], left_lo[...]), onehot(0, rows, heads_ref[:, span]), NN)
        head_out[:, span] = h
        q = split(turned(h, rel_ref[:, span], half))
        hub = (hub_hi[...], hub_lo[...])
        coef = split(weight * jax.nn.sigmoid(dot3(hub, q, TN)))
        query_grad[:, span] = dot3(hub, coef, NN)
        hub_grad[...] += dot3(q, coef, NT)

    hub_keep[...], hub_send[...] = keep_and_send(core_ref[0], hub_grad[:half], hub_grad[half:])


def hub_step(core, heads, left, rel_rows, hub_rows, negatives):
    features, rows = left.shape
    edges, hubs = heads.shape[1], hub_rows.shape[1]
    return pl.pallas_call(
        functools.partial(hub_kernel, negatives),
        in_specs=[SMEM] + [VMEM] * 4,
        out_specs=[VMEM] * 4,
        out_shape=[like(rel_rows), like(rel_rows)] + [like(hub_rows, features // 2)] * 2,
        scratch_shapes=[
            pltpu.VMEM((features, rows), BF16),
            pltpu.VMEM((features, rows), BF16),
            pltpu.VMEM((features, hubs), BF16),
            pltpu.VMEM((features, hubs), BF16),
            pltpu.VMEM((features, hubs), F32),
        ],
        compiler_params=PARAMS,
        cost_estimate=pl.CostEstimate(
            flops=18 * features * edges * hubs + 4 * features * edges * rows,
            bytes_accessed=24 * features * rows,
            transcendentals=edges * hubs,
        ),
    )(core, heads, left, rel_rows, hub_rows)


def tables_kernel(
    hubs, core_ref, heads_ref, tails_ref, negs_ref, head_rows, query_grad,
    left_ref, left_sums_ref, right_ref, right_sums_ref, rel_ref,
    left_out, right_out, rel_keep, rel_send,
    right_hi, right_lo, left_grad, right_grad,
):
    features, rows = left_ref.shape
    half = features // 2
    core = core_ref[0]
    counts = table_counts(rows, negs_ref[...], 1.0 / (negs_ref.shape[1] + hubs))
    right_hi[...], right_lo[...] = split(right_ref[...])
    left_grad[...] = jnp.zeros_like(left_grad)
    right_grad[...] = jnp.zeros_like(right_grad)
    tile = EDGE_TILE

    @pl.loop(0, heads_ref.shape[1] // tile)
    def _(step):
        span = pl.ds(pl.multiple_of(step * tile, tile), tile)
        head_hot = onehot(0, rows, heads_ref[:, span])
        tail_here = lax.broadcasted_iota(jnp.int32, (rows, tile), 0) == tails_ref[:, span]
        h, r = head_rows[:, span], rel_ref[:, span]
        q = split(turned(h, r, half))
        right = (right_hi[...], right_lo[...])
        chance = jax.nn.sigmoid(dot3(right, q, TN))
        coef = split(counts * chance + jnp.where(tail_here, chance - 1.0, 0.0))
        dq = dot3(right, coef, NN) + query_grad[:, span]
        right_grad[...] += dot3(q, coef, NT)
        rel_keep[:, span], rel_send[:, span] = keep_and_send(core, *turned_back(dq, h, half))
        dh = jnp.concatenate(turned_back(dq, r, half), axis=0)
        left_grad[...] += dot2(split(dh), head_hot, NT)

    left_out[...], unused = adagrad(left_ref[...], left_sums_ref[...], left_grad[...])
    right_out[...], unused = adagrad(right_ref[...], right_sums_ref[...], right_grad[...])


def tables_step(hubs, core, heads, tails, negs, head_rows, query_grad, left, left_sums, right, right_sums, rel_rows):
    features, rows = left.shape
    edges = heads.shape[1]
    return pl.pallas_call(
        functools.partial(tables_kernel, hubs),
        in_specs=[SMEM] + [VMEM] * 10,
        out_specs=[VMEM] * 4,
        out_shape=[like(left), like(right)] + [like(rel_rows, features // 2)] * 2,
        scratch_shapes=[
            pltpu.VMEM((features, rows), BF16),
            pltpu.VMEM((features, rows), BF16),
            pltpu.VMEM((features, rows), F32),
            pltpu.VMEM((features, rows), F32),
        ],
        compiler_params=PARAMS,
        cost_estimate=pl.CostEstimate(
            flops=22 * features * edges * rows, bytes_accessed=24 * features * rows, transcendentals=edges * rows
        ),
    )(core, heads, tails, negs, head_rows, query_grad, left, left_sums, right, right_sums, rel_rows)


def from_behind(x, axis, by):
    size = lax.axis_size(axis)
    return lax.ppermute(x, axis, [(i, (i + by) % size) for i in range(size)])


def flipped(x, axis, bit):
    return lax.ppermute(x, axis, [(i, i ^ (1 << bit)) for i in range(lax.axis_size(axis))])


def other_core(x):
    return flipped(x, "blk", 0)


def across(x, place):
    sub_bits = lax.axis_size("sub").bit_length() - 1
    if place < sub_bits:
        return flipped(x, "sub", place)
    return flipped(x, "blk", place - sub_bits + 1)


def stream_orders():
    sub_bits = lax.axis_size("sub").bit_length() - 1
    bits = sub_bits + lax.axis_size("blk").bit_length() - 2
    x, y, z, far = sub_bits, sub_bits + 1, 0, 1
    rest = [p for p in range(bits) if p not in (x, y, z, far)]
    return [[x, y, z, far] + rest, [y, z, x, far] + rest, [z, x, far, y] + rest]


def row_spans(rows, parts):
    ends = [-(-rows * (i + 1) // (8 * parts)) * 8 for i in range(parts - 1)] + [rows]
    return list(zip([0] + ends[:-1], ends))


def shards(
    left_emb, left_state, right_emb, right_state, relation_emb, relation_state, hub_emb, hub_state,
    heads, relations, tails, negatives, hub_ids,
):
    components, half_width, row_count = left_emb.shape
    features = components * half_width
    rel_count, hub_count = relation_emb.shape[2], hub_emb.shape[2]
    left = left_emb.reshape(features, row_count)
    right = right_emb.reshape(features, row_count)
    rel_table = relation_emb.reshape(features, rel_count)
    hub_table = hub_emb.reshape(features, hub_count)
    left_sums = left_state.reshape(1, row_count)
    right_sums = right_state.reshape(1, row_count)
    buckets, edges = heads.shape
    hubs = hub_ids.shape[1]

    core_id = lax.axis_index("blk") % 2
    chip_id = (lax.axis_index("blk") // 2) * lax.axis_size("sub") + lax.axis_index("sub")
    core, chip = core_id.astype(jnp.int32).reshape(1), chip_id.astype(jnp.int32).reshape(1)
    orders = stream_orders()
    spans = row_spans(half_width, len(orders))
    chunks = 1 << len(orders[0])
    hub_width, rel_width = hub_count // chunks, rel_count // chunks

    all_rel = relations.reshape(1, buckets * edges)
    all_hub = hub_ids.reshape(1, buckets * hubs)
    far_rel, far_hub = other_core((all_rel, all_hub))
    rel_rows = gather_columns(rel_table, all_rel, 1)
    hub_rows = [gather_columns(hub_table, hub_ids[b : b + 1], 4) for b in range(buckets)]
    rel_keep, rel_far, hub_keep, hub_far = [], [], [], []
    for b in range(buckets):
        rows_b = rel_rows[:, b * edges : (b + 1) * edges]
        at = slice(b, b + 1)
        if b < buckets - 1:
            left, left_sums, right, right_sums, rk, rs, hk, hs = bucket_step(
                core, heads[at], tails[at], negatives[at], left, left_sums, right, right_sums, rows_b, hub_rows[b]
            )
            right, right_sums = from_behind((right, right_sums), "blk", 1)
            hub_far.append(other_core(hs))
            rel_far.append(other_core(rs))
            hub_keep.append(hk)
            rel_keep.append(rk)
        else:
            head_rows, query_grad, hk, hs = hub_step(core, heads[at], left, rows_b, hub_rows[b], negatives.shape[1])
            hub_far.append(other_core(hs))
            hub_keep.append(hk)
            hub_send, hub_own = chunk_columns(
                hub_chunks_kernel, hub_count, chip, (all_hub, far_hub), hub_keep + hub_far, orders, spans
            )
            hub_got = [across(x, order[0]) for x, order in zip(hub_send, orders)]
            left, right, rk, rs = tables_step(
                hubs, core, heads[at], tails[at], negatives[at], head_rows, query_grad,
                left, left_sums, right, right_sums, rows_b,
            )
            rel_far.append(other_core(rs))
            rel_keep.append(rk)
    rel_send, rel_own = chunk_columns(
        rel_chunks_kernel, rel_count, chip, (all_rel, far_rel), rel_keep + rel_far, orders, spans
    )
    rel_got = [across(x, order[0]) for x, order in zip(rel_send, orders)]

    totals = []
    for s, order in enumerate(orders):
        half = chunks // 4

        def joined(part):
            return jnp.concatenate(
                [hub_own[s][part] + hub_got[s][part], rel_own[s][part] + rel_got[s][part]], axis=2
            )

        send, own = joined(slice(half, None)), joined(slice(0, half))
        for step, place in enumerate(order[1:]):
            got = across(send, place)
            if half > 1:
                half //= 2
                send, own = own[half:] + got[half:], own[:half] + got[:half]
            else:
                own = own + got
        totals.append(own[0])

    squares = sum(jnp.sum(g * g, axis=0, keepdims=True) for g in totals)
    squares = squares + other_core(squares)
    cut = lambda x, width: lax.dynamic_slice(x, (core_id, 0, chip_id * width), (1, half_width, width))[0]
    cut_sums = lambda x, width: lax.dynamic_slice(x, (chip_id * width,), (width,))
    owned = jnp.concatenate([cut(hub_emb, hub_width), cut(relation_emb, rel_width)], axis=1)
    sums = jnp.concatenate([cut_sums(hub_state, hub_width), cut_sums(relation_state, rel_width)])[None]
    scale = step_rate / jnp.sqrt(sums + squares * (1.0 / features))
    near, far = [], []
    for (low, high), g, order in zip(spans, totals, orders):
        have = (owned[low:high] - g * scale)[None]
        for place in order[:0:-1]:
            have = jnp.concatenate([have, across(have, place)], axis=0)
        near.append(have)
        far.append(across(have, order[0]))
    shapes = (hub_emb.shape, relation_emb.shape)
    out = place_chunks(jnp.concatenate([chip, core]), near, far, orders, spans, *shapes, ())
    out = place_chunks(
        jnp.concatenate([chip, 1 - core]), other_core(near), other_core(far), orders, spans, *shapes, tuple(out)
    )
    return (
        left.reshape(components, half_width, row_count),
        right.reshape(components, half_width, row_count),
        out[1],
        out[0],
    )


def solution(mesh):
    both = ("blk", "sub")
    block, table, whole = P(None, None, both), P(None, both), P()
    return jax.shard_map(
        shards,
        mesh=mesh,
        in_specs=(block, P(both), block, P(both), whole, whole, whole, whole, table, table, table, table, table),
        out_specs=(block, block, whole, whole),
        check_vma=False,
    )
```

time: 265 us -> 193 us (0.73)
  waiting for transfers between devices: 194 us -> 76.1 us
  starting transfers between devices: 3.14 us -> 37.7 us
  Pallas kernels: 34.9 us -> 56 us
  local copies, waits for them, and re-layouts: 4.93 us -> 19 us
  between operations: 14.2 us -> 1.12 us
  other arithmetic: 13.3 us -> 2.43 us
    psum x1 -> x0, waiting for transfers between devices: 184 us -> none  [shards(): rel_total, hub_total = lax.psum((rel_total, hub_total), ('blk', 'sub'))]
    ppermute x0 -> x40, waiting for transfers between devices: none -> 76.1 us  [flipped(): lax.ppermute(x, axis, [(i, i ^ 1 << bit) for i in range(lax.axis_size(axi...]
    ppermute x0 -> x40, starting transfers between devices: none -> 37.2 us  [flipped(): lax.ppermute(x, axis, [(i, i ^ 1 << bit) for i in range(lax.axis_size(axi...]
    pallas_call x4 -> x7, Pallas kernels: 25.7 us -> 43.3 us  [the longest x2 17.3 us: chunk_columns(): pl.pallas_call(functools.partial(kernel, orders, spans, len(grads)), in_s...]
    sub x2 -> x0, other arithmetic: 10.5 us -> none  [adagrad(): return (table - grads * (step_rate / jnp.sqrt(new_state)), new_state)]
    ppermute x2, waiting for transfers between devices: 10.3 us -> 0.01 us  [from_behind(): return lax.ppermute(x, axis, [(i, (i + by) % size) for i in range(size)])]
    unnamed x24 -> x52, local copies, waits for them, and re-layouts: 3.96 us -> 13.9 us
    pallas_call x2 -> x3, Pallas kernels: 9.16 us -> 12.7 us  [gather_columns(): pl.pallas_call(functools.partial(gather_kernel, tile), grid=(steps,), in_...]
  transfers between devices with their start and end apart: 3 -> 42, of which waited for: 2 -> 20; matrix products, arithmetic and copies ran while one was open for 0% -> 3% of each run, Pallas kernels for 0% -> 19%
where the time goes in v1:
time: 193 us; the launch traced here: 192 us
  waiting for transfers between devices  76.1 us (39%)
  Pallas kernels  56 us (29%)
  starting transfers between devices  37.7 us (20%)
  local copies, waits for them, and re-layouts  19 us (10%)
  other arithmetic  2.43 us (1%)
    ppermute x40, waiting for transfers between devices, flipped(): lax.ppermute(x, axis, [(i, i ^ 1 << bit) for i in range(lax.axis_size(axi...  76.1 us
    ppermute x40, starting transfers between devices, flipped(): lax.ppermute(x, axis, [(i, i ^ 1 << bit) for i in range(lax.axis_size(axi...  37.2 us
    pallas_call x2, Pallas kernels, chunk_columns(): pl.pallas_call(functools.partial(kernel, orders, spans, len(grads)), in_s...  17.3 us
    unnamed x52, local copies, waits for them, and re-layouts  13.9 us
    pallas_call x3, Pallas kernels, gather_columns(): pl.pallas_call(functools.partial(gather_kernel, tile), grid=(steps,), in_...  12.7 us
    pallas_call x1, Pallas kernels, bucket_step(): pl.pallas_call(bucket_kernel, in_specs=[SMEM] + [VMEM] * 9, out_specs=[VM...  8.33 us
    pallas_call x1, Pallas kernels, tables_step(): pl.pallas_call(functools.partial(tables_kernel, hubs), in_specs=[SMEM] +...  7.96 us
    pallas_call x2, Pallas kernels, place_chunks(): pl.pallas_call(functools.partial(place_kernel, orders, spans), grid_spec=...  6.25 us
  transfers between devices with their start and end apart: 42, of which 20 were waited for; matrix products, arithmetic and copies ran while one was open for 3% of the time, Pallas kernels for 19%

profile of v1, /device:TPU:0, one launch (start us, length us, event | category | flops | bytes accessed | tf_op | source)
XLA Modules:
  0.0 192.3 jit_solution(4882843742308214887)
XLA Ops:
  2.9 1.6 copy-done
  4.5 2.6 %shard_map.156 = f32[400,1024]{1,0:T(8,128)S(1)} custom-call(s32[1,1024]{1,0:T(1,128)S(1)} %bitcast.45, f32[400,1280]{1,0:T(8,128)S(1)} %bitcast.44), custom_call_target="tpu_custom_call" | custom-call | flops 2097152000 | bytes 2048000 | tf_op jit(solution)/shard_map/pallas_call | solution.py:57
  7.9 5.1 %shard_map.157.hub_ref = f32[400,256]{1,0:T(8,128)S(1)} custom-call(s32[1,256]{1,0:T(1,128)S(1)} %get-tuple-element.97.idx_ref, f32[400,4096]{1,0:T(8,128)} %bitcast.54), custom_call_target="tpu_custom_call" | custom-call | flops 1677721600 | bytes 6553600 | tf_op jit(solution)/shard_map/pallas_call | solution.py:57
  13.0 8.3 %shard_map.158 = (f32[400,512]{1,0:T(8,128)S(1)}, f32[1,512]{1,0:T(1,128)S(1)}, f32[400,512]{1,0:T(8,128)S(1)}, f32[1,512]{1,0:T(1,128)S(1)}, f32[200,512]{1,0:T...) custom-call(s32[1]{0:T(128)} %bitcast.core_ref, ...), custom_call_target="tpu_custom_call" | custom-call | flops 2831155200 | bytes 4915200 | tf_op jit(solution)/shard_map/pallas_call | solution.py:287
  21.9 5.0 %shard_map.159.hub_ref = f32[400,256]{1,0:T(8,128)S(1)} custom-call(s32[1,256]{1,0:T(1,128)S(1)} %get-tuple-element.96.idx_ref, f32[400,4096]{1,0:T(8,128)} %bitcast.55), custom_call_target="tpu_custom_call" | custom-call | flops 1677721600 | bytes 6553600 | tf_op jit(solution)/shard_map/pallas_call | solution.py:57
  26.9 3.4 %shard_map.160 = (f32[400,512]{1,0:T(8,128)S(1)}, f32[400,512]{1,0:T(8,128)S(1)}, f32[200,256]{1,0:T(8,128)S(1)}, f32[200,256]{1,0:T(8,128)S(1)}) custom-call(s32[1]{0:T(128)} %bitcast.core_ref, s32[1,512]{1,0:T(1,128)S(1)} %get-tuple-element.98.heads_ref, f32[400,512]{1,0:T(8,128)S(1)} %get-tuple-element.36.left_ref, ...), custom_call_target="tpu_custom_call" | custom-call | flops 1363148800 | bytes 4915200 | tf_op jit(solution)/shard_map/pallas_call | solution.py:339
  33.4 2.6 %collective-permute-start.2 = (s32[1,512]{1,0:T(1,128)S(1)}, s32[1,512]{1,0:T(1,128)S(1)}, u32[]{:S(2)}, u32[]{:S(2)}) collective-permute-start(s32[1,512]{1,0:T(1,128)S(1)} %bitcast.48), channel_id=1, source_target_pairs={{0,4},{4,0},{8,12},{12,8},{16,20},{20,16},{24,28},{28,24},{1,5},{5... | collective-permute-start | bytes 6152 | tf_op jit(solution)/shard_map/ppermute | solution.py:422
  40.3 9.3 %shard_map.162 = (f32[8,72,256]{2,1,0:T(8,128)S(1)}, f32[8,64,256]{2,1,0:T(8,128)}, f32[8,64,256]{2,1,0:T(8,128)S(1)}, f32[8,72,256]{2,1,0:T(8,128)S(1)}, f32[8,...) custom-call(s32[1]{0:T(128)} %bitcast.9.chip_ref, s32[1,512]{1,0:T(1,128)S(1)} %bitcast.49, ...), custom_call_target="tpu_custom_call" | custom-call | flops 3355443200 | bytes 3276800 | tf_op jit(solution)/shard_map/pallas_call | solution.py:150
  51.2 1.6 collective-permute-start.13
  54.3 1.6 collective-permute-start.18
  63.3 8.0 %shard_map.161 = (f32[400,512]{1,0:T(8,128)}, f32[400,512]{1,0:T(8,128)}, f32[200,512]{1,0:T(8,128)S(1)}, f32[200,512]{1,0:T(8,128)S(1)}) custom-call(s32[1]{0:T(128)} %bitcast.core_ref, s32[1,512]{1,0:T(1,128)S(1)} %get-tuple-element.98.heads_ref, s32[1,512]{1,0:T(1,128)S(1)} %get-tuple-element.93.tails_ref, s32[1,1024]{1,0:T(1,128)S(1)} %get-tuple-element.91.negs_ref, ...), custom_call_target="tpu_custom_call" | custom-call | flops 2306867200 | bytes 4915200 | tf_op jit(solution)/shard_map/pallas_call | solution.py:398
  73.0 8.0 %shard_map.163 = (f32[8,72,80]{2,1,0:T(8,128)S(1)}, f32[8,64,80]{2,1,0:T(8,128)S(1)}, f32[8,64,80]{2,1,0:T(8,128)S(1)}, f32[8,72,80]{2,1,0:T(8,128)S(1)}, f32[8,...) custom-call(s32[1]{0:T(128)} %bitcast.9.chip_ref, s32[1,1024]{1,0:T(1,128)S(1)} %bitcast.47, ...), custom_call_target="tpu_custom_call" | custom-call | flops 2097152000 | bytes 1024000 | tf_op jit(solution)/shard_map/pallas_call | solution.py:150
  81.0 1.5 collective-permute-start.14
  83.6 5.7 %collective-permute-done.14 = f32[8,64,80]{2,1,0:T(8,128)S(1)} collective-permute-done((f32[8,64,80]{2,1,0:T(8,128)S(1)}, f32[8,64,80]{2,1,0:T(8,128)S(1)}, u32[]{:S(2)}, u32[]{:S(2)}) %collective-permute-start.14) | collective-permute-done | bytes 163872 | tf_op jit(solution)/shard_map/ppermute | solution.py:422
  92.9 7.0 %collective-permute-done.15 = f32[4,64,336]{2,1,0:T(8,128)S(1)} collective-permute-done((f32[4,64,336]{2,1,0:T(8,128)S(1)}, f32[4,64,336]{2,1,0:T(8,128)S(1)}, u32[]{:S(2)}, u32[]{:S(2)}) %collective-permute-start.15) | collective-permute-done | bytes 344096 | tf_op jit(solution)/shard_map/ppermute | solution.py:422
  101.3 2.7 %collective-permute-start.21 = (f32[2,64,336]{2,1,0:T(8,128)S(1)}, f32[2,64,336]{2,1,0:T(8,128)S(1)}, u32[]{:S(2)}, u32[]{:S(2)}) collective-permute-start(f32[2,64,336]{2,1,0:T(8,128)S(1)} %get-tuple-element.81), channel_id=1, source_target_pairs={{0,2},{1,3},{2,0},{3,1},{4,6},{5,7},{6,4},{7,5},{8,10},{9,11},{10,... | collective-permute-start | bytes 516104 | tf_op jit(solution)/shard_map/ppermute | solution.py:422
  105.7 2.7 %collective-permute-start.17 = (f32[1,64,336]{2,1,0:T(8,128)S(1)}, f32[1,64,336]{2,1,0:T(8,128)S(1)}, u32[]{:S(2)}, u32[]{:S(2)}) collective-permute-start(f32[1,64,336]{2,1,0:T(8,128)S(1)} %slice_add_fusion.19), channel_id=1, source_target_pairs={{0,2},{1,3},{2,0},{3,1},{4,6},{5,7},{6,4},{7,5},{8,10},{9,11},{10,... | collective-permute-start | bytes 258056 | tf_op jit(solution)/shard_map/ppermute | solution.py:422
  108.4 6.0 %collective-permute-done.21 = f32[2,64,336]{2,1,0:T(8,128)S(1)} collective-permute-done((f32[2,64,336]{2,1,0:T(8,128)S(1)}, f32[2,64,336]{2,1,0:T(8,128)S(1)}, u32[]{:S(2)}, u32[]{:S(2)}) %collective-permute-start.21) | collective-permute-done | bytes 172064 | tf_op jit(solution)/shard_map/ppermute | solution.py:422
  115.7 3.4 %collective-permute-done.22 = f32[1,64,336]{2,1,0:T(8,128)S(1)} collective-permute-done((f32[1,64,336]{2,1,0:T(8,128)S(1)}, f32[1,64,336]{2,1,0:T(8,128)S(1)}, u32[]{:S(2)}, u32[]{:S(2)}) %collective-permute-start.22) | collective-permute-done | bytes 86048 | tf_op jit(solution)/shard_map/ppermute | solution.py:422
  121.8 2.9 %collective-permute-start.28 = (f32[1,64,336]{2,1,0:T(8,128)S(1)}, f32[1,64,336]{2,1,0:T(8,128)S(1)}, u32[]{:S(2)}, u32[]{:S(2)}) collective-permute-start(f32[1,64,336]{2,1,0:T(8,128)S(1)} %get-tuple-element.89), channel_id=1, source_target_pairs={{0,2},{1,3},{2,0},{3,1},{4,6},{5,7},{6,4},{7,5},{8,10},{9,11},{10,... | collective-permute-start | bytes 258056 | tf_op jit(solution)/shard_map/ppermute | solution.py:422
  124.7 8.3 %collective-permute-done.24 = f32[1,72,336]{2,1,0:T(8,128)S(1)} collective-permute-done((f32[1,72,336]{2,1,0:T(8,128)S(1)}, f32[1,72,336]{2,1,0:T(8,128)S(1)}, u32[]{:S(2)}, u32[]{:S(2)}) %collective-permute-start.24) | collective-permute-done | bytes 96800 | tf_op jit(solution)/shard_map/ppermute | solution.py:422
  133.2 1.9 %collective-permute-start.32 = (f32[1,64,336]{2,1,0:T(8,128)S(1)}, f32[1,64,336]{2,1,0:T(8,128)S(1)}, u32[]{:S(2)}, u32[]{:S(2)}) collective-permute-start(f32[1,64,336]{2,1,0:T(8,128)S(1)} %get-tuple-element.88), channel_id=1, source_target_pairs={{0,16},{4,20},{8,24},{12,28},{16,0},{20,4},{24,8},{28,12},{1,17},{... | collective-permute-start | bytes 258056 | tf_op jit(solution)/shard_map/ppermute | solution.py:422
  136.0 3.1 %collective-permute-done.25 = f32[2,72,336]{2,1,0:T(8,128)S(1)} collective-permute-done((f32[2,72,336]{2,1,0:T(8,128)S(1)}, f32[2,72,336]{2,1,0:T(8,128)S(1)}, u32[]{:S(2)}, u32[]{:S(2)}) %collective-permute-start.25) | collective-permute-done | bytes 193568 | tf_op jit(solution)/shard_map/ppermute | solution.py:422
  139.1 3.3 %collective-permute-start.26 = (f32[4,72,336]{2,1,0:T(8,128)S(1)}, f32[4,72,336]{2,1,0:T(8,128)S(1)}, u32[]{:S(2)}, u32[]{:S(2)}) collective-permute-start(f32[4,72,336]{2,1,0:T(8,128)S(1)} %pad_maximum_fusion.4), channel_id=1, source_target_pairs={{0,16},{4,20},{8,24},{12,28},{16,0},{20,4},{24,8},{28,12},{1,17},{... | collective-permute-start | bytes 1161224 | tf_op jit(solution)/shard_map/ppermute | solution.py:422
  143.1 1.8 collective-permute-start.30
  144.9 8.5 %collective-permute-done.33 = f32[2,64,336]{2,1,0:T(8,128)S(1)} collective-permute-done((f32[2,64,336]{2,1,0:T(8,128)S(1)}, f32[2,64,336]{2,1,0:T(8,128)S(1)}, u32[]{:S(2)}, u32[]{:S(2)}) %collective-permute-start.33) | collective-permute-done | bytes 172064 | tf_op jit(solution)/shard_map/ppermute | solution.py:422
  153.6 2.1 %collective-permute-start.36 = (f32[8,72,336]{2,1,0:T(8,128)S(1)}, f32[8,72,336]{2,1,0:T(8,128)S(1)}, u32[]{:S(2)}, u32[]{:S(2)}) collective-permute-start(f32[8,72,336]{2,1,0:T(8,128)S(1)} %pad_maximum_fusion.refs_0_), channel_id=1, source_target_pairs={{0,8},{4,12},{8,0},{12,4},{16,24},{20,28},{24,16},{28,20},{1,9},{5... | collective-permute-start | bytes 2322440 | tf_op jit(solution)/shard_map/ppermute | solution.py:422
  155.6 1.6 collective-permute-done.30
  158.4 7.1 %collective-permute-done.34 = f32[4,64,336]{2,1,0:T(8,128)S(1)} collective-permute-done((f32[4,64,336]{2,1,0:T(8,128)S(1)}, f32[4,64,336]{2,1,0:T(8,128)S(1)}, u32[]{:S(2)}, u32[]{:S(2)}) %collective-permute-start.34) | collective-permute-done | bytes 344096 | tf_op jit(solution)/shard_map/ppermute | solution.py:422
  165.7 17.7 %collective-permute-done.36.refs_3_ = f32[8,72,336]{2,1,0:T(8,128)S(1)} collective-permute-done((f32[8,72,336]{2,1,0:T(8,128)S(1)}, f32[8,72,336]{2,1,0:T(8,128)S(1)}, u32[]{:S(2)}, u32[]{:S(2)}) %collective-permute-start.36) | collective-permute-done | bytes 774176 | tf_op jit(solution)/shard_map/ppermute | solution.py:422
  184.6 3.1 %shard_map.164 = (f32[2,200,4096]{2,1,0:T(8,128)}, f32[2,200,1280]{2,1,0:T(8,128)}) custom-call(s32[2]{0:T(128)S(1)} %pad_add_fusion.1.spot_ref, f32[8,72,336]{2,1,0:T(8,128)S(1)} %pad_maximum_fusion.refs_0_, f32[8,64,336]{2,1,0:T(8,128)S(1)} %pad_maximum_fusion.1.refs_1_, f32[8,64,336]{2,1,0:T(8,128)S(1)} %pad_maximum_fusion.2.refs_2_, ...), custom_call_target="tpu_custom_call" | custom-call | bytes 8601600 | tf_op jit(solution)/shard_map/pallas_call | solution.py:189
  189.2 3.1 %shard_map.165 = (f32[2,200,4096]{2,1,0:T(8,128)}, f32[2,200,1280]{2,1,0:T(8,128)}) custom-call(s32[2]{0:T(128)S(1)} %pad_add_fusion.spot_ref, f32[8,72,336]{2,1,0:T(8,128)S(1)} %collective-permute-done.27.refs_0_, f32[8,64,336]{2,1,0:T(8,128)S(1)} %collective-permute-done.31.refs_1_, ...), custom_call_target="tpu_custom_call", output_to_operand_aliasing={{0}: (7, {}), {1}: (8, {})} | custom-call | bytes 8601600 | tf_op jit(solution)/shard_map/pallas_call | solution.py:189
  (157 shorter events, 40.4 us)
Async XLA Ops:
  21.4 15.5 %collective-permute-start.3 = (f32[200,256]{1,0:T(8,128)S(1)}, f32[200,256]{1,0:T(8,128)S(1)}, u32[]{:S(2)}, u32[]{:S(2)}) collective-permute-start(f32[200,256]{1,0:T(8,128)S(1)} %get-tuple-element.46), channel_id=1, source_target_pairs={{0,4},{4,0},{8,12},{12,8},{16,20},{20,16},{24,28},{28,24},{1,5},{5... | collective-permute-start | bytes 614408 | tf_op jit(solution)/shard_map/ppermute | solution.py:422
  33.4 25.8 %collective-permute-start = (f32[400,512]{1,0:T(8,128)S(1)}, f32[400,512]{1,0:T(8,128)}, u32[]{:S(2)}, u32[]{:S(2)}) collective-permute-start(f32[400,512]{1,0:T(8,128)S(1)} %get-tuple-element.40), channel_id=1, source_target_pairs={{0,4},{4,8},{8,12},{12,16},{16,20},{20,24},{24,28},{28,0},{1,5},{5... | collective-permute-start | bytes 2457608 | tf_op jit(solution)/shard_map/ppermute | solution.py:418
  51.2 20.0 %collective-permute-start.13 = (f32[8,64,256]{2,1,0:T(8,128)}, f32[8,64,256]{2,1,0:T(8,128)}, u32[]{:S(2)}, u32[]{:S(2)}) collective-permute-start(f32[8,64,256]{2,1,0:T(8,128)} %get-tuple-element.57), channel_id=1, source_target_pairs={{0,16},{4,20},{8,24},{12,28},{16,0},{20,4},{24,8},{28,12},{1,17},{... | collective-permute-start | bytes 1572872 | tf_op jit(solution)/shard_map/ppermute | solution.py:422
  52.8 19.8 %collective-permute-start.6 = (s32[1,1024]{1,0:T(1,128)S(1)}, s32[1,1024]{1,0:T(1,128)S(1)}, u32[]{:S(2)}, u32[]{:S(2)}) collective-permute-start(s32[1,1024]{1,0:T(1,128)S(1)} %bitcast.46), channel_id=1, source_target_pairs={{0,4},{4,0},{8,12},{12,8},{16,20},{20,16},{24,28},{28,24},{1,5},{5... | collective-permute-start | bytes 12296 | tf_op jit(solution)/shard_map/ppermute | solution.py:422
  54.3 18.3 %collective-permute-start.18 = (f32[8,64,256]{2,1,0:T(8,128)}, f32[8,64,256]{2,1,0:T(8,128)S(1)}, u32[]{:S(2)}, u32[]{:S(2)}) collective-permute-start(f32[8,64,256]{2,1,0:T(8,128)} %copy-done.4), channel_id=1, source_target_pairs={{0,1},{1,0},{2,3},{3,2},{4,5},{5,4},{6,7},{7,6},{8,9},{9,8},{10,11... | collective-permute-start | bytes 1572872 | tf_op jit(solution)/shard_map/ppermute | solution.py:422
  58.5 14.2 %collective-permute-start.7 = (f32[200,512]{1,0:T(8,128)}, f32[200,512]{1,0:T(8,128)S(1)}, u32[]{:S(2)}, u32[]{:S(2)}) collective-permute-start(f32[200,512]{1,0:T(8,128)} %copy-done.5), channel_id=1, source_target_pairs={{0,4},{4,0},{8,12},{12,8},{16,20},{20,16},{24,28},{28,24},{1,5},{5... | collective-permute-start | bytes 1228808 | tf_op jit(solution)/shard_map/ppermute | solution.py:422
  59.2 23.4 %collective-permute-start.5 = (f32[8,72,256]{2,1,0:T(8,128)}, f32[8,72,256]{2,1,0:T(8,128)S(1)}, u32[]{:S(2)}, u32[]{:S(2)}) collective-permute-start(f32[8,72,256]{2,1,0:T(8,128)} %copy-done.3), channel_id=1, source_target_pairs={{0,8},{4,12},{8,0},{12,4},{16,24},{20,28},{24,16},{28,20},{1,9},{5... | collective-permute-start | bytes 1769480 | tf_op jit(solution)/shard_map/ppermute | solution.py:422
  81.0 8.4 %collective-permute-start.14 = (f32[8,64,80]{2,1,0:T(8,128)S(1)}, f32[8,64,80]{2,1,0:T(8,128)S(1)}, u32[]{:S(2)}, u32[]{:S(2)}) collective-permute-start(f32[8,64,80]{2,1,0:T(8,128)S(1)} %get-tuple-element.59), channel_id=1, source_target_pairs={{0,16},{4,20},{8,24},{12,28},{16,0},{20,4},{24,8},{28,12},{1,17},{... | collective-permute-start | bytes 491528 | tf_op jit(solution)/shard_map/ppermute | solution.py:422
  82.6 8.1 %collective-permute-start.19 = (f32[8,64,80]{2,1,0:T(8,128)S(1)}, f32[8,64,80]{2,1,0:T(8,128)S(1)}, u32[]{:S(2)}, u32[]{:S(2)}) collective-permute-start(f32[8,64,80]{2,1,0:T(8,128)S(1)} %get-tuple-element.63), channel_id=1, source_target_pairs={{0,1},{1,0},{2,3},{3,2},{4,5},{5,4},{6,7},{7,6},{8,9},{9,8},{10,11... | collective-permute-start | bytes 491528 | tf_op jit(solution)/shard_map/ppermute | solution.py:422
  83.1 8.5 %collective-permute-start.9 = (f32[8,72,80]{2,1,0:T(8,128)S(1)}, f32[8,72,80]{2,1,0:T(8,128)S(1)}, u32[]{:S(2)}, u32[]{:S(2)}) collective-permute-start(f32[8,72,80]{2,1,0:T(8,128)S(1)} %get-tuple-element.55), channel_id=1, source_target_pairs={{0,8},{4,12},{8,0},{12,4},{16,24},{20,28},{24,16},{28,20},{1,9},{5... | collective-permute-start | bytes 552968 | tf_op jit(solution)/shard_map/ppermute | solution.py:422
  89.4 10.4 %collective-permute-start.15 = (f32[4,64,336]{2,1,0:T(8,128)S(1)}, f32[4,64,336]{2,1,0:T(8,128)S(1)}, u32[]{:S(2)}, u32[]{:S(2)}) collective-permute-start(f32[4,64,336]{2,1,0:T(8,128)S(1)} %pad_maximum_fusion.5), channel_id=1, source_target_pairs={{0,1},{1,0},{2,3},{3,2},{4,5},{5,4},{6,7},{7,6},{8,9},{9,8},{10,11... | collective-permute-start | bytes 1032200 | tf_op jit(solution)/shard_map/ppermute | solution.py:422
  90.8 10.5 %collective-permute-start.20 = (f32[4,64,336]{2,1,0:T(8,128)S(1)}, f32[4,64,336]{2,1,0:T(8,128)S(1)}, u32[]{:S(2)}, u32[]{:S(2)}) collective-permute-start(f32[4,64,336]{2,1,0:T(8,128)S(1)} %pad_maximum_fusion.6), channel_id=1, source_target_pairs={{0,8},{4,12},{8,0},{12,4},{16,24},{20,28},{24,16},{28,20},{1,9},{5... | collective-permute-start | bytes 1032200 | tf_op jit(solution)/shard_map/ppermute | solution.py:422
  91.7 12.4 %collective-permute-start.10 = (f32[4,72,336]{2,1,0:T(8,128)S(1)}, f32[4,72,336]{2,1,0:T(8,128)S(1)}, u32[]{:S(2)}, u32[]{:S(2)}) collective-permute-start(f32[4,72,336]{2,1,0:T(8,128)S(1)} %pad_maximum_fusion.3), channel_id=1, source_target_pairs={{0,16},{4,20},{8,24},{12,28},{16,0},{20,4},{24,8},{28,12},{1,17},{... | collective-permute-start | bytes 1161224 | tf_op jit(solution)/shard_map/ppermute | solution.py:422
  99.9 5.7 %collective-permute-start.16 = (f32[2,64,336]{2,1,0:T(8,128)S(1)}, f32[2,64,336]{2,1,0:T(8,128)S(1)}, u32[]{:S(2)}, u32[]{:S(2)}) collective-permute-start(f32[2,64,336]{2,1,0:T(8,128)S(1)} %get-tuple-element.79), channel_id=1, source_target_pairs={{0,8},{4,12},{8,0},{12,4},{16,24},{20,28},{24,16},{28,20},{1,9},{5... | collective-permute-start | bytes 516104 | tf_op jit(solution)/shard_map/ppermute | solution.py:422
  101.3 13.1 %collective-permute-start.21 = (f32[2,64,336]{2,1,0:T(8,128)S(1)}, f32[2,64,336]{2,1,0:T(8,128)S(1)}, u32[]{:S(2)}, u32[]{:S(2)}) collective-permute-start(f32[2,64,336]{2,1,0:T(8,128)S(1)} %get-tuple-element.81), channel_id=1, source_target_pairs={{0,2},{1,3},{2,0},{3,1},{4,6},{5,7},{6,4},{7,5},{8,10},{9,11},{10,... | collective-permute-start | bytes 516104 | tf_op jit(solution)/shard_map/ppermute | solution.py:422
  104.1 10.4 %collective-permute-start.11 = (f32[2,72,336]{2,1,0:T(8,128)S(1)}, f32[2,72,336]{2,1,0:T(8,128)S(1)}, u32[]{:S(2)}, u32[]{:S(2)}) collective-permute-start(f32[2,72,336]{2,1,0:T(8,128)S(1)} %get-tuple-element.77), channel_id=1, source_target_pairs={{0,1},{1,0},{2,3},{3,2},{4,5},{5,4},{6,7},{7,6},{8,9},{9,8},{10,11... | collective-permute-start | bytes 580616 | tf_op jit(solution)/shard_map/ppermute | solution.py:422
  105.7 10.0 %collective-permute-start.17 = (f32[1,64,336]{2,1,0:T(8,128)S(1)}, f32[1,64,336]{2,1,0:T(8,128)S(1)}, u32[]{:S(2)}, u32[]{:S(2)}) collective-permute-start(f32[1,64,336]{2,1,0:T(8,128)S(1)} %slice_add_fusion.19), channel_id=1, source_target_pairs={{0,2},{1,3},{2,0},{3,1},{4,6},{5,7},{6,4},{7,5},{8,10},{9,11},{10,... | collective-permute-start | bytes 258056 | tf_op jit(solution)/shard_map/ppermute | solution.py:422
  121.6 11.4 %collective-permute-start.24 = (f32[1,72,336]{2,1,0:T(8,128)S(1)}, f32[1,72,336]{2,1,0:T(8,128)S(1)}, u32[]{:S(2)}, u32[]{:S(2)}) collective-permute-start(f32[1,72,336]{2,1,0:T(8,128)S(1)} %fusion.8), channel_id=1, source_target_pairs={{0,2},{1,3},{2,0},{3,1},{4,6},{5,7},{6,4},{7,5},{8,10},{9,11},{10,... | collective-permute-start | bytes 290312 | tf_op jit(solution)/shard_map/ppermute | solution.py:422
  121.8 13.3 %collective-permute-start.28 = (f32[1,64,336]{2,1,0:T(8,128)S(1)}, f32[1,64,336]{2,1,0:T(8,128)S(1)}, u32[]{:S(2)}, u32[]{:S(2)}) collective-permute-start(f32[1,64,336]{2,1,0:T(8,128)S(1)} %get-tuple-element.89), channel_id=1, source_target_pairs={{0,2},{1,3},{2,0},{3,1},{4,6},{5,7},{6,4},{7,5},{8,10},{9,11},{10,... | collective-permute-start | bytes 258056 | tf_op jit(solution)/shard_map/ppermute | solution.py:422
  133.1 6.0 %collective-permute-start.25 = (f32[2,72,336]{2,1,0:T(8,128)S(1)}, f32[2,72,336]{2,1,0:T(8,128)S(1)}, u32[]{:S(2)}, u32[]{:S(2)}) collective-permute-start(f32[2,72,336]{2,1,0:T(8,128)S(1)} %pad_maximum_fusion.10), channel_id=1, source_target_pairs={{0,1},{1,0},{2,3},{3,2},{4,5},{5,4},{6,7},{7,6},{8,9},{9,8},{10,11... | collective-permute-start | bytes 580616 | tf_op jit(solution)/shard_map/ppermute | solution.py:422
  133.2 9.3 %collective-permute-start.32 = (f32[1,64,336]{2,1,0:T(8,128)S(1)}, f32[1,64,336]{2,1,0:T(8,128)S(1)}, u32[]{:S(2)}, u32[]{:S(2)}) collective-permute-start(f32[1,64,336]{2,1,0:T(8,128)S(1)} %get-tuple-element.88), channel_id=1, source_target_pairs={{0,16},{4,20},{8,24},{12,28},{16,0},{20,4},{24,8},{28,12},{1,17},{... | collective-permute-start | bytes 258056 | tf_op jit(solution)/shard_map/ppermute | solution.py:422
  135.1 7.9 %collective-permute-start.29 = (f32[2,64,336]{2,1,0:T(8,128)S(1)}, f32[2,64,336]{2,1,0:T(8,128)S(1)}, u32[]{:S(2)}, u32[]{:S(2)}) collective-permute-start(f32[2,64,336]{2,1,0:T(8,128)S(1)} %pad_maximum_fusion.13), channel_id=1, source_target_pairs={{0,8},{4,12},{8,0},{12,4},{16,24},{20,28},{24,16},{28,20},{1,9},{5... | collective-permute-start | bytes 516104 | tf_op jit(solution)/shard_map/ppermute | solution.py:422
  139.1 14.4 %collective-permute-start.26 = (f32[4,72,336]{2,1,0:T(8,128)S(1)}, f32[4,72,336]{2,1,0:T(8,128)S(1)}, u32[]{:S(2)}, u32[]{:S(2)}) collective-permute-start(f32[4,72,336]{2,1,0:T(8,128)S(1)} %pad_maximum_fusion.4), channel_id=1, source_target_pairs={{0,16},{4,20},{8,24},{12,28},{16,0},{20,4},{24,8},{28,12},{1,17},{... | collective-permute-start | bytes 1161224 | tf_op jit(solution)/shard_map/ppermute | solution.py:422
  142.5 10.9 %collective-permute-start.33 = (f32[2,64,336]{2,1,0:T(8,128)S(1)}, f32[2,64,336]{2,1,0:T(8,128)S(1)}, u32[]{:S(2)}, u32[]{:S(2)}) collective-permute-start(f32[2,64,336]{2,1,0:T(8,128)S(1)} %pad_maximum_fusion.14), channel_id=1, source_target_pairs={{0,2},{1,3},{2,0},{3,1},{4,6},{5,7},{6,4},{7,5},{8,10},{9,11},{10,... | collective-permute-start | bytes 516104 | tf_op jit(solution)/shard_map/ppermute | solution.py:422
  143.1 14.2 %collective-permute-start.30 = (f32[4,64,336]{2,1,0:T(8,128)S(1)}, f32[4,64,336]{2,1,0:T(8,128)S(1)}, u32[]{:S(2)}, u32[]{:S(2)}) collective-permute-start(f32[4,64,336]{2,1,0:T(8,128)S(1)} %pad_maximum_fusion.7), channel_id=1, source_target_pairs={{0,1},{1,0},{2,3},{3,2},{4,5},{5,4},{6,7},{7,6},{8,9},{9,8},{10,11... | collective-permute-start | bytes 1032200 | tf_op jit(solution)/shard_map/ppermute | solution.py:422
  153.4 12.1 %collective-permute-start.34 = (f32[4,64,336]{2,1,0:T(8,128)S(1)}, f32[4,64,336]{2,1,0:T(8,128)S(1)}, u32[]{:S(2)}, u32[]{:S(2)}) collective-permute-start(f32[4,64,336]{2,1,0:T(8,128)S(1)} %pad_maximum_fusion.8), channel_id=1, source_target_pairs={{0,8},{4,12},{8,0},{12,4},{16,24},{20,28},{24,16},{28,20},{1,9},{5... | collective-permute-start | bytes 1032200 | tf_op jit(solution)/shard_map/ppermute | solution.py:422
  153.6 29.8 %collective-permute-start.36 = (f32[8,72,336]{2,1,0:T(8,128)S(1)}, f32[8,72,336]{2,1,0:T(8,128)S(1)}, u32[]{:S(2)}, u32[]{:S(2)}) collective-permute-start(f32[8,72,336]{2,1,0:T(8,128)S(1)} %pad_maximum_fusion.refs_0_), channel_id=1, source_target_pairs={{0,8},{4,12},{8,0},{12,4},{16,24},{20,28},{24,16},{28,20},{1,9},{5... | collective-permute-start | bytes 2322440 | tf_op jit(solution)/shard_map/ppermute | solution.py:422
  157.3 26.1 %collective-permute-start.38 = (f32[8,64,336]{2,1,0:T(8,128)S(1)}, f32[8,64,336]{2,1,0:T(8,128)S(1)}, u32[]{:S(2)}, u32[]{:S(2)}) collective-permute-start(f32[8,64,336]{2,1,0:T(8,128)S(1)} %pad_maximum_fusion.1.refs_1_), channel_id=1, source_target_pairs={{0,16},{4,20},{8,24},{12,28},{16,0},{20,4},{24,8},{28,12},{1,17},{... | collective-permute-start | bytes 2064392 | tf_op jit(solution)/shard_map/ppermute | solution.py:422
  158.4 25.5 %collective-permute-start.31 = (f32[8,64,336]{2,1,0:T(8,128)S(1)}, f32[8,64,336]{2,1,0:T(8,128)S(1)}, u32[]{:S(2)}, u32[]{:S(2)}) collective-permute-start(f32[8,64,336]{2,1,0:T(8,128)S(1)} %pad_maximum_fusion.1.refs_1_), channel_id=1, source_target_pairs={{0,4},{4,0},{8,12},{12,8},{16,20},{20,16},{24,28},{28,24},{1,5},{5... | collective-permute-start | bytes 2064392 | tf_op jit(solution)/shard_map/ppermute | solution.py:422
  165.5 18.4 %collective-permute-start.40 = (f32[8,64,336]{2,1,0:T(8,128)S(1)}, f32[8,64,336]{2,1,0:T(8,128)S(1)}, u32[]{:S(2)}, u32[]{:S(2)}) collective-permute-start(f32[8,64,336]{2,1,0:T(8,128)S(1)} %pad_maximum_fusion.2.refs_2_), channel_id=1, source_target_pairs={{0,1},{1,0},{2,3},{3,2},{4,5},{5,4},{6,7},{7,6},{8,9},{9,8},{10,11... | collective-permute-start | bytes 2064392 | tf_op jit(solution)/shard_map/ppermute | solution.py:422
  165.6 22.1 %collective-permute-start.27 = (f32[8,72,336]{2,1,0:T(8,128)S(1)}, f32[8,72,336]{2,1,0:T(8,128)S(1)}, u32[]{:S(2)}, u32[]{:S(2)}) collective-permute-start(f32[8,72,336]{2,1,0:T(8,128)S(1)} %pad_maximum_fusion.refs_0_), channel_id=1, source_target_pairs={{0,4},{4,0},{8,12},{12,8},{16,20},{20,16},{24,28},{28,24},{1,5},{5... | collective-permute-start | bytes 2322440 | tf_op jit(solution)/shard_map/ppermute | solution.py:422
  183.4 5.8 %collective-permute-start.37 = (f32[8,72,336]{2,1,0:T(8,128)S(1)}, f32[8,72,336]{2,1,0:T(8,128)S(1)}, u32[]{:S(2)}, u32[]{:S(2)}) collective-permute-start(f32[8,72,336]{2,1,0:T(8,128)S(1)} %collective-permute-done.36.refs_3_), channel_id=1, source_target_pairs={{0,4},{4,0},{8,12},{12,8},{16,20},{20,16},{24,28},{28,24},{1,5},{5... | collective-permute-start | bytes 2322440 | tf_op jit(solution)/shard_map/ppermute | solution.py:422
  (35 other events, 105.0 us)

commit v2 on v1

v2 whole, which is shorter than its diff:
```python
import functools
import jax
import jax.numpy as jnp
from jax import lax
from jax.experimental import pallas as pl
from jax.experimental.pallas import tpu as pltpu
from jax.sharding import PartitionSpec as P

step_rate = 0.25
F32, BF16 = jnp.float32, jnp.bfloat16
NN = (((1,), (0,)), ((), ()))
NT = (((1,), (1,)), ((), ()))
TN = (((0,), (0,)), ((), ()))
VMEM = pl.BlockSpec(memory_space=pltpu.VMEM)
SMEM = pl.BlockSpec(memory_space=pltpu.SMEM)
PARAMS = pltpu.CompilerParams(vmem_limit_bytes=24 * 1024 * 1024)
COST = pl.CostEstimate(flops=10000, bytes_accessed=10000, transcendentals=0)


def split(x):
    hi = x.astype(BF16)
    return hi, (x - hi.astype(F32)).astype(BF16)


def dot(a, b, dims):
    return lax.dot_general(a, b, dims, preferred_element_type=F32)


def dot3(a, b, dims):
    return dot(a[0], b[0], dims) + (dot(a[0], b[1], dims) + dot(a[1], b[0], dims))


def dot2(a, onehot, dims):
    return dot(a[0], onehot, dims) + dot(a[1], onehot, dims)


def onehot(first, rows, idx):
    place = lax.broadcasted_iota(jnp.int32, (rows, idx.shape[1]), 0) + first
    return jnp.where(place == idx, 1.0, 0.0).astype(BF16)


def laid_out(idx):
    return jnp.concatenate([idx[b : b + 1] for b in range(idx.shape[0])], axis=1)


def add_part(first, part, out_ref):
    @pl.when(first)
    def _():
        out_ref[...] = part

    @pl.when(jnp.logical_not(first))
    def _():
        out_ref[...] += part


def gather_kernel(hub_steps, hub_idx, rel_idx, hub_ref, rel_ref, hub_out, rel_out):
    step = pl.program_id(0)

    @pl.when(step < hub_steps)
    def _():
        tile = hub_ref.shape[1]
        hot = onehot(step * tile, tile, laid_out(hub_idx[...]))
        add_part(step == 0, dot2(split(hub_ref[...]), hot, NN), hub_out)

    @pl.when(step >= hub_steps)
    def _():
        tile = rel_ref.shape[1]
        hot = onehot((step - hub_steps) * tile, tile, laid_out(rel_idx[...]))
        add_part(step == hub_steps, dot2(split(rel_ref[...]), hot, NN), rel_out)


def gather_rows(hub_table, hub_idx, rel_table, rel_idx):
    features = hub_table.shape[0]
    hub_steps, rel_steps = 4, 2
    fixed = lambda shape: pl.BlockSpec(shape, lambda k: (0, 0))
    shapes = [(features, hub_idx.size), (features, rel_idx.size)]
    return pl.pallas_call(
        functools.partial(gather_kernel, hub_steps),
        grid=(hub_steps + rel_steps,),
        in_specs=[
            fixed(hub_idx.shape),
            fixed(rel_idx.shape),
            pl.BlockSpec((features, hub_table.shape[1] // hub_steps), lambda k: (0, jnp.minimum(k, hub_steps - 1))),
            pl.BlockSpec((features, rel_table.shape[1] // rel_steps), lambda k: (0, jnp.maximum(k - hub_steps, 0))),
        ],
        out_specs=[fixed(shape) for shape in shapes],
        out_shape=[jax.ShapeDtypeStruct(shape, F32) for shape in shapes],
        compiler_params=PARAMS,
        cost_estimate=COST,
    )(hub_idx, rel_idx, hub_table, rel_table)


def spread_bits(place, order):
    bits = len(order)
    return sum((((place >> p) & 1) << (bits - 1 - i)) for i, p in enumerate(order))


def load_columns(idx_refs, grad_refs, idx_down, hi_all, lo_all):
    idx = jnp.concatenate([laid_out(ref[...]) for ref in idx_refs], axis=1)
    idx_down[...] = jnp.transpose(jnp.broadcast_to(idx, (128, idx.shape[1])))
    at = 0
    for ref in grad_refs:
        width = ref.shape[1]
        hi_all[:, at : at + width], lo_all[:, at : at + width] = split(ref[...])
        at += width


def onehot_across(idx_down, targets):
    width = targets.shape[1]
    idx = idx_down[...]
    wide = jnp.concatenate([idx] * -(-width // 128), axis=1)[:, :width]
    return jnp.where(wide == targets, 1.0, 0.0).astype(BF16)


def out_for(place, order, sends, keeps, s):
    index = spread_bits(place, order)
    half = keeps[s].shape[0]
    return sends[s].at[index - half] if index >= half else keeps[s].at[index]


def hub_chunks_kernel(orders, spans, grads, chip_ref, *refs):
    idx_refs, grad_refs, refs = refs[:2], refs[2 : 2 + grads], refs[2 + grads :]
    streams = len(orders)
    sends, keeps = refs[:streams], refs[streams : 2 * streams]
    idx_down, hi_all, lo_all = refs[2 * streams :]
    load_columns(idx_refs, grad_refs, idx_down, hi_all, lo_all)
    chunks, width = 2 * keeps[0].shape[0], keeps[0].shape[2]
    lane = lax.broadcasted_iota(jnp.int32, (1, width), 1)
    for place in range(chunks):
        hot = onehot_across(idx_down, lane + (chip_ref[0] ^ place) * width)
        chunk = dot2((hi_all[...], lo_all[...]), hot, NN)
        for s, (low, high) in enumerate(spans):
            out_for(place, orders[s], sends, keeps, s)[...] = chunk[low:high]


def third_of(spans):
    return -(-max(high - low for low, high in spans) // 24) * 8


def packed_pieces(spans):
    third = third_of(spans)
    for block, (low, high) in enumerate(spans):
        for s in range(len(spans)):
            count = min(third, high - low - third * s)
            if count > 0:
                yield block, s, low + third * s, count


def rel_chunks_kernel(orders, spans, rows, grads, chip_ref, *refs):
    idx_refs, grad_refs, refs = refs[:2], refs[2 : 2 + grads], refs[2 + grads :]
    streams = len(orders)
    sends, keeps = refs[:streams], refs[streams : 2 * streams]
    idx_down, hi_all, lo_all = refs[2 * streams :]
    load_columns(idx_refs, grad_refs, idx_down, hi_all, lo_all)
    for ref in refs[: 2 * streams]:
        ref[...] = jnp.zeros_like(ref)
    chunks, lanes = 2 * keeps[0].shape[0], keeps[0].shape[2]
    width = rows // chunks
    group = lanes // width
    lane = lax.broadcasted_iota(jnp.int32, (1, lanes), 1)
    for first in range(0, chunks, group):
        targets = jnp.full((1, lanes), -1, jnp.int32)
        places = range(first, min(first + group, chunks))
        for slot, place in enumerate(places):
            here = (lane >= slot * width) & (lane < (slot + 1) * width)
            targets = jnp.where(here, lane + ((chip_ref[0] ^ place) * width - slot * width), targets)
        dense = dot2((hi_all[...], lo_all[...]), onehot_across(idx_down, targets), NN)
        for slot, place in enumerate(places):
            chunk = dense[:, slot * width : (slot + 1) * width]
            for block, s, low, count in packed_pieces(spans):
                out = out_for(place, orders[s], sends, keeps, s)
                out[:count, block * width : (block + 1) * width] = chunk[low : low + count]


def chunk_columns(kernel, heights, lanes, chip, idx, grads, chunks):
    half_width = grads[0].shape[0]
    count = sum(g.shape[1] for g in grads)
    shapes = [jax.ShapeDtypeStruct((chunks // 2, height, lanes), F32) for height in heights] * 2
    out = pl.pallas_call(
        kernel,
        in_specs=[SMEM] + [VMEM] * (2 + len(grads)),
        out_specs=[VMEM] * len(shapes),
        out_shape=shapes,
        scratch_shapes=[
            pltpu.VMEM((count, 128), jnp.int32),
            pltpu.VMEM((half_width, count), BF16),
            pltpu.VMEM((half_width, count), BF16),
        ],
        compiler_params=PARAMS,
        cost_estimate=COST,
    )(chip, *idx, *grads)
    return out[: len(heights)], out[len(heights) :]


def call(kernel, ins, shapes):
    return pl.pallas_call(
        kernel,
        in_specs=[VMEM] * len(ins),
        out_specs=[VMEM] * len(shapes),
        out_shape=[jax.ShapeDtypeStruct(shape, F32) for shape in shapes],
        compiler_params=PARAMS,
        cost_estimate=COST,
    )(*ins)


def first_sums_kernel(*refs):
    streams = len(refs) // 6
    hub_own, hub_got, rel_own, rel_got, sends, keeps = [refs[i * streams : (i + 1) * streams] for i in range(6)]
    for s in range(streams):
        half, height = sends[s].shape[0], hub_own[s].shape[1]
        for out, part in ((sends[s], pl.ds(half, half)), (keeps[s], pl.ds(0, half))):
            out[:, :height] = hub_own[s][part] + hub_got[s][part]
            out[:, height:] = rel_own[s][part] + rel_got[s][part]


def sums_kernel(*refs):
    streams = len(refs) // 4
    own, got, sends, keeps = [refs[i * streams : (i + 1) * streams] for i in range(4)]
    for s in range(streams):
        half = sends[s].shape[0]
        sends[s][...] = own[s][half:] + got[s][half:]
        keeps[s][...] = own[s][:half] + got[s][:half]


def halves(kernel, groups, shapes):
    shapes = [(shape[0] // 2,) + shape[1:] for shape in shapes]
    out = call(kernel, [x for group in groups for x in group], shapes * 2)
    return out[: len(shapes)], out[len(shapes) :]


def join_kernel(*refs):
    streams = len(refs) // 3
    for s in range(streams):
        own, got, out = refs[s], refs[streams + s], refs[2 * streams + s]
        count = own.shape[0]
        out[:count] = own[...]
        out[count:] = got[...]


def join(own, got):
    return call(join_kernel, [*own, *got], [(2 * x.shape[0],) + x.shape[1:] for x in own])


def squares_kernel(spans, width, *refs):
    streams = len(spans)
    own, got, totals, out = [refs[i * streams : (i + 1) * streams] for i in range(3)] + [refs[-1]]
    lanes = out.shape[1]
    hub, rel = jnp.zeros((1, lanes), F32), jnp.zeros((1, lanes), F32)
    for s, (low, high) in enumerate(spans):
        total = own[s][0] + got[s][0]
        totals[s][0] = total
        square = total * total
        hub += jnp.sum(square[: high - low], axis=0, keepdims=True)
        rel += jnp.sum(square[high - low :], axis=0, keepdims=True)
    out[...] = jnp.zeros_like(out)
    out[0:1] = hub
    out[1:2, :width] = sum(rel[:, b * width : (b + 1) * width] for b in range(streams))


def update_kernel(spans, width, features, *refs):
    streams = len(spans)
    totals, news = refs[:streams], refs[-streams:]
    mine, other, hub_ref, rel_ref, hub_sums, rel_sums = refs[streams:-streams]
    means = (mine[...] + other[...]) * (1.0 / features)
    hub_scale = step_rate / jnp.sqrt(hub_sums[...] + means[0:1])
    rel_scale = step_rate / jnp.sqrt(rel_sums[...] + means[1:2, :width])
    for s, (low, high) in enumerate(spans):
        height = high - low
        news[s][0, :height] = hub_ref[low:high] - totals[s][0, :height] * hub_scale
        news[s][0, height:] = jnp.zeros_like(news[s][0, height:])
    for block, s, low, count in packed_pieces(spans):
        at = spans[s][1] - spans[s][0]
        lanes = slice(block * width, (block + 1) * width)
        news[s][0, at : at + count, lanes] = (
            rel_ref[low : low + count] - totals[s][0, at : at + count, lanes] * rel_scale
        )


def place_kernel(orders, spans, spot_ref, *refs):
    streams = len(orders)
    lows, highs = refs[:streams], refs[streams : 2 * streams]
    hub_ref, rel_ref = refs[-2:]
    half = lows[0].shape[0]
    width, rel_width = hub_ref.shape[2] // (2 * half), rel_ref.shape[2] // (2 * half)
    pieces = list(packed_pieces(spans))
    for chunk in range(2 * half):
        place = spot_ref[0] ^ chunk
        for s, (low, high) in enumerate(spans):
            index = spread_bits(place, orders[s])
            spot = index & (half - 1)
            value = jnp.where(index >= half, highs[s][spot], lows[s][spot])
            height = high - low
            hub_ref[0, low:high, chunk * width : (chunk + 1) * width] = value[:height]
            for block, stream, row, count in pieces:
                if stream == s:
                    part = value[height : height + count, block * rel_width : (block + 1) * rel_width]
                    rel_ref[0, row : row + count, chunk * rel_width : (chunk + 1) * rel_width] = part


def place_chunks(spot, near, far, orders, spans, hub_shape, rel_shape, earlier):
    whole = [pl.BlockSpec(memory_space=pltpu.VMEM)] * (2 * len(spans))
    kept = [pl.BlockSpec(memory_space=pl.ANY)] * len(earlier)
    mine = lambda shape: pl.BlockSpec((1,) + shape[1:], lambda i, spot: (spot[1], 0, 0))
    return pl.pallas_call(
        functools.partial(place_kernel, orders, spans),
        grid_spec=pltpu.PrefetchScalarGridSpec(
            num_scalar_prefetch=1,
            grid=(1,),
            in_specs=whole + kept,
            out_specs=[mine(hub_shape), mine(rel_shape)],
        ),
        out_shape=[jax.ShapeDtypeStruct(hub_shape, F32), jax.ShapeDtypeStruct(rel_shape, F32)],
        input_output_aliases={1 + len(whole) + i: i for i in range(len(earlier))},
        compiler_params=PARAMS,
        cost_estimate=COST,
    )(spot, *near, *far, *earlier)


def adagrad(table, state, grads):
    new_state = state + jnp.sum(grads * grads, axis=0, keepdims=True) * (1.0 / grads.shape[0])
    return table - grads * (step_rate / jnp.sqrt(new_state)), new_state


def keep_and_send(core, first, second):
    return jnp.where(core == 0, first, second), jnp.where(core == 0, second, first)


def table_counts(rows, negs, weight):
    place = lax.broadcasted_iota(jnp.int32, (rows, negs.shape[1]), 0)
    return jnp.sum(jnp.where(place == negs, weight, 0.0), axis=1, keepdims=True)


def turned(x, r, half):
    x0, x1, r0, r1 = x[:half], x[half:], r[:half], r[half:]
    return jnp.concatenate([x0 * r0 - x1 * r1, x0 * r1 + x1 * r0], axis=0)


def turned_back(x, r, half):
    x0, x1, r0, r1 = x[:half], x[half:], r[:half], r[half:]
    return x0 * r0 + x1 * r1, x1 * r0 - x0 * r1


EDGE_TILE = 256


def edge_spans(step, bucket, edges):
    tile = EDGE_TILE
    here = pl.multiple_of(step * tile, tile)
    return pl.ds(here, tile), pl.ds(pl.multiple_of(bucket * edges + here, tile), tile)


def lay_down(idx, out_ref):
    out_ref[...] = jnp.transpose(jnp.broadcast_to(idx, (128, idx.shape[1])))


def head_hot_down(heads_down, span, rows):
    return onehot_across(heads_down.at[span], lax.broadcasted_iota(jnp.int32, (1, rows), 1))


def bucket_kernel(
    bucket, core_ref, heads_ref, tails_ref, negs_ref, left_ref, left_sums_ref, right_ref, right_sums_ref, rel_ref, hub_ref,
    left_out, left_sums_out, right_out, right_sums_out, rel_keep, rel_send, hub_keep, hub_send,
    left_hi, left_lo, both_hi, both_lo, down_hi, down_lo, left_grad, both_grad, heads_down,
):
    features, rows = left_ref.shape
    half = features // 2
    core = core_ref[0]
    edges, hubs = heads_ref.shape[1], hub_keep.shape[1]
    at = slice(bucket, bucket + 1)
    hub_rows = hub_ref[:, bucket * hubs : (bucket + 1) * hubs]
    weight = 1.0 / (negs_ref.shape[1] + hubs)
    counts = table_counts(rows, negs_ref[at], weight)
    lay_down(heads_ref[at], heads_down)
    left_hi[...], left_lo[...] = split(left_ref[...])
    both_hi[:, :rows], both_lo[:, :rows] = split(right_ref[...])
    both_hi[:, rows:], both_lo[:, rows:] = split(hub_rows)
    down_hi[:rows], down_lo[:rows] = split(jnp.transpose(right_ref[...]))
    down_hi[rows:], down_lo[rows:] = split(jnp.transpose(hub_rows))
    left_grad[...] = jnp.zeros_like(left_grad)
    both_grad[...] = jnp.zeros_like(both_grad)

    @pl.loop(0, edges // EDGE_TILE)
    def _(step):
        span, wide_span = edge_spans(step, bucket, edges)
        tail_here = lax.broadcasted_iota(jnp.int32, (rows, EDGE_TILE), 0) == tails_ref[at, span]
        h = dot2((left_hi[...], left_lo[...]), onehot(0, rows, heads_ref[at, span]), NN)
        r = rel_ref[:, wide_span]
        q = split(turned(h, r, half))
        scores = dot3((down_hi[...], down_lo[...]), q, NN)
        chance = jax.nn.sigmoid(scores[:rows])
        coef = jnp.concatenate(
            [
                counts * chance + jnp.where(tail_here, chance - 1.0, 0.0),
                weight * jax.nn.sigmoid(scores[rows:]),
            ],
            axis=0,
        )
        coef = split(coef)
        dq = dot3((both_hi[...], both_lo[...]), coef, NN)
        both_grad[...] += dot3(q, coef, NT)
        dh = jnp.concatenate(turned_back(dq, r, half), axis=0)
        left_grad[...] += dot2(split(dh), head_hot_down(heads_down, span, rows), NN)
        rel_keep[:, span], rel_send[:, span] = keep_and_send(core, *turned_back(dq, h, half))

    left_out[...], left_sums_out[...] = adagrad(left_ref[...], left_sums_ref[...], left_grad[...])
    right_out[...], right_sums_out[...] = adagrad(right_ref[...], right_sums_ref[...], both_grad[:, :rows])
    hub_keep[...], hub_send[...] = keep_and_send(core, both_grad[:half, rows:], both_grad[half:, rows:])


def bucket_step(bucket, core, heads, tails, negs, left, left_sums, right, right_sums, rel_rows, hub_rows):
    features, rows = left.shape
    edges, hubs = heads.shape[1], hub_rows.shape[1] // heads.shape[0]
    width = rows + hubs
    shapes = [(features, rows), (1, rows)] * 2 + [(features // 2, edges)] * 2 + [(features // 2, hubs)] * 2
    return pl.pallas_call(
        functools.partial(bucket_kernel, bucket),
        in_specs=[SMEM] + [VMEM] * 9,
        out_specs=[VMEM] * 8,
        out_shape=[jax.ShapeDtypeStruct(shape, F32) for shape in shapes],
        scratch_shapes=[pltpu.VMEM((features, rows), BF16)] * 2
        + [pltpu.VMEM((features, width), BF16)] * 2
        + [pltpu.VMEM((width, features), BF16)] * 2
        + [
            pltpu.VMEM((features, rows), F32),
            pltpu.VMEM((features, width), F32),
            pltpu.VMEM((edges, 128), jnp.int32),
        ],
        compiler_params=PARAMS,
        cost_estimate=COST,
    )(core, heads, tails, negs, left, left_sums, right, right_sums, rel_rows, hub_rows)


def hub_kernel(
    bucket, negatives, core_ref, heads_ref, left_ref, rel_ref, hub_ref,
    head_out, query_grad, hub_keep, hub_send,
    left_hi, left_lo, hub_hi, hub_lo, down_hi, down_lo, hub_grad,
):
    features, rows = left_ref.shape
    half = features // 2
    edges, hubs = heads_ref.shape[1], hub_keep.shape[1]
    at = slice(bucket, bucket + 1)
    hub_rows = hub_ref[:, bucket * hubs : (bucket + 1) * hubs]
    weight = 1.0 / (negatives + hubs)
    left_hi[...], left_lo[...] = split(left_ref[...])
    hub_hi[...], hub_lo[...] = split(hub_rows)
    down_hi[...], down_lo[...] = split(jnp.transpose(hub_rows))
    hub_grad[...] = jnp.zeros_like(hub_grad)

    @pl.loop(0, edges // EDGE_TILE)
    def _(step):
        span, wide_span = edge_spans(step, bucket, edges)
        h = dot2((left_hi[...], left_lo[...]), onehot(0, rows, heads_ref[at, span]), NN)
        head_out[:, span] = h
        q = split(turned(h, rel_ref[:, wide_span], half))
        coef = split(weight * jax.nn.sigmoid(dot3((down_hi[...], down_lo[...]), q, NN)))
        query_grad[:, span] = dot3((hub_hi[...], hub_lo[...]), coef, NN)
        hub_grad[...] += dot3(q, coef, NT)

    hub_keep[...], hub_send[...] = keep_and_send(core_ref[0], hub_grad[:half], hub_grad[half:])


def hub_step(bucket, negatives, core, heads, left, rel_rows, hub_rows):
    features, rows = left.shape
    edges, hubs = heads.shape[1], hub_rows.shape[1] // heads.shape[0]
    shapes = [(features, edges)] * 2 + [(features // 2, hubs)] * 2
    return pl.pallas_call(
        functools.partial(hub_kernel, bucket, negatives),
        in_specs=[SMEM] + [VMEM] * 4,
        out_specs=[VMEM] * 4,
        out_shape=[jax.ShapeDtypeStruct(shape, F32) for shape in shapes],
        scratch_shapes=[pltpu.VMEM((features, rows), BF16)] * 2
        + [pltpu.VMEM((features, hubs), BF16)] * 2
        + [pltpu.VMEM((hubs, features), BF16)] * 2
        + [pltpu.VMEM((features, hubs), F32)],
        compiler_params=PARAMS,
        cost_estimate=COST,
    )(core, heads, left, rel_rows, hub_rows)


def tables_kernel(
    bucket, hubs, core_ref, heads_ref, tails_ref, negs_ref, head_rows, query_grad,
    left_ref, left_sums_ref, right_ref, right_sums_ref, rel_ref,
    left_out, right_out, rel_keep, rel_send,
    right_hi, right_lo, down_hi, down_lo, left_grad, right_grad, heads_down,
):
    features, rows = left_ref.shape
    half = features // 2
    edges = heads_ref.shape[1]
    at = slice(bucket, bucket + 1)
    core = core_ref[0]
    counts = table_counts(rows, negs_ref[at], 1.0 / (negs_ref.shape[1] + hubs))
    lay_down(heads_ref[at], heads_down)
    right_hi[...], right_lo[...] = split(right_ref[...])
    down_hi[...], down_lo[...] = split(jnp.transpose(right_ref[...]))
    left_grad[...] = jnp.zeros_like(left_grad)
    right_grad[...] = jnp.zeros_like(right_grad)

    @pl.loop(0, edges // EDGE_TILE)
    def _(step):
        span, wide_span = edge_spans(step, bucket, edges)
        tail_here = lax.broadcasted_iota(jnp.int32, (rows, EDGE_TILE), 0) == tails_ref[at, span]
        h, r = head_rows[:, span], rel_ref[:, wide_span]
        q = split(turned(h, r, half))
        chance = jax.nn.sigmoid(dot3((down_hi[...], down_lo[...]), q, NN))
        coef = split(counts * chance + jnp.where(tail_here, chance - 1.0, 0.0))
        dq = dot3((right_hi[...], right_lo[...]), coef, NN) + query_grad[:, span]
        right_grad[...] += dot3(q, coef, NT)
        rel_keep[:, span], rel_send[:, span] = keep_and_send(core, *turned_back(dq, h, half))
        dh = jnp.concatenate(turned_back(dq, r, half), axis=0)
        left_grad[...] += dot2(split(dh), head_hot_down(heads_down, span, rows), NN)

    left_out[...], unused = adagrad(left_ref[...], left_sums_ref[...], left_grad[...])
    right_out[...], unused = adagrad(right_ref[...], right_sums_ref[...], right_grad[...])


def tables_step(bucket, hubs, core, heads, tails, negs, head_rows, query_grad, left, left_sums, right, right_sums, rel_rows):
    features, rows = left.shape
    edges = heads.shape[1]
    shapes = [(features, rows)] * 2 + [(features // 2, edges)] * 2
    return pl.pallas_call(
        functools.partial(tables_kernel, bucket, hubs),
        in_specs=[SMEM] + [VMEM] * 10,
        out_specs=[VMEM] * 4,
        out_shape=[jax.ShapeDtypeStruct(shape, F32) for shape in shapes],
        scratch_shapes=[pltpu.VMEM((features, rows), BF16)] * 2
        + [pltpu.VMEM((rows, features), BF16)] * 2
        + [pltpu.VMEM((features, rows), F32)] * 2
        + [pltpu.VMEM((edges, 128), jnp.int32)],
        compiler_params=PARAMS,
        cost_estimate=COST,
    )(core, heads, tails, negs, head_rows, query_grad, left, left_sums, right, right_sums, rel_rows)


def from_behind(x, axis, by):
    size = lax.axis_size(axis)
    return lax.ppermute(x, axis, [(i, (i + by) % size) for i in range(size)])


def flipped(x, axis, bit):
    return lax.ppermute(x, axis, [(i, i ^ (1 << bit)) for i in range(lax.axis_size(axis))])


def other_core(x):
    return flipped(x, "blk", 0)


def across(x, place):
    sub_bits = lax.axis_size("sub").bit_length() - 1
    if place < sub_bits:
        return flipped(x, "sub", place)
    return flipped(x, "blk", place - sub_bits + 1)


def stream_orders():
    sub_bits = lax.axis_size("sub").bit_length() - 1
    bits = sub_bits + lax.axis_size("blk").bit_length() - 2
    x, y, z, far = sub_bits, sub_bits + 1, 0, 1
    rest = [p for p in range(bits) if p not in (x, y, z, far)]
    return [[x, y, z, far] + rest, [y, z, x, far] + rest, [z, x, far, y] + rest]


def row_spans(rows, parts):
    ends = [-(-rows * (i + 1) // (8 * parts)) * 8 for i in range(parts - 1)] + [rows]
    return list(zip([0] + ends[:-1], ends))


def shards(
    left_emb, left_state, right_emb, right_state, relation_emb, relation_state, hub_emb, hub_state,
    heads, relations, tails, negatives, hub_ids,
):
    components, half_width, row_count = left_emb.shape
    features = components * half_width
    rel_count, hub_count = relation_emb.shape[2], hub_emb.shape[2]
    left = left_emb.reshape(features, row_count)
    right = right_emb.reshape(features, row_count)
    left_sums = left_state.reshape(1, row_count)
    right_sums = right_state.reshape(1, row_count)
    buckets, hubs = heads.shape[0], hub_ids.shape[1]

    core_id = lax.axis_index("blk") % 2
    chip_id = (lax.axis_index("blk") // 2) * lax.axis_size("sub") + lax.axis_index("sub")
    core, chip = core_id.astype(jnp.int32).reshape(1), chip_id.astype(jnp.int32).reshape(1)
    orders = stream_orders()
    spans = row_spans(half_width, len(orders))
    heights = [high - low for low, high in spans]
    third = third_of(spans)
    chunks = 1 << len(orders[0])
    width, rel_width = hub_count // chunks, rel_count // chunks

    def exchanged(parts, step):
        return [across(x, order[step]) for x, order in zip(parts, orders)]

    far_rel, far_hub = other_core((relations, hub_ids))
    hub_rows, rel_rows = gather_rows(
        hub_emb.reshape(features, hub_count), hub_ids, relation_emb.reshape(features, rel_count), relations
    )
    rel_keep, rel_far, hub_keep, hub_far = [], [], [], []
    for b in range(buckets - 1):
        left, left_sums, right, right_sums, rk, rs, hk, hs = bucket_step(
            b, core, heads, tails, negatives, left, left_sums, right, right_sums, rel_rows, hub_rows
        )
        right, right_sums = from_behind((right, right_sums), "blk", 1)
        hub_far.append(other_core(hs))
        rel_far.append(other_core(rs))
        hub_keep.append(hk)
        rel_keep.append(rk)
    last = buckets - 1
    head_rows, query_grad, hk, hs = hub_step(last, negatives.shape[1], core, heads, left, rel_rows, hub_rows)
    hub_grads = hub_keep + [hk] + hub_far + [other_core(hs)]
    hub_send, hub_own = chunk_columns(
        functools.partial(hub_chunks_kernel, orders, spans, len(hub_grads)),
        heights, width, chip, (hub_ids, far_hub), hub_grads, chunks,
    )
    hub_got = exchanged(hub_send, 0)
    left, right, rk, rs = tables_step(
        last, hubs, core, heads, tails, negatives, head_rows, query_grad, left, left_sums, right, right_sums, rel_rows
    )
    rel_grads = rel_keep + [rk] + rel_far + [other_core(rs)]
    rel_send, rel_own = chunk_columns(
        functools.partial(rel_chunks_kernel, orders, spans, rel_count, len(rel_grads)),
        [third] * len(spans), width, chip, (relations, far_rel), rel_grads, chunks,
    )
    rel_got = exchanged(rel_send, 0)

    send, own = halves(
        first_sums_kernel,
        (hub_own, hub_got, rel_own, rel_got),
        [(chunks // 2, height + third, width) for height in heights],
    )
    for step in range(1, len(orders[0]) - 1):
        got = exchanged(send, step)
        send, own = halves(sums_kernel, (own, got), [x.shape for x in own])
    late, send = lax.optimization_barrier((jnp.stack([core_id, chip_id]), send))
    got = exchanged(send, -1)
    *totals, squares = call(
        functools.partial(squares_kernel, spans, rel_width), [*own, *got], [x.shape for x in own] + [(2, width)]
    )
    far_squares = other_core(squares)
    cut = lambda x, span: lax.dynamic_slice(x, (late[0], 0, late[1] * span), (1, half_width, span))[0]
    cut_sums = lambda x, span: lax.dynamic_slice(x[None], (0, late[1] * span), (1, span))
    have = call(
        functools.partial(update_kernel, spans, rel_width, features),
        [
            *totals, squares, far_squares, cut(hub_emb, width), cut(relation_emb, rel_width),
            cut_sums(hub_state, width), cut_sums(relation_state, rel_width),
        ],
        [x.shape for x in totals],
    )
    for step in range(len(orders[0]) - 1, 0, -1):
        have = join(have, exchanged(have, step))
    far = exchanged(have, 0)
    shapes = (hub_emb.shape, relation_emb.shape)
    out = place_chunks(jnp.concatenate([chip, core]), have, far, orders, spans, *shapes, ())
    out = place_chunks(
        jnp.concatenate([chip, 1 - core]), other_core(have), other_core(far), orders, spans, *shapes, tuple(out)
    )
    return (
        left.reshape(components, half_width, row_count),
        right.reshape(components, half_width, row_count),
        out[1],
        out[0],
    )


def solution(mesh):
    both = ("blk", "sub")
    block, table, whole = P(None, None, both), P(None, both), P()
    return jax.shard_map(
        shards,
        mesh=mesh,
        in_specs=(block, P(both), block, P(both), whole, whole, whole, whole, table, table, table, table, table),
        out_specs=(block, block, whole, whole),
        check_vma=False,
    )
```

time: 193 us -> 177 us (0.917)
  Pallas kernels: 56 us -> 45.9 us
  local copies, waits for them, and re-layouts: 19 us -> 15 us
  between operations: 1.12 us -> 4.18 us
  starting transfers between devices: 37.7 us -> 34.8 us
  other arithmetic: 2.43 us -> 0.22 us
    pallas_call x8 -> x14, Pallas kernels: 49.7 us -> 39.6 us  [the longest x1 9.66 us: bucket_step(): pl.pallas_call(functools.partial(bucket_kernel, bucket), in_specs=[SMEM]...]
    ppermute x2, waiting for transfers between devices: 0.01 us -> 3.69 us  [from_behind(): return lax.ppermute(x, axis, [(i, (i + by) % size) for i in range(size)])]
    ppermute x40, waiting for transfers between devices: 76.1 us -> 73 us  [flipped(): lax.ppermute(x, axis, [(i, i ^ 1 << bit) for i in range(lax.axis_size(axi...]
    ppermute x40, starting transfers between devices: 37.2 us -> 34.3 us  [flipped(): lax.ppermute(x, axis, [(i, i ^ 1 << bit) for i in range(lax.axis_size(axi...]
    unnamed x52 -> x42, local copies, waits for them, and re-layouts: 13.9 us -> 11.6 us
  transfers between devices with their start and end apart: 42 -> 42, of which waited for: 20 -> 19; matrix products, arithmetic and copies ran while one was open for 3% -> 2% of each run, Pallas kernels for 19% -> 13%
where the time goes in v2:
time: 177 us
  waiting for transfers between devices  76.7 us (43%)
  Pallas kernels  45.9 us (26%)
  starting transfers between devices  34.8 us (20%)
  local copies, waits for them, and re-layouts  15 us (8%)
  between operations  4.18 us (2%)
    ppermute x40, waiting for transfers between devices, flipped(): lax.ppermute(x, axis, [(i, i ^ 1 << bit) for i in range(lax.axis_size(axi...  73 us
    ppermute x40, starting transfers between devices, flipped(): lax.ppermute(x, axis, [(i, i ^ 1 << bit) for i in range(lax.axis_size(axi...  34.3 us
    unnamed x42, local copies, waits for them, and re-layouts  11.6 us
    pallas_call x1, Pallas kernels, bucket_step(): pl.pallas_call(functools.partial(bucket_kernel, bucket), in_specs=[SMEM]...  9.66 us
    pallas_call x1, Pallas kernels, gather_rows(): pl.pallas_call(functools.partial(gather_kernel, hub_steps), grid=(hub_ste...  9.2 us
    pallas_call x2, Pallas kernels, chunk_columns(): pl.pallas_call(kernel, in_specs=[SMEM] + [VMEM] * (2 + len(grads)), out_s...  8.23 us
    pallas_call x1, Pallas kernels, tables_step(): pl.pallas_call(functools.partial(tables_kernel, bucket, hubs), in_specs=[...  7.2 us
    pallas_call x2, Pallas kernels, place_chunks(): pl.pallas_call(functools.partial(place_kernel, orders, spans), grid_spec=...  6.3 us
  transfers between devices with their start and end apart: 42, of which 19 were waited for; matrix products, arithmetic and copies ran while one was open for 2% of the time, Pallas kernels for 13%

profile of v2, /device:TPU:0, one launch (start us, length us, event | category | flops | bytes accessed | tf_op | source)
XLA Modules:
  0.0 176.8 jit_solution(4903705754742553581)
XLA Ops:
  0.7 2.9 %copy-done.1 = f32[2,200,4096]{2,1,0:T(8,128)S(1)} copy-done((f32[2,200,4096]{2,1,0:T(8,128)S(1)}, f32[2,200,4096]{2,1,0:T(8,128)}, u32[]{:S(2)}) %copy-start.1) | copy-done | bytes 6553624
  3.5 1.6 copy-done.2
  5.8 9.2 %shard_map.156 = (f32[400,512]{1,0:T(8,128)S(1)}, f32[400,1024]{1,0:T(8,128)S(1)}) custom-call(s32[2,256]{1,0:T(2,128)} %refs_0_.2, s32[2,512]{1,0:T(2,128)S(1)} %copy-done.15, f32[400,4096]{1,0:T(8,128)S(1)} %bitcast.20, f32[400,1280]{1,0:T(8,128)S(1)} %bitcast.21), custom_call_target="tpu_custom_call" | custom-call | flops 10000 | bytes 10000 | tf_op jit(solution)/shard_map/pallas_call | solution.py:77
  15.1 9.7 %shard_map.157 = (f32[400,512]{1,0:T(8,128)S(1)}, f32[1,512]{1,0:T(1,128)S(1)}, f32[400,512]{1,0:T(8,128)}, f32[1,512]{1,0:T(1,128)S(1)}, f32[200,512]{1,0:T(8,1...) custom-call(s32[1]{0:T(128)} %bitcast.core_ref, s32[2,512]{1,0:T(2,128)S(1)} %copy-done.13, ...), custom_call_target="tpu_custom_call" | custom-call | flops 10000 | bytes 10000 | tf_op jit(solution)/shard_map/pallas_call | solution.py:415
  26.0 2.6 %collective-permute-start.3 = (f32[200,256]{1,0:T(8,128)}, f32[200,256]{1,0:T(8,128)}, u32[]{:S(2)}, u32[]{:S(2)}) collective-permute-start(f32[200,256]{1,0:T(8,128)} %get-tuple-element.88), channel_id=1, source_target_pairs={{0,4},{4,0},{8,12},{12,8},{16,20},{20,16},{24,28},{28,24},{1,5},{5... | collective-permute-start | bytes 614408 | tf_op jit(solution)/shard_map/ppermute | solution.py:540
  28.6 4.3 %shard_map.158 = (f32[400,512]{1,0:T(8,128)S(1)}, f32[400,512]{1,0:T(8,128)S(1)}, f32[200,256]{1,0:T(8,128)S(1)}, f32[200,256]{1,0:T(8,128)}) custom-call(s32[1]{0:T(128)} %bitcast.core_ref, s32[2,512]{1,0:T(2,128)S(1)} %copy-done.13, f32[400,512]{1,0:T(8,128)S(1)} %get-tuple-element.78.left_ref, f32[400,1024]{1,0:T(8,128)S(1)} %get-tuple-element.76.rel_ref, ...), custom_call_target="tpu_custom_call" | custom-call | flops 10000 | bytes 10000 | tf_op jit(solution)/shard_map/pallas_call | solution.py:466
  38.1 5.0 %shard_map.160 = (f32[8,72,256]{2,1,0:T(8,128)S(1)}, f32[8,64,256]{2,1,0:T(8,128)S(1)}, f32[8,64,256]{2,1,0:T(8,128)S(1)}, f32[8,72,256]{2,1,0:T(8,128)S(1)}, f3...) custom-call(s32[1]{0:T(128)} %bitcast.9.chip_ref, s32[2,256]{1,0:T(2,128)} %refs_0_.2, ...), custom_call_target="tpu_custom_call" | custom-call | flops 10000 | bytes 10000 | tf_op jit(solution)/shard_map/pallas_call | solution.py:179
  43.1 1.6 collective-permute-start.6
  45.0 3.7 %collective-permute-done.1.right_sums_ref = f32[1,512]{1,0:T(1,128)S(1)} collective-permute-done((f32[1,512]{1,0:T(1,128)S(1)}, f32[1,512]{1,0:T(1,128)S(1)}, u32[]{:S(2)}, u32[]{:S(2)}) %collective-permute-start.1) | collective-permute-done | bytes 2080 | tf_op jit(solution)/shard_map/ppermute | solution.py:536
  51.0 7.2 %shard_map.159 = (f32[400,512]{1,0:T(8,128)}, f32[400,512]{1,0:T(8,128)}, f32[200,512]{1,0:T(8,128)S(1)}, f32[200,512]{1,0:T(8,128)S(1)}) custom-call(s32[1]{0:T(128)} %bitcast.core_ref, s32[2,512]{1,0:T(2,128)S(1)} %copy-done.13, s32[2,512]{1,0:T(2,128)S(1)} %copy-done.17, s32[2,1024]{1,0:T(2,128)S(1)} %copy-done.14, f32[400,512]{1,0:T(8,128)S(1)} %copy-done.6, ...), custom_call_target="tpu_custom_call" | custom-call | flops 10000 | bytes 10000 | tf_op jit(solution)/shard_map/pallas_call | solution.py:520
  59.9 1.6 collective-permute-start.7
  61.5 3.3 %shard_map.161 = (f32[8,24,256]{2,1,0:T(8,128)S(1)}, f32[8,24,256]{2,1,0:T(8,128)S(1)}, f32[8,24,256]{2,1,0:T(8,128)S(1)}, f32[8,24,256]{2,1,0:T(8,128)S(1)}, f3...) custom-call(s32[1]{0:T(128)} %bitcast.9.chip_ref, s32[2,512]{1,0:T(2,128)S(1)} %copy-done.16, ...), custom_call_target="tpu_custom_call" | custom-call | flops 10000 | bytes 10000 | tf_op jit(solution)/shard_map/pallas_call | solution.py:179
  67.3 7.4 %collective-permute-done.7.refs_5_ = f32[8,64,256]{2,1,0:T(8,128)S(1)} collective-permute-done((f32[8,64,256]{2,1,0:T(8,128)S(1)}, f32[8,64,256]{2,1,0:T(8,128)S(1)}, u32[]{:S(2)}, u32[]{:S(2)}) %collective-permute-start.7) | collective-permute-done | bytes 524320 | tf_op jit(solution)/shard_map/ppermute | solution.py:540
  74.7 3.4 %collective-permute-done.11.refs_9_ = f32[8,24,256]{2,1,0:T(8,128)S(1)} collective-permute-done((f32[8,24,256]{2,1,0:T(8,128)S(1)}, f32[8,24,256]{2,1,0:T(8,128)S(1)}, u32[]{:S(2)}, u32[]{:S(2)}) %collective-permute-start.11) | collective-permute-done | bytes 196640 | tf_op jit(solution)/shard_map/ppermute | solution.py:540
  78.9 1.6 collective-permute-start.15
  82.0 6.7 %collective-permute-done.15.refs_4_ = f32[4,88,256]{2,1,0:T(8,128)S(1)} collective-permute-done((f32[4,88,256]{2,1,0:T(8,128)S(1)}, f32[4,88,256]{2,1,0:T(8,128)S(1)}, u32[]{:S(2)}, u32[]{:S(2)}) %collective-permute-start.15) | collective-permute-done | bytes 360480 | tf_op jit(solution)/shard_map/ppermute | solution.py:540
  92.1 2.6 %collective-permute-start.19 = (f32[2,88,256]{2,1,0:T(8,128)S(1)}, f32[2,88,256]{2,1,0:T(8,128)S(1)}, u32[]{:S(2)}, u32[]{:S(2)}) collective-permute-start(f32[2,88,256]{2,1,0:T(8,128)S(1)} %get-tuple-element.117), channel_id=1, source_target_pairs={{0,2},{1,3},{2,0},{3,1},{4,6},{5,7},{6,4},{7,5},{8,10},{9,11},{10,... | collective-permute-start | bytes 540680 | tf_op jit(solution)/shard_map/ppermute | solution.py:540
  94.8 1.7 collective-permute-done.18.refs_4_
  96.4 4.9 %collective-permute-done.19.refs_5_ = f32[2,88,256]{2,1,0:T(8,128)S(1)} collective-permute-done((f32[2,88,256]{2,1,0:T(8,128)S(1)}, f32[2,88,256]{2,1,0:T(8,128)S(1)}, u32[]{:S(2)}, u32[]{:S(2)}) %collective-permute-start.19) | collective-permute-done | bytes 180256 | tf_op jit(solution)/shard_map/ppermute | solution.py:540
  106.0 1.6 collective-permute-start.20
  110.2 1.8 %collective-permute-done.21.refs_4_ = f32[1,88,256]{2,1,0:T(8,128)S(1)} collective-permute-done((f32[1,88,256]{2,1,0:T(8,128)S(1)}, f32[1,88,256]{2,1,0:T(8,128)S(1)}, u32[]{:S(2)}, u32[]{:S(2)}) %collective-permute-start.21) | collective-permute-done | bytes 90144 | tf_op jit(solution)/shard_map/ppermute | solution.py:540
  114.8 2.8 %collective-permute-start.25 = (f32[1,88,256]{2,1,0:T(8,128)S(1)}, f32[1,88,256]{2,1,0:T(8,128)S(1)}, u32[]{:S(2)}, u32[]{:S(2)}) collective-permute-start(f32[1,88,256]{2,1,0:T(8,128)S(1)} %get-tuple-element.133.refs_1_), channel_id=1, source_target_pairs={{0,2},{1,3},{2,0},{3,1},{4,6},{5,7},{6,4},{7,5},{8,10},{9,11},{10,... | collective-permute-start | bytes 270344 | tf_op jit(solution)/shard_map/ppermute | solution.py:540
  118.5 7.9 %collective-permute-done.25.refs_4_ = f32[1,88,256]{2,1,0:T(8,128)S(1)} collective-permute-done((f32[1,88,256]{2,1,0:T(8,128)S(1)}, f32[1,88,256]{2,1,0:T(8,128)S(1)}, u32[]{:S(2)}, u32[]{:S(2)}) %collective-permute-start.25) | collective-permute-done | bytes 90144 | tf_op jit(solution)/shard_map/ppermute | solution.py:540
  127.7 1.7 collective-permute-start.29
  129.4 3.1 %collective-permute-done.28.refs_4_ = f32[2,88,256]{2,1,0:T(8,128)S(1)} collective-permute-done((f32[2,88,256]{2,1,0:T(8,128)S(1)}, f32[2,88,256]{2,1,0:T(8,128)S(1)}, u32[]{:S(2)}, u32[]{:S(2)}) %collective-permute-start.28) | collective-permute-done | bytes 180256 | tf_op jit(solution)/shard_map/ppermute | solution.py:540
  132.5 5.6 %collective-permute-done.29.refs_5_ = f32[2,88,256]{2,1,0:T(8,128)S(1)} collective-permute-done((f32[2,88,256]{2,1,0:T(8,128)S(1)}, f32[2,88,256]{2,1,0:T(8,128)S(1)}, u32[]{:S(2)}, u32[]{:S(2)}) %collective-permute-start.29) | collective-permute-done | bytes 180256 | tf_op jit(solution)/shard_map/ppermute | solution.py:540
  138.1 2.8 %collective-permute-start.30 = (f32[4,96,256]{2,1,0:T(8,128)S(1)}, f32[4,96,256]{2,1,0:T(8,128)S(1)}, u32[]{:S(2)}, u32[]{:S(2)}) collective-permute-start(f32[4,96,256]{2,1,0:T(8,128)S(1)} %get-tuple-element.138.refs_0_), channel_id=1, source_target_pairs={{0,16},{4,20},{8,24},{12,28},{16,0},{20,4},{24,8},{28,12},{1,17},{... | collective-permute-start | bytes 1179656 | tf_op jit(solution)/shard_map/ppermute | solution.py:540
  141.3 8.6 %collective-permute-done.31.refs_4_ = f32[4,88,256]{2,1,0:T(8,128)S(1)} collective-permute-done((f32[4,88,256]{2,1,0:T(8,128)S(1)}, f32[4,88,256]{2,1,0:T(8,128)S(1)}, u32[]{:S(2)}, u32[]{:S(2)}) %collective-permute-start.31) | collective-permute-done | bytes 360480 | tf_op jit(solution)/shard_map/ppermute | solution.py:540
  153.1 14.2 %collective-permute-done.36.refs_3_ = f32[8,96,256]{2,1,0:T(8,128)S(1)} collective-permute-done((f32[8,96,256]{2,1,0:T(8,128)S(1)}, f32[8,96,256]{2,1,0:T(8,128)S(1)}, u32[]{:S(2)}, u32[]{:S(2)}) %collective-permute-start.36) | collective-permute-done | bytes 786464 | tf_op jit(solution)/shard_map/ppermute | solution.py:540
  167.9 2.4 %collective-permute-done.40.refs_5_ = f32[8,88,256]{2,1,0:T(8,128)S(1)} collective-permute-done((f32[8,88,256]{2,1,0:T(8,128)S(1)}, f32[8,88,256]{2,1,0:T(8,128)S(1)}, u32[]{:S(2)}, u32[]{:S(2)}) %collective-permute-start.40) | collective-permute-done | bytes 720928 | tf_op jit(solution)/shard_map/ppermute | solution.py:540
  170.4 3.1 %shard_map.170 = (f32[2,200,4096]{2,1,0:T(8,128)}, f32[2,200,1280]{2,1,0:T(8,128)}) custom-call(s32[2]{0:T(128)S(1)} %pad_add_fusion.2.spot_ref, f32[8,96,256]{2,1,0:T(8,128)S(1)} %get-tuple-element.141.refs_0_, f32[8,88,256]{2,1,0:T(8,128)S(1)} %get-tuple-element.142.refs_1_, f32[8,88,256]{2,1,0:T(8,128)S(1)} %get-tuple-element.143.refs_2_, ...), custom_call_target="tpu_custom_call" | custom-call | flops 10000 | bytes 10000 | tf_op jit(solution)/shard_map/pallas_call | solution.py:304
  173.6 3.2 %shard_map.171 = (f32[2,200,4096]{2,1,0:T(8,128)}, f32[2,200,1280]{2,1,0:T(8,128)}) custom-call(s32[2]{0:T(128)S(1)} %pad_add_fusion.spot_ref, f32[8,96,256]{2,1,0:T(8,128)S(1)} %collective-permute-done.33.refs_0_, f32[8,88,256]{2,1,0:T(8,128)S(1)} %collective-permute-done.34.refs_1_, ...), custom_call_target="tpu_custom_call", output_to_operand_aliasing={{0}: (7, {}), {1}: (8, {})} | custom-call | flops 10000 | bytes 10000 | tf_op jit(solution)/shard_map/pallas_call | solution.py:304
  (118 shorter events, 33.0 us)
Async XLA Ops:
  25.5 23.1 %collective-permute-start = (f32[400,512]{1,0:T(8,128)}, f32[400,512]{1,0:T(8,128)S(1)}, u32[]{:S(2)}, u32[]{:S(2)}) collective-permute-start(f32[400,512]{1,0:T(8,128)} %get-tuple-element.82), channel_id=1, source_target_pairs={{0,4},{4,8},{8,12},{12,16},{16,20},{20,24},{24,28},{28,0},{1,5},{5... | collective-permute-start | bytes 2457608 | tf_op jit(solution)/shard_map/ppermute | solution.py:536
  26.0 10.9 %collective-permute-start.3 = (f32[200,256]{1,0:T(8,128)}, f32[200,256]{1,0:T(8,128)}, u32[]{:S(2)}, u32[]{:S(2)}) collective-permute-start(f32[200,256]{1,0:T(8,128)} %get-tuple-element.88), channel_id=1, source_target_pairs={{0,4},{4,0},{8,12},{12,8},{16,20},{20,16},{24,28},{28,24},{1,5},{5... | collective-permute-start | bytes 614408 | tf_op jit(solution)/shard_map/ppermute | solution.py:540
  43.1 23.7 %collective-permute-start.6 = (f32[8,64,256]{2,1,0:T(8,128)S(1)}, f32[8,64,256]{2,1,0:T(8,128)S(1)}, u32[]{:S(2)}, u32[]{:S(2)}) collective-permute-start(f32[8,64,256]{2,1,0:T(8,128)S(1)} %get-tuple-element.94), channel_id=1, source_target_pairs={{0,16},{4,20},{8,24},{12,28},{16,0},{20,4},{24,8},{28,12},{1,17},{... | collective-permute-start | bytes 1572872 | tf_op jit(solution)/shard_map/ppermute | solution.py:540
  44.7 16.8 %collective-permute-start.9 = (f32[200,512]{1,0:T(8,128)}, f32[200,512]{1,0:T(8,128)S(1)}, u32[]{:S(2)}, u32[]{:S(2)}) collective-permute-start(f32[200,512]{1,0:T(8,128)} %copy-done.20), channel_id=1, source_target_pairs={{0,4},{4,0},{8,12},{12,8},{16,20},{20,16},{24,28},{28,24},{1,5},{5... | collective-permute-start | bytes 1228808 | tf_op jit(solution)/shard_map/ppermute | solution.py:540
  58.2 16.5 %collective-permute-start.5 = (f32[8,72,256]{2,1,0:T(8,128)S(1)}, f32[8,72,256]{2,1,0:T(8,128)S(1)}, u32[]{:S(2)}, u32[]{:S(2)}) collective-permute-start(f32[8,72,256]{2,1,0:T(8,128)S(1)} %get-tuple-element.93), channel_id=1, source_target_pairs={{0,8},{4,12},{8,0},{12,4},{16,24},{20,28},{24,16},{28,20},{1,9},{5... | collective-permute-start | bytes 1769480 | tf_op jit(solution)/shard_map/ppermute | solution.py:540
  59.9 14.8 %collective-permute-start.7 = (f32[8,64,256]{2,1,0:T(8,128)S(1)}, f32[8,64,256]{2,1,0:T(8,128)S(1)}, u32[]{:S(2)}, u32[]{:S(2)}) collective-permute-start(f32[8,64,256]{2,1,0:T(8,128)S(1)} %get-tuple-element.95), channel_id=1, source_target_pairs={{0,1},{1,0},{2,3},{3,2},{4,5},{5,4},{6,7},{7,6},{8,9},{9,8},{10,11... | collective-permute-start | bytes 1572872 | tf_op jit(solution)/shard_map/ppermute | solution.py:540
  64.8 13.3 %collective-permute-start.11 = (f32[8,24,256]{2,1,0:T(8,128)S(1)}, f32[8,24,256]{2,1,0:T(8,128)S(1)}, u32[]{:S(2)}, u32[]{:S(2)}) collective-permute-start(f32[8,24,256]{2,1,0:T(8,128)S(1)} %get-tuple-element.103), channel_id=1, source_target_pairs={{0,8},{4,12},{8,0},{12,4},{16,24},{20,28},{24,16},{28,20},{1,9},{5... | collective-permute-start | bytes 589832 | tf_op jit(solution)/shard_map/ppermute | solution.py:540
  66.3 11.8 %collective-permute-start.12 = (f32[8,24,256]{2,1,0:T(8,128)S(1)}, f32[8,24,256]{2,1,0:T(8,128)S(1)}, u32[]{:S(2)}, u32[]{:S(2)}) collective-permute-start(f32[8,24,256]{2,1,0:T(8,128)S(1)} %get-tuple-element.104), channel_id=1, source_target_pairs={{0,16},{4,20},{8,24},{12,28},{16,0},{20,4},{24,8},{28,12},{1,17},{... | collective-permute-start | bytes 589832 | tf_op jit(solution)/shard_map/ppermute | solution.py:540
  66.8 11.3 %collective-permute-start.13 = (f32[8,24,256]{2,1,0:T(8,128)S(1)}, f32[8,24,256]{2,1,0:T(8,128)S(1)}, u32[]{:S(2)}, u32[]{:S(2)}) collective-permute-start(f32[8,24,256]{2,1,0:T(8,128)S(1)} %get-tuple-element.105), channel_id=1, source_target_pairs={{0,1},{1,0},{2,3},{3,2},{4,5},{5,4},{6,7},{7,6},{8,9},{9,8},{10,11... | collective-permute-start | bytes 589832 | tf_op jit(solution)/shard_map/ppermute | solution.py:540
  78.4 11.6 %collective-permute-start.14 = (f32[4,96,256]{2,1,0:T(8,128)S(1)}, f32[4,96,256]{2,1,0:T(8,128)S(1)}, u32[]{:S(2)}, u32[]{:S(2)}) collective-permute-start(f32[4,96,256]{2,1,0:T(8,128)S(1)} %get-tuple-element.109), channel_id=1, source_target_pairs={{0,16},{4,20},{8,24},{12,28},{16,0},{20,4},{24,8},{28,12},{1,17},{... | collective-permute-start | bytes 1179656 | tf_op jit(solution)/shard_map/ppermute | solution.py:540
  78.9 9.8 %collective-permute-start.15 = (f32[4,88,256]{2,1,0:T(8,128)S(1)}, f32[4,88,256]{2,1,0:T(8,128)S(1)}, u32[]{:S(2)}, u32[]{:S(2)}) collective-permute-start(f32[4,88,256]{2,1,0:T(8,128)S(1)} %get-tuple-element.110), channel_id=1, source_target_pairs={{0,1},{1,0},{2,3},{3,2},{4,5},{5,4},{6,7},{7,6},{8,9},{9,8},{10,11... | collective-permute-start | bytes 1081352 | tf_op jit(solution)/shard_map/ppermute | solution.py:540
  80.5 9.5 %collective-permute-start.16 = (f32[4,88,256]{2,1,0:T(8,128)S(1)}, f32[4,88,256]{2,1,0:T(8,128)S(1)}, u32[]{:S(2)}, u32[]{:S(2)}) collective-permute-start(f32[4,88,256]{2,1,0:T(8,128)S(1)} %get-tuple-element.111), channel_id=1, source_target_pairs={{0,8},{4,12},{8,0},{12,4},{16,24},{20,28},{24,16},{28,20},{1,9},{5... | collective-permute-start | bytes 1081352 | tf_op jit(solution)/shard_map/ppermute | solution.py:540
  90.1 11.2 %collective-permute-start.17 = (f32[2,96,256]{2,1,0:T(8,128)S(1)}, f32[2,96,256]{2,1,0:T(8,128)S(1)}, u32[]{:S(2)}, u32[]{:S(2)}) collective-permute-start(f32[2,96,256]{2,1,0:T(8,128)S(1)} %get-tuple-element.115), channel_id=1, source_target_pairs={{0,1},{1,0},{2,3},{3,2},{4,5},{5,4},{6,7},{7,6},{8,9},{9,8},{10,11... | collective-permute-start | bytes 589832 | tf_op jit(solution)/shard_map/ppermute | solution.py:540
  92.1 9.2 %collective-permute-start.19 = (f32[2,88,256]{2,1,0:T(8,128)S(1)}, f32[2,88,256]{2,1,0:T(8,128)S(1)}, u32[]{:S(2)}, u32[]{:S(2)}) collective-permute-start(f32[2,88,256]{2,1,0:T(8,128)S(1)} %get-tuple-element.117), channel_id=1, source_target_pairs={{0,2},{1,3},{2,0},{3,1},{4,6},{5,7},{6,4},{7,5},{8,10},{9,11},{10,... | collective-permute-start | bytes 540680 | tf_op jit(solution)/shard_map/ppermute | solution.py:540
  104.6 7.5 %collective-permute-start.21 = (f32[1,88,256]{2,1,0:T(8,128)S(1)}, f32[1,88,256]{2,1,0:T(8,128)S(1)}, u32[]{:S(2)}, u32[]{:S(2)}) collective-permute-start(f32[1,88,256]{2,1,0:T(8,128)S(1)} %get-tuple-element.125), channel_id=1, source_target_pairs={{0,2},{1,3},{2,0},{3,1},{4,6},{5,7},{6,4},{7,5},{8,10},{9,11},{10,... | collective-permute-start | bytes 270344 | tf_op jit(solution)/shard_map/ppermute | solution.py:540
  104.7 7.4 %collective-permute-start.22 = (f32[1,88,256]{2,1,0:T(8,128)S(1)}, f32[1,88,256]{2,1,0:T(8,128)S(1)}, u32[]{:S(2)}, u32[]{:S(2)}) collective-permute-start(f32[1,88,256]{2,1,0:T(8,128)S(1)} %get-tuple-element.126), channel_id=1, source_target_pairs={{0,16},{4,20},{8,24},{12,28},{16,0},{20,4},{24,8},{28,12},{1,17},{... | collective-permute-start | bytes 270344 | tf_op jit(solution)/shard_map/ppermute | solution.py:540
  106.0 7.1 %collective-permute-start.20 = (f32[1,96,256]{2,1,0:T(8,128)S(1)}, f32[1,96,256]{2,1,0:T(8,128)S(1)}, u32[]{:S(2)}, u32[]{:S(2)}) collective-permute-start(f32[1,96,256]{2,1,0:T(8,128)S(1)} %get-tuple-element.124), channel_id=1, source_target_pairs={{0,2},{1,3},{2,0},{3,1},{4,6},{5,7},{6,4},{7,5},{8,10},{9,11},{10,... | collective-permute-start | bytes 294920 | tf_op jit(solution)/shard_map/ppermute | solution.py:540
  114.6 11.8 %collective-permute-start.24 = (f32[1,96,256]{2,1,0:T(8,128)S(1)}, f32[1,96,256]{2,1,0:T(8,128)S(1)}, u32[]{:S(2)}, u32[]{:S(2)}) collective-permute-start(f32[1,96,256]{2,1,0:T(8,128)S(1)} %get-tuple-element.132.refs_0_), channel_id=1, source_target_pairs={{0,2},{1,3},{2,0},{3,1},{4,6},{5,7},{6,4},{7,5},{8,10},{9,11},{10,... | collective-permute-start | bytes 294920 | tf_op jit(solution)/shard_map/ppermute | solution.py:540
  114.8 11.7 %collective-permute-start.25 = (f32[1,88,256]{2,1,0:T(8,128)S(1)}, f32[1,88,256]{2,1,0:T(8,128)S(1)}, u32[]{:S(2)}, u32[]{:S(2)}) collective-permute-start(f32[1,88,256]{2,1,0:T(8,128)S(1)} %get-tuple-element.133.refs_1_), channel_id=1, source_target_pairs={{0,2},{1,3},{2,0},{3,1},{4,6},{5,7},{6,4},{7,5},{8,10},{9,11},{10,... | collective-permute-start | bytes 270344 | tf_op jit(solution)/shard_map/ppermute | solution.py:540
  117.6 8.8 %collective-permute-start.26 = (f32[1,88,256]{2,1,0:T(8,128)S(1)}, f32[1,88,256]{2,1,0:T(8,128)S(1)}, u32[]{:S(2)}, u32[]{:S(2)}) collective-permute-start(f32[1,88,256]{2,1,0:T(8,128)S(1)} %get-tuple-element.134.refs_2_), channel_id=1, source_target_pairs={{0,16},{4,20},{8,24},{12,28},{16,0},{20,4},{24,8},{28,12},{1,17},{... | collective-permute-start | bytes 270344 | tf_op jit(solution)/shard_map/ppermute | solution.py:540
  126.5 11.5 %collective-permute-start.27 = (f32[2,96,256]{2,1,0:T(8,128)S(1)}, f32[2,96,256]{2,1,0:T(8,128)S(1)}, u32[]{:S(2)}, u32[]{:S(2)}) collective-permute-start(f32[2,96,256]{2,1,0:T(8,128)S(1)} %get-tuple-element.135.refs_0_), channel_id=1, source_target_pairs={{0,1},{1,0},{2,3},{3,2},{4,5},{5,4},{6,7},{7,6},{8,9},{9,8},{10,11... | collective-permute-start | bytes 589832 | tf_op jit(solution)/shard_map/ppermute | solution.py:540
  127.7 10.4 %collective-permute-start.29 = (f32[2,88,256]{2,1,0:T(8,128)S(1)}, f32[2,88,256]{2,1,0:T(8,128)S(1)}, u32[]{:S(2)}, u32[]{:S(2)}) collective-permute-start(f32[2,88,256]{2,1,0:T(8,128)S(1)} %get-tuple-element.137.refs_2_), channel_id=1, source_target_pairs={{0,2},{1,3},{2,0},{3,1},{4,6},{5,7},{6,4},{7,5},{8,10},{9,11},{10,... | collective-permute-start | bytes 540680 | tf_op jit(solution)/shard_map/ppermute | solution.py:540
  138.1 11.8 %collective-permute-start.30 = (f32[4,96,256]{2,1,0:T(8,128)S(1)}, f32[4,96,256]{2,1,0:T(8,128)S(1)}, u32[]{:S(2)}, u32[]{:S(2)}) collective-permute-start(f32[4,96,256]{2,1,0:T(8,128)S(1)} %get-tuple-element.138.refs_0_), channel_id=1, source_target_pairs={{0,16},{4,20},{8,24},{12,28},{16,0},{20,4},{24,8},{28,12},{1,17},{... | collective-permute-start | bytes 1179656 | tf_op jit(solution)/shard_map/ppermute | solution.py:540
  140.9 9.0 %collective-permute-start.31 = (f32[4,88,256]{2,1,0:T(8,128)S(1)}, f32[4,88,256]{2,1,0:T(8,128)S(1)}, u32[]{:S(2)}, u32[]{:S(2)}) collective-permute-start(f32[4,88,256]{2,1,0:T(8,128)S(1)} %get-tuple-element.139.refs_1_), channel_id=1, source_target_pairs={{0,1},{1,0},{2,3},{3,2},{4,5},{5,4},{6,7},{7,6},{8,9},{9,8},{10,11... | collective-permute-start | bytes 1081352 | tf_op jit(solution)/shard_map/ppermute | solution.py:540
  140.9 9.0 %collective-permute-start.32 = (f32[4,88,256]{2,1,0:T(8,128)S(1)}, f32[4,88,256]{2,1,0:T(8,128)S(1)}, u32[]{:S(2)}, u32[]{:S(2)}) collective-permute-start(f32[4,88,256]{2,1,0:T(8,128)S(1)} %get-tuple-element.140.refs_2_), channel_id=1, source_target_pairs={{0,8},{4,12},{8,0},{12,4},{16,24},{20,28},{24,16},{28,20},{1,9},{5... | collective-permute-start | bytes 1081352 | tf_op jit(solution)/shard_map/ppermute | solution.py:540
  150.1 17.3 %collective-permute-start.36 = (f32[8,96,256]{2,1,0:T(8,128)S(1)}, f32[8,96,256]{2,1,0:T(8,128)S(1)}, u32[]{:S(2)}, u32[]{:S(2)}) collective-permute-start(f32[8,96,256]{2,1,0:T(8,128)S(1)} %get-tuple-element.141.refs_0_), channel_id=1, source_target_pairs={{0,8},{4,12},{8,0},{12,4},{16,24},{20,28},{24,16},{28,20},{1,9},{5... | collective-permute-start | bytes 2359304 | tf_op jit(solution)/shard_map/ppermute | solution.py:540
  150.8 16.6 %collective-permute-start.38 = (f32[8,88,256]{2,1,0:T(8,128)S(1)}, f32[8,88,256]{2,1,0:T(8,128)S(1)}, u32[]{:S(2)}, u32[]{:S(2)}) collective-permute-start(f32[8,88,256]{2,1,0:T(8,128)S(1)} %get-tuple-element.142.refs_1_), channel_id=1, source_target_pairs={{0,16},{4,20},{8,24},{12,28},{16,0},{20,4},{24,8},{28,12},{1,17},{... | collective-permute-start | bytes 2162696 | tf_op jit(solution)/shard_map/ppermute | solution.py:540
  151.7 16.1 %collective-permute-start.34 = (f32[8,88,256]{2,1,0:T(8,128)S(1)}, f32[8,88,256]{2,1,0:T(8,128)S(1)}, u32[]{:S(2)}, u32[]{:S(2)}) collective-permute-start(f32[8,88,256]{2,1,0:T(8,128)S(1)} %get-tuple-element.142.refs_1_), channel_id=1, source_target_pairs={{0,4},{4,0},{8,12},{12,8},{16,20},{20,16},{24,28},{28,24},{1,5},{5... | collective-permute-start | bytes 2162696 | tf_op jit(solution)/shard_map/ppermute | solution.py:540
  151.7 18.5 %collective-permute-start.40 = (f32[8,88,256]{2,1,0:T(8,128)S(1)}, f32[8,88,256]{2,1,0:T(8,128)S(1)}, u32[]{:S(2)}, u32[]{:S(2)}) collective-permute-start(f32[8,88,256]{2,1,0:T(8,128)S(1)} %get-tuple-element.143.refs_2_), channel_id=1, source_target_pairs={{0,1},{1,0},{2,3},{3,2},{4,5},{5,4},{6,7},{7,6},{8,9},{9,8},{10,11... | collective-permute-start | bytes 2162696 | tf_op jit(solution)/shard_map/ppermute | solution.py:540
  152.9 20.7 %collective-permute-start.33 = (f32[8,96,256]{2,1,0:T(8,128)S(1)}, f32[8,96,256]{2,1,0:T(8,128)S(1)}, u32[]{:S(2)}, u32[]{:S(2)}) collective-permute-start(f32[8,96,256]{2,1,0:T(8,128)S(1)} %get-tuple-element.141.refs_0_), channel_id=1, source_target_pairs={{0,4},{4,0},{8,12},{12,8},{16,20},{20,16},{24,28},{28,24},{1,5},{5... | collective-permute-start | bytes 2359304 | tf_op jit(solution)/shard_map/ppermute | solution.py:540
  167.3 6.3 %collective-permute-start.37 = (f32[8,96,256]{2,1,0:T(8,128)S(1)}, f32[8,96,256]{2,1,0:T(8,128)S(1)}, u32[]{:S(2)}, u32[]{:S(2)}) collective-permute-start(f32[8,96,256]{2,1,0:T(8,128)S(1)} %collective-permute-done.36.refs_3_), channel_id=1, source_target_pairs={{0,4},{4,0},{8,12},{12,8},{16,20},{20,16},{24,28},{28,24},{1,5},{5... | collective-permute-start | bytes 2359304 | tf_op jit(solution)/shard_map/ppermute | solution.py:540
  167.3 6.2 %collective-permute-start.35 = (f32[8,88,256]{2,1,0:T(8,128)S(1)}, f32[8,88,256]{2,1,0:T(8,128)S(1)}, u32[]{:S(2)}, u32[]{:S(2)}) collective-permute-start(f32[8,88,256]{2,1,0:T(8,128)S(1)} %get-tuple-element.143.refs_2_), channel_id=1, source_target_pairs={{0,4},{4,0},{8,12},{12,8},{16,20},{20,16},{24,28},{28,24},{1,5},{5... | collective-permute-start | bytes 2162696 | tf_op jit(solution)/shard_map/ppermute | solution.py:540
  (31 other events, 248.3 us)

commit v3 on v2

v3 whole, which is shorter than its diff:
```python
import functools
import jax
import jax.numpy as jnp
from jax import lax
from jax.experimental import pallas as pl
from jax.experimental.pallas import tpu as pltpu
from jax.sharding import PartitionSpec as P

step_rate = 0.25
F32, BF16 = jnp.float32, jnp.bfloat16
NN = (((1,), (0,)), ((), ()))
NT = (((1,), (1,)), ((), ()))
TN = (((0,), (0,)), ((), ()))
VMEM = pl.BlockSpec(memory_space=pltpu.VMEM)
SMEM = pl.BlockSpec(memory_space=pltpu.SMEM)
PARAMS = pltpu.CompilerParams(vmem_limit_bytes=16 * 1024 * 1024)
ALL_VMEM = pltpu.CompilerParams(vmem_limit_bytes=56 * 1024 * 1024)
COST = pl.CostEstimate(flops=10000, bytes_accessed=10000, transcendentals=0)


def split(x):
    hi = x.astype(BF16)
    return hi, (x - hi.astype(F32)).astype(BF16)


def dot(a, b, dims):
    return lax.dot_general(a, b, dims, preferred_element_type=F32)


def dot3(a, b, dims):
    return dot(a[0], b[0], dims) + (dot(a[0], b[1], dims) + dot(a[1], b[0], dims))


def dot2(a, onehot, dims):
    return dot(a[0], onehot, dims) + dot(a[1], onehot, dims)


def onehot(first, rows, idx):
    place = lax.broadcasted_iota(jnp.int32, (rows, idx.shape[1]), 0) + first
    return jnp.where(place == idx, 1.0, 0.0).astype(BF16)


def laid_out(idx):
    return jnp.concatenate([idx[b : b + 1] for b in range(idx.shape[0])], axis=1)


def add_part(first, part, out_ref):
    @pl.when(first)
    def _():
        out_ref[...] = part

    @pl.when(jnp.logical_not(first))
    def _():
        out_ref[...] += part


def gather_kernel(hub_steps, hub_idx, rel_idx, hub_ref, rel_ref, hub_out, rel_out):
    step = pl.program_id(0)

    @pl.when(step < hub_steps)
    def _():
        tile = hub_ref.shape[1]
        hot = onehot(step * tile, tile, laid_out(hub_idx[...]))
        add_part(step == 0, dot2(split(hub_ref[...]), hot, NN), hub_out)

    @pl.when(step >= hub_steps)
    def _():
        tile = rel_ref.shape[1]
        hot = onehot((step - hub_steps) * tile, tile, laid_out(rel_idx[...]))
        add_part(step == hub_steps, dot2(split(rel_ref[...]), hot, NN), rel_out)


def gather_rows(hub_table, hub_idx, rel_table, rel_idx):
    features = hub_table.shape[0]
    hub_steps, rel_steps = 4, 2
    fixed = lambda shape: pl.BlockSpec(shape, lambda k: (0, 0))
    shapes = [(features, hub_idx.size), (features, rel_idx.size)]
    return pl.pallas_call(
        functools.partial(gather_kernel, hub_steps),
        grid=(hub_steps + rel_steps,),
        in_specs=[
            fixed(hub_idx.shape),
            fixed(rel_idx.shape),
            pl.BlockSpec((features, hub_table.shape[1] // hub_steps), lambda k: (0, jnp.minimum(k, hub_steps - 1))),
            pl.BlockSpec((features, rel_table.shape[1] // rel_steps), lambda k: (0, jnp.maximum(k - hub_steps, 0))),
        ],
        out_specs=[fixed(shape) for shape in shapes],
        out_shape=[jax.ShapeDtypeStruct(shape, F32) for shape in shapes],
        compiler_params=ALL_VMEM,
        cost_estimate=COST,
    )(hub_idx, rel_idx, hub_table, rel_table)


def spread_bits(place, order):
    bits = len(order)
    return sum((((place >> p) & 1) << (bits - 1 - i)) for i, p in enumerate(order))


def gather_bits(index, order):
    bits = len(order)
    return sum((((index >> (bits - 1 - i)) & 1) << p) for i, p in enumerate(order))


def load_columns(id_refs, id_lanes, grad_refs, idx_down, hi_all, lo_all):
    low, high = id_lanes
    idx = jnp.concatenate([laid_out(ref[:, low:high]) for ref in id_refs], axis=1)
    idx_down[...] = jnp.transpose(jnp.broadcast_to(idx, (128, idx.shape[1])))
    at = 0
    for ref, (low, high) in grad_refs:
        width = high - low
        hi_all[:, at : at + width], lo_all[:, at : at + width] = split(ref[:, low:high])
        at += width


def onehot_across(idx_down, targets):
    width = targets.shape[1]
    idx = idx_down[...]
    wide = jnp.concatenate([idx] * -(-width // 128), axis=1)[:, :width]
    return jnp.where(wide == targets, 1.0, 0.0).astype(BF16)


def out_for(place, order, sends, keeps, s):
    index = spread_bits(place, order)
    half = keeps[s].shape[0]
    return sends[s].at[index - half] if index >= half else keeps[s].at[index]


def chunk_refs(orders, grad_lanes, refs):
    ids, refs = refs[:2], refs[2:]
    grads, refs = list(zip(refs, grad_lanes)), refs[len(grad_lanes) :]
    streams = len(orders)
    return ids, grads, refs[:streams], refs[streams : 2 * streams], refs[2 * streams :]


def hub_chunks_kernel(orders, spans, id_lanes, grad_lanes, chip_ref, *refs):
    ids, grads, sends, keeps, (idx_down, hi_all, lo_all) = chunk_refs(orders, grad_lanes, refs)
    load_columns(ids, id_lanes, grads, idx_down, hi_all, lo_all)
    chunks, width = 2 * keeps[0].shape[0], keeps[0].shape[2]
    lane = lax.broadcasted_iota(jnp.int32, (1, width), 1)
    for place in range(chunks):
        hot = onehot_across(idx_down, lane + (chip_ref[0] ^ place) * width)
        chunk = dot2((hi_all[...], lo_all[...]), hot, NN)
        for s, (low, high) in enumerate(spans):
            out_for(place, orders[s], sends, keeps, s)[...] = chunk[low:high]


def rel_layout(half_width, streams):
    blocks = row_spans(half_width, 3)
    spans = row_spans(max(high - low for low, high in blocks), streams)
    pieces = []
    for block, (low, high) in enumerate(blocks):
        for s, (first, end) in enumerate(spans):
            count = min(end, high - low) - first
            if count > 0:
                pieces.append((block, s, low + first, count))
    return spans, pieces


def rel_chunks_kernel(orders, pieces, rows, id_lanes, grad_lanes, chip_ref, *refs):
    ids, grads, sends, keeps, (idx_down, hi_all, lo_all) = chunk_refs(orders, grad_lanes, refs)
    load_columns(ids, id_lanes, grads, idx_down, hi_all, lo_all)
    for ref in [*sends, *keeps]:
        ref[...] = jnp.zeros_like(ref)
    chunks, lanes = 2 * keeps[0].shape[0], keeps[0].shape[2]
    width = rows // chunks
    group = lanes // width
    lane = lax.broadcasted_iota(jnp.int32, (1, lanes), 1)
    for first in range(0, chunks, group):
        targets = jnp.full((1, lanes), -1, jnp.int32)
        places = range(first, min(first + group, chunks))
        for slot, place in enumerate(places):
            here = (lane >= slot * width) & (lane < (slot + 1) * width)
            targets = jnp.where(here, lane + ((chip_ref[0] ^ place) * width - slot * width), targets)
        dense = dot2((hi_all[...], lo_all[...]), onehot_across(idx_down, targets), NN)
        for slot, place in enumerate(places):
            chunk = dense[:, slot * width : (slot + 1) * width]
            for block, s, low, count in pieces:
                out = out_for(place, orders[s], sends, keeps, s)
                out[:count, block * width : (block + 1) * width] = chunk[low : low + count]


def chunk_columns(kernel, heights, lanes, chip, ids, grads, chunks):
    half_width = grads[0][0].shape[0]
    grad_lanes = [lanes_of for unused, lanes_of in grads]
    count = sum(high - low for low, high in grad_lanes)
    shapes = [jax.ShapeDtypeStruct((chunks // 2, height, lanes), F32) for height in heights] * 2
    out = pl.pallas_call(
        functools.partial(kernel, grad_lanes),
        in_specs=[SMEM] + [VMEM] * (2 + len(grads)),
        out_specs=[VMEM] * len(shapes),
        out_shape=shapes,
        scratch_shapes=[
            pltpu.VMEM((count, 128), jnp.int32),
            pltpu.VMEM((half_width, count), BF16),
            pltpu.VMEM((half_width, count), BF16),
        ],
        compiler_params=PARAMS,
        cost_estimate=COST,
    )(chip, *ids, *[g for g, unused in grads])
    return out[: len(heights)], out[len(heights) :]


def call(kernel, ins, shapes):
    return pl.pallas_call(
        kernel,
        in_specs=[VMEM] * len(ins),
        out_specs=[VMEM] * len(shapes),
        out_shape=[jax.ShapeDtypeStruct(shape, F32) for shape in shapes],
        compiler_params=PARAMS,
        cost_estimate=COST,
    )(*ins)


def sums_kernel(*refs):
    streams = len(refs) // 4
    own, got, sends, keeps = [refs[i * streams : (i + 1) * streams] for i in range(4)]
    for s in range(streams):
        half = sends[s].shape[0]
        sends[s][...] = own[s][half:] + got[s][half:]
        keeps[s][...] = own[s][:half] + got[s][:half]


def halves(own, got):
    shapes = [(x.shape[0] // 2,) + x.shape[1:] for x in own]
    out = call(sums_kernel, [*own, *got], shapes * 2)
    return out[: len(shapes)], out[len(shapes) :]


def join_kernel(*refs):
    streams = len(refs) // 3
    for s in range(streams):
        own, got, out = refs[s], refs[streams + s], refs[2 * streams + s]
        count = own.shape[0]
        out[:count] = own[...]
        out[count:] = got[...]


def join(own, got):
    return call(join_kernel, [*own, *got], [(2 * x.shape[0],) + x.shape[1:] for x in own])


def squares_kernel(*refs):
    streams = len(refs) // 3
    own, got, totals, out = [refs[i * streams : (i + 1) * streams] for i in range(3)] + [refs[-1]]
    squares = jnp.zeros(out.shape, F32)
    for s in range(streams):
        total = own[s][0] + got[s][0]
        totals[s][0] = total
        squares += jnp.sum(total * total, axis=0, keepdims=True)
    out[...] = squares


def squares_of(own, got):
    *totals, squares = call(squares_kernel, [*own, *got], [x.shape for x in own] + [(1, own[0].shape[2])])
    return totals, squares


def hub_update_kernel(spans, features, *refs):
    streams = len(spans)
    totals, news = refs[:streams], refs[-streams:]
    mine, other, table_ref, sums_ref = refs[streams:-streams]
    scale = step_rate / jnp.sqrt(sums_ref[...] + (mine[...] + other[...]) * (1.0 / features))
    for s, (low, high) in enumerate(spans):
        news[s][0] = table_ref[low:high] - totals[s][0] * scale


def rel_update_kernel(streams, pieces, features, *refs):
    totals, news = refs[:streams], refs[-streams:]
    mine, other, table_ref, sums_ref = refs[streams:-streams]
    width = table_ref.shape[1]
    squares = mine[...] + other[...]
    squares = sum(squares[:, b * width : (b + 1) * width] for b in range(3))
    scale = step_rate / jnp.sqrt(sums_ref[...] + squares * (1.0 / features))
    for new in news:
        new[...] = jnp.zeros_like(new)
    for block, s, low, count in pieces:
        lanes = slice(block * width, (block + 1) * width)
        news[s][0, :count, lanes] = table_ref[low : low + count] - totals[s][0, :count, lanes] * scale


def place_kernel(orders, pieces, spot_ref, *refs):
    streams = len(orders)
    lows, highs, out_ref = refs[:streams], refs[streams : 2 * streams], refs[-1]
    half = lows[0].shape[0]
    width = out_ref.shape[2] // (2 * half)
    for chunk in range(2 * half):
        place = spot_ref[0] ^ chunk
        for s in range(streams):
            index = spread_bits(place, orders[s])
            spot = index & (half - 1)
            value = jnp.where(index >= half, highs[s][spot], lows[s][spot])
            for block, stream, row, count in pieces:
                if stream == s:
                    part = value[:count, block * width : (block + 1) * width]
                    out_ref[0, row : row + count, chunk * width : (chunk + 1) * width] = part


def place_chunks(spot, near, far, orders, pieces, shape, earlier):
    whole = [pl.BlockSpec(memory_space=pltpu.VMEM)] * (2 * len(orders))
    kept = [pl.BlockSpec(memory_space=pl.ANY)] * len(earlier)
    return pl.pallas_call(
        functools.partial(place_kernel, orders, pieces),
        grid_spec=pltpu.PrefetchScalarGridSpec(
            num_scalar_prefetch=1,
            grid=(1,),
            in_specs=whole + kept,
            out_specs=pl.BlockSpec((1,) + shape[1:], lambda i, spot: (spot[1], 0, 0)),
        ),
        out_shape=jax.ShapeDtypeStruct(shape, F32),
        input_output_aliases={1 + len(whole): 0} if earlier else {},
        compiler_params=PARAMS,
        cost_estimate=COST,
    )(spot, *near, *far, *earlier)


def copy_kernel(orders, spans, upper, spot_ref, *refs):
    streams = len(orders)
    parts, out_ref, sems = refs[:streams], refs[-2], refs[-1]
    half, width = parts[0].shape[0], parts[0].shape[2]
    copies = []
    for s, (low, high) in enumerate(spans):
        for index in range(half):
            chunk = spot_ref[0] ^ gather_bits(index + half * upper, orders[s])
            lanes = pl.ds(pl.multiple_of(chunk * width, width), width)
            target = out_ref.at[spot_ref[1], pl.ds(low, high - low), lanes]
            copies.append(pltpu.make_async_copy(parts[s].at[index], target, sems.at[len(copies)]))
    for copy in copies:
        copy.start()
    for copy in copies:
        copy.wait()


def copy_chunks(spot, parts, upper, orders, spans, shape, earlier):
    anywhere = pl.BlockSpec(memory_space=pl.ANY)
    return pl.pallas_call(
        functools.partial(copy_kernel, orders, spans, upper),
        in_specs=[SMEM] + [anywhere] * (len(parts) + len(earlier)),
        out_specs=anywhere,
        out_shape=jax.ShapeDtypeStruct(shape, F32),
        scratch_shapes=[pltpu.SemaphoreType.DMA((len(parts) * parts[0].shape[0],))],
        input_output_aliases={1 + len(parts): 0} if earlier else {},
        compiler_params=PARAMS,
        cost_estimate=COST,
    )(spot, *parts, *earlier)


def adagrad(table, state, grads):
    new_state = state + jnp.sum(grads * grads, axis=0, keepdims=True) * (1.0 / grads.shape[0])
    return table - grads * (step_rate / jnp.sqrt(new_state)), new_state


def keep_and_send(core, first, second):
    return jnp.where(core == 0, first, second), jnp.where(core == 0, second, first)


def table_counts(rows, negs, weight):
    place = lax.broadcasted_iota(jnp.int32, (rows, negs.shape[1]), 0)
    return jnp.sum(jnp.where(place == negs, weight, 0.0), axis=1, keepdims=True)


def turned(x, r, half):
    x0, x1, r0, r1 = x[:half], x[half:], r[:half], r[half:]
    return jnp.concatenate([x0 * r0 - x1 * r1, x0 * r1 + x1 * r0], axis=0)


def turned_back(x, r, half):
    x0, x1, r0, r1 = x[:half], x[half:], r[:half], r[half:]
    return x0 * r0 + x1 * r1, x1 * r0 - x0 * r1


EDGE_TILE = 256


def edge_spans(step, bucket, edges):
    tile = EDGE_TILE
    here = pl.multiple_of(step * tile, tile)
    return pl.ds(here, tile), pl.ds(pl.multiple_of(bucket * edges + here, tile), tile)


def lay_down(idx, out_ref):
    out_ref[...] = jnp.transpose(jnp.broadcast_to(idx, (128, idx.shape[1])))


def head_hot_down(heads_down, span, rows):
    return onehot_across(heads_down.at[span], lax.broadcasted_iota(jnp.int32, (1, rows), 1))


def bucket_kernel(
    bucket, core_ref, heads_ref, tails_ref, negs_ref, left_ref, left_sums_ref, right_ref, right_sums_ref, rel_ref, hub_ref,
    left_out, left_sums_out, right_out, keep_out, send_out,
    left_hi, left_lo, both_hi, both_lo, left_grad, both_grad, heads_down,
):
    features, rows = left_ref.shape
    half = features // 2
    core = core_ref[0]
    edges = heads_ref.shape[1]
    hubs = keep_out.shape[1] - edges
    at = slice(bucket, bucket + 1)
    hub_rows = hub_ref[:, bucket * hubs : (bucket + 1) * hubs]
    weight = 1.0 / (negs_ref.shape[1] + hubs)
    counts = table_counts(rows, negs_ref[at], weight)
    lay_down(heads_ref[at], heads_down)
    left_hi[...], left_lo[...] = split(left_ref[...])
    both_hi[:, :rows], both_lo[:, :rows] = split(right_ref[...])
    both_hi[:, rows:], both_lo[:, rows:] = split(hub_rows)
    left_grad[...] = jnp.zeros_like(left_grad)
    both_grad[...] = jnp.zeros_like(both_grad)

    @pl.loop(0, edges // EDGE_TILE)
    def _(step):
        span, wide_span = edge_spans(step, bucket, edges)
        tail_here = lax.broadcasted_iota(jnp.int32, (rows, EDGE_TILE), 0) == tails_ref[at, span]
        h = dot2((left_hi[...], left_lo[...]), onehot(0, rows, heads_ref[at, span]), NN)
        r = rel_ref[:, wide_span]
        q = split(turned(h, r, half))
        both = (both_hi[...], both_lo[...])
        scores = dot3(both, q, TN)
        chance = jax.nn.sigmoid(scores[:rows])
        coef = jnp.concatenate(
            [
                counts * chance + jnp.where(tail_here, chance - 1.0, 0.0),
                weight * jax.nn.sigmoid(scores[rows:]),
            ],
            axis=0,
        )
        coef = split(coef)
        dq = dot3(both, coef, NN)
        both_grad[...] += dot3(q, coef, NT)
        dh = jnp.concatenate(turned_back(dq, r, half), axis=0)
        left_grad[...] += dot2(split(dh), head_hot_down(heads_down, span, rows), NN)
        out_span = pl.ds(pl.multiple_of(hubs + step * EDGE_TILE, 128), EDGE_TILE)
        keep_out[:, out_span], send_out[:, out_span] = keep_and_send(core, *turned_back(dq, h, half))

    left_out[...], left_sums_out[...] = adagrad(left_ref[...], left_sums_ref[...], left_grad[...])
    new_right, new_sums = adagrad(right_ref[...], right_sums_ref[...], both_grad[:, :rows])
    right_out[:features] = new_right
    right_out[features:] = jnp.broadcast_to(new_sums, (right_out.shape[0] - features, rows))
    keep_out[:, :hubs], send_out[:, :hubs] = keep_and_send(core, both_grad[:half, rows:], both_grad[half:, rows:])


def bucket_step(bucket, core, heads, tails, negs, left, left_sums, right, right_sums, rel_rows, hub_rows):
    features, rows = left.shape
    edges, hubs = heads.shape[1], hub_rows.shape[1] // heads.shape[0]
    width = rows + hubs
    shapes = [(features, rows), (1, rows), (features + 8, rows)] + [(features // 2, hubs + edges)] * 2
    return pl.pallas_call(
        functools.partial(bucket_kernel, bucket),
        in_specs=[SMEM] + [VMEM] * 9,
        out_specs=[VMEM] * 5,
        out_shape=[jax.ShapeDtypeStruct(shape, F32) for shape in shapes],
        scratch_shapes=[pltpu.VMEM((features, rows), BF16)] * 2
        + [pltpu.VMEM((features, width), BF16)] * 2
        + [
            pltpu.VMEM((features, rows), F32),
            pltpu.VMEM((features, width), F32),
            pltpu.VMEM((edges, 128), jnp.int32),
        ],
        compiler_params=PARAMS,
        cost_estimate=COST,
    )(core, heads, tails, negs, left, left_sums, right, right_sums, rel_rows, hub_rows)


def hub_kernel(
    bucket, negatives, core_ref, heads_ref, left_ref, rel_ref, hub_ref,
    head_out, query_grad, hub_keep, hub_send,
    left_hi, left_lo, hub_hi, hub_lo, hub_grad,
):
    features, rows = left_ref.shape
    half = features // 2
    edges, hubs = heads_ref.shape[1], hub_keep.shape[1]
    at = slice(bucket, bucket + 1)
    hub_rows = hub_ref[:, bucket * hubs : (bucket + 1) * hubs]
    weight = 1.0 / (negatives + hubs)
    left_hi[...], left_lo[...] = split(left_ref[...])
    hub_hi[...], hub_lo[...] = split(hub_rows)
    hub_grad[...] = jnp.zeros_like(hub_grad)

    @pl.loop(0, edges // EDGE_TILE)
    def _(step):
        span, wide_span = edge_spans(step, bucket, edges)
        h = dot2((left_hi[...], left_lo[...]), onehot(0, rows, heads_ref[at, span]), NN)
        head_out[:, span] = h
        q = split(turned(h, rel_ref[:, wide_span], half))
        hub = (hub_hi[...], hub_lo[...])
        coef = split(weight * jax.nn.sigmoid(dot3(hub, q, TN)))
        query_grad[:, span] = dot3(hub, coef, NN)
        hub_grad[...] += dot3(q, coef, NT)

    hub_keep[...], hub_send[...] = keep_and_send(core_ref[0], hub_grad[:half], hub_grad[half:])


def hub_step(bucket, negatives, core, heads, left, rel_rows, hub_rows):
    features, rows = left.shape
    edges, hubs = heads.shape[1], hub_rows.shape[1] // heads.shape[0]
    shapes = [(features, edges)] * 2 + [(features // 2, hubs)] * 2
    return pl.pallas_call(
        functools.partial(hub_kernel, bucket, negatives),
        in_specs=[SMEM] + [VMEM] * 4,
        out_specs=[VMEM] * 4,
        out_shape=[jax.ShapeDtypeStruct(shape, F32) for shape in shapes],
        scratch_shapes=[pltpu.VMEM((features, rows), BF16)] * 2
        + [pltpu.VMEM((features, hubs), BF16)] * 2
        + [pltpu.VMEM((features, hubs), F32)],
        compiler_params=PARAMS,
        cost_estimate=COST,
    )(core, heads, left, rel_rows, hub_rows)


def tables_kernel(
    bucket, hubs, core_ref, heads_ref, tails_ref, negs_ref, head_rows, query_grad,
    left_ref, left_sums_ref, right_ref, rel_ref,
    left_out, right_out, rel_keep, rel_send,
    right_hi, right_lo, left_grad, right_grad, heads_down,
):
    features, rows = left_ref.shape
    half = features // 2
    edges = heads_ref.shape[1]
    at = slice(bucket, bucket + 1)
    core = core_ref[0]
    counts = table_counts(rows, negs_ref[at], 1.0 / (negs_ref.shape[1] + hubs))
    lay_down(heads_ref[at], heads_down)
    right_hi[...], right_lo[...] = split(right_ref[:features])
    left_grad[...] = jnp.zeros_like(left_grad)
    right_grad[...] = jnp.zeros_like(right_grad)

    @pl.loop(0, edges // EDGE_TILE)
    def _(step):
        span, wide_span = edge_spans(step, bucket, edges)
        tail_here = lax.broadcasted_iota(jnp.int32, (rows, EDGE_TILE), 0) == tails_ref[at, span]
        h, r = head_rows[:, span], rel_ref[:, wide_span]
        q = split(turned(h, r, half))
        right = (right_hi[...], right_lo[...])
        chance = jax.nn.sigmoid(dot3(right, q, TN))
        coef = split(counts * chance + jnp.where(tail_here, chance - 1.0, 0.0))
        dq = dot3(right, coef, NN) + query_grad[:, span]
        right_grad[...] += dot3(q, coef, NT)
        rel_keep[:, span], rel_send[:, span] = keep_and_send(core, *turned_back(dq, h, half))
        dh = jnp.concatenate(turned_back(dq, r, half), axis=0)
        left_grad[...] += dot2(split(dh), head_hot_down(heads_down, span, rows), NN)

    left_out[...], unused = adagrad(left_ref[...], left_sums_ref[...], left_grad[...])
    right_out[...], unused = adagrad(right_ref[:features], right_ref[features : features + 1], right_grad[...])


def tables_step(bucket, hubs, core, heads, tails, negs, head_rows, query_grad, left, left_sums, right, rel_rows):
    features, rows = left.shape
    edges = heads.shape[1]
    shapes = [(features, rows)] * 2 + [(features // 2, edges)] * 2
    return pl.pallas_call(
        functools.partial(tables_kernel, bucket, hubs),
        in_specs=[SMEM] + [VMEM] * 9,
        out_specs=[VMEM] * 4,
        out_shape=[jax.ShapeDtypeStruct(shape, F32) for shape in shapes],
        scratch_shapes=[pltpu.VMEM((features, rows), BF16)] * 2
        + [pltpu.VMEM((features, rows), F32)] * 2
        + [pltpu.VMEM((edges, 128), jnp.int32)],
        compiler_params=PARAMS,
        cost_estimate=COST,
    )(core, heads, tails, negs, head_rows, query_grad, left, left_sums, right, rel_rows)


def from_behind(x, axis, by):
    size = lax.axis_size(axis)
    return lax.ppermute(x, axis, [(i, (i + by) % size) for i in range(size)])


def flipped(x, axis, bit):
    return lax.ppermute(x, axis, [(i, i ^ (1 << bit)) for i in range(lax.axis_size(axis))])


def other_core(x):
    return flipped(x, "blk", 0)


def across(x, place):
    sub_bits = lax.axis_size("sub").bit_length() - 1
    if place < sub_bits:
        return flipped(x, "sub", place)
    return flipped(x, "blk", place - sub_bits + 1)


def stream_orders():
    sub_bits = lax.axis_size("sub").bit_length() - 1
    bits = sub_bits + lax.axis_size("blk").bit_length() - 2
    x, y, z, far = sub_bits, sub_bits + 1, 0, 1
    rest = [p for p in range(bits) if p not in (x, y, z, far)]
    return [[x, y, z, far] + rest, [y, z, x, far] + rest, [z, x, far, y] + rest]


def row_spans(rows, parts):
    ends = [-(-rows * (i + 1) // (8 * parts)) * 8 for i in range(parts - 1)] + [rows]
    return list(zip([0] + ends[:-1], ends))


def shards(
    left_emb, left_state, right_emb, right_state, relation_emb, relation_state, hub_emb, hub_state,
    heads, relations, tails, negatives, hub_ids,
):
    components, half_width, row_count = left_emb.shape
    features = components * half_width
    rel_count, hub_count = relation_emb.shape[2], hub_emb.shape[2]
    left = left_emb.reshape(features, row_count)
    right = right_emb.reshape(features, row_count)
    left_sums = left_state.reshape(1, row_count)
    right_sums = right_state.reshape(1, row_count)
    buckets, edges = heads.shape
    hubs = hub_ids.shape[1]

    core_id = lax.axis_index("blk") % 2
    chip_id = (lax.axis_index("blk") // 2) * lax.axis_size("sub") + lax.axis_index("sub")
    core, chip = core_id.astype(jnp.int32).reshape(1), chip_id.astype(jnp.int32).reshape(1)
    hub_orders = stream_orders()
    rel_orders = hub_orders[:2]
    spans = row_spans(half_width, len(hub_orders))
    hub_pieces = [(0, s, low, high - low) for s, (low, high) in enumerate(spans)]
    rel_spans, rel_pieces = rel_layout(half_width, len(rel_orders))
    heights, rel_heights = [[high - low for low, high in x] for x in (spans, rel_spans)]
    stages = len(hub_orders[0])
    chunks = 1 << stages
    width, rel_width = hub_count // chunks, rel_count // chunks
    hub_lanes, rel_lanes = (0, hubs), (hubs, hubs + edges)

    def exchanged(parts, orders, step):
        return [across(x, order[step]) for x, order in zip(parts, orders)]

    def in_turn(first, then):
        return lax.optimization_barrier((first, then))

    ids = jnp.concatenate([hub_ids, relations], axis=1)
    far_ids = other_core(ids)
    hub_rows, rel_rows = gather_rows(
        hub_emb.reshape(features, hub_count), hub_ids, relation_emb.reshape(features, rel_count), relations
    )
    far_ids, rel_rows = in_turn(far_ids, rel_rows)
    keeps, fars = [], []
    for b in range(buckets - 1):
        if b > 0:
            right, right_sums = right[:features], right[features : features + 1]
        left, left_sums, right, keep, send = bucket_step(
            b, core, heads, tails, negatives, left, left_sums, right, right_sums, rel_rows, hub_rows
        )
        right = from_behind(right, "blk", 1)
        keeps.append(keep)
        fars.append(other_core(send))
    last = buckets - 1
    head_rows, query_grad, hub_keep, hub_send = hub_step(
        last, negatives.shape[1], core, heads, left, rel_rows, hub_rows
    )
    hub_far = other_core(hub_send)
    grads = lambda early, late, lanes: [(x, lanes) for x in early] + [(late, (0, late.shape[1]))]
    send, own = chunk_columns(
        functools.partial(hub_chunks_kernel, hub_orders, spans, hub_lanes),
        heights, width, chip, (ids, far_ids),
        grads(keeps, hub_keep, hub_lanes) + grads(fars, hub_far, hub_lanes), chunks,
    )
    got = exchanged(send, hub_orders, 0)
    left, right, rel_keep, rel_send = tables_step(
        last, hubs, core, heads, tails, negatives, head_rows, query_grad, left, left_sums, right, rel_rows
    )
    rel_far = other_core(rel_send)

    rel_keep, got = in_turn(rel_keep, got)
    send, own = halves(own, got)
    got = exchanged(send, hub_orders, 1)
    own, rel_far = in_turn(own, rel_far)
    rel_out, rel_own = chunk_columns(
        functools.partial(rel_chunks_kernel, rel_orders, rel_pieces, rel_count, rel_lanes),
        rel_heights, width, chip, (ids, far_ids),
        grads(keeps, rel_keep, rel_lanes) + grads(fars, rel_far, rel_lanes), chunks,
    )
    rel_got = exchanged(rel_out, rel_orders, 0)
    for step in range(2, stages):
        rel_own, got = in_turn(rel_own, got)
        send, own = halves(own, got)
        got = exchanged(send, hub_orders, step)
        own, rel_got = in_turn(own, rel_got)
        rel_out, rel_own = halves(rel_own, rel_got)
        rel_got = exchanged(rel_out, rel_orders, step - 1)

    late, rel_own, got = lax.optimization_barrier((jnp.stack([core_id, chip_id]), rel_own, got))
    cut = lambda x, span: lax.dynamic_slice(x, (late[0], 0, late[1] * span), (1, half_width, span))[0]
    cut_sums = lambda x, span: lax.dynamic_slice(x[None], (0, late[1] * span), (1, span))
    totals, squares = squares_of(own, got)
    far_squares = other_core(squares)
    totals, rel_got = in_turn(totals, rel_got)
    rel_out, rel_own = halves(rel_own, rel_got)
    rel_got = exchanged(rel_out, rel_orders, stages - 1)
    rel_own, far_squares = in_turn(rel_own, far_squares)
    have = call(
        functools.partial(hub_update_kernel, spans, features),
        [*totals, squares, far_squares, cut(hub_emb, width), cut_sums(hub_state, width)],
        [x.shape for x in totals],
    )
    got = exchanged(have, hub_orders, stages - 1)
    have, rel_got = in_turn(have, rel_got)
    rel_totals, rel_squares = squares_of(rel_own, rel_got)
    rel_far_squares = other_core(rel_squares)
    rel_totals, got = in_turn(rel_totals, got)
    have = join(have, got)
    got = exchanged(have, hub_orders, stages - 2)
    have, rel_far_squares = in_turn(have, rel_far_squares)
    rel_have = call(
        functools.partial(rel_update_kernel, len(rel_orders), rel_pieces, features),
        [*rel_totals, rel_squares, rel_far_squares, cut(relation_emb, rel_width), cut_sums(relation_state, rel_width)],
        [x.shape for x in rel_totals],
    )
    rel_got = exchanged(rel_have, rel_orders, stages - 1)
    for step in range(stages - 3, -1, -1):
        rel_have, got = in_turn(rel_have, got)
        have = join(have, got)
        got = exchanged(have, hub_orders, step)
        have, rel_got = in_turn(have, rel_got)
        rel_have = join(rel_have, rel_got)
        rel_got = exchanged(rel_have, rel_orders, step + 1)
    rel_have = join(rel_have, rel_got)
    rel_got = exchanged(rel_have, rel_orders, 0)

    mine, others = jnp.concatenate([chip, core]), jnp.concatenate([chip, 1 - core])
    shape = hub_emb.shape
    if width % 128 == 0:
        hub_new = copy_chunks(mine, have, 0, hub_orders, spans, shape, ())
        hub_new = copy_chunks(others, other_core(have), 0, hub_orders, spans, shape, (hub_new,))
        hub_new = copy_chunks(mine, got, 1, hub_orders, spans, shape, (hub_new,))
        hub_new = copy_chunks(others, other_core(got), 1, hub_orders, spans, shape, (hub_new,))
    else:
        hub_new = place_chunks(mine, have, got, hub_orders, hub_pieces, shape, ())
        hub_new = place_chunks(others, other_core(have), other_core(got), hub_orders, hub_pieces, shape, (hub_new,))
    shape = relation_emb.shape
    rel_new = place_chunks(mine, rel_have, rel_got, rel_orders, rel_pieces, shape, ())
    rel_new = place_chunks(
        others, other_core(rel_have), other_core(rel_got), rel_orders, rel_pieces, shape, (rel_new,)
    )
    return (
        left.reshape(components, half_width, row_count),
        right.reshape(components, half_width, row_count),
        rel_new,
        hub_new,
    )


def solution(mesh):
    both = ("blk", "sub")
    block, table, whole = P(None, None, both), P(None, both), P()
    return jax.shard_map(
        shards,
        mesh=mesh,
        in_specs=(block, P(both), block, P(both), whole, whole, whole, whole, table, table, table, table, table),
        out_specs=(block, block, whole, whole),
        check_vma=False,
    )
```

time: 177 us -> 178 us (level)
  waiting for transfers between devices: 76.7 us -> 48.9 us
  starting transfers between devices: 34.8 us -> 54.1 us
  Pallas kernels: 45.9 us -> 55.3 us
    ppermute x40 -> x56, waiting for transfers between devices: 73 us -> 48.9 us  [flipped(): lax.ppermute(x, axis, [(i, i ^ 1 << bit) for i in range(lax.axis_size(axi...]
    ppermute x40 -> x56, starting transfers between devices: 34.3 us -> 53.6 us  [flipped(): lax.ppermute(x, axis, [(i, i ^ 1 << bit) for i in range(lax.axis_size(axi...]
    pallas_call x4 -> x8, Pallas kernels: 14.5 us -> 21 us  [the longest x2 9.26 us: chunk_columns(): pl.pallas_call(functools.partial(kernel, grad_lanes), in_specs=[SMEM] + [...]
    ppermute x2 -> x1, waiting for transfers between devices: 3.69 us -> 0.01 us  [from_behind(): return lax.ppermute(x, axis, [(i, (i + by) % size) for i in range(size)])]
    pallas_call x1, Pallas kernels: 9.2 us -> 11.3 us  [gather_rows(): pl.pallas_call(functools.partial(gather_kernel, hub_steps), grid=(hub_ste...]
    unnamed x42 -> x31, local copies, waits for them, and re-layouts: 11.6 us -> 9.68 us
  transfers between devices with their start and end apart: 42 -> 57, of which waited for: 19 -> 22; matrix products, arithmetic and copies ran while one was open for 2% -> 2% of each run, Pallas kernels for 13% -> 25%
where the time goes in v3:
time: 178 us; the launch traced here: 177 us
  Pallas kernels  55.3 us (31%)
  starting transfers between devices  54.1 us (30%)
  waiting for transfers between devices  48.9 us (27%)
  local copies, waits for them, and re-layouts  13.8 us (8%)
  between operations  4.46 us (3%)
    ppermute x56, starting transfers between devices, flipped(): lax.ppermute(x, axis, [(i, i ^ 1 << bit) for i in range(lax.axis_size(axi...  53.6 us
    ppermute x56, waiting for transfers between devices, flipped(): lax.ppermute(x, axis, [(i, i ^ 1 << bit) for i in range(lax.axis_size(axi...  48.9 us
    pallas_call x1, Pallas kernels, gather_rows(): pl.pallas_call(functools.partial(gather_kernel, hub_steps), grid=(hub_ste...  11.3 us
    unnamed x31, local copies, waits for them, and re-layouts  9.68 us
    pallas_call x1, Pallas kernels, bucket_step(): pl.pallas_call(functools.partial(bucket_kernel, bucket), in_specs=[SMEM]...  9.48 us
    pallas_call x2, Pallas kernels, chunk_columns(): pl.pallas_call(functools.partial(kernel, grad_lanes), in_specs=[SMEM] + [...  9.26 us
    pallas_call x1, Pallas kernels, tables_step(): pl.pallas_call(functools.partial(tables_kernel, bucket, hubs), in_specs=[...  8.28 us
    pallas_call x4, Pallas kernels, copy_chunks(): pl.pallas_call(functools.partial(copy_kernel, orders, spans, upper), in_s...  7.6 us
  transfers between devices with their start and end apart: 57, of which 22 were waited for; matrix products, arithmetic and copies ran while one was open for 2% of the time, Pallas kernels for 25%

profile of v3, /device:TPU:0, one launch (start us, length us, event | category | flops | bytes accessed | tf_op | source)
XLA Modules:
  0.0 176.8 jit_solution(4878295618774066196)
XLA Ops:
  2.6 11.3 %shard_map.156 = (f32[400,512]{1,0:T(8,128)}, f32[400,1024]{1,0:T(8,128)}) custom-call(s32[2,256]{1,0:T(2,128)} %hub_idx.1, s32[2,512]{1,0:T(2,128)} %rel_idx.1, f32[400,4096]{1,0:T(8,128)} %bitcast.25, f32[400,1280]{1,0:T(8,128)} %bitcast.26), custom_call_target="tpu_custom_call" | custom-call | flops 10000 | bytes 10000 | tf_op jit(solution)/shard_map/pallas_call | solution.py:78
  18.8 9.5 %shard_map.157 = (f32[400,512]{1,0:T(8,128)S(1)}, f32[1,512]{1,0:T(1,128)S(1)}, f32[408,512]{1,0:T(8,128)}, f32[200,768]{1,0:T(8,128)S(1)}, f32[200,768]{1,0:T(8,128)}) custom-call(s32[1]{0:T(128)} %bitcast.core_ref, s32[2,512]{1,0:T(2,128)S(1)} %copy-done.10, s32[2,512]{1,0:T(2,128)S(1)} %copy-done.12, s32[2,1024]{1,0:T(2,128)S(1)} %copy-done.11, ...), custom_call_target="tpu_custom_call" | custom-call | flops 10000 | bytes 10000 | tf_op jit(solution)/shard_map/pallas_call | solution.py:446
  28.8 4.1 %shard_map.158 = (f32[400,512]{1,0:T(8,128)S(1)}, f32[400,512]{1,0:T(8,128)S(1)}, f32[200,256]{1,0:T(8,128)S(1)}, f32[200,256]{1,0:T(8,128)}) custom-call(s32[1]{0:T(128)} %bitcast.core_ref, s32[2,512]{1,0:T(2,128)S(1)} %copy-done.10, f32[400,512]{1,0:T(8,128)S(1)} %get-tuple-element.167.left_ref, f32[400,1024]{1,0:T(8,128)S(1)} %copy-done.1, ...), custom_call_target="tpu_custom_call" | custom-call | flops 10000 | bytes 10000 | tf_op jit(solution)/shard_map/pallas_call | solution.py:496
  34.7 2.6 %collective-permute-start.3 = (f32[200,256]{1,0:T(8,128)}, f32[200,256]{1,0:T(8,128)S(1)}, u32[]{:S(2)}, u32[]{:S(2)}) collective-permute-start(f32[200,256]{1,0:T(8,128)} %get-tuple-element.179), channel_id=1, source_target_pairs={{0,4},{4,0},{8,12},{12,8},{16,20},{20,16},{24,28},{28,24},{1,5},{5... | collective-permute-start | bytes 614408 | tf_op jit(solution)/shard_map/ppermute | solution.py:568
  38.6 5.0 %shard_map.160 = (f32[8,72,256]{2,1,0:T(8,128)S(1)}, f32[8,64,256]{2,1,0:T(8,128)S(1)}, f32[8,64,256]{2,1,0:T(8,128)S(1)}, f32[8,72,256]{2,1,0:T(8,128)S(1)}, f3...) custom-call(s32[1]{0:T(128)} %bitcast.9.chip_ref, s32[2,768]{1,0:T(2,128)S(1)} %constant_dynamic-update-slice_fusion.refs_0_, ...), custom_call_target="tpu_custom_call" | custom-call | flops 10000 | bytes 10000 | tf_op jit(solution)/shard_map/pallas_call | solution.py:187
  45.5 1.8 %collective-permute-start.6 = (f32[8,64,256]{2,1,0:T(8,128)S(1)}, f32[8,64,256]{2,1,0:T(8,128)S(1)}, u32[]{:S(2)}, u32[]{:S(2)}) collective-permute-start(f32[8,64,256]{2,1,0:T(8,128)S(1)} %get-tuple-element.182), channel_id=1, source_target_pairs={{0,1},{1,0},{2,3},{3,2},{4,5},{5,4},{6,7},{7,6},{8,9},{9,8},{10,11... | collective-permute-start | bytes 1572872 | tf_op jit(solution)/shard_map/ppermute | solution.py:568
  49.6 8.3 %shard_map.159 = (f32[400,512]{1,0:T(8,128)}, f32[400,512]{1,0:T(8,128)}, f32[200,512]{1,0:T(8,128)S(1)}, f32[200,512]{1,0:T(8,128)S(1)}) custom-call(s32[1]{0:T(128)} %bitcast.core_ref, s32[2,512]{1,0:T(2,128)S(1)} %copy-done.10, s32[2,512]{1,0:T(2,128)S(1)} %copy-done.12, s32[2,1024]{1,0:T(2,128)S(1)} %copy-done.11, f32[400,512]{1,0:T(8,128)S(1)} %copy-done.7, ...), custom_call_target="tpu_custom_call" | custom-call | flops 10000 | bytes 10000 | tf_op jit(solution)/shard_map/pallas_call | solution.py:549
  63.2 4.3 %shard_map.162 = (f32[8,40,256]{2,1,0:T(8,128)S(1)}, f32[8,32,256]{2,1,0:T(8,128)S(1)}, f32[8,40,256]{2,1,0:T(8,128)S(1)}, f32[8,32,256]{2,1,0:T(8,128)S(1)}) custom-call(s32[1]{0:T(128)} %bitcast.9.chip_ref, s32[2,768]{1,0:T(2,128)S(1)} %constant_dynamic-update-slice_fusion.refs_0_, s32[2,768]{1,0:T(2,128)S(1)} %collective-permute-done.refs_1_, ...), custom_call_target="tpu_custom_call" | custom-call | flops 10000 | bytes 10000 | tf_op jit(solution)/shard_map/pallas_call | solution.py:187
  72.0 2.6 %collective-permute-start.15 = (f32[2,64,256]{2,1,0:T(8,128)S(1)}, f32[2,64,256]{2,1,0:T(8,128)S(1)}, u32[]{:S(2)}, u32[]{:S(2)}) collective-permute-start(f32[2,64,256]{2,1,0:T(8,128)S(1)} %get-tuple-element.219), channel_id=1, source_target_pairs={{0,2},{1,3},{2,0},{3,1},{4,6},{5,7},{6,4},{7,5},{8,10},{9,11},{10,... | collective-permute-start | bytes 393224 | tf_op jit(solution)/shard_map/ppermute | solution.py:568
  79.4 2.6 %collective-permute-start.18 = (f32[1,72,256]{2,1,0:T(8,128)S(1)}, f32[1,72,256]{2,1,0:T(8,128)S(1)}, u32[]{:S(2)}, u32[]{:S(2)}) collective-permute-start(f32[1,72,256]{2,1,0:T(8,128)S(1)} %get-tuple-element.237), channel_id=1, source_target_pairs={{0,2},{1,3},{2,0},{3,1},{4,6},{5,7},{6,4},{7,5},{8,10},{9,11},{10,... | collective-permute-start | bytes 221192 | tf_op jit(solution)/shard_map/ppermute | solution.py:568
  84.6 2.9 %collective-permute-done.19.refs_4_ = f32[1,64,256]{2,1,0:T(8,128)S(1)} collective-permute-done((f32[1,64,256]{2,1,0:T(8,128)S(1)}, f32[1,64,256]{2,1,0:T(8,128)S(1)}, u32[]{:S(2)}, u32[]{:S(2)}) %collective-permute-start.19) | collective-permute-done | bytes 65568 | tf_op jit(solution)/shard_map/ppermute | solution.py:568
  95.7 2.2 %collective-permute-start.26 = (f32[1,72,256]{2,1,0:T(8,128)S(1)}, f32[1,72,256]{2,1,0:T(8,128)S(1)}, u32[]{:S(2)}, u32[]{:S(2)}) collective-permute-start(f32[1,72,256]{2,1,0:T(8,128)S(1)} %get-tuple-element.277.refs_0_), channel_id=1, source_target_pairs={{0,2},{1,3},{2,0},{3,1},{4,6},{5,7},{6,4},{7,5},{8,10},{9,11},{10,... | collective-permute-start | bytes 221192 | tf_op jit(solution)/shard_map/ppermute | solution.py:568
  99.4 2.1 %collective-permute-start.24 = (f32[1,40,256]{2,1,0:T(8,128)S(1)}, f32[1,40,256]{2,1,0:T(8,128)S(1)}, u32[]{:S(2)}, u32[]{:S(2)}) collective-permute-start(f32[1,40,256]{2,1,0:T(8,128)S(1)} %get-tuple-element.268), channel_id=1, source_target_pairs={{0,2},{1,3},{2,0},{3,1},{4,6},{5,7},{6,4},{7,5},{8,10},{9,11},{10,... | collective-permute-start | bytes 122888 | tf_op jit(solution)/shard_map/ppermute | solution.py:568
  103.0 5.3 %collective-permute-done.25.refs_3_ = f32[1,32,256]{2,1,0:T(8,128)S(1)} collective-permute-done((f32[1,32,256]{2,1,0:T(8,128)S(1)}, f32[1,32,256]{2,1,0:T(8,128)S(1)}, u32[]{:S(2)}, u32[]{:S(2)}) %collective-permute-start.25) | collective-permute-done | bytes 32800 | tf_op jit(solution)/shard_map/ppermute | solution.py:568
  109.4 2.5 %collective-permute-start.32 = (f32[2,64,256]{2,1,0:T(8,128)S(1)}, f32[2,64,256]{2,1,0:T(8,128)S(1)}, u32[]{:S(2)}, u32[]{:S(2)}) collective-permute-start(f32[2,64,256]{2,1,0:T(8,128)S(1)} %get-tuple-element.293.refs_2_), channel_id=1, source_target_pairs={{0,2},{1,3},{2,0},{3,1},{4,6},{5,7},{6,4},{7,5},{8,10},{9,11},{10,... | collective-permute-start | bytes 393224 | tf_op jit(solution)/shard_map/ppermute | solution.py:568
  114.5 3.6 %collective-permute-done.32.refs_5_ = f32[2,64,256]{2,1,0:T(8,128)S(1)} collective-permute-done((f32[2,64,256]{2,1,0:T(8,128)S(1)}, f32[2,64,256]{2,1,0:T(8,128)S(1)}, u32[]{:S(2)}, u32[]{:S(2)}) %collective-permute-start.32) | collective-permute-done | bytes 131104 | tf_op jit(solution)/shard_map/ppermute | solution.py:568
  120.4 2.0 %collective-permute-start.33 = (f32[1,40,256]{2,1,0:T(8,128)S(1)}, f32[1,40,256]{2,1,0:T(8,128)S(1)}, u32[]{:S(2)}, u32[]{:S(2)}) collective-permute-start(f32[1,40,256]{2,1,0:T(8,128)S(1)} %get-tuple-element.289.refs_0_), channel_id=1, source_target_pairs={{0,2},{1,3},{2,0},{3,1},{4,6},{5,7},{6,4},{7,5},{8,10},{9,11},{10,... | collective-permute-start | bytes 122888 | tf_op jit(solution)/shard_map/ppermute | solution.py:568
  123.3 4.1 %collective-permute-done.34.refs_3_ = f32[1,32,256]{2,1,0:T(8,128)S(1)} collective-permute-done((f32[1,32,256]{2,1,0:T(8,128)S(1)}, f32[1,32,256]{2,1,0:T(8,128)S(1)}, u32[]{:S(2)}, u32[]{:S(2)}) %collective-permute-start.34) | collective-permute-done | bytes 32800 | tf_op jit(solution)/shard_map/ppermute | solution.py:568
  129.1 3.2 %collective-permute-done.39.refs_3_ = f32[2,32,256]{2,1,0:T(8,128)S(1)} collective-permute-done((f32[2,32,256]{2,1,0:T(8,128)S(1)}, f32[2,32,256]{2,1,0:T(8,128)S(1)}, u32[]{:S(2)}, u32[]{:S(2)}) %collective-permute-start.39) | collective-permute-done | bytes 65568 | tf_op jit(solution)/shard_map/ppermute | solution.py:568
  133.3 1.8 %collective-permute-start.41 = (f32[4,32,256]{2,1,0:T(8,128)S(1)}, f32[4,32,256]{2,1,0:T(8,128)S(1)}, u32[]{:S(2)}, u32[]{:S(2)}) collective-permute-start(f32[4,32,256]{2,1,0:T(8,128)S(1)} %get-tuple-element.318.refs_1_), channel_id=1, source_target_pairs={{0,1},{1,0},{2,3},{3,2},{4,5},{5,4},{6,7},{7,6},{8,9},{9,8},{10,11... | collective-permute-start | bytes 393224 | tf_op jit(solution)/shard_map/ppermute | solution.py:568
  135.1 3.2 %collective-permute-done.41.refs_3_ = f32[4,32,256]{2,1,0:T(8,128)S(1)} collective-permute-done((f32[4,32,256]{2,1,0:T(8,128)S(1)}, f32[4,32,256]{2,1,0:T(8,128)S(1)}, u32[]{:S(2)}, u32[]{:S(2)}) %collective-permute-start.41) | collective-permute-done | bytes 131104 | tf_op jit(solution)/shard_map/ppermute | solution.py:568
  140.1 1.9 %collective-permute-start.44 = (f32[8,40,256]{2,1,0:T(8,128)S(1)}, f32[8,40,256]{2,1,0:T(8,128)S(1)}, u32[]{:S(2)}, u32[]{:S(2)}) collective-permute-start(f32[8,40,256]{2,1,0:T(8,128)S(1)} %get-tuple-element.319.refs_0_), channel_id=1, source_target_pairs={{0,8},{4,12},{8,0},{12,4},{16,24},{20,28},{24,16},{28,20},{1,9},{5... | collective-permute-start | bytes 983048 | tf_op jit(solution)/shard_map/ppermute | solution.py:568
  142.5 3.7 %collective-permute-done.46.refs_3_ = f32[8,32,256]{2,1,0:T(8,128)S(1)} collective-permute-done((f32[8,32,256]{2,1,0:T(8,128)S(1)}, f32[8,32,256]{2,1,0:T(8,128)S(1)}, u32[]{:S(2)}, u32[]{:S(2)}) %collective-permute-start.46) | collective-permute-done | bytes 262176 | tf_op jit(solution)/shard_map/ppermute | solution.py:568
  148.4 2.3 %collective-permute-done.44.refs_2_ = f32[8,40,256]{2,1,0:T(8,128)S(1)} collective-permute-done((f32[8,40,256]{2,1,0:T(8,128)S(1)}, f32[8,40,256]{2,1,0:T(8,128)S(1)}, u32[]{:S(2)}, u32[]{:S(2)}) %collective-permute-start.44) | collective-permute-done | bytes 327712 | tf_op jit(solution)/shard_map/ppermute | solution.py:568
  150.7 1.9 %collective-permute-start.52 = (f32[8,64,256]{2,1,0:T(8,128)S(1)}, f32[8,64,256]{2,1,0:T(8,128)S(1)}, u32[]{:S(2)}, u32[]{:S(2)}) collective-permute-start(f32[8,64,256]{2,1,0:T(8,128)S(1)} %get-tuple-element.323.refs_2_), channel_id=1, source_target_pairs={{0,1},{1,0},{2,3},{3,2},{4,5},{5,4},{6,7},{7,6},{8,9},{9,8},{10,11... | collective-permute-start | bytes 1572872 | tf_op jit(solution)/shard_map/ppermute | solution.py:568
  153.1 9.9 %collective-permute-done.48.refs_0_ = f32[8,72,256]{2,1,0:T(8,128)S(1)} collective-permute-done((f32[8,72,256]{2,1,0:T(8,128)S(1)}, f32[8,72,256]{2,1,0:T(8,128)S(1)}, u32[]{:S(2)}, u32[]{:S(2)}) %collective-permute-start.48) | collective-permute-done | bytes 589856 | tf_op jit(solution)/shard_map/ppermute | solution.py:568
  164.8 1.9 %shard_map.180.refs_3_ = f32[2,200,4096]{2,1,0:T(8,128)} custom-call(s32[2]{0:T(128)S(1)} %pad_add_fusion.2.spot_ref, f32[8,72,256]{2,1,0:T(8,128)S(1)} %get-tuple-element.321.refs_0_, f32[8,64,256]{2,1,0:T(8,128)S(1)} %get-tuple-element.322.refs_1_, f32[8,64,256]{2,1,0:T(8,128)S(1)} %get-tuple-element.323.refs_2_), custom_call_target="tpu_custom_call" | custom-call | flops 10000 | bytes 10000 | tf_op jit(solution)/shard_map/pallas_call | solution.py:335
  166.7 1.9 %shard_map.181.refs_3_ = f32[2,200,4096]{2,1,0:T(8,128)} custom-call(s32[2]{0:T(128)S(1)} %pad_add_fusion.spot_ref, f32[8,72,256]{2,1,0:T(8,128)S(1)} %collective-permute-done.54.refs_0_, f32[8,64,256]{2,1,0:T(8,128)S(1)} %collective-permute-done.55.refs_1_, f32[8,64,256]{2,1,0:T(8,128)S(1)} %collective-permute-done.56.refs_2_, ...), custom_call_target="tpu_custom_call", output_to_operand_aliasing={{}: (4, {})} | custom-call | flops 10000 | bytes 10000 | tf_op jit(solution)/shard_map/pallas_call | solution.py:335
  168.6 2.1 %shard_map.178.refs_4_ = f32[2,200,1280]{2,1,0:T(8,128)} custom-call(s32[2]{0:T(128)S(1)} %pad_add_fusion.2.spot_ref, f32[8,40,256]{2,1,0:T(8,128)S(1)} %get-tuple-element.319.refs_0_, f32[8,32,256]{2,1,0:T(8,128)S(1)} %get-tuple-element.320.refs_1_, f32[8,40,256]{2,1,0:T(8,128)S(1)} %collective-permute-done.44.refs_2_, ...), custom_call_target="tpu_custom_call" | custom-call | flops 10000 | bytes 10000 | tf_op jit(solution)/shard_map/pallas_call | solution.py:301
  170.7 1.9 %shard_map.182.refs_3_ = f32[2,200,4096]{2,1,0:T(8,128)} custom-call(s32[2]{0:T(128)S(1)} %pad_add_fusion.2.spot_ref, f32[8,72,256]{2,1,0:T(8,128)S(1)} %collective-permute-done.48.refs_0_, f32[8,64,256]{2,1,0:T(8,128)S(1)} %collective-permute-done.50.refs_1_, f32[8,64,256]{2,1,0:T(8,128)S(1)} %collective-permute-done.52.refs_2_, ...), custom_call_target="tpu_custom_call", output_to_operand_aliasing={{}: (4, {})} | custom-call | flops 10000 | bytes 10000 | tf_op jit(solution)/shard_map/pallas_call | solution.py:335
  172.6 2.1 %shard_map.179 = f32[2,200,1280]{2,1,0:T(8,128)} custom-call(s32[2]{0:T(128)S(1)} %pad_add_fusion.spot_ref, f32[8,40,256]{2,1,0:T(8,128)S(1)} %collective-permute-done.42.refs_0_, f32[8,32,256]{2,1,0:T(8,128)S(1)} %collective-permute-done.43.refs_1_, f32[8,40,256]{2,1,0:T(8,128)S(1)} %collective-permute-done.45.refs_2_, ...), custom_call_target="tpu_custom_call", output_to_operand_aliasing={{}: (5, {})} | custom-call | flops 10000 | bytes 10000 | tf_op jit(solution)/shard_map/pallas_call | solution.py:301
  174.7 1.9 %shard_map.183 = f32[2,200,4096]{2,1,0:T(8,128)} custom-call(s32[2]{0:T(128)S(1)} %pad_add_fusion.spot_ref, f32[8,72,256]{2,1,0:T(8,128)S(1)} %collective-permute-done.49.refs_0_, f32[8,64,256]{2,1,0:T(8,128)S(1)} %collective-permute-done.51.refs_1_, f32[8,64,256]{2,1,0:T(8,128)S(1)} %collective-permute-done.53.refs_2_, ...), custom_call_target="tpu_custom_call", output_to_operand_aliasing={{}: (4, {})} | custom-call | flops 10000 | bytes 10000 | tf_op jit(solution)/shard_map/pallas_call | solution.py:335
  (150 shorter events, 56.0 us)
Async XLA Ops:
  2.1 11.8 %collective-permute-start = (s32[2,768]{1,0:T(2,128)S(1)}, s32[2,768]{1,0:T(2,128)S(1)}, u32[]{:S(2)}, u32[]{:S(2)}) collective-permute-start(s32[2,768]{1,0:T(2,128)S(1)} %constant_dynamic-update-slice_fusion.refs_0_), channel_id=1, source_target_pairs={{0,4},{4,0},{8,12},{12,8},{16,20},{20,16},{24,28},{28,24},{1,5},{5... | collective-permute-start | bytes 18440 | tf_op jit(solution)/shard_map/ppermute | solution.py:568
  28.3 10.3 %collective-permute-start.2 = (f32[200,768]{1,0:T(8,128)}, f32[200,768]{1,0:T(8,128)}, u32[]{:S(2)}, u32[]{:S(2)}) collective-permute-start(f32[200,768]{1,0:T(8,128)} %get-tuple-element.178), channel_id=1, source_target_pairs={{0,4},{4,0},{8,12},{12,8},{16,20},{20,16},{24,28},{28,24},{1,5},{5... | collective-permute-start | bytes 1843208 | tf_op jit(solution)/shard_map/ppermute | solution.py:568
  28.3 18.9 %collective-permute-start.1 = (f32[408,512]{1,0:T(8,128)}, f32[408,512]{1,0:T(8,128)}, u32[]{:S(2)}, u32[]{:S(2)}) collective-permute-start(f32[408,512]{1,0:T(8,128)} %get-tuple-element.171), channel_id=1, source_target_pairs={{0,4},{4,8},{8,12},{12,16},{16,20},{20,24},{24,28},{28,0},{1,5},{5... | collective-permute-start | bytes 2506760 | tf_op jit(solution)/shard_map/ppermute | solution.py:564
  43.6 15.7 %collective-permute-start.4 = (f32[8,72,256]{2,1,0:T(8,128)S(1)}, f32[8,72,256]{2,1,0:T(8,128)S(1)}, u32[]{:S(2)}, u32[]{:S(2)}) collective-permute-start(f32[8,72,256]{2,1,0:T(8,128)S(1)} %get-tuple-element.180), channel_id=1, source_target_pairs={{0,8},{4,12},{8,0},{12,4},{16,24},{20,28},{24,16},{28,20},{1,9},{5... | collective-permute-start | bytes 1769480 | tf_op jit(solution)/shard_map/ppermute | solution.py:568
  45.2 13.9 %collective-permute-start.5 = (f32[8,64,256]{2,1,0:T(8,128)S(1)}, f32[8,64,256]{2,1,0:T(8,128)S(1)}, u32[]{:S(2)}, u32[]{:S(2)}) collective-permute-start(f32[8,64,256]{2,1,0:T(8,128)S(1)} %get-tuple-element.181), channel_id=1, source_target_pairs={{0,16},{4,20},{8,24},{12,28},{16,0},{20,4},{24,8},{28,12},{1,17},{... | collective-permute-start | bytes 1572872 | tf_op jit(solution)/shard_map/ppermute | solution.py:568
  45.5 13.7 %collective-permute-start.6 = (f32[8,64,256]{2,1,0:T(8,128)S(1)}, f32[8,64,256]{2,1,0:T(8,128)S(1)}, u32[]{:S(2)}, u32[]{:S(2)}) collective-permute-start(f32[8,64,256]{2,1,0:T(8,128)S(1)} %get-tuple-element.182), channel_id=1, source_target_pairs={{0,1},{1,0},{2,3},{3,2},{4,5},{5,4},{6,7},{7,6},{8,9},{9,8},{10,11... | collective-permute-start | bytes 1572872 | tf_op jit(solution)/shard_map/ppermute | solution.py:568
  59.4 10.1 %collective-permute-start.8 = (f32[4,72,256]{2,1,0:T(8,128)S(1)}, f32[4,72,256]{2,1,0:T(8,128)S(1)}, u32[]{:S(2)}, u32[]{:S(2)}) collective-permute-start(f32[4,72,256]{2,1,0:T(8,128)S(1)} %get-tuple-element.197), channel_id=1, source_target_pairs={{0,16},{4,20},{8,24},{12,28},{16,0},{20,4},{24,8},{28,12},{1,17},{... | collective-permute-start | bytes 884744 | tf_op jit(solution)/shard_map/ppermute | solution.py:568
  61.0 8.5 %collective-permute-start.10 = (f32[4,64,256]{2,1,0:T(8,128)S(1)}, f32[4,64,256]{2,1,0:T(8,128)S(1)}, u32[]{:S(2)}, u32[]{:S(2)}) collective-permute-start(f32[4,64,256]{2,1,0:T(8,128)S(1)} %get-tuple-element.199), channel_id=1, source_target_pairs={{0,8},{4,12},{8,0},{12,4},{16,24},{20,28},{24,16},{28,20},{1,9},{5... | collective-permute-start | bytes 786440 | tf_op jit(solution)/shard_map/ppermute | solution.py:568
  67.4 9.8 %collective-permute-start.11 = (f32[8,40,256]{2,1,0:T(8,128)S(1)}, f32[8,40,256]{2,1,0:T(8,128)S(1)}, u32[]{:S(2)}, u32[]{:S(2)}) collective-permute-start(f32[8,40,256]{2,1,0:T(8,128)S(1)} %get-tuple-element.211), channel_id=1, source_target_pairs={{0,8},{4,12},{8,0},{12,4},{16,24},{20,28},{24,16},{28,20},{1,9},{5... | collective-permute-start | bytes 983048 | tf_op jit(solution)/shard_map/ppermute | solution.py:568
  69.6 9.7 %collective-permute-start.13 = (f32[2,72,256]{2,1,0:T(8,128)S(1)}, f32[2,72,256]{2,1,0:T(8,128)S(1)}, u32[]{:S(2)}, u32[]{:S(2)}) collective-permute-start(f32[2,72,256]{2,1,0:T(8,128)S(1)} %get-tuple-element.217), channel_id=1, source_target_pairs={{0,1},{1,0},{2,3},{3,2},{4,5},{5,4},{6,7},{7,6},{8,9},{9,8},{10,11... | collective-permute-start | bytes 442376 | tf_op jit(solution)/shard_map/ppermute | solution.py:568
  79.4 8.1 %collective-permute-start.18 = (f32[1,72,256]{2,1,0:T(8,128)S(1)}, f32[1,72,256]{2,1,0:T(8,128)S(1)}, u32[]{:S(2)}, u32[]{:S(2)}) collective-permute-start(f32[1,72,256]{2,1,0:T(8,128)S(1)} %get-tuple-element.237), channel_id=1, source_target_pairs={{0,2},{1,3},{2,0},{3,1},{4,6},{5,7},{6,4},{7,5},{8,10},{9,11},{10,... | collective-permute-start | bytes 221192 | tf_op jit(solution)/shard_map/ppermute | solution.py:568
  95.7 12.6 %collective-permute-start.26 = (f32[1,72,256]{2,1,0:T(8,128)S(1)}, f32[1,72,256]{2,1,0:T(8,128)S(1)}, u32[]{:S(2)}, u32[]{:S(2)}) collective-permute-start(f32[1,72,256]{2,1,0:T(8,128)S(1)} %get-tuple-element.277.refs_0_), channel_id=1, source_target_pairs={{0,2},{1,3},{2,0},{3,1},{4,6},{5,7},{6,4},{7,5},{8,10},{9,11},{10,... | collective-permute-start | bytes 221192 | tf_op jit(solution)/shard_map/ppermute | solution.py:568
  97.9 10.4 %collective-permute-start.27 = (f32[1,64,256]{2,1,0:T(8,128)S(1)}, f32[1,64,256]{2,1,0:T(8,128)S(1)}, u32[]{:S(2)}, u32[]{:S(2)}) collective-permute-start(f32[1,64,256]{2,1,0:T(8,128)S(1)} %get-tuple-element.278.refs_1_), channel_id=1, source_target_pairs={{0,2},{1,3},{2,0},{3,1},{4,6},{5,7},{6,4},{7,5},{8,10},{9,11},{10,... | collective-permute-start | bytes 196616 | tf_op jit(solution)/shard_map/ppermute | solution.py:568
  98.7 9.6 %collective-permute-start.28 = (f32[1,64,256]{2,1,0:T(8,128)S(1)}, f32[1,64,256]{2,1,0:T(8,128)S(1)}, u32[]{:S(2)}, u32[]{:S(2)}) collective-permute-start(f32[1,64,256]{2,1,0:T(8,128)S(1)} %get-tuple-element.279.refs_2_), channel_id=1, source_target_pairs={{0,16},{4,20},{8,24},{12,28},{16,0},{20,4},{24,8},{28,12},{1,17},{... | collective-permute-start | bytes 196616 | tf_op jit(solution)/shard_map/ppermute | solution.py:568
  99.4 8.9 %collective-permute-start.24 = (f32[1,40,256]{2,1,0:T(8,128)S(1)}, f32[1,40,256]{2,1,0:T(8,128)S(1)}, u32[]{:S(2)}, u32[]{:S(2)}) collective-permute-start(f32[1,40,256]{2,1,0:T(8,128)S(1)} %get-tuple-element.268), channel_id=1, source_target_pairs={{0,2},{1,3},{2,0},{3,1},{4,6},{5,7},{6,4},{7,5},{8,10},{9,11},{10,... | collective-permute-start | bytes 122888 | tf_op jit(solution)/shard_map/ppermute | solution.py:568
  108.4 9.7 %collective-permute-start.30 = (f32[2,72,256]{2,1,0:T(8,128)S(1)}, f32[2,72,256]{2,1,0:T(8,128)S(1)}, u32[]{:S(2)}, u32[]{:S(2)}) collective-permute-start(f32[2,72,256]{2,1,0:T(8,128)S(1)} %get-tuple-element.291.refs_0_), channel_id=1, source_target_pairs={{0,1},{1,0},{2,3},{3,2},{4,5},{5,4},{6,7},{7,6},{8,9},{9,8},{10,11... | collective-permute-start | bytes 442376 | tf_op jit(solution)/shard_map/ppermute | solution.py:568
  109.4 8.7 %collective-permute-start.32 = (f32[2,64,256]{2,1,0:T(8,128)S(1)}, f32[2,64,256]{2,1,0:T(8,128)S(1)}, u32[]{:S(2)}, u32[]{:S(2)}) collective-permute-start(f32[2,64,256]{2,1,0:T(8,128)S(1)} %get-tuple-element.293.refs_2_), channel_id=1, source_target_pairs={{0,2},{1,3},{2,0},{3,1},{4,6},{5,7},{6,4},{7,5},{8,10},{9,11},{10,... | collective-permute-start | bytes 393224 | tf_op jit(solution)/shard_map/ppermute | solution.py:568
  118.2 10.8 %collective-permute-start.35 = (f32[4,72,256]{2,1,0:T(8,128)S(1)}, f32[4,72,256]{2,1,0:T(8,128)S(1)}, u32[]{:S(2)}, u32[]{:S(2)}) collective-permute-start(f32[4,72,256]{2,1,0:T(8,128)S(1)} %get-tuple-element.306.refs_0_), channel_id=1, source_target_pairs={{0,16},{4,20},{8,24},{12,28},{16,0},{20,4},{24,8},{28,12},{1,17},{... | collective-permute-start | bytes 884744 | tf_op jit(solution)/shard_map/ppermute | solution.py:568
  118.9 10.0 %collective-permute-start.36 = (f32[4,64,256]{2,1,0:T(8,128)S(1)}, f32[4,64,256]{2,1,0:T(8,128)S(1)}, u32[]{:S(2)}, u32[]{:S(2)}) collective-permute-start(f32[4,64,256]{2,1,0:T(8,128)S(1)} %get-tuple-element.307.refs_1_), channel_id=1, source_target_pairs={{0,1},{1,0},{2,3},{3,2},{4,5},{5,4},{6,7},{7,6},{8,9},{9,8},{10,11... | collective-permute-start | bytes 786440 | tf_op jit(solution)/shard_map/ppermute | solution.py:568
  118.9 10.0 %collective-permute-start.37 = (f32[4,64,256]{2,1,0:T(8,128)S(1)}, f32[4,64,256]{2,1,0:T(8,128)S(1)}, u32[]{:S(2)}, u32[]{:S(2)}) collective-permute-start(f32[4,64,256]{2,1,0:T(8,128)S(1)} %get-tuple-element.308.refs_2_), channel_id=1, source_target_pairs={{0,8},{4,12},{8,0},{12,4},{16,24},{20,28},{24,16},{28,20},{1,9},{5... | collective-permute-start | bytes 786440 | tf_op jit(solution)/shard_map/ppermute | solution.py:568
  140.1 12.5 %collective-permute-start.55 = (f32[8,64,256]{2,1,0:T(8,128)S(1)}, f32[8,64,256]{2,1,0:T(8,128)S(1)}, u32[]{:S(2)}, u32[]{:S(2)}) collective-permute-start(f32[8,64,256]{2,1,0:T(8,128)S(1)} %get-tuple-element.322.refs_1_), channel_id=1, source_target_pairs={{0,4},{4,0},{8,12},{12,8},{16,20},{20,16},{24,28},{28,24},{1,5},{5... | collective-permute-start | bytes 1572872 | tf_op jit(solution)/shard_map/ppermute | solution.py:568
  140.1 10.6 %collective-permute-start.44 = (f32[8,40,256]{2,1,0:T(8,128)S(1)}, f32[8,40,256]{2,1,0:T(8,128)S(1)}, u32[]{:S(2)}, u32[]{:S(2)}) collective-permute-start(f32[8,40,256]{2,1,0:T(8,128)S(1)} %get-tuple-element.319.refs_0_), channel_id=1, source_target_pairs={{0,8},{4,12},{8,0},{12,4},{16,24},{20,28},{24,16},{28,20},{1,9},{5... | collective-permute-start | bytes 983048 | tf_op jit(solution)/shard_map/ppermute | solution.py:568
  142.2 10.4 %collective-permute-start.42 = (f32[8,40,256]{2,1,0:T(8,128)S(1)}, f32[8,40,256]{2,1,0:T(8,128)S(1)}, u32[]{:S(2)}, u32[]{:S(2)}) collective-permute-start(f32[8,40,256]{2,1,0:T(8,128)S(1)} %get-tuple-element.319.refs_0_), channel_id=1, source_target_pairs={{0,4},{4,0},{8,12},{12,8},{16,20},{20,16},{24,28},{28,24},{1,5},{5... | collective-permute-start | bytes 983048 | tf_op jit(solution)/shard_map/ppermute | solution.py:568
  146.2 16.8 %collective-permute-start.48 = (f32[8,72,256]{2,1,0:T(8,128)S(1)}, f32[8,72,256]{2,1,0:T(8,128)S(1)}, u32[]{:S(2)}, u32[]{:S(2)}) collective-permute-start(f32[8,72,256]{2,1,0:T(8,128)S(1)} %get-tuple-element.321.refs_0_), channel_id=1, source_target_pairs={{0,8},{4,12},{8,0},{12,4},{16,24},{20,28},{24,16},{28,20},{1,9},{5... | collective-permute-start | bytes 1769480 | tf_op jit(solution)/shard_map/ppermute | solution.py:568
  146.9 16.2 %collective-permute-start.50 = (f32[8,64,256]{2,1,0:T(8,128)S(1)}, f32[8,64,256]{2,1,0:T(8,128)S(1)}, u32[]{:S(2)}, u32[]{:S(2)}) collective-permute-start(f32[8,64,256]{2,1,0:T(8,128)S(1)} %get-tuple-element.322.refs_1_), channel_id=1, source_target_pairs={{0,16},{4,20},{8,24},{12,28},{16,0},{20,4},{24,8},{28,12},{1,17},{... | collective-permute-start | bytes 1572872 | tf_op jit(solution)/shard_map/ppermute | solution.py:568
  150.7 13.3 %collective-permute-start.52 = (f32[8,64,256]{2,1,0:T(8,128)S(1)}, f32[8,64,256]{2,1,0:T(8,128)S(1)}, u32[]{:S(2)}, u32[]{:S(2)}) collective-permute-start(f32[8,64,256]{2,1,0:T(8,128)S(1)} %get-tuple-element.323.refs_2_), channel_id=1, source_target_pairs={{0,1},{1,0},{2,3},{3,2},{4,5},{5,4},{6,7},{7,6},{8,9},{9,8},{10,11... | collective-permute-start | bytes 1572872 | tf_op jit(solution)/shard_map/ppermute | solution.py:568
  152.6 11.9 %collective-permute-start.54 = (f32[8,72,256]{2,1,0:T(8,128)S(1)}, f32[8,72,256]{2,1,0:T(8,128)S(1)}, u32[]{:S(2)}, u32[]{:S(2)}) collective-permute-start(f32[8,72,256]{2,1,0:T(8,128)S(1)} %get-tuple-element.321.refs_0_), channel_id=1, source_target_pairs={{0,4},{4,0},{8,12},{12,8},{16,20},{20,16},{24,28},{28,24},{1,5},{5... | collective-permute-start | bytes 1769480 | tf_op jit(solution)/shard_map/ppermute | solution.py:568
  152.6 11.4 %collective-permute-start.56 = (f32[8,64,256]{2,1,0:T(8,128)S(1)}, f32[8,64,256]{2,1,0:T(8,128)S(1)}, u32[]{:S(2)}, u32[]{:S(2)}) collective-permute-start(f32[8,64,256]{2,1,0:T(8,128)S(1)} %get-tuple-element.323.refs_2_), channel_id=1, source_target_pairs={{0,4},{4,0},{8,12},{12,8},{16,20},{20,16},{24,28},{28,24},{1,5},{5... | collective-permute-start | bytes 1572872 | tf_op jit(solution)/shard_map/ppermute | solution.py:568
  163.0 11.7 %collective-permute-start.49 = (f32[8,72,256]{2,1,0:T(8,128)S(1)}, f32[8,72,256]{2,1,0:T(8,128)S(1)}, u32[]{:S(2)}, u32[]{:S(2)}) collective-permute-start(f32[8,72,256]{2,1,0:T(8,128)S(1)} %collective-permute-done.48.refs_0_), channel_id=1, source_target_pairs={{0,4},{4,0},{8,12},{12,8},{16,20},{20,16},{24,28},{28,24},{1,5},{5... | collective-permute-start | bytes 1769480 | tf_op jit(solution)/shard_map/ppermute | solution.py:568
  163.0 11.6 %collective-permute-start.51 = (f32[8,64,256]{2,1,0:T(8,128)S(1)}, f32[8,64,256]{2,1,0:T(8,128)S(1)}, u32[]{:S(2)}, u32[]{:S(2)}) collective-permute-start(f32[8,64,256]{2,1,0:T(8,128)S(1)} %collective-permute-done.50.refs_1_), channel_id=1, source_target_pairs={{0,4},{4,0},{8,12},{12,8},{16,20},{20,16},{24,28},{28,24},{1,5},{5... | collective-permute-start | bytes 1572872 | tf_op jit(solution)/shard_map/ppermute | solution.py:568
  164.1 10.6 %collective-permute-start.53 = (f32[8,64,256]{2,1,0:T(8,128)S(1)}, f32[8,64,256]{2,1,0:T(8,128)S(1)}, u32[]{:S(2)}, u32[]{:S(2)}) collective-permute-start(f32[8,64,256]{2,1,0:T(8,128)S(1)} %collective-permute-done.52.refs_2_), channel_id=1, source_target_pairs={{0,4},{4,0},{8,12},{12,8},{16,20},{20,16},{24,28},{28,24},{1,5},{5... | collective-permute-start | bytes 1572872 | tf_op jit(solution)/shard_map/ppermute | solution.py:568
  164.1 8.5 %collective-permute-start.45 = (f32[8,40,256]{2,1,0:T(8,128)S(1)}, f32[8,40,256]{2,1,0:T(8,128)S(1)}, u32[]{:S(2)}, u32[]{:S(2)}) collective-permute-start(f32[8,40,256]{2,1,0:T(8,128)S(1)} %collective-permute-done.44.refs_2_), channel_id=1, source_target_pairs={{0,4},{4,0},{8,12},{12,8},{16,20},{20,16},{24,28},{28,24},{1,5},{5... | collective-permute-start | bytes 983048 | tf_op jit(solution)/shard_map/ppermute | solution.py:568
  (40 other events, 359.3 us)

commit v4 on v3

--- a/solution.py
+++ b/solution.py
@@ -14,7 +14,7 @@
 VMEM = pl.BlockSpec(memory_space=pltpu.VMEM)
 SMEM = pl.BlockSpec(memory_space=pltpu.SMEM)
 PARAMS = pltpu.CompilerParams(vmem_limit_bytes=16 * 1024 * 1024)
-ALL_VMEM = pltpu.CompilerParams(vmem_limit_bytes=56 * 1024 * 1024)
+GATHER_PARAMS = pltpu.CompilerParams(vmem_limit_bytes=32 * 1024 * 1024)
 COST = pl.CostEstimate(flops=10000, bytes_accessed=10000, transcendentals=0)
 
 
@@ -31,8 +31,31 @@
     return dot(a[0], b[0], dims) + (dot(a[0], b[1], dims) + dot(a[1], b[0], dims))
 
 
-def dot2(a, onehot, dims):
-    return dot(a[0], onehot, dims) + dot(a[1], onehot, dims)
+def dot2(stacked, onehot, dims):
+    half = stacked.shape[0] // 2
+    both = dot(stacked, onehot, dims)
+    return both[:half] + both[half:]
+
+
+def stack(parts):
+    return jnp.concatenate(parts, axis=0)
+
+
+def stack_into(ref, x, lanes=slice(None)):
+    rows, half = x.shape[0], ref.shape[0] // 2
+    hi, lo = split(x)
+    ref[:rows, lanes] = hi
+    ref[half : half + rows, lanes] = lo
+    if half > rows:
+        blank = jnp.zeros((half - rows, x.shape[1]), BF16)
+        ref[rows:half, lanes] = blank
+        ref[half + rows :, lanes] = blank
+
+
+def dot3_stacked(stacked, b, dims):
+    half = stacked.shape[0] // 2
+    both = dot(stacked, b[0], dims)
+    return both[:half] + (both[half:] + dot(stacked[:half], b[1], dims))
 
 
 def onehot(first, rows, idx):
@@ -44,51 +67,59 @@
     return jnp.concatenate([idx[b : b + 1] for b in range(idx.shape[0])], axis=1)
 
 
-def add_part(first, part, out_ref):
-    @pl.when(first)
-    def _():
-        out_ref[...] = part
-
-    @pl.when(jnp.logical_not(first))
-    def _():
-        out_ref[...] += part
-
-
-def gather_kernel(hub_steps, hub_idx, rel_idx, hub_ref, rel_ref, hub_out, rel_out):
-    step = pl.program_id(0)
-
-    @pl.when(step < hub_steps)
-    def _():
-        tile = hub_ref.shape[1]
-        hot = onehot(step * tile, tile, laid_out(hub_idx[...]))
-        add_part(step == 0, dot2(split(hub_ref[...]), hot, NN), hub_out)
-
-    @pl.when(step >= hub_steps)
-    def _():
-        tile = rel_ref.shape[1]
-        hot = onehot((step - hub_steps) * tile, tile, laid_out(rel_idx[...]))
-        add_part(step == hub_steps, dot2(split(rel_ref[...]), hot, NN), rel_out)
+def gather_kernel(hub_steps, rel_steps, hub_idx, rel_idx, hub_ref, rel_ref, *refs):
+    buckets = hub_idx.shape[0]
+    ids_out, hub_outs, rel_outs = refs[0], refs[1 : 1 + buckets], refs[1 + buckets : 1 + 2 * buckets]
+    hub_buf, rel_buf, stacked, sems = refs[1 + 2 * buckets :]
+    hubs, edges = hub_idx.shape[1], rel_idx.shape[1]
+    hub_tile, rel_tile = hub_buf.shape[2], rel_buf.shape[2]
+    steps = [(hub_ref, hub_buf, hub_tile, k) for k in range(hub_steps)]
+    steps += [(rel_ref, rel_buf, rel_tile, k) for k in range(rel_steps)]
+    copies = [
+        pltpu.make_async_copy(table.at[:, pl.ds(k * tile, tile)], buf.at[k % 2], sems.at[i])
+        for i, (table, buf, tile, k) in enumerate(steps)
+    ]
+    copies[0].start()
+    ids_out[:, :hubs] = hub_idx[...]
+    ids_out[:, hubs:] = rel_idx[...]
+    for i, (table, buf, tile, k) in enumerate(steps):
+        if i + 1 < len(steps):
+            copies[i + 1].start()
+        idx, outs = (hub_idx, hub_outs) if table is hub_ref else (rel_idx, rel_outs)
+        count = idx.shape[1]
+        hot = onehot(k * tile, tile, laid_out(idx[...]))
+        copies[i].wait()
+        stack_into(stacked, buf[k % 2], slice(0, tile))
+        part = dot2(stacked[:, :tile], hot, NN)
+        for b, out in enumerate(outs):
+            here = part[:, b * count : (b + 1) * count]
+            out[...] = here if k == 0 else out[...] + here
 
 
 def gather_rows(hub_table, hub_idx, rel_table, rel_idx):
     features = hub_table.shape[0]
     hub_steps, rel_steps = 4, 2
-    fixed = lambda shape: pl.BlockSpec(shape, lambda k: (0, 0))
-    shapes = [(features, hub_idx.size), (features, rel_idx.size)]
-    return pl.pallas_call(
-        functools.partial(gather_kernel, hub_steps),
-        grid=(hub_steps + rel_steps,),
-        in_specs=[
-            fixed(hub_idx.shape),
-            fixed(rel_idx.shape),
-            pl.BlockSpec((features, hub_table.shape[1] // hub_steps), lambda k: (0, jnp.minimum(k, hub_steps - 1))),
-            pl.BlockSpec((features, rel_table.shape[1] // rel_steps), lambda k: (0, jnp.maximum(k - hub_steps, 0))),
+    hub_tile, rel_tile = hub_table.shape[1] // hub_steps, rel_table.shape[1] // rel_steps
+    buckets, hubs = hub_idx.shape
+    edges = rel_idx.shape[1]
+    shapes = [(features, hubs)] * buckets + [(features, edges)] * buckets
+    anywhere = pl.BlockSpec(memory_space=pl.ANY)
+    out = pl.pallas_call(
+        functools.partial(gather_kernel, hub_steps, rel_steps),
+        in_specs=[VMEM, VMEM, anywhere, anywhere],
+        out_specs=[VMEM] * (1 + len(shapes)),
+        out_shape=[jax.ShapeDtypeStruct((buckets, hubs + edges), jnp.int32)]
+        + [jax.ShapeDtypeStruct(shape, F32) for shape in shapes],
+        scratch_shapes=[
+            pltpu.VMEM((2, features, hub_tile), F32),
+            pltpu.VMEM((2, features, rel_tile), F32),
+            pltpu.VMEM((2 * features, max(hub_tile, rel_tile)), BF16),
+            pltpu.SemaphoreType.DMA((hub_steps + rel_steps,)),
         ],
-        out_specs=[fixed(shape) for shape in shapes],
-        out_shape=[jax.ShapeDtypeStruct(shape, F32) for shape in shapes],
-        compiler_params=ALL_VMEM,
+        compiler_params=GATHER_PARAMS,
         cost_estimate=COST,
     )(hub_idx, rel_idx, hub_table, rel_table)
+    return out[0], out[1 : 1 + buckets], out[1 + buckets :]
 
 
 def spread_bits(place, order):
@@ -101,14 +132,14 @@
     return sum((((index >> (bits - 1 - i)) & 1) << p) for i, p in enumerate(order))
 
 
-def load_columns(id_refs, id_lanes, grad_refs, idx_down, hi_all, lo_all):
+def load_columns(id_refs, id_lanes, grad_refs, idx_down, stacked):
     low, high = id_lanes
     idx = jnp.concatenate([laid_out(ref[:, low:high]) for ref in id_refs], axis=1)
     idx_down[...] = jnp.transpose(jnp.broadcast_to(idx, (128, idx.shape[1])))
     at = 0
     for ref, (low, high) in grad_refs:
         width = high - low
-        hi_all[:, at : at + width], lo_all[:, at : at + width] = split(ref[:, low:high])
+        stack_into(stacked, ref[:, low:high], slice(at, at + width))
         at += width
 
 
@@ -133,13 +164,13 @@
 
 
 def hub_chunks_kernel(orders, spans, id_lanes, grad_lanes, chip_ref, *refs):
-    ids, grads, sends, keeps, (idx_down, hi_all, lo_all) = chunk_refs(orders, grad_lanes, refs)
-    load_columns(ids, id_lanes, grads, idx_down, hi_all, lo_all)
+    ids, grads, sends, keeps, (idx_down, stacked) = chunk_refs(orders, grad_lanes, refs)
+    load_columns(ids, id_lanes, grads, idx_down, stacked)
     chunks, width = 2 * keeps[0].shape[0], keeps[0].shape[2]
     lane = lax.broadcasted_iota(jnp.int32, (1, width), 1)
     for place in range(chunks):
         hot = onehot_across(idx_down, lane + (chip_ref[0] ^ place) * width)
-        chunk = dot2((hi_all[...], lo_all[...]), hot, NN)
+        chunk = dot2(stacked[...], hot, NN)
         for s, (low, high) in enumerate(spans):
             out_for(place, orders[s], sends, keeps, s)[...] = chunk[low:high]
 
@@ -152,13 +183,13 @@
         for s, (first, end) in enumerate(spans):
             count = min(end, high - low) - first
             if count > 0:
-                pieces.append((block, s, low + first, count))
+                pieces.append((block, s, low + first, first, count))
     return spans, pieces
 
 
 def rel_chunks_kernel(orders, pieces, rows, id_lanes, grad_lanes, chip_ref, *refs):
-    ids, grads, sends, keeps, (idx_down, hi_all, lo_all) = chunk_refs(orders, grad_lanes, refs)
-    load_columns(ids, id_lanes, grads, idx_down, hi_all, lo_all)
+    ids, grads, sends, keeps, (idx_down, stacked) = chunk_refs(orders, grad_lanes, refs)
+    load_columns(ids, id_lanes, grads, idx_down, stacked)
     for ref in [*sends, *keeps]:
         ref[...] = jnp.zeros_like(ref)
     chunks, lanes = 2 * keeps[0].shape[0], keeps[0].shape[2]
@@ -171,10 +202,10 @@
         for slot, place in enumerate(places):
             here = (lane >= slot * width) & (lane < (slot + 1) * width)
             targets = jnp.where(here, lane + ((chip_ref[0] ^ place) * width - slot * width), targets)
-        dense = dot2((hi_all[...], lo_all[...]), onehot_across(idx_down, targets), NN)
+        dense = dot2(stacked[...], onehot_across(idx_down, targets), NN)
         for slot, place in enumerate(places):
             chunk = dense[:, slot * width : (slot + 1) * width]
-            for block, s, low, count in pieces:
+            for block, s, low, unused, count in pieces:
                 out = out_for(place, orders[s], sends, keeps, s)
                 out[:count, block * width : (block + 1) * width] = chunk[low : low + count]
 
@@ -191,8 +222,7 @@
         out_shape=shapes,
         scratch_shapes=[
             pltpu.VMEM((count, 128), jnp.int32),
-            pltpu.VMEM((half_width, count), BF16),
-            pltpu.VMEM((half_width, count), BF16),
+            pltpu.VMEM((2 * (-(-half_width // 16) * 16), count), BF16),
         ],
         compiler_params=PARAMS,
         cost_estimate=COST,
@@ -273,57 +303,66 @@
     scale = step_rate / jnp.sqrt(sums_ref[...] + squares * (1.0 / features))
     for new in news:
         new[...] = jnp.zeros_like(new)
-    for block, s, low, count in pieces:
+    for block, s, low, unused, count in pieces:
         lanes = slice(block * width, (block + 1) * width)
         news[s][0, :count, lanes] = table_ref[low : low + count] - totals[s][0, :count, lanes] * scale
 
 
-def place_kernel(orders, pieces, spot_ref, *refs):
-    streams = len(orders)
-    lows, highs, out_ref = refs[:streams], refs[streams : 2 * streams], refs[-1]
-    half = lows[0].shape[0]
-    width = out_ref.shape[2] // (2 * half)
-    for chunk in range(2 * half):
+def combine_kernel(spans, *refs):
+    streams, out = len(spans), refs[-1]
+    for i, ref in enumerate(refs[:-1]):
+        low, high = spans[i % streams]
+        count = ref.shape[0]
+        first = (i // streams) * count
+        out[first : first + count, low:high] = ref[...]
+
+
+def combine(spans, *groups):
+    parts = [x for group in groups for x in group]
+    count = sum(group[0].shape[0] for group in groups)
+    return call(functools.partial(combine_kernel, spans), parts, [(count, spans[-1][1], parts[0].shape[2])])[0]
+
+
+def place_kernel(orders, pieces, spot_ref, all_ref, *refs):
+    out_ref = refs[-1]
+    chunks = all_ref.shape[0]
+    width = out_ref.shape[2] // chunks
+    for chunk in range(chunks):
         place = spot_ref[0] ^ chunk
-        for s in range(streams):
-            index = spread_bits(place, orders[s])
-            spot = index & (half - 1)
-            value = jnp.where(index >= half, highs[s][spot], lows[s][spot])
-            for block, stream, row, count in pieces:
-                if stream == s:
-                    part = value[:count, block * width : (block + 1) * width]
-                    out_ref[0, row : row + count, chunk * width : (chunk + 1) * width] = part
-
-
-def place_chunks(spot, near, far, orders, pieces, shape, earlier):
-    whole = [pl.BlockSpec(memory_space=pltpu.VMEM)] * (2 * len(orders))
+        values = [all_ref[spread_bits(place, order)] for order in orders]
+        for block, s, row, source, count in pieces:
+            part = values[s][source : source + count, block * width : (block + 1) * width]
+            out_ref[0, row : row + count, chunk * width : (chunk + 1) * width] = part
+
+
+def place_chunks(spot, parts, orders, pieces, shape, earlier):
     kept = [pl.BlockSpec(memory_space=pl.ANY)] * len(earlier)
     return pl.pallas_call(
         functools.partial(place_kernel, orders, pieces),
         grid_spec=pltpu.PrefetchScalarGridSpec(
             num_scalar_prefetch=1,
             grid=(1,),
-            in_specs=whole + kept,
+            in_specs=[pl.BlockSpec(memory_space=pltpu.VMEM)] + kept,
             out_specs=pl.BlockSpec((1,) + shape[1:], lambda i, spot: (spot[1], 0, 0)),
         ),
         out_shape=jax.ShapeDtypeStruct(shape, F32),
-        input_output_aliases={1 + len(whole): 0} if earlier else {},
+        input_output_aliases={2: 0} if earlier else {},
         compiler_params=PARAMS,
-        cost_estimate=COST,
-    )(spot, *near, *far, *earlier)
+        cost_estimate=pl.CostEstimate(flops=0, bytes_accessed=4 * shape[1] * shape[2], transcendentals=0),
+    )(spot, parts, *earlier)
 
 
 def copy_kernel(orders, spans, upper, spot_ref, *refs):
-    streams = len(orders)
-    parts, out_ref, sems = refs[:streams], refs[-2], refs[-1]
-    half, width = parts[0].shape[0], parts[0].shape[2]
+    out_ref, sems = refs[-2], refs[-1]
     copies = []
     for s, (low, high) in enumerate(spans):
+        part = refs[s] if upper else refs[0].at[:, pl.ds(low, high - low)]
+        half, width = part.shape[0], part.shape[2]
         for index in range(half):
             chunk = spot_ref[0] ^ gather_bits(index + half * upper, orders[s])
             lanes = pl.ds(pl.multiple_of(chunk * width, width), width)
             target = out_ref.at[spot_ref[1], pl.ds(low, high - low), lanes]
-            copies.append(pltpu.make_async_copy(parts[s].at[index], target, sems.at[len(copies)]))
+            copies.append(pltpu.make_async_copy(part.at[index], target, sems.at[len(copies)]))
     for copy in copies:
         copy.start()
     for copy in copies:
@@ -337,10 +376,10 @@
         in_specs=[SMEM] + [anywhere] * (len(parts) + len(earlier)),
         out_specs=anywhere,
         out_shape=jax.ShapeDtypeStruct(shape, F32),
-        scratch_shapes=[pltpu.SemaphoreType.DMA((len(parts) * parts[0].shape[0],))],
+        scratch_shapes=[pltpu.SemaphoreType.DMA((len(spans) * parts[0].shape[0],))],
         input_output_aliases={1 + len(parts): 0} if earlier else {},
         compiler_params=PARAMS,
-        cost_estimate=COST,
+        cost_estimate=pl.CostEstimate(flops=0, bytes_accessed=4 * shape[1] * shape[2], transcendentals=0),
     )(spot, *parts, *earlier)
 
 
@@ -371,24 +410,14 @@
 EDGE_TILE = 256
 
 
-def edge_spans(step, bucket, edges):
-    tile = EDGE_TILE
-    here = pl.multiple_of(step * tile, tile)
-    return pl.ds(here, tile), pl.ds(pl.multiple_of(bucket * edges + here, tile), tile)
-
-
-def lay_down(idx, out_ref):
-    out_ref[...] = jnp.transpose(jnp.broadcast_to(idx, (128, idx.shape[1])))
-
-
-def head_hot_down(heads_down, span, rows):
-    return onehot_across(heads_down.at[span], lax.broadcasted_iota(jnp.int32, (1, rows), 1))
+def edge_span(step):
+    return pl.ds(pl.multiple_of(step * EDGE_TILE, EDGE_TILE), EDGE_TILE)
 
 
 def bucket_kernel(
     bucket, core_ref, heads_ref, tails_ref, negs_ref, left_ref, left_sums_ref, right_ref, right_sums_ref, rel_ref, hub_ref,
     left_out, left_sums_out, right_out, keep_out, send_out,
-    left_hi, left_lo, both_hi, both_lo, left_grad, both_grad, heads_down,
+    left_parts, both_parts, left_grad, both_grad,
 ):
     features, rows = left_ref.shape
     half = features // 2
@@ -396,25 +425,23 @@
     edges = heads_ref.shape[1]
     hubs = keep_out.shape[1] - edges
     at = slice(bucket, bucket + 1)
-    hub_rows = hub_ref[:, bucket * hubs : (bucket + 1) * hubs]
     weight = 1.0 / (negs_ref.shape[1] + hubs)
     counts = table_counts(rows, negs_ref[at], weight)
-    lay_down(heads_ref[at], heads_down)
-    left_hi[...], left_lo[...] = split(left_ref[...])
-    both_hi[:, :rows], both_lo[:, :rows] = split(right_ref[...])
-    both_hi[:, rows:], both_lo[:, rows:] = split(hub_rows)
+    stack_into(left_parts, left_ref[...])
+    stack_into(both_parts, right_ref[...], slice(0, rows))
+    stack_into(both_parts, hub_ref[...], slice(rows, rows + hubs))
     left_grad[...] = jnp.zeros_like(left_grad)
     both_grad[...] = jnp.zeros_like(both_grad)
 
     @pl.loop(0, edges // EDGE_TILE)
     def _(step):
-        span, wide_span = edge_spans(step, bucket, edges)
+        span = edge_span(step)
         tail_here = lax.broadcasted_iota(jnp.int32, (rows, EDGE_TILE), 0) == tails_ref[at, span]
-        h = dot2((left_hi[...], left_lo[...]), onehot(0, rows, heads_ref[at, span]), NN)
-        r = rel_ref[:, wide_span]
+        head_hot = onehot(0, rows, heads_ref[at, span])
+        h = dot2(left_parts[...], head_hot, NN)
+        r = rel_ref[:, span]
         q = split(turned(h, r, half))
-        both = (both_hi[...], both_lo[...])
-        scores = dot3(both, q, TN)
+        scores = dot3((both_parts[:features], both_parts[features:]), q, TN)
         chance = jax.nn.sigmoid(scores[:rows])
         coef = jnp.concatenate(
             [
@@ -424,10 +451,10 @@
             axis=0,
         )
         coef = split(coef)
-        dq = dot3(both, coef, NN)
-        both_grad[...] += dot3(q, coef, NT)
+        dq = dot3_stacked(both_parts[...], coef, NN)
+        both_grad[...] += dot3_stacked(stack(q), coef, NT)
         dh = jnp.concatenate(turned_back(dq, r, half), axis=0)
-        left_grad[...] += dot2(split(dh), head_hot_down(heads_down, span, rows), NN)
+        left_grad[...] += dot2(stack(split(dh)), head_hot, NT)
         out_span = pl.ds(pl.multiple_of(hubs + step * EDGE_TILE, 128), EDGE_TILE)
         keep_out[:, out_span], send_out[:, out_span] = keep_and_send(core, *turned_back(dq, h, half))
 
@@ -440,7 +467,7 @@
 
 def bucket_step(bucket, core, heads, tails, negs, left, left_sums, right, right_sums, rel_rows, hub_rows):
     features, rows = left.shape
-    edges, hubs = heads.shape[1], hub_rows.shape[1] // heads.shape[0]
+    edges, hubs = heads.shape[1], hub_rows.shape[1]
     width = rows + hubs
     shapes = [(features, rows), (1, rows), (features + 8, rows)] + [(features // 2, hubs + edges)] * 2
     return pl.pallas_call(
@@ -448,12 +475,11 @@
         in_specs=[SMEM] + [VMEM] * 9,
         out_specs=[VMEM] * 5,
         out_shape=[jax.ShapeDtypeStruct(shape, F32) for shape in shapes],
-        scratch_shapes=[pltpu.VMEM((features, rows), BF16)] * 2
-        + [pltpu.VMEM((features, width), BF16)] * 2
-        + [
+        scratch_shapes=[
+            pltpu.VMEM((2 * features, rows), BF16),
+            pltpu.VMEM((2 * features, width), BF16),
             pltpu.VMEM((features, rows), F32),
             pltpu.VMEM((features, width), F32),
-            pltpu.VMEM((edges, 128), jnp.int32),
         ],
         compiler_params=PARAMS,
         cost_estimate=COST,
@@ -462,55 +488,55 @@
 
 def hub_kernel(
     bucket, negatives, core_ref, heads_ref, left_ref, rel_ref, hub_ref,
-    head_out, query_grad, hub_keep, hub_send,
-    left_hi, left_lo, hub_hi, hub_lo, hub_grad,
+    query_grad, hub_keep, hub_send,
+    left_parts, hub_parts, hub_grad,
 ):
     features, rows = left_ref.shape
     half = features // 2
     edges, hubs = heads_ref.shape[1], hub_keep.shape[1]
     at = slice(bucket, bucket + 1)
-    hub_rows = hub_ref[:, bucket * hubs : (bucket + 1) * hubs]
     weight = 1.0 / (negatives + hubs)
-    left_hi[...], left_lo[...] = split(left_ref[...])
-    hub_hi[...], hub_lo[...] = split(hub_rows)
+    stack_into(left_parts, left_ref[...])
+    stack_into(hub_parts, hub_ref[...])
     hub_grad[...] = jnp.zeros_like(hub_grad)
 
     @pl.loop(0, edges // EDGE_TILE)
     def _(step):
-        span, wide_span = edge_spans(step, bucket, edges)
-        h = dot2((left_hi[...], left_lo[...]), onehot(0, rows, heads_ref[at, span]), NN)
-        head_out[:, span] = h
-        q = split(turned(h, rel_ref[:, wide_span], half))
-        hub = (hub_hi[...], hub_lo[...])
-        coef = split(weight * jax.nn.sigmoid(dot3(hub, q, TN)))
-        query_grad[:, span] = dot3(hub, coef, NN)
-        hub_grad[...] += dot3(q, coef, NT)
+        span = edge_span(step)
+        head_hot = onehot(0, rows, heads_ref[at, span])
+        h = dot2(left_parts[...], head_hot, NN)
+        q = split(turned(h, rel_ref[:, span], half))
+        coef = split(weight * jax.nn.sigmoid(dot3((hub_parts[:features], hub_parts[features:]), q, TN)))
+        query_grad[:, span] = dot3_stacked(hub_parts[...], coef, NN)
+        hub_grad[...] += dot3_stacked(stack(q), coef, NT)
 
     hub_keep[...], hub_send[...] = keep_and_send(core_ref[0], hub_grad[:half], hub_grad[half:])
 
 
 def hub_step(bucket, negatives, core, heads, left, rel_rows, hub_rows):
     features, rows = left.shape
-    edges, hubs = heads.shape[1], hub_rows.shape[1] // heads.shape[0]
-    shapes = [(features, edges)] * 2 + [(features // 2, hubs)] * 2
+    edges, hubs = heads.shape[1], hub_rows.shape[1]
+    shapes = [(features, edges)] + [(features // 2, hubs)] * 2
     return pl.pallas_call(
         functools.partial(hub_kernel, bucket, negatives),
         in_specs=[SMEM] + [VMEM] * 4,
-        out_specs=[VMEM] * 4,
+        out_specs=[VMEM] * 3,
         out_shape=[jax.ShapeDtypeStruct(shape, F32) for shape in shapes],
-        scratch_shapes=[pltpu.VMEM((features, rows), BF16)] * 2
-        + [pltpu.VMEM((features, hubs), BF16)] * 2
-        + [pltpu.VMEM((features, hubs), F32)],
+        scratch_shapes=[
+            pltpu.VMEM((2 * features, rows), BF16),
+            pltpu.VMEM((2 * features, hubs), BF16),
+            pltpu.VMEM((features, hubs), F32),
+        ],
         compiler_params=PARAMS,
         cost_estimate=COST,
     )(core, heads, left, rel_rows, hub_rows)
 
 
 def tables_kernel(
-    bucket, hubs, core_ref, heads_ref, tails_ref, negs_ref, head_rows, query_grad,
+    bucket, hubs, core_ref, heads_ref, tails_ref, negs_ref, query_grad,
     left_ref, left_sums_ref, right_ref, rel_ref,
     left_out, right_out, rel_keep, rel_send,
-    right_hi, right_lo, left_grad, right_grad, heads_down,
+    left_parts, right_parts, left_grad, right_grad,
 ):
     features, rows = left_ref.shape
     half = features // 2
@@ -518,45 +544,45 @@
     at = slice(bucket, bucket + 1)
     core = core_ref[0]
     counts = table_counts(rows, negs_ref[at], 1.0 / (negs_ref.shape[1] + hubs))
-    lay_down(heads_ref[at], heads_down)
-    right_hi[...], right_lo[...] = split(right_ref[:features])
+    stack_into(left_parts, left_ref[...])
+    stack_into(right_parts, right_ref[:features])
     left_grad[...] = jnp.zeros_like(left_grad)
     right_grad[...] = jnp.zeros_like(right_grad)
 
     @pl.loop(0, edges // EDGE_TILE)
     def _(step):
-        span, wide_span = edge_spans(step, bucket, edges)
+        span = edge_span(step)
         tail_here = lax.broadcasted_iota(jnp.int32, (rows, EDGE_TILE), 0) == tails_ref[at, span]
-        h, r = head_rows[:, span], rel_ref[:, wide_span]
+        head_hot = onehot(0, rows, heads_ref[at, span])
+        h = dot2(left_parts[...], head_hot, NN)
+        r = rel_ref[:, span]
         q = split(turned(h, r, half))
-        right = (right_hi[...], right_lo[...])
-        chance = jax.nn.sigmoid(dot3(right, q, TN))
+        chance = jax.nn.sigmoid(dot3((right_parts[:features], right_parts[features:]), q, TN))
         coef = split(counts * chance + jnp.where(tail_here, chance - 1.0, 0.0))
-        dq = dot3(right, coef, NN) + query_grad[:, span]
-        right_grad[...] += dot3(q, coef, NT)
+        dq = dot3_stacked(right_parts[...], coef, NN) + query_grad[:, span]
+        right_grad[...] += dot3_stacked(stack(q), coef, NT)
         rel_keep[:, span], rel_send[:, span] = keep_and_send(core, *turned_back(dq, h, half))
         dh = jnp.concatenate(turned_back(dq, r, half), axis=0)
-        left_grad[...] += dot2(split(dh), head_hot_down(heads_down, span, rows), NN)
+        left_grad[...] += dot2(stack(split(dh)), head_hot, NT)
 
     left_out[...], unused = adagrad(left_ref[...], left_sums_ref[...], left_grad[...])
     right_out[...], unused = adagrad(right_ref[:features], right_ref[features : features + 1], right_grad[...])
 
 
-def tables_step(bucket, hubs, core, heads, tails, negs, head_rows, query_grad, left, left_sums, right, rel_rows):
+def tables_step(bucket, hubs, core, heads, tails, negs, query_grad, left, left_sums, right, rel_rows):
     features, rows = left.shape
     edges = heads.shape[1]
     shapes = [(features, rows)] * 2 + [(features // 2, edges)] * 2
     return pl.pallas_call(
         functools.partial(tables_kernel, bucket, hubs),
-        in_specs=[SMEM] + [VMEM] * 9,
+        in_specs=[SMEM] + [VMEM] * 8,
         out_specs=[VMEM] * 4,
         out_shape=[jax.ShapeDtypeStruct(shape, F32) for shape in shapes],
-        scratch_shapes=[pltpu.VMEM((features, rows), BF16)] * 2
-        + [pltpu.VMEM((features, rows), F32)] * 2
-        + [pltpu.VMEM((edges, 128), jnp.int32)],
+        scratch_shapes=[pltpu.VMEM((2 * features, rows), BF16)] * 2
+        + [pltpu.VMEM((features, rows), F32)] * 2,
         compiler_params=PARAMS,
         cost_estimate=COST,
-    )(core, heads, tails, negs, head_rows, query_grad, left, left_sums, right, rel_rows)
+    )(core, heads, tails, negs, query_grad, left, left_sums, right, rel_rows)
 
 
 def from_behind(x, axis, by):
@@ -612,7 +638,7 @@
     hub_orders = stream_orders()
     rel_orders = hub_orders[:2]
     spans = row_spans(half_width, len(hub_orders))
-    hub_pieces = [(0, s, low, high - low) for s, (low, high) in enumerate(spans)]
+    hub_pieces = [(0, s, low, low, high - low) for s, (low, high) in enumerate(spans)]
     rel_spans, rel_pieces = rel_layout(half_width, len(rel_orders))
     heights, rel_heights = [[high - low for low, high in x] for x in (spans, rel_spans)]
     stages = len(hub_orders[0])
@@ -626,25 +652,23 @@
     def in_turn(first, then):
         return lax.optimization_barrier((first, then))
 
-    ids = jnp.concatenate([hub_ids, relations], axis=1)
+    ids, hub_rows, rel_rows = gather_rows(
+        hub_emb.reshape(features, hub_count), hub_ids, relation_emb.reshape(features, rel_count), relations
+    )
     far_ids = other_core(ids)
-    hub_rows, rel_rows = gather_rows(
-        hub_emb.reshape(features, hub_count), hub_ids, relation_emb.reshape(features, rel_count), relations
-    )
-    far_ids, rel_rows = in_turn(far_ids, rel_rows)
     keeps, fars = [], []
     for b in range(buckets - 1):
         if b > 0:
             right, right_sums = right[:features], right[features : features + 1]
         left, left_sums, right, keep, send = bucket_step(
-            b, core, heads, tails, negatives, left, left_sums, right, right_sums, rel_rows, hub_rows
+            b, core, heads, tails, negatives, left, left_sums, right, right_sums, rel_rows[b], hub_rows[b]
         )
         right = from_behind(right, "blk", 1)
         keeps.append(keep)
         fars.append(other_core(send))
     last = buckets - 1
-    head_rows, query_grad, hub_keep, hub_send = hub_step(
-        last, negatives.shape[1], core, heads, left, rel_rows, hub_rows
+    query_grad, hub_keep, hub_send = hub_step(
+        last, negatives.shape[1], core, heads, left, rel_rows[last], hub_rows[last]
     )
     hub_far = other_core(hub_send)
     grads = lambda early, late, lanes: [(x, lanes) for x in early] + [(late, (0, late.shape[1]))]
@@ -655,7 +679,7 @@
     )
     got = exchanged(send, hub_orders, 0)
     left, right, rel_keep, rel_send = tables_step(
-        last, hubs, core, heads, tails, negatives, head_rows, query_grad, left, left_sums, right, rel_rows
+        last, hubs, core, heads, tails, negatives, query_grad, left, left_sums, right, rel_rows[last]
     )
     rel_far = other_core(rel_send)
 
@@ -705,31 +729,36 @@
         [x.shape for x in rel_totals],
     )
     rel_got = exchanged(rel_have, rel_orders, stages - 1)
-    for step in range(stages - 3, -1, -1):
-        rel_have, got = in_turn(rel_have, got)
-        have = join(have, got)
-        got = exchanged(have, hub_orders, step)
-        have, rel_got = in_turn(have, rel_got)
-        rel_have = join(rel_have, rel_got)
-        rel_got = exchanged(rel_have, rel_orders, step + 1)
-    rel_have = join(rel_have, rel_got)
-    rel_got = exchanged(rel_have, rel_orders, 0)
+    rel_step, step = stages - 2, stages - 3
+    turns = ["rel", "hub"] * (stages - 3) + ["rel"] * 2 + ["hub"]
+    for turn in turns:
+        if turn == "rel":
+            have, rel_got = in_turn(have, rel_got)
+            rel_have = join(rel_have, rel_got)
+            rel_got = exchanged(rel_have, rel_orders, rel_step)
+            rel_step -= 1
+        else:
+            rel_have, got = in_turn(rel_have, got)
+            near = combine(spans, have, got)
+            have = join(have, got)
+            got = exchanged(have, hub_orders, step)
+            step -= 1
 
     mine, others = jnp.concatenate([chip, core]), jnp.concatenate([chip, 1 - core])
     shape = hub_emb.shape
     if width % 128 == 0:
-        hub_new = copy_chunks(mine, have, 0, hub_orders, spans, shape, ())
-        hub_new = copy_chunks(others, other_core(have), 0, hub_orders, spans, shape, (hub_new,))
+        hub_new = copy_chunks(mine, [near], 0, hub_orders, spans, shape, ())
+        hub_new = copy_chunks(others, [other_core(near)], 0, hub_orders, spans, shape, (hub_new,))
         hub_new = copy_chunks(mine, got, 1, hub_orders, spans, shape, (hub_new,))
         hub_new = copy_chunks(others, other_core(got), 1, hub_orders, spans, shape, (hub_new,))
     else:
-        hub_new = place_chunks(mine, have, got, hub_orders, hub_pieces, shape, ())
-        hub_new = place_chunks(others, other_core(have), other_core(got), hub_orders, hub_pieces, shape, (hub_new,))
+        whole = combine(spans, have, got)
+        hub_new = place_chunks(mine, whole, hub_orders, hub_pieces, shape, ())
+        hub_new = place_chunks(others, other_core(whole), hub_orders, hub_pieces, shape, (hub_new,))
     shape = relation_emb.shape
-    rel_new = place_chunks(mine, rel_have, rel_got, rel_orders, rel_pieces, shape, ())
-    rel_new = place_chunks(
-        others, other_core(rel_have), other_core(rel_got), rel_orders, rel_pieces, shape, (rel_new,)
-    )
+    rel_whole = combine(rel_spans, rel_have, rel_got)
+    rel_new = place_chunks(mine, rel_whole, rel_orders, rel_pieces, shape, ())
+    rel_new = place_chunks(others, other_core(rel_whole), rel_orders, rel_pieces, shape, (rel_new,))
     return (
         left.reshape(components, half_width, row_count),
         right.reshape(components, half_width, row_count),

time: 178 us -> 170 us (0.955)
  Pallas kernels: 55.3 us -> 49.8 us
  local copies, waits for them, and re-layouts: 13.8 us -> 10.1 us
    pallas_call x1, Pallas kernels: 11.3 us -> 8.17 us  [gather_rows(): pl.pallas_call(functools.partial(gather_kernel, hub_steps, rel_steps), in...]
    unnamed x31 -> x28, local copies, waits for them, and re-layouts: 9.68 us -> 6.72 us
    pallas_call x2, Pallas kernels: 9.26 us -> 6.83 us  [chunk_columns(): pl.pallas_call(functools.partial(kernel, grad_lanes), in_specs=[SMEM] + [...]
    ppermute x56 -> x51, waiting for transfers between devices: 48.9 us -> 50.1 us  [flipped(): lax.ppermute(x, axis, [(i, i ^ 1 << bit) for i in range(lax.axis_size(axi...]
    ppermute x56 -> x51, starting transfers between devices: 53.6 us -> 54.5 us  [flipped(): lax.ppermute(x, axis, [(i, i ^ 1 << bit) for i in range(lax.axis_size(axi...]
  transfers between devices with their start and end apart: 57 -> 52, of which waited for: 22 -> 17; matrix products, arithmetic and copies ran while one was open for 2% -> 2% of each run, Pallas kernels for 25% -> 18%
where the time goes in v4:
time: 170 us; the launch traced here: 169 us
  starting transfers between devices  54.6 us (32%)
  waiting for transfers between devices  50.1 us (29%)
  Pallas kernels  49.8 us (29%)
  local copies, waits for them, and re-layouts  10.1 us (6%)
  between operations  4.44 us (3%)
    ppermute x51, starting transfers between devices, flipped(): lax.ppermute(x, axis, [(i, i ^ 1 << bit) for i in range(lax.axis_size(axi...  54.5 us
    ppermute x51, waiting for transfers between devices, flipped(): lax.ppermute(x, axis, [(i, i ^ 1 << bit) for i in range(lax.axis_size(axi...  50.1 us
    pallas_call x1, Pallas kernels, tables_step(): pl.pallas_call(functools.partial(tables_kernel, bucket, hubs), in_specs=[...  9.26 us
    pallas_call x1, Pallas kernels, bucket_step(): pl.pallas_call(functools.partial(bucket_kernel, bucket), in_specs=[SMEM]...  9.06 us
    pallas_call x1, Pallas kernels, gather_rows(): pl.pallas_call(functools.partial(gather_kernel, hub_steps, rel_steps), in...  8.17 us
    pallas_call x4, Pallas kernels, copy_chunks(): pl.pallas_call(functools.partial(copy_kernel, orders, spans, upper), in_s...  7.6 us
    pallas_call x2, Pallas kernels, chunk_columns(): pl.pallas_call(functools.partial(kernel, grad_lanes), in_specs=[SMEM] + [...  6.83 us
    unnamed x28, local copies, waits for them, and re-layouts  6.72 us
  transfers between devices with their start and end apart: 52, of which 17 were waited for; matrix products, arithmetic and copies ran while one was open for 2% of the time, Pallas kernels for 18%

profile of v4, /device:TPU:0, one launch (start us, length us, event | category | flops | bytes accessed | tf_op | source)
XLA Modules:
  0.0 169.2 jit_solution(6391149784708164990)
XLA Ops:
  0.7 2.9 %copy-done.1 = f32[2,200,4096]{2,1,0:T(8,128)S(1)} copy-done((f32[2,200,4096]{2,1,0:T(8,128)S(1)}, f32[2,200,4096]{2,1,0:T(8,128)}, u32[]{:S(2)}) %copy-start.1) | copy-done | bytes 6553624
  6.5 8.2 %shard_map.156 = (s32[2,768]{1,0:T(2,128)S(1)}, f32[400,256]{1,0:T(8,128)S(1)}, f32[400,256]{1,0:T(8,128)S(1)}, f32[400,512]{1,0:T(8,128)S(1)}, f32[400,512]{1,0:T(8,128)S(1)}) custom-call(s32[2,256]{1,0:T(2,128)S(1)} %copy-done.11, s32[2,512]{1,0:T(2,128)S(1)} %copy-done.10, f32[400,4096]{1,0:T(8,128)S(1)} %bitcast.20, f32[400,1280]{1,0:T(8,128)S(1)} %bitcast.21), custom_call_target="tpu_custom_call" | custom-call | flops 10000 | bytes 10000 | tf_op jit(solution)/shard_map/pallas_call | solution.py:107
  14.8 9.1 %shard_map.157 = (f32[400,512]{1,0:T(8,128)S(1)}, f32[1,512]{1,0:T(1,128)S(1)}, f32[408,512]{1,0:T(8,128)}, f32[200,768]{1,0:T(8,128)S(1)}, f32[200,768]{1,0:T(8,128)}) custom-call(s32[1]{0:T(128)} %bitcast.core_ref, s32[2,512]{1,0:T(2,128)S(1)} %copy-done.7, s32[2,512]{1,0:T(2,128)S(1)} %copy-done.9, s32[2,1024]{1,0:T(2,128)S(1)} %copy-done.8, ...), custom_call_target="tpu_custom_call" | custom-call | flops 10000 | bytes 10000 | tf_op jit(solution)/shard_map/pallas_call | solution.py:473
  24.3 3.4 %shard_map.158 = (f32[400,512]{1,0:T(8,128)S(1)}, f32[200,256]{1,0:T(8,128)S(1)}, f32[200,256]{1,0:T(8,128)S(1)}) custom-call(s32[1]{0:T(128)} %bitcast.core_ref, s32[2,512]{1,0:T(2,128)S(1)} %copy-done.7, f32[400,512]{1,0:T(8,128)S(1)} %get-tuple-element.171.left_ref, f32[400,512]{1,0:T(8,128)S(1)} %get-tuple-element.172.rel_ref, ...), custom_call_target="tpu_custom_call" | custom-call | flops 10000 | bytes 10000 | tf_op jit(solution)/shard_map/pallas_call | solution.py:520
  28.7 2.6 %collective-permute-start.3 = (f32[200,256]{1,0:T(8,128)S(1)}, f32[200,256]{1,0:T(8,128)S(1)}, u32[]{:S(2)}, u32[]{:S(2)}) collective-permute-start(f32[200,256]{1,0:T(8,128)S(1)} %get-tuple-element.184), channel_id=1, source_target_pairs={{0,4},{4,0},{8,12},{12,8},{16,20},{20,16},{24,28},{28,24},{1,5},{5... | collective-permute-start | bytes 614408 | tf_op jit(solution)/shard_map/ppermute | solution.py:594
  32.4 3.8 %shard_map.160 = (f32[8,72,256]{2,1,0:T(8,128)S(1)}, f32[8,64,256]{2,1,0:T(8,128)S(1)}, f32[8,64,256]{2,1,0:T(8,128)S(1)}, f32[8,72,256]{2,1,0:T(8,128)S(1)}, f3...) custom-call(s32[1]{0:T(128)} %bitcast.9.chip_ref, s32[2,768]{1,0:T(2,128)S(1)} %get-tuple-element.179.refs_0_, ...), custom_call_target="tpu_custom_call" | custom-call | flops 10000 | bytes 10000 | tf_op jit(solution)/shard_map/pallas_call | solution.py:218
  40.0 9.3 %shard_map.159 = (f32[400,512]{1,0:T(8,128)}, f32[400,512]{1,0:T(8,128)}, f32[200,512]{1,0:T(8,128)S(1)}, f32[200,512]{1,0:T(8,128)S(1)}) custom-call(s32[1]{0:T(128)} %bitcast.core_ref, s32[2,512]{1,0:T(2,128)S(1)} %copy-done.7, s32[2,512]{1,0:T(2,128)S(1)} %copy-done.9, s32[2,1024]{1,0:T(2,128)S(1)} %copy-done.8, f32[400,512]{1,0:T(8,128)S(1)} %copy-done.6, ...), custom_call_target="tpu_custom_call" | custom-call | flops 10000 | bytes 10000 | tf_op jit(solution)/shard_map/pallas_call | solution.py:576
  49.3 2.3 %collective-permute-done.5.refs_4_ = f32[8,64,256]{2,1,0:T(8,128)S(1)} collective-permute-done((f32[8,64,256]{2,1,0:T(8,128)S(1)}, f32[8,64,256]{2,1,0:T(8,128)S(1)}, u32[]{:S(2)}, u32[]{:S(2)}) %collective-permute-start.5) | collective-permute-done | bytes 524320 | tf_op jit(solution)/shard_map/ppermute | solution.py:594
  55.7 3.1 %shard_map.162 = (f32[8,40,256]{2,1,0:T(8,128)S(1)}, f32[8,32,256]{2,1,0:T(8,128)S(1)}, f32[8,40,256]{2,1,0:T(8,128)S(1)}, f32[8,32,256]{2,1,0:T(8,128)S(1)}) custom-call(s32[1]{0:T(128)} %bitcast.9.chip_ref, s32[2,768]{1,0:T(2,128)S(1)} %get-tuple-element.179.refs_0_, s32[2,768]{1,0:T(2,128)S(1)} %collective-permute-done.1.refs_1_, ...), custom_call_target="tpu_custom_call" | custom-call | flops 10000 | bytes 10000 | tf_op jit(solution)/shard_map/pallas_call | solution.py:218
  61.9 2.6 %collective-permute-start.13 = (f32[2,72,256]{2,1,0:T(8,128)S(1)}, f32[2,72,256]{2,1,0:T(8,128)S(1)}, u32[]{:S(2)}, u32[]{:S(2)}) collective-permute-start(f32[2,72,256]{2,1,0:T(8,128)S(1)} %get-tuple-element.222), channel_id=1, source_target_pairs={{0,1},{1,0},{2,3},{3,2},{4,5},{5,4},{6,7},{7,6},{8,9},{9,8},{10,11... | collective-permute-start | bytes 442376 | tf_op jit(solution)/shard_map/ppermute | solution.py:594
  64.8 2.6 %collective-permute-start.15 = (f32[2,64,256]{2,1,0:T(8,128)S(1)}, f32[2,64,256]{2,1,0:T(8,128)S(1)}, u32[]{:S(2)}, u32[]{:S(2)}) collective-permute-start(f32[2,64,256]{2,1,0:T(8,128)S(1)} %get-tuple-element.224), channel_id=1, source_target_pairs={{0,2},{1,3},{2,0},{3,1},{4,6},{5,7},{6,4},{7,5},{8,10},{9,11},{10,... | collective-permute-start | bytes 393224 | tf_op jit(solution)/shard_map/ppermute | solution.py:594
  67.4 1.9 %collective-permute-done.11.refs_2_ = f32[8,40,256]{2,1,0:T(8,128)S(1)} collective-permute-done((f32[8,40,256]{2,1,0:T(8,128)S(1)}, f32[8,40,256]{2,1,0:T(8,128)S(1)}, u32[]{:S(2)}, u32[]{:S(2)}) %collective-permute-start.11) | collective-permute-done | bytes 327712 | tf_op jit(solution)/shard_map/ppermute | solution.py:594
  72.2 2.4 %collective-permute-start.18 = (f32[1,72,256]{2,1,0:T(8,128)S(1)}, f32[1,72,256]{2,1,0:T(8,128)S(1)}, u32[]{:S(2)}, u32[]{:S(2)}) collective-permute-start(f32[1,72,256]{2,1,0:T(8,128)S(1)} %get-tuple-element.242), channel_id=1, source_target_pairs={{0,2},{1,3},{2,0},{3,1},{4,6},{5,7},{6,4},{7,5},{8,10},{9,11},{10,... | collective-permute-start | bytes 221192 | tf_op jit(solution)/shard_map/ppermute | solution.py:594
  77.0 3.3 %collective-permute-done.19.refs_4_ = f32[1,64,256]{2,1,0:T(8,128)S(1)} collective-permute-done((f32[1,64,256]{2,1,0:T(8,128)S(1)}, f32[1,64,256]{2,1,0:T(8,128)S(1)}, u32[]{:S(2)}, u32[]{:S(2)}) %collective-permute-start.19) | collective-permute-done | bytes 65568 | tf_op jit(solution)/shard_map/ppermute | solution.py:594
  87.4 2.3 %collective-permute-start.24 = (f32[1,40,256]{2,1,0:T(8,128)S(1)}, f32[1,40,256]{2,1,0:T(8,128)S(1)}, u32[]{:S(2)}, u32[]{:S(2)}) collective-permute-start(f32[1,40,256]{2,1,0:T(8,128)S(1)} %get-tuple-element.273), channel_id=1, source_target_pairs={{0,2},{1,3},{2,0},{3,1},{4,6},{5,7},{6,4},{7,5},{8,10},{9,11},{10,... | collective-permute-start | bytes 122888 | tf_op jit(solution)/shard_map/ppermute | solution.py:594
  90.4 2.3 %collective-permute-start.26 = (f32[1,72,256]{2,1,0:T(8,128)S(1)}, f32[1,72,256]{2,1,0:T(8,128)S(1)}, u32[]{:S(2)}, u32[]{:S(2)}) collective-permute-start(f32[1,72,256]{2,1,0:T(8,128)S(1)} %get-tuple-element.282.refs_0_), channel_id=1, source_target_pairs={{0,2},{1,3},{2,0},{3,1},{4,6},{5,7},{6,4},{7,5},{8,10},{9,11},{10,... | collective-permute-start | bytes 221192 | tf_op jit(solution)/shard_map/ppermute | solution.py:594
  95.6 2.2 %collective-permute-done.25.refs_3_ = f32[1,32,256]{2,1,0:T(8,128)S(1)} collective-permute-done((f32[1,32,256]{2,1,0:T(8,128)S(1)}, f32[1,32,256]{2,1,0:T(8,128)S(1)}, u32[]{:S(2)}, u32[]{:S(2)}) %collective-permute-start.25) | collective-permute-done | bytes 32800 | tf_op jit(solution)/shard_map/ppermute | solution.py:594
  97.9 3.1 %collective-permute-done.27.refs_4_ = f32[1,64,256]{2,1,0:T(8,128)S(1)} collective-permute-done((f32[1,64,256]{2,1,0:T(8,128)S(1)}, f32[1,64,256]{2,1,0:T(8,128)S(1)}, u32[]{:S(2)}, u32[]{:S(2)}) %collective-permute-start.27) | collective-permute-done | bytes 65568 | tf_op jit(solution)/shard_map/ppermute | solution.py:594
  102.3 2.5 %collective-permute-start.34 = (f32[2,64,256]{2,1,0:T(8,128)S(1)}, f32[2,64,256]{2,1,0:T(8,128)S(1)}, u32[]{:S(2)}, u32[]{:S(2)}) collective-permute-start(f32[2,64,256]{2,1,0:T(8,128)S(1)} %get-tuple-element.305.refs_2_), channel_id=1, source_target_pairs={{0,2},{1,3},{2,0},{3,1},{4,6},{5,7},{6,4},{7,5},{8,10},{9,11},{10,... | collective-permute-start | bytes 393224 | tf_op jit(solution)/shard_map/ppermute | solution.py:594
  105.7 2.5 %collective-permute-start.31 = (f32[1,32,256]{2,1,0:T(8,128)S(1)}, f32[1,32,256]{2,1,0:T(8,128)S(1)}, u32[]{:S(2)}, u32[]{:S(2)}) collective-permute-start(f32[1,32,256]{2,1,0:T(8,128)S(1)} %get-tuple-element.293.refs_1_), channel_id=1, source_target_pairs={{0,2},{1,3},{2,0},{3,1},{4,6},{5,7},{6,4},{7,5},{8,10},{9,11},{10,... | collective-permute-start | bytes 98312 | tf_op jit(solution)/shard_map/ppermute | solution.py:594
  108.2 5.8 %collective-permute-done.31.refs_3_ = f32[1,32,256]{2,1,0:T(8,128)S(1)} collective-permute-done((f32[1,32,256]{2,1,0:T(8,128)S(1)}, f32[1,32,256]{2,1,0:T(8,128)S(1)}, u32[]{:S(2)}, u32[]{:S(2)}) %collective-permute-start.31) | collective-permute-done | bytes 32800 | tf_op jit(solution)/shard_map/ppermute | solution.py:594
  116.2 2.0 %collective-permute-start.35 = (f32[2,40,256]{2,1,0:T(8,128)S(1)}, f32[2,40,256]{2,1,0:T(8,128)S(1)}, u32[]{:S(2)}, u32[]{:S(2)}) collective-permute-start(f32[2,40,256]{2,1,0:T(8,128)S(1)} %get-tuple-element.301.refs_0_), channel_id=1, source_target_pairs={{0,1},{1,0},{2,3},{3,2},{4,5},{5,4},{6,7},{7,6},{8,9},{9,8},{10,11... | collective-permute-start | bytes 245768 | tf_op jit(solution)/shard_map/ppermute | solution.py:594
  119.4 4.5 %collective-permute-done.36.refs_3_ = f32[2,32,256]{2,1,0:T(8,128)S(1)} collective-permute-done((f32[2,32,256]{2,1,0:T(8,128)S(1)}, f32[2,32,256]{2,1,0:T(8,128)S(1)}, u32[]{:S(2)}, u32[]{:S(2)}) %collective-permute-start.36) | collective-permute-done | bytes 65568 | tf_op jit(solution)/shard_map/ppermute | solution.py:594
  126.5 3.6 %collective-permute-done.38.refs_3_ = f32[4,32,256]{2,1,0:T(8,128)S(1)} collective-permute-done((f32[4,32,256]{2,1,0:T(8,128)S(1)}, f32[4,32,256]{2,1,0:T(8,128)S(1)}, u32[]{:S(2)}, u32[]{:S(2)}) %collective-permute-start.38) | collective-permute-done | bytes 131104 | tf_op jit(solution)/shard_map/ppermute | solution.py:594
  132.6 7.1 %collective-permute-done.43.refs_3_ = f32[8,32,256]{2,1,0:T(8,128)S(1)} collective-permute-done((f32[8,32,256]{2,1,0:T(8,128)S(1)}, f32[8,32,256]{2,1,0:T(8,128)S(1)}, u32[]{:S(2)}, u32[]{:S(2)}) %collective-permute-start.43) | collective-permute-done | bytes 262176 | tf_op jit(solution)/shard_map/ppermute | solution.py:594
  144.4 12.1 %collective-permute-done.45.refs_0_ = f32[8,72,256]{2,1,0:T(8,128)S(1)} collective-permute-done((f32[8,72,256]{2,1,0:T(8,128)S(1)}, f32[8,72,256]{2,1,0:T(8,128)S(1)}, u32[]{:S(2)}, u32[]{:S(2)}) %collective-permute-start.45) | collective-permute-done | bytes 589856 | tf_op jit(solution)/shard_map/ppermute | solution.py:594
  157.2 1.9 %shard_map.182.refs_1_ = f32[2,200,4096]{2,1,0:T(8,128)} custom-call(s32[2]{0:T(128)S(1)} %get-tuple-element.337.spot_ref, f32[8,200,256]{2,1,0:T(8,128)S(1)} %shard_map.181.refs_0_), custom_call_target="tpu_custom_call" | custom-call | bytes 3276800 | tf_op jit(solution)/shard_map/pallas_call | solution.py:374
  159.1 2.1 %shard_map.178.refs_0_ = f32[2,200,1280]{2,1,0:T(8,128)} custom-call(s32[2]{0:T(128)S(1)} %get-tuple-element.337.spot_ref, f32[16,72,256]{2,1,0:T(8,128)S(1)} %shard_map.177.all_ref), custom_call_target="tpu_custom_call" | custom-call | bytes 1024000 | tf_op jit(solution)/shard_map/pallas_call | solution.py:340
  161.2 2.1 %shard_map.179 = f32[2,200,1280]{2,1,0:T(8,128)} custom-call(s32[2]{0:T(128)S(1)} %get-tuple-element.336.spot_ref, f32[16,72,256]{2,1,0:T(8,128)S(1)} %collective-permute-done.44.all_ref, f32[2,200,1280]{2,1,0:T(8,128)} %shard_map.178.refs_0_), custom_call_target="tpu_custom_call", output_to_operand_aliasing={{}: (2, {})} | custom-call | bytes 1024000 | tf_op jit(solution)/shard_map/pallas_call | solution.py:340
  163.2 1.9 %shard_map.183.refs_3_ = f32[2,200,4096]{2,1,0:T(8,128)} custom-call(s32[2]{0:T(128)S(1)} %get-tuple-element.336.spot_ref, f32[8,200,256]{2,1,0:T(8,128)S(1)} %collective-permute-done.51.refs_0_, f32[2,200,4096]{2,1,0:T(8,128)} %shard_map.182.refs_1_), custom_call_target="tpu_custom_call", output_to_operand_aliasing={{}: (2, {})} | custom-call | bytes 3276800 | tf_op jit(solution)/shard_map/pallas_call | solution.py:374
  165.1 1.9 %shard_map.184.refs_3_ = f32[2,200,4096]{2,1,0:T(8,128)} custom-call(s32[2]{0:T(128)S(1)} %get-tuple-element.337.spot_ref, f32[8,72,256]{2,1,0:T(8,128)S(1)} %collective-permute-done.45.refs_0_, f32[8,64,256]{2,1,0:T(8,128)S(1)} %collective-permute-done.47.refs_1_, ...), custom_call_target="tpu_custom_call", output_to_operand_aliasing={{}: (4, {})} | custom-call | bytes 3276800 | tf_op jit(solution)/shard_map/pallas_call | solution.py:374
  167.1 1.9 %shard_map.185 = f32[2,200,4096]{2,1,0:T(8,128)} custom-call(s32[2]{0:T(128)S(1)} %get-tuple-element.336.spot_ref, f32[8,72,256]{2,1,0:T(8,128)S(1)} %collective-permute-done.46.refs_0_, f32[8,64,256]{2,1,0:T(8,128)S(1)} %collective-permute-done.48.refs_1_, f32[8,64,256]{2,1,0:T(8,128)S(1)} %collective-permute-done.50.refs_2_, ...), custom_call_target="tpu_custom_call", output_to_operand_aliasing={{}: (4, {})} | custom-call | bytes 3276800 | tf_op jit(solution)/shard_map/pallas_call | solution.py:374
  (137 shorter events, 45.7 us)
Async XLA Ops:
  23.8 8.6 %collective-permute-start.2 = (f32[200,768]{1,0:T(8,128)}, f32[200,768]{1,0:T(8,128)S(1)}, u32[]{:S(2)}, u32[]{:S(2)}) collective-permute-start(f32[200,768]{1,0:T(8,128)} %get-tuple-element.183), channel_id=1, source_target_pairs={{0,4},{4,0},{8,12},{12,8},{16,20},{20,16},{24,28},{28,24},{1,5},{5... | collective-permute-start | bytes 1843208 | tf_op jit(solution)/shard_map/ppermute | solution.py:594
  24.3 15.7 %collective-permute-start = (f32[408,512]{1,0:T(8,128)}, f32[408,512]{1,0:T(8,128)}, u32[]{:S(2)}, u32[]{:S(2)}) collective-permute-start(f32[408,512]{1,0:T(8,128)} %get-tuple-element.176), channel_id=1, source_target_pairs={{0,4},{4,8},{8,12},{12,16},{16,20},{20,24},{24,28},{28,0},{1,5},{5... | collective-permute-start | bytes 2506760 | tf_op jit(solution)/shard_map/ppermute | solution.py:590
  36.2 15.8 %collective-permute-start.4 = (f32[8,72,256]{2,1,0:T(8,128)S(1)}, f32[8,72,256]{2,1,0:T(8,128)S(1)}, u32[]{:S(2)}, u32[]{:S(2)}) collective-permute-start(f32[8,72,256]{2,1,0:T(8,128)S(1)} %get-tuple-element.185), channel_id=1, source_target_pairs={{0,8},{4,12},{8,0},{12,4},{16,24},{20,28},{24,16},{28,20},{1,9},{5... | collective-permute-start | bytes 1769480 | tf_op jit(solution)/shard_map/ppermute | solution.py:594
  37.7 13.8 %collective-permute-start.5 = (f32[8,64,256]{2,1,0:T(8,128)S(1)}, f32[8,64,256]{2,1,0:T(8,128)S(1)}, u32[]{:S(2)}, u32[]{:S(2)}) collective-permute-start(f32[8,64,256]{2,1,0:T(8,128)S(1)} %get-tuple-element.186), channel_id=1, source_target_pairs={{0,16},{4,20},{8,24},{12,28},{16,0},{20,4},{24,8},{28,12},{1,17},{... | collective-permute-start | bytes 1572872 | tf_op jit(solution)/shard_map/ppermute | solution.py:594
  38.4 13.5 %collective-permute-start.6 = (f32[8,64,256]{2,1,0:T(8,128)S(1)}, f32[8,64,256]{2,1,0:T(8,128)S(1)}, u32[]{:S(2)}, u32[]{:S(2)}) collective-permute-start(f32[8,64,256]{2,1,0:T(8,128)S(1)} %get-tuple-element.187), channel_id=1, source_target_pairs={{0,1},{1,0},{2,3},{3,2},{4,5},{5,4},{6,7},{7,6},{8,9},{9,8},{10,11... | collective-permute-start | bytes 1572872 | tf_op jit(solution)/shard_map/ppermute | solution.py:594
  52.1 9.7 %collective-permute-start.8 = (f32[4,72,256]{2,1,0:T(8,128)S(1)}, f32[4,72,256]{2,1,0:T(8,128)S(1)}, u32[]{:S(2)}, u32[]{:S(2)}) collective-permute-start(f32[4,72,256]{2,1,0:T(8,128)S(1)} %get-tuple-element.202), channel_id=1, source_target_pairs={{0,16},{4,20},{8,24},{12,28},{16,0},{20,4},{24,8},{28,12},{1,17},{... | collective-permute-start | bytes 884744 | tf_op jit(solution)/shard_map/ppermute | solution.py:594
  53.5 8.2 %collective-permute-start.10 = (f32[4,64,256]{2,1,0:T(8,128)S(1)}, f32[4,64,256]{2,1,0:T(8,128)S(1)}, u32[]{:S(2)}, u32[]{:S(2)}) collective-permute-start(f32[4,64,256]{2,1,0:T(8,128)S(1)} %get-tuple-element.204), channel_id=1, source_target_pairs={{0,8},{4,12},{8,0},{12,4},{16,24},{20,28},{24,16},{28,20},{1,9},{5... | collective-permute-start | bytes 786440 | tf_op jit(solution)/shard_map/ppermute | solution.py:594
  58.8 10.6 %collective-permute-start.11 = (f32[8,40,256]{2,1,0:T(8,128)S(1)}, f32[8,40,256]{2,1,0:T(8,128)S(1)}, u32[]{:S(2)}, u32[]{:S(2)}) collective-permute-start(f32[8,40,256]{2,1,0:T(8,128)S(1)} %get-tuple-element.216), channel_id=1, source_target_pairs={{0,8},{4,12},{8,0},{12,4},{16,24},{20,28},{24,16},{28,20},{1,9},{5... | collective-permute-start | bytes 983048 | tf_op jit(solution)/shard_map/ppermute | solution.py:594
  61.9 10.2 %collective-permute-start.13 = (f32[2,72,256]{2,1,0:T(8,128)S(1)}, f32[2,72,256]{2,1,0:T(8,128)S(1)}, u32[]{:S(2)}, u32[]{:S(2)}) collective-permute-start(f32[2,72,256]{2,1,0:T(8,128)S(1)} %get-tuple-element.222), channel_id=1, source_target_pairs={{0,1},{1,0},{2,3},{3,2},{4,5},{5,4},{6,7},{7,6},{8,9},{9,8},{10,11... | collective-permute-start | bytes 442376 | tf_op jit(solution)/shard_map/ppermute | solution.py:594
  72.2 8.2 %collective-permute-start.18 = (f32[1,72,256]{2,1,0:T(8,128)S(1)}, f32[1,72,256]{2,1,0:T(8,128)S(1)}, u32[]{:S(2)}, u32[]{:S(2)}) collective-permute-start(f32[1,72,256]{2,1,0:T(8,128)S(1)} %get-tuple-element.242), channel_id=1, source_target_pairs={{0,2},{1,3},{2,0},{3,1},{4,6},{5,7},{6,4},{7,5},{8,10},{9,11},{10,... | collective-permute-start | bytes 221192 | tf_op jit(solution)/shard_map/ppermute | solution.py:594
  87.4 10.5 %collective-permute-start.24 = (f32[1,40,256]{2,1,0:T(8,128)S(1)}, f32[1,40,256]{2,1,0:T(8,128)S(1)}, u32[]{:S(2)}, u32[]{:S(2)}) collective-permute-start(f32[1,40,256]{2,1,0:T(8,128)S(1)} %get-tuple-element.273), channel_id=1, source_target_pairs={{0,2},{1,3},{2,0},{3,1},{4,6},{5,7},{6,4},{7,5},{8,10},{9,11},{10,... | collective-permute-start | bytes 122888 | tf_op jit(solution)/shard_map/ppermute | solution.py:594
  89.7 8.2 %collective-permute-start.25 = (f32[1,32,256]{2,1,0:T(8,128)S(1)}, f32[1,32,256]{2,1,0:T(8,128)S(1)}, u32[]{:S(2)}, u32[]{:S(2)}) collective-permute-start(f32[1,32,256]{2,1,0:T(8,128)S(1)} %get-tuple-element.274), channel_id=1, source_target_pairs={{0,2},{1,3},{2,0},{3,1},{4,6},{5,7},{6,4},{7,5},{8,10},{9,11},{10,... | collective-permute-start | bytes 98312 | tf_op jit(solution)/shard_map/ppermute | solution.py:594
  90.4 10.6 %collective-permute-start.26 = (f32[1,72,256]{2,1,0:T(8,128)S(1)}, f32[1,72,256]{2,1,0:T(8,128)S(1)}, u32[]{:S(2)}, u32[]{:S(2)}) collective-permute-start(f32[1,72,256]{2,1,0:T(8,128)S(1)} %get-tuple-element.282.refs_0_), channel_id=1, source_target_pairs={{0,2},{1,3},{2,0},{3,1},{4,6},{5,7},{6,4},{7,5},{8,10},{9,11},{10,... | collective-permute-start | bytes 221192 | tf_op jit(solution)/shard_map/ppermute | solution.py:594
  92.7 8.3 %collective-permute-start.27 = (f32[1,64,256]{2,1,0:T(8,128)S(1)}, f32[1,64,256]{2,1,0:T(8,128)S(1)}, u32[]{:S(2)}, u32[]{:S(2)}) collective-permute-start(f32[1,64,256]{2,1,0:T(8,128)S(1)} %get-tuple-element.283.refs_1_), channel_id=1, source_target_pairs={{0,2},{1,3},{2,0},{3,1},{4,6},{5,7},{6,4},{7,5},{8,10},{9,11},{10,... | collective-permute-start | bytes 196616 | tf_op jit(solution)/shard_map/ppermute | solution.py:594
  101.0 13.0 %collective-permute-start.32 = (f32[2,72,256]{2,1,0:T(8,128)S(1)}, f32[2,72,256]{2,1,0:T(8,128)S(1)}, u32[]{:S(2)}, u32[]{:S(2)}) collective-permute-start(f32[2,72,256]{2,1,0:T(8,128)S(1)} %get-tuple-element.303.refs_0_), channel_id=1, source_target_pairs={{0,1},{1,0},{2,3},{3,2},{4,5},{5,4},{6,7},{7,6},{8,9},{9,8},{10,11... | collective-permute-start | bytes 442376 | tf_op jit(solution)/shard_map/ppermute | solution.py:594
  101.1 12.9 %collective-permute-start.33 = (f32[2,64,256]{2,1,0:T(8,128)S(1)}, f32[2,64,256]{2,1,0:T(8,128)S(1)}, u32[]{:S(2)}, u32[]{:S(2)}) collective-permute-start(f32[2,64,256]{2,1,0:T(8,128)S(1)} %get-tuple-element.304.refs_1_), channel_id=1, source_target_pairs={{0,8},{4,12},{8,0},{12,4},{16,24},{20,28},{24,16},{28,20},{1,9},{5... | collective-permute-start | bytes 393224 | tf_op jit(solution)/shard_map/ppermute | solution.py:594
  102.3 11.8 %collective-permute-start.34 = (f32[2,64,256]{2,1,0:T(8,128)S(1)}, f32[2,64,256]{2,1,0:T(8,128)S(1)}, u32[]{:S(2)}, u32[]{:S(2)}) collective-permute-start(f32[2,64,256]{2,1,0:T(8,128)S(1)} %get-tuple-element.305.refs_2_), channel_id=1, source_target_pairs={{0,2},{1,3},{2,0},{3,1},{4,6},{5,7},{6,4},{7,5},{8,10},{9,11},{10,... | collective-permute-start | bytes 393224 | tf_op jit(solution)/shard_map/ppermute | solution.py:594
  105.2 8.8 %collective-permute-start.30 = (f32[1,40,256]{2,1,0:T(8,128)S(1)}, f32[1,40,256]{2,1,0:T(8,128)S(1)}, u32[]{:S(2)}, u32[]{:S(2)}) collective-permute-start(f32[1,40,256]{2,1,0:T(8,128)S(1)} %get-tuple-element.292.refs_0_), channel_id=1, source_target_pairs={{0,2},{1,3},{2,0},{3,1},{4,6},{5,7},{6,4},{7,5},{8,10},{9,11},{10,... | collective-permute-start | bytes 122888 | tf_op jit(solution)/shard_map/ppermute | solution.py:594
  105.7 8.4 %collective-permute-start.31 = (f32[1,32,256]{2,1,0:T(8,128)S(1)}, f32[1,32,256]{2,1,0:T(8,128)S(1)}, u32[]{:S(2)}, u32[]{:S(2)}) collective-permute-start(f32[1,32,256]{2,1,0:T(8,128)S(1)} %get-tuple-element.293.refs_1_), channel_id=1, source_target_pairs={{0,2},{1,3},{2,0},{3,1},{4,6},{5,7},{6,4},{7,5},{8,10},{9,11},{10,... | collective-permute-start | bytes 98312 | tf_op jit(solution)/shard_map/ppermute | solution.py:594
  114.1 16.0 %collective-permute-start.39 = (f32[4,72,256]{2,1,0:T(8,128)S(1)}, f32[4,72,256]{2,1,0:T(8,128)S(1)}, u32[]{:S(2)}, u32[]{:S(2)}) collective-permute-start(f32[4,72,256]{2,1,0:T(8,128)S(1)} %get-tuple-element.325.refs_0_), channel_id=1, source_target_pairs={{0,16},{4,20},{8,24},{12,28},{16,0},{20,4},{24,8},{28,12},{1,17},{... | collective-permute-start | bytes 884744 | tf_op jit(solution)/shard_map/ppermute | solution.py:594
  115.3 14.8 %collective-permute-start.40 = (f32[4,64,256]{2,1,0:T(8,128)S(1)}, f32[4,64,256]{2,1,0:T(8,128)S(1)}, u32[]{:S(2)}, u32[]{:S(2)}) collective-permute-start(f32[4,64,256]{2,1,0:T(8,128)S(1)} %get-tuple-element.326.refs_1_), channel_id=1, source_target_pairs={{0,1},{1,0},{2,3},{3,2},{4,5},{5,4},{6,7},{7,6},{8,9},{9,8},{10,11... | collective-permute-start | bytes 786440 | tf_op jit(solution)/shard_map/ppermute | solution.py:594
  115.3 14.8 %collective-permute-start.41 = (f32[4,64,256]{2,1,0:T(8,128)S(1)}, f32[4,64,256]{2,1,0:T(8,128)S(1)}, u32[]{:S(2)}, u32[]{:S(2)}) collective-permute-start(f32[4,64,256]{2,1,0:T(8,128)S(1)} %get-tuple-element.327.refs_2_), channel_id=1, source_target_pairs={{0,8},{4,12},{8,0},{12,4},{16,24},{20,28},{24,16},{28,20},{1,9},{5... | collective-permute-start | bytes 786440 | tf_op jit(solution)/shard_map/ppermute | solution.py:594
  130.3 33.0 %collective-permute-start.51 = (f32[8,200,256]{2,1,0:T(8,128)S(1)}, f32[8,200,256]{2,1,0:T(8,128)S(1)}, u32[]{:S(2)}, u32[]{:S(2)}) collective-permute-start(f32[8,200,256]{2,1,0:T(8,128)S(1)} %shard_map.181.refs_0_), channel_id=1, source_target_pairs={{0,4},{4,0},{8,12},{12,8},{16,20},{20,16},{24,28},{28,24},{1,5},{5... | collective-permute-start | bytes 4915208 | tf_op jit(solution)/shard_map/ppermute | solution.py:594
  130.3 10.1 %collective-permute-start.42 = (f32[8,40,256]{2,1,0:T(8,128)S(1)}, f32[8,40,256]{2,1,0:T(8,128)S(1)}, u32[]{:S(2)}, u32[]{:S(2)}) collective-permute-start(f32[8,40,256]{2,1,0:T(8,128)S(1)} %get-tuple-element.323.refs_0_), channel_id=1, source_target_pairs={{0,8},{4,12},{8,0},{12,4},{16,24},{20,28},{24,16},{28,20},{1,9},{5... | collective-permute-start | bytes 983048 | tf_op jit(solution)/shard_map/ppermute | solution.py:594
  131.3 8.4 %collective-permute-start.43 = (f32[8,32,256]{2,1,0:T(8,128)S(1)}, f32[8,32,256]{2,1,0:T(8,128)S(1)}, u32[]{:S(2)}, u32[]{:S(2)}) collective-permute-start(f32[8,32,256]{2,1,0:T(8,128)S(1)} %get-tuple-element.324.refs_1_), channel_id=1, source_target_pairs={{0,16},{4,20},{8,24},{12,28},{16,0},{20,4},{24,8},{28,12},{1,17},{... | collective-permute-start | bytes 786440 | tf_op jit(solution)/shard_map/ppermute | solution.py:594
  140.5 20.6 %collective-permute-start.44 = (f32[16,72,256]{2,1,0:T(8,128)S(1)}, f32[16,72,256]{2,1,0:T(8,128)S(1)}, u32[]{:S(2)}, u32[]{:S(2)}) collective-permute-start(f32[16,72,256]{2,1,0:T(8,128)S(1)} %shard_map.177.all_ref), channel_id=1, source_target_pairs={{0,4},{4,0},{8,12},{12,8},{16,20},{20,16},{24,28},{28,24},{1,5},{5... | collective-permute-start | bytes 3538952 | tf_op jit(solution)/shard_map/ppermute | solution.py:594
  140.7 15.8 %collective-permute-start.45 = (f32[8,72,256]{2,1,0:T(8,128)S(1)}, f32[8,72,256]{2,1,0:T(8,128)S(1)}, u32[]{:S(2)}, u32[]{:S(2)}) collective-permute-start(f32[8,72,256]{2,1,0:T(8,128)S(1)} %get-tuple-element.331), channel_id=1, source_target_pairs={{0,8},{4,12},{8,0},{12,4},{16,24},{20,28},{24,16},{28,20},{1,9},{5... | collective-permute-start | bytes 1769480 | tf_op jit(solution)/shard_map/ppermute | solution.py:594
  141.7 14.8 %collective-permute-start.47 = (f32[8,64,256]{2,1,0:T(8,128)S(1)}, f32[8,64,256]{2,1,0:T(8,128)S(1)}, u32[]{:S(2)}, u32[]{:S(2)}) collective-permute-start(f32[8,64,256]{2,1,0:T(8,128)S(1)} %get-tuple-element.332), channel_id=1, source_target_pairs={{0,16},{4,20},{8,24},{12,28},{16,0},{20,4},{24,8},{28,12},{1,17},{... | collective-permute-start | bytes 1572872 | tf_op jit(solution)/shard_map/ppermute | solution.py:594
  143.0 14.0 %collective-permute-start.49 = (f32[8,64,256]{2,1,0:T(8,128)S(1)}, f32[8,64,256]{2,1,0:T(8,128)S(1)}, u32[]{:S(2)}, u32[]{:S(2)}) collective-permute-start(f32[8,64,256]{2,1,0:T(8,128)S(1)} %get-tuple-element.333), channel_id=1, source_target_pairs={{0,1},{1,0},{2,3},{3,2},{4,5},{5,4},{6,7},{7,6},{8,9},{9,8},{10,11... | collective-permute-start | bytes 1572872 | tf_op jit(solution)/shard_map/ppermute | solution.py:594
  156.5 10.5 %collective-permute-start.46 = (f32[8,72,256]{2,1,0:T(8,128)S(1)}, f32[8,72,256]{2,1,0:T(8,128)S(1)}, u32[]{:S(2)}, u32[]{:S(2)}) collective-permute-start(f32[8,72,256]{2,1,0:T(8,128)S(1)} %collective-permute-done.45.refs_0_), channel_id=1, source_target_pairs={{0,4},{4,0},{8,12},{12,8},{16,20},{20,16},{24,28},{28,24},{1,5},{5... | collective-permute-start | bytes 1769480 | tf_op jit(solution)/shard_map/ppermute | solution.py:594
  156.5 10.5 %collective-permute-start.48 = (f32[8,64,256]{2,1,0:T(8,128)S(1)}, f32[8,64,256]{2,1,0:T(8,128)S(1)}, u32[]{:S(2)}, u32[]{:S(2)}) collective-permute-start(f32[8,64,256]{2,1,0:T(8,128)S(1)} %collective-permute-done.47.refs_1_), channel_id=1, source_target_pairs={{0,4},{4,0},{8,12},{12,8},{16,20},{20,16},{24,28},{28,24},{1,5},{5... | collective-permute-start | bytes 1572872 | tf_op jit(solution)/shard_map/ppermute | solution.py:594
  157.0 10.0 %collective-permute-start.50 = (f32[8,64,256]{2,1,0:T(8,128)S(1)}, f32[8,64,256]{2,1,0:T(8,128)S(1)}, u32[]{:S(2)}, u32[]{:S(2)}) collective-permute-start(f32[8,64,256]{2,1,0:T(8,128)S(1)} %collective-permute-done.49.refs_2_), channel_id=1, source_target_pairs={{0,4},{4,0},{8,12},{12,8},{16,20},{20,16},{24,28},{28,24},{1,5},{5... | collective-permute-start | bytes 1572872 | tf_op jit(solution)/shard_map/ppermute | solution.py:594
  (34 other events, 294.3 us)

commit v5 on v4

--- a/solution.py
+++ b/solution.py
@@ -15,6 +15,7 @@
 SMEM = pl.BlockSpec(memory_space=pltpu.SMEM)
 PARAMS = pltpu.CompilerParams(vmem_limit_bytes=16 * 1024 * 1024)
 GATHER_PARAMS = pltpu.CompilerParams(vmem_limit_bytes=32 * 1024 * 1024)
+HBM = pl.BlockSpec(memory_space=pltpu.HBM)
 COST = pl.CostEstimate(flops=10000, bytes_accessed=10000, transcendentals=0)
 
 
@@ -103,10 +104,9 @@
     buckets, hubs = hub_idx.shape
     edges = rel_idx.shape[1]
     shapes = [(features, hubs)] * buckets + [(features, edges)] * buckets
-    anywhere = pl.BlockSpec(memory_space=pl.ANY)
     out = pl.pallas_call(
         functools.partial(gather_kernel, hub_steps, rel_steps),
-        in_specs=[VMEM, VMEM, anywhere, anywhere],
+        in_specs=[VMEM, VMEM, HBM, HBM],
         out_specs=[VMEM] * (1 + len(shapes)),
         out_shape=[jax.ShapeDtypeStruct((buckets, hubs + edges), jnp.int32)]
         + [jax.ShapeDtypeStruct(shape, F32) for shape in shapes],
@@ -156,16 +156,17 @@
     return sends[s].at[index - half] if index >= half else keeps[s].at[index]
 
 
-def chunk_refs(orders, grad_lanes, refs):
+def chunk_refs(grad_lanes, refs):
     ids, refs = refs[:2], refs[2:]
     grads, refs = list(zip(refs, grad_lanes)), refs[len(grad_lanes) :]
+    return ids, grads, refs[:-2], refs[-2:]
+
+
+def hub_chunks_kernel(orders, spans, id_lanes, grad_lanes, chip_ref, *refs):
+    ids, grads, outs, (idx_down, stacked) = chunk_refs(grad_lanes, refs)
+    load_columns(ids, id_lanes, grads, idx_down, stacked)
     streams = len(orders)
-    return ids, grads, refs[:streams], refs[streams : 2 * streams], refs[2 * streams :]
-
-
-def hub_chunks_kernel(orders, spans, id_lanes, grad_lanes, chip_ref, *refs):
-    ids, grads, sends, keeps, (idx_down, stacked) = chunk_refs(orders, grad_lanes, refs)
-    load_columns(ids, id_lanes, grads, idx_down, stacked)
+    sends, keeps = outs[:streams], outs[streams:]
     chunks, width = 2 * keeps[0].shape[0], keeps[0].shape[2]
     lane = lax.broadcasted_iota(jnp.int32, (1, width), 1)
     for place in range(chunks):
@@ -183,16 +184,17 @@
         for s, (first, end) in enumerate(spans):
             count = min(end, high - low) - first
             if count > 0:
-                pieces.append((block, s, low + first, first, count))
+                pieces.append((block, s, low + first, count))
     return spans, pieces
 
 
-def rel_chunks_kernel(orders, pieces, rows, id_lanes, grad_lanes, chip_ref, *refs):
-    ids, grads, sends, keeps, (idx_down, stacked) = chunk_refs(orders, grad_lanes, refs)
+def rel_chunks_kernel(pieces, rows, id_lanes, grad_lanes, chip_ref, *refs):
+    ids, grads, outs, (idx_down, stacked) = chunk_refs(grad_lanes, refs)
     load_columns(ids, id_lanes, grads, idx_down, stacked)
-    for ref in [*sends, *keeps]:
+    for ref in outs:
         ref[...] = jnp.zeros_like(ref)
-    chunks, lanes = 2 * keeps[0].shape[0], keeps[0].shape[2]
+    depth, lanes = outs[0].shape[0], outs[0].shape[2]
+    chunks = depth * len(outs)
     width = rows // chunks
     group = lanes // width
     lane = lax.broadcasted_iota(jnp.int32, (1, lanes), 1)
@@ -204,22 +206,21 @@
             targets = jnp.where(here, lane + ((chip_ref[0] ^ place) * width - slot * width), targets)
         dense = dot2(stacked[...], onehot_across(idx_down, targets), NN)
         for slot, place in enumerate(places):
+            out = outs[place // depth].at[place % depth]
             chunk = dense[:, slot * width : (slot + 1) * width]
-            for block, s, low, unused, count in pieces:
-                out = out_for(place, orders[s], sends, keeps, s)
+            for block, unused, low, count in pieces:
                 out[:count, block * width : (block + 1) * width] = chunk[low : low + count]
 
 
-def chunk_columns(kernel, heights, lanes, chip, ids, grads, chunks):
+def chunk_columns(kernel, shapes, chip, ids, grads):
     half_width = grads[0][0].shape[0]
     grad_lanes = [lanes_of for unused, lanes_of in grads]
     count = sum(high - low for low, high in grad_lanes)
-    shapes = [jax.ShapeDtypeStruct((chunks // 2, height, lanes), F32) for height in heights] * 2
-    out = pl.pallas_call(
+    return pl.pallas_call(
         functools.partial(kernel, grad_lanes),
         in_specs=[SMEM] + [VMEM] * (2 + len(grads)),
         out_specs=[VMEM] * len(shapes),
-        out_shape=shapes,
+        out_shape=[jax.ShapeDtypeStruct(shape, F32) for shape in shapes],
         scratch_shapes=[
             pltpu.VMEM((count, 128), jnp.int32),
             pltpu.VMEM((2 * (-(-half_width // 16) * 16), count), BF16),
@@ -227,7 +228,6 @@
         compiler_params=PARAMS,
         cost_estimate=COST,
     )(chip, *ids, *[g for g, unused in grads])
-    return out[: len(heights)], out[len(heights) :]
 
 
 def call(kernel, ins, shapes):
@@ -269,118 +269,133 @@
     return call(join_kernel, [*own, *got], [(2 * x.shape[0],) + x.shape[1:] for x in own])
 
 
-def squares_kernel(*refs):
-    streams = len(refs) // 3
-    own, got, totals, out = [refs[i * streams : (i + 1) * streams] for i in range(3)] + [refs[-1]]
-    squares = jnp.zeros(out.shape, F32)
+def plane_sums_kernel(*refs):
+    ins, outs = refs[: -refs[0].shape[0]], refs[-refs[0].shape[0] :]
+    for place, out in enumerate(outs):
+        out[0] = sum(ref[place] for ref in ins)
+
+
+def squares_kernel(streams, *refs):
+    own, got, rels = refs[:streams], refs[streams : 2 * streams], refs[2 * streams : -streams - 2]
+    totals, rel_total, out = refs[-streams - 2 : -2], refs[-2], refs[-1]
+    squares = jnp.zeros((1, out.shape[1]), F32)
     for s in range(streams):
         total = own[s][0] + got[s][0]
         totals[s][0] = total
         squares += jnp.sum(total * total, axis=0, keepdims=True)
-    out[...] = squares
-
-
-def squares_of(own, got):
-    *totals, squares = call(squares_kernel, [*own, *got], [x.shape for x in own] + [(1, own[0].shape[2])])
-    return totals, squares
-
-
-def hub_update_kernel(spans, features, *refs):
+    total = sum(ref[0] for ref in rels)
+    rel_total[0] = total
+    out[0:1] = squares
+    out[1:2] = jnp.sum(total * total, axis=0, keepdims=True)
+
+
+def update_kernel(spans, rel_spans, pieces, features, *refs):
     streams = len(spans)
     totals, news = refs[:streams], refs[-streams:]
-    mine, other, table_ref, sums_ref = refs[streams:-streams]
-    scale = step_rate / jnp.sqrt(sums_ref[...] + (mine[...] + other[...]) * (1.0 / features))
+    rel_total, mine, other, hub_ref, hub_sums, rel_ref, rel_sums = refs[streams:-streams]
+    width = rel_ref.shape[1]
+    squares = mine[...] + other[...]
+    hub_scale = step_rate / jnp.sqrt(hub_sums[...] + squares[0:1] * (1.0 / features))
+    rel_squares = sum(squares[1:2, b * width : (b + 1) * width] for b in range(3))
+    rel_scale = step_rate / jnp.sqrt(rel_sums[...] + rel_squares * (1.0 / features))
     for s, (low, high) in enumerate(spans):
-        news[s][0] = table_ref[low:high] - totals[s][0] * scale
-
-
-def rel_update_kernel(streams, pieces, features, *refs):
-    totals, news = refs[:streams], refs[-streams:]
-    mine, other, table_ref, sums_ref = refs[streams:-streams]
-    width = table_ref.shape[1]
-    squares = mine[...] + other[...]
-    squares = sum(squares[:, b * width : (b + 1) * width] for b in range(3))
-    scale = step_rate / jnp.sqrt(sums_ref[...] + squares * (1.0 / features))
-    for new in news:
-        new[...] = jnp.zeros_like(new)
-    for block, s, low, unused, count in pieces:
-        lanes = slice(block * width, (block + 1) * width)
-        news[s][0, :count, lanes] = table_ref[low : low + count] - totals[s][0, :count, lanes] * scale
-
-
-def combine_kernel(spans, *refs):
-    streams, out = len(spans), refs[-1]
-    for i, ref in enumerate(refs[:-1]):
-        low, high = spans[i % streams]
-        count = ref.shape[0]
-        first = (i // streams) * count
-        out[first : first + count, low:high] = ref[...]
-
-
-def combine(spans, *groups):
-    parts = [x for group in groups for x in group]
-    count = sum(group[0].shape[0] for group in groups)
-    return call(functools.partial(combine_kernel, spans), parts, [(count, spans[-1][1], parts[0].shape[2])])[0]
-
-
-def place_kernel(orders, pieces, spot_ref, all_ref, *refs):
-    out_ref = refs[-1]
-    chunks = all_ref.shape[0]
-    width = out_ref.shape[2] // chunks
-    for chunk in range(chunks):
-        place = spot_ref[0] ^ chunk
-        values = [all_ref[spread_bits(place, order)] for order in orders]
-        for block, s, row, source, count in pieces:
-            part = values[s][source : source + count, block * width : (block + 1) * width]
-            out_ref[0, row : row + count, chunk * width : (chunk + 1) * width] = part
-
-
-def place_chunks(spot, parts, orders, pieces, shape, earlier):
-    kept = [pl.BlockSpec(memory_space=pl.ANY)] * len(earlier)
-    return pl.pallas_call(
-        functools.partial(place_kernel, orders, pieces),
-        grid_spec=pltpu.PrefetchScalarGridSpec(
-            num_scalar_prefetch=1,
-            grid=(1,),
-            in_specs=[pl.BlockSpec(memory_space=pltpu.VMEM)] + kept,
-            out_specs=pl.BlockSpec((1,) + shape[1:], lambda i, spot: (spot[1], 0, 0)),
-        ),
-        out_shape=jax.ShapeDtypeStruct(shape, F32),
-        input_output_aliases={2: 0} if earlier else {},
-        compiler_params=PARAMS,
-        cost_estimate=pl.CostEstimate(flops=0, bytes_accessed=4 * shape[1] * shape[2], transcendentals=0),
-    )(spot, parts, *earlier)
-
-
-def copy_kernel(orders, spans, upper, spot_ref, *refs):
-    out_ref, sems = refs[-2], refs[-1]
+        height = high - low
+        news[s][0, :height] = hub_ref[low:high] - totals[s][0] * hub_scale
+        news[s][0, height:] = jnp.zeros_like(news[s][0, height:])
+    for block, s, low, count in pieces:
+        lanes, height = slice(block * width, (block + 1) * width), spans[s][1] - spans[s][0]
+        first = rel_spans[s][0]
+        news[s][0, height : height + count, lanes] = (
+            rel_ref[low : low + count] - rel_total[0, first : first + count, lanes] * rel_scale
+        )
+
+
+def join_all_kernel(bases, *refs):
+    streams = len(bases)
+    join_kernel(*refs[:-1])
+    for s, base in enumerate(bases):
+        for i, ref in enumerate((refs[s], refs[streams + s])):
+            count, height = ref.shape[0], ref.shape[1]
+            refs[-1][i * count : (i + 1) * count, base : base + height] = ref[...]
+
+
+def join_all(own, got):
+    heights = [x.shape[1] for x in own]
+    bases = [sum(heights[:s]) for s in range(len(own))]
+    count, width = 2 * own[0].shape[0], own[0].shape[2]
+    shapes = [(count, height, width) for height in heights] + [(count, sum(heights), width)]
+    *have, near = call(functools.partial(join_all_kernel, bases), [*own, *got], shapes)
+    return have, near, bases
+
+
+def chunk_copies(part, base, first, order, span, spot_ref, out_ref, sems, at):
+    low, high = span
+    width = part.shape[2]
+    for index in range(part.shape[0]):
+        chunk = spot_ref[0] ^ gather_bits(first + index, order)
+        lanes = pl.ds(pl.multiple_of(chunk * width, width), width)
+        target = out_ref.at[spot_ref[1], pl.ds(low, high - low), lanes]
+        yield pltpu.make_async_copy(part.at[index, pl.ds(base, high - low)], target, sems.at[at + index])
+
+
+def near_kernel(orders, spans, bases, spot_ref, near_ref, *refs):
+    out_ref, sems = refs[-2:]
     copies = []
-    for s, (low, high) in enumerate(spans):
-        part = refs[s] if upper else refs[0].at[:, pl.ds(low, high - low)]
-        half, width = part.shape[0], part.shape[2]
-        for index in range(half):
-            chunk = spot_ref[0] ^ gather_bits(index + half * upper, orders[s])
-            lanes = pl.ds(pl.multiple_of(chunk * width, width), width)
-            target = out_ref.at[spot_ref[1], pl.ds(low, high - low), lanes]
-            copies.append(pltpu.make_async_copy(part.at[index], target, sems.at[len(copies)]))
+    for order, span, base in zip(orders, spans, bases):
+        copies += chunk_copies(near_ref, base, 0, order, span, spot_ref, out_ref, sems, len(copies))
     for copy in copies:
         copy.start()
     for copy in copies:
         copy.wait()
 
 
-def copy_chunks(spot, parts, upper, orders, spans, shape, earlier):
-    anywhere = pl.BlockSpec(memory_space=pl.ANY)
+def far_kernel(orders, spans, bases, pieces, by_copy, spot_ref, near_ref, *refs):
+    streams = len(orders)
+    fars = refs[:streams]
+    hub_out, rel_out, hub_all, rel_all, sems = refs[-5:]
+    half = near_ref.shape[0]
+    hub_width, rel_width = hub_out.shape[2] // (2 * half), rel_out.shape[2] // (2 * half)
+    copies = []
+    if by_copy:
+        for far, order, span in zip(fars, orders, spans):
+            copies += chunk_copies(far, 0, half, order, span, spot_ref, hub_out, sems, len(copies))
+        for copy in copies:
+            copy.start()
+    for chunk in range(2 * half):
+        place = spot_ref[0] ^ chunk
+        for s, (low, high) in enumerate(spans):
+            index = spread_bits(place, orders[s])
+            spot = index & (half - 1)
+            height, end = high - low, fars[s].shape[1]
+            if not by_copy:
+                value = jnp.where(index >= half, fars[s][spot, :height], near_ref[spot, bases[s] : bases[s] + height])
+                hub_all[low:high, chunk * hub_width : (chunk + 1) * hub_width] = value
+            value = jnp.where(index >= half, fars[s][spot, height:], near_ref[spot, bases[s] + height : bases[s] + end])
+            for block, stream, row, count in pieces:
+                if stream == s:
+                    part = value[:count, block * rel_width : (block + 1) * rel_width]
+                    rel_all[row : row + count, chunk * rel_width : (chunk + 1) * rel_width] = part
+    copies.append(pltpu.make_async_copy(rel_all, rel_out.at[spot_ref[1]], sems.at[len(copies)]))
+    copies[-1].start()
+    if not by_copy:
+        copies.append(pltpu.make_async_copy(hub_all, hub_out.at[spot_ref[1]], sems.at[len(copies)]))
+        copies[-1].start()
+    for copy in copies:
+        copy.wait()
+
+
+def placed(kernel, scratch, spot, near, fars, outs, earlier):
+    sems = pltpu.SemaphoreType.DMA((3 * near.shape[0] + 2,))
     return pl.pallas_call(
-        functools.partial(copy_kernel, orders, spans, upper),
-        in_specs=[SMEM] + [anywhere] * (len(parts) + len(earlier)),
-        out_specs=anywhere,
-        out_shape=jax.ShapeDtypeStruct(shape, F32),
-        scratch_shapes=[pltpu.SemaphoreType.DMA((len(spans) * parts[0].shape[0],))],
-        input_output_aliases={1 + len(parts): 0} if earlier else {},
+        kernel,
+        in_specs=[SMEM] + [VMEM] * (1 + len(fars)) + [HBM] * len(earlier),
+        out_specs=[HBM] * len(outs),
+        out_shape=[jax.ShapeDtypeStruct(shape, F32) for shape in outs],
+        scratch_shapes=scratch + [sems],
+        input_output_aliases={2 + len(fars) + i: i for i in range(len(earlier))},
         compiler_params=PARAMS,
-        cost_estimate=pl.CostEstimate(flops=0, bytes_accessed=4 * shape[1] * shape[2], transcendentals=0),
-    )(spot, *parts, *earlier)
+        cost_estimate=pl.CostEstimate(flops=0, bytes_accessed=4 * outs[0][1] * outs[0][2], transcendentals=0),
+    )(spot, near, *fars, *earlier)
 
 
 def adagrad(table, state, grads):
@@ -407,7 +422,7 @@
     return x0 * r0 + x1 * r1, x1 * r0 - x0 * r1
 
 
-EDGE_TILE = 256
+EDGE_TILE = 512
 
 
 def edge_span(step):
@@ -594,6 +609,10 @@
     return lax.ppermute(x, axis, [(i, i ^ (1 << bit)) for i in range(lax.axis_size(axis))])
 
 
+def flipped_by(x, axis, offset):
+    return lax.ppermute(x, axis, [(i, i ^ offset) for i in range(lax.axis_size(axis))])
+
+
 def other_core(x):
     return flipped(x, "blk", 0)
 
@@ -635,18 +654,18 @@
     core_id = lax.axis_index("blk") % 2
     chip_id = (lax.axis_index("blk") // 2) * lax.axis_size("sub") + lax.axis_index("sub")
     core, chip = core_id.astype(jnp.int32).reshape(1), chip_id.astype(jnp.int32).reshape(1)
-    hub_orders = stream_orders()
-    rel_orders = hub_orders[:2]
-    spans = row_spans(half_width, len(hub_orders))
-    hub_pieces = [(0, s, low, low, high - low) for s, (low, high) in enumerate(spans)]
-    rel_spans, rel_pieces = rel_layout(half_width, len(rel_orders))
-    heights, rel_heights = [[high - low for low, high in x] for x in (spans, rel_spans)]
-    stages = len(hub_orders[0])
-    chunks = 1 << stages
+    orders = stream_orders()
+    streams, stages = len(orders), len(orders[0])
+    chunks, depth = 1 << stages, lax.axis_size("sub")
+    planes = chunks // depth
+    spans = row_spans(half_width, streams)
+    unused, rel_pieces = rel_layout(half_width, 1)
+    rel_spans, joint_pieces = rel_layout(half_width, streams)
+    rel_height = rel_spans[-1][1]
     width, rel_width = hub_count // chunks, rel_count // chunks
     hub_lanes, rel_lanes = (0, hubs), (hubs, hubs + edges)
 
-    def exchanged(parts, orders, step):
+    def exchanged(parts, step):
         return [across(x, order[step]) for x, order in zip(parts, orders)]
 
     def in_turn(first, then):
@@ -666,18 +685,20 @@
         right = from_behind(right, "blk", 1)
         keeps.append(keep)
         fars.append(other_core(send))
+    far_ids, left = in_turn(far_ids, left)
     last = buckets - 1
     query_grad, hub_keep, hub_send = hub_step(
         last, negatives.shape[1], core, heads, left, rel_rows[last], hub_rows[last]
     )
     hub_far = other_core(hub_send)
     grads = lambda early, late, lanes: [(x, lanes) for x in early] + [(late, (0, late.shape[1]))]
-    send, own = chunk_columns(
-        functools.partial(hub_chunks_kernel, hub_orders, spans, hub_lanes),
-        heights, width, chip, (ids, far_ids),
-        grads(keeps, hub_keep, hub_lanes) + grads(fars, hub_far, hub_lanes), chunks,
-    )
-    got = exchanged(send, hub_orders, 0)
+    parts = chunk_columns(
+        functools.partial(hub_chunks_kernel, orders, spans, hub_lanes),
+        [(chunks // 2, high - low, width) for low, high in spans] * 2, chip, (ids, far_ids),
+        grads(keeps, hub_keep, hub_lanes) + grads(fars, hub_far, hub_lanes),
+    )
+    send, own = parts[:streams], parts[streams:]
+    got = exchanged(send, 0)
     left, right, rel_keep, rel_send = tables_step(
         last, hubs, core, heads, tails, negatives, query_grad, left, left_sums, right, rel_rows[last]
     )
@@ -685,80 +706,60 @@
 
     rel_keep, got = in_turn(rel_keep, got)
     send, own = halves(own, got)
-    got = exchanged(send, hub_orders, 1)
+    got = exchanged(send, 1)
     own, rel_far = in_turn(own, rel_far)
-    rel_out, rel_own = chunk_columns(
-        functools.partial(rel_chunks_kernel, rel_orders, rel_pieces, rel_count, rel_lanes),
-        rel_heights, width, chip, (ids, far_ids),
-        grads(keeps, rel_keep, rel_lanes) + grads(fars, rel_far, rel_lanes), chunks,
-    )
-    rel_got = exchanged(rel_out, rel_orders, 0)
+    rel_own, *rel_out = chunk_columns(
+        functools.partial(rel_chunks_kernel, rel_pieces, rel_count, rel_lanes),
+        [(depth, rel_height, width)] * planes, chip, (ids, far_ids),
+        grads(keeps, rel_keep, rel_lanes) + grads(fars, rel_far, rel_lanes),
+    )
+    rel_got = [flipped_by(x, "blk", 2 * (p + 1)) for p, x in enumerate(rel_out)]
     for step in range(2, stages):
         rel_own, got = in_turn(rel_own, got)
         send, own = halves(own, got)
-        got = exchanged(send, hub_orders, step)
-        own, rel_got = in_turn(own, rel_got)
-        rel_out, rel_own = halves(rel_own, rel_got)
-        rel_got = exchanged(rel_out, rel_orders, step - 1)
-
-    late, rel_own, got = lax.optimization_barrier((jnp.stack([core_id, chip_id]), rel_own, got))
+        got = exchanged(send, step)
+        if step == 2:
+            late, own, rel_got = lax.optimization_barrier((jnp.stack([core_id, chip_id]), own, rel_got))
+            rel_own, *rel_out = call(plane_sums_kernel, [rel_own, *rel_got], [(1, rel_height, width)] * depth)
+            rel_got = [flipped_by(x, "sub", q + 1) for q, x in enumerate(rel_out)]
+
     cut = lambda x, span: lax.dynamic_slice(x, (late[0], 0, late[1] * span), (1, half_width, span))[0]
     cut_sums = lambda x, span: lax.dynamic_slice(x[None], (0, late[1] * span), (1, span))
-    totals, squares = squares_of(own, got)
-    far_squares = other_core(squares)
-    totals, rel_got = in_turn(totals, rel_got)
-    rel_out, rel_own = halves(rel_own, rel_got)
-    rel_got = exchanged(rel_out, rel_orders, stages - 1)
-    rel_own, far_squares = in_turn(rel_own, far_squares)
+    *totals, rel_total, squares = call(
+        functools.partial(squares_kernel, streams), [*own, *got, rel_own, *rel_got],
+        [x.shape for x in own] + [rel_own.shape, (2, width)],
+    )
     have = call(
-        functools.partial(hub_update_kernel, spans, features),
-        [*totals, squares, far_squares, cut(hub_emb, width), cut_sums(hub_state, width)],
-        [x.shape for x in totals],
-    )
-    got = exchanged(have, hub_orders, stages - 1)
-    have, rel_got = in_turn(have, rel_got)
-    rel_totals, rel_squares = squares_of(rel_own, rel_got)
-    rel_far_squares = other_core(rel_squares)
-    rel_totals, got = in_turn(rel_totals, got)
-    have = join(have, got)
-    got = exchanged(have, hub_orders, stages - 2)
-    have, rel_far_squares = in_turn(have, rel_far_squares)
-    rel_have = call(
-        functools.partial(rel_update_kernel, len(rel_orders), rel_pieces, features),
-        [*rel_totals, rel_squares, rel_far_squares, cut(relation_emb, rel_width), cut_sums(relation_state, rel_width)],
-        [x.shape for x in rel_totals],
-    )
-    rel_got = exchanged(rel_have, rel_orders, stages - 1)
-    rel_step, step = stages - 2, stages - 3
-    turns = ["rel", "hub"] * (stages - 3) + ["rel"] * 2 + ["hub"]
-    for turn in turns:
-        if turn == "rel":
-            have, rel_got = in_turn(have, rel_got)
-            rel_have = join(rel_have, rel_got)
-            rel_got = exchanged(rel_have, rel_orders, rel_step)
-            rel_step -= 1
-        else:
-            rel_have, got = in_turn(rel_have, got)
-            near = combine(spans, have, got)
-            have = join(have, got)
-            got = exchanged(have, hub_orders, step)
-            step -= 1
+        functools.partial(update_kernel, spans, rel_spans, joint_pieces, features),
+        [
+            *totals, rel_total, squares, other_core(squares), cut(hub_emb, width), cut_sums(hub_state, width),
+            cut(relation_emb, rel_width), cut_sums(relation_state, rel_width),
+        ],
+        [(1, high - low + end - first, width) for (low, high), (first, end) in zip(spans, rel_spans)],
+    )
+    for step in range(stages - 1, 1, -1):
+        have = join(have, exchanged(have, step))
+    have, near, bases = join_all(have, exchanged(have, 1))
+    got = exchanged(have, 0)
+    far_near = other_core(near)
 
     mine, others = jnp.concatenate([chip, core]), jnp.concatenate([chip, 1 - core])
-    shape = hub_emb.shape
-    if width % 128 == 0:
-        hub_new = copy_chunks(mine, [near], 0, hub_orders, spans, shape, ())
-        hub_new = copy_chunks(others, [other_core(near)], 0, hub_orders, spans, shape, (hub_new,))
-        hub_new = copy_chunks(mine, got, 1, hub_orders, spans, shape, (hub_new,))
-        hub_new = copy_chunks(others, other_core(got), 1, hub_orders, spans, shape, (hub_new,))
-    else:
-        whole = combine(spans, have, got)
-        hub_new = place_chunks(mine, whole, hub_orders, hub_pieces, shape, ())
-        hub_new = place_chunks(others, other_core(whole), hub_orders, hub_pieces, shape, (hub_new,))
-    shape = relation_emb.shape
-    rel_whole = combine(rel_spans, rel_have, rel_got)
-    rel_new = place_chunks(mine, rel_whole, rel_orders, rel_pieces, shape, ())
-    rel_new = place_chunks(others, other_core(rel_whole), rel_orders, rel_pieces, shape, (rel_new,))
+    shapes = [hub_emb.shape, relation_emb.shape]
+    by_copy = width % 128 == 0
+    hub_new = []
+    if by_copy:
+        near_step = functools.partial(near_kernel, orders, spans, bases)
+        hub_new = placed(near_step, [], mine, near, [], shapes[:1], [])
+        hub_new = placed(near_step, [], others, far_near, [], shapes[:1], hub_new)
+        got, hub_new = in_turn(got, hub_new)
+    far_step = functools.partial(far_kernel, orders, spans, bases, joint_pieces, by_copy)
+    scratch = [
+        pltpu.VMEM((8, 128) if by_copy else (half_width, hub_count), F32),
+        pltpu.VMEM((half_width, rel_count), F32),
+    ]
+    far_got = other_core(got)
+    hub_new, rel_new = placed(far_step, scratch, mine, near, got, shapes, hub_new)
+    hub_new, rel_new = placed(far_step, scratch, others, far_near, far_got, shapes, [hub_new, rel_new])
     return (
         left.reshape(components, half_width, row_count),
         right.reshape(components, half_width, row_count),

time: 170 us -> 161 us (0.947)
  waiting for transfers between devices: 50.1 us -> 62.8 us
  starting transfers between devices: 54.6 us -> 42.2 us
  Pallas kernels: 49.8 us -> 39.6 us
    ppermute x51 -> x33, starting transfers between devices: 54.5 us -> 34 us  [flipped(): lax.ppermute(x, axis, [(i, i ^ 1 << bit) for i in range(lax.axis_size(axi...]
    ppermute x51 -> x33, waiting for transfers between devices: 50.1 us -> 62.8 us  [flipped(): lax.ppermute(x, axis, [(i, i ^ 1 << bit) for i in range(lax.axis_size(axi...]
    ppermute x0 -> x6, starting transfers between devices: none -> 8.07 us  [flipped_by(): lax.ppermute(x, axis, [(i, i ^ offset) for i in range(lax.axis_size(axis))])]
    pallas_call x1, Pallas kernels: 9.06 us -> 5.82 us  [bucket_step(): pl.pallas_call(functools.partial(bucket_kernel, bucket), in_specs=[SMEM]...]
    pallas_call x1, Pallas kernels: 9.26 us -> 6.15 us  [tables_step(): pl.pallas_call(functools.partial(tables_kernel, bucket, hubs), in_specs=[...]
    pallas_call x6 -> x4, Pallas kernels: 11.7 us -> 9.35 us  [placed(): pl.pallas_call(kernel, in_specs=[SMEM] + [VMEM] * (1 + len(fars)) + [HBM]...]
  transfers between devices with their start and end apart: 52 -> 40, of which waited for: 17 -> 18; matrix products, arithmetic and copies ran while one was open for 2% -> 2% of each run, Pallas kernels for 18% -> 14%
where the time goes in v5:
time: 161 us; the launch traced here: 160 us
  waiting for transfers between devices  62.8 us (39%)
  starting transfers between devices  42.2 us (26%)
  Pallas kernels  39.6 us (25%)
  local copies, waits for them, and re-layouts  11.3 us (7%)
  between operations  4.33 us (3%)
    ppermute x33, waiting for transfers between devices, flipped(): lax.ppermute(x, axis, [(i, i ^ 1 << bit) for i in range(lax.axis_size(axi...  62.8 us
    ppermute x33, starting transfers between devices, flipped(): lax.ppermute(x, axis, [(i, i ^ 1 << bit) for i in range(lax.axis_size(axi...  34 us
    pallas_call x4, Pallas kernels, placed(): pl.pallas_call(kernel, in_specs=[SMEM] + [VMEM] * (1 + len(fars)) + [HBM]...  9.35 us
    pallas_call x1, Pallas kernels, gather_rows(): pl.pallas_call(functools.partial(gather_kernel, hub_steps, rel_steps), in...  8.16 us
    ppermute x6, starting transfers between devices, flipped_by(): lax.ppermute(x, axis, [(i, i ^ offset) for i in range(lax.axis_size(axis))])  8.07 us
    unnamed x28, local copies, waits for them, and re-layouts  7.88 us
    pallas_call x2, Pallas kernels, chunk_columns(): pl.pallas_call(functools.partial(kernel, grad_lanes), in_specs=[SMEM] + [...  6.81 us
    pallas_call x1, Pallas kernels, tables_step(): pl.pallas_call(functools.partial(tables_kernel, bucket, hubs), in_specs=[...  6.15 us
  transfers between devices with their start and end apart: 40, of which 18 were waited for; matrix products, arithmetic and copies ran while one was open for 2% of the time, Pallas kernels for 14%

profile of v5, /device:TPU:0, one launch (start us, length us, event | category | flops | bytes accessed | tf_op | source)
XLA Modules:
  0.0 160.5 jit_solution(2595064722931928488)
XLA Ops:
  0.7 2.9 %copy-done.1 = f32[2,200,4096]{2,1,0:T(8,128)S(1)} copy-done((f32[2,200,4096]{2,1,0:T(8,128)S(1)}, f32[2,200,4096]{2,1,0:T(8,128)}, u32[]{:S(2)}) %copy-start.1) | copy-done | bytes 6553624
  6.5 8.2 %shard_map.156 = (s32[2,768]{1,0:T(2,128)S(1)}, f32[400,256]{1,0:T(8,128)S(1)}, f32[400,256]{1,0:T(8,128)S(1)}, f32[400,512]{1,0:T(8,128)S(1)}, f32[400,512]{1,0:T(8,128)S(1)}) custom-call(s32[2,256]{1,0:T(2,128)S(1)} %copy-done.11, s32[2,512]{1,0:T(2,128)S(1)} %copy-done.10, f32[400,4096]{1,0:T(8,128)S(1)} %bitcast.20, f32[400,1280]{1,0:T(8,128)S(1)} %bitcast.21), custom_call_target="tpu_custom_call" | custom-call | flops 10000 | bytes 10000 | tf_op jit(solution)/shard_map/pallas_call | solution.py:107
  14.8 5.8 %shard_map.157 = (f32[400,512]{1,0:T(8,128)S(1)}, f32[1,512]{1,0:T(1,128)S(1)}, f32[408,512]{1,0:T(8,128)}, f32[200,768]{1,0:T(8,128)S(1)}, f32[200,768]{1,0:T(8,128)}) custom-call(s32[1]{0:T(128)} %bitcast.core_ref, s32[2,512]{1,0:T(2,128)S(1)} %copy-done.7, s32[2,512]{1,0:T(2,128)S(1)} %copy-done.9, s32[2,1024]{1,0:T(2,128)S(1)} %copy-done.8, ...), custom_call_target="tpu_custom_call" | custom-call | flops 10000 | bytes 10000 | tf_op jit(solution)/shard_map/pallas_call | solution.py:488
  21.1 2.5 %collective-permute-start = (s32[2,768]{1,0:T(2,128)S(1)}, s32[2,768]{1,0:T(2,128)S(1)}, u32[]{:S(2)}, u32[]{:S(2)}) collective-permute-start(s32[2,768]{1,0:T(2,128)S(1)} %get-tuple-element.104.refs_0_), channel_id=1, source_target_pairs={{0,4},{4,0},{8,12},{12,8},{16,20},{20,16},{24,28},{28,24},{1,5},{5... | collective-permute-start | bytes 18440 | tf_op jit(solution)/shard_map/ppermute | solution.py:609
  24.5 2.2 %shard_map.158 = (f32[400,512]{1,0:T(8,128)S(1)}, f32[200,256]{1,0:T(8,128)S(1)}, f32[200,256]{1,0:T(8,128)S(1)}) custom-call(s32[1]{0:T(128)} %bitcast.core_ref, s32[2,512]{1,0:T(2,128)S(1)} %copy-done.7, f32[400,512]{1,0:T(8,128)S(1)} %get-tuple-element.108.left_ref, f32[400,512]{1,0:T(8,128)S(1)} %get-tuple-element.109.rel_ref, ...), custom_call_target="tpu_custom_call" | custom-call | flops 10000 | bytes 10000 | tf_op jit(solution)/shard_map/pallas_call | solution.py:535
  29.0 3.8 %shard_map.160 = (f32[8,72,256]{2,1,0:T(8,128)S(1)}, f32[8,64,256]{2,1,0:T(8,128)S(1)}, f32[8,64,256]{2,1,0:T(8,128)S(1)}, f32[8,72,256]{2,1,0:T(8,128)S(1)}, f3...) custom-call(s32[1]{0:T(128)} %bitcast.9.chip_ref, s32[2,768]{1,0:T(2,128)S(1)} %get-tuple-element.104.refs_0_, ...), custom_call_target="tpu_custom_call" | custom-call | flops 10000 | bytes 10000 | tf_op jit(solution)/shard_map/pallas_call | solution.py:219
  32.8 2.0 %collective-permute-start.4 = (f32[8,72,256]{2,1,0:T(8,128)S(1)}, f32[8,72,256]{2,1,0:T(8,128)S(1)}, u32[]{:S(2)}, u32[]{:S(2)}) collective-permute-start(f32[8,72,256]{2,1,0:T(8,128)S(1)} %get-tuple-element.125), channel_id=1, source_target_pairs={{0,8},{4,12},{8,0},{12,4},{16,24},{20,28},{24,16},{28,20},{1,9},{5... | collective-permute-start | bytes 1769480 | tf_op jit(solution)/shard_map/ppermute | solution.py:609
  35.5 1.6 collective-permute-start.6
  38.2 6.2 %shard_map.159 = (f32[400,512]{1,0:T(8,128)}, f32[400,512]{1,0:T(8,128)}, f32[200,512]{1,0:T(8,128)S(1)}, f32[200,512]{1,0:T(8,128)S(1)}) custom-call(s32[1]{0:T(128)} %bitcast.core_ref, s32[2,512]{1,0:T(2,128)S(1)} %copy-done.7, s32[2,512]{1,0:T(2,128)S(1)} %copy-done.9, s32[2,1024]{1,0:T(2,128)S(1)} %copy-done.8, f32[400,512]{1,0:T(8,128)S(1)} %copy-done.6, ...), custom_call_target="tpu_custom_call" | custom-call | flops 10000 | bytes 10000 | tf_op jit(solution)/shard_map/pallas_call | solution.py:591
  44.4 4.3 %collective-permute-done.5.refs_4_ = f32[8,64,256]{2,1,0:T(8,128)S(1)} collective-permute-done((f32[8,64,256]{2,1,0:T(8,128)S(1)}, f32[8,64,256]{2,1,0:T(8,128)S(1)}, u32[]{:S(2)}, u32[]{:S(2)}) %collective-permute-start.5) | collective-permute-done | bytes 524320 | tf_op jit(solution)/shard_map/ppermute | solution.py:609
  49.1 1.7 %collective-permute-start.9 = (f32[4,64,256]{2,1,0:T(8,128)S(1)}, f32[4,64,256]{2,1,0:T(8,128)S(1)}, u32[]{:S(2)}, u32[]{:S(2)}) collective-permute-start(f32[4,64,256]{2,1,0:T(8,128)S(1)} %get-tuple-element.142), channel_id=1, source_target_pairs={{0,1},{1,0},{2,3},{3,2},{4,5},{5,4},{6,7},{7,6},{8,9},{9,8},{10,11... | collective-permute-start | bytes 786440 | tf_op jit(solution)/shard_map/ppermute | solution.py:609
  52.3 3.0 %shard_map.162 = (f32[4,72,256]{2,1,0:T(8,128)S(1)}, f32[4,72,256]{2,1,0:T(8,128)S(1)}, f32[4,72,256]{2,1,0:T(8,128)S(1)}, f32[4,72,256]{2,1,0:T(8,128)S(1)}) custom-call(s32[1]{0:T(128)} %bitcast.9.chip_ref, s32[2,768]{1,0:T(2,128)S(1)} %get-tuple-element.104.refs_0_, s32[2,768]{1,0:T(2,128)S(1)} %collective-permute-done.refs_1_, ...), custom_call_target="tpu_custom_call" | custom-call | flops 10000 | bytes 10000 | tf_op jit(solution)/shard_map/pallas_call | solution.py:219
  59.5 15.8 %collective-permute-done.10.refs_5_ = f32[4,64,256]{2,1,0:T(8,128)S(1)} collective-permute-done((f32[4,64,256]{2,1,0:T(8,128)S(1)}, f32[4,64,256]{2,1,0:T(8,128)S(1)}, u32[]{:S(2)}, u32[]{:S(2)}) %collective-permute-start.10) | collective-permute-done | bytes 262176 | tf_op jit(solution)/shard_map/ppermute | solution.py:609
  75.7 2.6 %collective-permute-start.16 = (f32[2,64,256]{2,1,0:T(8,128)S(1)}, f32[2,64,256]{2,1,0:T(8,128)S(1)}, u32[]{:S(2)}, u32[]{:S(2)}) collective-permute-start(f32[2,64,256]{2,1,0:T(8,128)S(1)} %get-tuple-element.163), channel_id=1, source_target_pairs={{0,2},{1,3},{2,0},{3,1},{4,6},{5,7},{6,4},{7,5},{8,10},{9,11},{10,... | collective-permute-start | bytes 393224 | tf_op jit(solution)/shard_map/ppermute | solution.py:609
  82.0 1.6 %collective-permute-start.20 = (f32[1,72,256]{2,1,0:T(8,128)S(1)}, f32[1,72,256]{2,1,0:T(8,128)S(1)}, u32[]{:S(2)}, u32[]{:S(2)}) collective-permute-start(f32[1,72,256]{2,1,0:T(8,128)S(1)} %get-tuple-element.174), channel_id=1, source_target_pairs={{0,1},{1,0},{2,3},{3,2},{4,5},{5,4},{6,7},{7,6},{8,9},{9,8},{10,11... | collective-permute-start | bytes 221192 | tf_op jit(solution)/shard_map/ppermute | solution.py:613
  85.6 2.5 %collective-permute-start.22 = (f32[1,72,256]{2,1,0:T(8,128)S(1)}, f32[1,72,256]{2,1,0:T(8,128)S(1)}, u32[]{:S(2)}, u32[]{:S(2)}) collective-permute-start(f32[1,72,256]{2,1,0:T(8,128)S(1)} %get-tuple-element.176), channel_id=1, source_target_pairs={{0,3},{1,2},{2,1},{3,0},{4,7},{5,6},{6,5},{7,4},{8,11},{9,10},{10,... | collective-permute-start | bytes 221192 | tf_op jit(solution)/shard_map/ppermute | solution.py:613
  88.3 1.7 %collective-permute-start.19 = (f32[1,64,256]{2,1,0:T(8,128)S(1)}, f32[1,64,256]{2,1,0:T(8,128)S(1)}, u32[]{:S(2)}, u32[]{:S(2)}) collective-permute-start(f32[1,64,256]{2,1,0:T(8,128)S(1)} %get-tuple-element.172), channel_id=1, source_target_pairs={{0,16},{4,20},{8,24},{12,28},{16,0},{20,4},{24,8},{28,12},{1,17},{... | collective-permute-start | bytes 196616 | tf_op jit(solution)/shard_map/ppermute | solution.py:609
  90.1 2.8 %collective-permute-start.17 = (f32[1,72,256]{2,1,0:T(8,128)S(1)}, f32[1,72,256]{2,1,0:T(8,128)S(1)}, u32[]{:S(2)}, u32[]{:S(2)}) collective-permute-start(f32[1,72,256]{2,1,0:T(8,128)S(1)} %get-tuple-element.170), channel_id=1, source_target_pairs={{0,2},{1,3},{2,0},{3,1},{4,6},{5,7},{6,4},{7,5},{8,10},{9,11},{10,... | collective-permute-start | bytes 221192 | tf_op jit(solution)/shard_map/ppermute | solution.py:609
  93.9 1.6 collective-permute-done.18.refs_4_
  95.5 1.6 collective-permute-done.17.refs_3_
  99.8 1.9 %collective-permute-start.25 = (f32[1,88,256]{2,1,0:T(8,128)S(1)}, f32[1,88,256]{2,1,0:T(8,128)S(1)}, u32[]{:S(2)}, u32[]{:S(2)}) collective-permute-start(f32[1,88,256]{2,1,0:T(8,128)S(1)} %get-tuple-element.184.refs_1_), channel_id=1, source_target_pairs={{0,2},{1,3},{2,0},{3,1},{4,6},{5,7},{6,4},{7,5},{8,10},{9,11},{10,... | collective-permute-start | bytes 270344 | tf_op jit(solution)/shard_map/ppermute | solution.py:609
  101.7 1.7 %collective-permute-start.26 = (f32[1,88,256]{2,1,0:T(8,128)S(1)}, f32[1,88,256]{2,1,0:T(8,128)S(1)}, u32[]{:S(2)}, u32[]{:S(2)}) collective-permute-start(f32[1,88,256]{2,1,0:T(8,128)S(1)} %get-tuple-element.185.refs_2_), channel_id=1, source_target_pairs={{0,16},{4,20},{8,24},{12,28},{16,0},{20,4},{24,8},{28,12},{1,17},{... | collective-permute-start | bytes 270344 | tf_op jit(solution)/shard_map/ppermute | solution.py:609
  103.4 6.6 %collective-permute-done.25.refs_4_ = f32[1,88,256]{2,1,0:T(8,128)S(1)} collective-permute-done((f32[1,88,256]{2,1,0:T(8,128)S(1)}, f32[1,88,256]{2,1,0:T(8,128)S(1)}, u32[]{:S(2)}, u32[]{:S(2)}) %collective-permute-start.25) | collective-permute-done | bytes 90144 | tf_op jit(solution)/shard_map/ppermute | solution.py:609
  111.7 2.4 %collective-permute-start.29 = (f32[2,88,256]{2,1,0:T(8,128)S(1)}, f32[2,88,256]{2,1,0:T(8,128)S(1)}, u32[]{:S(2)}, u32[]{:S(2)}) collective-permute-start(f32[2,88,256]{2,1,0:T(8,128)S(1)} %get-tuple-element.188.refs_2_), channel_id=1, source_target_pairs={{0,2},{1,3},{2,0},{3,1},{4,6},{5,7},{6,4},{7,5},{8,10},{9,11},{10,... | collective-permute-start | bytes 540680 | tf_op jit(solution)/shard_map/ppermute | solution.py:609
  114.1 2.6 %collective-permute-done.28.refs_4_ = f32[2,88,256]{2,1,0:T(8,128)S(1)} collective-permute-done((f32[2,88,256]{2,1,0:T(8,128)S(1)}, f32[2,88,256]{2,1,0:T(8,128)S(1)}, u32[]{:S(2)}, u32[]{:S(2)}) %collective-permute-start.28) | collective-permute-done | bytes 180256 | tf_op jit(solution)/shard_map/ppermute | solution.py:609
  116.7 6.0 %collective-permute-done.29.refs_5_ = f32[2,88,256]{2,1,0:T(8,128)S(1)} collective-permute-done((f32[2,88,256]{2,1,0:T(8,128)S(1)}, f32[2,88,256]{2,1,0:T(8,128)S(1)}, u32[]{:S(2)}, u32[]{:S(2)}) %collective-permute-start.29) | collective-permute-done | bytes 180256 | tf_op jit(solution)/shard_map/ppermute | solution.py:609
  124.9 7.4 %collective-permute-done.31.refs_4_ = f32[4,88,256]{2,1,0:T(8,128)S(1)} collective-permute-done((f32[4,88,256]{2,1,0:T(8,128)S(1)}, f32[4,88,256]{2,1,0:T(8,128)S(1)}, u32[]{:S(2)}, u32[]{:S(2)}) %collective-permute-start.31) | collective-permute-done | bytes 360480 | tf_op jit(solution)/shard_map/ppermute | solution.py:609
  136.5 1.9 %shard_map.171.refs_0_ = f32[2,200,4096]{2,1,0:T(8,128)} custom-call(s32[2]{0:T(128)S(1)} %pad_add_fusion.2.spot_ref, f32[8,272,256]{2,1,0:T(8,128)S(1)} %get-tuple-element.192.near_ref), custom_call_target="tpu_custom_call" | custom-call | bytes 3276800 | tf_op jit(solution)/shard_map/pallas_call | solution.py:389
  138.5 1.9 %shard_map.172.refs_3_ = f32[2,200,4096]{2,1,0:T(8,128)} custom-call(s32[2]{0:T(128)S(1)} %pad_add_fusion.spot_ref, f32[8,272,256]{2,1,0:T(8,128)S(1)} %collective-permute-done.33.near_ref, f32[2,200,4096]{2,1,0:T(8,128)} %shard_map.171.refs_0_), custom_call_target="tpu_custom_call", output_to_operand_aliasing={{}: (2, {})} | custom-call | bytes 3276800 | tf_op jit(solution)/shard_map/pallas_call | solution.py:389
  140.4 12.0 %collective-permute-done.35.refs_1_ = f32[8,88,256]{2,1,0:T(8,128)S(1)} collective-permute-done((f32[8,88,256]{2,1,0:T(8,128)S(1)}, f32[8,88,256]{2,1,0:T(8,128)S(1)}, u32[]{:S(2)}, u32[]{:S(2)}) %collective-permute-start.35) | collective-permute-done | bytes 720928 | tf_op jit(solution)/shard_map/ppermute | solution.py:609
  153.7 2.8 %shard_map.173 = (f32[2,200,4096]{2,1,0:T(8,128)}, f32[2,200,1280]{2,1,0:T(8,128)}) custom-call(s32[2]{0:T(128)S(1)} %pad_add_fusion.2.spot_ref, f32[8,272,256]{2,1,0:T(8,128)S(1)} %get-tuple-element.192.near_ref, f32[8,96,256]{2,1,0:T(8,128)S(1)} %collective-permute-done.34.refs_0_, ...), custom_call_target="tpu_custom_call", output_to_operand_aliasing={{0}: (5, {})} | custom-call | bytes 3276800 | tf_op jit(solution)/shard_map/pallas_call | solution.py:389
  157.5 2.8 %shard_map.174 = (f32[2,200,4096]{2,1,0:T(8,128)}, f32[2,200,1280]{2,1,0:T(8,128)}) custom-call(s32[2]{0:T(128)S(1)} %pad_add_fusion.spot_ref, f32[8,272,256]{2,1,0:T(8,128)S(1)} %collective-permute-done.33.near_ref, f32[8,96,256]{2,1,0:T(8,128)S(1)} %collective-permute-done.37.refs_0_, ...), custom_call_target="tpu_custom_call", output_to_operand_aliasing={{0}: (5, {}), {1}: (6, {})} | custom-call | bytes 3276800 | tf_op jit(solution)/shard_map/pallas_call | solution.py:389
  (103 shorter events, 31.9 us)
Async XLA Ops:
  20.6 8.4 %collective-permute-start.2 = (f32[200,768]{1,0:T(8,128)}, f32[200,768]{1,0:T(8,128)S(1)}, u32[]{:S(2)}, u32[]{:S(2)}) collective-permute-start(f32[200,768]{1,0:T(8,128)} %get-tuple-element.119), channel_id=1, source_target_pairs={{0,4},{4,0},{8,12},{12,8},{16,20},{20,16},{24,28},{28,24},{1,5},{5... | collective-permute-start | bytes 1843208 | tf_op jit(solution)/shard_map/ppermute | solution.py:609
  21.1 16.0 %collective-permute-start.1 = (f32[408,512]{1,0:T(8,128)}, f32[408,512]{1,0:T(8,128)}, u32[]{:S(2)}, u32[]{:S(2)}) collective-permute-start(f32[408,512]{1,0:T(8,128)} %get-tuple-element.113), channel_id=1, source_target_pairs={{0,4},{4,8},{8,12},{12,16},{16,20},{20,24},{24,28},{28,0},{1,5},{5... | collective-permute-start | bytes 2506760 | tf_op jit(solution)/shard_map/ppermute | solution.py:605
  32.8 16.1 %collective-permute-start.4 = (f32[8,72,256]{2,1,0:T(8,128)S(1)}, f32[8,72,256]{2,1,0:T(8,128)S(1)}, u32[]{:S(2)}, u32[]{:S(2)}) collective-permute-start(f32[8,72,256]{2,1,0:T(8,128)S(1)} %get-tuple-element.125), channel_id=1, source_target_pairs={{0,8},{4,12},{8,0},{12,4},{16,24},{20,28},{24,16},{28,20},{1,9},{5... | collective-permute-start | bytes 1769480 | tf_op jit(solution)/shard_map/ppermute | solution.py:609
  34.8 13.9 %collective-permute-start.5 = (f32[8,64,256]{2,1,0:T(8,128)S(1)}, f32[8,64,256]{2,1,0:T(8,128)S(1)}, u32[]{:S(2)}, u32[]{:S(2)}) collective-permute-start(f32[8,64,256]{2,1,0:T(8,128)S(1)} %get-tuple-element.126), channel_id=1, source_target_pairs={{0,16},{4,20},{8,24},{12,28},{16,0},{20,4},{24,8},{28,12},{1,17},{... | collective-permute-start | bytes 1572872 | tf_op jit(solution)/shard_map/ppermute | solution.py:609
  35.5 13.4 %collective-permute-start.6 = (f32[8,64,256]{2,1,0:T(8,128)S(1)}, f32[8,64,256]{2,1,0:T(8,128)S(1)}, u32[]{:S(2)}, u32[]{:S(2)}) collective-permute-start(f32[8,64,256]{2,1,0:T(8,128)S(1)} %get-tuple-element.127), channel_id=1, source_target_pairs={{0,1},{1,0},{2,3},{3,2},{4,5},{5,4},{6,7},{7,6},{8,9},{9,8},{10,11... | collective-permute-start | bytes 1572872 | tf_op jit(solution)/shard_map/ppermute | solution.py:609
  44.4 7.9 %collective-permute-start.7 = (f32[200,512]{1,0:T(8,128)S(1)}, f32[200,512]{1,0:T(8,128)S(1)}, u32[]{:S(2)}, u32[]{:S(2)}) collective-permute-start(f32[200,512]{1,0:T(8,128)S(1)} %get-tuple-element.134), channel_id=1, source_target_pairs={{0,4},{4,0},{8,12},{12,8},{16,20},{20,16},{24,28},{28,24},{1,5},{5... | collective-permute-start | bytes 1228808 | tf_op jit(solution)/shard_map/ppermute | solution.py:609
  49.1 9.8 %collective-permute-start.9 = (f32[4,64,256]{2,1,0:T(8,128)S(1)}, f32[4,64,256]{2,1,0:T(8,128)S(1)}, u32[]{:S(2)}, u32[]{:S(2)}) collective-permute-start(f32[4,64,256]{2,1,0:T(8,128)S(1)} %get-tuple-element.142), channel_id=1, source_target_pairs={{0,1},{1,0},{2,3},{3,2},{4,5},{5,4},{6,7},{7,6},{8,9},{9,8},{10,11... | collective-permute-start | bytes 786440 | tf_op jit(solution)/shard_map/ppermute | solution.py:609
  50.7 24.5 %collective-permute-start.8 = (f32[4,72,256]{2,1,0:T(8,128)S(1)}, f32[4,72,256]{2,1,0:T(8,128)S(1)}, u32[]{:S(2)}, u32[]{:S(2)}) collective-permute-start(f32[4,72,256]{2,1,0:T(8,128)S(1)} %get-tuple-element.141), channel_id=1, source_target_pairs={{0,16},{4,20},{8,24},{12,28},{16,0},{20,4},{24,8},{28,12},{1,17},{... | collective-permute-start | bytes 884744 | tf_op jit(solution)/shard_map/ppermute | solution.py:609
  55.3 23.0 %collective-permute-start.11 = (f32[4,72,256]{2,1,0:T(8,128)S(1)}, f32[4,72,256]{2,1,0:T(8,128)S(1)}, u32[]{:S(2)}, u32[]{:S(2)}) collective-permute-start(f32[4,72,256]{2,1,0:T(8,128)S(1)} %get-tuple-element.150), channel_id=1, source_target_pairs={{0,8},{4,12},{8,0},{12,4},{16,24},{20,28},{24,16},{28,20},{1,9},{5... | collective-permute-start | bytes 884744 | tf_op jit(solution)/shard_map/ppermute | solution.py:613
  55.9 22.8 %collective-permute-start.12 = (f32[4,72,256]{2,1,0:T(8,128)S(1)}, f32[4,72,256]{2,1,0:T(8,128)S(1)}, u32[]{:S(2)}, u32[]{:S(2)}) collective-permute-start(f32[4,72,256]{2,1,0:T(8,128)S(1)} %get-tuple-element.151), channel_id=1, source_target_pairs={{0,16},{4,20},{8,24},{12,28},{16,0},{20,4},{24,8},{28,12},{1,17},{... | collective-permute-start | bytes 884744 | tf_op jit(solution)/shard_map/ppermute | solution.py:613
  57.5 21.3 %collective-permute-start.13 = (f32[4,72,256]{2,1,0:T(8,128)S(1)}, f32[4,72,256]{2,1,0:T(8,128)S(1)}, u32[]{:S(2)}, u32[]{:S(2)}) collective-permute-start(f32[4,72,256]{2,1,0:T(8,128)S(1)} %get-tuple-element.152), channel_id=1, source_target_pairs={{0,24},{4,28},{8,16},{12,20},{16,8},{20,12},{24,0},{28,4},{1,25},{... | collective-permute-start | bytes 884744 | tf_op jit(solution)/shard_map/ppermute | solution.py:613
  58.9 16.4 %collective-permute-start.10 = (f32[4,64,256]{2,1,0:T(8,128)S(1)}, f32[4,64,256]{2,1,0:T(8,128)S(1)}, u32[]{:S(2)}, u32[]{:S(2)}) collective-permute-start(f32[4,64,256]{2,1,0:T(8,128)S(1)} %get-tuple-element.143), channel_id=1, source_target_pairs={{0,8},{4,12},{8,0},{12,4},{16,24},{20,28},{24,16},{28,20},{1,9},{5... | collective-permute-start | bytes 786440 | tf_op jit(solution)/shard_map/ppermute | solution.py:609
  75.4 10.2 %collective-permute-start.15 = (f32[2,64,256]{2,1,0:T(8,128)S(1)}, f32[2,64,256]{2,1,0:T(8,128)S(1)}, u32[]{:S(2)}, u32[]{:S(2)}) collective-permute-start(f32[2,64,256]{2,1,0:T(8,128)S(1)} %get-tuple-element.162), channel_id=1, source_target_pairs={{0,8},{4,12},{8,0},{12,4},{16,24},{20,28},{24,16},{28,20},{1,9},{5... | collective-permute-start | bytes 393224 | tf_op jit(solution)/shard_map/ppermute | solution.py:609
  75.7 12.4 %collective-permute-start.16 = (f32[2,64,256]{2,1,0:T(8,128)S(1)}, f32[2,64,256]{2,1,0:T(8,128)S(1)}, u32[]{:S(2)}, u32[]{:S(2)}) collective-permute-start(f32[2,64,256]{2,1,0:T(8,128)S(1)} %get-tuple-element.163), channel_id=1, source_target_pairs={{0,2},{1,3},{2,0},{3,1},{4,6},{5,7},{6,4},{7,5},{8,10},{9,11},{10,... | collective-permute-start | bytes 393224 | tf_op jit(solution)/shard_map/ppermute | solution.py:609
  78.3 9.8 %collective-permute-start.14 = (f32[2,72,256]{2,1,0:T(8,128)S(1)}, f32[2,72,256]{2,1,0:T(8,128)S(1)}, u32[]{:S(2)}, u32[]{:S(2)}) collective-permute-start(f32[2,72,256]{2,1,0:T(8,128)S(1)} %get-tuple-element.161), channel_id=1, source_target_pairs={{0,1},{1,0},{2,3},{3,2},{4,5},{5,4},{6,7},{7,6},{8,9},{9,8},{10,11... | collective-permute-start | bytes 442376 | tf_op jit(solution)/shard_map/ppermute | solution.py:609
  82.0 8.1 %collective-permute-start.20 = (f32[1,72,256]{2,1,0:T(8,128)S(1)}, f32[1,72,256]{2,1,0:T(8,128)S(1)}, u32[]{:S(2)}, u32[]{:S(2)}) collective-permute-start(f32[1,72,256]{2,1,0:T(8,128)S(1)} %get-tuple-element.174), channel_id=1, source_target_pairs={{0,1},{1,0},{2,3},{3,2},{4,5},{5,4},{6,7},{7,6},{8,9},{9,8},{10,11... | collective-permute-start | bytes 221192 | tf_op jit(solution)/shard_map/ppermute | solution.py:613
  83.6 10.3 %collective-permute-start.21 = (f32[1,72,256]{2,1,0:T(8,128)S(1)}, f32[1,72,256]{2,1,0:T(8,128)S(1)}, u32[]{:S(2)}, u32[]{:S(2)}) collective-permute-start(f32[1,72,256]{2,1,0:T(8,128)S(1)} %get-tuple-element.175), channel_id=1, source_target_pairs={{0,2},{1,3},{2,0},{3,1},{4,6},{5,7},{6,4},{7,5},{8,10},{9,11},{10,... | collective-permute-start | bytes 221192 | tf_op jit(solution)/shard_map/ppermute | solution.py:613
  85.6 8.3 %collective-permute-start.22 = (f32[1,72,256]{2,1,0:T(8,128)S(1)}, f32[1,72,256]{2,1,0:T(8,128)S(1)}, u32[]{:S(2)}, u32[]{:S(2)}) collective-permute-start(f32[1,72,256]{2,1,0:T(8,128)S(1)} %get-tuple-element.176), channel_id=1, source_target_pairs={{0,3},{1,2},{2,1},{3,0},{4,7},{5,6},{6,5},{7,4},{8,11},{9,10},{10,... | collective-permute-start | bytes 221192 | tf_op jit(solution)/shard_map/ppermute | solution.py:613
  88.1 7.4 %collective-permute-start.18 = (f32[1,64,256]{2,1,0:T(8,128)S(1)}, f32[1,64,256]{2,1,0:T(8,128)S(1)}, u32[]{:S(2)}, u32[]{:S(2)}) collective-permute-start(f32[1,64,256]{2,1,0:T(8,128)S(1)} %get-tuple-element.171), channel_id=1, source_target_pairs={{0,2},{1,3},{2,0},{3,1},{4,6},{5,7},{6,4},{7,5},{8,10},{9,11},{10,... | collective-permute-start | bytes 196616 | tf_op jit(solution)/shard_map/ppermute | solution.py:609
  88.3 7.2 %collective-permute-start.19 = (f32[1,64,256]{2,1,0:T(8,128)S(1)}, f32[1,64,256]{2,1,0:T(8,128)S(1)}, u32[]{:S(2)}, u32[]{:S(2)}) collective-permute-start(f32[1,64,256]{2,1,0:T(8,128)S(1)} %get-tuple-element.172), channel_id=1, source_target_pairs={{0,16},{4,20},{8,24},{12,28},{16,0},{20,4},{24,8},{28,12},{1,17},{... | collective-permute-start | bytes 196616 | tf_op jit(solution)/shard_map/ppermute | solution.py:609
  90.1 7.0 %collective-permute-start.17 = (f32[1,72,256]{2,1,0:T(8,128)S(1)}, f32[1,72,256]{2,1,0:T(8,128)S(1)}, u32[]{:S(2)}, u32[]{:S(2)}) collective-permute-start(f32[1,72,256]{2,1,0:T(8,128)S(1)} %get-tuple-element.170), channel_id=1, source_target_pairs={{0,2},{1,3},{2,0},{3,1},{4,6},{5,7},{6,4},{7,5},{8,10},{9,11},{10,... | collective-permute-start | bytes 221192 | tf_op jit(solution)/shard_map/ppermute | solution.py:609
  98.7 11.4 %collective-permute-start.24 = (f32[1,96,256]{2,1,0:T(8,128)S(1)}, f32[1,96,256]{2,1,0:T(8,128)S(1)}, u32[]{:S(2)}, u32[]{:S(2)}) collective-permute-start(f32[1,96,256]{2,1,0:T(8,128)S(1)} %get-tuple-element.183.refs_0_), channel_id=1, source_target_pairs={{0,2},{1,3},{2,0},{3,1},{4,6},{5,7},{6,4},{7,5},{8,10},{9,11},{10,... | collective-permute-start | bytes 294920 | tf_op jit(solution)/shard_map/ppermute | solution.py:609
  99.8 10.3 %collective-permute-start.25 = (f32[1,88,256]{2,1,0:T(8,128)S(1)}, f32[1,88,256]{2,1,0:T(8,128)S(1)}, u32[]{:S(2)}, u32[]{:S(2)}) collective-permute-start(f32[1,88,256]{2,1,0:T(8,128)S(1)} %get-tuple-element.184.refs_1_), channel_id=1, source_target_pairs={{0,2},{1,3},{2,0},{3,1},{4,6},{5,7},{6,4},{7,5},{8,10},{9,11},{10,... | collective-permute-start | bytes 270344 | tf_op jit(solution)/shard_map/ppermute | solution.py:609
  101.7 8.4 %collective-permute-start.26 = (f32[1,88,256]{2,1,0:T(8,128)S(1)}, f32[1,88,256]{2,1,0:T(8,128)S(1)}, u32[]{:S(2)}, u32[]{:S(2)}) collective-permute-start(f32[1,88,256]{2,1,0:T(8,128)S(1)} %get-tuple-element.185.refs_2_), channel_id=1, source_target_pairs={{0,16},{4,20},{8,24},{12,28},{16,0},{20,4},{24,8},{28,12},{1,17},{... | collective-permute-start | bytes 270344 | tf_op jit(solution)/shard_map/ppermute | solution.py:609
  110.1 12.7 %collective-permute-start.27 = (f32[2,96,256]{2,1,0:T(8,128)S(1)}, f32[2,96,256]{2,1,0:T(8,128)S(1)}, u32[]{:S(2)}, u32[]{:S(2)}) collective-permute-start(f32[2,96,256]{2,1,0:T(8,128)S(1)} %get-tuple-element.186.refs_0_), channel_id=1, source_target_pairs={{0,1},{1,0},{2,3},{3,2},{4,5},{5,4},{6,7},{7,6},{8,9},{9,8},{10,11... | collective-permute-start | bytes 589832 | tf_op jit(solution)/shard_map/ppermute | solution.py:609
  111.7 11.0 %collective-permute-start.29 = (f32[2,88,256]{2,1,0:T(8,128)S(1)}, f32[2,88,256]{2,1,0:T(8,128)S(1)}, u32[]{:S(2)}, u32[]{:S(2)}) collective-permute-start(f32[2,88,256]{2,1,0:T(8,128)S(1)} %get-tuple-element.188.refs_2_), channel_id=1, source_target_pairs={{0,2},{1,3},{2,0},{3,1},{4,6},{5,7},{6,4},{7,5},{8,10},{9,11},{10,... | collective-permute-start | bytes 540680 | tf_op jit(solution)/shard_map/ppermute | solution.py:609
  122.8 10.0 %collective-permute-start.30 = (f32[4,96,256]{2,1,0:T(8,128)S(1)}, f32[4,96,256]{2,1,0:T(8,128)S(1)}, u32[]{:S(2)}, u32[]{:S(2)}) collective-permute-start(f32[4,96,256]{2,1,0:T(8,128)S(1)} %get-tuple-element.189.refs_0_), channel_id=1, source_target_pairs={{0,16},{4,20},{8,24},{12,28},{16,0},{20,4},{24,8},{28,12},{1,17},{... | collective-permute-start | bytes 1179656 | tf_op jit(solution)/shard_map/ppermute | solution.py:609
  123.5 8.7 %collective-permute-start.31 = (f32[4,88,256]{2,1,0:T(8,128)S(1)}, f32[4,88,256]{2,1,0:T(8,128)S(1)}, u32[]{:S(2)}, u32[]{:S(2)}) collective-permute-start(f32[4,88,256]{2,1,0:T(8,128)S(1)} %get-tuple-element.190.refs_1_), channel_id=1, source_target_pairs={{0,1},{1,0},{2,3},{3,2},{4,5},{5,4},{6,7},{7,6},{8,9},{9,8},{10,11... | collective-permute-start | bytes 1081352 | tf_op jit(solution)/shard_map/ppermute | solution.py:609
  123.5 9.0 %collective-permute-start.32 = (f32[4,88,256]{2,1,0:T(8,128)S(1)}, f32[4,88,256]{2,1,0:T(8,128)S(1)}, u32[]{:S(2)}, u32[]{:S(2)}) collective-permute-start(f32[4,88,256]{2,1,0:T(8,128)S(1)} %get-tuple-element.191.refs_2_), channel_id=1, source_target_pairs={{0,8},{4,12},{8,0},{12,4},{16,24},{20,28},{24,16},{28,20},{1,9},{5... | collective-permute-start | bytes 1081352 | tf_op jit(solution)/shard_map/ppermute | solution.py:609
  133.2 20.0 %collective-permute-start.34 = (f32[8,96,256]{2,1,0:T(8,128)S(1)}, f32[8,96,256]{2,1,0:T(8,128)S(1)}, u32[]{:S(2)}, u32[]{:S(2)}) collective-permute-start(f32[8,96,256]{2,1,0:T(8,128)S(1)} %get-tuple-element.193), channel_id=1, source_target_pairs={{0,8},{4,12},{8,0},{12,4},{16,24},{20,28},{24,16},{28,20},{1,9},{5... | collective-permute-start | bytes 2359304 | tf_op jit(solution)/shard_map/ppermute | solution.py:609
  134.1 18.2 %collective-permute-start.35 = (f32[8,88,256]{2,1,0:T(8,128)S(1)}, f32[8,88,256]{2,1,0:T(8,128)S(1)}, u32[]{:S(2)}, u32[]{:S(2)}) collective-permute-start(f32[8,88,256]{2,1,0:T(8,128)S(1)} %get-tuple-element.194), channel_id=1, source_target_pairs={{0,16},{4,20},{8,24},{12,28},{16,0},{20,4},{24,8},{28,12},{1,17},{... | collective-permute-start | bytes 2162696 | tf_op jit(solution)/shard_map/ppermute | solution.py:609
  135.0 17.9 %collective-permute-start.36 = (f32[8,88,256]{2,1,0:T(8,128)S(1)}, f32[8,88,256]{2,1,0:T(8,128)S(1)}, u32[]{:S(2)}, u32[]{:S(2)}) collective-permute-start(f32[8,88,256]{2,1,0:T(8,128)S(1)} %get-tuple-element.195), channel_id=1, source_target_pairs={{0,1},{1,0},{2,3},{3,2},{4,5},{5,4},{6,7},{7,6},{8,9},{9,8},{10,11... | collective-permute-start | bytes 2162696 | tf_op jit(solution)/shard_map/ppermute | solution.py:609
  (22 other events, 220.6 us)

commit v6 on v5

--- a/solution.py
+++ b/solution.py
@@ -13,8 +13,8 @@
 TN = (((0,), (0,)), ((), ()))
 VMEM = pl.BlockSpec(memory_space=pltpu.VMEM)
 SMEM = pl.BlockSpec(memory_space=pltpu.SMEM)
-PARAMS = pltpu.CompilerParams(vmem_limit_bytes=16 * 1024 * 1024)
-GATHER_PARAMS = pltpu.CompilerParams(vmem_limit_bytes=32 * 1024 * 1024)
+PARAMS = pltpu.CompilerParams(vmem_limit_bytes=12 * 1024 * 1024)
+GATHER_PARAMS = pltpu.CompilerParams(vmem_limit_bytes=48 * 1024 * 1024)
 HBM = pl.BlockSpec(memory_space=pltpu.HBM)
 COST = pl.CostEstimate(flops=10000, bytes_accessed=10000, transcendentals=0)
 
@@ -68,12 +68,24 @@
     return jnp.concatenate([idx[b : b + 1] for b in range(idx.shape[0])], axis=1)
 
 
-def gather_kernel(hub_steps, rel_steps, hub_idx, rel_idx, hub_ref, rel_ref, *refs):
+def take_owned(spot_ref, chunks, span, first, piece_of, out_ref):
+    width = out_ref.shape[1]
+    for chunk in range(chunks):
+        if first <= chunk * width < first + span:
+
+            @pl.when(spot_ref[0] == chunk)
+            def _():
+                out_ref[...] = piece_of(slice(chunk * width - first, (chunk + 1) * width - first))
+
+
+def gather_kernel(hub_steps, rel_steps, spot_ref, hub_idx, rel_idx, hub_sums, rel_sums, hub_ref, rel_ref, *refs):
     buckets = hub_idx.shape[0]
-    ids_out, hub_outs, rel_outs = refs[0], refs[1 : 1 + buckets], refs[1 + buckets : 1 + 2 * buckets]
-    hub_buf, rel_buf, stacked, sems = refs[1 + 2 * buckets :]
-    hubs, edges = hub_idx.shape[1], rel_idx.shape[1]
+    hub_outs, rel_outs = refs[:buckets], refs[buckets : 2 * buckets]
+    spot_out, hub_own, rel_own, hub_own_sums, rel_own_sums = refs[2 * buckets : 2 * buckets + 5]
+    hub_buf, rel_buf, stacked, sems = refs[2 * buckets + 5 :]
     hub_tile, rel_tile = hub_buf.shape[2], rel_buf.shape[2]
+    chunks = hub_ref.shape[1] // hub_own.shape[1]
+    half = hub_own.shape[0]
     steps = [(hub_ref, hub_buf, hub_tile, k) for k in range(hub_steps)]
     steps += [(rel_ref, rel_buf, rel_tile, k) for k in range(rel_steps)]
     copies = [
@@ -81,12 +93,15 @@
         for i, (table, buf, tile, k) in enumerate(steps)
     ]
     copies[0].start()
-    ids_out[:, :hubs] = hub_idx[...]
-    ids_out[:, hubs:] = rel_idx[...]
+    spot_out[0] = spot_ref[0]
+    spot_out[1] = spot_ref[1]
+    take_owned(spot_ref, chunks, hub_sums.shape[1], 0, lambda lanes: hub_sums[:, lanes], hub_own_sums)
+    take_owned(spot_ref, chunks, rel_sums.shape[1], 0, lambda lanes: rel_sums[:, lanes], rel_own_sums)
+    rows = pl.ds(pl.multiple_of(spot_ref[1] * half, 8), half)
     for i, (table, buf, tile, k) in enumerate(steps):
         if i + 1 < len(steps):
             copies[i + 1].start()
-        idx, outs = (hub_idx, hub_outs) if table is hub_ref else (rel_idx, rel_outs)
+        idx, outs, own = (hub_idx, hub_outs, hub_own) if table is hub_ref else (rel_idx, rel_outs, rel_own)
         count = idx.shape[1]
         hot = onehot(k * tile, tile, laid_out(idx[...]))
         copies[i].wait()
@@ -95,21 +110,24 @@
         for b, out in enumerate(outs):
             here = part[:, b * count : (b + 1) * count]
             out[...] = here if k == 0 else out[...] + here
-
-
-def gather_rows(hub_table, hub_idx, rel_table, rel_idx):
+        take_owned(spot_ref, chunks, tile, k * tile, lambda lanes: buf[k % 2, rows, lanes], own)
+
+
+def gather_rows(spot, hub_table, hub_idx, hub_sums, rel_table, rel_idx, rel_sums, chunks):
     features = hub_table.shape[0]
     hub_steps, rel_steps = 4, 2
     hub_tile, rel_tile = hub_table.shape[1] // hub_steps, rel_table.shape[1] // rel_steps
     buckets, hubs = hub_idx.shape
     edges = rel_idx.shape[1]
+    hub_width, rel_width = hub_table.shape[1] // chunks, rel_table.shape[1] // chunks
     shapes = [(features, hubs)] * buckets + [(features, edges)] * buckets
+    own_shapes = [(features // 2, hub_width), (features // 2, rel_width), (1, hub_width), (1, rel_width)]
+    floats = lambda shapes: [jax.ShapeDtypeStruct(shape, F32) for shape in shapes]
     out = pl.pallas_call(
         functools.partial(gather_kernel, hub_steps, rel_steps),
-        in_specs=[VMEM, VMEM, HBM, HBM],
-        out_specs=[VMEM] * (1 + len(shapes)),
-        out_shape=[jax.ShapeDtypeStruct((buckets, hubs + edges), jnp.int32)]
-        + [jax.ShapeDtypeStruct(shape, F32) for shape in shapes],
+        in_specs=[SMEM] + [VMEM] * 4 + [HBM, HBM],
+        out_specs=[VMEM] * len(shapes) + [SMEM] + [VMEM] * len(own_shapes),
+        out_shape=floats(shapes) + [jax.ShapeDtypeStruct((2,), jnp.int32)] + floats(own_shapes),
         scratch_shapes=[
             pltpu.VMEM((2, features, hub_tile), F32),
             pltpu.VMEM((2, features, rel_tile), F32),
@@ -118,8 +136,8 @@
         ],
         compiler_params=GATHER_PARAMS,
         cost_estimate=COST,
-    )(hub_idx, rel_idx, hub_table, rel_table)
-    return out[0], out[1 : 1 + buckets], out[1 + buckets :]
+    )(spot, hub_idx, rel_idx, hub_sums, rel_sums, hub_table, rel_table)
+    return out[:buckets], out[buckets : 2 * buckets], out[2 * buckets], out[2 * buckets + 1 :]
 
 
 def spread_bits(place, order):
@@ -132,9 +150,8 @@
     return sum((((index >> (bits - 1 - i)) & 1) << p) for i, p in enumerate(order))
 
 
-def load_columns(id_refs, id_lanes, grad_refs, idx_down, stacked):
-    low, high = id_lanes
-    idx = jnp.concatenate([laid_out(ref[:, low:high]) for ref in id_refs], axis=1)
+def load_columns(id_refs, grad_refs, idx_down, stacked):
+    idx = jnp.concatenate([laid_out(ref[...]) for ref in id_refs], axis=1)
     idx_down[...] = jnp.transpose(jnp.broadcast_to(idx, (128, idx.shape[1])))
     at = 0
     for ref, (low, high) in grad_refs:
@@ -150,10 +167,32 @@
     return jnp.where(wide == targets, 1.0, 0.0).astype(BF16)
 
 
-def out_for(place, order, sends, keeps, s):
-    index = spread_bits(place, order)
-    half = keeps[s].shape[0]
-    return sends[s].at[index - half] if index >= half else keeps[s].at[index]
+def grouped(orders, step, heights):
+    groups, where = [], []
+    for s, order in enumerate(orders):
+        for g, (place, members) in enumerate(groups):
+            if place == order[step]:
+                where.append((g, sum(heights[m] for m in members)))
+                members.append(s)
+                break
+        else:
+            where.append((len(groups), 0))
+            groups.append((order[step], [s]))
+    return [(place, sum(heights[m] for m in members)) for place, members in groups], where
+
+
+def rows_of(where, heights, s):
+    group, base = where[s]
+    return group, slice(base, base + heights[s])
+
+
+def put_chunk(place, orders, heights, where, sends, keeps, s, value):
+    index, half = spread_bits(place, orders[s]), keeps[s].shape[0]
+    if index < half:
+        keeps[s][index] = value
+    else:
+        group, rows = rows_of(where, heights, s)
+        sends[group][index - half, rows] = value
 
 
 def chunk_refs(grad_lanes, refs):
@@ -162,18 +201,19 @@
     return ids, grads, refs[:-2], refs[-2:]
 
 
-def hub_chunks_kernel(orders, spans, id_lanes, grad_lanes, chip_ref, *refs):
+def hub_chunks_kernel(orders, spans, where, grad_lanes, spot_ref, *refs):
     ids, grads, outs, (idx_down, stacked) = chunk_refs(grad_lanes, refs)
-    load_columns(ids, id_lanes, grads, idx_down, stacked)
+    load_columns(ids, grads, idx_down, stacked)
     streams = len(orders)
-    sends, keeps = outs[:streams], outs[streams:]
+    sends, keeps = outs[:-streams], outs[-streams:]
+    heights = [high - low for low, high in spans]
     chunks, width = 2 * keeps[0].shape[0], keeps[0].shape[2]
     lane = lax.broadcasted_iota(jnp.int32, (1, width), 1)
     for place in range(chunks):
-        hot = onehot_across(idx_down, lane + (chip_ref[0] ^ place) * width)
+        hot = onehot_across(idx_down, lane + (spot_ref[0] ^ place) * width)
         chunk = dot2(stacked[...], hot, NN)
         for s, (low, high) in enumerate(spans):
-            out_for(place, orders[s], sends, keeps, s)[...] = chunk[low:high]
+            put_chunk(place, orders, heights, where, sends, keeps, s, chunk[low:high])
 
 
 def rel_layout(half_width, streams):
@@ -188,13 +228,15 @@
     return spans, pieces
 
 
-def rel_chunks_kernel(pieces, rows, id_lanes, grad_lanes, chip_ref, *refs):
+def rel_chunks_kernel(orders, pieces, rows, grad_lanes, spot_ref, *refs):
     ids, grads, outs, (idx_down, stacked) = chunk_refs(grad_lanes, refs)
-    load_columns(ids, id_lanes, grads, idx_down, stacked)
+    load_columns(ids, grads, idx_down, stacked)
     for ref in outs:
         ref[...] = jnp.zeros_like(ref)
-    depth, lanes = outs[0].shape[0], outs[0].shape[2]
-    chunks = depth * len(outs)
+    streams = len(orders)
+    sends, keeps = outs[:streams], outs[streams:]
+    half, lanes = keeps[0].shape[0], keeps[0].shape[2]
+    chunks = 2 * half
     width = rows // chunks
     group = lanes // width
     lane = lax.broadcasted_iota(jnp.int32, (1, lanes), 1)
@@ -203,16 +245,17 @@
         places = range(first, min(first + group, chunks))
         for slot, place in enumerate(places):
             here = (lane >= slot * width) & (lane < (slot + 1) * width)
-            targets = jnp.where(here, lane + ((chip_ref[0] ^ place) * width - slot * width), targets)
+            targets = jnp.where(here, lane + ((spot_ref[0] ^ place) * width - slot * width), targets)
         dense = dot2(stacked[...], onehot_across(idx_down, targets), NN)
         for slot, place in enumerate(places):
-            out = outs[place // depth].at[place % depth]
             chunk = dense[:, slot * width : (slot + 1) * width]
-            for block, unused, low, count in pieces:
+            for block, s, low, count in pieces:
+                index = spread_bits(place, orders[s])
+                out = sends[s].at[index - half] if index >= half else keeps[s].at[index]
                 out[:count, block * width : (block + 1) * width] = chunk[low : low + count]
 
 
-def chunk_columns(kernel, shapes, chip, ids, grads):
+def chunk_columns(kernel, shapes, spot, ids, grads):
     half_width = grads[0][0].shape[0]
     grad_lanes = [lanes_of for unused, lanes_of in grads]
     count = sum(high - low for low, high in grad_lanes)
@@ -227,7 +270,7 @@
         ],
         compiler_params=PARAMS,
         cost_estimate=COST,
-    )(chip, *ids, *[g for g, unused in grads])
+    )(spot, *ids, *[g for g, unused in grads])
 
 
 def call(kernel, ins, shapes):
@@ -241,46 +284,62 @@
     )(*ins)
 
 
-def sums_kernel(*refs):
-    streams = len(refs) // 4
-    own, got, sends, keeps = [refs[i * streams : (i + 1) * streams] for i in range(4)]
+def sums_kernel(heights, here, there, *refs):
+    streams, groups = len(heights), 1 + max(g for g, unused in here)
+    own, got, sends, keeps = refs[:streams], refs[streams : streams + groups], refs[streams + groups : -streams], refs[-streams:]
     for s in range(streams):
-        half = sends[s].shape[0]
-        sends[s][...] = own[s][half:] + got[s][half:]
-        keeps[s][...] = own[s][:half] + got[s][:half]
-
-
-def halves(own, got):
-    shapes = [(x.shape[0] // 2,) + x.shape[1:] for x in own]
-    out = call(sums_kernel, [*own, *got], shapes * 2)
-    return out[: len(shapes)], out[len(shapes) :]
-
-
-def join_kernel(*refs):
-    streams = len(refs) // 3
-    for s in range(streams):
-        own, got, out = refs[s], refs[streams + s], refs[2 * streams + s]
-        count = own.shape[0]
-        out[:count] = own[...]
-        out[count:] = got[...]
-
-
-def join(own, got):
-    return call(join_kernel, [*own, *got], [(2 * x.shape[0],) + x.shape[1:] for x in own])
-
-
-def plane_sums_kernel(*refs):
-    ins, outs = refs[: -refs[0].shape[0]], refs[-refs[0].shape[0] :]
+        half = keeps[s].shape[0]
+        group, rows = rows_of(here, heights, s)
+        out, out_rows = rows_of(there, heights, s)
+        sends[out][:, out_rows] = own[s][half:] + got[group][half:, rows]
+        keeps[s][...] = own[s][:half] + got[group][:half, rows]
+
+
+def halves(own, got, orders, step):
+    heights = [x.shape[1] for x in own]
+    half, width = own[0].shape[0] // 2, own[0].shape[2]
+    unused, here = grouped(orders, step, heights)
+    groups, there = grouped(orders, step + 1, heights)
+    shapes = [(half, height, width) for height in [h for unused, h in groups] + heights]
+    out = call(functools.partial(sums_kernel, heights, here, there), [*own, *got], shapes)
+    return out[: len(groups)], out[len(groups) :]
+
+
+def join_kernel(heights, here, there, *refs):
+    groups = 1 + max(g for g, unused in here)
+    own, got, outs = refs[:groups], refs[groups : 2 * groups], refs[2 * groups :]
+    count = own[0].shape[0]
+    for s in range(len(heights)):
+        group, rows = rows_of(here, heights, s)
+        out, out_rows = rows_of(there, heights, s)
+        outs[out][:count, out_rows] = own[group][:, rows]
+        outs[out][count:, out_rows] = got[group][:, rows]
+
+
+def join(have, got, orders, step, heights):
+    count, width = have[0].shape[0], have[0].shape[2]
+    unused, here = grouped(orders, step, heights)
+    groups, there = grouped(orders, step - 1, heights)
+    shapes = [(2 * count, height, width) for unused, height in groups]
+    return call(functools.partial(join_kernel, heights, here, there), [*have, *got], shapes)
+
+
+def z_sums_kernel(spans, *refs):
+    streams = len(spans)
+    own, got, outs = refs[:streams], refs[streams : 2 * streams], refs[2 * streams :]
     for place, out in enumerate(outs):
-        out[0] = sum(ref[place] for ref in ins)
-
-
-def squares_kernel(streams, *refs):
-    own, got, rels = refs[:streams], refs[streams : 2 * streams], refs[2 * streams : -streams - 2]
+        for s, (low, high) in enumerate(spans):
+            out[0, low:high] = own[s][place] + got[s][place]
+
+
+def squares_kernel(heights, here, *refs):
+    streams, groups = len(heights), 1 + max(g for g, unused in here)
+    own, got, rels = refs[:streams], refs[streams : streams + groups], refs[streams + groups : -streams - 2]
     totals, rel_total, out = refs[-streams - 2 : -2], refs[-2], refs[-1]
     squares = jnp.zeros((1, out.shape[1]), F32)
     for s in range(streams):
-        total = own[s][0] + got[s][0]
+        group, rows = rows_of(here, heights, s)
+        total = own[s][0] + got[group][0, rows]
         totals[s][0] = total
         squares += jnp.sum(total * total, axis=0, keepdims=True)
     total = sum(ref[0] for ref in rels)
@@ -289,67 +348,79 @@
     out[1:2] = jnp.sum(total * total, axis=0, keepdims=True)
 
 
-def update_kernel(spans, rel_spans, pieces, features, *refs):
-    streams = len(spans)
-    totals, news = refs[:streams], refs[-streams:]
-    rel_total, mine, other, hub_ref, hub_sums, rel_ref, rel_sums = refs[streams:-streams]
+def update_kernel(spans, rel_spans, pieces, there, features, *refs):
+    streams, groups = len(spans), 1 + max(g for g, unused in there)
+    totals, news = refs[:streams], refs[-groups:]
+    rel_total, mine, other, hub_ref, hub_sums, rel_ref, rel_sums = refs[streams:-groups]
     width = rel_ref.shape[1]
     squares = mine[...] + other[...]
     hub_scale = step_rate / jnp.sqrt(hub_sums[...] + squares[0:1] * (1.0 / features))
     rel_squares = sum(squares[1:2, b * width : (b + 1) * width] for b in range(3))
     rel_scale = step_rate / jnp.sqrt(rel_sums[...] + rel_squares * (1.0 / features))
     for s, (low, high) in enumerate(spans):
-        height = high - low
-        news[s][0, :height] = hub_ref[low:high] - totals[s][0] * hub_scale
-        news[s][0, height:] = jnp.zeros_like(news[s][0, height:])
+        new, base = there[s]
+        first, end = rel_spans[s]
+        middle = base + high - low
+        news[new][0, base:middle] = hub_ref[low:high] - totals[s][0] * hub_scale
+        news[new][0, middle : middle + end - first] = jnp.zeros((end - first, news[new].shape[2]), F32)
     for block, s, low, count in pieces:
-        lanes, height = slice(block * width, (block + 1) * width), spans[s][1] - spans[s][0]
-        first = rel_spans[s][0]
-        news[s][0, height : height + count, lanes] = (
+        new, base = there[s]
+        base += spans[s][1] - spans[s][0]
+        lanes, first = slice(block * width, (block + 1) * width), rel_spans[s][0]
+        news[new][0, base : base + count, lanes] = (
             rel_ref[low : low + count] - rel_total[0, first : first + count, lanes] * rel_scale
         )
 
 
-def join_all_kernel(bases, *refs):
-    streams = len(bases)
-    join_kernel(*refs[:-1])
-    for s, base in enumerate(bases):
-        for i, ref in enumerate((refs[s], refs[streams + s])):
-            count, height = ref.shape[0], ref.shape[1]
-            refs[-1][i * count : (i + 1) * count, base : base + height] = ref[...]
-
-
-def join_all(own, got):
-    heights = [x.shape[1] for x in own]
-    bases = [sum(heights[:s]) for s in range(len(own))]
-    count, width = 2 * own[0].shape[0], own[0].shape[2]
-    shapes = [(count, height, width) for height in heights] + [(count, sum(heights), width)]
-    *have, near = call(functools.partial(join_all_kernel, bases), [*own, *got], shapes)
-    return have, near, bases
-
-
-def chunk_copies(part, base, first, order, span, spot_ref, out_ref, sems, at):
+def join_all_kernel(heights, here, there, *refs):
+    groups = 1 + max(g for g, unused in here)
+    join_kernel(heights, here, there, *refs[:-1])
+    base = 0
+    for s, height in enumerate(heights):
+        group, rows = rows_of(here, heights, s)
+        for i, ref in enumerate((refs[group], refs[groups + group])):
+            count = ref.shape[0]
+            refs[-1][i * count : (i + 1) * count, base : base + height] = ref[:, rows]
+        base += height
+
+
+def join_all(have, got, orders, step, heights):
+    count, width = 2 * have[0].shape[0], have[0].shape[2]
+    unused, here = grouped(orders, step, heights)
+    groups, there = grouped(orders, step - 1, heights)
+    shapes = [(count, height, width) for height in [h for unused, h in groups] + [sum(heights)]]
+    *have, near = call(functools.partial(join_all_kernel, heights, here, there), [*have, *got], shapes)
+    return have, near
+
+
+def chunk_copies(part, base, first, order, span, chip, component, out_ref, sems, at):
     low, high = span
     width = part.shape[2]
     for index in range(part.shape[0]):
-        chunk = spot_ref[0] ^ gather_bits(first + index, order)
+        chunk = chip ^ gather_bits(first + index, order)
         lanes = pl.ds(pl.multiple_of(chunk * width, width), width)
-        target = out_ref.at[spot_ref[1], pl.ds(low, high - low), lanes]
+        target = out_ref.at[component, pl.ds(low, high - low), lanes]
         yield pltpu.make_async_copy(part.at[index, pl.ds(base, high - low)], target, sems.at[at + index])
 
 
-def near_kernel(orders, spans, bases, spot_ref, near_ref, *refs):
+def component_of(spot_ref, mine):
+    return spot_ref[1] if mine else 1 - spot_ref[1]
+
+
+def near_kernel(orders, spans, bases, mine, spot_ref, near_ref, *refs):
+    component = component_of(spot_ref, mine)
     out_ref, sems = refs[-2:]
     copies = []
     for order, span, base in zip(orders, spans, bases):
-        copies += chunk_copies(near_ref, base, 0, order, span, spot_ref, out_ref, sems, len(copies))
+        copies += chunk_copies(near_ref, base, 0, order, span, spot_ref[0], component, out_ref, sems, len(copies))
     for copy in copies:
         copy.start()
     for copy in copies:
         copy.wait()
 
 
-def far_kernel(orders, spans, bases, pieces, by_copy, spot_ref, near_ref, *refs):
+def far_kernel(orders, spans, bases, pieces, by_copy, mine, spot_ref, near_ref, *refs):
+    component = component_of(spot_ref, mine)
     streams = len(orders)
     fars = refs[:streams]
     hub_out, rel_out, hub_all, rel_all, sems = refs[-5:]
@@ -358,7 +429,7 @@
     copies = []
     if by_copy:
         for far, order, span in zip(fars, orders, spans):
-            copies += chunk_copies(far, 0, half, order, span, spot_ref, hub_out, sems, len(copies))
+            copies += chunk_copies(far, 0, half, order, span, spot_ref[0], component, hub_out, sems, len(copies))
         for copy in copies:
             copy.start()
     for chunk in range(2 * half):
@@ -375,10 +446,10 @@
                 if stream == s:
                     part = value[:count, block * rel_width : (block + 1) * rel_width]
                     rel_all[row : row + count, chunk * rel_width : (chunk + 1) * rel_width] = part
-    copies.append(pltpu.make_async_copy(rel_all, rel_out.at[spot_ref[1]], sems.at[len(copies)]))
+    copies.append(pltpu.make_async_copy(rel_all, rel_out.at[component], sems.at[len(copies)]))
     copies[-1].start()
     if not by_copy:
-        copies.append(pltpu.make_async_copy(hub_all, hub_out.at[spot_ref[1]], sems.at[len(copies)]))
+        copies.append(pltpu.make_async_copy(hub_all, hub_out.at[component], sems.at[len(copies)]))
         copies[-1].start()
     for copy in copies:
         copy.wait()
@@ -436,7 +507,7 @@
 ):
     features, rows = left_ref.shape
     half = features // 2
-    core = core_ref[0]
+    core = core_ref[1]
     edges = heads_ref.shape[1]
     hubs = keep_out.shape[1] - edges
     at = slice(bucket, bucket + 1)
@@ -525,7 +596,7 @@
         query_grad[:, span] = dot3_stacked(hub_parts[...], coef, NN)
         hub_grad[...] += dot3_stacked(stack(q), coef, NT)
 
-    hub_keep[...], hub_send[...] = keep_and_send(core_ref[0], hub_grad[:half], hub_grad[half:])
+    hub_keep[...], hub_send[...] = keep_and_send(core_ref[1], hub_grad[:half], hub_grad[half:])
 
 
 def hub_step(bucket, negatives, core, heads, left, rel_rows, hub_rows):
@@ -557,7 +628,7 @@
     half = features // 2
     edges = heads_ref.shape[1]
     at = slice(bucket, bucket + 1)
-    core = core_ref[0]
+    core = core_ref[1]
     counts = table_counts(rows, negs_ref[at], 1.0 / (negs_ref.shape[1] + hubs))
     stack_into(left_parts, left_ref[...])
     stack_into(right_parts, right_ref[:features])
@@ -632,6 +703,11 @@
     return [[x, y, z, far] + rest, [y, z, x, far] + rest, [z, x, far, y] + rest]
 
 
+def plane_orders(sub_bits, bits):
+    plane, depth = list(range(sub_bits, bits)), list(range(sub_bits - 1, -1, -1))
+    return [plane + depth, plane[1:] + plane[:1] + depth]
+
+
 def row_spans(rows, parts):
     ends = [-(-rows * (i + 1) // (8 * parts)) * 8 for i in range(parts - 1)] + [rows]
     return list(zip([0] + ends[:-1], ends))
@@ -651,106 +727,113 @@
     buckets, edges = heads.shape
     hubs = hub_ids.shape[1]
 
-    core_id = lax.axis_index("blk") % 2
-    chip_id = (lax.axis_index("blk") // 2) * lax.axis_size("sub") + lax.axis_index("sub")
-    core, chip = core_id.astype(jnp.int32).reshape(1), chip_id.astype(jnp.int32).reshape(1)
     orders = stream_orders()
     streams, stages = len(orders), len(orders[0])
     chunks, depth = 1 << stages, lax.axis_size("sub")
+    sub_bits = depth.bit_length() - 1
     planes = chunks // depth
     spans = row_spans(half_width, streams)
-    unused, rel_pieces = rel_layout(half_width, 1)
+    rel_orders = plane_orders(sub_bits, stages)
+    plane_spans, plane_pieces = rel_layout(half_width, len(rel_orders))
     rel_spans, joint_pieces = rel_layout(half_width, streams)
-    rel_height = rel_spans[-1][1]
-    width, rel_width = hub_count // chunks, rel_count // chunks
+    heights, rel_heights, plane_heights = [[high - low for low, high in x] for x in (spans, rel_spans, plane_spans)]
+    joint_heights = [h + r for h, r in zip(heights, rel_heights)]
+    bases = [sum(joint_heights[:s]) for s in range(streams)]
+    width = hub_count // chunks
     hub_lanes, rel_lanes = (0, hubs), (hubs, hubs + edges)
 
     def exchanged(parts, step):
-        return [across(x, order[step]) for x, order in zip(parts, orders)]
+        return [across(x, place) for x, (place, unused) in zip(parts, grouped(orders, step, heights)[0])]
 
     def in_turn(first, then):
         return lax.optimization_barrier((first, then))
 
-    ids, hub_rows, rel_rows = gather_rows(
-        hub_emb.reshape(features, hub_count), hub_ids, relation_emb.reshape(features, rel_count), relations
-    )
-    far_ids = other_core(ids)
+    blk = lax.axis_index("blk")
+    spot = jnp.stack([(blk >> 1) * depth + lax.axis_index("sub"), blk & 1]).astype(jnp.int32)
+    far_ids = other_core((hub_ids, relations))
+    hub_rows, rel_rows, spot, owned = gather_rows(
+        spot, hub_emb.reshape(features, hub_count), hub_ids, hub_state[None],
+        relation_emb.reshape(features, rel_count), relations, relation_state[None], chunks,
+    )
+    far_ids, hub_rows = in_turn(far_ids, hub_rows)
     keeps, fars = [], []
     for b in range(buckets - 1):
         if b > 0:
             right, right_sums = right[:features], right[features : features + 1]
         left, left_sums, right, keep, send = bucket_step(
-            b, core, heads, tails, negatives, left, left_sums, right, right_sums, rel_rows[b], hub_rows[b]
+            b, spot, heads, tails, negatives, left, left_sums, right, right_sums, rel_rows[b], hub_rows[b]
         )
         right = from_behind(right, "blk", 1)
         keeps.append(keep)
         fars.append(other_core(send))
-    far_ids, left = in_turn(far_ids, left)
     last = buckets - 1
     query_grad, hub_keep, hub_send = hub_step(
-        last, negatives.shape[1], core, heads, left, rel_rows[last], hub_rows[last]
+        last, negatives.shape[1], spot, heads, left, rel_rows[last], hub_rows[last]
     )
     hub_far = other_core(hub_send)
     grads = lambda early, late, lanes: [(x, lanes) for x in early] + [(late, (0, late.shape[1]))]
+    groups, where = grouped(orders, 0, heights)
     parts = chunk_columns(
-        functools.partial(hub_chunks_kernel, orders, spans, hub_lanes),
-        [(chunks // 2, high - low, width) for low, high in spans] * 2, chip, (ids, far_ids),
-        grads(keeps, hub_keep, hub_lanes) + grads(fars, hub_far, hub_lanes),
-    )
-    send, own = parts[:streams], parts[streams:]
+        functools.partial(hub_chunks_kernel, orders, spans, where),
+        [(chunks // 2, height, width) for height in [h for unused, h in groups] + heights],
+        spot, (hub_ids, far_ids[0]), grads(keeps, hub_keep, hub_lanes) + grads(fars, hub_far, hub_lanes),
+    )
+    send, own = parts[: len(groups)], parts[len(groups) :]
     got = exchanged(send, 0)
     left, right, rel_keep, rel_send = tables_step(
-        last, hubs, core, heads, tails, negatives, query_grad, left, left_sums, right, rel_rows[last]
+        last, hubs, spot, heads, tails, negatives, query_grad, left, left_sums, right, rel_rows[last]
     )
     rel_far = other_core(rel_send)
 
     rel_keep, got = in_turn(rel_keep, got)
-    send, own = halves(own, got)
+    send, own = halves(own, got, orders, 0)
     got = exchanged(send, 1)
     own, rel_far = in_turn(own, rel_far)
-    rel_own, *rel_out = chunk_columns(
-        functools.partial(rel_chunks_kernel, rel_pieces, rel_count, rel_lanes),
-        [(depth, rel_height, width)] * planes, chip, (ids, far_ids),
-        grads(keeps, rel_keep, rel_lanes) + grads(fars, rel_far, rel_lanes),
-    )
-    rel_got = [flipped_by(x, "blk", 2 * (p + 1)) for p, x in enumerate(rel_out)]
-    for step in range(2, stages):
+    parts = chunk_columns(
+        functools.partial(rel_chunks_kernel, rel_orders, plane_pieces, rel_count),
+        [(chunks // 2, height, width) for height in plane_heights * 2],
+        spot, (relations, far_ids[1]), grads(keeps, rel_keep, rel_lanes) + grads(fars, rel_far, rel_lanes),
+    )
+    rel_send, rel_own = parts[: len(rel_orders)], parts[len(rel_orders) :]
+    rel_got = [across(x, order[0]) for x, order in zip(rel_send, rel_orders)]
+    for step in range(1, stages - 1):
         rel_own, got = in_turn(rel_own, got)
-        send, own = halves(own, got)
-        got = exchanged(send, step)
-        if step == 2:
-            late, own, rel_got = lax.optimization_barrier((jnp.stack([core_id, chip_id]), own, rel_got))
-            rel_own, *rel_out = call(plane_sums_kernel, [rel_own, *rel_got], [(1, rel_height, width)] * depth)
-            rel_got = [flipped_by(x, "sub", q + 1) for q, x in enumerate(rel_out)]
-
-    cut = lambda x, span: lax.dynamic_slice(x, (late[0], 0, late[1] * span), (1, half_width, span))[0]
-    cut_sums = lambda x, span: lax.dynamic_slice(x[None], (0, late[1] * span), (1, span))
+        send, own = halves(own, got, orders, step)
+        got = exchanged(send, step + 1)
+        if step < stages - sub_bits:
+            own, rel_got = in_turn(own, rel_got)
+            rel_send, rel_own = halves(rel_own, rel_got, rel_orders, step - 1)
+            rel_got = [across(x, order[step]) for x, order in zip(rel_send, rel_orders)]
+    own, rel_got = in_turn(own, rel_got)
+    rel_own, *rel_out = call(
+        functools.partial(z_sums_kernel, plane_spans), [*rel_own, *rel_got], [(1, plane_spans[-1][1], width)] * depth
+    )
+    rel_got = [flipped_by(x, "sub", q + 1) for q, x in enumerate(rel_out)]
+
     *totals, rel_total, squares = call(
-        functools.partial(squares_kernel, streams), [*own, *got, rel_own, *rel_got],
-        [x.shape for x in own] + [rel_own.shape, (2, width)],
-    )
+        functools.partial(squares_kernel, heights, grouped(orders, stages - 1, heights)[1]),
+        [*own, *got, rel_own, *rel_got], [x.shape for x in own] + [rel_own.shape, (2, width)],
+    )
+    hub_own, rel_own, hub_sums, rel_sums = owned
+    groups, there = grouped(orders, stages - 1, joint_heights)
     have = call(
-        functools.partial(update_kernel, spans, rel_spans, joint_pieces, features),
-        [
-            *totals, rel_total, squares, other_core(squares), cut(hub_emb, width), cut_sums(hub_state, width),
-            cut(relation_emb, rel_width), cut_sums(relation_state, rel_width),
-        ],
-        [(1, high - low + end - first, width) for (low, high), (first, end) in zip(spans, rel_spans)],
+        functools.partial(update_kernel, spans, rel_spans, joint_pieces, there, features),
+        [*totals, rel_total, squares, other_core(squares), hub_own, hub_sums, rel_own, rel_sums],
+        [(1, height, width) for unused, height in groups],
     )
     for step in range(stages - 1, 1, -1):
-        have = join(have, exchanged(have, step))
-    have, near, bases = join_all(have, exchanged(have, 1))
+        have = join(have, exchanged(have, step), orders, step, joint_heights)
+    have, near = join_all(have, exchanged(have, 1), orders, 1, joint_heights)
     got = exchanged(have, 0)
     far_near = other_core(near)
 
-    mine, others = jnp.concatenate([chip, core]), jnp.concatenate([chip, 1 - core])
     shapes = [hub_emb.shape, relation_emb.shape]
     by_copy = width % 128 == 0
     hub_new = []
     if by_copy:
         near_step = functools.partial(near_kernel, orders, spans, bases)
-        hub_new = placed(near_step, [], mine, near, [], shapes[:1], [])
-        hub_new = placed(near_step, [], others, far_near, [], shapes[:1], hub_new)
+        hub_new = placed(functools.partial(near_step, True), [], spot, near, [], shapes[:1], [])
+        hub_new = placed(functools.partial(near_step, False), [], spot, far_near, [], shapes[:1], hub_new)
         got, hub_new = in_turn(got, hub_new)
     far_step = functools.partial(far_kernel, orders, spans, bases, joint_pieces, by_copy)
     scratch = [
@@ -758,8 +841,8 @@
         pltpu.VMEM((half_width, rel_count), F32),
     ]
     far_got = other_core(got)
-    hub_new, rel_new = placed(far_step, scratch, mine, near, got, shapes, hub_new)
-    hub_new, rel_new = placed(far_step, scratch, others, far_near, far_got, shapes, [hub_new, rel_new])
+    out = placed(functools.partial(far_step, True), scratch, spot, near, got, shapes, hub_new)
+    hub_new, rel_new = placed(functools.partial(far_step, False), scratch, spot, far_near, far_got, shapes, out)
     return (
         left.reshape(components, half_width, row_count),
         right.reshape(components, half_width, row_count),

time: 161 us -> 154 us (0.957)
  local copies, waits for them, and re-layouts: 11.3 us -> 4.39 us
  between operations: 4.33 us -> 1.11 us
  Pallas kernels: 39.6 us -> 42.8 us
    unnamed x28 -> x22, local copies, waits for them, and re-layouts: 7.88 us -> 3.69 us
    ppermute x6 -> x3, starting transfers between devices: 8.07 us -> 4.45 us  [flipped_by(): lax.ppermute(x, axis, [(i, i ^ offset) for i in range(lax.axis_size(axis))])]
    pallas_call x1, Pallas kernels: 8.16 us -> 10.3 us  [gather_rows(): pl.pallas_call(functools.partial(gather_kernel, hub_steps, rel_steps), in...]
    squeeze x2 -> x0, local copies, waits for them, and re-layouts: 1.97 us -> none  [shards(): lax.dynamic_slice(x, (late[0], 0, late[1] * span), (1, half_width, span))[0]]
    ppermute x33 -> x36, starting transfers between devices: 34 us -> 35.8 us  [flipped(): lax.ppermute(x, axis, [(i, i ^ 1 << bit) for i in range(lax.axis_size(axi...]
    ppermute x33 -> x36, waiting for transfers between devices: 62.8 us -> 63.5 us  [flipped(): lax.ppermute(x, axis, [(i, i ^ 1 << bit) for i in range(lax.axis_size(axi...]
  transfers between devices with their start and end apart: 40 -> 40, of which waited for: 18 -> 23; matrix products, arithmetic and copies ran while one was open for 2% -> 1% of each run, Pallas kernels for 14% -> 22%
where the time goes in v6:
time: 154 us
  waiting for transfers between devices  64.3 us (42%)
  Pallas kernels  42.8 us (28%)
  starting transfers between devices  40.9 us (27%)
  local copies, waits for them, and re-layouts  4.39 us (3%)
    ppermute x36, waiting for transfers between devices, flipped(): lax.ppermute(x, axis, [(i, i ^ 1 << bit) for i in range(lax.axis_size(axi...  63.5 us
    ppermute x36, starting transfers between devices, flipped(): lax.ppermute(x, axis, [(i, i ^ 1 << bit) for i in range(lax.axis_size(axi...  35.8 us
    pallas_call x1, Pallas kernels, gather_rows(): pl.pallas_call(functools.partial(gather_kernel, hub_steps, rel_steps), in...  10.3 us
    pallas_call x4, Pallas kernels, placed(): pl.pallas_call(kernel, in_specs=[SMEM] + [VMEM] * (1 + len(fars)) + [HBM]...  9.34 us
    pallas_call x2, Pallas kernels, chunk_columns(): pl.pallas_call(functools.partial(kernel, grad_lanes), in_specs=[SMEM] + [...  7.92 us
    pallas_call x1, Pallas kernels, bucket_step(): pl.pallas_call(functools.partial(bucket_kernel, bucket), in_specs=[SMEM]...  5.72 us
    pallas_call x1, Pallas kernels, tables_step(): pl.pallas_call(functools.partial(tables_kernel, bucket, hubs), in_specs=[...  5.53 us
    ppermute x3, starting transfers between devices, flipped_by(): lax.ppermute(x, axis, [(i, i ^ offset) for i in range(lax.axis_size(axis))])  4.45 us
  transfers between devices with their start and end apart: 40, of which 23 were waited for; matrix products, arithmetic and copies ran while one was open for 1% of the time, Pallas kernels for 22%

profile of v6, /device:TPU:0, one launch (start us, length us, event | category | flops | bytes accessed | tf_op | source)
XLA Modules:
  0.0 153.6 jit_solution(13577594283092216656)
XLA Ops:
  5.7 10.3 %shard_map.156 = (f32[400,256]{1,0:T(8,128)S(1)}, f32[400,256]{1,0:T(8,128)S(1)}, f32[400,512]{1,0:T(8,128)S(1)}, f32[400,512]{1,0:T(8,128)S(1)}, s32[2]{0:T(128...) custom-call(s32[2]{0:T(128)S(1)} %pad_add_fusion.spot_ref, ...), custom_call_target="tpu_custom_call" | custom-call | flops 10000 | bytes 10000 | tf_op jit(solution)/shard_map/pallas_call | solution.py:126
  16.1 5.7 %shard_map.157 = (f32[400,512]{1,0:T(8,128)S(1)}, f32[1,512]{1,0:T(1,128)S(1)}, f32[408,512]{1,0:T(8,128)S(1)}, f32[200,768]{1,0:T(8,128)S(1)}, f32[200,768]{1,0:T(8,128)S(1)}) custom-call(s32[2]{0:T(128)S(1)} %get-tuple-element.117.core_ref.spot_ref, s32[2,512]{1,0:T(2,128)S(1)} %copy-done.3, s32[2,512]{1,0:T(2,128)S(1)} %copy-done.6, ...), custom_call_target="tpu_custom_call" | custom-call | flops 10000 | bytes 10000 | tf_op jit(solution)/shard_map/pallas_call | solution.py:559
  22.5 2.7 %collective-permute-start.3 = (f32[200,768]{1,0:T(8,128)S(1)}, f32[200,768]{1,0:T(8,128)S(1)}, u32[]{:S(2)}, u32[]{:S(2)}) collective-permute-start(f32[200,768]{1,0:T(8,128)S(1)} %get-tuple-element.133), channel_id=1, source_target_pairs={{0,4},{4,0},{8,12},{12,8},{16,20},{20,16},{24,28},{28,24},{1,5},{5... | collective-permute-start | bytes 1843208 | tf_op jit(solution)/shard_map/ppermute | solution.py:680
  25.3 2.7 %shard_map.158 = (f32[400,512]{1,0:T(8,128)S(1)}, f32[200,256]{1,0:T(8,128)S(1)}, f32[200,256]{1,0:T(8,128)S(1)}) custom-call(s32[2]{0:T(128)S(1)} %get-tuple-element.117.core_ref.spot_ref, s32[2,512]{1,0:T(2,128)S(1)} %copy-done.3, f32[400,512]{1,0:T(8,128)S(1)} %get-tuple-element.122.left_ref, f32[400,512]{1,0:T(8,128)S(1)} %get-tuple-element.123.rel_ref, ...), custom_call_target="tpu_custom_call" | custom-call | flops 10000 | bytes 10000 | tf_op jit(solution)/shard_map/pallas_call | solution.py:606
  29.5 4.3 %shard_map.160 = (f32[8,72,256]{2,1,0:T(8,128)S(1)}, f32[8,64,256]{2,1,0:T(8,128)S(1)}, f32[8,64,256]{2,1,0:T(8,128)S(1)}, f32[8,72,256]{2,1,0:T(8,128)S(1)}, f3...) custom-call(s32[2]{0:T(128)S(1)} %get-tuple-element.117.core_ref.spot_ref, s32[2,256]{1,0:T(2,128)S(1)} %copy-done.8, ...), custom_call_target="tpu_custom_call" | custom-call | flops 10000 | bytes 10000 | tf_op jit(solution)/shard_map/pallas_call | solution.py:262
  35.5 2.0 %collective-permute-start.7 = (f32[8,64,256]{2,1,0:T(8,128)S(1)}, f32[8,64,256]{2,1,0:T(8,128)S(1)}, u32[]{:S(2)}, u32[]{:S(2)}) collective-permute-start(f32[8,64,256]{2,1,0:T(8,128)S(1)} %get-tuple-element.141), channel_id=1, source_target_pairs={{0,1},{1,0},{2,3},{3,2},{4,5},{5,4},{6,7},{7,6},{8,9},{9,8},{10,11... | collective-permute-start | bytes 1572872 | tf_op jit(solution)/shard_map/ppermute | solution.py:680
  37.5 5.5 %shard_map.159 = (f32[400,512]{1,0:T(8,128)}, f32[400,512]{1,0:T(8,128)}, f32[200,512]{1,0:T(8,128)S(1)}, f32[200,512]{1,0:T(8,128)S(1)}) custom-call(s32[2]{0:T(128)S(1)} %get-tuple-element.117.core_ref.spot_ref, s32[2,512]{1,0:T(2,128)S(1)} %copy-done.3, s32[2,512]{1,0:T(2,128)S(1)} %copy-done.6, s32[2,1024]{1,0:T(2,128)S(1)} %copy-done.4, ...), custom_call_target="tpu_custom_call" | custom-call | flops 10000 | bytes 10000 | tf_op jit(solution)/shard_map/pallas_call | solution.py:662
  43.0 5.9 %collective-permute-done.6.refs_4_ = f32[8,64,256]{2,1,0:T(8,128)S(1)} collective-permute-done((f32[8,64,256]{2,1,0:T(8,128)S(1)}, f32[8,64,256]{2,1,0:T(8,128)S(1)}, u32[]{:S(2)}, u32[]{:S(2)}) %collective-permute-start.6) | collective-permute-done | bytes 524320 | tf_op jit(solution)/shard_map/ppermute | solution.py:680
  51.0 3.6 %shard_map.162 = (f32[8,40,256]{2,1,0:T(8,128)S(1)}, f32[8,32,256]{2,1,0:T(8,128)S(1)}, f32[8,40,256]{2,1,0:T(8,128)S(1)}, f32[8,32,256]{2,1,0:T(8,128)S(1)}) custom-call(s32[2]{0:T(128)S(1)} %get-tuple-element.117.core_ref.spot_ref, s32[2,512]{1,0:T(2,128)S(1)} %copy-done.7, s32[2,512]{1,0:T(2,128)S(1)} %collective-permute-done.1.refs_1_, ...), custom_call_target="tpu_custom_call" | custom-call | flops 10000 | bytes 10000 | tf_op jit(solution)/shard_map/pallas_call | solution.py:262
  55.3 1.6 %collective-permute-start.10 = (f32[4,64,256]{2,1,0:T(8,128)S(1)}, f32[4,64,256]{2,1,0:T(8,128)S(1)}, u32[]{:S(2)}, u32[]{:S(2)}) collective-permute-start(f32[4,64,256]{2,1,0:T(8,128)S(1)} %get-tuple-element.158), channel_id=1, source_target_pairs={{0,1},{1,0},{2,3},{3,2},{4,5},{5,4},{6,7},{7,6},{8,9},{9,8},{10,11... | collective-permute-start | bytes 786440 | tf_op jit(solution)/shard_map/ppermute | solution.py:680
  58.9 3.5 %collective-permute-done.10.refs_4_ = f32[4,64,256]{2,1,0:T(8,128)S(1)} collective-permute-done((f32[4,64,256]{2,1,0:T(8,128)S(1)}, f32[4,64,256]{2,1,0:T(8,128)S(1)}, u32[]{:S(2)}, u32[]{:S(2)}) %collective-permute-start.10) | collective-permute-done | bytes 262176 | tf_op jit(solution)/shard_map/ppermute | solution.py:680
  62.4 6.6 %collective-permute-done.11.refs_5_ = f32[4,64,256]{2,1,0:T(8,128)S(1)} collective-permute-done((f32[4,64,256]{2,1,0:T(8,128)S(1)}, f32[4,64,256]{2,1,0:T(8,128)S(1)}, u32[]{:S(2)}, u32[]{:S(2)}) %collective-permute-start.11) | collective-permute-done | bytes 262176 | tf_op jit(solution)/shard_map/ppermute | solution.py:680
  69.1 1.6 %collective-permute-start.14 = (f32[2,72,256]{2,1,0:T(8,128)S(1)}, f32[2,72,256]{2,1,0:T(8,128)S(1)}, u32[]{:S(2)}, u32[]{:S(2)}) collective-permute-start(f32[2,72,256]{2,1,0:T(8,128)S(1)} %get-tuple-element.177), channel_id=1, source_target_pairs={{0,1},{1,0},{2,3},{3,2},{4,5},{5,4},{6,7},{7,6},{8,9},{9,8},{10,11... | collective-permute-start | bytes 442376 | tf_op jit(solution)/shard_map/ppermute | solution.py:680
  71.2 2.6 %collective-permute-start.16 = (f32[2,64,256]{2,1,0:T(8,128)S(1)}, f32[2,64,256]{2,1,0:T(8,128)S(1)}, u32[]{:S(2)}, u32[]{:S(2)}) collective-permute-start(f32[2,64,256]{2,1,0:T(8,128)S(1)} %get-tuple-element.179), channel_id=1, source_target_pairs={{0,2},{1,3},{2,0},{3,1},{4,6},{5,7},{6,4},{7,5},{8,10},{9,11},{10,... | collective-permute-start | bytes 393224 | tf_op jit(solution)/shard_map/ppermute | solution.py:680
  73.9 1.6 %collective-permute-start.17 = (f32[4,40,256]{2,1,0:T(8,128)S(1)}, f32[4,40,256]{2,1,0:T(8,128)S(1)}, u32[]{:S(2)}, u32[]{:S(2)}) collective-permute-start(f32[4,40,256]{2,1,0:T(8,128)S(1)} %get-tuple-element.186), channel_id=1, source_target_pairs={{0,16},{4,20},{8,24},{12,28},{16,0},{20,4},{24,8},{28,12},{1,17},{... | collective-permute-start | bytes 491528 | tf_op jit(solution)/shard_map/ppermute | solution.py:680
  76.4 3.7 %collective-permute-done.16.refs_5_ = f32[2,64,256]{2,1,0:T(8,128)S(1)} collective-permute-done((f32[2,64,256]{2,1,0:T(8,128)S(1)}, f32[2,64,256]{2,1,0:T(8,128)S(1)}, u32[]{:S(2)}, u32[]{:S(2)}) %collective-permute-start.16) | collective-permute-done | bytes 131104 | tf_op jit(solution)/shard_map/ppermute | solution.py:680
  83.3 1.6 %collective-permute-start.23 = (f32[1,72,256]{2,1,0:T(8,128)S(1)}, f32[1,72,256]{2,1,0:T(8,128)S(1)}, u32[]{:S(2)}, u32[]{:S(2)}) collective-permute-start(f32[1,72,256]{2,1,0:T(8,128)S(1)} %get-tuple-element.200), channel_id=1, source_target_pairs={{0,3},{1,2},{2,1},{3,0},{4,7},{5,6},{6,5},{7,4},{8,11},{9,10},{10,... | collective-permute-start | bytes 221192 | tf_op jit(solution)/shard_map/ppermute | solution.py:684
  84.9 1.9 %collective-permute-start.20 = (f32[1,64,256]{2,1,0:T(8,128)S(1)}, f32[1,64,256]{2,1,0:T(8,128)S(1)}, u32[]{:S(2)}, u32[]{:S(2)}) collective-permute-start(f32[1,64,256]{2,1,0:T(8,128)S(1)} %get-tuple-element.192), channel_id=1, source_target_pairs={{0,16},{4,20},{8,24},{12,28},{16,0},{20,4},{24,8},{28,12},{1,17},{... | collective-permute-start | bytes 196616 | tf_op jit(solution)/shard_map/ppermute | solution.py:680
  86.8 2.4 %collective-permute-done.20.refs_4_ = f32[1,64,256]{2,1,0:T(8,128)S(1)} collective-permute-done((f32[1,64,256]{2,1,0:T(8,128)S(1)}, f32[1,64,256]{2,1,0:T(8,128)S(1)}, u32[]{:S(2)}, u32[]{:S(2)}) %collective-permute-start.20) | collective-permute-done | bytes 65568 | tf_op jit(solution)/shard_map/ppermute | solution.py:680
  91.7 2.3 %collective-permute-start.25 = (f32[1,184,256]{2,1,0:T(8,128)S(1)}, f32[1,184,256]{2,1,0:T(8,128)S(1)}, u32[]{:S(2)}, u32[]{:S(2)}) collective-permute-start(f32[1,184,256]{2,1,0:T(8,128)S(1)} %get-tuple-element.210.refs_0_), channel_id=1, source_target_pairs={{0,2},{1,3},{2,0},{3,1},{4,6},{5,7},{6,4},{7,5},{8,10},{9,11},{10,... | collective-permute-start | bytes 565256 | tf_op jit(solution)/shard_map/ppermute | solution.py:680
  95.5 3.0 %collective-permute-done.26.refs_3_ = f32[1,88,256]{2,1,0:T(8,128)S(1)} collective-permute-done((f32[1,88,256]{2,1,0:T(8,128)S(1)}, f32[1,88,256]{2,1,0:T(8,128)S(1)}, u32[]{:S(2)}, u32[]{:S(2)}) %collective-permute-start.26) | collective-permute-done | bytes 90144 | tf_op jit(solution)/shard_map/ppermute | solution.py:680
  98.5 4.9 %collective-permute-done.25.refs_2_ = f32[1,184,256]{2,1,0:T(8,128)S(1)} collective-permute-done((f32[1,184,256]{2,1,0:T(8,128)S(1)}, f32[1,184,256]{2,1,0:T(8,128)S(1)}, u32[]{:S(2)}, u32[]{:S(2)}) %collective-permute-start.25) | collective-permute-done | bytes 188448 | tf_op jit(solution)/shard_map/ppermute | solution.py:680
  103.6 1.9 %collective-permute-start.28 = (f32[2,88,256]{2,1,0:T(8,128)S(1)}, f32[2,88,256]{2,1,0:T(8,128)S(1)}, u32[]{:S(2)}, u32[]{:S(2)}) collective-permute-start(f32[2,88,256]{2,1,0:T(8,128)S(1)} %get-tuple-element.213.refs_1_), channel_id=1, source_target_pairs={{0,8},{4,12},{8,0},{12,4},{16,24},{20,28},{24,16},{28,20},{1,9},{5... | collective-permute-start | bytes 540680 | tf_op jit(solution)/shard_map/ppermute | solution.py:680
  105.5 2.7 %collective-permute-start.29 = (f32[2,88,256]{2,1,0:T(8,128)S(1)}, f32[2,88,256]{2,1,0:T(8,128)S(1)}, u32[]{:S(2)}, u32[]{:S(2)}) collective-permute-start(f32[2,88,256]{2,1,0:T(8,128)S(1)} %get-tuple-element.214.refs_2_), channel_id=1, source_target_pairs={{0,2},{1,3},{2,0},{3,1},{4,6},{5,7},{6,4},{7,5},{8,10},{9,11},{10,... | collective-permute-start | bytes 540680 | tf_op jit(solution)/shard_map/ppermute | solution.py:680
  108.1 1.7 %collective-permute-done.28.refs_4_ = f32[2,88,256]{2,1,0:T(8,128)S(1)} collective-permute-done((f32[2,88,256]{2,1,0:T(8,128)S(1)}, f32[2,88,256]{2,1,0:T(8,128)S(1)}, u32[]{:S(2)}, u32[]{:S(2)}) %collective-permute-start.28) | collective-permute-done | bytes 180256 | tf_op jit(solution)/shard_map/ppermute | solution.py:680
  109.8 6.3 %collective-permute-done.29.refs_5_ = f32[2,88,256]{2,1,0:T(8,128)S(1)} collective-permute-done((f32[2,88,256]{2,1,0:T(8,128)S(1)}, f32[2,88,256]{2,1,0:T(8,128)S(1)}, u32[]{:S(2)}, u32[]{:S(2)}) %collective-permute-start.29) | collective-permute-done | bytes 180256 | tf_op jit(solution)/shard_map/ppermute | solution.py:680
  118.1 7.3 %collective-permute-done.31.refs_4_ = f32[4,88,256]{2,1,0:T(8,128)S(1)} collective-permute-done((f32[4,88,256]{2,1,0:T(8,128)S(1)}, f32[4,88,256]{2,1,0:T(8,128)S(1)}, u32[]{:S(2)}, u32[]{:S(2)}) %collective-permute-start.31) | collective-permute-done | bytes 360480 | tf_op jit(solution)/shard_map/ppermute | solution.py:680
  129.5 1.9 %shard_map.172.refs_0_ = f32[2,200,4096]{2,1,0:T(8,128)} custom-call(s32[2]{0:T(128)S(1)} %get-tuple-element.117.core_ref.spot_ref, f32[8,272,256]{2,1,0:T(8,128)S(1)} %get-tuple-element.218.near_ref), custom_call_target="tpu_custom_call" | custom-call | bytes 3276800 | tf_op jit(solution)/shard_map/pallas_call | solution.py:460
  131.4 1.9 %shard_map.173.refs_3_ = f32[2,200,4096]{2,1,0:T(8,128)} custom-call(s32[2]{0:T(128)S(1)} %get-tuple-element.117.core_ref.spot_ref, f32[8,272,256]{2,1,0:T(8,128)S(1)} %collective-permute-done.33.near_ref, f32[2,200,4096]{2,1,0:T(8,128)} %shard_map.172.refs_0_), custom_call_target="tpu_custom_call", output_to_operand_aliasing={{}: (2, {})} | custom-call | bytes 3276800 | tf_op jit(solution)/shard_map/pallas_call | solution.py:460
  133.3 12.1 %collective-permute-done.35.refs_1_ = f32[8,88,256]{2,1,0:T(8,128)S(1)} collective-permute-done((f32[8,88,256]{2,1,0:T(8,128)S(1)}, f32[8,88,256]{2,1,0:T(8,128)S(1)}, u32[]{:S(2)}, u32[]{:S(2)}) %collective-permute-start.35) | collective-permute-done | bytes 720928 | tf_op jit(solution)/shard_map/ppermute | solution.py:680
  146.8 2.7 %shard_map.174 = (f32[2,200,4096]{2,1,0:T(8,128)}, f32[2,200,1280]{2,1,0:T(8,128)}) custom-call(s32[2]{0:T(128)S(1)} %get-tuple-element.117.core_ref.spot_ref, f32[8,272,256]{2,1,0:T(8,128)S(1)} %get-tuple-element.218.near_ref, f32[8,96,256]{2,1,0:T(8,128)S(1)} %collective-permute-done.34.refs_0_, ...), custom_call_target="tpu_custom_call", output_to_operand_aliasing={{0}: (5, {})} | custom-call | bytes 3276800 | tf_op jit(solution)/shard_map/pallas_call | solution.py:460
  150.6 2.8 %shard_map.175 = (f32[2,200,4096]{2,1,0:T(8,128)}, f32[2,200,1280]{2,1,0:T(8,128)}) custom-call(s32[2]{0:T(128)S(1)} %get-tuple-element.117.core_ref.spot_ref, f32[8,272,256]{2,1,0:T(8,128)S(1)} %collective-permute-done.33.near_ref, f32[8,96,256]{2,1,0:T(8,128)S(1)} %collective-permute-done.37.refs_0_, ...), custom_call_target="tpu_custom_call", output_to_operand_aliasing={{0}: (5, {}), {1}: (6, {})} | custom-call | bytes 3276800 | tf_op jit(solution)/shard_map/pallas_call | solution.py:460
  (92 shorter events, 31.1 us)
Async XLA Ops:
  0.7 15.4 %collective-permute-start = (s32[2,256]{1,0:T(2,128)}, s32[2,256]{1,0:T(2,128)S(1)}, u32[]{:S(2)}, u32[]{:S(2)}) collective-permute-start(s32[2,256]{1,0:T(2,128)} %refs_0_.2), channel_id=1, source_target_pairs={{0,4},{4,0},{8,12},{12,8},{16,20},{20,16},{24,28},{28,24},{1,5},{5... | collective-permute-start | bytes 6152 | tf_op jit(solution)/shard_map/ppermute | solution.py:680
  1.2 14.9 %collective-permute-start.1 = (s32[2,512]{1,0:T(2,128)}, s32[2,512]{1,0:T(2,128)S(1)}, u32[]{:S(2)}, u32[]{:S(2)}) collective-permute-start(s32[2,512]{1,0:T(2,128)} %refs_0_.3), channel_id=1, source_target_pairs={{0,4},{4,0},{8,12},{12,8},{16,20},{20,16},{24,28},{28,24},{1,5},{5... | collective-permute-start | bytes 12296 | tf_op jit(solution)/shard_map/ppermute | solution.py:680
  21.9 15.6 %collective-permute-start.2 = (f32[408,512]{1,0:T(8,128)S(1)}, f32[408,512]{1,0:T(8,128)S(1)}, u32[]{:S(2)}, u32[]{:S(2)}) collective-permute-start(f32[408,512]{1,0:T(8,128)S(1)} %get-tuple-element.127), channel_id=1, source_target_pairs={{0,4},{4,8},{8,12},{12,16},{16,20},{20,24},{24,28},{28,0},{1,5},{5... | collective-permute-start | bytes 2506760 | tf_op jit(solution)/shard_map/ppermute | solution.py:676
  22.5 6.9 %collective-permute-start.3 = (f32[200,768]{1,0:T(8,128)S(1)}, f32[200,768]{1,0:T(8,128)S(1)}, u32[]{:S(2)}, u32[]{:S(2)}) collective-permute-start(f32[200,768]{1,0:T(8,128)S(1)} %get-tuple-element.133), channel_id=1, source_target_pairs={{0,4},{4,0},{8,12},{12,8},{16,20},{20,16},{24,28},{28,24},{1,5},{5... | collective-permute-start | bytes 1843208 | tf_op jit(solution)/shard_map/ppermute | solution.py:680
  33.8 15.4 %collective-permute-start.5 = (f32[8,72,256]{2,1,0:T(8,128)S(1)}, f32[8,72,256]{2,1,0:T(8,128)S(1)}, u32[]{:S(2)}, u32[]{:S(2)}) collective-permute-start(f32[8,72,256]{2,1,0:T(8,128)S(1)} %get-tuple-element.139), channel_id=1, source_target_pairs={{0,8},{4,12},{8,0},{12,4},{16,24},{20,28},{24,16},{28,20},{1,9},{5... | collective-permute-start | bytes 1769480 | tf_op jit(solution)/shard_map/ppermute | solution.py:680
  35.3 13.7 %collective-permute-start.6 = (f32[8,64,256]{2,1,0:T(8,128)S(1)}, f32[8,64,256]{2,1,0:T(8,128)S(1)}, u32[]{:S(2)}, u32[]{:S(2)}) collective-permute-start(f32[8,64,256]{2,1,0:T(8,128)S(1)} %get-tuple-element.140), channel_id=1, source_target_pairs={{0,16},{4,20},{8,24},{12,28},{16,0},{20,4},{24,8},{28,12},{1,17},{... | collective-permute-start | bytes 1572872 | tf_op jit(solution)/shard_map/ppermute | solution.py:680
  35.5 13.7 %collective-permute-start.7 = (f32[8,64,256]{2,1,0:T(8,128)S(1)}, f32[8,64,256]{2,1,0:T(8,128)S(1)}, u32[]{:S(2)}, u32[]{:S(2)}) collective-permute-start(f32[8,64,256]{2,1,0:T(8,128)S(1)} %get-tuple-element.141), channel_id=1, source_target_pairs={{0,1},{1,0},{2,3},{3,2},{4,5},{5,4},{6,7},{7,6},{8,9},{9,8},{10,11... | collective-permute-start | bytes 1572872 | tf_op jit(solution)/shard_map/ppermute | solution.py:680
  43.0 8.0 %collective-permute-start.8 = (f32[200,512]{1,0:T(8,128)S(1)}, f32[200,512]{1,0:T(8,128)S(1)}, u32[]{:S(2)}, u32[]{:S(2)}) collective-permute-start(f32[200,512]{1,0:T(8,128)S(1)} %get-tuple-element.148), channel_id=1, source_target_pairs={{0,4},{4,0},{8,12},{12,8},{16,20},{20,16},{24,28},{28,24},{1,5},{5... | collective-permute-start | bytes 1228808 | tf_op jit(solution)/shard_map/ppermute | solution.py:680
  49.5 19.5 %collective-permute-start.9 = (f32[4,72,256]{2,1,0:T(8,128)S(1)}, f32[4,72,256]{2,1,0:T(8,128)S(1)}, u32[]{:S(2)}, u32[]{:S(2)}) collective-permute-start(f32[4,72,256]{2,1,0:T(8,128)S(1)} %get-tuple-element.157), channel_id=1, source_target_pairs={{0,16},{4,20},{8,24},{12,28},{16,0},{20,4},{24,8},{28,12},{1,17},{... | collective-permute-start | bytes 884744 | tf_op jit(solution)/shard_map/ppermute | solution.py:680
  54.6 19.2 %collective-permute-start.12 = (f32[8,40,256]{2,1,0:T(8,128)S(1)}, f32[8,40,256]{2,1,0:T(8,128)S(1)}, u32[]{:S(2)}, u32[]{:S(2)}) collective-permute-start(f32[8,40,256]{2,1,0:T(8,128)S(1)} %get-tuple-element.166), channel_id=1, source_target_pairs={{0,8},{4,12},{8,0},{12,4},{16,24},{20,28},{24,16},{28,20},{1,9},{5... | collective-permute-start | bytes 983048 | tf_op jit(solution)/shard_map/ppermute | solution.py:680
  55.3 7.1 %collective-permute-start.10 = (f32[4,64,256]{2,1,0:T(8,128)S(1)}, f32[4,64,256]{2,1,0:T(8,128)S(1)}, u32[]{:S(2)}, u32[]{:S(2)}) collective-permute-start(f32[4,64,256]{2,1,0:T(8,128)S(1)} %get-tuple-element.158), channel_id=1, source_target_pairs={{0,1},{1,0},{2,3},{3,2},{4,5},{5,4},{6,7},{7,6},{8,9},{9,8},{10,11... | collective-permute-start | bytes 786440 | tf_op jit(solution)/shard_map/ppermute | solution.py:680
  56.9 12.1 %collective-permute-start.11 = (f32[4,64,256]{2,1,0:T(8,128)S(1)}, f32[4,64,256]{2,1,0:T(8,128)S(1)}, u32[]{:S(2)}, u32[]{:S(2)}) collective-permute-start(f32[4,64,256]{2,1,0:T(8,128)S(1)} %get-tuple-element.159), channel_id=1, source_target_pairs={{0,8},{4,12},{8,0},{12,4},{16,24},{20,28},{24,16},{28,20},{1,9},{5... | collective-permute-start | bytes 786440 | tf_op jit(solution)/shard_map/ppermute | solution.py:680
  58.4 15.5 %collective-permute-start.13 = (f32[8,32,256]{2,1,0:T(8,128)S(1)}, f32[8,32,256]{2,1,0:T(8,128)S(1)}, u32[]{:S(2)}, u32[]{:S(2)}) collective-permute-start(f32[8,32,256]{2,1,0:T(8,128)S(1)} %get-tuple-element.167), channel_id=1, source_target_pairs={{0,16},{4,20},{8,24},{12,28},{16,0},{20,4},{24,8},{28,12},{1,17},{... | collective-permute-start | bytes 786440 | tf_op jit(solution)/shard_map/ppermute | solution.py:680
  69.1 11.0 %collective-permute-start.14 = (f32[2,72,256]{2,1,0:T(8,128)S(1)}, f32[2,72,256]{2,1,0:T(8,128)S(1)}, u32[]{:S(2)}, u32[]{:S(2)}) collective-permute-start(f32[2,72,256]{2,1,0:T(8,128)S(1)} %get-tuple-element.177), channel_id=1, source_target_pairs={{0,1},{1,0},{2,3},{3,2},{4,5},{5,4},{6,7},{7,6},{8,9},{9,8},{10,11... | collective-permute-start | bytes 442376 | tf_op jit(solution)/shard_map/ppermute | solution.py:680
  70.7 5.7 %collective-permute-start.15 = (f32[2,64,256]{2,1,0:T(8,128)S(1)}, f32[2,64,256]{2,1,0:T(8,128)S(1)}, u32[]{:S(2)}, u32[]{:S(2)}) collective-permute-start(f32[2,64,256]{2,1,0:T(8,128)S(1)} %get-tuple-element.178), channel_id=1, source_target_pairs={{0,8},{4,12},{8,0},{12,4},{16,24},{20,28},{24,16},{28,20},{1,9},{5... | collective-permute-start | bytes 393224 | tf_op jit(solution)/shard_map/ppermute | solution.py:680
  71.2 8.9 %collective-permute-start.16 = (f32[2,64,256]{2,1,0:T(8,128)S(1)}, f32[2,64,256]{2,1,0:T(8,128)S(1)}, u32[]{:S(2)}, u32[]{:S(2)}) collective-permute-start(f32[2,64,256]{2,1,0:T(8,128)S(1)} %get-tuple-element.179), channel_id=1, source_target_pairs={{0,2},{1,3},{2,0},{3,1},{4,6},{5,7},{6,4},{7,5},{8,10},{9,11},{10,... | collective-permute-start | bytes 393224 | tf_op jit(solution)/shard_map/ppermute | solution.py:680
  73.9 6.5 %collective-permute-start.17 = (f32[4,40,256]{2,1,0:T(8,128)S(1)}, f32[4,40,256]{2,1,0:T(8,128)S(1)}, u32[]{:S(2)}, u32[]{:S(2)}) collective-permute-start(f32[4,40,256]{2,1,0:T(8,128)S(1)} %get-tuple-element.186), channel_id=1, source_target_pairs={{0,16},{4,20},{8,24},{12,28},{16,0},{20,4},{24,8},{28,12},{1,17},{... | collective-permute-start | bytes 491528 | tf_op jit(solution)/shard_map/ppermute | solution.py:680
  80.2 9.0 %collective-permute-start.19 = (f32[1,136,256]{2,1,0:T(8,128)S(1)}, f32[1,136,256]{2,1,0:T(8,128)S(1)}, u32[]{:S(2)}, u32[]{:S(2)}) collective-permute-start(f32[1,136,256]{2,1,0:T(8,128)S(1)} %get-tuple-element.191), channel_id=1, source_target_pairs={{0,2},{1,3},{2,0},{3,1},{4,6},{5,7},{6,4},{7,5},{8,10},{9,11},{10,... | collective-permute-start | bytes 417800 | tf_op jit(solution)/shard_map/ppermute | solution.py:680
  80.5 8.7 %collective-permute-start.21 = (f32[1,72,256]{2,1,0:T(8,128)S(1)}, f32[1,72,256]{2,1,0:T(8,128)S(1)}, u32[]{:S(2)}, u32[]{:S(2)}) collective-permute-start(f32[1,72,256]{2,1,0:T(8,128)S(1)} %get-tuple-element.198), channel_id=1, source_target_pairs={{0,1},{1,0},{2,3},{3,2},{4,5},{5,4},{6,7},{7,6},{8,9},{9,8},{10,11... | collective-permute-start | bytes 221192 | tf_op jit(solution)/shard_map/ppermute | solution.py:684
  82.0 8.0 %collective-permute-start.22 = (f32[1,72,256]{2,1,0:T(8,128)S(1)}, f32[1,72,256]{2,1,0:T(8,128)S(1)}, u32[]{:S(2)}, u32[]{:S(2)}) collective-permute-start(f32[1,72,256]{2,1,0:T(8,128)S(1)} %get-tuple-element.199), channel_id=1, source_target_pairs={{0,2},{1,3},{2,0},{3,1},{4,6},{5,7},{6,4},{7,5},{8,10},{9,11},{10,... | collective-permute-start | bytes 221192 | tf_op jit(solution)/shard_map/ppermute | solution.py:684
  83.3 6.7 %collective-permute-start.23 = (f32[1,72,256]{2,1,0:T(8,128)S(1)}, f32[1,72,256]{2,1,0:T(8,128)S(1)}, u32[]{:S(2)}, u32[]{:S(2)}) collective-permute-start(f32[1,72,256]{2,1,0:T(8,128)S(1)} %get-tuple-element.200), channel_id=1, source_target_pairs={{0,3},{1,2},{2,1},{3,0},{4,7},{5,6},{6,5},{7,4},{8,11},{9,10},{10,... | collective-permute-start | bytes 221192 | tf_op jit(solution)/shard_map/ppermute | solution.py:684
  91.7 11.8 %collective-permute-start.25 = (f32[1,184,256]{2,1,0:T(8,128)S(1)}, f32[1,184,256]{2,1,0:T(8,128)S(1)}, u32[]{:S(2)}, u32[]{:S(2)}) collective-permute-start(f32[1,184,256]{2,1,0:T(8,128)S(1)} %get-tuple-element.210.refs_0_), channel_id=1, source_target_pairs={{0,2},{1,3},{2,0},{3,1},{4,6},{5,7},{6,4},{7,5},{8,10},{9,11},{10,... | collective-permute-start | bytes 565256 | tf_op jit(solution)/shard_map/ppermute | solution.py:680
  103.5 12.6 %collective-permute-start.27 = (f32[2,96,256]{2,1,0:T(8,128)S(1)}, f32[2,96,256]{2,1,0:T(8,128)S(1)}, u32[]{:S(2)}, u32[]{:S(2)}) collective-permute-start(f32[2,96,256]{2,1,0:T(8,128)S(1)} %get-tuple-element.212.refs_0_), channel_id=1, source_target_pairs={{0,1},{1,0},{2,3},{3,2},{4,5},{5,4},{6,7},{7,6},{8,9},{9,8},{10,11... | collective-permute-start | bytes 589832 | tf_op jit(solution)/shard_map/ppermute | solution.py:680
  103.6 6.2 %collective-permute-start.28 = (f32[2,88,256]{2,1,0:T(8,128)S(1)}, f32[2,88,256]{2,1,0:T(8,128)S(1)}, u32[]{:S(2)}, u32[]{:S(2)}) collective-permute-start(f32[2,88,256]{2,1,0:T(8,128)S(1)} %get-tuple-element.213.refs_1_), channel_id=1, source_target_pairs={{0,8},{4,12},{8,0},{12,4},{16,24},{20,28},{24,16},{28,20},{1,9},{5... | collective-permute-start | bytes 540680 | tf_op jit(solution)/shard_map/ppermute | solution.py:680
  105.5 10.6 %collective-permute-start.29 = (f32[2,88,256]{2,1,0:T(8,128)S(1)}, f32[2,88,256]{2,1,0:T(8,128)S(1)}, u32[]{:S(2)}, u32[]{:S(2)}) collective-permute-start(f32[2,88,256]{2,1,0:T(8,128)S(1)} %get-tuple-element.214.refs_2_), channel_id=1, source_target_pairs={{0,2},{1,3},{2,0},{3,1},{4,6},{5,7},{6,4},{7,5},{8,10},{9,11},{10,... | collective-permute-start | bytes 540680 | tf_op jit(solution)/shard_map/ppermute | solution.py:680
  116.2 9.8 %collective-permute-start.30 = (f32[4,96,256]{2,1,0:T(8,128)S(1)}, f32[4,96,256]{2,1,0:T(8,128)S(1)}, u32[]{:S(2)}, u32[]{:S(2)}) collective-permute-start(f32[4,96,256]{2,1,0:T(8,128)S(1)} %get-tuple-element.215.refs_0_), channel_id=1, source_target_pairs={{0,16},{4,20},{8,24},{12,28},{16,0},{20,4},{24,8},{28,12},{1,17},{... | collective-permute-start | bytes 1179656 | tf_op jit(solution)/shard_map/ppermute | solution.py:680
  116.4 9.0 %collective-permute-start.31 = (f32[4,88,256]{2,1,0:T(8,128)S(1)}, f32[4,88,256]{2,1,0:T(8,128)S(1)}, u32[]{:S(2)}, u32[]{:S(2)}) collective-permute-start(f32[4,88,256]{2,1,0:T(8,128)S(1)} %get-tuple-element.216.refs_1_), channel_id=1, source_target_pairs={{0,1},{1,0},{2,3},{3,2},{4,5},{5,4},{6,7},{7,6},{8,9},{9,8},{10,11... | collective-permute-start | bytes 1081352 | tf_op jit(solution)/shard_map/ppermute | solution.py:680
  116.6 8.8 %collective-permute-start.32 = (f32[4,88,256]{2,1,0:T(8,128)S(1)}, f32[4,88,256]{2,1,0:T(8,128)S(1)}, u32[]{:S(2)}, u32[]{:S(2)}) collective-permute-start(f32[4,88,256]{2,1,0:T(8,128)S(1)} %get-tuple-element.217.refs_2_), channel_id=1, source_target_pairs={{0,8},{4,12},{8,0},{12,4},{16,24},{20,28},{24,16},{28,20},{1,9},{5... | collective-permute-start | bytes 1081352 | tf_op jit(solution)/shard_map/ppermute | solution.py:680
  126.3 5.1 %collective-permute-start.33 = (f32[8,272,256]{2,1,0:T(8,128)S(1)}, f32[8,272,256]{2,1,0:T(8,128)S(1)}, u32[]{:S(2)}, u32[]{:S(2)}) collective-permute-start(f32[8,272,256]{2,1,0:T(8,128)S(1)} %get-tuple-element.218.near_ref), channel_id=1, source_target_pairs={{0,4},{4,0},{8,12},{12,8},{16,20},{20,16},{24,28},{28,24},{1,5},{5... | collective-permute-start | bytes 6684680 | tf_op jit(solution)/shard_map/ppermute | solution.py:680
  126.3 20.0 %collective-permute-start.34 = (f32[8,96,256]{2,1,0:T(8,128)S(1)}, f32[8,96,256]{2,1,0:T(8,128)S(1)}, u32[]{:S(2)}, u32[]{:S(2)}) collective-permute-start(f32[8,96,256]{2,1,0:T(8,128)S(1)} %get-tuple-element.219), channel_id=1, source_target_pairs={{0,8},{4,12},{8,0},{12,4},{16,24},{20,28},{24,16},{28,20},{1,9},{5... | collective-permute-start | bytes 2359304 | tf_op jit(solution)/shard_map/ppermute | solution.py:680
  127.2 18.2 %collective-permute-start.35 = (f32[8,88,256]{2,1,0:T(8,128)S(1)}, f32[8,88,256]{2,1,0:T(8,128)S(1)}, u32[]{:S(2)}, u32[]{:S(2)}) collective-permute-start(f32[8,88,256]{2,1,0:T(8,128)S(1)} %get-tuple-element.220), channel_id=1, source_target_pairs={{0,16},{4,20},{8,24},{12,28},{16,0},{20,4},{24,8},{28,12},{1,17},{... | collective-permute-start | bytes 2162696 | tf_op jit(solution)/shard_map/ppermute | solution.py:680
  128.2 17.9 %collective-permute-start.36 = (f32[8,88,256]{2,1,0:T(8,128)S(1)}, f32[8,88,256]{2,1,0:T(8,128)S(1)}, u32[]{:S(2)}, u32[]{:S(2)}) collective-permute-start(f32[8,88,256]{2,1,0:T(8,128)S(1)} %get-tuple-element.221), channel_id=1, source_target_pairs={{0,1},{1,0},{2,3},{3,2},{4,5},{5,4},{6,7},{7,6},{8,9},{9,8},{10,11... | collective-permute-start | bytes 2162696 | tf_op jit(solution)/shard_map/ppermute | solution.py:680
  (19 other events, 129.7 us)

commit v7 on v6

--- a/solution.py
+++ b/solution.py
@@ -14,7 +14,7 @@
 VMEM = pl.BlockSpec(memory_space=pltpu.VMEM)
 SMEM = pl.BlockSpec(memory_space=pltpu.SMEM)
 PARAMS = pltpu.CompilerParams(vmem_limit_bytes=12 * 1024 * 1024)
-GATHER_PARAMS = pltpu.CompilerParams(vmem_limit_bytes=48 * 1024 * 1024)
+GATHER_PARAMS = pltpu.CompilerParams(vmem_limit_bytes=50 * 1024 * 1024)
 HBM = pl.BlockSpec(memory_space=pltpu.HBM)
 COST = pl.CostEstimate(flops=10000, bytes_accessed=10000, transcendentals=0)
 
@@ -78,11 +78,11 @@
                 out_ref[...] = piece_of(slice(chunk * width - first, (chunk + 1) * width - first))
 
 
-def gather_kernel(hub_steps, rel_steps, spot_ref, hub_idx, rel_idx, hub_sums, rel_sums, hub_ref, rel_ref, *refs):
-    buckets = hub_idx.shape[0]
+def gather_kernel(hub_steps, rel_steps, spot_ref, hub_ids, rel_ids, hub_ref, rel_ref, *refs):
+    buckets = hub_ids.shape[0]
     hub_outs, rel_outs = refs[:buckets], refs[buckets : 2 * buckets]
-    spot_out, hub_own, rel_own, hub_own_sums, rel_own_sums = refs[2 * buckets : 2 * buckets + 5]
-    hub_buf, rel_buf, stacked, sems = refs[2 * buckets + 5 :]
+    spot_out, hub_own, rel_own = refs[2 * buckets : 2 * buckets + 3]
+    hub_buf, rel_buf, hub_idx, rel_idx, stacked, sems = refs[2 * buckets + 3 :]
     hub_tile, rel_tile = hub_buf.shape[2], rel_buf.shape[2]
     chunks = hub_ref.shape[1] // hub_own.shape[1]
     half = hub_own.shape[0]
@@ -92,11 +92,16 @@
         pltpu.make_async_copy(table.at[:, pl.ds(k * tile, tile)], buf.at[k % 2], sems.at[i])
         for i, (table, buf, tile, k) in enumerate(steps)
     ]
-    copies[0].start()
+    id_copies = [
+        pltpu.make_async_copy(ids, out, sems.at[len(copies) + i])
+        for i, (ids, out) in enumerate([(hub_ids, hub_idx), (rel_ids, rel_idx)])
+    ]
+    for copy in [*id_copies, copies[0]]:
+        copy.start()
     spot_out[0] = spot_ref[0]
     spot_out[1] = spot_ref[1]
-    take_owned(spot_ref, chunks, hub_sums.shape[1], 0, lambda lanes: hub_sums[:, lanes], hub_own_sums)
-    take_owned(spot_ref, chunks, rel_sums.shape[1], 0, lambda lanes: rel_sums[:, lanes], rel_own_sums)
+    for copy in id_copies:
+        copy.wait()
     rows = pl.ds(pl.multiple_of(spot_ref[1] * half, 8), half)
     for i, (table, buf, tile, k) in enumerate(steps):
         if i + 1 < len(steps):
@@ -113,7 +118,7 @@
         take_owned(spot_ref, chunks, tile, k * tile, lambda lanes: buf[k % 2, rows, lanes], own)
 
 
-def gather_rows(spot, hub_table, hub_idx, hub_sums, rel_table, rel_idx, rel_sums, chunks):
+def gather_rows(spot, hub_table, hub_idx, rel_table, rel_idx, chunks):
     features = hub_table.shape[0]
     hub_steps, rel_steps = 4, 2
     hub_tile, rel_tile = hub_table.shape[1] // hub_steps, rel_table.shape[1] // rel_steps
@@ -121,22 +126,24 @@
     edges = rel_idx.shape[1]
     hub_width, rel_width = hub_table.shape[1] // chunks, rel_table.shape[1] // chunks
     shapes = [(features, hubs)] * buckets + [(features, edges)] * buckets
-    own_shapes = [(features // 2, hub_width), (features // 2, rel_width), (1, hub_width), (1, rel_width)]
+    own_shapes = [(features // 2, hub_width), (features // 2, rel_width)]
     floats = lambda shapes: [jax.ShapeDtypeStruct(shape, F32) for shape in shapes]
     out = pl.pallas_call(
         functools.partial(gather_kernel, hub_steps, rel_steps),
-        in_specs=[SMEM] + [VMEM] * 4 + [HBM, HBM],
+        in_specs=[SMEM] + [HBM] * 4,
         out_specs=[VMEM] * len(shapes) + [SMEM] + [VMEM] * len(own_shapes),
         out_shape=floats(shapes) + [jax.ShapeDtypeStruct((2,), jnp.int32)] + floats(own_shapes),
         scratch_shapes=[
             pltpu.VMEM((2, features, hub_tile), F32),
             pltpu.VMEM((2, features, rel_tile), F32),
+            pltpu.VMEM(hub_idx.shape, jnp.int32),
+            pltpu.VMEM(rel_idx.shape, jnp.int32),
             pltpu.VMEM((2 * features, max(hub_tile, rel_tile)), BF16),
-            pltpu.SemaphoreType.DMA((hub_steps + rel_steps,)),
+            pltpu.SemaphoreType.DMA((hub_steps + rel_steps + 2,)),
         ],
         compiler_params=GATHER_PARAMS,
         cost_estimate=COST,
-    )(spot, hub_idx, rel_idx, hub_sums, rel_sums, hub_table, rel_table)
+    )(spot, hub_idx, rel_idx, hub_table, rel_table)
     return out[:buckets], out[buckets : 2 * buckets], out[2 * buckets], out[2 * buckets + 1 :]
 
 
@@ -348,10 +355,13 @@
     out[1:2] = jnp.sum(total * total, axis=0, keepdims=True)
 
 
-def update_kernel(spans, rel_spans, pieces, there, features, *refs):
+def update_kernel(spans, rel_spans, pieces, there, features, spot_ref, *refs):
     streams, groups = len(spans), 1 + max(g for g, unused in there)
-    totals, news = refs[:streams], refs[-groups:]
-    rel_total, mine, other, hub_ref, hub_sums, rel_ref, rel_sums = refs[streams:-groups]
+    totals, (hub_sums, rel_sums), news = refs[:streams], refs[-2:], refs[-groups - 2 : -2]
+    rel_total, mine, other, hub_ref, hub_all, rel_ref, rel_all = refs[streams : -groups - 2]
+    chunks = hub_all.shape[1] // hub_ref.shape[1]
+    take_owned(spot_ref, chunks, hub_all.shape[1], 0, lambda lanes: hub_all[:, lanes], hub_sums)
+    take_owned(spot_ref, chunks, rel_all.shape[1], 0, lambda lanes: rel_all[:, lanes], rel_sums)
     width = rel_ref.shape[1]
     squares = mine[...] + other[...]
     hub_scale = step_rate / jnp.sqrt(hub_sums[...] + squares[0:1] * (1.0 / features))
@@ -752,8 +762,7 @@
     spot = jnp.stack([(blk >> 1) * depth + lax.axis_index("sub"), blk & 1]).astype(jnp.int32)
     far_ids = other_core((hub_ids, relations))
     hub_rows, rel_rows, spot, owned = gather_rows(
-        spot, hub_emb.reshape(features, hub_count), hub_ids, hub_state[None],
-        relation_emb.reshape(features, rel_count), relations, relation_state[None], chunks,
+        spot, hub_emb.reshape(features, hub_count), hub_ids, relation_emb.reshape(features, rel_count), relations, chunks
     )
     far_ids, hub_rows = in_turn(far_ids, hub_rows)
     keeps, fars = [], []
@@ -785,10 +794,6 @@
     )
     rel_far = other_core(rel_send)
 
-    rel_keep, got = in_turn(rel_keep, got)
-    send, own = halves(own, got, orders, 0)
-    got = exchanged(send, 1)
-    own, rel_far = in_turn(own, rel_far)
     parts = chunk_columns(
         functools.partial(rel_chunks_kernel, rel_orders, plane_pieces, rel_count),
         [(chunks // 2, height, width) for height in plane_heights * 2],
@@ -796,31 +801,42 @@
     )
     rel_send, rel_own = parts[: len(rel_orders)], parts[len(rel_orders) :]
     rel_got = [across(x, order[0]) for x, order in zip(rel_send, rel_orders)]
-    for step in range(1, stages - 1):
+    plane_steps = stages - sub_bits
+    for step in range(stages - 1):
+        if 0 < step < plane_steps:
+            own, rel_got = in_turn(own, rel_got)
+            rel_send, rel_own = halves(rel_own, rel_got, rel_orders, step - 1)
+            rel_got = [across(x, order[step]) for x, order in zip(rel_send, rel_orders)]
+        elif step == plane_steps:
+            own, rel_got = in_turn(own, rel_got)
+            rel_own, *rel_out = call(
+                functools.partial(z_sums_kernel, plane_spans), [*rel_own, *rel_got],
+                [(1, plane_spans[-1][1], width)] * depth,
+            )
+            rel_got = [flipped_by(x, "sub", q + 1) for q, x in enumerate(rel_out)]
         rel_own, got = in_turn(rel_own, got)
         send, own = halves(own, got, orders, step)
         got = exchanged(send, step + 1)
-        if step < stages - sub_bits:
-            own, rel_got = in_turn(own, rel_got)
-            rel_send, rel_own = halves(rel_own, rel_got, rel_orders, step - 1)
-            rel_got = [across(x, order[step]) for x, order in zip(rel_send, rel_orders)]
-    own, rel_got = in_turn(own, rel_got)
-    rel_own, *rel_out = call(
-        functools.partial(z_sums_kernel, plane_spans), [*rel_own, *rel_got], [(1, plane_spans[-1][1], width)] * depth
-    )
-    rel_got = [flipped_by(x, "sub", q + 1) for q, x in enumerate(rel_out)]
 
     *totals, rel_total, squares = call(
         functools.partial(squares_kernel, heights, grouped(orders, stages - 1, heights)[1]),
         [*own, *got, rel_own, *rel_got], [x.shape for x in own] + [rel_own.shape, (2, width)],
     )
-    hub_own, rel_own, hub_sums, rel_sums = owned
+    hub_own, rel_own = owned
     groups, there = grouped(orders, stages - 1, joint_heights)
-    have = call(
+    ins = [
+        *totals, rel_total, squares, other_core(squares),
+        hub_own, hub_state[None], rel_own, relation_state[None],
+    ]
+    have = pl.pallas_call(
         functools.partial(update_kernel, spans, rel_spans, joint_pieces, there, features),
-        [*totals, rel_total, squares, other_core(squares), hub_own, hub_sums, rel_own, rel_sums],
-        [(1, height, width) for unused, height in groups],
-    )
+        in_specs=[SMEM] + [VMEM] * len(ins),
+        out_specs=[VMEM] * len(groups),
+        out_shape=[jax.ShapeDtypeStruct((1, height, width), F32) for unused, height in groups],
+        scratch_shapes=[pltpu.VMEM((1, x.shape[1]), F32) for x in owned],
+        compiler_params=PARAMS,
+        cost_estimate=COST,
+    )(spot, *ins)
     for step in range(stages - 1, 1, -1):
         have = join(have, exchanged(have, step), orders, step, joint_heights)
     have, near = join_all(have, exchanged(have, 1), orders, 1, joint_heights)

time: 154 us -> 150 us (0.974)
  waiting for transfers between devices: 64.3 us -> 59.2 us
  local copies, waits for them, and re-layouts: 4.39 us -> 1.41 us
  starting transfers between devices: 40.9 us -> 43.7 us
    ppermute x36, waiting for transfers between devices: 63.5 us -> 59.2 us  [flipped(): lax.ppermute(x, axis, [(i, i ^ 1 << bit) for i in range(lax.axis_size(axi...]
    unnamed x22, local copies, waits for them, and re-layouts: 3.69 us -> 1.4 us
    ppermute x3, starting transfers between devices: 4.45 us -> 6.1 us  [flipped_by(): lax.ppermute(x, axis, [(i, i ^ offset) for i in range(lax.axis_size(axis))])]
  transfers between devices with their start and end apart: 40 -> 40, of which waited for: 23 -> 19; matrix products, arithmetic and copies ran while one was open for 1% -> 0% of each run, Pallas kernels for 22% -> 23%
where the time goes in v7:
time: 150 us
  waiting for transfers between devices  59.2 us (39%)
  Pallas kernels  44.1 us (29%)
  starting transfers between devices  43.7 us (29%)
    ppermute x36, waiting for transfers between devices, flipped(): lax.ppermute(x, axis, [(i, i ^ 1 << bit) for i in range(lax.axis_size(axi...  59.2 us
    ppermute x36, starting transfers between devices, flipped(): lax.ppermute(x, axis, [(i, i ^ 1 << bit) for i in range(lax.axis_size(axi...  37.1 us
    pallas_call x1, Pallas kernels, gather_rows(): pl.pallas_call(functools.partial(gather_kernel, hub_steps, rel_steps), in...  11 us
    pallas_call x4, Pallas kernels, placed(): pl.pallas_call(kernel, in_specs=[SMEM] + [VMEM] * (1 + len(fars)) + [HBM]...  9.34 us
    pallas_call x2, Pallas kernels, chunk_columns(): pl.pallas_call(functools.partial(kernel, grad_lanes), in_specs=[SMEM] + [...  7.91 us
    ppermute x3, starting transfers between devices, flipped_by(): lax.ppermute(x, axis, [(i, i ^ offset) for i in range(lax.axis_size(axis))])  6.1 us
    pallas_call x1, Pallas kernels, bucket_step(): pl.pallas_call(functools.partial(bucket_kernel, bucket), in_specs=[SMEM]...  5.66 us
    pallas_call x1, Pallas kernels, tables_step(): pl.pallas_call(functools.partial(tables_kernel, bucket, hubs), in_specs=[...  5.54 us
  transfers between devices with their start and end apart: 40, of which 19 were waited for; matrix products, arithmetic and copies ran while one was open for 0% of the time, Pallas kernels for 23%

profile of v7, /device:TPU:0, one launch (start us, length us, event | category | flops | bytes accessed | tf_op | source)
XLA Modules:
  0.0 149.6 jit_solution(7893340865790447061)
XLA Ops:
  2.7 11.0 %shard_map.156 = (f32[400,256]{1,0:T(8,128)S(1)}, f32[400,256]{1,0:T(8,128)S(1)}, f32[400,512]{1,0:T(8,128)S(1)}, f32[400,512]{1,0:T(8,128)S(1)}, s32[2]{0:T(128...) custom-call(s32[2]{0:T(128)S(1)} %pad_add_fusion.spot_ref, s32[2,256]{1,0:T(2,128)S(1)} %copy-done.7, ...), custom_call_target="tpu_custom_call" | custom-call | flops 10000 | bytes 10000 | tf_op jit(solution)/shard_map/pallas_call | solution.py:131
  13.8 5.7 %shard_map.157 = (f32[400,512]{1,0:T(8,128)S(1)}, f32[1,512]{1,0:T(1,128)S(1)}, f32[408,512]{1,0:T(8,128)S(1)}, f32[200,768]{1,0:T(8,128)S(1)}, f32[200,768]{1,0:T(8,128)S(1)}) custom-call(s32[2]{0:T(128)S(1)} %get-tuple-element.111.core_ref.spot_ref, s32[2,512]{1,0:T(2,128)S(1)} %copy-done.2, s32[2,512]{1,0:T(2,128)S(1)} %copy-done.4, ...), custom_call_target="tpu_custom_call" | custom-call | flops 10000 | bytes 10000 | tf_op jit(solution)/shard_map/pallas_call | solution.py:569
  19.9 2.7 %collective-permute-start.3 = (f32[200,768]{1,0:T(8,128)S(1)}, f32[200,768]{1,0:T(8,128)S(1)}, u32[]{:S(2)}, u32[]{:S(2)}) collective-permute-start(f32[200,768]{1,0:T(8,128)S(1)} %get-tuple-element.127), channel_id=1, source_target_pairs={{0,4},{4,0},{8,12},{12,8},{16,20},{20,16},{24,28},{28,24},{1,5},{5... | collective-permute-start | bytes 1843208 | tf_op jit(solution)/shard_map/ppermute | solution.py:690
  22.6 2.7 %shard_map.158 = (f32[400,512]{1,0:T(8,128)S(1)}, f32[200,256]{1,0:T(8,128)S(1)}, f32[200,256]{1,0:T(8,128)S(1)}) custom-call(s32[2]{0:T(128)S(1)} %get-tuple-element.111.core_ref.spot_ref, s32[2,512]{1,0:T(2,128)S(1)} %copy-done.2, f32[400,512]{1,0:T(8,128)S(1)} %get-tuple-element.116.left_ref, f32[400,512]{1,0:T(8,128)S(1)} %get-tuple-element.117.rel_ref, ...), custom_call_target="tpu_custom_call" | custom-call | flops 10000 | bytes 10000 | tf_op jit(solution)/shard_map/pallas_call | solution.py:616
  26.9 4.3 %shard_map.160 = (f32[8,72,256]{2,1,0:T(8,128)S(1)}, f32[8,64,256]{2,1,0:T(8,128)S(1)}, f32[8,64,256]{2,1,0:T(8,128)S(1)}, f32[8,72,256]{2,1,0:T(8,128)S(1)}, f3...) custom-call(s32[2]{0:T(128)S(1)} %get-tuple-element.111.core_ref.spot_ref, s32[2,256]{1,0:T(2,128)S(1)} %copy-done.7, ...), custom_call_target="tpu_custom_call" | custom-call | flops 10000 | bytes 10000 | tf_op jit(solution)/shard_map/pallas_call | solution.py:269
  32.9 2.0 %collective-permute-start.8 = (f32[8,64,256]{2,1,0:T(8,128)S(1)}, f32[8,64,256]{2,1,0:T(8,128)S(1)}, u32[]{:S(2)}, u32[]{:S(2)}) collective-permute-start(f32[8,64,256]{2,1,0:T(8,128)S(1)} %get-tuple-element.139), channel_id=1, source_target_pairs={{0,1},{1,0},{2,3},{3,2},{4,5},{5,4},{6,7},{7,6},{8,9},{9,8},{10,11... | collective-permute-start | bytes 1572872 | tf_op jit(solution)/shard_map/ppermute | solution.py:690
  34.9 5.5 %shard_map.159 = (f32[400,512]{1,0:T(8,128)}, f32[400,512]{1,0:T(8,128)}, f32[200,512]{1,0:T(8,128)S(1)}, f32[200,512]{1,0:T(8,128)S(1)}) custom-call(s32[2]{0:T(128)S(1)} %get-tuple-element.111.core_ref.spot_ref, s32[2,512]{1,0:T(2,128)S(1)} %copy-done.2, s32[2,512]{1,0:T(2,128)S(1)} %copy-done.4, s32[2,1024]{1,0:T(2,128)S(1)} %copy-done.3, ...), custom_call_target="tpu_custom_call" | custom-call | flops 10000 | bytes 10000 | tf_op jit(solution)/shard_map/pallas_call | solution.py:672
  40.4 1.7 %collective-permute-done.5.refs_5_ = f32[200,512]{1,0:T(8,128)S(1)} collective-permute-done((f32[200,512]{1,0:T(8,128)S(1)}, f32[200,512]{1,0:T(8,128)S(1)}, u32[]{:S(2)}, u32[]{:S(2)}) %collective-permute-start.5) | collective-permute-done | bytes 409632 | tf_op jit(solution)/shard_map/ppermute | solution.py:690
  42.2 3.6 %shard_map.161 = (f32[8,40,256]{2,1,0:T(8,128)S(1)}, f32[8,32,256]{2,1,0:T(8,128)S(1)}, f32[8,40,256]{2,1,0:T(8,128)S(1)}, f32[8,32,256]{2,1,0:T(8,128)S(1)}) custom-call(s32[2]{0:T(128)S(1)} %get-tuple-element.111.core_ref.spot_ref, s32[2,512]{1,0:T(2,128)S(1)} %copy-done.5, s32[2,512]{1,0:T(2,128)S(1)} %collective-permute-done.1.refs_1_, ...), custom_call_target="tpu_custom_call" | custom-call | flops 10000 | bytes 10000 | tf_op jit(solution)/shard_map/pallas_call | solution.py:269
  45.8 1.5 %collective-permute-start.9 = (f32[8,40,256]{2,1,0:T(8,128)S(1)}, f32[8,40,256]{2,1,0:T(8,128)S(1)}, u32[]{:S(2)}, u32[]{:S(2)}) collective-permute-start(f32[8,40,256]{2,1,0:T(8,128)S(1)} %get-tuple-element.146), channel_id=1, source_target_pairs={{0,8},{4,12},{8,0},{12,4},{16,24},{20,28},{24,16},{28,20},{1,9},{5... | collective-permute-start | bytes 983048 | tf_op jit(solution)/shard_map/ppermute | solution.py:690
  50.6 1.5 collective-permute-start.13
  52.1 9.9 %collective-permute-done.10.refs_3_ = f32[8,32,256]{2,1,0:T(8,128)S(1)} collective-permute-done((f32[8,32,256]{2,1,0:T(8,128)S(1)}, f32[8,32,256]{2,1,0:T(8,128)S(1)}, u32[]{:S(2)}, u32[]{:S(2)}) %collective-permute-start.10) | collective-permute-done | bytes 262176 | tf_op jit(solution)/shard_map/ppermute | solution.py:690
  66.2 2.6 %collective-permute-start.18 = (f32[2,64,256]{2,1,0:T(8,128)S(1)}, f32[2,64,256]{2,1,0:T(8,128)S(1)}, u32[]{:S(2)}, u32[]{:S(2)}) collective-permute-start(f32[2,64,256]{2,1,0:T(8,128)S(1)} %get-tuple-element.178), channel_id=1, source_target_pairs={{0,2},{1,3},{2,0},{3,1},{4,6},{5,7},{6,4},{7,5},{8,10},{9,11},{10,... | collective-permute-start | bytes 393224 | tf_op jit(solution)/shard_map/ppermute | solution.py:690
  70.5 3.2 %collective-permute-done.18.refs_5_ = f32[2,64,256]{2,1,0:T(8,128)S(1)} collective-permute-done((f32[2,64,256]{2,1,0:T(8,128)S(1)}, f32[2,64,256]{2,1,0:T(8,128)S(1)}, u32[]{:S(2)}, u32[]{:S(2)}) %collective-permute-start.18) | collective-permute-done | bytes 131104 | tf_op jit(solution)/shard_map/ppermute | solution.py:690
  74.8 3.7 %collective-permute-start.21 = (f32[1,72,256]{2,1,0:T(8,128)S(1)}, f32[1,72,256]{2,1,0:T(8,128)S(1)}, u32[]{:S(2)}, u32[]{:S(2)}) collective-permute-start(f32[1,72,256]{2,1,0:T(8,128)S(1)} %get-tuple-element.188), channel_id=1, source_target_pairs={{0,1},{1,0},{2,3},{3,2},{4,5},{5,4},{6,7},{7,6},{8,9},{9,8},{10,11... | collective-permute-start | bytes 221192 | tf_op jit(solution)/shard_map/ppermute | solution.py:694
  78.6 2.3 %collective-permute-start.23 = (f32[1,72,256]{2,1,0:T(8,128)S(1)}, f32[1,72,256]{2,1,0:T(8,128)S(1)}, u32[]{:S(2)}, u32[]{:S(2)}) collective-permute-start(f32[1,72,256]{2,1,0:T(8,128)S(1)} %get-tuple-element.190), channel_id=1, source_target_pairs={{0,3},{1,2},{2,1},{3,0},{4,7},{5,6},{6,5},{7,4},{8,11},{9,10},{10,... | collective-permute-start | bytes 221192 | tf_op jit(solution)/shard_map/ppermute | solution.py:694
  80.9 2.0 %collective-permute-start.20 = (f32[1,64,256]{2,1,0:T(8,128)S(1)}, f32[1,64,256]{2,1,0:T(8,128)S(1)}, u32[]{:S(2)}, u32[]{:S(2)}) collective-permute-start(f32[1,64,256]{2,1,0:T(8,128)S(1)} %get-tuple-element.186), channel_id=1, source_target_pairs={{0,16},{4,20},{8,24},{12,28},{16,0},{20,4},{24,8},{28,12},{1,17},{... | collective-permute-start | bytes 196616 | tf_op jit(solution)/shard_map/ppermute | solution.py:690
  82.9 2.2 %collective-permute-done.20.refs_4_ = f32[1,64,256]{2,1,0:T(8,128)S(1)} collective-permute-done((f32[1,64,256]{2,1,0:T(8,128)S(1)}, f32[1,64,256]{2,1,0:T(8,128)S(1)}, u32[]{:S(2)}, u32[]{:S(2)}) %collective-permute-start.20) | collective-permute-done | bytes 65568 | tf_op jit(solution)/shard_map/ppermute | solution.py:690
  87.6 2.5 %collective-permute-start.25 = (f32[1,184,256]{2,1,0:T(8,128)S(1)}, f32[1,184,256]{2,1,0:T(8,128)S(1)}, u32[]{:S(2)}, u32[]{:S(2)}) collective-permute-start(f32[1,184,256]{2,1,0:T(8,128)S(1)} %get-tuple-element.198.refs_0_), channel_id=1, source_target_pairs={{0,2},{1,3},{2,0},{3,1},{4,6},{5,7},{6,4},{7,5},{8,10},{9,11},{10,... | collective-permute-start | bytes 565256 | tf_op jit(solution)/shard_map/ppermute | solution.py:690
  91.5 3.1 %collective-permute-done.26.refs_3_ = f32[1,88,256]{2,1,0:T(8,128)S(1)} collective-permute-done((f32[1,88,256]{2,1,0:T(8,128)S(1)}, f32[1,88,256]{2,1,0:T(8,128)S(1)}, u32[]{:S(2)}, u32[]{:S(2)}) %collective-permute-start.26) | collective-permute-done | bytes 90144 | tf_op jit(solution)/shard_map/ppermute | solution.py:690
  94.6 4.8 %collective-permute-done.25.refs_2_ = f32[1,184,256]{2,1,0:T(8,128)S(1)} collective-permute-done((f32[1,184,256]{2,1,0:T(8,128)S(1)}, f32[1,184,256]{2,1,0:T(8,128)S(1)}, u32[]{:S(2)}, u32[]{:S(2)}) %collective-permute-start.25) | collective-permute-done | bytes 188448 | tf_op jit(solution)/shard_map/ppermute | solution.py:690
  99.5 2.2 %collective-permute-start.28 = (f32[2,88,256]{2,1,0:T(8,128)S(1)}, f32[2,88,256]{2,1,0:T(8,128)S(1)}, u32[]{:S(2)}, u32[]{:S(2)}) collective-permute-start(f32[2,88,256]{2,1,0:T(8,128)S(1)} %get-tuple-element.201.refs_1_), channel_id=1, source_target_pairs={{0,8},{4,12},{8,0},{12,4},{16,24},{20,28},{24,16},{28,20},{1,9},{5... | collective-permute-start | bytes 540680 | tf_op jit(solution)/shard_map/ppermute | solution.py:690
  101.8 2.5 %collective-permute-start.29 = (f32[2,88,256]{2,1,0:T(8,128)S(1)}, f32[2,88,256]{2,1,0:T(8,128)S(1)}, u32[]{:S(2)}, u32[]{:S(2)}) collective-permute-start(f32[2,88,256]{2,1,0:T(8,128)S(1)} %get-tuple-element.202.refs_2_), channel_id=1, source_target_pairs={{0,2},{1,3},{2,0},{3,1},{4,6},{5,7},{6,4},{7,5},{8,10},{9,11},{10,... | collective-permute-start | bytes 540680 | tf_op jit(solution)/shard_map/ppermute | solution.py:690
  104.2 1.8 %collective-permute-done.28.refs_4_ = f32[2,88,256]{2,1,0:T(8,128)S(1)} collective-permute-done((f32[2,88,256]{2,1,0:T(8,128)S(1)}, f32[2,88,256]{2,1,0:T(8,128)S(1)}, u32[]{:S(2)}, u32[]{:S(2)}) %collective-permute-start.28) | collective-permute-done | bytes 180256 | tf_op jit(solution)/shard_map/ppermute | solution.py:690
  106.0 6.3 %collective-permute-done.29.refs_5_ = f32[2,88,256]{2,1,0:T(8,128)S(1)} collective-permute-done((f32[2,88,256]{2,1,0:T(8,128)S(1)}, f32[2,88,256]{2,1,0:T(8,128)S(1)}, u32[]{:S(2)}, u32[]{:S(2)}) %collective-permute-start.29) | collective-permute-done | bytes 180256 | tf_op jit(solution)/shard_map/ppermute | solution.py:690
  112.7 1.6 %collective-permute-start.32 = (f32[4,88,256]{2,1,0:T(8,128)S(1)}, f32[4,88,256]{2,1,0:T(8,128)S(1)}, u32[]{:S(2)}, u32[]{:S(2)}) collective-permute-start(f32[4,88,256]{2,1,0:T(8,128)S(1)} %get-tuple-element.205.refs_2_), channel_id=1, source_target_pairs={{0,8},{4,12},{8,0},{12,4},{16,24},{20,28},{24,16},{28,20},{1,9},{5... | collective-permute-start | bytes 1081352 | tf_op jit(solution)/shard_map/ppermute | solution.py:690
  114.3 7.2 %collective-permute-done.31.refs_4_ = f32[4,88,256]{2,1,0:T(8,128)S(1)} collective-permute-done((f32[4,88,256]{2,1,0:T(8,128)S(1)}, f32[4,88,256]{2,1,0:T(8,128)S(1)}, u32[]{:S(2)}, u32[]{:S(2)}) %collective-permute-start.31) | collective-permute-done | bytes 360480 | tf_op jit(solution)/shard_map/ppermute | solution.py:690
  125.6 1.9 %shard_map.172.refs_0_ = f32[2,200,4096]{2,1,0:T(8,128)} custom-call(s32[2]{0:T(128)S(1)} %get-tuple-element.111.core_ref.spot_ref, f32[8,272,256]{2,1,0:T(8,128)S(1)} %get-tuple-element.206.near_ref), custom_call_target="tpu_custom_call" | custom-call | bytes 3276800 | tf_op jit(solution)/shard_map/pallas_call | solution.py:470
  127.5 1.9 %shard_map.173.refs_3_ = f32[2,200,4096]{2,1,0:T(8,128)} custom-call(s32[2]{0:T(128)S(1)} %get-tuple-element.111.core_ref.spot_ref, f32[8,272,256]{2,1,0:T(8,128)S(1)} %collective-permute-done.33.near_ref, f32[2,200,4096]{2,1,0:T(8,128)} %shard_map.172.refs_0_), custom_call_target="tpu_custom_call", output_to_operand_aliasing={{}: (2, {})} | custom-call | bytes 3276800 | tf_op jit(solution)/shard_map/pallas_call | solution.py:470
  129.4 12.1 %collective-permute-done.35.refs_1_ = f32[8,88,256]{2,1,0:T(8,128)S(1)} collective-permute-done((f32[8,88,256]{2,1,0:T(8,128)S(1)}, f32[8,88,256]{2,1,0:T(8,128)S(1)}, u32[]{:S(2)}, u32[]{:S(2)}) %collective-permute-start.35) | collective-permute-done | bytes 720928 | tf_op jit(solution)/shard_map/ppermute | solution.py:690
  142.9 2.7 %shard_map.174 = (f32[2,200,4096]{2,1,0:T(8,128)}, f32[2,200,1280]{2,1,0:T(8,128)}) custom-call(s32[2]{0:T(128)S(1)} %get-tuple-element.111.core_ref.spot_ref, f32[8,272,256]{2,1,0:T(8,128)S(1)} %get-tuple-element.206.near_ref, f32[8,96,256]{2,1,0:T(8,128)S(1)} %collective-permute-done.34.refs_0_, ...), custom_call_target="tpu_custom_call", output_to_operand_aliasing={{0}: (5, {})} | custom-call | bytes 3276800 | tf_op jit(solution)/shard_map/pallas_call | solution.py:470
  146.7 2.8 %shard_map.175 = (f32[2,200,4096]{2,1,0:T(8,128)}, f32[2,200,1280]{2,1,0:T(8,128)}) custom-call(s32[2]{0:T(128)S(1)} %get-tuple-element.111.core_ref.spot_ref, f32[8,272,256]{2,1,0:T(8,128)S(1)} %collective-permute-done.33.near_ref, f32[8,96,256]{2,1,0:T(8,128)S(1)} %collective-permute-done.37.refs_0_, ...), custom_call_target="tpu_custom_call", output_to_operand_aliasing={{0}: (5, {}), {1}: (6, {})} | custom-call | bytes 3276800 | tf_op jit(solution)/shard_map/pallas_call | solution.py:470
  (92 shorter events, 26.9 us)
Async XLA Ops:
  0.7 13.0 %collective-permute-start = (s32[2,256]{1,0:T(2,128)}, s32[2,256]{1,0:T(2,128)S(1)}, u32[]{:S(2)}, u32[]{:S(2)}) collective-permute-start(s32[2,256]{1,0:T(2,128)} %refs_0_.2), channel_id=1, source_target_pairs={{0,4},{4,0},{8,12},{12,8},{16,20},{20,16},{24,28},{28,24},{1,5},{5... | collective-permute-start | bytes 6152 | tf_op jit(solution)/shard_map/ppermute | solution.py:690
  1.2 12.5 %collective-permute-start.1 = (s32[2,512]{1,0:T(2,128)}, s32[2,512]{1,0:T(2,128)S(1)}, u32[]{:S(2)}, u32[]{:S(2)}) collective-permute-start(s32[2,512]{1,0:T(2,128)} %refs_0_.3), channel_id=1, source_target_pairs={{0,4},{4,0},{8,12},{12,8},{16,20},{20,16},{24,28},{28,24},{1,5},{5... | collective-permute-start | bytes 12296 | tf_op jit(solution)/shard_map/ppermute | solution.py:690
  19.5 15.4 %collective-permute-start.2 = (f32[408,512]{1,0:T(8,128)S(1)}, f32[408,512]{1,0:T(8,128)S(1)}, u32[]{:S(2)}, u32[]{:S(2)}) collective-permute-start(f32[408,512]{1,0:T(8,128)S(1)} %get-tuple-element.121), channel_id=1, source_target_pairs={{0,4},{4,8},{8,12},{12,16},{16,20},{20,24},{24,28},{28,0},{1,5},{5... | collective-permute-start | bytes 2506760 | tf_op jit(solution)/shard_map/ppermute | solution.py:686
  19.9 6.9 %collective-permute-start.3 = (f32[200,768]{1,0:T(8,128)S(1)}, f32[200,768]{1,0:T(8,128)S(1)}, u32[]{:S(2)}, u32[]{:S(2)}) collective-permute-start(f32[200,768]{1,0:T(8,128)S(1)} %get-tuple-element.127), channel_id=1, source_target_pairs={{0,4},{4,0},{8,12},{12,8},{16,20},{20,16},{24,28},{28,24},{1,5},{5... | collective-permute-start | bytes 1843208 | tf_op jit(solution)/shard_map/ppermute | solution.py:690
  31.2 16.1 %collective-permute-start.6 = (f32[8,72,256]{2,1,0:T(8,128)S(1)}, f32[8,72,256]{2,1,0:T(8,128)S(1)}, u32[]{:S(2)}, u32[]{:S(2)}) collective-permute-start(f32[8,72,256]{2,1,0:T(8,128)S(1)} %get-tuple-element.137), channel_id=1, source_target_pairs={{0,8},{4,12},{8,0},{12,4},{16,24},{20,28},{24,16},{28,20},{1,9},{5... | collective-permute-start | bytes 1769480 | tf_op jit(solution)/shard_map/ppermute | solution.py:690
  32.6 14.7 %collective-permute-start.7 = (f32[8,64,256]{2,1,0:T(8,128)S(1)}, f32[8,64,256]{2,1,0:T(8,128)S(1)}, u32[]{:S(2)}, u32[]{:S(2)}) collective-permute-start(f32[8,64,256]{2,1,0:T(8,128)S(1)} %get-tuple-element.138), channel_id=1, source_target_pairs={{0,16},{4,20},{8,24},{12,28},{16,0},{20,4},{24,8},{28,12},{1,17},{... | collective-permute-start | bytes 1572872 | tf_op jit(solution)/shard_map/ppermute | solution.py:690
  32.9 14.4 %collective-permute-start.8 = (f32[8,64,256]{2,1,0:T(8,128)S(1)}, f32[8,64,256]{2,1,0:T(8,128)S(1)}, u32[]{:S(2)}, u32[]{:S(2)}) collective-permute-start(f32[8,64,256]{2,1,0:T(8,128)S(1)} %get-tuple-element.139), channel_id=1, source_target_pairs={{0,1},{1,0},{2,3},{3,2},{4,5},{5,4},{6,7},{7,6},{8,9},{9,8},{10,11... | collective-permute-start | bytes 1572872 | tf_op jit(solution)/shard_map/ppermute | solution.py:690
  45.8 16.2 %collective-permute-start.9 = (f32[8,40,256]{2,1,0:T(8,128)S(1)}, f32[8,40,256]{2,1,0:T(8,128)S(1)}, u32[]{:S(2)}, u32[]{:S(2)}) collective-permute-start(f32[8,40,256]{2,1,0:T(8,128)S(1)} %get-tuple-element.146), channel_id=1, source_target_pairs={{0,8},{4,12},{8,0},{12,4},{16,24},{20,28},{24,16},{28,20},{1,9},{5... | collective-permute-start | bytes 983048 | tf_op jit(solution)/shard_map/ppermute | solution.py:690
  47.5 15.1 %collective-permute-start.11 = (f32[4,72,256]{2,1,0:T(8,128)S(1)}, f32[4,72,256]{2,1,0:T(8,128)S(1)}, u32[]{:S(2)}, u32[]{:S(2)}) collective-permute-start(f32[4,72,256]{2,1,0:T(8,128)S(1)} %get-tuple-element.157), channel_id=1, source_target_pairs={{0,16},{4,20},{8,24},{12,28},{16,0},{20,4},{24,8},{28,12},{1,17},{... | collective-permute-start | bytes 884744 | tf_op jit(solution)/shard_map/ppermute | solution.py:690
  48.4 13.6 %collective-permute-start.10 = (f32[8,32,256]{2,1,0:T(8,128)S(1)}, f32[8,32,256]{2,1,0:T(8,128)S(1)}, u32[]{:S(2)}, u32[]{:S(2)}) collective-permute-start(f32[8,32,256]{2,1,0:T(8,128)S(1)} %get-tuple-element.147), channel_id=1, source_target_pairs={{0,16},{4,20},{8,24},{12,28},{16,0},{20,4},{24,8},{28,12},{1,17},{... | collective-permute-start | bytes 786440 | tf_op jit(solution)/shard_map/ppermute | solution.py:690
  49.6 13.0 %collective-permute-start.12 = (f32[4,64,256]{2,1,0:T(8,128)S(1)}, f32[4,64,256]{2,1,0:T(8,128)S(1)}, u32[]{:S(2)}, u32[]{:S(2)}) collective-permute-start(f32[4,64,256]{2,1,0:T(8,128)S(1)} %get-tuple-element.158), channel_id=1, source_target_pairs={{0,1},{1,0},{2,3},{3,2},{4,5},{5,4},{6,7},{7,6},{8,9},{9,8},{10,11... | collective-permute-start | bytes 786440 | tf_op jit(solution)/shard_map/ppermute | solution.py:690
  50.6 12.1 %collective-permute-start.13 = (f32[4,64,256]{2,1,0:T(8,128)S(1)}, f32[4,64,256]{2,1,0:T(8,128)S(1)}, u32[]{:S(2)}, u32[]{:S(2)}) collective-permute-start(f32[4,64,256]{2,1,0:T(8,128)S(1)} %get-tuple-element.159), channel_id=1, source_target_pairs={{0,8},{4,12},{8,0},{12,4},{16,24},{20,28},{24,16},{28,20},{1,9},{5... | collective-permute-start | bytes 786440 | tf_op jit(solution)/shard_map/ppermute | solution.py:690
  62.1 7.0 %collective-permute-start.14 = (f32[4,40,256]{2,1,0:T(8,128)S(1)}, f32[4,40,256]{2,1,0:T(8,128)S(1)}, u32[]{:S(2)}, u32[]{:S(2)}) collective-permute-start(f32[4,40,256]{2,1,0:T(8,128)S(1)} %get-tuple-element.166), channel_id=1, source_target_pairs={{0,16},{4,20},{8,24},{12,28},{16,0},{20,4},{24,8},{28,12},{1,17},{... | collective-permute-start | bytes 491528 | tf_op jit(solution)/shard_map/ppermute | solution.py:690
  62.7 10.9 %collective-permute-start.16 = (f32[2,72,256]{2,1,0:T(8,128)S(1)}, f32[2,72,256]{2,1,0:T(8,128)S(1)}, u32[]{:S(2)}, u32[]{:S(2)}) collective-permute-start(f32[2,72,256]{2,1,0:T(8,128)S(1)} %get-tuple-element.176), channel_id=1, source_target_pairs={{0,1},{1,0},{2,3},{3,2},{4,5},{5,4},{6,7},{7,6},{8,9},{9,8},{10,11... | collective-permute-start | bytes 442376 | tf_op jit(solution)/shard_map/ppermute | solution.py:690
  64.1 5.0 %collective-permute-start.15 = (f32[4,32,256]{2,1,0:T(8,128)S(1)}, f32[4,32,256]{2,1,0:T(8,128)S(1)}, u32[]{:S(2)}, u32[]{:S(2)}) collective-permute-start(f32[4,32,256]{2,1,0:T(8,128)S(1)} %get-tuple-element.167), channel_id=1, source_target_pairs={{0,8},{4,12},{8,0},{12,4},{16,24},{20,28},{24,16},{28,20},{1,9},{5... | collective-permute-start | bytes 393224 | tf_op jit(solution)/shard_map/ppermute | solution.py:690
  64.9 5.6 %collective-permute-start.17 = (f32[2,64,256]{2,1,0:T(8,128)S(1)}, f32[2,64,256]{2,1,0:T(8,128)S(1)}, u32[]{:S(2)}, u32[]{:S(2)}) collective-permute-start(f32[2,64,256]{2,1,0:T(8,128)S(1)} %get-tuple-element.177), channel_id=1, source_target_pairs={{0,8},{4,12},{8,0},{12,4},{16,24},{20,28},{24,16},{28,20},{1,9},{5... | collective-permute-start | bytes 393224 | tf_op jit(solution)/shard_map/ppermute | solution.py:690
  66.2 7.5 %collective-permute-start.18 = (f32[2,64,256]{2,1,0:T(8,128)S(1)}, f32[2,64,256]{2,1,0:T(8,128)S(1)}, u32[]{:S(2)}, u32[]{:S(2)}) collective-permute-start(f32[2,64,256]{2,1,0:T(8,128)S(1)} %get-tuple-element.178), channel_id=1, source_target_pairs={{0,2},{1,3},{2,0},{3,1},{4,6},{5,7},{6,4},{7,5},{8,10},{9,11},{10,... | collective-permute-start | bytes 393224 | tf_op jit(solution)/shard_map/ppermute | solution.py:690
  73.7 11.5 %collective-permute-start.19 = (f32[1,136,256]{2,1,0:T(8,128)S(1)}, f32[1,136,256]{2,1,0:T(8,128)S(1)}, u32[]{:S(2)}, u32[]{:S(2)}) collective-permute-start(f32[1,136,256]{2,1,0:T(8,128)S(1)} %get-tuple-element.185), channel_id=1, source_target_pairs={{0,2},{1,3},{2,0},{3,1},{4,6},{5,7},{6,4},{7,5},{8,10},{9,11},{10,... | collective-permute-start | bytes 417800 | tf_op jit(solution)/shard_map/ppermute | solution.py:690
  74.8 10.4 %collective-permute-start.21 = (f32[1,72,256]{2,1,0:T(8,128)S(1)}, f32[1,72,256]{2,1,0:T(8,128)S(1)}, u32[]{:S(2)}, u32[]{:S(2)}) collective-permute-start(f32[1,72,256]{2,1,0:T(8,128)S(1)} %get-tuple-element.188), channel_id=1, source_target_pairs={{0,1},{1,0},{2,3},{3,2},{4,5},{5,4},{6,7},{7,6},{8,9},{9,8},{10,11... | collective-permute-start | bytes 221192 | tf_op jit(solution)/shard_map/ppermute | solution.py:694
  78.5 6.6 %collective-permute-start.22 = (f32[1,72,256]{2,1,0:T(8,128)S(1)}, f32[1,72,256]{2,1,0:T(8,128)S(1)}, u32[]{:S(2)}, u32[]{:S(2)}) collective-permute-start(f32[1,72,256]{2,1,0:T(8,128)S(1)} %get-tuple-element.189), channel_id=1, source_target_pairs={{0,2},{1,3},{2,0},{3,1},{4,6},{5,7},{6,4},{7,5},{8,10},{9,11},{10,... | collective-permute-start | bytes 221192 | tf_op jit(solution)/shard_map/ppermute | solution.py:694
  78.6 6.6 %collective-permute-start.23 = (f32[1,72,256]{2,1,0:T(8,128)S(1)}, f32[1,72,256]{2,1,0:T(8,128)S(1)}, u32[]{:S(2)}, u32[]{:S(2)}) collective-permute-start(f32[1,72,256]{2,1,0:T(8,128)S(1)} %get-tuple-element.190), channel_id=1, source_target_pairs={{0,3},{1,2},{2,1},{3,0},{4,7},{5,6},{6,5},{7,4},{8,11},{9,10},{10,... | collective-permute-start | bytes 221192 | tf_op jit(solution)/shard_map/ppermute | solution.py:694
  87.6 11.8 %collective-permute-start.25 = (f32[1,184,256]{2,1,0:T(8,128)S(1)}, f32[1,184,256]{2,1,0:T(8,128)S(1)}, u32[]{:S(2)}, u32[]{:S(2)}) collective-permute-start(f32[1,184,256]{2,1,0:T(8,128)S(1)} %get-tuple-element.198.refs_0_), channel_id=1, source_target_pairs={{0,2},{1,3},{2,0},{3,1},{4,6},{5,7},{6,4},{7,5},{8,10},{9,11},{10,... | collective-permute-start | bytes 565256 | tf_op jit(solution)/shard_map/ppermute | solution.py:690
  99.5 12.8 %collective-permute-start.27 = (f32[2,96,256]{2,1,0:T(8,128)S(1)}, f32[2,96,256]{2,1,0:T(8,128)S(1)}, u32[]{:S(2)}, u32[]{:S(2)}) collective-permute-start(f32[2,96,256]{2,1,0:T(8,128)S(1)} %get-tuple-element.200.refs_0_), channel_id=1, source_target_pairs={{0,1},{1,0},{2,3},{3,2},{4,5},{5,4},{6,7},{7,6},{8,9},{9,8},{10,11... | collective-permute-start | bytes 589832 | tf_op jit(solution)/shard_map/ppermute | solution.py:690
  99.5 6.4 %collective-permute-start.28 = (f32[2,88,256]{2,1,0:T(8,128)S(1)}, f32[2,88,256]{2,1,0:T(8,128)S(1)}, u32[]{:S(2)}, u32[]{:S(2)}) collective-permute-start(f32[2,88,256]{2,1,0:T(8,128)S(1)} %get-tuple-element.201.refs_1_), channel_id=1, source_target_pairs={{0,8},{4,12},{8,0},{12,4},{16,24},{20,28},{24,16},{28,20},{1,9},{5... | collective-permute-start | bytes 540680 | tf_op jit(solution)/shard_map/ppermute | solution.py:690
  101.8 10.5 %collective-permute-start.29 = (f32[2,88,256]{2,1,0:T(8,128)S(1)}, f32[2,88,256]{2,1,0:T(8,128)S(1)}, u32[]{:S(2)}, u32[]{:S(2)}) collective-permute-start(f32[2,88,256]{2,1,0:T(8,128)S(1)} %get-tuple-element.202.refs_2_), channel_id=1, source_target_pairs={{0,2},{1,3},{2,0},{3,1},{4,6},{5,7},{6,4},{7,5},{8,10},{9,11},{10,... | collective-permute-start | bytes 540680 | tf_op jit(solution)/shard_map/ppermute | solution.py:690
  112.3 9.7 %collective-permute-start.30 = (f32[4,96,256]{2,1,0:T(8,128)S(1)}, f32[4,96,256]{2,1,0:T(8,128)S(1)}, u32[]{:S(2)}, u32[]{:S(2)}) collective-permute-start(f32[4,96,256]{2,1,0:T(8,128)S(1)} %get-tuple-element.203.refs_0_), channel_id=1, source_target_pairs={{0,16},{4,20},{8,24},{12,28},{16,0},{20,4},{24,8},{28,12},{1,17},{... | collective-permute-start | bytes 1179656 | tf_op jit(solution)/shard_map/ppermute | solution.py:690
  112.6 8.8 %collective-permute-start.31 = (f32[4,88,256]{2,1,0:T(8,128)S(1)}, f32[4,88,256]{2,1,0:T(8,128)S(1)}, u32[]{:S(2)}, u32[]{:S(2)}) collective-permute-start(f32[4,88,256]{2,1,0:T(8,128)S(1)} %get-tuple-element.204.refs_1_), channel_id=1, source_target_pairs={{0,1},{1,0},{2,3},{3,2},{4,5},{5,4},{6,7},{7,6},{8,9},{9,8},{10,11... | collective-permute-start | bytes 1081352 | tf_op jit(solution)/shard_map/ppermute | solution.py:690
  112.7 8.8 %collective-permute-start.32 = (f32[4,88,256]{2,1,0:T(8,128)S(1)}, f32[4,88,256]{2,1,0:T(8,128)S(1)}, u32[]{:S(2)}, u32[]{:S(2)}) collective-permute-start(f32[4,88,256]{2,1,0:T(8,128)S(1)} %get-tuple-element.205.refs_2_), channel_id=1, source_target_pairs={{0,8},{4,12},{8,0},{12,4},{16,24},{20,28},{24,16},{28,20},{1,9},{5... | collective-permute-start | bytes 1081352 | tf_op jit(solution)/shard_map/ppermute | solution.py:690
  122.3 5.1 %collective-permute-start.33 = (f32[8,272,256]{2,1,0:T(8,128)S(1)}, f32[8,272,256]{2,1,0:T(8,128)S(1)}, u32[]{:S(2)}, u32[]{:S(2)}) collective-permute-start(f32[8,272,256]{2,1,0:T(8,128)S(1)} %get-tuple-element.206.near_ref), channel_id=1, source_target_pairs={{0,4},{4,0},{8,12},{12,8},{16,20},{20,16},{24,28},{28,24},{1,5},{5... | collective-permute-start | bytes 6684680 | tf_op jit(solution)/shard_map/ppermute | solution.py:690
  122.4 20.0 %collective-permute-start.34 = (f32[8,96,256]{2,1,0:T(8,128)S(1)}, f32[8,96,256]{2,1,0:T(8,128)S(1)}, u32[]{:S(2)}, u32[]{:S(2)}) collective-permute-start(f32[8,96,256]{2,1,0:T(8,128)S(1)} %get-tuple-element.207), channel_id=1, source_target_pairs={{0,8},{4,12},{8,0},{12,4},{16,24},{20,28},{24,16},{28,20},{1,9},{5... | collective-permute-start | bytes 2359304 | tf_op jit(solution)/shard_map/ppermute | solution.py:690
  123.3 18.2 %collective-permute-start.35 = (f32[8,88,256]{2,1,0:T(8,128)S(1)}, f32[8,88,256]{2,1,0:T(8,128)S(1)}, u32[]{:S(2)}, u32[]{:S(2)}) collective-permute-start(f32[8,88,256]{2,1,0:T(8,128)S(1)} %get-tuple-element.208), channel_id=1, source_target_pairs={{0,16},{4,20},{8,24},{12,28},{16,0},{20,4},{24,8},{28,12},{1,17},{... | collective-permute-start | bytes 2162696 | tf_op jit(solution)/shard_map/ppermute | solution.py:690
  124.3 17.9 %collective-permute-start.36 = (f32[8,88,256]{2,1,0:T(8,128)S(1)}, f32[8,88,256]{2,1,0:T(8,128)S(1)}, u32[]{:S(2)}, u32[]{:S(2)}) collective-permute-start(f32[8,88,256]{2,1,0:T(8,128)S(1)} %get-tuple-element.209), channel_id=1, source_target_pairs={{0,1},{1,0},{2,3},{3,2},{4,5},{5,4},{6,7},{7,6},{8,9},{9,8},{10,11... | collective-permute-start | bytes 2162696 | tf_op jit(solution)/shard_map/ppermute | solution.py:690
  (19 other events, 215.9 us)

commit v8 on v7

--- a/solution.py
+++ b/solution.py
@@ -59,9 +59,13 @@
     return both[:half] + (both[half:] + dot(stacked[:half], b[1], dims))
 
 
+def hot_where(here):
+    return jnp.where(here, jnp.ones((), BF16), jnp.zeros((), BF16))
+
+
 def onehot(first, rows, idx):
-    place = lax.broadcasted_iota(jnp.int32, (rows, idx.shape[1]), 0) + first
-    return jnp.where(place == idx, 1.0, 0.0).astype(BF16)
+    place = lax.broadcasted_iota(jnp.int16, (rows, idx.shape[1]), 0)
+    return hot_where(place == (idx - first).astype(jnp.int16))
 
 
 def laid_out(idx):
@@ -159,7 +163,7 @@
 
 def load_columns(id_refs, grad_refs, idx_down, stacked):
     idx = jnp.concatenate([laid_out(ref[...]) for ref in id_refs], axis=1)
-    idx_down[...] = jnp.transpose(jnp.broadcast_to(idx, (128, idx.shape[1])))
+    idx_down[...] = jnp.transpose(jnp.broadcast_to(idx, (128, idx.shape[1]))).astype(jnp.int16)
     at = 0
     for ref, (low, high) in grad_refs:
         width = high - low
@@ -171,7 +175,7 @@
     width = targets.shape[1]
     idx = idx_down[...]
     wide = jnp.concatenate([idx] * -(-width // 128), axis=1)[:, :width]
-    return jnp.where(wide == targets, 1.0, 0.0).astype(BF16)
+    return hot_where(wide == targets.astype(jnp.int16))
 
 
 def grouped(orders, step, heights):
@@ -272,7 +276,7 @@
         out_specs=[VMEM] * len(shapes),
         out_shape=[jax.ShapeDtypeStruct(shape, F32) for shape in shapes],
         scratch_shapes=[
-            pltpu.VMEM((count, 128), jnp.int32),
+            pltpu.VMEM((count, 128), jnp.int16),
             pltpu.VMEM((2 * (-(-half_width // 16) * 16), count), BF16),
         ],
         compiler_params=PARAMS,
@@ -506,14 +510,10 @@
 EDGE_TILE = 512
 
 
-def edge_span(step):
-    return pl.ds(pl.multiple_of(step * EDGE_TILE, EDGE_TILE), EDGE_TILE)
-
-
 def bucket_kernel(
     bucket, core_ref, heads_ref, tails_ref, negs_ref, left_ref, left_sums_ref, right_ref, right_sums_ref, rel_ref, hub_ref,
     left_out, left_sums_out, right_out, keep_out, send_out,
-    left_parts, both_parts, left_grad, both_grad,
+    left_parts, both_parts,
 ):
     features, rows = left_ref.shape
     half = features // 2
@@ -526,35 +526,29 @@
     stack_into(left_parts, left_ref[...])
     stack_into(both_parts, right_ref[...], slice(0, rows))
     stack_into(both_parts, hub_ref[...], slice(rows, rows + hubs))
-    left_grad[...] = jnp.zeros_like(left_grad)
-    both_grad[...] = jnp.zeros_like(both_grad)
-
-    @pl.loop(0, edges // EDGE_TILE)
-    def _(step):
-        span = edge_span(step)
-        tail_here = lax.broadcasted_iota(jnp.int32, (rows, EDGE_TILE), 0) == tails_ref[at, span]
-        head_hot = onehot(0, rows, heads_ref[at, span])
-        h = dot2(left_parts[...], head_hot, NN)
-        r = rel_ref[:, span]
-        q = split(turned(h, r, half))
-        scores = dot3((both_parts[:features], both_parts[features:]), q, TN)
-        chance = jax.nn.sigmoid(scores[:rows])
-        coef = jnp.concatenate(
-            [
-                counts * chance + jnp.where(tail_here, chance - 1.0, 0.0),
-                weight * jax.nn.sigmoid(scores[rows:]),
-            ],
-            axis=0,
-        )
-        coef = split(coef)
-        dq = dot3_stacked(both_parts[...], coef, NN)
-        both_grad[...] += dot3_stacked(stack(q), coef, NT)
-        dh = jnp.concatenate(turned_back(dq, r, half), axis=0)
-        left_grad[...] += dot2(stack(split(dh)), head_hot, NT)
-        out_span = pl.ds(pl.multiple_of(hubs + step * EDGE_TILE, 128), EDGE_TILE)
-        keep_out[:, out_span], send_out[:, out_span] = keep_and_send(core, *turned_back(dq, h, half))
-
-    left_out[...], left_sums_out[...] = adagrad(left_ref[...], left_sums_ref[...], left_grad[...])
+
+    tail_here = lax.broadcasted_iota(jnp.int32, (rows, edges), 0) == tails_ref[at]
+    head_hot = onehot(0, rows, heads_ref[at])
+    h = dot2(left_parts[...], head_hot, NN)
+    r = rel_ref[...]
+    q = split(turned(h, r, half))
+    scores = dot3((both_parts[:features], both_parts[features:]), q, TN)
+    chance = jax.nn.sigmoid(scores[:rows])
+    coef = jnp.concatenate(
+        [
+            counts * chance + jnp.where(tail_here, chance - 1.0, 0.0),
+            weight * jax.nn.sigmoid(scores[rows:]),
+        ],
+        axis=0,
+    )
+    coef = split(coef)
+    dq = dot3_stacked(both_parts[...], coef, NN)
+    both_grad = dot3_stacked(stack(q), coef, NT)
+    dh = jnp.concatenate(turned_back(dq, r, half), axis=0)
+    left_grad = dot2(stack(split(dh)), head_hot, NT)
+    keep_out[:, hubs:], send_out[:, hubs:] = keep_and_send(core, *turned_back(dq, h, half))
+
+    left_out[...], left_sums_out[...] = adagrad(left_ref[...], left_sums_ref[...], left_grad)
     new_right, new_sums = adagrad(right_ref[...], right_sums_ref[...], both_grad[:, :rows])
     right_out[:features] = new_right
     right_out[features:] = jnp.broadcast_to(new_sums, (right_out.shape[0] - features, rows))
@@ -574,8 +568,6 @@
         scratch_shapes=[
             pltpu.VMEM((2 * features, rows), BF16),
             pltpu.VMEM((2 * features, width), BF16),
-            pltpu.VMEM((features, rows), F32),
-            pltpu.VMEM((features, width), F32),
         ],
         compiler_params=PARAMS,
         cost_estimate=COST,
@@ -585,7 +577,7 @@
 def hub_kernel(
     bucket, negatives, core_ref, heads_ref, left_ref, rel_ref, hub_ref,
     query_grad, hub_keep, hub_send,
-    left_parts, hub_parts, hub_grad,
+    left_parts, hub_parts,
 ):
     features, rows = left_ref.shape
     half = features // 2
@@ -594,17 +586,13 @@
     weight = 1.0 / (negatives + hubs)
     stack_into(left_parts, left_ref[...])
     stack_into(hub_parts, hub_ref[...])
-    hub_grad[...] = jnp.zeros_like(hub_grad)
-
-    @pl.loop(0, edges // EDGE_TILE)
-    def _(step):
-        span = edge_span(step)
-        head_hot = onehot(0, rows, heads_ref[at, span])
-        h = dot2(left_parts[...], head_hot, NN)
-        q = split(turned(h, rel_ref[:, span], half))
-        coef = split(weight * jax.nn.sigmoid(dot3((hub_parts[:features], hub_parts[features:]), q, TN)))
-        query_grad[:, span] = dot3_stacked(hub_parts[...], coef, NN)
-        hub_grad[...] += dot3_stacked(stack(q), coef, NT)
+
+    head_hot = onehot(0, rows, heads_ref[at])
+    h = dot2(left_parts[...], head_hot, NN)
+    q = split(turned(h, rel_ref[...], half))
+    coef = split(weight * jax.nn.sigmoid(dot3((hub_parts[:features], hub_parts[features:]), q, TN)))
+    query_grad[...] = dot3_stacked(hub_parts[...], coef, NN)
+    hub_grad = dot3_stacked(stack(q), coef, NT)
 
     hub_keep[...], hub_send[...] = keep_and_send(core_ref[1], hub_grad[:half], hub_grad[half:])
 
@@ -621,7 +609,6 @@
         scratch_shapes=[
             pltpu.VMEM((2 * features, rows), BF16),
             pltpu.VMEM((2 * features, hubs), BF16),
-            pltpu.VMEM((features, hubs), F32),
         ],
         compiler_params=PARAMS,
         cost_estimate=COST,
@@ -632,7 +619,7 @@
     bucket, hubs, core_ref, heads_ref, tails_ref, negs_ref, query_grad,
     left_ref, left_sums_ref, right_ref, rel_ref,
     left_out, right_out, rel_keep, rel_send,
-    left_parts, right_parts, left_grad, right_grad,
+    left_parts, right_parts,
 ):
     features, rows = left_ref.shape
     half = features // 2
@@ -642,27 +629,22 @@
     counts = table_counts(rows, negs_ref[at], 1.0 / (negs_ref.shape[1] + hubs))
     stack_into(left_parts, left_ref[...])
     stack_into(right_parts, right_ref[:features])
-    left_grad[...] = jnp.zeros_like(left_grad)
-    right_grad[...] = jnp.zeros_like(right_grad)
-
-    @pl.loop(0, edges // EDGE_TILE)
-    def _(step):
-        span = edge_span(step)
-        tail_here = lax.broadcasted_iota(jnp.int32, (rows, EDGE_TILE), 0) == tails_ref[at, span]
-        head_hot = onehot(0, rows, heads_ref[at, span])
-        h = dot2(left_parts[...], head_hot, NN)
-        r = rel_ref[:, span]
-        q = split(turned(h, r, half))
-        chance = jax.nn.sigmoid(dot3((right_parts[:features], right_parts[features:]), q, TN))
-        coef = split(counts * chance + jnp.where(tail_here, chance - 1.0, 0.0))
-        dq = dot3_stacked(right_parts[...], coef, NN) + query_grad[:, span]
-        right_grad[...] += dot3_stacked(stack(q), coef, NT)
-        rel_keep[:, span], rel_send[:, span] = keep_and_send(core, *turned_back(dq, h, half))
-        dh = jnp.concatenate(turned_back(dq, r, half), axis=0)
-        left_grad[...] += dot2(stack(split(dh)), head_hot, NT)
-
-    left_out[...], unused = adagrad(left_ref[...], left_sums_ref[...], left_grad[...])
-    right_out[...], unused = adagrad(right_ref[:features], right_ref[features : features + 1], right_grad[...])
+
+    tail_here = lax.broadcasted_iota(jnp.int32, (rows, edges), 0) == tails_ref[at]
+    head_hot = onehot(0, rows, heads_ref[at])
+    h = dot2(left_parts[...], head_hot, NN)
+    r = rel_ref[...]
+    q = split(turned(h, r, half))
+    chance = jax.nn.sigmoid(dot3((right_parts[:features], right_parts[features:]), q, TN))
+    coef = split(counts * chance + jnp.where(tail_here, chance - 1.0, 0.0))
+    dq = dot3_stacked(right_parts[...], coef, NN) + query_grad[...]
+    right_grad = dot3_stacked(stack(q), coef, NT)
+    rel_keep[...], rel_send[...] = keep_and_send(core, *turned_back(dq, h, half))
+    dh = jnp.concatenate(turned_back(dq, r, half), axis=0)
+    left_grad = dot2(stack(split(dh)), head_hot, NT)
+
+    left_out[...], unused = adagrad(left_ref[...], left_sums_ref[...], left_grad)
+    right_out[...], unused = adagrad(right_ref[:features], right_ref[features : features + 1], right_grad)
 
 
 def tables_step(bucket, hubs, core, heads, tails, negs, query_grad, left, left_sums, right, rel_rows):
@@ -674,8 +656,7 @@
         in_specs=[SMEM] + [VMEM] * 8,
         out_specs=[VMEM] * 4,
         out_shape=[jax.ShapeDtypeStruct(shape, F32) for shape in shapes],
-        scratch_shapes=[pltpu.VMEM((2 * features, rows), BF16)] * 2
-        + [pltpu.VMEM((features, rows), F32)] * 2,
+        scratch_shapes=[pltpu.VMEM((2 * features, rows), BF16)] * 2,
         compiler_params=PARAMS,
         cost_estimate=COST,
     )(core, heads, tails, negs, query_grad, left, left_sums, right, rel_rows)
@@ -710,7 +691,7 @@
     bits = sub_bits + lax.axis_size("blk").bit_length() - 2
     x, y, z, far = sub_bits, sub_bits + 1, 0, 1
     rest = [p for p in range(bits) if p not in (x, y, z, far)]
-    return [[x, y, z, far] + rest, [y, z, x, far] + rest, [z, x, far, y] + rest]
+    return [[x, y, z, far] + rest, [y, z, x, far] + rest, [z, x, y, far] + rest]
 
 
 def plane_orders(sub_bits, bits):
@@ -768,18 +749,20 @@
     keeps, fars = [], []
     for b in range(buckets - 1):
         if b > 0:
+            right = from_behind(right, "blk", 1)
             right, right_sums = right[:features], right[features : features + 1]
         left, left_sums, right, keep, send = bucket_step(
             b, spot, heads, tails, negatives, left, left_sums, right, right_sums, rel_rows[b], hub_rows[b]
         )
-        right = from_behind(right, "blk", 1)
         keeps.append(keep)
         fars.append(other_core(send))
     last = buckets - 1
     query_grad, hub_keep, hub_send = hub_step(
         last, negatives.shape[1], spot, heads, left, rel_rows[last], hub_rows[last]
     )
+    right, hub_send = in_turn(right, hub_send)
     hub_far = other_core(hub_send)
+    right = from_behind(right, "blk", 1)
     grads = lambda early, late, lanes: [(x, lanes) for x in early] + [(late, (0, late.shape[1]))]
     groups, where = grouped(orders, 0, heights)
     parts = chunk_columns(

time: 150 us -> 154 us (1.027)
  waiting for transfers between devices: 59.2 us -> 66.8 us
  starting transfers between devices: 43.7 us -> 40.9 us
    ppermute x3, waiting for transfers between devices: 0.01 us -> 8.61 us  [flipped_by(): lax.ppermute(x, axis, [(i, i ^ offset) for i in range(lax.axis_size(axis))])]
    ppermute x3, starting transfers between devices: 6.1 us -> 4.39 us  [flipped_by(): lax.ppermute(x, axis, [(i, i ^ offset) for i in range(lax.axis_size(axis))])]
    ppermute x36 -> x34, starting transfers between devices: 37.1 us -> 35.9 us  [flipped(): lax.ppermute(x, axis, [(i, i ^ 1 << bit) for i in range(lax.axis_size(axi...]
    ppermute x36 -> x34, waiting for transfers between devices: 59.2 us -> 58.1 us  [flipped(): lax.ppermute(x, axis, [(i, i ^ 1 << bit) for i in range(lax.axis_size(axi...]
  transfers between devices with their start and end apart: 40 -> 38, of which waited for: 19 -> 18; matrix products, arithmetic and copies ran while one was open for 0% -> 0% of each run, Pallas kernels for 23% -> 20%
where the time goes in v8:
time: 154 us
  waiting for transfers between devices  66.8 us (43%)
  Pallas kernels  43.3 us (28%)
  starting transfers between devices  40.9 us (27%)
    ppermute x34, waiting for transfers between devices, flipped(): lax.ppermute(x, axis, [(i, i ^ 1 << bit) for i in range(lax.axis_size(axi...  58.1 us
    ppermute x34, starting transfers between devices, flipped(): lax.ppermute(x, axis, [(i, i ^ 1 << bit) for i in range(lax.axis_size(axi...  35.9 us
    pallas_call x1, Pallas kernels, gather_rows(): pl.pallas_call(functools.partial(gather_kernel, hub_steps, rel_steps), in...  10 us
    pallas_call x4, Pallas kernels, placed(): pl.pallas_call(kernel, in_specs=[SMEM] + [VMEM] * (1 + len(fars)) + [HBM]...  9.33 us
    ppermute x3, waiting for transfers between devices, flipped_by(): lax.ppermute(x, axis, [(i, i ^ offset) for i in range(lax.axis_size(axis))])  8.61 us
    pallas_call x2, Pallas kernels, chunk_columns(): pl.pallas_call(functools.partial(kernel, grad_lanes), in_specs=[SMEM] + [...  7.98 us
    pallas_call x1, Pallas kernels, bucket_step(): pl.pallas_call(functools.partial(bucket_kernel, bucket), in_specs=[SMEM]...  5.58 us
    pallas_call x1, Pallas kernels, tables_step(): pl.pallas_call(functools.partial(tables_kernel, bucket, hubs), in_specs=[...  5.42 us
  transfers between devices with their start and end apart: 38, of which 18 were waited for; matrix products, arithmetic and copies ran while one was open for 0% of the time, Pallas kernels for 20%

profile of v8, /device:TPU:0, one launch (start us, length us, event | category | flops | bytes accessed | tf_op | source)
XLA Modules:
  0.0 153.7 jit_solution(18192720802712524718)
XLA Ops:
  2.7 10.0 %shard_map.156 = (f32[400,256]{1,0:T(8,128)S(1)}, f32[400,256]{1,0:T(8,128)S(1)}, f32[400,512]{1,0:T(8,128)S(1)}, f32[400,512]{1,0:T(8,128)S(1)}, s32[2]{0:T(128...) custom-call(s32[2]{0:T(128)S(1)} %pad_add_fusion.spot_ref, s32[2,256]{1,0:T(2,128)S(1)} %copy-done.7, ...), custom_call_target="tpu_custom_call" | custom-call | flops 10000 | bytes 10000 | tf_op jit(solution)/shard_map/pallas_call | solution.py:135
  12.9 5.6 %shard_map.157 = (f32[400,512]{1,0:T(8,128)S(1)}, f32[1,512]{1,0:T(1,128)S(1)}, f32[408,512]{1,0:T(8,128)S(1)}, f32[200,768]{1,0:T(8,128)S(1)}, f32[200,768]{1,0:T(8,128)S(1)}) custom-call(s32[2]{0:T(128)S(1)} %get-tuple-element.110.core_ref.spot_ref, s32[2,512]{1,0:T(2,128)S(1)} %copy-done.2, s32[2,512]{1,0:T(2,128)S(1)} %copy-done.4, ...), custom_call_target="tpu_custom_call" | custom-call | flops 10000 | bytes 10000 | tf_op jit(solution)/shard_map/pallas_call | solution.py:563
  18.5 2.7 %shard_map.158 = (f32[400,512]{1,0:T(8,128)S(1)}, f32[200,256]{1,0:T(8,128)S(1)}, f32[200,256]{1,0:T(8,128)S(1)}) custom-call(s32[2]{0:T(128)S(1)} %get-tuple-element.110.core_ref.spot_ref, s32[2,512]{1,0:T(2,128)S(1)} %copy-done.2, f32[400,512]{1,0:T(8,128)S(1)} %get-tuple-element.115.left_ref, f32[400,512]{1,0:T(8,128)S(1)} %get-tuple-element.116.rel_ref, ...), custom_call_target="tpu_custom_call" | custom-call | flops 10000 | bytes 10000 | tf_op jit(solution)/shard_map/pallas_call | solution.py:604
  21.8 2.7 %collective-permute-start.3 = (f32[200,768]{1,0:T(8,128)S(1)}, f32[200,768]{1,0:T(8,128)S(1)}, u32[]{:S(2)}, u32[]{:S(2)}) collective-permute-start(f32[200,768]{1,0:T(8,128)S(1)} %get-tuple-element.128), channel_id=1, source_target_pairs={{0,4},{4,0},{8,12},{12,8},{16,20},{20,16},{24,28},{28,24},{1,5},{5... | collective-permute-start | bytes 1843208 | tf_op jit(solution)/shard_map/ppermute | solution.py:671
  24.5 2.0 %collective-permute-done.4.refs_5_ = f32[200,256]{1,0:T(8,128)S(1)} collective-permute-done((f32[200,256]{1,0:T(8,128)S(1)}, f32[200,256]{1,0:T(8,128)S(1)}, u32[]{:S(2)}, u32[]{:S(2)}) %collective-permute-start.4) | collective-permute-done | bytes 204832 | tf_op jit(solution)/shard_map/ppermute | solution.py:671
  26.5 4.3 %shard_map.160 = (f32[8,72,256]{2,1,0:T(8,128)S(1)}, f32[8,64,256]{2,1,0:T(8,128)S(1)}, f32[8,64,256]{2,1,0:T(8,128)S(1)}, f32[8,72,256]{2,1,0:T(8,128)S(1)}, f3...) custom-call(s32[2]{0:T(128)S(1)} %get-tuple-element.110.core_ref.spot_ref, s32[2,256]{1,0:T(2,128)S(1)} %copy-done.7, ...), custom_call_target="tpu_custom_call" | custom-call | flops 10000 | bytes 10000 | tf_op jit(solution)/shard_map/pallas_call | solution.py:273
  33.6 1.6 %collective-permute-start.8 = (f32[8,64,256]{2,1,0:T(8,128)S(1)}, f32[8,64,256]{2,1,0:T(8,128)S(1)}, u32[]{:S(2)}, u32[]{:S(2)}) collective-permute-start(f32[8,64,256]{2,1,0:T(8,128)S(1)} %get-tuple-element.140), channel_id=1, source_target_pairs={{0,1},{1,0},{2,3},{3,2},{4,5},{5,4},{6,7},{7,6},{8,9},{9,8},{10,11... | collective-permute-start | bytes 1572872 | tf_op jit(solution)/shard_map/ppermute | solution.py:671
  35.3 5.4 %shard_map.159 = (f32[400,512]{1,0:T(8,128)}, f32[400,512]{1,0:T(8,128)}, f32[200,512]{1,0:T(8,128)S(1)}, f32[200,512]{1,0:T(8,128)S(1)}) custom-call(s32[2]{0:T(128)S(1)} %get-tuple-element.110.core_ref.spot_ref, s32[2,512]{1,0:T(2,128)S(1)} %copy-done.2, s32[2,512]{1,0:T(2,128)S(1)} %copy-done.4, s32[2,1024]{1,0:T(2,128)S(1)} %copy-done.3, ...), custom_call_target="tpu_custom_call" | custom-call | flops 10000 | bytes 10000 | tf_op jit(solution)/shard_map/pallas_call | solution.py:654
  40.7 1.7 %collective-permute-done.5.refs_5_ = f32[200,512]{1,0:T(8,128)S(1)} collective-permute-done((f32[200,512]{1,0:T(8,128)S(1)}, f32[200,512]{1,0:T(8,128)S(1)}, u32[]{:S(2)}, u32[]{:S(2)}) %collective-permute-start.5) | collective-permute-done | bytes 409632 | tf_op jit(solution)/shard_map/ppermute | solution.py:671
  42.5 3.6 %shard_map.161 = (f32[8,40,256]{2,1,0:T(8,128)S(1)}, f32[8,32,256]{2,1,0:T(8,128)S(1)}, f32[8,40,256]{2,1,0:T(8,128)S(1)}, f32[8,32,256]{2,1,0:T(8,128)S(1)}) custom-call(s32[2]{0:T(128)S(1)} %get-tuple-element.110.core_ref.spot_ref, s32[2,512]{1,0:T(2,128)S(1)} %copy-done.5, s32[2,512]{1,0:T(2,128)S(1)} %collective-permute-done.1.refs_1_, ...), custom_call_target="tpu_custom_call" | custom-call | flops 10000 | bytes 10000 | tf_op jit(solution)/shard_map/pallas_call | solution.py:273
  46.1 1.6 %collective-permute-start.9 = (f32[8,40,256]{2,1,0:T(8,128)S(1)}, f32[8,40,256]{2,1,0:T(8,128)S(1)}, u32[]{:S(2)}, u32[]{:S(2)}) collective-permute-start(f32[8,40,256]{2,1,0:T(8,128)S(1)} %get-tuple-element.147), channel_id=1, source_target_pairs={{0,8},{4,12},{8,0},{12,4},{16,24},{20,28},{24,16},{28,20},{1,9},{5... | collective-permute-start | bytes 983048 | tf_op jit(solution)/shard_map/ppermute | solution.py:671
  47.9 1.8 %collective-permute-start.11 = (f32[4,72,256]{2,1,0:T(8,128)S(1)}, f32[4,72,256]{2,1,0:T(8,128)S(1)}, u32[]{:S(2)}, u32[]{:S(2)}) collective-permute-start(f32[4,72,256]{2,1,0:T(8,128)S(1)} %get-tuple-element.158), channel_id=1, source_target_pairs={{0,16},{4,20},{8,24},{12,28},{16,0},{20,4},{24,8},{28,12},{1,17},{... | collective-permute-start | bytes 884744 | tf_op jit(solution)/shard_map/ppermute | solution.py:671
  50.0 1.5 collective-permute-start.12
  51.5 2.0 %collective-permute-start.13 = (f32[4,64,256]{2,1,0:T(8,128)S(1)}, f32[4,64,256]{2,1,0:T(8,128)S(1)}, u32[]{:S(2)}, u32[]{:S(2)}) collective-permute-start(f32[4,64,256]{2,1,0:T(8,128)S(1)} %get-tuple-element.160), channel_id=1, source_target_pairs={{0,8},{4,12},{8,0},{12,4},{16,24},{20,28},{24,16},{28,20},{1,9},{5... | collective-permute-start | bytes 786440 | tf_op jit(solution)/shard_map/ppermute | solution.py:671
  53.5 9.5 %collective-permute-done.10.refs_3_ = f32[8,32,256]{2,1,0:T(8,128)S(1)} collective-permute-done((f32[8,32,256]{2,1,0:T(8,128)S(1)}, f32[8,32,256]{2,1,0:T(8,128)S(1)}, u32[]{:S(2)}, u32[]{:S(2)}) %collective-permute-start.10) | collective-permute-done | bytes 262176 | tf_op jit(solution)/shard_map/ppermute | solution.py:671
  64.5 1.9 %collective-permute-start.16 = (f32[2,72,256]{2,1,0:T(8,128)S(1)}, f32[2,72,256]{2,1,0:T(8,128)S(1)}, u32[]{:S(2)}, u32[]{:S(2)}) collective-permute-start(f32[2,72,256]{2,1,0:T(8,128)S(1)} %get-tuple-element.177), channel_id=1, source_target_pairs={{0,1},{1,0},{2,3},{3,2},{4,5},{5,4},{6,7},{7,6},{8,9},{9,8},{10,11... | collective-permute-start | bytes 442376 | tf_op jit(solution)/shard_map/ppermute | solution.py:671
  66.4 1.7 %collective-permute-start.15 = (f32[4,32,256]{2,1,0:T(8,128)S(1)}, f32[4,32,256]{2,1,0:T(8,128)S(1)}, u32[]{:S(2)}, u32[]{:S(2)}) collective-permute-start(f32[4,32,256]{2,1,0:T(8,128)S(1)} %get-tuple-element.168), channel_id=1, source_target_pairs={{0,8},{4,12},{8,0},{12,4},{16,24},{20,28},{24,16},{28,20},{1,9},{5... | collective-permute-start | bytes 393224 | tf_op jit(solution)/shard_map/ppermute | solution.py:671
  69.0 2.9 %collective-permute-done.15.refs_3_ = f32[4,32,256]{2,1,0:T(8,128)S(1)} collective-permute-done((f32[4,32,256]{2,1,0:T(8,128)S(1)}, f32[4,32,256]{2,1,0:T(8,128)S(1)}, u32[]{:S(2)}, u32[]{:S(2)}) %collective-permute-start.15) | collective-permute-done | bytes 131104 | tf_op jit(solution)/shard_map/ppermute | solution.py:671
  73.4 2.7 %collective-permute-start.19 = (f32[1,200,256]{2,1,0:T(8,128)S(1)}, f32[1,200,256]{2,1,0:T(8,128)S(1)}, u32[]{:S(2)}, u32[]{:S(2)}) collective-permute-start(f32[1,200,256]{2,1,0:T(8,128)S(1)} %get-tuple-element.186), channel_id=1, source_target_pairs={{0,2},{1,3},{2,0},{3,1},{4,6},{5,7},{6,4},{7,5},{8,10},{9,11},{10,... | collective-permute-start | bytes 614408 | tf_op jit(solution)/shard_map/ppermute | solution.py:671
  76.7 3.7 %collective-permute-start.22 = (f32[1,72,256]{2,1,0:T(8,128)S(1)}, f32[1,72,256]{2,1,0:T(8,128)S(1)}, u32[]{:S(2)}, u32[]{:S(2)}) collective-permute-start(f32[1,72,256]{2,1,0:T(8,128)S(1)} %get-tuple-element.190), channel_id=1, source_target_pairs={{0,3},{1,2},{2,1},{3,0},{4,7},{5,6},{6,5},{7,4},{8,11},{9,10},{10,... | collective-permute-start | bytes 221192 | tf_op jit(solution)/shard_map/ppermute | solution.py:675
  81.6 7.4 %collective-permute-done.21.refs_6_ = f32[1,72,256]{2,1,0:T(8,128)S(1)} collective-permute-done((f32[1,72,256]{2,1,0:T(8,128)S(1)}, f32[1,72,256]{2,1,0:T(8,128)S(1)}, u32[]{:S(2)}, u32[]{:S(2)}) %collective-permute-start.21) | collective-permute-done | bytes 73760 | tf_op jit(solution)/shard_map/ppermute | solution.py:675
  91.7 3.1 %collective-permute-start.24 = (f32[1,272,256]{2,1,0:T(8,128)S(1)}, f32[1,272,256]{2,1,0:T(8,128)S(1)}, u32[]{:S(2)}, u32[]{:S(2)}) collective-permute-start(f32[1,272,256]{2,1,0:T(8,128)S(1)} %shard_map.168.refs_0_), channel_id=1, source_target_pairs={{0,2},{1,3},{2,0},{3,1},{4,6},{5,7},{6,4},{7,5},{8,10},{9,11},{10,... | collective-permute-start | bytes 835592 | tf_op jit(solution)/shard_map/ppermute | solution.py:671
  94.9 13.0 %collective-permute-done.24.refs_1_ = f32[1,272,256]{2,1,0:T(8,128)S(1)} collective-permute-done((f32[1,272,256]{2,1,0:T(8,128)S(1)}, f32[1,272,256]{2,1,0:T(8,128)S(1)}, u32[]{:S(2)}, u32[]{:S(2)}) %collective-permute-start.24) | collective-permute-done | bytes 278560 | tf_op jit(solution)/shard_map/ppermute | solution.py:671
  110.2 4.1 %collective-permute-done.26.refs_4_ = f32[2,88,256]{2,1,0:T(8,128)S(1)} collective-permute-done((f32[2,88,256]{2,1,0:T(8,128)S(1)}, f32[2,88,256]{2,1,0:T(8,128)S(1)}, u32[]{:S(2)}, u32[]{:S(2)}) %collective-permute-start.26) | collective-permute-done | bytes 180256 | tf_op jit(solution)/shard_map/ppermute | solution.py:671
  114.6 1.7 %collective-permute-start.28 = (f32[4,96,256]{2,1,0:T(8,128)S(1)}, f32[4,96,256]{2,1,0:T(8,128)S(1)}, u32[]{:S(2)}, u32[]{:S(2)}) collective-permute-start(f32[4,96,256]{2,1,0:T(8,128)S(1)} %get-tuple-element.201.refs_0_), channel_id=1, source_target_pairs={{0,16},{4,20},{8,24},{12,28},{16,0},{20,4},{24,8},{28,12},{1,17},{... | collective-permute-start | bytes 1179656 | tf_op jit(solution)/shard_map/ppermute | solution.py:671
  116.3 1.7 %collective-permute-start.29 = (f32[4,88,256]{2,1,0:T(8,128)S(1)}, f32[4,88,256]{2,1,0:T(8,128)S(1)}, u32[]{:S(2)}, u32[]{:S(2)}) collective-permute-start(f32[4,88,256]{2,1,0:T(8,128)S(1)} %get-tuple-element.202.refs_1_), channel_id=1, source_target_pairs={{0,1},{1,0},{2,3},{3,2},{4,5},{5,4},{6,7},{7,6},{8,9},{9,8},{10,11... | collective-permute-start | bytes 1081352 | tf_op jit(solution)/shard_map/ppermute | solution.py:671
  118.6 6.3 %collective-permute-done.29.refs_4_ = f32[4,88,256]{2,1,0:T(8,128)S(1)} collective-permute-done((f32[4,88,256]{2,1,0:T(8,128)S(1)}, f32[4,88,256]{2,1,0:T(8,128)S(1)}, u32[]{:S(2)}, u32[]{:S(2)}) %collective-permute-start.29) | collective-permute-done | bytes 360480 | tf_op jit(solution)/shard_map/ppermute | solution.py:671
  128.9 1.9 %shard_map.172.refs_0_ = f32[2,200,4096]{2,1,0:T(8,128)} custom-call(s32[2]{0:T(128)S(1)} %get-tuple-element.110.core_ref.spot_ref, f32[8,272,256]{2,1,0:T(8,128)S(1)} %get-tuple-element.204.near_ref), custom_call_target="tpu_custom_call" | custom-call | bytes 3276800 | tf_op jit(solution)/shard_map/pallas_call | solution.py:474
  130.8 1.9 %shard_map.173.refs_3_ = f32[2,200,4096]{2,1,0:T(8,128)} custom-call(s32[2]{0:T(128)S(1)} %get-tuple-element.110.core_ref.spot_ref, f32[8,272,256]{2,1,0:T(8,128)S(1)} %collective-permute-done.31.near_ref, f32[2,200,4096]{2,1,0:T(8,128)} %shard_map.172.refs_0_), custom_call_target="tpu_custom_call", output_to_operand_aliasing={{}: (2, {})} | custom-call | bytes 3276800 | tf_op jit(solution)/shard_map/pallas_call | solution.py:474
  132.8 12.5 %collective-permute-done.33.refs_1_ = f32[8,88,256]{2,1,0:T(8,128)S(1)} collective-permute-done((f32[8,88,256]{2,1,0:T(8,128)S(1)}, f32[8,88,256]{2,1,0:T(8,128)S(1)}, u32[]{:S(2)}, u32[]{:S(2)}) %collective-permute-start.33) | collective-permute-done | bytes 720928 | tf_op jit(solution)/shard_map/ppermute | solution.py:671
  146.9 2.7 %shard_map.174 = (f32[2,200,4096]{2,1,0:T(8,128)}, f32[2,200,1280]{2,1,0:T(8,128)}) custom-call(s32[2]{0:T(128)S(1)} %get-tuple-element.110.core_ref.spot_ref, f32[8,272,256]{2,1,0:T(8,128)S(1)} %get-tuple-element.204.near_ref, f32[8,96,256]{2,1,0:T(8,128)S(1)} %collective-permute-done.32.refs_0_, ...), custom_call_target="tpu_custom_call", output_to_operand_aliasing={{0}: (5, {})} | custom-call | bytes 3276800 | tf_op jit(solution)/shard_map/pallas_call | solution.py:474
  150.7 2.7 %shard_map.175 = (f32[2,200,4096]{2,1,0:T(8,128)}, f32[2,200,1280]{2,1,0:T(8,128)}) custom-call(s32[2]{0:T(128)S(1)} %get-tuple-element.110.core_ref.spot_ref, f32[8,272,256]{2,1,0:T(8,128)S(1)} %collective-permute-done.31.near_ref, f32[8,96,256]{2,1,0:T(8,128)S(1)} %collective-permute-done.35.refs_0_, ...), custom_call_target="tpu_custom_call", output_to_operand_aliasing={{0}: (5, {}), {1}: (6, {})} | custom-call | bytes 3276800 | tf_op jit(solution)/shard_map/pallas_call | solution.py:474
  (88 shorter events, 24.4 us)
Async XLA Ops:
  0.7 12.1 %collective-permute-start = (s32[2,256]{1,0:T(2,128)}, s32[2,256]{1,0:T(2,128)S(1)}, u32[]{:S(2)}, u32[]{:S(2)}) collective-permute-start(s32[2,256]{1,0:T(2,128)} %refs_0_.2), channel_id=1, source_target_pairs={{0,4},{4,0},{8,12},{12,8},{16,20},{20,16},{24,28},{28,24},{1,5},{5... | collective-permute-start | bytes 6152 | tf_op jit(solution)/shard_map/ppermute | solution.py:671
  1.2 11.6 %collective-permute-start.1 = (s32[2,512]{1,0:T(2,128)}, s32[2,512]{1,0:T(2,128)S(1)}, u32[]{:S(2)}, u32[]{:S(2)}) collective-permute-start(s32[2,512]{1,0:T(2,128)} %refs_0_.3), channel_id=1, source_target_pairs={{0,4},{4,0},{8,12},{12,8},{16,20},{20,16},{24,28},{28,24},{1,5},{5... | collective-permute-start | bytes 12296 | tf_op jit(solution)/shard_map/ppermute | solution.py:671
  21.2 14.1 %collective-permute-start.2 = (f32[408,512]{1,0:T(8,128)S(1)}, f32[408,512]{1,0:T(8,128)S(1)}, u32[]{:S(2)}, u32[]{:S(2)}) collective-permute-start(f32[408,512]{1,0:T(8,128)S(1)} %get-tuple-element.122), channel_id=1, source_target_pairs={{0,4},{4,8},{8,12},{12,16},{16,20},{20,24},{24,28},{28,0},{1,5},{5... | collective-permute-start | bytes 2506760 | tf_op jit(solution)/shard_map/ppermute | solution.py:667
  21.8 4.7 %collective-permute-start.3 = (f32[200,768]{1,0:T(8,128)S(1)}, f32[200,768]{1,0:T(8,128)S(1)}, u32[]{:S(2)}, u32[]{:S(2)}) collective-permute-start(f32[200,768]{1,0:T(8,128)S(1)} %get-tuple-element.128), channel_id=1, source_target_pairs={{0,4},{4,0},{8,12},{12,8},{16,20},{20,16},{24,28},{28,24},{1,5},{5... | collective-permute-start | bytes 1843208 | tf_op jit(solution)/shard_map/ppermute | solution.py:671
  30.8 16.8 %collective-permute-start.6 = (f32[8,72,256]{2,1,0:T(8,128)S(1)}, f32[8,72,256]{2,1,0:T(8,128)S(1)}, u32[]{:S(2)}, u32[]{:S(2)}) collective-permute-start(f32[8,72,256]{2,1,0:T(8,128)S(1)} %get-tuple-element.138), channel_id=1, source_target_pairs={{0,8},{4,12},{8,0},{12,4},{16,24},{20,28},{24,16},{28,20},{1,9},{5... | collective-permute-start | bytes 1769480 | tf_op jit(solution)/shard_map/ppermute | solution.py:671
  32.3 15.4 %collective-permute-start.7 = (f32[8,64,256]{2,1,0:T(8,128)S(1)}, f32[8,64,256]{2,1,0:T(8,128)S(1)}, u32[]{:S(2)}, u32[]{:S(2)}) collective-permute-start(f32[8,64,256]{2,1,0:T(8,128)S(1)} %get-tuple-element.139), channel_id=1, source_target_pairs={{0,16},{4,20},{8,24},{12,28},{16,0},{20,4},{24,8},{28,12},{1,17},{... | collective-permute-start | bytes 1572872 | tf_op jit(solution)/shard_map/ppermute | solution.py:671
  33.6 14.1 %collective-permute-start.8 = (f32[8,64,256]{2,1,0:T(8,128)S(1)}, f32[8,64,256]{2,1,0:T(8,128)S(1)}, u32[]{:S(2)}, u32[]{:S(2)}) collective-permute-start(f32[8,64,256]{2,1,0:T(8,128)S(1)} %get-tuple-element.140), channel_id=1, source_target_pairs={{0,1},{1,0},{2,3},{3,2},{4,5},{5,4},{6,7},{7,6},{8,9},{9,8},{10,11... | collective-permute-start | bytes 1572872 | tf_op jit(solution)/shard_map/ppermute | solution.py:671
  46.1 16.9 %collective-permute-start.9 = (f32[8,40,256]{2,1,0:T(8,128)S(1)}, f32[8,40,256]{2,1,0:T(8,128)S(1)}, u32[]{:S(2)}, u32[]{:S(2)}) collective-permute-start(f32[8,40,256]{2,1,0:T(8,128)S(1)} %get-tuple-element.147), channel_id=1, source_target_pairs={{0,8},{4,12},{8,0},{12,4},{16,24},{20,28},{24,16},{28,20},{1,9},{5... | collective-permute-start | bytes 983048 | tf_op jit(solution)/shard_map/ppermute | solution.py:671
  47.9 16.5 %collective-permute-start.11 = (f32[4,72,256]{2,1,0:T(8,128)S(1)}, f32[4,72,256]{2,1,0:T(8,128)S(1)}, u32[]{:S(2)}, u32[]{:S(2)}) collective-permute-start(f32[4,72,256]{2,1,0:T(8,128)S(1)} %get-tuple-element.158), channel_id=1, source_target_pairs={{0,16},{4,20},{8,24},{12,28},{16,0},{20,4},{24,8},{28,12},{1,17},{... | collective-permute-start | bytes 884744 | tf_op jit(solution)/shard_map/ppermute | solution.py:671
  49.7 13.3 %collective-permute-start.10 = (f32[8,32,256]{2,1,0:T(8,128)S(1)}, f32[8,32,256]{2,1,0:T(8,128)S(1)}, u32[]{:S(2)}, u32[]{:S(2)}) collective-permute-start(f32[8,32,256]{2,1,0:T(8,128)S(1)} %get-tuple-element.148), channel_id=1, source_target_pairs={{0,16},{4,20},{8,24},{12,28},{16,0},{20,4},{24,8},{28,12},{1,17},{... | collective-permute-start | bytes 786440 | tf_op jit(solution)/shard_map/ppermute | solution.py:671
  50.0 14.4 %collective-permute-start.12 = (f32[4,64,256]{2,1,0:T(8,128)S(1)}, f32[4,64,256]{2,1,0:T(8,128)S(1)}, u32[]{:S(2)}, u32[]{:S(2)}) collective-permute-start(f32[4,64,256]{2,1,0:T(8,128)S(1)} %get-tuple-element.159), channel_id=1, source_target_pairs={{0,1},{1,0},{2,3},{3,2},{4,5},{5,4},{6,7},{7,6},{8,9},{9,8},{10,11... | collective-permute-start | bytes 786440 | tf_op jit(solution)/shard_map/ppermute | solution.py:671
  51.5 12.9 %collective-permute-start.13 = (f32[4,64,256]{2,1,0:T(8,128)S(1)}, f32[4,64,256]{2,1,0:T(8,128)S(1)}, u32[]{:S(2)}, u32[]{:S(2)}) collective-permute-start(f32[4,64,256]{2,1,0:T(8,128)S(1)} %get-tuple-element.160), channel_id=1, source_target_pairs={{0,8},{4,12},{8,0},{12,4},{16,24},{20,28},{24,16},{28,20},{1,9},{5... | collective-permute-start | bytes 786440 | tf_op jit(solution)/shard_map/ppermute | solution.py:671
  63.0 8.9 %collective-permute-start.14 = (f32[4,40,256]{2,1,0:T(8,128)S(1)}, f32[4,40,256]{2,1,0:T(8,128)S(1)}, u32[]{:S(2)}, u32[]{:S(2)}) collective-permute-start(f32[4,40,256]{2,1,0:T(8,128)S(1)} %get-tuple-element.167), channel_id=1, source_target_pairs={{0,16},{4,20},{8,24},{12,28},{16,0},{20,4},{24,8},{28,12},{1,17},{... | collective-permute-start | bytes 491528 | tf_op jit(solution)/shard_map/ppermute | solution.py:671
  64.5 8.9 %collective-permute-start.16 = (f32[2,72,256]{2,1,0:T(8,128)S(1)}, f32[2,72,256]{2,1,0:T(8,128)S(1)}, u32[]{:S(2)}, u32[]{:S(2)}) collective-permute-start(f32[2,72,256]{2,1,0:T(8,128)S(1)} %get-tuple-element.177), channel_id=1, source_target_pairs={{0,1},{1,0},{2,3},{3,2},{4,5},{5,4},{6,7},{7,6},{8,9},{9,8},{10,11... | collective-permute-start | bytes 442376 | tf_op jit(solution)/shard_map/ppermute | solution.py:671
  66.4 5.6 %collective-permute-start.15 = (f32[4,32,256]{2,1,0:T(8,128)S(1)}, f32[4,32,256]{2,1,0:T(8,128)S(1)}, u32[]{:S(2)}, u32[]{:S(2)}) collective-permute-start(f32[4,32,256]{2,1,0:T(8,128)S(1)} %get-tuple-element.168), channel_id=1, source_target_pairs={{0,8},{4,12},{8,0},{12,4},{16,24},{20,28},{24,16},{28,20},{1,9},{5... | collective-permute-start | bytes 393224 | tf_op jit(solution)/shard_map/ppermute | solution.py:671
  68.1 5.2 %collective-permute-start.17 = (f32[2,64,256]{2,1,0:T(8,128)S(1)}, f32[2,64,256]{2,1,0:T(8,128)S(1)}, u32[]{:S(2)}, u32[]{:S(2)}) collective-permute-start(f32[2,64,256]{2,1,0:T(8,128)S(1)} %get-tuple-element.178), channel_id=1, source_target_pairs={{0,8},{4,12},{8,0},{12,4},{16,24},{20,28},{24,16},{28,20},{1,9},{5... | collective-permute-start | bytes 393224 | tf_op jit(solution)/shard_map/ppermute | solution.py:671
  68.4 5.0 %collective-permute-start.18 = (f32[2,64,256]{2,1,0:T(8,128)S(1)}, f32[2,64,256]{2,1,0:T(8,128)S(1)}, u32[]{:S(2)}, u32[]{:S(2)}) collective-permute-start(f32[2,64,256]{2,1,0:T(8,128)S(1)} %get-tuple-element.179), channel_id=1, source_target_pairs={{0,16},{4,20},{8,24},{12,28},{16,0},{20,4},{24,8},{28,12},{1,17},{... | collective-permute-start | bytes 393224 | tf_op jit(solution)/shard_map/ppermute | solution.py:671
  73.4 15.7 %collective-permute-start.19 = (f32[1,200,256]{2,1,0:T(8,128)S(1)}, f32[1,200,256]{2,1,0:T(8,128)S(1)}, u32[]{:S(2)}, u32[]{:S(2)}) collective-permute-start(f32[1,200,256]{2,1,0:T(8,128)S(1)} %get-tuple-element.186), channel_id=1, source_target_pairs={{0,2},{1,3},{2,0},{3,1},{4,6},{5,7},{6,4},{7,5},{8,10},{9,11},{10,... | collective-permute-start | bytes 614408 | tf_op jit(solution)/shard_map/ppermute | solution.py:671
  76.1 5.5 %collective-permute-start.20 = (f32[1,72,256]{2,1,0:T(8,128)S(1)}, f32[1,72,256]{2,1,0:T(8,128)S(1)}, u32[]{:S(2)}, u32[]{:S(2)}) collective-permute-start(f32[1,72,256]{2,1,0:T(8,128)S(1)} %get-tuple-element.188), channel_id=1, source_target_pairs={{0,1},{1,0},{2,3},{3,2},{4,5},{5,4},{6,7},{7,6},{8,9},{9,8},{10,11... | collective-permute-start | bytes 221192 | tf_op jit(solution)/shard_map/ppermute | solution.py:675
  76.4 12.7 %collective-permute-start.21 = (f32[1,72,256]{2,1,0:T(8,128)S(1)}, f32[1,72,256]{2,1,0:T(8,128)S(1)}, u32[]{:S(2)}, u32[]{:S(2)}) collective-permute-start(f32[1,72,256]{2,1,0:T(8,128)S(1)} %get-tuple-element.189), channel_id=1, source_target_pairs={{0,2},{1,3},{2,0},{3,1},{4,6},{5,7},{6,4},{7,5},{8,10},{9,11},{10,... | collective-permute-start | bytes 221192 | tf_op jit(solution)/shard_map/ppermute | solution.py:675
  76.7 12.3 %collective-permute-start.22 = (f32[1,72,256]{2,1,0:T(8,128)S(1)}, f32[1,72,256]{2,1,0:T(8,128)S(1)}, u32[]{:S(2)}, u32[]{:S(2)}) collective-permute-start(f32[1,72,256]{2,1,0:T(8,128)S(1)} %get-tuple-element.190), channel_id=1, source_target_pairs={{0,3},{1,2},{2,1},{3,0},{4,7},{5,6},{6,5},{7,4},{8,11},{9,10},{10,... | collective-permute-start | bytes 221192 | tf_op jit(solution)/shard_map/ppermute | solution.py:675
  91.7 16.1 %collective-permute-start.24 = (f32[1,272,256]{2,1,0:T(8,128)S(1)}, f32[1,272,256]{2,1,0:T(8,128)S(1)}, u32[]{:S(2)}, u32[]{:S(2)}) collective-permute-start(f32[1,272,256]{2,1,0:T(8,128)S(1)} %shard_map.168.refs_0_), channel_id=1, source_target_pairs={{0,2},{1,3},{2,0},{3,1},{4,6},{5,7},{6,4},{7,5},{8,10},{9,11},{10,... | collective-permute-start | bytes 835592 | tf_op jit(solution)/shard_map/ppermute | solution.py:671
  107.9 6.6 %collective-permute-start.25 = (f32[2,96,256]{2,1,0:T(8,128)S(1)}, f32[2,96,256]{2,1,0:T(8,128)S(1)}, u32[]{:S(2)}, u32[]{:S(2)}) collective-permute-start(f32[2,96,256]{2,1,0:T(8,128)S(1)} %get-tuple-element.198.refs_0_), channel_id=1, source_target_pairs={{0,1},{1,0},{2,3},{3,2},{4,5},{5,4},{6,7},{7,6},{8,9},{9,8},{10,11... | collective-permute-start | bytes 589832 | tf_op jit(solution)/shard_map/ppermute | solution.py:671
  108.0 6.3 %collective-permute-start.26 = (f32[2,88,256]{2,1,0:T(8,128)S(1)}, f32[2,88,256]{2,1,0:T(8,128)S(1)}, u32[]{:S(2)}, u32[]{:S(2)}) collective-permute-start(f32[2,88,256]{2,1,0:T(8,128)S(1)} %get-tuple-element.199.refs_1_), channel_id=1, source_target_pairs={{0,8},{4,12},{8,0},{12,4},{16,24},{20,28},{24,16},{28,20},{1,9},{5... | collective-permute-start | bytes 540680 | tf_op jit(solution)/shard_map/ppermute | solution.py:671
  108.8 5.7 %collective-permute-start.27 = (f32[2,88,256]{2,1,0:T(8,128)S(1)}, f32[2,88,256]{2,1,0:T(8,128)S(1)}, u32[]{:S(2)}, u32[]{:S(2)}) collective-permute-start(f32[2,88,256]{2,1,0:T(8,128)S(1)} %get-tuple-element.200.refs_2_), channel_id=1, source_target_pairs={{0,16},{4,20},{8,24},{12,28},{16,0},{20,4},{24,8},{28,12},{1,17},{... | collective-permute-start | bytes 540680 | tf_op jit(solution)/shard_map/ppermute | solution.py:671
  114.6 11.5 %collective-permute-start.28 = (f32[4,96,256]{2,1,0:T(8,128)S(1)}, f32[4,96,256]{2,1,0:T(8,128)S(1)}, u32[]{:S(2)}, u32[]{:S(2)}) collective-permute-start(f32[4,96,256]{2,1,0:T(8,128)S(1)} %get-tuple-element.201.refs_0_), channel_id=1, source_target_pairs={{0,16},{4,20},{8,24},{12,28},{16,0},{20,4},{24,8},{28,12},{1,17},{... | collective-permute-start | bytes 1179656 | tf_op jit(solution)/shard_map/ppermute | solution.py:671
  116.3 8.7 %collective-permute-start.29 = (f32[4,88,256]{2,1,0:T(8,128)S(1)}, f32[4,88,256]{2,1,0:T(8,128)S(1)}, u32[]{:S(2)}, u32[]{:S(2)}) collective-permute-start(f32[4,88,256]{2,1,0:T(8,128)S(1)} %get-tuple-element.202.refs_1_), channel_id=1, source_target_pairs={{0,1},{1,0},{2,3},{3,2},{4,5},{5,4},{6,7},{7,6},{8,9},{9,8},{10,11... | collective-permute-start | bytes 1081352 | tf_op jit(solution)/shard_map/ppermute | solution.py:671
  118.0 8.1 %collective-permute-start.30 = (f32[4,88,256]{2,1,0:T(8,128)S(1)}, f32[4,88,256]{2,1,0:T(8,128)S(1)}, u32[]{:S(2)}, u32[]{:S(2)}) collective-permute-start(f32[4,88,256]{2,1,0:T(8,128)S(1)} %get-tuple-element.203.refs_2_), channel_id=1, source_target_pairs={{0,8},{4,12},{8,0},{12,4},{16,24},{20,28},{24,16},{28,20},{1,9},{5... | collective-permute-start | bytes 1081352 | tf_op jit(solution)/shard_map/ppermute | solution.py:671
  126.4 4.5 %collective-permute-start.31 = (f32[8,272,256]{2,1,0:T(8,128)S(1)}, f32[8,272,256]{2,1,0:T(8,128)S(1)}, u32[]{:S(2)}, u32[]{:S(2)}) collective-permute-start(f32[8,272,256]{2,1,0:T(8,128)S(1)} %get-tuple-element.204.near_ref), channel_id=1, source_target_pairs={{0,4},{4,0},{8,12},{12,8},{16,20},{20,16},{24,28},{28,24},{1,5},{5... | collective-permute-start | bytes 6684680 | tf_op jit(solution)/shard_map/ppermute | solution.py:671
  126.4 20.0 %collective-permute-start.32 = (f32[8,96,256]{2,1,0:T(8,128)S(1)}, f32[8,96,256]{2,1,0:T(8,128)S(1)}, u32[]{:S(2)}, u32[]{:S(2)}) collective-permute-start(f32[8,96,256]{2,1,0:T(8,128)S(1)} %get-tuple-element.205), channel_id=1, source_target_pairs={{0,8},{4,12},{8,0},{12,4},{16,24},{20,28},{24,16},{28,20},{1,9},{5... | collective-permute-start | bytes 2359304 | tf_op jit(solution)/shard_map/ppermute | solution.py:671
  127.1 18.2 %collective-permute-start.33 = (f32[8,88,256]{2,1,0:T(8,128)S(1)}, f32[8,88,256]{2,1,0:T(8,128)S(1)}, u32[]{:S(2)}, u32[]{:S(2)}) collective-permute-start(f32[8,88,256]{2,1,0:T(8,128)S(1)} %get-tuple-element.206), channel_id=1, source_target_pairs={{0,16},{4,20},{8,24},{12,28},{16,0},{20,4},{24,8},{28,12},{1,17},{... | collective-permute-start | bytes 2162696 | tf_op jit(solution)/shard_map/ppermute | solution.py:671
  128.3 17.9 %collective-permute-start.34 = (f32[8,88,256]{2,1,0:T(8,128)S(1)}, f32[8,88,256]{2,1,0:T(8,128)S(1)}, u32[]{:S(2)}, u32[]{:S(2)}) collective-permute-start(f32[8,88,256]{2,1,0:T(8,128)S(1)} %get-tuple-element.207), channel_id=1, source_target_pairs={{0,1},{1,0},{2,3},{3,2},{4,5},{5,4},{6,7},{7,6},{8,9},{9,8},{10,11... | collective-permute-start | bytes 2162696 | tf_op jit(solution)/shard_map/ppermute | solution.py:671
  (17 other events, 208.0 us)

commit v9 on v8

--- a/solution.py
+++ b/solution.py
@@ -691,7 +691,7 @@
     bits = sub_bits + lax.axis_size("blk").bit_length() - 2
     x, y, z, far = sub_bits, sub_bits + 1, 0, 1
     rest = [p for p in range(bits) if p not in (x, y, z, far)]
-    return [[x, y, z, far] + rest, [y, z, x, far] + rest, [z, x, y, far] + rest]
+    return [[x, y, z, far] + rest, [y, z, x, far] + rest, [z, x, far, y] + rest]
 
 
 def plane_orders(sub_bits, bits):
@@ -746,23 +746,23 @@
         spot, hub_emb.reshape(features, hub_count), hub_ids, relation_emb.reshape(features, rel_count), relations, chunks
     )
     far_ids, hub_rows = in_turn(far_ids, hub_rows)
-    keeps, fars = [], []
+    keeps, sends = [], []
     for b in range(buckets - 1):
         if b > 0:
-            right = from_behind(right, "blk", 1)
             right, right_sums = right[:features], right[features : features + 1]
         left, left_sums, right, keep, send = bucket_step(
             b, spot, heads, tails, negatives, left, left_sums, right, right_sums, rel_rows[b], hub_rows[b]
         )
+        right = from_behind(right, "blk", 1)
         keeps.append(keep)
-        fars.append(other_core(send))
+        sends.append(send)
     last = buckets - 1
     query_grad, hub_keep, hub_send = hub_step(
         last, negatives.shape[1], spot, heads, left, rel_rows[last], hub_rows[last]
     )
-    right, hub_send = in_turn(right, hub_send)
+    sends, hub_send = in_turn(sends, hub_send)
     hub_far = other_core(hub_send)
-    right = from_behind(right, "blk", 1)
+    fars = [other_core(x) for x in sends]
     grads = lambda early, late, lanes: [(x, lanes) for x in early] + [(late, (0, late.shape[1]))]
     groups, where = grouped(orders, 0, heights)
     parts = chunk_columns(

time: 154 us -> 149 us (0.968)
  waiting for transfers between devices: 66.8 us -> 61.6 us
    ppermute x3, waiting for transfers between devices: 8.61 us -> 0.19 us  [flipped_by(): lax.ppermute(x, axis, [(i, i ^ offset) for i in range(lax.axis_size(axis))])]
    ppermute x34 -> x36, waiting for transfers between devices: 58.1 us -> 61.5 us  [flipped(): lax.ppermute(x, axis, [(i, i ^ 1 << bit) for i in range(lax.axis_size(axi...]
    ppermute x34 -> x36, starting transfers between devices: 35.9 us -> 35.7 us  [flipped(): lax.ppermute(x, axis, [(i, i ^ 1 << bit) for i in range(lax.axis_size(axi...]
  transfers between devices with their start and end apart: 38 -> 40, of which waited for: 18 -> 18; matrix products, arithmetic and copies ran while one was open for 0% -> 0% of each run, Pallas kernels for 20% -> 22%
where the time goes in v9:
time: 149 us
  waiting for transfers between devices  61.6 us (41%)
  Pallas kernels  43.3 us (29%)
  starting transfers between devices  41.1 us (28%)
    ppermute x36, waiting for transfers between devices, flipped(): lax.ppermute(x, axis, [(i, i ^ 1 << bit) for i in range(lax.axis_size(axi...  61.5 us
    ppermute x36, starting transfers between devices, flipped(): lax.ppermute(x, axis, [(i, i ^ 1 << bit) for i in range(lax.axis_size(axi...  35.7 us
    pallas_call x1, Pallas kernels, gather_rows(): pl.pallas_call(functools.partial(gather_kernel, hub_steps, rel_steps), in...  10 us
    pallas_call x4, Pallas kernels, placed(): pl.pallas_call(kernel, in_specs=[SMEM] + [VMEM] * (1 + len(fars)) + [HBM]...  9.34 us
    pallas_call x2, Pallas kernels, chunk_columns(): pl.pallas_call(functools.partial(kernel, grad_lanes), in_specs=[SMEM] + [...  7.99 us
    pallas_call x1, Pallas kernels, bucket_step(): pl.pallas_call(functools.partial(bucket_kernel, bucket), in_specs=[SMEM]...  5.58 us
    pallas_call x1, Pallas kernels, tables_step(): pl.pallas_call(functools.partial(tables_kernel, bucket, hubs), in_specs=[...  5.42 us
    ppermute x3, starting transfers between devices, flipped_by(): lax.ppermute(x, axis, [(i, i ^ offset) for i in range(lax.axis_size(axis))])  4.72 us
  transfers between devices with their start and end apart: 40, of which 18 were waited for; matrix products, arithmetic and copies ran while one was open for 0% of the time, Pallas kernels for 22%

profile of v9, /device:TPU:0, one launch (start us, length us, event | category | flops | bytes accessed | tf_op | source)
XLA Modules:
  0.0 148.7 jit_solution(9714192101763135456)
XLA Ops:
  2.7 10.0 %shard_map.156 = (f32[400,256]{1,0:T(8,128)S(1)}, f32[400,256]{1,0:T(8,128)S(1)}, f32[400,512]{1,0:T(8,128)S(1)}, f32[400,512]{1,0:T(8,128)S(1)}, s32[2]{0:T(128...) custom-call(s32[2]{0:T(128)S(1)} %pad_add_fusion.spot_ref, s32[2,256]{1,0:T(2,128)S(1)} %copy-done.7, ...), custom_call_target="tpu_custom_call" | custom-call | flops 10000 | bytes 10000 | tf_op jit(solution)/shard_map/pallas_call | solution.py:135
  12.9 5.6 %shard_map.157 = (f32[400,512]{1,0:T(8,128)S(1)}, f32[1,512]{1,0:T(1,128)S(1)}, f32[408,512]{1,0:T(8,128)S(1)}, f32[200,768]{1,0:T(8,128)S(1)}, f32[200,768]{1,0:T(8,128)S(1)}) custom-call(s32[2]{0:T(128)S(1)} %get-tuple-element.113.core_ref.spot_ref, s32[2,512]{1,0:T(2,128)S(1)} %copy-done.2, s32[2,512]{1,0:T(2,128)S(1)} %copy-done.4, ...), custom_call_target="tpu_custom_call" | custom-call | flops 10000 | bytes 10000 | tf_op jit(solution)/shard_map/pallas_call | solution.py:563
  19.1 2.7 %shard_map.158 = (f32[400,512]{1,0:T(8,128)S(1)}, f32[200,256]{1,0:T(8,128)S(1)}, f32[200,256]{1,0:T(8,128)S(1)}) custom-call(s32[2]{0:T(128)S(1)} %get-tuple-element.113.core_ref.spot_ref, s32[2,512]{1,0:T(2,128)S(1)} %copy-done.2, f32[400,512]{1,0:T(8,128)S(1)} %get-tuple-element.118.left_ref, f32[400,512]{1,0:T(8,128)S(1)} %get-tuple-element.119.rel_ref, ...), custom_call_target="tpu_custom_call" | custom-call | flops 10000 | bytes 10000 | tf_op jit(solution)/shard_map/pallas_call | solution.py:604
  21.8 2.8 %collective-permute-start.3 = (f32[200,768]{1,0:T(8,128)S(1)}, f32[200,768]{1,0:T(8,128)S(1)}, u32[]{:S(2)}, u32[]{:S(2)}) collective-permute-start(f32[200,768]{1,0:T(8,128)S(1)} %get-tuple-element.131), channel_id=1, source_target_pairs={{0,4},{4,0},{8,12},{12,8},{16,20},{20,16},{24,28},{28,24},{1,5},{5... | collective-permute-start | bytes 1843208 | tf_op jit(solution)/shard_map/ppermute | solution.py:671
  24.7 1.9 %collective-permute-done.4.refs_5_ = f32[200,256]{1,0:T(8,128)S(1)} collective-permute-done((f32[200,256]{1,0:T(8,128)S(1)}, f32[200,256]{1,0:T(8,128)S(1)}, u32[]{:S(2)}, u32[]{:S(2)}) %collective-permute-start.4) | collective-permute-done | bytes 204832 | tf_op jit(solution)/shard_map/ppermute | solution.py:671
  26.6 4.3 %shard_map.160 = (f32[8,72,256]{2,1,0:T(8,128)S(1)}, f32[8,64,256]{2,1,0:T(8,128)S(1)}, f32[8,64,256]{2,1,0:T(8,128)S(1)}, f32[8,72,256]{2,1,0:T(8,128)S(1)}, f3...) custom-call(s32[2]{0:T(128)S(1)} %get-tuple-element.113.core_ref.spot_ref, s32[2,256]{1,0:T(2,128)S(1)} %copy-done.7, ...), custom_call_target="tpu_custom_call" | custom-call | flops 10000 | bytes 10000 | tf_op jit(solution)/shard_map/pallas_call | solution.py:273
  32.8 1.8 %collective-permute-start.8 = (f32[8,64,256]{2,1,0:T(8,128)S(1)}, f32[8,64,256]{2,1,0:T(8,128)S(1)}, u32[]{:S(2)}, u32[]{:S(2)}) collective-permute-start(f32[8,64,256]{2,1,0:T(8,128)S(1)} %get-tuple-element.143), channel_id=1, source_target_pairs={{0,1},{1,0},{2,3},{3,2},{4,5},{5,4},{6,7},{7,6},{8,9},{9,8},{10,11... | collective-permute-start | bytes 1572872 | tf_op jit(solution)/shard_map/ppermute | solution.py:671
  34.6 5.4 %shard_map.159 = (f32[400,512]{1,0:T(8,128)}, f32[400,512]{1,0:T(8,128)}, f32[200,512]{1,0:T(8,128)S(1)}, f32[200,512]{1,0:T(8,128)S(1)}) custom-call(s32[2]{0:T(128)S(1)} %get-tuple-element.113.core_ref.spot_ref, s32[2,512]{1,0:T(2,128)S(1)} %copy-done.2, s32[2,512]{1,0:T(2,128)S(1)} %copy-done.4, s32[2,1024]{1,0:T(2,128)S(1)} %copy-done.3, ...), custom_call_target="tpu_custom_call" | custom-call | flops 10000 | bytes 10000 | tf_op jit(solution)/shard_map/pallas_call | solution.py:654
  40.0 1.7 %collective-permute-done.5.refs_5_ = f32[200,512]{1,0:T(8,128)S(1)} collective-permute-done((f32[200,512]{1,0:T(8,128)S(1)}, f32[200,512]{1,0:T(8,128)S(1)}, u32[]{:S(2)}, u32[]{:S(2)}) %collective-permute-start.5) | collective-permute-done | bytes 409632 | tf_op jit(solution)/shard_map/ppermute | solution.py:671
  41.8 3.6 %shard_map.161 = (f32[8,40,256]{2,1,0:T(8,128)S(1)}, f32[8,32,256]{2,1,0:T(8,128)S(1)}, f32[8,40,256]{2,1,0:T(8,128)S(1)}, f32[8,32,256]{2,1,0:T(8,128)S(1)}) custom-call(s32[2]{0:T(128)S(1)} %get-tuple-element.113.core_ref.spot_ref, s32[2,512]{1,0:T(2,128)S(1)} %copy-done.5, s32[2,512]{1,0:T(2,128)S(1)} %collective-permute-done.1.refs_1_, ...), custom_call_target="tpu_custom_call" | custom-call | flops 10000 | bytes 10000 | tf_op jit(solution)/shard_map/pallas_call | solution.py:273
  45.4 1.5 %collective-permute-start.9 = (f32[8,40,256]{2,1,0:T(8,128)S(1)}, f32[8,40,256]{2,1,0:T(8,128)S(1)}, u32[]{:S(2)}, u32[]{:S(2)}) collective-permute-start(f32[8,40,256]{2,1,0:T(8,128)S(1)} %get-tuple-element.150), channel_id=1, source_target_pairs={{0,8},{4,12},{8,0},{12,4},{16,24},{20,28},{24,16},{28,20},{1,9},{5... | collective-permute-start | bytes 983048 | tf_op jit(solution)/shard_map/ppermute | solution.py:671
  50.5 1.5 collective-permute-start.13
  52.0 9.6 %collective-permute-done.10.refs_3_ = f32[8,32,256]{2,1,0:T(8,128)S(1)} collective-permute-done((f32[8,32,256]{2,1,0:T(8,128)S(1)}, f32[8,32,256]{2,1,0:T(8,128)S(1)}, u32[]{:S(2)}, u32[]{:S(2)}) %collective-permute-start.10) | collective-permute-done | bytes 262176 | tf_op jit(solution)/shard_map/ppermute | solution.py:671
  62.7 1.6 %collective-permute-start.16 = (f32[2,72,256]{2,1,0:T(8,128)S(1)}, f32[2,72,256]{2,1,0:T(8,128)S(1)}, u32[]{:S(2)}, u32[]{:S(2)}) collective-permute-start(f32[2,72,256]{2,1,0:T(8,128)S(1)} %get-tuple-element.180), channel_id=1, source_target_pairs={{0,1},{1,0},{2,3},{3,2},{4,5},{5,4},{6,7},{7,6},{8,9},{9,8},{10,11... | collective-permute-start | bytes 442376 | tf_op jit(solution)/shard_map/ppermute | solution.py:671
  66.3 2.6 %collective-permute-start.18 = (f32[2,64,256]{2,1,0:T(8,128)S(1)}, f32[2,64,256]{2,1,0:T(8,128)S(1)}, u32[]{:S(2)}, u32[]{:S(2)}) collective-permute-start(f32[2,64,256]{2,1,0:T(8,128)S(1)} %get-tuple-element.182), channel_id=1, source_target_pairs={{0,2},{1,3},{2,0},{3,1},{4,6},{5,7},{6,4},{7,5},{8,10},{9,11},{10,... | collective-permute-start | bytes 393224 | tf_op jit(solution)/shard_map/ppermute | solution.py:671
  70.7 5.4 %collective-permute-done.18.refs_5_ = f32[2,64,256]{2,1,0:T(8,128)S(1)} collective-permute-done((f32[2,64,256]{2,1,0:T(8,128)S(1)}, f32[2,64,256]{2,1,0:T(8,128)S(1)}, u32[]{:S(2)}, u32[]{:S(2)}) %collective-permute-start.18) | collective-permute-done | bytes 131104 | tf_op jit(solution)/shard_map/ppermute | solution.py:671
  76.2 2.4 %collective-permute-start.21 = (f32[1,72,256]{2,1,0:T(8,128)S(1)}, f32[1,72,256]{2,1,0:T(8,128)S(1)}, u32[]{:S(2)}, u32[]{:S(2)}) collective-permute-start(f32[1,72,256]{2,1,0:T(8,128)S(1)} %get-tuple-element.192), channel_id=1, source_target_pairs={{0,1},{1,0},{2,3},{3,2},{4,5},{5,4},{6,7},{7,6},{8,9},{9,8},{10,11... | collective-permute-start | bytes 221192 | tf_op jit(solution)/shard_map/ppermute | solution.py:675
  79.1 1.8 %collective-permute-start.23 = (f32[1,72,256]{2,1,0:T(8,128)S(1)}, f32[1,72,256]{2,1,0:T(8,128)S(1)}, u32[]{:S(2)}, u32[]{:S(2)}) collective-permute-start(f32[1,72,256]{2,1,0:T(8,128)S(1)} %get-tuple-element.194), channel_id=1, source_target_pairs={{0,3},{1,2},{2,1},{3,0},{4,7},{5,6},{6,5},{7,4},{8,11},{9,10},{10,... | collective-permute-start | bytes 221192 | tf_op jit(solution)/shard_map/ppermute | solution.py:675
  80.9 1.6 %collective-permute-start.20 = (f32[1,64,256]{2,1,0:T(8,128)S(1)}, f32[1,64,256]{2,1,0:T(8,128)S(1)}, u32[]{:S(2)}, u32[]{:S(2)}) collective-permute-start(f32[1,64,256]{2,1,0:T(8,128)S(1)} %get-tuple-element.190), channel_id=1, source_target_pairs={{0,16},{4,20},{8,24},{12,28},{16,0},{20,4},{24,8},{28,12},{1,17},{... | collective-permute-start | bytes 196616 | tf_op jit(solution)/shard_map/ppermute | solution.py:671
  82.5 2.7 %collective-permute-done.20.refs_4_ = f32[1,64,256]{2,1,0:T(8,128)S(1)} collective-permute-done((f32[1,64,256]{2,1,0:T(8,128)S(1)}, f32[1,64,256]{2,1,0:T(8,128)S(1)}, u32[]{:S(2)}, u32[]{:S(2)}) %collective-permute-start.20) | collective-permute-done | bytes 65568 | tf_op jit(solution)/shard_map/ppermute | solution.py:671
  88.0 2.2 %collective-permute-start.25 = (f32[1,184,256]{2,1,0:T(8,128)S(1)}, f32[1,184,256]{2,1,0:T(8,128)S(1)}, u32[]{:S(2)}, u32[]{:S(2)}) collective-permute-start(f32[1,184,256]{2,1,0:T(8,128)S(1)} %get-tuple-element.202.refs_0_), channel_id=1, source_target_pairs={{0,2},{1,3},{2,0},{3,1},{4,6},{5,7},{6,4},{7,5},{8,10},{9,11},{10,... | collective-permute-start | bytes 565256 | tf_op jit(solution)/shard_map/ppermute | solution.py:671
  91.4 3.3 %collective-permute-done.26.refs_3_ = f32[1,88,256]{2,1,0:T(8,128)S(1)} collective-permute-done((f32[1,88,256]{2,1,0:T(8,128)S(1)}, f32[1,88,256]{2,1,0:T(8,128)S(1)}, u32[]{:S(2)}, u32[]{:S(2)}) %collective-permute-start.26) | collective-permute-done | bytes 90144 | tf_op jit(solution)/shard_map/ppermute | solution.py:671
  94.7 5.1 %collective-permute-done.25.refs_2_ = f32[1,184,256]{2,1,0:T(8,128)S(1)} collective-permute-done((f32[1,184,256]{2,1,0:T(8,128)S(1)}, f32[1,184,256]{2,1,0:T(8,128)S(1)}, u32[]{:S(2)}, u32[]{:S(2)}) %collective-permute-start.25) | collective-permute-done | bytes 188448 | tf_op jit(solution)/shard_map/ppermute | solution.py:671
  101.4 2.7 %collective-permute-start.29 = (f32[2,88,256]{2,1,0:T(8,128)S(1)}, f32[2,88,256]{2,1,0:T(8,128)S(1)}, u32[]{:S(2)}, u32[]{:S(2)}) collective-permute-start(f32[2,88,256]{2,1,0:T(8,128)S(1)} %get-tuple-element.206.refs_2_), channel_id=1, source_target_pairs={{0,2},{1,3},{2,0},{3,1},{4,6},{5,7},{6,4},{7,5},{8,10},{9,11},{10,... | collective-permute-start | bytes 540680 | tf_op jit(solution)/shard_map/ppermute | solution.py:671
  104.0 1.8 %collective-permute-done.28.refs_4_ = f32[2,88,256]{2,1,0:T(8,128)S(1)} collective-permute-done((f32[2,88,256]{2,1,0:T(8,128)S(1)}, f32[2,88,256]{2,1,0:T(8,128)S(1)}, u32[]{:S(2)}, u32[]{:S(2)}) %collective-permute-start.28) | collective-permute-done | bytes 180256 | tf_op jit(solution)/shard_map/ppermute | solution.py:671
  105.8 6.0 %collective-permute-done.29.refs_5_ = f32[2,88,256]{2,1,0:T(8,128)S(1)} collective-permute-done((f32[2,88,256]{2,1,0:T(8,128)S(1)}, f32[2,88,256]{2,1,0:T(8,128)S(1)}, u32[]{:S(2)}, u32[]{:S(2)}) %collective-permute-start.29) | collective-permute-done | bytes 180256 | tf_op jit(solution)/shard_map/ppermute | solution.py:671
  114.0 6.1 %collective-permute-done.31.refs_4_ = f32[4,88,256]{2,1,0:T(8,128)S(1)} collective-permute-done((f32[4,88,256]{2,1,0:T(8,128)S(1)}, f32[4,88,256]{2,1,0:T(8,128)S(1)}, u32[]{:S(2)}, u32[]{:S(2)}) %collective-permute-start.31) | collective-permute-done | bytes 360480 | tf_op jit(solution)/shard_map/ppermute | solution.py:671
  124.4 1.9 %shard_map.172.refs_0_ = f32[2,200,4096]{2,1,0:T(8,128)} custom-call(s32[2]{0:T(128)S(1)} %get-tuple-element.113.core_ref.spot_ref, f32[8,272,256]{2,1,0:T(8,128)S(1)} %get-tuple-element.210.near_ref), custom_call_target="tpu_custom_call" | custom-call | bytes 3276800 | tf_op jit(solution)/shard_map/pallas_call | solution.py:474
  126.3 1.9 %shard_map.173.refs_3_ = f32[2,200,4096]{2,1,0:T(8,128)} custom-call(s32[2]{0:T(128)S(1)} %get-tuple-element.113.core_ref.spot_ref, f32[8,272,256]{2,1,0:T(8,128)S(1)} %collective-permute-done.33.near_ref, f32[2,200,4096]{2,1,0:T(8,128)} %shard_map.172.refs_0_), custom_call_target="tpu_custom_call", output_to_operand_aliasing={{}: (2, {})} | custom-call | bytes 3276800 | tf_op jit(solution)/shard_map/pallas_call | solution.py:474
  128.3 12.1 %collective-permute-done.35.refs_1_ = f32[8,88,256]{2,1,0:T(8,128)S(1)} collective-permute-done((f32[8,88,256]{2,1,0:T(8,128)S(1)}, f32[8,88,256]{2,1,0:T(8,128)S(1)}, u32[]{:S(2)}, u32[]{:S(2)}) %collective-permute-start.35) | collective-permute-done | bytes 720928 | tf_op jit(solution)/shard_map/ppermute | solution.py:671
  141.9 2.7 %shard_map.174 = (f32[2,200,4096]{2,1,0:T(8,128)}, f32[2,200,1280]{2,1,0:T(8,128)}) custom-call(s32[2]{0:T(128)S(1)} %get-tuple-element.113.core_ref.spot_ref, f32[8,272,256]{2,1,0:T(8,128)S(1)} %get-tuple-element.210.near_ref, f32[8,96,256]{2,1,0:T(8,128)S(1)} %collective-permute-done.34.refs_0_, ...), custom_call_target="tpu_custom_call", output_to_operand_aliasing={{0}: (5, {})} | custom-call | bytes 3276800 | tf_op jit(solution)/shard_map/pallas_call | solution.py:474
  145.7 2.8 %shard_map.175 = (f32[2,200,4096]{2,1,0:T(8,128)}, f32[2,200,1280]{2,1,0:T(8,128)}) custom-call(s32[2]{0:T(128)S(1)} %get-tuple-element.113.core_ref.spot_ref, f32[8,272,256]{2,1,0:T(8,128)S(1)} %collective-permute-done.33.near_ref, f32[8,96,256]{2,1,0:T(8,128)S(1)} %collective-permute-done.37.refs_0_, ...), custom_call_target="tpu_custom_call", output_to_operand_aliasing={{0}: (5, {}), {1}: (6, {})} | custom-call | bytes 3276800 | tf_op jit(solution)/shard_map/pallas_call | solution.py:474
  (92 shorter events, 28.4 us)
Async XLA Ops:
  0.7 12.1 %collective-permute-start = (s32[2,256]{1,0:T(2,128)}, s32[2,256]{1,0:T(2,128)S(1)}, u32[]{:S(2)}, u32[]{:S(2)}) collective-permute-start(s32[2,256]{1,0:T(2,128)} %refs_0_.2), channel_id=1, source_target_pairs={{0,4},{4,0},{8,12},{12,8},{16,20},{20,16},{24,28},{28,24},{1,5},{5... | collective-permute-start | bytes 6152 | tf_op jit(solution)/shard_map/ppermute | solution.py:671
  1.2 11.6 %collective-permute-start.1 = (s32[2,512]{1,0:T(2,128)}, s32[2,512]{1,0:T(2,128)S(1)}, u32[]{:S(2)}, u32[]{:S(2)}) collective-permute-start(s32[2,512]{1,0:T(2,128)} %refs_0_.3), channel_id=1, source_target_pairs={{0,4},{4,0},{8,12},{12,8},{16,20},{20,16},{24,28},{28,24},{1,5},{5... | collective-permute-start | bytes 12296 | tf_op jit(solution)/shard_map/ppermute | solution.py:671
  18.5 16.2 %collective-permute-start.2 = (f32[408,512]{1,0:T(8,128)S(1)}, f32[408,512]{1,0:T(8,128)S(1)}, u32[]{:S(2)}, u32[]{:S(2)}) collective-permute-start(f32[408,512]{1,0:T(8,128)S(1)} %get-tuple-element.123), channel_id=1, source_target_pairs={{0,4},{4,8},{8,12},{12,16},{16,20},{20,24},{24,28},{28,0},{1,5},{5... | collective-permute-start | bytes 2506760 | tf_op jit(solution)/shard_map/ppermute | solution.py:667
  21.8 4.7 %collective-permute-start.3 = (f32[200,768]{1,0:T(8,128)S(1)}, f32[200,768]{1,0:T(8,128)S(1)}, u32[]{:S(2)}, u32[]{:S(2)}) collective-permute-start(f32[200,768]{1,0:T(8,128)S(1)} %get-tuple-element.131), channel_id=1, source_target_pairs={{0,4},{4,0},{8,12},{12,8},{16,20},{20,16},{24,28},{28,24},{1,5},{5... | collective-permute-start | bytes 1843208 | tf_op jit(solution)/shard_map/ppermute | solution.py:671
  30.9 16.1 %collective-permute-start.6 = (f32[8,72,256]{2,1,0:T(8,128)S(1)}, f32[8,72,256]{2,1,0:T(8,128)S(1)}, u32[]{:S(2)}, u32[]{:S(2)}) collective-permute-start(f32[8,72,256]{2,1,0:T(8,128)S(1)} %get-tuple-element.141), channel_id=1, source_target_pairs={{0,8},{4,12},{8,0},{12,4},{16,24},{20,28},{24,16},{28,20},{1,9},{5... | collective-permute-start | bytes 1769480 | tf_op jit(solution)/shard_map/ppermute | solution.py:671
  32.4 14.6 %collective-permute-start.7 = (f32[8,64,256]{2,1,0:T(8,128)S(1)}, f32[8,64,256]{2,1,0:T(8,128)S(1)}, u32[]{:S(2)}, u32[]{:S(2)}) collective-permute-start(f32[8,64,256]{2,1,0:T(8,128)S(1)} %get-tuple-element.142), channel_id=1, source_target_pairs={{0,16},{4,20},{8,24},{12,28},{16,0},{20,4},{24,8},{28,12},{1,17},{... | collective-permute-start | bytes 1572872 | tf_op jit(solution)/shard_map/ppermute | solution.py:671
  32.8 14.2 %collective-permute-start.8 = (f32[8,64,256]{2,1,0:T(8,128)S(1)}, f32[8,64,256]{2,1,0:T(8,128)S(1)}, u32[]{:S(2)}, u32[]{:S(2)}) collective-permute-start(f32[8,64,256]{2,1,0:T(8,128)S(1)} %get-tuple-element.143), channel_id=1, source_target_pairs={{0,1},{1,0},{2,3},{3,2},{4,5},{5,4},{6,7},{7,6},{8,9},{9,8},{10,11... | collective-permute-start | bytes 1572872 | tf_op jit(solution)/shard_map/ppermute | solution.py:671
  45.4 16.2 %collective-permute-start.9 = (f32[8,40,256]{2,1,0:T(8,128)S(1)}, f32[8,40,256]{2,1,0:T(8,128)S(1)}, u32[]{:S(2)}, u32[]{:S(2)}) collective-permute-start(f32[8,40,256]{2,1,0:T(8,128)S(1)} %get-tuple-element.150), channel_id=1, source_target_pairs={{0,8},{4,12},{8,0},{12,4},{16,24},{20,28},{24,16},{28,20},{1,9},{5... | collective-permute-start | bytes 983048 | tf_op jit(solution)/shard_map/ppermute | solution.py:671
  47.2 15.4 %collective-permute-start.11 = (f32[4,72,256]{2,1,0:T(8,128)S(1)}, f32[4,72,256]{2,1,0:T(8,128)S(1)}, u32[]{:S(2)}, u32[]{:S(2)}) collective-permute-start(f32[4,72,256]{2,1,0:T(8,128)S(1)} %get-tuple-element.161), channel_id=1, source_target_pairs={{0,16},{4,20},{8,24},{12,28},{16,0},{20,4},{24,8},{28,12},{1,17},{... | collective-permute-start | bytes 884744 | tf_op jit(solution)/shard_map/ppermute | solution.py:671
  48.3 13.3 %collective-permute-start.10 = (f32[8,32,256]{2,1,0:T(8,128)S(1)}, f32[8,32,256]{2,1,0:T(8,128)S(1)}, u32[]{:S(2)}, u32[]{:S(2)}) collective-permute-start(f32[8,32,256]{2,1,0:T(8,128)S(1)} %get-tuple-element.151), channel_id=1, source_target_pairs={{0,16},{4,20},{8,24},{12,28},{16,0},{20,4},{24,8},{28,12},{1,17},{... | collective-permute-start | bytes 786440 | tf_op jit(solution)/shard_map/ppermute | solution.py:671
  49.3 13.3 %collective-permute-start.12 = (f32[4,64,256]{2,1,0:T(8,128)S(1)}, f32[4,64,256]{2,1,0:T(8,128)S(1)}, u32[]{:S(2)}, u32[]{:S(2)}) collective-permute-start(f32[4,64,256]{2,1,0:T(8,128)S(1)} %get-tuple-element.162), channel_id=1, source_target_pairs={{0,1},{1,0},{2,3},{3,2},{4,5},{5,4},{6,7},{7,6},{8,9},{9,8},{10,11... | collective-permute-start | bytes 786440 | tf_op jit(solution)/shard_map/ppermute | solution.py:671
  50.5 12.1 %collective-permute-start.13 = (f32[4,64,256]{2,1,0:T(8,128)S(1)}, f32[4,64,256]{2,1,0:T(8,128)S(1)}, u32[]{:S(2)}, u32[]{:S(2)}) collective-permute-start(f32[4,64,256]{2,1,0:T(8,128)S(1)} %get-tuple-element.163), channel_id=1, source_target_pairs={{0,8},{4,12},{8,0},{12,4},{16,24},{20,28},{24,16},{28,20},{1,9},{5... | collective-permute-start | bytes 786440 | tf_op jit(solution)/shard_map/ppermute | solution.py:671
  61.7 7.6 %collective-permute-start.14 = (f32[4,40,256]{2,1,0:T(8,128)S(1)}, f32[4,40,256]{2,1,0:T(8,128)S(1)}, u32[]{:S(2)}, u32[]{:S(2)}) collective-permute-start(f32[4,40,256]{2,1,0:T(8,128)S(1)} %get-tuple-element.170), channel_id=1, source_target_pairs={{0,16},{4,20},{8,24},{12,28},{16,0},{20,4},{24,8},{28,12},{1,17},{... | collective-permute-start | bytes 491528 | tf_op jit(solution)/shard_map/ppermute | solution.py:671
  62.7 13.4 %collective-permute-start.16 = (f32[2,72,256]{2,1,0:T(8,128)S(1)}, f32[2,72,256]{2,1,0:T(8,128)S(1)}, u32[]{:S(2)}, u32[]{:S(2)}) collective-permute-start(f32[2,72,256]{2,1,0:T(8,128)S(1)} %get-tuple-element.180), channel_id=1, source_target_pairs={{0,1},{1,0},{2,3},{3,2},{4,5},{5,4},{6,7},{7,6},{8,9},{9,8},{10,11... | collective-permute-start | bytes 442376 | tf_op jit(solution)/shard_map/ppermute | solution.py:671
  64.3 5.0 %collective-permute-start.15 = (f32[4,32,256]{2,1,0:T(8,128)S(1)}, f32[4,32,256]{2,1,0:T(8,128)S(1)}, u32[]{:S(2)}, u32[]{:S(2)}) collective-permute-start(f32[4,32,256]{2,1,0:T(8,128)S(1)} %get-tuple-element.171), channel_id=1, source_target_pairs={{0,8},{4,12},{8,0},{12,4},{16,24},{20,28},{24,16},{28,20},{1,9},{5... | collective-permute-start | bytes 393224 | tf_op jit(solution)/shard_map/ppermute | solution.py:671
  64.9 5.8 %collective-permute-start.17 = (f32[2,64,256]{2,1,0:T(8,128)S(1)}, f32[2,64,256]{2,1,0:T(8,128)S(1)}, u32[]{:S(2)}, u32[]{:S(2)}) collective-permute-start(f32[2,64,256]{2,1,0:T(8,128)S(1)} %get-tuple-element.181), channel_id=1, source_target_pairs={{0,8},{4,12},{8,0},{12,4},{16,24},{20,28},{24,16},{28,20},{1,9},{5... | collective-permute-start | bytes 393224 | tf_op jit(solution)/shard_map/ppermute | solution.py:671
  66.3 9.7 %collective-permute-start.18 = (f32[2,64,256]{2,1,0:T(8,128)S(1)}, f32[2,64,256]{2,1,0:T(8,128)S(1)}, u32[]{:S(2)}, u32[]{:S(2)}) collective-permute-start(f32[2,64,256]{2,1,0:T(8,128)S(1)} %get-tuple-element.182), channel_id=1, source_target_pairs={{0,2},{1,3},{2,0},{3,1},{4,6},{5,7},{6,4},{7,5},{8,10},{9,11},{10,... | collective-permute-start | bytes 393224 | tf_op jit(solution)/shard_map/ppermute | solution.py:671
  76.1 9.3 %collective-permute-start.19 = (f32[1,136,256]{2,1,0:T(8,128)S(1)}, f32[1,136,256]{2,1,0:T(8,128)S(1)}, u32[]{:S(2)}, u32[]{:S(2)}) collective-permute-start(f32[1,136,256]{2,1,0:T(8,128)S(1)} %get-tuple-element.189), channel_id=1, source_target_pairs={{0,2},{1,3},{2,0},{3,1},{4,6},{5,7},{6,4},{7,5},{8,10},{9,11},{10,... | collective-permute-start | bytes 417800 | tf_op jit(solution)/shard_map/ppermute | solution.py:671
  76.2 9.0 %collective-permute-start.21 = (f32[1,72,256]{2,1,0:T(8,128)S(1)}, f32[1,72,256]{2,1,0:T(8,128)S(1)}, u32[]{:S(2)}, u32[]{:S(2)}) collective-permute-start(f32[1,72,256]{2,1,0:T(8,128)S(1)} %get-tuple-element.192), channel_id=1, source_target_pairs={{0,1},{1,0},{2,3},{3,2},{4,5},{5,4},{6,7},{7,6},{8,9},{9,8},{10,11... | collective-permute-start | bytes 221192 | tf_op jit(solution)/shard_map/ppermute | solution.py:675
  78.5 6.6 %collective-permute-start.22 = (f32[1,72,256]{2,1,0:T(8,128)S(1)}, f32[1,72,256]{2,1,0:T(8,128)S(1)}, u32[]{:S(2)}, u32[]{:S(2)}) collective-permute-start(f32[1,72,256]{2,1,0:T(8,128)S(1)} %get-tuple-element.193), channel_id=1, source_target_pairs={{0,2},{1,3},{2,0},{3,1},{4,6},{5,7},{6,4},{7,5},{8,10},{9,11},{10,... | collective-permute-start | bytes 221192 | tf_op jit(solution)/shard_map/ppermute | solution.py:675
  79.1 6.3 %collective-permute-start.23 = (f32[1,72,256]{2,1,0:T(8,128)S(1)}, f32[1,72,256]{2,1,0:T(8,128)S(1)}, u32[]{:S(2)}, u32[]{:S(2)}) collective-permute-start(f32[1,72,256]{2,1,0:T(8,128)S(1)} %get-tuple-element.194), channel_id=1, source_target_pairs={{0,3},{1,2},{2,1},{3,0},{4,7},{5,6},{6,5},{7,4},{8,11},{9,10},{10,... | collective-permute-start | bytes 221192 | tf_op jit(solution)/shard_map/ppermute | solution.py:675
  88.0 11.8 %collective-permute-start.25 = (f32[1,184,256]{2,1,0:T(8,128)S(1)}, f32[1,184,256]{2,1,0:T(8,128)S(1)}, u32[]{:S(2)}, u32[]{:S(2)}) collective-permute-start(f32[1,184,256]{2,1,0:T(8,128)S(1)} %get-tuple-element.202.refs_0_), channel_id=1, source_target_pairs={{0,2},{1,3},{2,0},{3,1},{4,6},{5,7},{6,4},{7,5},{8,10},{9,11},{10,... | collective-permute-start | bytes 565256 | tf_op jit(solution)/shard_map/ppermute | solution.py:671
  99.8 12.0 %collective-permute-start.27 = (f32[2,96,256]{2,1,0:T(8,128)S(1)}, f32[2,96,256]{2,1,0:T(8,128)S(1)}, u32[]{:S(2)}, u32[]{:S(2)}) collective-permute-start(f32[2,96,256]{2,1,0:T(8,128)S(1)} %get-tuple-element.204.refs_0_), channel_id=1, source_target_pairs={{0,1},{1,0},{2,3},{3,2},{4,5},{5,4},{6,7},{7,6},{8,9},{9,8},{10,11... | collective-permute-start | bytes 589832 | tf_op jit(solution)/shard_map/ppermute | solution.py:671
  99.9 5.9 %collective-permute-start.28 = (f32[2,88,256]{2,1,0:T(8,128)S(1)}, f32[2,88,256]{2,1,0:T(8,128)S(1)}, u32[]{:S(2)}, u32[]{:S(2)}) collective-permute-start(f32[2,88,256]{2,1,0:T(8,128)S(1)} %get-tuple-element.205.refs_1_), channel_id=1, source_target_pairs={{0,8},{4,12},{8,0},{12,4},{16,24},{20,28},{24,16},{28,20},{1,9},{5... | collective-permute-start | bytes 540680 | tf_op jit(solution)/shard_map/ppermute | solution.py:671
  101.4 10.5 %collective-permute-start.29 = (f32[2,88,256]{2,1,0:T(8,128)S(1)}, f32[2,88,256]{2,1,0:T(8,128)S(1)}, u32[]{:S(2)}, u32[]{:S(2)}) collective-permute-start(f32[2,88,256]{2,1,0:T(8,128)S(1)} %get-tuple-element.206.refs_2_), channel_id=1, source_target_pairs={{0,2},{1,3},{2,0},{3,1},{4,6},{5,7},{6,4},{7,5},{8,10},{9,11},{10,... | collective-permute-start | bytes 540680 | tf_op jit(solution)/shard_map/ppermute | solution.py:671
  111.9 9.0 %collective-permute-start.30 = (f32[4,96,256]{2,1,0:T(8,128)S(1)}, f32[4,96,256]{2,1,0:T(8,128)S(1)}, u32[]{:S(2)}, u32[]{:S(2)}) collective-permute-start(f32[4,96,256]{2,1,0:T(8,128)S(1)} %get-tuple-element.207.refs_0_), channel_id=1, source_target_pairs={{0,16},{4,20},{8,24},{12,28},{16,0},{20,4},{24,8},{28,12},{1,17},{... | collective-permute-start | bytes 1179656 | tf_op jit(solution)/shard_map/ppermute | solution.py:671
  112.7 7.4 %collective-permute-start.31 = (f32[4,88,256]{2,1,0:T(8,128)S(1)}, f32[4,88,256]{2,1,0:T(8,128)S(1)}, u32[]{:S(2)}, u32[]{:S(2)}) collective-permute-start(f32[4,88,256]{2,1,0:T(8,128)S(1)} %get-tuple-element.208.refs_1_), channel_id=1, source_target_pairs={{0,1},{1,0},{2,3},{3,2},{4,5},{5,4},{6,7},{7,6},{8,9},{9,8},{10,11... | collective-permute-start | bytes 1081352 | tf_op jit(solution)/shard_map/ppermute | solution.py:671
  112.7 8.3 %collective-permute-start.32 = (f32[4,88,256]{2,1,0:T(8,128)S(1)}, f32[4,88,256]{2,1,0:T(8,128)S(1)}, u32[]{:S(2)}, u32[]{:S(2)}) collective-permute-start(f32[4,88,256]{2,1,0:T(8,128)S(1)} %get-tuple-element.209.refs_2_), channel_id=1, source_target_pairs={{0,8},{4,12},{8,0},{12,4},{16,24},{20,28},{24,16},{28,20},{1,9},{5... | collective-permute-start | bytes 1081352 | tf_op jit(solution)/shard_map/ppermute | solution.py:671
  121.2 5.1 %collective-permute-start.33 = (f32[8,272,256]{2,1,0:T(8,128)S(1)}, f32[8,272,256]{2,1,0:T(8,128)S(1)}, u32[]{:S(2)}, u32[]{:S(2)}) collective-permute-start(f32[8,272,256]{2,1,0:T(8,128)S(1)} %get-tuple-element.210.near_ref), channel_id=1, source_target_pairs={{0,4},{4,0},{8,12},{12,8},{16,20},{20,16},{24,28},{28,24},{1,5},{5... | collective-permute-start | bytes 6684680 | tf_op jit(solution)/shard_map/ppermute | solution.py:671
  121.3 20.1 %collective-permute-start.34 = (f32[8,96,256]{2,1,0:T(8,128)S(1)}, f32[8,96,256]{2,1,0:T(8,128)S(1)}, u32[]{:S(2)}, u32[]{:S(2)}) collective-permute-start(f32[8,96,256]{2,1,0:T(8,128)S(1)} %get-tuple-element.211), channel_id=1, source_target_pairs={{0,8},{4,12},{8,0},{12,4},{16,24},{20,28},{24,16},{28,20},{1,9},{5... | collective-permute-start | bytes 2359304 | tf_op jit(solution)/shard_map/ppermute | solution.py:671
  122.2 18.2 %collective-permute-start.35 = (f32[8,88,256]{2,1,0:T(8,128)S(1)}, f32[8,88,256]{2,1,0:T(8,128)S(1)}, u32[]{:S(2)}, u32[]{:S(2)}) collective-permute-start(f32[8,88,256]{2,1,0:T(8,128)S(1)} %get-tuple-element.212), channel_id=1, source_target_pairs={{0,16},{4,20},{8,24},{12,28},{16,0},{20,4},{24,8},{28,12},{1,17},{... | collective-permute-start | bytes 2162696 | tf_op jit(solution)/shard_map/ppermute | solution.py:671
  123.5 17.9 %collective-permute-start.36 = (f32[8,88,256]{2,1,0:T(8,128)S(1)}, f32[8,88,256]{2,1,0:T(8,128)S(1)}, u32[]{:S(2)}, u32[]{:S(2)}) collective-permute-start(f32[8,88,256]{2,1,0:T(8,128)S(1)} %get-tuple-element.213), channel_id=1, source_target_pairs={{0,1},{1,0},{2,3},{3,2},{4,5},{5,4},{6,7},{7,6},{8,9},{9,8},{10,11... | collective-permute-start | bytes 2162696 | tf_op jit(solution)/shard_map/ppermute | solution.py:671
  (19 other events, 210.6 us)

commit v10 on v9

--- a/solution.py
+++ b/solution.py
@@ -227,16 +227,23 @@
             put_chunk(place, orders, heights, where, sends, keeps, s, chunk[low:high])
 
 
-def rel_layout(half_width, streams):
-    blocks = row_spans(half_width, 3)
-    spans = row_spans(max(high - low for low, high in blocks), streams)
+def packed_map(half_width, width, lanes):
+    rows = half_width // 24 * 8
+    gap, extra = lanes - 3 * width, half_width - 3 * rows
+    entries = [(rows * b, 0, width, 0, b * width, rows) for b in range(3)]
+    for i in range(-(-width // gap)):
+        entries.append((3 * rows, i * gap, min(gap, width - i * gap), extra * i, 3 * width, extra))
+    return rows, entries
+
+
+def split_pieces(entries, spans):
     pieces = []
-    for block, (low, high) in enumerate(blocks):
+    for row, lane, lanes, to, to_lane, count in entries:
         for s, (first, end) in enumerate(spans):
-            count = min(end, high - low) - first
-            if count > 0:
-                pieces.append((block, s, low + first, count))
-    return spans, pieces
+            low, high = max(to, first), min(to + count, end)
+            if low < high:
+                pieces.append((s, row + low - to, high - low, lane, lanes, low - first, to_lane))
+    return pieces
 
 
 def rel_chunks_kernel(orders, pieces, rows, grad_lanes, spot_ref, *refs):
@@ -260,10 +267,10 @@
         dense = dot2(stacked[...], onehot_across(idx_down, targets), NN)
         for slot, place in enumerate(places):
             chunk = dense[:, slot * width : (slot + 1) * width]
-            for block, s, low, count in pieces:
+            for s, row, count, low, wide, to, to_lane in pieces:
                 index = spread_bits(place, orders[s])
                 out = sends[s].at[index - half] if index >= half else keeps[s].at[index]
-                out[:count, block * width : (block + 1) * width] = chunk[low : low + count]
+                out[to : to + count, to_lane : to_lane + wide] = chunk[row : row + count, low : low + wide]
 
 
 def chunk_columns(kernel, shapes, spot, ids, grads):
@@ -335,15 +342,20 @@
     return call(functools.partial(join_kernel, heights, here, there), [*have, *got], shapes)
 
 
-def z_sums_kernel(spans, *refs):
-    streams = len(spans)
-    own, got, outs = refs[:streams], refs[streams : 2 * streams], refs[2 * streams :]
-    for place, out in enumerate(outs):
+def last_sums_kernel(heights, here, there, spans, carried, *refs):
+    streams, planes = len(heights), len(spans)
+    groups, out_groups = [1 + max(g for g, unused in where) for where in (here, there)]
+    rels, outs = refs[streams + groups : streams + groups + 2 * planes], refs[streams + groups + 2 * planes :]
+    sums_kernel(heights, here, there, *refs[: streams + groups], *outs[: out_groups + streams])
+    rel_outs = list(outs[out_groups + streams :])
+    for place in range(rels[0].shape[0]):
+        group, base = carried[place] if place in carried else (None, 0)
+        out = rel_outs.pop(0) if group is None else outs[group]
         for s, (low, high) in enumerate(spans):
-            out[0, low:high] = own[s][place] + got[s][place]
-
-
-def squares_kernel(heights, here, *refs):
+            out[0, base + low : base + high] = rels[s][place] + rels[planes + s][place]
+
+
+def squares_kernel(heights, here, entries, carried, *refs):
     streams, groups = len(heights), 1 + max(g for g, unused in here)
     own, got, rels = refs[:streams], refs[streams : streams + groups], refs[streams + groups : -streams - 2]
     totals, rel_total, out = refs[-streams - 2 : -2], refs[-2], refs[-1]
@@ -353,10 +365,17 @@
         total = own[s][0] + got[group][0, rows]
         totals[s][0] = total
         squares += jnp.sum(total * total, axis=0, keepdims=True)
+    height = rel_total.shape[1]
     total = sum(ref[0] for ref in rels)
+    for group, base in carried.values():
+        total = total + got[group][0, base : base + height]
     rel_total[0] = total
     out[0:1] = squares
-    out[1:2] = jnp.sum(total * total, axis=0, keepdims=True)
+    out[1:2] = jnp.zeros_like(squares)
+    square = total * total
+    for row, lane, lanes, to, to_lane, count in entries:
+        part = jnp.sum(square[to : to + count, to_lane : to_lane + lanes], axis=0, keepdims=True)
+        out[1:2, lane : lane + lanes] += part
 
 
 def update_kernel(spans, rel_spans, pieces, there, features, spot_ref, *refs):
@@ -369,20 +388,20 @@
     width = rel_ref.shape[1]
     squares = mine[...] + other[...]
     hub_scale = step_rate / jnp.sqrt(hub_sums[...] + squares[0:1] * (1.0 / features))
-    rel_squares = sum(squares[1:2, b * width : (b + 1) * width] for b in range(3))
-    rel_scale = step_rate / jnp.sqrt(rel_sums[...] + rel_squares * (1.0 / features))
+    rel_scale = step_rate / jnp.sqrt(rel_sums[...] + squares[1:2, :width] * (1.0 / features))
     for s, (low, high) in enumerate(spans):
         new, base = there[s]
         first, end = rel_spans[s]
         middle = base + high - low
         news[new][0, base:middle] = hub_ref[low:high] - totals[s][0] * hub_scale
         news[new][0, middle : middle + end - first] = jnp.zeros((end - first, news[new].shape[2]), F32)
-    for block, s, low, count in pieces:
+    for s, row, count, low, wide, to, to_lane in pieces:
         new, base = there[s]
-        base += spans[s][1] - spans[s][0]
-        lanes, first = slice(block * width, (block + 1) * width), rel_spans[s][0]
+        base += spans[s][1] - spans[s][0] + to
+        lanes, first = slice(to_lane, to_lane + wide), rel_spans[s][0] + to
         news[new][0, base : base + count, lanes] = (
-            rel_ref[low : low + count] - rel_total[0, first : first + count, lanes] * rel_scale
+            rel_ref[row : row + count, low : low + wide]
+            - rel_total[0, first : first + count, lanes] * rel_scale[:, low : low + wide]
         )
 
 
@@ -456,10 +475,10 @@
                 value = jnp.where(index >= half, fars[s][spot, :height], near_ref[spot, bases[s] : bases[s] + height])
                 hub_all[low:high, chunk * hub_width : (chunk + 1) * hub_width] = value
             value = jnp.where(index >= half, fars[s][spot, height:], near_ref[spot, bases[s] + height : bases[s] + end])
-            for block, stream, row, count in pieces:
+            for stream, row, count, low, wide, to, to_lane in pieces:
                 if stream == s:
-                    part = value[:count, block * rel_width : (block + 1) * rel_width]
-                    rel_all[row : row + count, chunk * rel_width : (chunk + 1) * rel_width] = part
+                    at = chunk * rel_width + low
+                    rel_all[row : row + count, at : at + wide] = value[to : to + count, to_lane : to_lane + wide]
     copies.append(pltpu.make_async_copy(rel_all, rel_out.at[component], sems.at[len(copies)]))
     copies[-1].start()
     if not by_copy:
@@ -725,12 +744,16 @@
     planes = chunks // depth
     spans = row_spans(half_width, streams)
     rel_orders = plane_orders(sub_bits, stages)
-    plane_spans, plane_pieces = rel_layout(half_width, len(rel_orders))
-    rel_spans, joint_pieces = rel_layout(half_width, streams)
+    width, rel_width = hub_count // chunks, rel_count // chunks
+    rel_height, entries = packed_map(half_width, rel_width, width)
+    plane_spans = row_spans(rel_height, len(rel_orders))
+    share = -(-(half_width + rel_height) // (8 * streams)) * 8
+    ends = [share * (s + 1) - spans[s][1] for s in range(streams - 1)] + [rel_height]
+    rel_spans = list(zip([0] + ends[:-1], ends))
+    plane_pieces, joint_pieces = split_pieces(entries, plane_spans), split_pieces(entries, rel_spans)
     heights, rel_heights, plane_heights = [[high - low for low, high in x] for x in (spans, rel_spans, plane_spans)]
     joint_heights = [h + r for h, r in zip(heights, rel_heights)]
     bases = [sum(joint_heights[:s]) for s in range(streams)]
-    width = hub_count // chunks
     hub_lanes, rel_lanes = (0, hubs), (hubs, hubs + edges)
 
     def exchanged(parts, step):
@@ -785,25 +808,31 @@
     rel_send, rel_own = parts[: len(rel_orders)], parts[len(rel_orders) :]
     rel_got = [across(x, order[0]) for x, order in zip(rel_send, rel_orders)]
     plane_steps = stages - sub_bits
-    for step in range(stages - 1):
+    for step in range(stages - 2):
         if 0 < step < plane_steps:
             own, rel_got = in_turn(own, rel_got)
             rel_send, rel_own = halves(rel_own, rel_got, rel_orders, step - 1)
             rel_got = [across(x, order[step]) for x, order in zip(rel_send, rel_orders)]
-        elif step == plane_steps:
-            own, rel_got = in_turn(own, rel_got)
-            rel_own, *rel_out = call(
-                functools.partial(z_sums_kernel, plane_spans), [*rel_own, *rel_got],
-                [(1, plane_spans[-1][1], width)] * depth,
-            )
-            rel_got = [flipped_by(x, "sub", q + 1) for q, x in enumerate(rel_out)]
         rel_own, got = in_turn(rel_own, got)
         send, own = halves(own, got, orders, step)
         got = exchanged(send, step + 1)
 
+    here = grouped(orders, stages - 2, heights)[1]
+    groups, there = grouped(orders, stages - 1, heights)
+    carried = {1 << place: (g, height) for g, (place, height) in enumerate(groups) if place < sub_bits}
+    tall = [height + (rel_height if place < sub_bits else 0) for place, height in groups]
+    alone = [q for q in range(depth) if q not in carried]
+    parts = call(
+        functools.partial(last_sums_kernel, heights, here, there, plane_spans, carried),
+        [*own, *got, *rel_own, *rel_got],
+        [(1, height, width) for height in tall + heights + [rel_height] * len(alone)],
+    )
+    send, own, rel_parts = parts[: len(groups)], parts[len(groups) : len(groups) + streams], parts[len(groups) + streams :]
+    got = exchanged(send, stages - 1)
+    rel_got = [flipped_by(x, "sub", q) for q, x in zip(alone[1:], rel_parts[1:])]
     *totals, rel_total, squares = call(
-        functools.partial(squares_kernel, heights, grouped(orders, stages - 1, heights)[1]),
-        [*own, *got, rel_own, *rel_got], [x.shape for x in own] + [rel_own.shape, (2, width)],
+        functools.partial(squares_kernel, heights, there, entries, carried),
+        [*own, *got, rel_parts[0], *rel_got], [x.shape for x in own] + [rel_parts[0].shape, (2, width)],
     )
     hub_own, rel_own = owned
     groups, there = grouped(orders, stages - 1, joint_heights)

time: 149 us -> 149 us (level)
    ppermute x3 -> x2, waiting for transfers between devices: 0.19 us -> 4.85 us  [flipped_by(): lax.ppermute(x, axis, [(i, i ^ offset) for i in range(lax.axis_size(axis))])]
    ppermute x36, waiting for transfers between devices: 61.5 us -> 57.1 us  [flipped(): lax.ppermute(x, axis, [(i, i ^ 1 << bit) for i in range(lax.axis_size(axi...]
    ppermute x3 -> x2, starting transfers between devices: 4.72 us -> 4.31 us  [flipped_by(): lax.ppermute(x, axis, [(i, i ^ offset) for i in range(lax.axis_size(axis))])]
  transfers between devices with their start and end apart: 40 -> 39, of which waited for: 18 -> 24; matrix products, arithmetic and copies ran while one was open for 0% -> 0% of each run, Pallas kernels for 22% -> 22%
where the time goes in v10:
time: 149 us
  waiting for transfers between devices  62 us (42%)
  Pallas kernels  43.4 us (29%)
  starting transfers between devices  41 us (28%)
    ppermute x36, waiting for transfers between devices, flipped(): lax.ppermute(x, axis, [(i, i ^ 1 << bit) for i in range(lax.axis_size(axi...  57.1 us
    ppermute x36, starting transfers between devices, flipped(): lax.ppermute(x, axis, [(i, i ^ 1 << bit) for i in range(lax.axis_size(axi...  36 us
    pallas_call x1, Pallas kernels, gather_rows(): pl.pallas_call(functools.partial(gather_kernel, hub_steps, rel_steps), in...  10 us
    pallas_call x4, Pallas kernels, placed(): pl.pallas_call(kernel, in_specs=[SMEM] + [VMEM] * (1 + len(fars)) + [HBM]...  9.41 us
    pallas_call x2, Pallas kernels, chunk_columns(): pl.pallas_call(functools.partial(kernel, grad_lanes), in_specs=[SMEM] + [...  8 us
    pallas_call x1, Pallas kernels, bucket_step(): pl.pallas_call(functools.partial(bucket_kernel, bucket), in_specs=[SMEM]...  5.58 us
    pallas_call x1, Pallas kernels, tables_step(): pl.pallas_call(functools.partial(tables_kernel, bucket, hubs), in_specs=[...  5.42 us
    ppermute x2, waiting for transfers between devices, flipped_by(): lax.ppermute(x, axis, [(i, i ^ offset) for i in range(lax.axis_size(axis))])  4.85 us
  transfers between devices with their start and end apart: 39, of which 24 were waited for; matrix products, arithmetic and copies ran while one was open for 0% of the time, Pallas kernels for 22%

profile of v10, /device:TPU:0, one launch (start us, length us, event | category | flops | bytes accessed | tf_op | source)
XLA Modules:
  0.0 148.9 jit_solution(13404077461107082361)
XLA Ops:
  2.7 10.0 %shard_map.156 = (f32[400,256]{1,0:T(8,128)S(1)}, f32[400,256]{1,0:T(8,128)S(1)}, f32[400,512]{1,0:T(8,128)S(1)}, f32[400,512]{1,0:T(8,128)S(1)}, s32[2]{0:T(128...) custom-call(s32[2]{0:T(128)S(1)} %pad_add_fusion.spot_ref, s32[2,256]{1,0:T(2,128)S(1)} %copy-done.7, ...), custom_call_target="tpu_custom_call" | custom-call | flops 10000 | bytes 10000 | tf_op jit(solution)/shard_map/pallas_call | solution.py:135
  12.9 5.6 %shard_map.157 = (f32[400,512]{1,0:T(8,128)S(1)}, f32[1,512]{1,0:T(1,128)S(1)}, f32[408,512]{1,0:T(8,128)S(1)}, f32[200,768]{1,0:T(8,128)S(1)}, f32[200,768]{1,0:T(8,128)S(1)}) custom-call(s32[2]{0:T(128)S(1)} %get-tuple-element.103.core_ref.spot_ref, s32[2,512]{1,0:T(2,128)S(1)} %copy-done.2, s32[2,512]{1,0:T(2,128)S(1)} %copy-done.4, ...), custom_call_target="tpu_custom_call" | custom-call | flops 10000 | bytes 10000 | tf_op jit(solution)/shard_map/pallas_call | solution.py:582
  19.1 2.7 %shard_map.158 = (f32[400,512]{1,0:T(8,128)S(1)}, f32[200,256]{1,0:T(8,128)S(1)}, f32[200,256]{1,0:T(8,128)S(1)}) custom-call(s32[2]{0:T(128)S(1)} %get-tuple-element.103.core_ref.spot_ref, s32[2,512]{1,0:T(2,128)S(1)} %copy-done.2, f32[400,512]{1,0:T(8,128)S(1)} %get-tuple-element.108.left_ref, f32[400,512]{1,0:T(8,128)S(1)} %get-tuple-element.109.rel_ref, ...), custom_call_target="tpu_custom_call" | custom-call | flops 10000 | bytes 10000 | tf_op jit(solution)/shard_map/pallas_call | solution.py:623
  21.8 2.8 %collective-permute-start.3 = (f32[200,768]{1,0:T(8,128)S(1)}, f32[200,768]{1,0:T(8,128)S(1)}, u32[]{:S(2)}, u32[]{:S(2)}) collective-permute-start(f32[200,768]{1,0:T(8,128)S(1)} %get-tuple-element.121), channel_id=1, source_target_pairs={{0,4},{4,0},{8,12},{12,8},{16,20},{20,16},{24,28},{28,24},{1,5},{5... | collective-permute-start | bytes 1843208 | tf_op jit(solution)/shard_map/ppermute | solution.py:690
  24.7 1.9 %collective-permute-done.4.refs_5_ = f32[200,256]{1,0:T(8,128)S(1)} collective-permute-done((f32[200,256]{1,0:T(8,128)S(1)}, f32[200,256]{1,0:T(8,128)S(1)}, u32[]{:S(2)}, u32[]{:S(2)}) %collective-permute-start.4) | collective-permute-done | bytes 204832 | tf_op jit(solution)/shard_map/ppermute | solution.py:690
  26.6 4.3 %shard_map.160 = (f32[8,72,256]{2,1,0:T(8,128)S(1)}, f32[8,64,256]{2,1,0:T(8,128)S(1)}, f32[8,64,256]{2,1,0:T(8,128)S(1)}, f32[8,72,256]{2,1,0:T(8,128)S(1)}, f3...) custom-call(s32[2]{0:T(128)S(1)} %get-tuple-element.103.core_ref.spot_ref, s32[2,256]{1,0:T(2,128)S(1)} %copy-done.7, ...), custom_call_target="tpu_custom_call" | custom-call | flops 10000 | bytes 10000 | tf_op jit(solution)/shard_map/pallas_call | solution.py:280
  32.8 1.8 %collective-permute-start.8 = (f32[8,64,256]{2,1,0:T(8,128)S(1)}, f32[8,64,256]{2,1,0:T(8,128)S(1)}, u32[]{:S(2)}, u32[]{:S(2)}) collective-permute-start(f32[8,64,256]{2,1,0:T(8,128)S(1)} %get-tuple-element.133), channel_id=1, source_target_pairs={{0,1},{1,0},{2,3},{3,2},{4,5},{5,4},{6,7},{7,6},{8,9},{9,8},{10,11... | collective-permute-start | bytes 1572872 | tf_op jit(solution)/shard_map/ppermute | solution.py:690
  34.6 5.4 %shard_map.159 = (f32[400,512]{1,0:T(8,128)}, f32[400,512]{1,0:T(8,128)}, f32[200,512]{1,0:T(8,128)S(1)}, f32[200,512]{1,0:T(8,128)S(1)}) custom-call(s32[2]{0:T(128)S(1)} %get-tuple-element.103.core_ref.spot_ref, s32[2,512]{1,0:T(2,128)S(1)} %copy-done.2, s32[2,512]{1,0:T(2,128)S(1)} %copy-done.4, s32[2,1024]{1,0:T(2,128)S(1)} %copy-done.3, ...), custom_call_target="tpu_custom_call" | custom-call | flops 10000 | bytes 10000 | tf_op jit(solution)/shard_map/pallas_call | solution.py:673
  40.0 1.7 %collective-permute-done.5.refs_5_ = f32[200,512]{1,0:T(8,128)S(1)} collective-permute-done((f32[200,512]{1,0:T(8,128)S(1)}, f32[200,512]{1,0:T(8,128)S(1)}, u32[]{:S(2)}, u32[]{:S(2)}) %collective-permute-start.5) | collective-permute-done | bytes 409632 | tf_op jit(solution)/shard_map/ppermute | solution.py:690
  41.8 3.7 %shard_map.161 = (f32[8,32,256]{2,1,0:T(8,128)S(1)}, f32[8,32,256]{2,1,0:T(8,128)S(1)}, f32[8,32,256]{2,1,0:T(8,128)S(1)}, f32[8,32,256]{2,1,0:T(8,128)S(1)}) custom-call(s32[2]{0:T(128)S(1)} %get-tuple-element.103.core_ref.spot_ref, s32[2,512]{1,0:T(2,128)S(1)} %copy-done.5, s32[2,512]{1,0:T(2,128)S(1)} %collective-permute-done.1.refs_1_, ...), custom_call_target="tpu_custom_call" | custom-call | flops 10000 | bytes 10000 | tf_op jit(solution)/shard_map/pallas_call | solution.py:280
  46.8 1.6 %collective-permute-start.11 = (f32[4,72,256]{2,1,0:T(8,128)S(1)}, f32[4,72,256]{2,1,0:T(8,128)S(1)}, u32[]{:S(2)}, u32[]{:S(2)}) collective-permute-start(f32[4,72,256]{2,1,0:T(8,128)S(1)} %get-tuple-element.151), channel_id=1, source_target_pairs={{0,16},{4,20},{8,24},{12,28},{16,0},{20,4},{24,8},{28,12},{1,17},{... | collective-permute-start | bytes 884744 | tf_op jit(solution)/shard_map/ppermute | solution.py:690
  52.6 5.0 %collective-permute-done.9.refs_2_ = f32[8,32,256]{2,1,0:T(8,128)S(1)} collective-permute-done((f32[8,32,256]{2,1,0:T(8,128)S(1)}, f32[8,32,256]{2,1,0:T(8,128)S(1)}, u32[]{:S(2)}, u32[]{:S(2)}) %collective-permute-start.9) | collective-permute-done | bytes 262176 | tf_op jit(solution)/shard_map/ppermute | solution.py:690
  57.6 3.3 %collective-permute-done.10.refs_3_ = f32[8,32,256]{2,1,0:T(8,128)S(1)} collective-permute-done((f32[8,32,256]{2,1,0:T(8,128)S(1)}, f32[8,32,256]{2,1,0:T(8,128)S(1)}, u32[]{:S(2)}, u32[]{:S(2)}) %collective-permute-start.10) | collective-permute-done | bytes 262176 | tf_op jit(solution)/shard_map/ppermute | solution.py:690
  61.5 1.6 %collective-permute-start.14 = (f32[2,72,256]{2,1,0:T(8,128)S(1)}, f32[2,72,256]{2,1,0:T(8,128)S(1)}, u32[]{:S(2)}, u32[]{:S(2)}) collective-permute-start(f32[2,72,256]{2,1,0:T(8,128)S(1)} %get-tuple-element.160), channel_id=1, source_target_pairs={{0,1},{1,0},{2,3},{3,2},{4,5},{5,4},{6,7},{7,6},{8,9},{9,8},{10,11... | collective-permute-start | bytes 442376 | tf_op jit(solution)/shard_map/ppermute | solution.py:690
  66.3 2.6 %collective-permute-start.16 = (f32[2,64,256]{2,1,0:T(8,128)S(1)}, f32[2,64,256]{2,1,0:T(8,128)S(1)}, u32[]{:S(2)}, u32[]{:S(2)}) collective-permute-start(f32[2,64,256]{2,1,0:T(8,128)S(1)} %get-tuple-element.162), channel_id=1, source_target_pairs={{0,2},{1,3},{2,0},{3,1},{4,6},{5,7},{6,4},{7,5},{8,10},{9,11},{10,... | collective-permute-start | bytes 393224 | tf_op jit(solution)/shard_map/ppermute | solution.py:690
  70.6 2.8 %collective-permute-done.16.refs_5_ = f32[2,64,256]{2,1,0:T(8,128)S(1)} collective-permute-done((f32[2,64,256]{2,1,0:T(8,128)S(1)}, f32[2,64,256]{2,1,0:T(8,128)S(1)}, u32[]{:S(2)}, u32[]{:S(2)}) %collective-permute-start.16) | collective-permute-done | bytes 131104 | tf_op jit(solution)/shard_map/ppermute | solution.py:690
  75.0 2.0 %collective-permute-start.20 = (f32[1,64,256]{2,1,0:T(8,128)S(1)}, f32[1,64,256]{2,1,0:T(8,128)S(1)}, u32[]{:S(2)}, u32[]{:S(2)}) collective-permute-start(f32[1,64,256]{2,1,0:T(8,128)S(1)} %get-tuple-element.171), channel_id=1, source_target_pairs={{0,16},{4,20},{8,24},{12,28},{16,0},{20,4},{24,8},{28,12},{1,17},{... | collective-permute-start | bytes 196616 | tf_op jit(solution)/shard_map/ppermute | solution.py:690
  77.0 3.1 %collective-permute-start.21 = (f32[1,64,256]{2,1,0:T(8,128)S(1)}, f32[1,64,256]{2,1,0:T(8,128)S(1)}, u32[]{:S(2)}, u32[]{:S(2)}) collective-permute-start(f32[1,64,256]{2,1,0:T(8,128)S(1)} %get-tuple-element.173), channel_id=1, source_target_pairs={{0,1},{1,0},{2,3},{3,2},{4,5},{5,4},{6,7},{7,6},{8,9},{9,8},{10,11... | collective-permute-start | bytes 196616 | tf_op jit(solution)/shard_map/ppermute | solution.py:694
  82.4 3.8 %collective-permute-done.22.refs_7_ = f32[1,64,256]{2,1,0:T(8,128)S(1)} collective-permute-done((f32[1,64,256]{2,1,0:T(8,128)S(1)}, f32[1,64,256]{2,1,0:T(8,128)S(1)}, u32[]{:S(2)}, u32[]{:S(2)}) %collective-permute-start.22) | collective-permute-done | bytes 65568 | tf_op jit(solution)/shard_map/ppermute | solution.py:694
  90.4 3.6 %collective-permute-done.25.refs_3_ = f32[1,88,256]{2,1,0:T(8,128)S(1)} collective-permute-done((f32[1,88,256]{2,1,0:T(8,128)S(1)}, f32[1,88,256]{2,1,0:T(8,128)S(1)}, u32[]{:S(2)}, u32[]{:S(2)}) %collective-permute-start.25) | collective-permute-done | bytes 90144 | tf_op jit(solution)/shard_map/ppermute | solution.py:690
  94.0 5.0 %collective-permute-done.24.refs_2_ = f32[1,176,256]{2,1,0:T(8,128)S(1)} collective-permute-done((f32[1,176,256]{2,1,0:T(8,128)S(1)}, f32[1,176,256]{2,1,0:T(8,128)S(1)}, u32[]{:S(2)}, u32[]{:S(2)}) %collective-permute-start.24) | collective-permute-done | bytes 180256 | tf_op jit(solution)/shard_map/ppermute | solution.py:690
  100.4 2.4 %collective-permute-start.28 = (f32[2,88,256]{2,1,0:T(8,128)S(1)}, f32[2,88,256]{2,1,0:T(8,128)S(1)}, u32[]{:S(2)}, u32[]{:S(2)}) collective-permute-start(f32[2,88,256]{2,1,0:T(8,128)S(1)} %get-tuple-element.186.refs_2_), channel_id=1, source_target_pairs={{0,2},{1,3},{2,0},{3,1},{4,6},{5,7},{6,4},{7,5},{8,10},{9,11},{10,... | collective-permute-start | bytes 540680 | tf_op jit(solution)/shard_map/ppermute | solution.py:690
  102.8 5.6 %collective-permute-done.26.refs_3_ = f32[2,88,256]{2,1,0:T(8,128)S(1)} collective-permute-done((f32[2,88,256]{2,1,0:T(8,128)S(1)}, f32[2,88,256]{2,1,0:T(8,128)S(1)}, u32[]{:S(2)}, u32[]{:S(2)}) %collective-permute-start.26) | collective-permute-done | bytes 180256 | tf_op jit(solution)/shard_map/ppermute | solution.py:690
  108.4 3.0 %collective-permute-done.28.refs_5_ = f32[2,88,256]{2,1,0:T(8,128)S(1)} collective-permute-done((f32[2,88,256]{2,1,0:T(8,128)S(1)}, f32[2,88,256]{2,1,0:T(8,128)S(1)}, u32[]{:S(2)}, u32[]{:S(2)}) %collective-permute-start.28) | collective-permute-done | bytes 180256 | tf_op jit(solution)/shard_map/ppermute | solution.py:690
  113.7 5.9 %collective-permute-done.29.refs_3_ = f32[4,88,256]{2,1,0:T(8,128)S(1)} collective-permute-done((f32[4,88,256]{2,1,0:T(8,128)S(1)}, f32[4,88,256]{2,1,0:T(8,128)S(1)}, u32[]{:S(2)}, u32[]{:S(2)}) %collective-permute-start.29) | collective-permute-done | bytes 360480 | tf_op jit(solution)/shard_map/ppermute | solution.py:690
  121.4 1.6 %collective-permute-start.33 = (f32[8,88,256]{2,1,0:T(8,128)S(1)}, f32[8,88,256]{2,1,0:T(8,128)S(1)}, u32[]{:S(2)}, u32[]{:S(2)}) collective-permute-start(f32[8,88,256]{2,1,0:T(8,128)S(1)} %get-tuple-element.191), channel_id=1, source_target_pairs={{0,8},{4,12},{8,0},{12,4},{16,24},{20,28},{24,16},{28,20},{1,9},{5... | collective-permute-start | bytes 2162696 | tf_op jit(solution)/shard_map/ppermute | solution.py:690
  123.8 1.7 %collective-permute-start.35 = (f32[8,88,256]{2,1,0:T(8,128)S(1)}, f32[8,88,256]{2,1,0:T(8,128)S(1)}, u32[]{:S(2)}, u32[]{:S(2)}) collective-permute-start(f32[8,88,256]{2,1,0:T(8,128)S(1)} %get-tuple-element.193), channel_id=1, source_target_pairs={{0,1},{1,0},{2,3},{3,2},{4,5},{5,4},{6,7},{7,6},{8,9},{9,8},{10,11... | collective-permute-start | bytes 2162696 | tf_op jit(solution)/shard_map/ppermute | solution.py:690
  125.5 1.9 %shard_map.171.refs_0_ = f32[2,200,4096]{2,1,0:T(8,128)} custom-call(s32[2]{0:T(128)S(1)} %get-tuple-element.103.core_ref.spot_ref, f32[8,264,256]{2,1,0:T(8,128)S(1)} %get-tuple-element.190.near_ref), custom_call_target="tpu_custom_call" | custom-call | bytes 3276800 | tf_op jit(solution)/shard_map/pallas_call | solution.py:493
  127.5 1.9 %shard_map.172.refs_3_ = f32[2,200,4096]{2,1,0:T(8,128)} custom-call(s32[2]{0:T(128)S(1)} %get-tuple-element.103.core_ref.spot_ref, f32[8,264,256]{2,1,0:T(8,128)S(1)} %collective-permute-done.32.near_ref, f32[2,200,4096]{2,1,0:T(8,128)} %shard_map.171.refs_0_), custom_call_target="tpu_custom_call", output_to_operand_aliasing={{}: (2, {})} | custom-call | bytes 3276800 | tf_op jit(solution)/shard_map/pallas_call | solution.py:493
  129.4 10.6 %collective-permute-done.33.refs_0_ = f32[8,88,256]{2,1,0:T(8,128)S(1)} collective-permute-done((f32[8,88,256]{2,1,0:T(8,128)S(1)}, f32[8,88,256]{2,1,0:T(8,128)S(1)}, u32[]{:S(2)}, u32[]{:S(2)}) %collective-permute-start.33) | collective-permute-done | bytes 720928 | tf_op jit(solution)/shard_map/ppermute | solution.py:690
  142.2 2.8 %shard_map.173 = (f32[2,200,4096]{2,1,0:T(8,128)}, f32[2,200,1280]{2,1,0:T(8,128)}) custom-call(s32[2]{0:T(128)S(1)} %get-tuple-element.103.core_ref.spot_ref, f32[8,264,256]{2,1,0:T(8,128)S(1)} %get-tuple-element.190.near_ref, f32[8,88,256]{2,1,0:T(8,128)S(1)} %collective-permute-done.33.refs_0_, ...), custom_call_target="tpu_custom_call", output_to_operand_aliasing={{0}: (5, {})} | custom-call | bytes 3276800 | tf_op jit(solution)/shard_map/pallas_call | solution.py:493
  146.0 2.8 %shard_map.174 = (f32[2,200,4096]{2,1,0:T(8,128)}, f32[2,200,1280]{2,1,0:T(8,128)}) custom-call(s32[2]{0:T(128)S(1)} %get-tuple-element.103.core_ref.spot_ref, f32[8,264,256]{2,1,0:T(8,128)S(1)} %collective-permute-done.32.near_ref, f32[8,88,256]{2,1,0:T(8,128)S(1)} %collective-permute-done.36.refs_0_, ...), custom_call_target="tpu_custom_call", output_to_operand_aliasing={{0}: (5, {}), {1}: (6, {})} | custom-call | bytes 3276800 | tf_op jit(solution)/shard_map/pallas_call | solution.py:493
  (89 shorter events, 33.0 us)
Async XLA Ops:
  0.7 12.1 %collective-permute-start = (s32[2,256]{1,0:T(2,128)}, s32[2,256]{1,0:T(2,128)S(1)}, u32[]{:S(2)}, u32[]{:S(2)}) collective-permute-start(s32[2,256]{1,0:T(2,128)} %refs_0_.2), channel_id=1, source_target_pairs={{0,4},{4,0},{8,12},{12,8},{16,20},{20,16},{24,28},{28,24},{1,5},{5... | collective-permute-start | bytes 6152 | tf_op jit(solution)/shard_map/ppermute | solution.py:690
  1.2 11.6 %collective-permute-start.1 = (s32[2,512]{1,0:T(2,128)}, s32[2,512]{1,0:T(2,128)S(1)}, u32[]{:S(2)}, u32[]{:S(2)}) collective-permute-start(s32[2,512]{1,0:T(2,128)} %refs_0_.3), channel_id=1, source_target_pairs={{0,4},{4,0},{8,12},{12,8},{16,20},{20,16},{24,28},{28,24},{1,5},{5... | collective-permute-start | bytes 12296 | tf_op jit(solution)/shard_map/ppermute | solution.py:690
  18.5 16.2 %collective-permute-start.2 = (f32[408,512]{1,0:T(8,128)S(1)}, f32[408,512]{1,0:T(8,128)S(1)}, u32[]{:S(2)}, u32[]{:S(2)}) collective-permute-start(f32[408,512]{1,0:T(8,128)S(1)} %get-tuple-element.113), channel_id=1, source_target_pairs={{0,4},{4,8},{8,12},{12,16},{16,20},{20,24},{24,28},{28,0},{1,5},{5... | collective-permute-start | bytes 2506760 | tf_op jit(solution)/shard_map/ppermute | solution.py:686
  21.8 4.7 %collective-permute-start.3 = (f32[200,768]{1,0:T(8,128)S(1)}, f32[200,768]{1,0:T(8,128)S(1)}, u32[]{:S(2)}, u32[]{:S(2)}) collective-permute-start(f32[200,768]{1,0:T(8,128)S(1)} %get-tuple-element.121), channel_id=1, source_target_pairs={{0,4},{4,0},{8,12},{12,8},{16,20},{20,16},{24,28},{28,24},{1,5},{5... | collective-permute-start | bytes 1843208 | tf_op jit(solution)/shard_map/ppermute | solution.py:690
  30.9 15.7 %collective-permute-start.6 = (f32[8,72,256]{2,1,0:T(8,128)S(1)}, f32[8,72,256]{2,1,0:T(8,128)S(1)}, u32[]{:S(2)}, u32[]{:S(2)}) collective-permute-start(f32[8,72,256]{2,1,0:T(8,128)S(1)} %get-tuple-element.131), channel_id=1, source_target_pairs={{0,8},{4,12},{8,0},{12,4},{16,24},{20,28},{24,16},{28,20},{1,9},{5... | collective-permute-start | bytes 1769480 | tf_op jit(solution)/shard_map/ppermute | solution.py:690
  32.4 13.9 %collective-permute-start.7 = (f32[8,64,256]{2,1,0:T(8,128)S(1)}, f32[8,64,256]{2,1,0:T(8,128)S(1)}, u32[]{:S(2)}, u32[]{:S(2)}) collective-permute-start(f32[8,64,256]{2,1,0:T(8,128)S(1)} %get-tuple-element.132), channel_id=1, source_target_pairs={{0,16},{4,20},{8,24},{12,28},{16,0},{20,4},{24,8},{28,12},{1,17},{... | collective-permute-start | bytes 1572872 | tf_op jit(solution)/shard_map/ppermute | solution.py:690
  32.8 13.7 %collective-permute-start.8 = (f32[8,64,256]{2,1,0:T(8,128)S(1)}, f32[8,64,256]{2,1,0:T(8,128)S(1)}, u32[]{:S(2)}, u32[]{:S(2)}) collective-permute-start(f32[8,64,256]{2,1,0:T(8,128)S(1)} %get-tuple-element.133), channel_id=1, source_target_pairs={{0,1},{1,0},{2,3},{3,2},{4,5},{5,4},{6,7},{7,6},{8,9},{9,8},{10,11... | collective-permute-start | bytes 1572872 | tf_op jit(solution)/shard_map/ppermute | solution.py:690
  46.8 14.7 %collective-permute-start.11 = (f32[4,72,256]{2,1,0:T(8,128)S(1)}, f32[4,72,256]{2,1,0:T(8,128)S(1)}, u32[]{:S(2)}, u32[]{:S(2)}) collective-permute-start(f32[4,72,256]{2,1,0:T(8,128)S(1)} %get-tuple-element.151), channel_id=1, source_target_pairs={{0,16},{4,20},{8,24},{12,28},{16,0},{20,4},{24,8},{28,12},{1,17},{... | collective-permute-start | bytes 884744 | tf_op jit(solution)/shard_map/ppermute | solution.py:690
  48.3 9.2 %collective-permute-start.9 = (f32[8,32,256]{2,1,0:T(8,128)S(1)}, f32[8,32,256]{2,1,0:T(8,128)S(1)}, u32[]{:S(2)}, u32[]{:S(2)}) collective-permute-start(f32[8,32,256]{2,1,0:T(8,128)S(1)} %get-tuple-element.140), channel_id=1, source_target_pairs={{0,8},{4,12},{8,0},{12,4},{16,24},{20,28},{24,16},{28,20},{1,9},{5... | collective-permute-start | bytes 786440 | tf_op jit(solution)/shard_map/ppermute | solution.py:690
  48.9 12.0 %collective-permute-start.10 = (f32[8,32,256]{2,1,0:T(8,128)S(1)}, f32[8,32,256]{2,1,0:T(8,128)S(1)}, u32[]{:S(2)}, u32[]{:S(2)}) collective-permute-start(f32[8,32,256]{2,1,0:T(8,128)S(1)} %get-tuple-element.141), channel_id=1, source_target_pairs={{0,16},{4,20},{8,24},{12,28},{16,0},{20,4},{24,8},{28,12},{1,17},{... | collective-permute-start | bytes 786440 | tf_op jit(solution)/shard_map/ppermute | solution.py:690
  50.4 10.6 %collective-permute-start.12 = (f32[4,64,256]{2,1,0:T(8,128)S(1)}, f32[4,64,256]{2,1,0:T(8,128)S(1)}, u32[]{:S(2)}, u32[]{:S(2)}) collective-permute-start(f32[4,64,256]{2,1,0:T(8,128)S(1)} %get-tuple-element.152), channel_id=1, source_target_pairs={{0,1},{1,0},{2,3},{3,2},{4,5},{5,4},{6,7},{7,6},{8,9},{9,8},{10,11... | collective-permute-start | bytes 786440 | tf_op jit(solution)/shard_map/ppermute | solution.py:690
  52.0 9.5 %collective-permute-start.13 = (f32[4,64,256]{2,1,0:T(8,128)S(1)}, f32[4,64,256]{2,1,0:T(8,128)S(1)}, u32[]{:S(2)}, u32[]{:S(2)}) collective-permute-start(f32[4,64,256]{2,1,0:T(8,128)S(1)} %get-tuple-element.153), channel_id=1, source_target_pairs={{0,8},{4,12},{8,0},{12,4},{16,24},{20,28},{24,16},{28,20},{1,9},{5... | collective-permute-start | bytes 786440 | tf_op jit(solution)/shard_map/ppermute | solution.py:690
  61.5 11.9 %collective-permute-start.14 = (f32[2,72,256]{2,1,0:T(8,128)S(1)}, f32[2,72,256]{2,1,0:T(8,128)S(1)}, u32[]{:S(2)}, u32[]{:S(2)}) collective-permute-start(f32[2,72,256]{2,1,0:T(8,128)S(1)} %get-tuple-element.160), channel_id=1, source_target_pairs={{0,1},{1,0},{2,3},{3,2},{4,5},{5,4},{6,7},{7,6},{8,9},{9,8},{10,11... | collective-permute-start | bytes 442376 | tf_op jit(solution)/shard_map/ppermute | solution.py:690
  63.2 5.7 %collective-permute-start.17 = (f32[4,32,256]{2,1,0:T(8,128)S(1)}, f32[4,32,256]{2,1,0:T(8,128)S(1)}, u32[]{:S(2)}, u32[]{:S(2)}) collective-permute-start(f32[4,32,256]{2,1,0:T(8,128)S(1)} %get-tuple-element.165), channel_id=1, source_target_pairs={{0,16},{4,20},{8,24},{12,28},{16,0},{20,4},{24,8},{28,12},{1,17},{... | collective-permute-start | bytes 393224 | tf_op jit(solution)/shard_map/ppermute | solution.py:690
  64.3 5.0 %collective-permute-start.18 = (f32[4,32,256]{2,1,0:T(8,128)S(1)}, f32[4,32,256]{2,1,0:T(8,128)S(1)}, u32[]{:S(2)}, u32[]{:S(2)}) collective-permute-start(f32[4,32,256]{2,1,0:T(8,128)S(1)} %get-tuple-element.166), channel_id=1, source_target_pairs={{0,8},{4,12},{8,0},{12,4},{16,24},{20,28},{24,16},{28,20},{1,9},{5... | collective-permute-start | bytes 393224 | tf_op jit(solution)/shard_map/ppermute | solution.py:690
  65.2 5.4 %collective-permute-start.15 = (f32[2,64,256]{2,1,0:T(8,128)S(1)}, f32[2,64,256]{2,1,0:T(8,128)S(1)}, u32[]{:S(2)}, u32[]{:S(2)}) collective-permute-start(f32[2,64,256]{2,1,0:T(8,128)S(1)} %get-tuple-element.161), channel_id=1, source_target_pairs={{0,8},{4,12},{8,0},{12,4},{16,24},{20,28},{24,16},{28,20},{1,9},{5... | collective-permute-start | bytes 393224 | tf_op jit(solution)/shard_map/ppermute | solution.py:690
  66.3 7.2 %collective-permute-start.16 = (f32[2,64,256]{2,1,0:T(8,128)S(1)}, f32[2,64,256]{2,1,0:T(8,128)S(1)}, u32[]{:S(2)}, u32[]{:S(2)}) collective-permute-start(f32[2,64,256]{2,1,0:T(8,128)S(1)} %get-tuple-element.162), channel_id=1, source_target_pairs={{0,2},{1,3},{2,0},{3,1},{4,6},{5,7},{6,4},{7,5},{8,10},{9,11},{10,... | collective-permute-start | bytes 393224 | tf_op jit(solution)/shard_map/ppermute | solution.py:690
  73.5 12.7 %collective-permute-start.19 = (f32[1,200,256]{2,1,0:T(8,128)S(1)}, f32[1,200,256]{2,1,0:T(8,128)S(1)}, u32[]{:S(2)}, u32[]{:S(2)}) collective-permute-start(f32[1,200,256]{2,1,0:T(8,128)S(1)} %get-tuple-element.170), channel_id=1, source_target_pairs={{0,2},{1,3},{2,0},{3,1},{4,6},{5,7},{6,4},{7,5},{8,10},{9,11},{10,... | collective-permute-start | bytes 614408 | tf_op jit(solution)/shard_map/ppermute | solution.py:690
  75.0 6.4 %collective-permute-start.20 = (f32[1,64,256]{2,1,0:T(8,128)S(1)}, f32[1,64,256]{2,1,0:T(8,128)S(1)}, u32[]{:S(2)}, u32[]{:S(2)}) collective-permute-start(f32[1,64,256]{2,1,0:T(8,128)S(1)} %get-tuple-element.171), channel_id=1, source_target_pairs={{0,16},{4,20},{8,24},{12,28},{16,0},{20,4},{24,8},{28,12},{1,17},{... | collective-permute-start | bytes 196616 | tf_op jit(solution)/shard_map/ppermute | solution.py:690
  77.0 5.3 %collective-permute-start.21 = (f32[1,64,256]{2,1,0:T(8,128)S(1)}, f32[1,64,256]{2,1,0:T(8,128)S(1)}, u32[]{:S(2)}, u32[]{:S(2)}) collective-permute-start(f32[1,64,256]{2,1,0:T(8,128)S(1)} %get-tuple-element.173), channel_id=1, source_target_pairs={{0,1},{1,0},{2,3},{3,2},{4,5},{5,4},{6,7},{7,6},{8,9},{9,8},{10,11... | collective-permute-start | bytes 196616 | tf_op jit(solution)/shard_map/ppermute | solution.py:694
  80.1 6.1 %collective-permute-start.22 = (f32[1,64,256]{2,1,0:T(8,128)S(1)}, f32[1,64,256]{2,1,0:T(8,128)S(1)}, u32[]{:S(2)}, u32[]{:S(2)}) collective-permute-start(f32[1,64,256]{2,1,0:T(8,128)S(1)} %get-tuple-element.174), channel_id=1, source_target_pairs={{0,3},{1,2},{2,1},{3,0},{4,7},{5,6},{6,5},{7,4},{8,11},{9,10},{10,... | collective-permute-start | bytes 196616 | tf_op jit(solution)/shard_map/ppermute | solution.py:694
  88.9 10.1 %collective-permute-start.24 = (f32[1,176,256]{2,1,0:T(8,128)S(1)}, f32[1,176,256]{2,1,0:T(8,128)S(1)}, u32[]{:S(2)}, u32[]{:S(2)}) collective-permute-start(f32[1,176,256]{2,1,0:T(8,128)S(1)} %get-tuple-element.182.refs_0_), channel_id=1, source_target_pairs={{0,2},{1,3},{2,0},{3,1},{4,6},{5,7},{6,4},{7,5},{8,10},{9,11},{10,... | collective-permute-start | bytes 540680 | tf_op jit(solution)/shard_map/ppermute | solution.py:690
  99.0 9.3 %collective-permute-start.26 = (f32[2,88,256]{2,1,0:T(8,128)S(1)}, f32[2,88,256]{2,1,0:T(8,128)S(1)}, u32[]{:S(2)}, u32[]{:S(2)}) collective-permute-start(f32[2,88,256]{2,1,0:T(8,128)S(1)} %get-tuple-element.184.refs_0_), channel_id=1, source_target_pairs={{0,1},{1,0},{2,3},{3,2},{4,5},{5,4},{6,7},{7,6},{8,9},{9,8},{10,11... | collective-permute-start | bytes 540680 | tf_op jit(solution)/shard_map/ppermute | solution.py:690
  99.1 9.2 %collective-permute-start.27 = (f32[2,88,256]{2,1,0:T(8,128)S(1)}, f32[2,88,256]{2,1,0:T(8,128)S(1)}, u32[]{:S(2)}, u32[]{:S(2)}) collective-permute-start(f32[2,88,256]{2,1,0:T(8,128)S(1)} %get-tuple-element.185.refs_1_), channel_id=1, source_target_pairs={{0,8},{4,12},{8,0},{12,4},{16,24},{20,28},{24,16},{28,20},{1,9},{5... | collective-permute-start | bytes 540680 | tf_op jit(solution)/shard_map/ppermute | solution.py:690
  100.4 11.0 %collective-permute-start.28 = (f32[2,88,256]{2,1,0:T(8,128)S(1)}, f32[2,88,256]{2,1,0:T(8,128)S(1)}, u32[]{:S(2)}, u32[]{:S(2)}) collective-permute-start(f32[2,88,256]{2,1,0:T(8,128)S(1)} %get-tuple-element.186.refs_2_), channel_id=1, source_target_pairs={{0,2},{1,3},{2,0},{3,1},{4,6},{5,7},{6,4},{7,5},{8,10},{9,11},{10,... | collective-permute-start | bytes 540680 | tf_op jit(solution)/shard_map/ppermute | solution.py:690
  111.5 8.1 %collective-permute-start.29 = (f32[4,88,256]{2,1,0:T(8,128)S(1)}, f32[4,88,256]{2,1,0:T(8,128)S(1)}, u32[]{:S(2)}, u32[]{:S(2)}) collective-permute-start(f32[4,88,256]{2,1,0:T(8,128)S(1)} %get-tuple-element.187.refs_0_), channel_id=1, source_target_pairs={{0,16},{4,20},{8,24},{12,28},{16,0},{20,4},{24,8},{28,12},{1,17},{... | collective-permute-start | bytes 1081352 | tf_op jit(solution)/shard_map/ppermute | solution.py:690
  112.2 8.9 %collective-permute-start.30 = (f32[4,88,256]{2,1,0:T(8,128)S(1)}, f32[4,88,256]{2,1,0:T(8,128)S(1)}, u32[]{:S(2)}, u32[]{:S(2)}) collective-permute-start(f32[4,88,256]{2,1,0:T(8,128)S(1)} %get-tuple-element.188.refs_1_), channel_id=1, source_target_pairs={{0,1},{1,0},{2,3},{3,2},{4,5},{5,4},{6,7},{7,6},{8,9},{9,8},{10,11... | collective-permute-start | bytes 1081352 | tf_op jit(solution)/shard_map/ppermute | solution.py:690
  112.2 8.9 %collective-permute-start.31 = (f32[4,88,256]{2,1,0:T(8,128)S(1)}, f32[4,88,256]{2,1,0:T(8,128)S(1)}, u32[]{:S(2)}, u32[]{:S(2)}) collective-permute-start(f32[4,88,256]{2,1,0:T(8,128)S(1)} %get-tuple-element.189.refs_2_), channel_id=1, source_target_pairs={{0,8},{4,12},{8,0},{12,4},{16,24},{20,28},{24,16},{28,20},{1,9},{5... | collective-permute-start | bytes 1081352 | tf_op jit(solution)/shard_map/ppermute | solution.py:690
  121.4 6.1 %collective-permute-start.32 = (f32[8,264,256]{2,1,0:T(8,128)S(1)}, f32[8,264,256]{2,1,0:T(8,128)S(1)}, u32[]{:S(2)}, u32[]{:S(2)}) collective-permute-start(f32[8,264,256]{2,1,0:T(8,128)S(1)} %get-tuple-element.190.near_ref), channel_id=1, source_target_pairs={{0,4},{4,0},{8,12},{12,8},{16,20},{20,16},{24,28},{28,24},{1,5},{5... | collective-permute-start | bytes 6488072 | tf_op jit(solution)/shard_map/ppermute | solution.py:690
  121.4 18.6 %collective-permute-start.33 = (f32[8,88,256]{2,1,0:T(8,128)S(1)}, f32[8,88,256]{2,1,0:T(8,128)S(1)}, u32[]{:S(2)}, u32[]{:S(2)}) collective-permute-start(f32[8,88,256]{2,1,0:T(8,128)S(1)} %get-tuple-element.191), channel_id=1, source_target_pairs={{0,8},{4,12},{8,0},{12,4},{16,24},{20,28},{24,16},{28,20},{1,9},{5... | collective-permute-start | bytes 2162696 | tf_op jit(solution)/shard_map/ppermute | solution.py:690
  123.1 18.2 %collective-permute-start.34 = (f32[8,88,256]{2,1,0:T(8,128)S(1)}, f32[8,88,256]{2,1,0:T(8,128)S(1)}, u32[]{:S(2)}, u32[]{:S(2)}) collective-permute-start(f32[8,88,256]{2,1,0:T(8,128)S(1)} %get-tuple-element.192), channel_id=1, source_target_pairs={{0,16},{4,20},{8,24},{12,28},{16,0},{20,4},{24,8},{28,12},{1,17},{... | collective-permute-start | bytes 2162696 | tf_op jit(solution)/shard_map/ppermute | solution.py:690
  123.8 17.9 %collective-permute-start.35 = (f32[8,88,256]{2,1,0:T(8,128)S(1)}, f32[8,88,256]{2,1,0:T(8,128)S(1)}, u32[]{:S(2)}, u32[]{:S(2)}) collective-permute-start(f32[8,88,256]{2,1,0:T(8,128)S(1)} %get-tuple-element.193), channel_id=1, source_target_pairs={{0,1},{1,0},{2,3},{3,2},{4,5},{5,4},{6,7},{7,6},{8,9},{9,8},{10,11... | collective-permute-start | bytes 2162696 | tf_op jit(solution)/shard_map/ppermute | solution.py:690
  (18 other events, 207.0 us)

commit v11 on v10

--- a/solution.py
+++ b/solution.py
@@ -342,20 +342,17 @@
     return call(functools.partial(join_kernel, heights, here, there), [*have, *got], shapes)
 
 
-def last_sums_kernel(heights, here, there, spans, carried, *refs):
+def last_sums_kernel(heights, here, there, spans, *refs):
     streams, planes = len(heights), len(spans)
     groups, out_groups = [1 + max(g for g, unused in where) for where in (here, there)]
     rels, outs = refs[streams + groups : streams + groups + 2 * planes], refs[streams + groups + 2 * planes :]
     sums_kernel(heights, here, there, *refs[: streams + groups], *outs[: out_groups + streams])
-    rel_outs = list(outs[out_groups + streams :])
-    for place in range(rels[0].shape[0]):
-        group, base = carried[place] if place in carried else (None, 0)
-        out = rel_outs.pop(0) if group is None else outs[group]
+    for place, out in enumerate(outs[out_groups + streams :]):
         for s, (low, high) in enumerate(spans):
-            out[0, base + low : base + high] = rels[s][place] + rels[planes + s][place]
-
-
-def squares_kernel(heights, here, entries, carried, *refs):
+            out[0, low:high] = rels[s][place] + rels[planes + s][place]
+
+
+def squares_kernel(heights, here, entries, *refs):
     streams, groups = len(heights), 1 + max(g for g, unused in here)
     own, got, rels = refs[:streams], refs[streams : streams + groups], refs[streams + groups : -streams - 2]
     totals, rel_total, out = refs[-streams - 2 : -2], refs[-2], refs[-1]
@@ -365,10 +362,7 @@
         total = own[s][0] + got[group][0, rows]
         totals[s][0] = total
         squares += jnp.sum(total * total, axis=0, keepdims=True)
-    height = rel_total.shape[1]
     total = sum(ref[0] for ref in rels)
-    for group, base in carried.values():
-        total = total + got[group][0, base : base + height]
     rel_total[0] = total
     out[0:1] = squares
     out[1:2] = jnp.zeros_like(squares)
@@ -705,12 +699,13 @@
     return flipped(x, "blk", place - sub_bits + 1)
 
 
-def stream_orders():
+def stream_orders(gathering):
     sub_bits = lax.axis_size("sub").bit_length() - 1
     bits = sub_bits + lax.axis_size("blk").bit_length() - 2
     x, y, z, far = sub_bits, sub_bits + 1, 0, 1
     rest = [p for p in range(bits) if p not in (x, y, z, far)]
-    return [[x, y, z, far] + rest, [y, z, x, far] + rest, [z, x, far, y] + rest]
+    last = [y, far] if gathering else [far, y]
+    return [[x, y, z, far] + rest, [y, z, x, far] + rest, [z, x, *last] + rest]
 
 
 def plane_orders(sub_bits, bits):
@@ -737,7 +732,7 @@
     buckets, edges = heads.shape
     hubs = hub_ids.shape[1]
 
-    orders = stream_orders()
+    orders, back_orders = stream_orders(False), stream_orders(True)
     streams, stages = len(orders), len(orders[0])
     chunks, depth = 1 << stages, lax.axis_size("sub")
     sub_bits = depth.bit_length() - 1
@@ -756,7 +751,7 @@
     bases = [sum(joint_heights[:s]) for s in range(streams)]
     hub_lanes, rel_lanes = (0, hubs), (hubs, hubs + edges)
 
-    def exchanged(parts, step):
+    def exchanged(parts, step, orders=orders):
         return [across(x, place) for x, (place, unused) in zip(parts, grouped(orders, step, heights)[0])]
 
     def in_turn(first, then):
@@ -819,23 +814,20 @@
 
     here = grouped(orders, stages - 2, heights)[1]
     groups, there = grouped(orders, stages - 1, heights)
-    carried = {1 << place: (g, height) for g, (place, height) in enumerate(groups) if place < sub_bits}
-    tall = [height + (rel_height if place < sub_bits else 0) for place, height in groups]
-    alone = [q for q in range(depth) if q not in carried]
     parts = call(
-        functools.partial(last_sums_kernel, heights, here, there, plane_spans, carried),
+        functools.partial(last_sums_kernel, heights, here, there, plane_spans),
         [*own, *got, *rel_own, *rel_got],
-        [(1, height, width) for height in tall + heights + [rel_height] * len(alone)],
+        [(1, height, width) for height in [h for unused, h in groups] + heights + [rel_height] * depth],
     )
     send, own, rel_parts = parts[: len(groups)], parts[len(groups) : len(groups) + streams], parts[len(groups) + streams :]
     got = exchanged(send, stages - 1)
-    rel_got = [flipped_by(x, "sub", q) for q, x in zip(alone[1:], rel_parts[1:])]
+    rel_got = [flipped_by(x, "sub", q + 1) for q, x in enumerate(rel_parts[1:])]
     *totals, rel_total, squares = call(
-        functools.partial(squares_kernel, heights, there, entries, carried),
+        functools.partial(squares_kernel, heights, there, entries),
         [*own, *got, rel_parts[0], *rel_got], [x.shape for x in own] + [rel_parts[0].shape, (2, width)],
     )
     hub_own, rel_own = owned
-    groups, there = grouped(orders, stages - 1, joint_heights)
+    groups, there = grouped(back_orders, stages - 1, joint_heights)
     ins = [
         *totals, rel_total, squares, other_core(squares),
         hub_own, hub_state[None], rel_own, relation_state[None],
@@ -850,20 +842,20 @@
         cost_estimate=COST,
     )(spot, *ins)
     for step in range(stages - 1, 1, -1):
-        have = join(have, exchanged(have, step), orders, step, joint_heights)
-    have, near = join_all(have, exchanged(have, 1), orders, 1, joint_heights)
-    got = exchanged(have, 0)
+        have = join(have, exchanged(have, step, back_orders), back_orders, step, joint_heights)
+    have, near = join_all(have, exchanged(have, 1, back_orders), back_orders, 1, joint_heights)
+    got = exchanged(have, 0, back_orders)
     far_near = other_core(near)
 
     shapes = [hub_emb.shape, relation_emb.shape]
     by_copy = width % 128 == 0
     hub_new = []
     if by_copy:
-        near_step = functools.partial(near_kernel, orders, spans, bases)
+        near_step = functools.partial(near_kernel, back_orders, spans, bases)
         hub_new = placed(functools.partial(near_step, True), [], spot, near, [], shapes[:1], [])
         hub_new = placed(functools.partial(near_step, False), [], spot, far_near, [], shapes[:1], hub_new)
         got, hub_new = in_turn(got, hub_new)
-    far_step = functools.partial(far_kernel, orders, spans, bases, joint_pieces, by_copy)
+    far_step = functools.partial(far_kernel, back_orders, spans, bases, joint_pieces, by_copy)
     scratch = [
         pltpu.VMEM((8, 128) if by_copy else (half_width, hub_count), F32),
         pltpu.VMEM((half_width, rel_count), F32),

time: 149 us -> 149 us (level)
    ppermute x36 -> x35, starting transfers between devices: 36 us -> 34.2 us  [flipped(): lax.ppermute(x, axis, [(i, i ^ 1 << bit) for i in range(lax.axis_size(axi...]
    ppermute x36 -> x35, waiting for transfers between devices: 57.1 us -> 58.9 us  [flipped(): lax.ppermute(x, axis, [(i, i ^ 1 << bit) for i in range(lax.axis_size(axi...]
    ppermute x2 -> x3, starting transfers between devices: 4.31 us -> 5.36 us  [flipped_by(): lax.ppermute(x, axis, [(i, i ^ offset) for i in range(lax.axis_size(axis))])]
    ppermute x2 -> x3, waiting for transfers between devices: 4.85 us -> 3.88 us  [flipped_by(): lax.ppermute(x, axis, [(i, i ^ offset) for i in range(lax.axis_size(axis))])]
  transfers between devices with their start and end apart: 39 -> 39, of which waited for: 24 -> 26; matrix products, arithmetic and copies ran while one was open for 0% -> 0% of each run, Pallas kernels for 22% -> 22%
where the time goes in v11:
time: 149 us
  waiting for transfers between devices  62.8 us (42%)
  Pallas kernels  43.4 us (29%)
  starting transfers between devices  40.2 us (27%)
    ppermute x35, waiting for transfers between devices, flipped(): lax.ppermute(x, axis, [(i, i ^ 1 << bit) for i in range(lax.axis_size(axi...  58.9 us
    ppermute x35, starting transfers between devices, flipped(): lax.ppermute(x, axis, [(i, i ^ 1 << bit) for i in range(lax.axis_size(axi...  34.2 us
    pallas_call x1, Pallas kernels, gather_rows(): pl.pallas_call(functools.partial(gather_kernel, hub_steps, rel_steps), in...  10 us
    pallas_call x4, Pallas kernels, placed(): pl.pallas_call(kernel, in_specs=[SMEM] + [VMEM] * (1 + len(fars)) + [HBM]...  9.41 us
    pallas_call x2, Pallas kernels, chunk_columns(): pl.pallas_call(functools.partial(kernel, grad_lanes), in_specs=[SMEM] + [...  8 us
    pallas_call x1, Pallas kernels, bucket_step(): pl.pallas_call(functools.partial(bucket_kernel, bucket), in_specs=[SMEM]...  5.58 us
    pallas_call x1, Pallas kernels, tables_step(): pl.pallas_call(functools.partial(tables_kernel, bucket, hubs), in_specs=[...  5.42 us
    ppermute x3, starting transfers between devices, flipped_by(): lax.ppermute(x, axis, [(i, i ^ offset) for i in range(lax.axis_size(axis))])  5.36 us
  transfers between devices with their start and end apart: 39, of which 26 were waited for; matrix products, arithmetic and copies ran while one was open for 0% of the time, Pallas kernels for 22%

profile of v11, /device:TPU:0, one launch (start us, length us, event | category | flops | bytes accessed | tf_op | source)
XLA Modules:
  0.0 149.0 jit_solution(4026963585541295064)
XLA Ops:
  2.7 10.0 %shard_map.156 = (f32[400,256]{1,0:T(8,128)S(1)}, f32[400,256]{1,0:T(8,128)S(1)}, f32[400,512]{1,0:T(8,128)S(1)}, f32[400,512]{1,0:T(8,128)S(1)}, s32[2]{0:T(128...) custom-call(s32[2]{0:T(128)S(1)} %pad_add_fusion.spot_ref, s32[2,256]{1,0:T(2,128)S(1)} %copy-done.7, ...), custom_call_target="tpu_custom_call" | custom-call | flops 10000 | bytes 10000 | tf_op jit(solution)/shard_map/pallas_call | solution.py:135
  12.9 5.6 %shard_map.157 = (f32[400,512]{1,0:T(8,128)S(1)}, f32[1,512]{1,0:T(1,128)S(1)}, f32[408,512]{1,0:T(8,128)S(1)}, f32[200,768]{1,0:T(8,128)S(1)}, f32[200,768]{1,0:T(8,128)S(1)}) custom-call(s32[2]{0:T(128)S(1)} %get-tuple-element.102.core_ref.spot_ref, s32[2,512]{1,0:T(2,128)S(1)} %copy-done.2, s32[2,512]{1,0:T(2,128)S(1)} %copy-done.4, ...), custom_call_target="tpu_custom_call" | custom-call | flops 10000 | bytes 10000 | tf_op jit(solution)/shard_map/pallas_call | solution.py:576
  19.1 2.7 %shard_map.158 = (f32[400,512]{1,0:T(8,128)S(1)}, f32[200,256]{1,0:T(8,128)S(1)}, f32[200,256]{1,0:T(8,128)S(1)}) custom-call(s32[2]{0:T(128)S(1)} %get-tuple-element.102.core_ref.spot_ref, s32[2,512]{1,0:T(2,128)S(1)} %copy-done.2, f32[400,512]{1,0:T(8,128)S(1)} %get-tuple-element.107.left_ref, f32[400,512]{1,0:T(8,128)S(1)} %get-tuple-element.108.rel_ref, ...), custom_call_target="tpu_custom_call" | custom-call | flops 10000 | bytes 10000 | tf_op jit(solution)/shard_map/pallas_call | solution.py:617
  21.8 2.8 %collective-permute-start.3 = (f32[200,768]{1,0:T(8,128)S(1)}, f32[200,768]{1,0:T(8,128)S(1)}, u32[]{:S(2)}, u32[]{:S(2)}) collective-permute-start(f32[200,768]{1,0:T(8,128)S(1)} %get-tuple-element.120), channel_id=1, source_target_pairs={{0,4},{4,0},{8,12},{12,8},{16,20},{20,16},{24,28},{28,24},{1,5},{5... | collective-permute-start | bytes 1843208 | tf_op jit(solution)/shard_map/ppermute | solution.py:684
  24.7 1.9 %collective-permute-done.4.refs_5_ = f32[200,256]{1,0:T(8,128)S(1)} collective-permute-done((f32[200,256]{1,0:T(8,128)S(1)}, f32[200,256]{1,0:T(8,128)S(1)}, u32[]{:S(2)}, u32[]{:S(2)}) %collective-permute-start.4) | collective-permute-done | bytes 204832 | tf_op jit(solution)/shard_map/ppermute | solution.py:684
  26.6 4.3 %shard_map.160 = (f32[8,72,256]{2,1,0:T(8,128)S(1)}, f32[8,64,256]{2,1,0:T(8,128)S(1)}, f32[8,64,256]{2,1,0:T(8,128)S(1)}, f32[8,72,256]{2,1,0:T(8,128)S(1)}, f3...) custom-call(s32[2]{0:T(128)S(1)} %get-tuple-element.102.core_ref.spot_ref, s32[2,256]{1,0:T(2,128)S(1)} %copy-done.7, ...), custom_call_target="tpu_custom_call" | custom-call | flops 10000 | bytes 10000 | tf_op jit(solution)/shard_map/pallas_call | solution.py:280
  30.9 1.5 collective-permute-start.6
  32.8 1.8 %collective-permute-start.8 = (f32[8,64,256]{2,1,0:T(8,128)S(1)}, f32[8,64,256]{2,1,0:T(8,128)S(1)}, u32[]{:S(2)}, u32[]{:S(2)}) collective-permute-start(f32[8,64,256]{2,1,0:T(8,128)S(1)} %get-tuple-element.132), channel_id=1, source_target_pairs={{0,1},{1,0},{2,3},{3,2},{4,5},{5,4},{6,7},{7,6},{8,9},{9,8},{10,11... | collective-permute-start | bytes 1572872 | tf_op jit(solution)/shard_map/ppermute | solution.py:684
  34.6 5.4 %shard_map.159 = (f32[400,512]{1,0:T(8,128)}, f32[400,512]{1,0:T(8,128)}, f32[200,512]{1,0:T(8,128)S(1)}, f32[200,512]{1,0:T(8,128)S(1)}) custom-call(s32[2]{0:T(128)S(1)} %get-tuple-element.102.core_ref.spot_ref, s32[2,512]{1,0:T(2,128)S(1)} %copy-done.2, s32[2,512]{1,0:T(2,128)S(1)} %copy-done.4, s32[2,1024]{1,0:T(2,128)S(1)} %copy-done.3, ...), custom_call_target="tpu_custom_call" | custom-call | flops 10000 | bytes 10000 | tf_op jit(solution)/shard_map/pallas_call | solution.py:667
  40.0 1.7 %collective-permute-done.5.refs_5_ = f32[200,512]{1,0:T(8,128)S(1)} collective-permute-done((f32[200,512]{1,0:T(8,128)S(1)}, f32[200,512]{1,0:T(8,128)S(1)}, u32[]{:S(2)}, u32[]{:S(2)}) %collective-permute-start.5) | collective-permute-done | bytes 409632 | tf_op jit(solution)/shard_map/ppermute | solution.py:684
  41.8 3.7 %shard_map.161 = (f32[8,32,256]{2,1,0:T(8,128)S(1)}, f32[8,32,256]{2,1,0:T(8,128)S(1)}, f32[8,32,256]{2,1,0:T(8,128)S(1)}, f32[8,32,256]{2,1,0:T(8,128)S(1)}) custom-call(s32[2]{0:T(128)S(1)} %get-tuple-element.102.core_ref.spot_ref, s32[2,512]{1,0:T(2,128)S(1)} %copy-done.5, s32[2,512]{1,0:T(2,128)S(1)} %collective-permute-done.1.refs_1_, ...), custom_call_target="tpu_custom_call" | custom-call | flops 10000 | bytes 10000 | tf_op jit(solution)/shard_map/pallas_call | solution.py:280
  46.8 1.6 %collective-permute-start.11 = (f32[4,72,256]{2,1,0:T(8,128)S(1)}, f32[4,72,256]{2,1,0:T(8,128)S(1)}, u32[]{:S(2)}, u32[]{:S(2)}) collective-permute-start(f32[4,72,256]{2,1,0:T(8,128)S(1)} %get-tuple-element.150), channel_id=1, source_target_pairs={{0,16},{4,20},{8,24},{12,28},{16,0},{20,4},{24,8},{28,12},{1,17},{... | collective-permute-start | bytes 884744 | tf_op jit(solution)/shard_map/ppermute | solution.py:684
  48.9 1.5 %collective-permute-start.10 = (f32[8,32,256]{2,1,0:T(8,128)S(1)}, f32[8,32,256]{2,1,0:T(8,128)S(1)}, u32[]{:S(2)}, u32[]{:S(2)}) collective-permute-start(f32[8,32,256]{2,1,0:T(8,128)S(1)} %get-tuple-element.140), channel_id=1, source_target_pairs={{0,16},{4,20},{8,24},{12,28},{16,0},{20,4},{24,8},{28,12},{1,17},{... | collective-permute-start | bytes 786440 | tf_op jit(solution)/shard_map/ppermute | solution.py:684
  50.4 1.6 %collective-permute-start.12 = (f32[4,64,256]{2,1,0:T(8,128)S(1)}, f32[4,64,256]{2,1,0:T(8,128)S(1)}, u32[]{:S(2)}, u32[]{:S(2)}) collective-permute-start(f32[4,64,256]{2,1,0:T(8,128)S(1)} %get-tuple-element.151), channel_id=1, source_target_pairs={{0,1},{1,0},{2,3},{3,2},{4,5},{5,4},{6,7},{7,6},{8,9},{9,8},{10,11... | collective-permute-start | bytes 786440 | tf_op jit(solution)/shard_map/ppermute | solution.py:684
  52.6 5.0 %collective-permute-done.9.refs_2_ = f32[8,32,256]{2,1,0:T(8,128)S(1)} collective-permute-done((f32[8,32,256]{2,1,0:T(8,128)S(1)}, f32[8,32,256]{2,1,0:T(8,128)S(1)}, u32[]{:S(2)}, u32[]{:S(2)}) %collective-permute-start.9) | collective-permute-done | bytes 262176 | tf_op jit(solution)/shard_map/ppermute | solution.py:684
  57.6 3.3 %collective-permute-done.10.refs_3_ = f32[8,32,256]{2,1,0:T(8,128)S(1)} collective-permute-done((f32[8,32,256]{2,1,0:T(8,128)S(1)}, f32[8,32,256]{2,1,0:T(8,128)S(1)}, u32[]{:S(2)}, u32[]{:S(2)}) %collective-permute-start.10) | collective-permute-done | bytes 262176 | tf_op jit(solution)/shard_map/ppermute | solution.py:684
  61.5 1.6 %collective-permute-start.14 = (f32[2,72,256]{2,1,0:T(8,128)S(1)}, f32[2,72,256]{2,1,0:T(8,128)S(1)}, u32[]{:S(2)}, u32[]{:S(2)}) collective-permute-start(f32[2,72,256]{2,1,0:T(8,128)S(1)} %get-tuple-element.159), channel_id=1, source_target_pairs={{0,1},{1,0},{2,3},{3,2},{4,5},{5,4},{6,7},{7,6},{8,9},{9,8},{10,11... | collective-permute-start | bytes 442376 | tf_op jit(solution)/shard_map/ppermute | solution.py:684
  66.3 2.6 %collective-permute-start.16 = (f32[2,64,256]{2,1,0:T(8,128)S(1)}, f32[2,64,256]{2,1,0:T(8,128)S(1)}, u32[]{:S(2)}, u32[]{:S(2)}) collective-permute-start(f32[2,64,256]{2,1,0:T(8,128)S(1)} %get-tuple-element.161), channel_id=1, source_target_pairs={{0,2},{1,3},{2,0},{3,1},{4,6},{5,7},{6,4},{7,5},{8,10},{9,11},{10,... | collective-permute-start | bytes 393224 | tf_op jit(solution)/shard_map/ppermute | solution.py:684
  70.6 2.8 %collective-permute-done.16.refs_5_ = f32[2,64,256]{2,1,0:T(8,128)S(1)} collective-permute-done((f32[2,64,256]{2,1,0:T(8,128)S(1)}, f32[2,64,256]{2,1,0:T(8,128)S(1)}, u32[]{:S(2)}, u32[]{:S(2)}) %collective-permute-start.16) | collective-permute-done | bytes 131104 | tf_op jit(solution)/shard_map/ppermute | solution.py:684
  76.4 3.0 %collective-permute-start.21 = (f32[1,64,256]{2,1,0:T(8,128)S(1)}, f32[1,64,256]{2,1,0:T(8,128)S(1)}, u32[]{:S(2)}, u32[]{:S(2)}) collective-permute-start(f32[1,64,256]{2,1,0:T(8,128)S(1)} %get-tuple-element.172), channel_id=1, source_target_pairs={{0,1},{1,0},{2,3},{3,2},{4,5},{5,4},{6,7},{7,6},{8,9},{9,8},{10,11... | collective-permute-start | bytes 196616 | tf_op jit(solution)/shard_map/ppermute | solution.py:688
  79.5 2.3 %collective-permute-start.23 = (f32[1,64,256]{2,1,0:T(8,128)S(1)}, f32[1,64,256]{2,1,0:T(8,128)S(1)}, u32[]{:S(2)}, u32[]{:S(2)}) collective-permute-start(f32[1,64,256]{2,1,0:T(8,128)S(1)} %get-tuple-element.174), channel_id=1, source_target_pairs={{0,3},{1,2},{2,1},{3,0},{4,7},{5,6},{6,5},{7,4},{8,11},{9,10},{10,... | collective-permute-start | bytes 196616 | tf_op jit(solution)/shard_map/ppermute | solution.py:688
  82.5 2.2 %collective-permute-done.22.refs_7_ = f32[1,64,256]{2,1,0:T(8,128)S(1)} collective-permute-done((f32[1,64,256]{2,1,0:T(8,128)S(1)}, f32[1,64,256]{2,1,0:T(8,128)S(1)}, u32[]{:S(2)}, u32[]{:S(2)}) %collective-permute-start.22) | collective-permute-done | bytes 65568 | tf_op jit(solution)/shard_map/ppermute | solution.py:688
  88.3 1.7 %collective-permute-start.25 = (f32[1,264,256]{2,1,0:T(8,128)S(1)}, f32[1,264,256]{2,1,0:T(8,128)S(1)}, u32[]{:S(2)}, u32[]{:S(2)}) collective-permute-start(f32[1,264,256]{2,1,0:T(8,128)S(1)} %shard_map.167.refs_0_), channel_id=1, source_target_pairs={{0,2},{1,3},{2,0},{3,1},{4,6},{5,7},{6,4},{7,5},{8,10},{9,11},{10,... | collective-permute-start | bytes 811016 | tf_op jit(solution)/shard_map/ppermute | solution.py:684
  90.1 13.6 %collective-permute-done.25.refs_1_ = f32[1,264,256]{2,1,0:T(8,128)S(1)} collective-permute-done((f32[1,264,256]{2,1,0:T(8,128)S(1)}, f32[1,264,256]{2,1,0:T(8,128)S(1)}, u32[]{:S(2)}, u32[]{:S(2)}) %collective-permute-start.25) | collective-permute-done | bytes 270368 | tf_op jit(solution)/shard_map/ppermute | solution.py:684
  105.7 4.1 %collective-permute-done.26.refs_3_ = f32[2,88,256]{2,1,0:T(8,128)S(1)} collective-permute-done((f32[2,88,256]{2,1,0:T(8,128)S(1)}, f32[2,88,256]{2,1,0:T(8,128)S(1)}, u32[]{:S(2)}, u32[]{:S(2)}) %collective-permute-start.26) | collective-permute-done | bytes 180256 | tf_op jit(solution)/shard_map/ppermute | solution.py:684
  111.7 1.7 %collective-permute-start.30 = (f32[4,88,256]{2,1,0:T(8,128)S(1)}, f32[4,88,256]{2,1,0:T(8,128)S(1)}, u32[]{:S(2)}, u32[]{:S(2)}) collective-permute-start(f32[4,88,256]{2,1,0:T(8,128)S(1)} %get-tuple-element.186.refs_1_), channel_id=1, source_target_pairs={{0,1},{1,0},{2,3},{3,2},{4,5},{5,4},{6,7},{7,6},{8,9},{9,8},{10,11... | collective-permute-start | bytes 1081352 | tf_op jit(solution)/shard_map/ppermute | solution.py:684
  114.5 4.9 %collective-permute-done.29.refs_3_ = f32[4,88,256]{2,1,0:T(8,128)S(1)} collective-permute-done((f32[4,88,256]{2,1,0:T(8,128)S(1)}, f32[4,88,256]{2,1,0:T(8,128)S(1)}, u32[]{:S(2)}, u32[]{:S(2)}) %collective-permute-start.29) | collective-permute-done | bytes 360480 | tf_op jit(solution)/shard_map/ppermute | solution.py:684
  124.4 1.9 %shard_map.171.refs_0_ = f32[2,200,4096]{2,1,0:T(8,128)} custom-call(s32[2]{0:T(128)S(1)} %get-tuple-element.102.core_ref.spot_ref, f32[8,264,256]{2,1,0:T(8,128)S(1)} %get-tuple-element.188.near_ref), custom_call_target="tpu_custom_call" | custom-call | bytes 3276800 | tf_op jit(solution)/shard_map/pallas_call | solution.py:487
  126.3 1.9 %shard_map.172.refs_3_ = f32[2,200,4096]{2,1,0:T(8,128)} custom-call(s32[2]{0:T(128)S(1)} %get-tuple-element.102.core_ref.spot_ref, f32[8,264,256]{2,1,0:T(8,128)S(1)} %collective-permute-done.32.near_ref, f32[2,200,4096]{2,1,0:T(8,128)} %shard_map.171.refs_0_), custom_call_target="tpu_custom_call", output_to_operand_aliasing={{}: (2, {})} | custom-call | bytes 3276800 | tf_op jit(solution)/shard_map/pallas_call | solution.py:487
  128.3 11.9 %collective-permute-done.33.refs_0_ = f32[8,88,256]{2,1,0:T(8,128)S(1)} collective-permute-done((f32[8,88,256]{2,1,0:T(8,128)S(1)}, f32[8,88,256]{2,1,0:T(8,128)S(1)}, u32[]{:S(2)}, u32[]{:S(2)}) %collective-permute-start.33) | collective-permute-done | bytes 720928 | tf_op jit(solution)/shard_map/ppermute | solution.py:684
  142.3 2.8 %shard_map.173 = (f32[2,200,4096]{2,1,0:T(8,128)}, f32[2,200,1280]{2,1,0:T(8,128)}) custom-call(s32[2]{0:T(128)S(1)} %get-tuple-element.102.core_ref.spot_ref, f32[8,264,256]{2,1,0:T(8,128)S(1)} %get-tuple-element.188.near_ref, f32[8,88,256]{2,1,0:T(8,128)S(1)} %collective-permute-done.33.refs_0_, ...), custom_call_target="tpu_custom_call", output_to_operand_aliasing={{0}: (5, {})} | custom-call | bytes 3276800 | tf_op jit(solution)/shard_map/pallas_call | solution.py:487
  146.0 2.8 %shard_map.174 = (f32[2,200,4096]{2,1,0:T(8,128)}, f32[2,200,1280]{2,1,0:T(8,128)}) custom-call(s32[2]{0:T(128)S(1)} %get-tuple-element.102.core_ref.spot_ref, f32[8,264,256]{2,1,0:T(8,128)S(1)} %collective-permute-done.32.near_ref, f32[8,88,256]{2,1,0:T(8,128)S(1)} %collective-permute-done.36.refs_0_, ...), custom_call_target="tpu_custom_call", output_to_operand_aliasing={{0}: (5, {}), {1}: (6, {})} | custom-call | bytes 3276800 | tf_op jit(solution)/shard_map/pallas_call | solution.py:487
  (89 shorter events, 31.6 us)
Async XLA Ops:
  0.7 12.1 %collective-permute-start = (s32[2,256]{1,0:T(2,128)}, s32[2,256]{1,0:T(2,128)S(1)}, u32[]{:S(2)}, u32[]{:S(2)}) collective-permute-start(s32[2,256]{1,0:T(2,128)} %refs_0_.2), channel_id=1, source_target_pairs={{0,4},{4,0},{8,12},{12,8},{16,20},{20,16},{24,28},{28,24},{1,5},{5... | collective-permute-start | bytes 6152 | tf_op jit(solution)/shard_map/ppermute | solution.py:684
  1.2 11.6 %collective-permute-start.1 = (s32[2,512]{1,0:T(2,128)}, s32[2,512]{1,0:T(2,128)S(1)}, u32[]{:S(2)}, u32[]{:S(2)}) collective-permute-start(s32[2,512]{1,0:T(2,128)} %refs_0_.3), channel_id=1, source_target_pairs={{0,4},{4,0},{8,12},{12,8},{16,20},{20,16},{24,28},{28,24},{1,5},{5... | collective-permute-start | bytes 12296 | tf_op jit(solution)/shard_map/ppermute | solution.py:684
  18.5 16.2 %collective-permute-start.2 = (f32[408,512]{1,0:T(8,128)S(1)}, f32[408,512]{1,0:T(8,128)S(1)}, u32[]{:S(2)}, u32[]{:S(2)}) collective-permute-start(f32[408,512]{1,0:T(8,128)S(1)} %get-tuple-element.112), channel_id=1, source_target_pairs={{0,4},{4,8},{8,12},{12,16},{16,20},{20,24},{24,28},{28,0},{1,5},{5... | collective-permute-start | bytes 2506760 | tf_op jit(solution)/shard_map/ppermute | solution.py:680
  30.9 15.7 %collective-permute-start.6 = (f32[8,72,256]{2,1,0:T(8,128)S(1)}, f32[8,72,256]{2,1,0:T(8,128)S(1)}, u32[]{:S(2)}, u32[]{:S(2)}) collective-permute-start(f32[8,72,256]{2,1,0:T(8,128)S(1)} %get-tuple-element.130), channel_id=1, source_target_pairs={{0,8},{4,12},{8,0},{12,4},{16,24},{20,28},{24,16},{28,20},{1,9},{5... | collective-permute-start | bytes 1769480 | tf_op jit(solution)/shard_map/ppermute | solution.py:684
  32.4 13.9 %collective-permute-start.7 = (f32[8,64,256]{2,1,0:T(8,128)S(1)}, f32[8,64,256]{2,1,0:T(8,128)S(1)}, u32[]{:S(2)}, u32[]{:S(2)}) collective-permute-start(f32[8,64,256]{2,1,0:T(8,128)S(1)} %get-tuple-element.131), channel_id=1, source_target_pairs={{0,16},{4,20},{8,24},{12,28},{16,0},{20,4},{24,8},{28,12},{1,17},{... | collective-permute-start | bytes 1572872 | tf_op jit(solution)/shard_map/ppermute | solution.py:684
  32.8 13.7 %collective-permute-start.8 = (f32[8,64,256]{2,1,0:T(8,128)S(1)}, f32[8,64,256]{2,1,0:T(8,128)S(1)}, u32[]{:S(2)}, u32[]{:S(2)}) collective-permute-start(f32[8,64,256]{2,1,0:T(8,128)S(1)} %get-tuple-element.132), channel_id=1, source_target_pairs={{0,1},{1,0},{2,3},{3,2},{4,5},{5,4},{6,7},{7,6},{8,9},{9,8},{10,11... | collective-permute-start | bytes 1572872 | tf_op jit(solution)/shard_map/ppermute | solution.py:684
  46.8 14.7 %collective-permute-start.11 = (f32[4,72,256]{2,1,0:T(8,128)S(1)}, f32[4,72,256]{2,1,0:T(8,128)S(1)}, u32[]{:S(2)}, u32[]{:S(2)}) collective-permute-start(f32[4,72,256]{2,1,0:T(8,128)S(1)} %get-tuple-element.150), channel_id=1, source_target_pairs={{0,16},{4,20},{8,24},{12,28},{16,0},{20,4},{24,8},{28,12},{1,17},{... | collective-permute-start | bytes 884744 | tf_op jit(solution)/shard_map/ppermute | solution.py:684
  48.3 9.2 %collective-permute-start.9 = (f32[8,32,256]{2,1,0:T(8,128)S(1)}, f32[8,32,256]{2,1,0:T(8,128)S(1)}, u32[]{:S(2)}, u32[]{:S(2)}) collective-permute-start(f32[8,32,256]{2,1,0:T(8,128)S(1)} %get-tuple-element.139), channel_id=1, source_target_pairs={{0,8},{4,12},{8,0},{12,4},{16,24},{20,28},{24,16},{28,20},{1,9},{5... | collective-permute-start | bytes 786440 | tf_op jit(solution)/shard_map/ppermute | solution.py:684
  48.9 12.0 %collective-permute-start.10 = (f32[8,32,256]{2,1,0:T(8,128)S(1)}, f32[8,32,256]{2,1,0:T(8,128)S(1)}, u32[]{:S(2)}, u32[]{:S(2)}) collective-permute-start(f32[8,32,256]{2,1,0:T(8,128)S(1)} %get-tuple-element.140), channel_id=1, source_target_pairs={{0,16},{4,20},{8,24},{12,28},{16,0},{20,4},{24,8},{28,12},{1,17},{... | collective-permute-start | bytes 786440 | tf_op jit(solution)/shard_map/ppermute | solution.py:684
  50.4 10.6 %collective-permute-start.12 = (f32[4,64,256]{2,1,0:T(8,128)S(1)}, f32[4,64,256]{2,1,0:T(8,128)S(1)}, u32[]{:S(2)}, u32[]{:S(2)}) collective-permute-start(f32[4,64,256]{2,1,0:T(8,128)S(1)} %get-tuple-element.151), channel_id=1, source_target_pairs={{0,1},{1,0},{2,3},{3,2},{4,5},{5,4},{6,7},{7,6},{8,9},{9,8},{10,11... | collective-permute-start | bytes 786440 | tf_op jit(solution)/shard_map/ppermute | solution.py:684
  52.0 9.5 %collective-permute-start.13 = (f32[4,64,256]{2,1,0:T(8,128)S(1)}, f32[4,64,256]{2,1,0:T(8,128)S(1)}, u32[]{:S(2)}, u32[]{:S(2)}) collective-permute-start(f32[4,64,256]{2,1,0:T(8,128)S(1)} %get-tuple-element.152), channel_id=1, source_target_pairs={{0,8},{4,12},{8,0},{12,4},{16,24},{20,28},{24,16},{28,20},{1,9},{5... | collective-permute-start | bytes 786440 | tf_op jit(solution)/shard_map/ppermute | solution.py:684
  61.5 11.9 %collective-permute-start.14 = (f32[2,72,256]{2,1,0:T(8,128)S(1)}, f32[2,72,256]{2,1,0:T(8,128)S(1)}, u32[]{:S(2)}, u32[]{:S(2)}) collective-permute-start(f32[2,72,256]{2,1,0:T(8,128)S(1)} %get-tuple-element.159), channel_id=1, source_target_pairs={{0,1},{1,0},{2,3},{3,2},{4,5},{5,4},{6,7},{7,6},{8,9},{9,8},{10,11... | collective-permute-start | bytes 442376 | tf_op jit(solution)/shard_map/ppermute | solution.py:684
  63.2 5.7 %collective-permute-start.17 = (f32[4,32,256]{2,1,0:T(8,128)S(1)}, f32[4,32,256]{2,1,0:T(8,128)S(1)}, u32[]{:S(2)}, u32[]{:S(2)}) collective-permute-start(f32[4,32,256]{2,1,0:T(8,128)S(1)} %get-tuple-element.164), channel_id=1, source_target_pairs={{0,16},{4,20},{8,24},{12,28},{16,0},{20,4},{24,8},{28,12},{1,17},{... | collective-permute-start | bytes 393224 | tf_op jit(solution)/shard_map/ppermute | solution.py:684
  64.3 5.0 %collective-permute-start.18 = (f32[4,32,256]{2,1,0:T(8,128)S(1)}, f32[4,32,256]{2,1,0:T(8,128)S(1)}, u32[]{:S(2)}, u32[]{:S(2)}) collective-permute-start(f32[4,32,256]{2,1,0:T(8,128)S(1)} %get-tuple-element.165), channel_id=1, source_target_pairs={{0,8},{4,12},{8,0},{12,4},{16,24},{20,28},{24,16},{28,20},{1,9},{5... | collective-permute-start | bytes 393224 | tf_op jit(solution)/shard_map/ppermute | solution.py:684
  65.2 5.4 %collective-permute-start.15 = (f32[2,64,256]{2,1,0:T(8,128)S(1)}, f32[2,64,256]{2,1,0:T(8,128)S(1)}, u32[]{:S(2)}, u32[]{:S(2)}) collective-permute-start(f32[2,64,256]{2,1,0:T(8,128)S(1)} %get-tuple-element.160), channel_id=1, source_target_pairs={{0,8},{4,12},{8,0},{12,4},{16,24},{20,28},{24,16},{28,20},{1,9},{5... | collective-permute-start | bytes 393224 | tf_op jit(solution)/shard_map/ppermute | solution.py:684
  66.3 7.2 %collective-permute-start.16 = (f32[2,64,256]{2,1,0:T(8,128)S(1)}, f32[2,64,256]{2,1,0:T(8,128)S(1)}, u32[]{:S(2)}, u32[]{:S(2)}) collective-permute-start(f32[2,64,256]{2,1,0:T(8,128)S(1)} %get-tuple-element.161), channel_id=1, source_target_pairs={{0,2},{1,3},{2,0},{3,1},{4,6},{5,7},{6,4},{7,5},{8,10},{9,11},{10,... | collective-permute-start | bytes 393224 | tf_op jit(solution)/shard_map/ppermute | solution.py:684
  73.5 12.1 %collective-permute-start.19 = (f32[1,136,256]{2,1,0:T(8,128)S(1)}, f32[1,136,256]{2,1,0:T(8,128)S(1)}, u32[]{:S(2)}, u32[]{:S(2)}) collective-permute-start(f32[1,136,256]{2,1,0:T(8,128)S(1)} %get-tuple-element.169), channel_id=1, source_target_pairs={{0,2},{1,3},{2,0},{3,1},{4,6},{5,7},{6,4},{7,5},{8,10},{9,11},{10,... | collective-permute-start | bytes 417800 | tf_op jit(solution)/shard_map/ppermute | solution.py:684
  75.0 6.8 %collective-permute-start.20 = (f32[1,64,256]{2,1,0:T(8,128)S(1)}, f32[1,64,256]{2,1,0:T(8,128)S(1)}, u32[]{:S(2)}, u32[]{:S(2)}) collective-permute-start(f32[1,64,256]{2,1,0:T(8,128)S(1)} %get-tuple-element.170), channel_id=1, source_target_pairs={{0,16},{4,20},{8,24},{12,28},{16,0},{20,4},{24,8},{28,12},{1,17},{... | collective-permute-start | bytes 196616 | tf_op jit(solution)/shard_map/ppermute | solution.py:684
  76.4 6.1 %collective-permute-start.21 = (f32[1,64,256]{2,1,0:T(8,128)S(1)}, f32[1,64,256]{2,1,0:T(8,128)S(1)}, u32[]{:S(2)}, u32[]{:S(2)}) collective-permute-start(f32[1,64,256]{2,1,0:T(8,128)S(1)} %get-tuple-element.172), channel_id=1, source_target_pairs={{0,1},{1,0},{2,3},{3,2},{4,5},{5,4},{6,7},{7,6},{8,9},{9,8},{10,11... | collective-permute-start | bytes 196616 | tf_op jit(solution)/shard_map/ppermute | solution.py:688
  79.4 5.3 %collective-permute-start.22 = (f32[1,64,256]{2,1,0:T(8,128)S(1)}, f32[1,64,256]{2,1,0:T(8,128)S(1)}, u32[]{:S(2)}, u32[]{:S(2)}) collective-permute-start(f32[1,64,256]{2,1,0:T(8,128)S(1)} %get-tuple-element.173), channel_id=1, source_target_pairs={{0,2},{1,3},{2,0},{3,1},{4,6},{5,7},{6,4},{7,5},{8,10},{9,11},{10,... | collective-permute-start | bytes 196616 | tf_op jit(solution)/shard_map/ppermute | solution.py:688
  79.5 6.2 %collective-permute-start.23 = (f32[1,64,256]{2,1,0:T(8,128)S(1)}, f32[1,64,256]{2,1,0:T(8,128)S(1)}, u32[]{:S(2)}, u32[]{:S(2)}) collective-permute-start(f32[1,64,256]{2,1,0:T(8,128)S(1)} %get-tuple-element.174), channel_id=1, source_target_pairs={{0,3},{1,2},{2,1},{3,0},{4,7},{5,6},{6,5},{7,4},{8,11},{9,10},{10,... | collective-permute-start | bytes 196616 | tf_op jit(solution)/shard_map/ppermute | solution.py:688
  88.3 15.3 %collective-permute-start.25 = (f32[1,264,256]{2,1,0:T(8,128)S(1)}, f32[1,264,256]{2,1,0:T(8,128)S(1)}, u32[]{:S(2)}, u32[]{:S(2)}) collective-permute-start(f32[1,264,256]{2,1,0:T(8,128)S(1)} %shard_map.167.refs_0_), channel_id=1, source_target_pairs={{0,2},{1,3},{2,0},{3,1},{4,6},{5,7},{6,4},{7,5},{8,10},{9,11},{10,... | collective-permute-start | bytes 811016 | tf_op jit(solution)/shard_map/ppermute | solution.py:684
  103.7 6.1 %collective-permute-start.26 = (f32[2,88,256]{2,1,0:T(8,128)S(1)}, f32[2,88,256]{2,1,0:T(8,128)S(1)}, u32[]{:S(2)}, u32[]{:S(2)}) collective-permute-start(f32[2,88,256]{2,1,0:T(8,128)S(1)} %get-tuple-element.182.refs_0_), channel_id=1, source_target_pairs={{0,1},{1,0},{2,3},{3,2},{4,5},{5,4},{6,7},{7,6},{8,9},{9,8},{10,11... | collective-permute-start | bytes 540680 | tf_op jit(solution)/shard_map/ppermute | solution.py:684
  103.8 6.1 %collective-permute-start.27 = (f32[2,88,256]{2,1,0:T(8,128)S(1)}, f32[2,88,256]{2,1,0:T(8,128)S(1)}, u32[]{:S(2)}, u32[]{:S(2)}) collective-permute-start(f32[2,88,256]{2,1,0:T(8,128)S(1)} %get-tuple-element.183.refs_1_), channel_id=1, source_target_pairs={{0,8},{4,12},{8,0},{12,4},{16,24},{20,28},{24,16},{28,20},{1,9},{5... | collective-permute-start | bytes 540680 | tf_op jit(solution)/shard_map/ppermute | solution.py:684
  104.8 5.8 %collective-permute-start.28 = (f32[2,88,256]{2,1,0:T(8,128)S(1)}, f32[2,88,256]{2,1,0:T(8,128)S(1)}, u32[]{:S(2)}, u32[]{:S(2)}) collective-permute-start(f32[2,88,256]{2,1,0:T(8,128)S(1)} %get-tuple-element.184.refs_2_), channel_id=1, source_target_pairs={{0,16},{4,20},{8,24},{12,28},{16,0},{20,4},{24,8},{28,12},{1,17},{... | collective-permute-start | bytes 540680 | tf_op jit(solution)/shard_map/ppermute | solution.py:684
  110.7 8.8 %collective-permute-start.29 = (f32[4,88,256]{2,1,0:T(8,128)S(1)}, f32[4,88,256]{2,1,0:T(8,128)S(1)}, u32[]{:S(2)}, u32[]{:S(2)}) collective-permute-start(f32[4,88,256]{2,1,0:T(8,128)S(1)} %get-tuple-element.185.refs_0_), channel_id=1, source_target_pairs={{0,16},{4,20},{8,24},{12,28},{16,0},{20,4},{24,8},{28,12},{1,17},{... | collective-permute-start | bytes 1081352 | tf_op jit(solution)/shard_map/ppermute | solution.py:684
  111.7 8.4 %collective-permute-start.30 = (f32[4,88,256]{2,1,0:T(8,128)S(1)}, f32[4,88,256]{2,1,0:T(8,128)S(1)}, u32[]{:S(2)}, u32[]{:S(2)}) collective-permute-start(f32[4,88,256]{2,1,0:T(8,128)S(1)} %get-tuple-element.186.refs_1_), channel_id=1, source_target_pairs={{0,1},{1,0},{2,3},{3,2},{4,5},{5,4},{6,7},{7,6},{8,9},{9,8},{10,11... | collective-permute-start | bytes 1081352 | tf_op jit(solution)/shard_map/ppermute | solution.py:684
  113.3 7.9 %collective-permute-start.31 = (f32[4,88,256]{2,1,0:T(8,128)S(1)}, f32[4,88,256]{2,1,0:T(8,128)S(1)}, u32[]{:S(2)}, u32[]{:S(2)}) collective-permute-start(f32[4,88,256]{2,1,0:T(8,128)S(1)} %get-tuple-element.187.refs_2_), channel_id=1, source_target_pairs={{0,8},{4,12},{8,0},{12,4},{16,24},{20,28},{24,16},{28,20},{1,9},{5... | collective-permute-start | bytes 1081352 | tf_op jit(solution)/shard_map/ppermute | solution.py:684
  121.5 4.8 %collective-permute-start.32 = (f32[8,264,256]{2,1,0:T(8,128)S(1)}, f32[8,264,256]{2,1,0:T(8,128)S(1)}, u32[]{:S(2)}, u32[]{:S(2)}) collective-permute-start(f32[8,264,256]{2,1,0:T(8,128)S(1)} %get-tuple-element.188.near_ref), channel_id=1, source_target_pairs={{0,4},{4,0},{8,12},{12,8},{16,20},{20,16},{24,28},{28,24},{1,5},{5... | collective-permute-start | bytes 6488072 | tf_op jit(solution)/shard_map/ppermute | solution.py:684
  121.6 18.6 %collective-permute-start.33 = (f32[8,88,256]{2,1,0:T(8,128)S(1)}, f32[8,88,256]{2,1,0:T(8,128)S(1)}, u32[]{:S(2)}, u32[]{:S(2)}) collective-permute-start(f32[8,88,256]{2,1,0:T(8,128)S(1)} %get-tuple-element.189), channel_id=1, source_target_pairs={{0,8},{4,12},{8,0},{12,4},{16,24},{20,28},{24,16},{28,20},{1,9},{5... | collective-permute-start | bytes 2162696 | tf_op jit(solution)/shard_map/ppermute | solution.py:684
  122.9 18.2 %collective-permute-start.34 = (f32[8,88,256]{2,1,0:T(8,128)S(1)}, f32[8,88,256]{2,1,0:T(8,128)S(1)}, u32[]{:S(2)}, u32[]{:S(2)}) collective-permute-start(f32[8,88,256]{2,1,0:T(8,128)S(1)} %get-tuple-element.190), channel_id=1, source_target_pairs={{0,16},{4,20},{8,24},{12,28},{16,0},{20,4},{24,8},{28,12},{1,17},{... | collective-permute-start | bytes 2162696 | tf_op jit(solution)/shard_map/ppermute | solution.py:684
  123.8 17.9 %collective-permute-start.35 = (f32[8,88,256]{2,1,0:T(8,128)S(1)}, f32[8,88,256]{2,1,0:T(8,128)S(1)}, u32[]{:S(2)}, u32[]{:S(2)}) collective-permute-start(f32[8,88,256]{2,1,0:T(8,128)S(1)} %get-tuple-element.191), channel_id=1, source_target_pairs={{0,1},{1,0},{2,3},{3,2},{4,5},{5,4},{6,7},{7,6},{8,9},{9,8},{10,11... | collective-permute-start | bytes 2162696 | tf_op jit(solution)/shard_map/ppermute | solution.py:684
  (18 other events, 206.2 us)

commit v12 on v11

--- a/solution.py
+++ b/solution.py
@@ -323,23 +323,30 @@
     return out[: len(groups)], out[len(groups) :]
 
 
-def join_kernel(heights, here, there, *refs):
-    groups = 1 + max(g for g, unused in here)
-    own, got, outs = refs[:groups], refs[groups : 2 * groups], refs[2 * groups :]
-    count = own[0].shape[0]
-    for s in range(len(heights)):
-        group, rows = rows_of(here, heights, s)
-        out, out_rows = rows_of(there, heights, s)
-        outs[out][:count, out_rows] = own[group][:, rows]
-        outs[out][count:, out_rows] = got[group][:, rows]
-
-
-def join(have, got, orders, step, heights):
-    count, width = have[0].shape[0], have[0].shape[2]
-    unused, here = grouped(orders, step, heights)
-    groups, there = grouped(orders, step - 1, heights)
-    shapes = [(2 * count, height, width) for unused, height in groups]
-    return call(functools.partial(join_kernel, heights, here, there), [*have, *got], shapes)
+def split_kernel(bases, *refs):
+    streams = len(bases)
+    for got, base, out in zip(refs[:streams], bases, refs[streams:]):
+        out[...] = got[:, base : base + out.shape[1]]
+
+
+def extend_kernel(bases, *refs):
+    streams = len(bases)
+    held, owned, got, outs = [refs[i * streams : (i + 1) * streams] for i in range(4)]
+    for s, base in enumerate(bases):
+        count, height = held[s].shape[0], held[s].shape[1]
+        outs[s][:count] = held[s][...]
+        outs[s][count] = owned[s][0, base : base + height]
+        outs[s][count + 1 :] = got[s][...]
+
+
+def near_chunks_kernel(bases, *refs):
+    streams = len(bases)
+    new, held, owned, out = refs[0], refs[1 : streams + 1], refs[streams + 1 : -1], refs[-1]
+    out[0] = new[0]
+    for s, base in enumerate(bases):
+        count, height = held[s].shape[0], held[s].shape[1]
+        out[1 : count + 1, base : base + height] = held[s][...]
+        out[count + 1, base : base + height] = owned[s][0, base : base + height]
 
 
 def last_sums_kernel(heights, here, there, spans, *refs):
@@ -399,27 +406,6 @@
         )
 
 
-def join_all_kernel(heights, here, there, *refs):
-    groups = 1 + max(g for g, unused in here)
-    join_kernel(heights, here, there, *refs[:-1])
-    base = 0
-    for s, height in enumerate(heights):
-        group, rows = rows_of(here, heights, s)
-        for i, ref in enumerate((refs[group], refs[groups + group])):
-            count = ref.shape[0]
-            refs[-1][i * count : (i + 1) * count, base : base + height] = ref[:, rows]
-        base += height
-
-
-def join_all(have, got, orders, step, heights):
-    count, width = 2 * have[0].shape[0], have[0].shape[2]
-    unused, here = grouped(orders, step, heights)
-    groups, there = grouped(orders, step - 1, heights)
-    shapes = [(count, height, width) for height in [h for unused, h in groups] + [sum(heights)]]
-    *have, near = call(functools.partial(join_all_kernel, heights, here, there), [*have, *got], shapes)
-    return have, near
-
-
 def chunk_copies(part, base, first, order, span, chip, component, out_ref, sems, at):
     low, high = span
     width = part.shape[2]
@@ -451,24 +437,25 @@
     streams = len(orders)
     fars = refs[:streams]
     hub_out, rel_out, hub_all, rel_all, sems = refs[-5:]
-    half = near_ref.shape[0]
-    hub_width, rel_width = hub_out.shape[2] // (2 * half), rel_out.shape[2] // (2 * half)
+    known = near_ref.shape[0]
+    chunks = known + fars[0].shape[0]
+    hub_width, rel_width = hub_out.shape[2] // chunks, rel_out.shape[2] // chunks
     copies = []
     if by_copy:
         for far, order, span in zip(fars, orders, spans):
-            copies += chunk_copies(far, 0, half, order, span, spot_ref[0], component, hub_out, sems, len(copies))
+            copies += chunk_copies(far, 0, known, order, span, spot_ref[0], component, hub_out, sems, len(copies))
         for copy in copies:
             copy.start()
-    for chunk in range(2 * half):
+    for chunk in range(chunks):
         place = spot_ref[0] ^ chunk
         for s, (low, high) in enumerate(spans):
             index = spread_bits(place, orders[s])
-            spot = index & (half - 1)
-            height, end = high - low, fars[s].shape[1]
+            near_at, far_at = jnp.minimum(index, known - 1), jnp.maximum(index - known, 0)
+            height, base, end = high - low, bases[s], fars[s].shape[1]
             if not by_copy:
-                value = jnp.where(index >= half, fars[s][spot, :height], near_ref[spot, bases[s] : bases[s] + height])
+                value = jnp.where(index >= known, fars[s][far_at, :height], near_ref[near_at, base : base + height])
                 hub_all[low:high, chunk * hub_width : (chunk + 1) * hub_width] = value
-            value = jnp.where(index >= half, fars[s][spot, height:], near_ref[spot, bases[s] + height : bases[s] + end])
+            value = jnp.where(index >= known, fars[s][far_at, height:], near_ref[near_at, base + height : base + end])
             for stream, row, count, low, wide, to, to_lane in pieces:
                 if stream == s:
                     at = chunk * rel_width + low
@@ -827,24 +814,34 @@
         [*own, *got, rel_parts[0], *rel_got], [x.shape for x in own] + [rel_parts[0].shape, (2, width)],
     )
     hub_own, rel_own = owned
-    groups, there = grouped(back_orders, stages - 1, joint_heights)
+    there = [(0, base) for base in bases]
     ins = [
         *totals, rel_total, squares, other_core(squares),
         hub_own, hub_state[None], rel_own, relation_state[None],
     ]
-    have = pl.pallas_call(
+    [new] = pl.pallas_call(
         functools.partial(update_kernel, spans, rel_spans, joint_pieces, there, features),
         in_specs=[SMEM] + [VMEM] * len(ins),
-        out_specs=[VMEM] * len(groups),
-        out_shape=[jax.ShapeDtypeStruct((1, height, width), F32) for unused, height in groups],
+        out_specs=[VMEM],
+        out_shape=[jax.ShapeDtypeStruct((1, sum(joint_heights), width), F32)],
         scratch_shapes=[pltpu.VMEM((1, x.shape[1]), F32) for x in owned],
         compiler_params=PARAMS,
         cost_estimate=COST,
     )(spot, *ins)
-    for step in range(stages - 1, 1, -1):
-        have = join(have, exchanged(have, step, back_orders), back_orders, step, joint_heights)
-    have, near = join_all(have, exchanged(have, 1, back_orders), back_orders, 1, joint_heights)
-    got = exchanged(have, 0, back_orders)
+    partners = [across(new, place) for place in range(stages)]
+    owned_at = lambda step: [partners[order[step]] for order in back_orders]
+    shapes = lambda count: [(count, height, width) for height in joint_heights]
+    have = call(functools.partial(split_kernel, bases), owned_at(stages - 1), shapes(1))
+    for step in range(stages - 2, 0, -1):
+        got = [across(x, order[step]) for x, order in zip(have, back_orders)]
+        have = call(
+            functools.partial(extend_kernel, bases), [*have, *owned_at(step), *got], shapes(2 * have[0].shape[0] + 1)
+        )
+    got = [across(x, order[0]) for x, order in zip(have, back_orders)]
+    [near] = call(
+        functools.partial(near_chunks_kernel, bases), [new, *have, *owned_at(0)],
+        [(have[0].shape[0] + 2, sum(joint_heights), width)],
+    )
     far_near = other_core(near)
 
     shapes = [hub_emb.shape, relation_emb.shape]

time: 149 us -> 145 us (0.973)
  waiting for transfers between devices: 62.8 us -> 55.1 us
  starting transfers between devices: 40.2 us -> 43.1 us
    ppermute x35 -> x38, waiting for transfers between devices: 58.9 us -> 51.2 us  [flipped(): lax.ppermute(x, axis, [(i, i ^ 1 << bit) for i in range(lax.axis_size(axi...]
    ppermute x35 -> x38, starting transfers between devices: 34.2 us -> 37.1 us  [flipped(): lax.ppermute(x, axis, [(i, i ^ 1 << bit) for i in range(lax.axis_size(axi...]
  transfers between devices with their start and end apart: 39 -> 42, of which waited for: 26 -> 27; matrix products, arithmetic and copies ran while one was open for 0% -> 0% of each run, Pallas kernels for 22% -> 23%
where the time goes in v12:
time: 145 us; the launch traced here: 144 us
  waiting for transfers between devices  55.1 us (38%)
  Pallas kernels  43.5 us (30%)
  starting transfers between devices  43.1 us (30%)
    ppermute x38, waiting for transfers between devices, flipped(): lax.ppermute(x, axis, [(i, i ^ 1 << bit) for i in range(lax.axis_size(axi...  51.2 us
    ppermute x38, starting transfers between devices, flipped(): lax.ppermute(x, axis, [(i, i ^ 1 << bit) for i in range(lax.axis_size(axi...  37.1 us
    pallas_call x1, Pallas kernels, gather_rows(): pl.pallas_call(functools.partial(gather_kernel, hub_steps, rel_steps), in...  10 us
    pallas_call x4, Pallas kernels, placed(): pl.pallas_call(kernel, in_specs=[SMEM] + [VMEM] * (1 + len(fars)) + [HBM]...  9.53 us
    pallas_call x2, Pallas kernels, chunk_columns(): pl.pallas_call(functools.partial(kernel, grad_lanes), in_specs=[SMEM] + [...  8 us
    pallas_call x1, Pallas kernels, bucket_step(): pl.pallas_call(functools.partial(bucket_kernel, bucket), in_specs=[SMEM]...  5.58 us
    pallas_call x1, Pallas kernels, tables_step(): pl.pallas_call(functools.partial(tables_kernel, bucket, hubs), in_specs=[...  5.42 us
    ppermute x3, starting transfers between devices, flipped_by(): lax.ppermute(x, axis, [(i, i ^ offset) for i in range(lax.axis_size(axis))])  5.36 us
  transfers between devices with their start and end apart: 42, of which 27 were waited for; matrix products, arithmetic and copies ran while one was open for 0% of the time, Pallas kernels for 23%

profile of v12, /device:TPU:0, one launch (start us, length us, event | category | flops | bytes accessed | tf_op | source)
XLA Modules:
  0.0 144.3 jit_solution(359865607507722217)
XLA Ops:
  2.7 10.0 %shard_map.156 = (f32[400,256]{1,0:T(8,128)S(1)}, f32[400,256]{1,0:T(8,128)S(1)}, f32[400,512]{1,0:T(8,128)S(1)}, f32[400,512]{1,0:T(8,128)S(1)}, s32[2]{0:T(128...) custom-call(s32[2]{0:T(128)S(1)} %pad_add_fusion.spot_ref, s32[2,256]{1,0:T(2,128)S(1)} %copy-done.7, ...), custom_call_target="tpu_custom_call" | custom-call | flops 10000 | bytes 10000 | tf_op jit(solution)/shard_map/pallas_call | solution.py:135
  12.9 5.6 %shard_map.157 = (f32[400,512]{1,0:T(8,128)S(1)}, f32[1,512]{1,0:T(1,128)S(1)}, f32[408,512]{1,0:T(8,128)S(1)}, f32[200,768]{1,0:T(8,128)S(1)}, f32[200,768]{1,0:T(8,128)S(1)}) custom-call(s32[2]{0:T(128)S(1)} %get-tuple-element.101.core_ref.spot_ref, s32[2,512]{1,0:T(2,128)S(1)} %copy-done.2, s32[2,512]{1,0:T(2,128)S(1)} %copy-done.4, ...), custom_call_target="tpu_custom_call" | custom-call | flops 10000 | bytes 10000 | tf_op jit(solution)/shard_map/pallas_call | solution.py:563
  19.1 2.7 %shard_map.158 = (f32[400,512]{1,0:T(8,128)S(1)}, f32[200,256]{1,0:T(8,128)S(1)}, f32[200,256]{1,0:T(8,128)S(1)}) custom-call(s32[2]{0:T(128)S(1)} %get-tuple-element.101.core_ref.spot_ref, s32[2,512]{1,0:T(2,128)S(1)} %copy-done.2, f32[400,512]{1,0:T(8,128)S(1)} %get-tuple-element.106.left_ref, f32[400,512]{1,0:T(8,128)S(1)} %get-tuple-element.107.rel_ref, ...), custom_call_target="tpu_custom_call" | custom-call | flops 10000 | bytes 10000 | tf_op jit(solution)/shard_map/pallas_call | solution.py:604
  21.8 2.8 %collective-permute-start.3 = (f32[200,768]{1,0:T(8,128)S(1)}, f32[200,768]{1,0:T(8,128)S(1)}, u32[]{:S(2)}, u32[]{:S(2)}) collective-permute-start(f32[200,768]{1,0:T(8,128)S(1)} %get-tuple-element.119), channel_id=1, source_target_pairs={{0,4},{4,0},{8,12},{12,8},{16,20},{20,16},{24,28},{28,24},{1,5},{5... | collective-permute-start | bytes 1843208 | tf_op jit(solution)/shard_map/ppermute | solution.py:671
  24.7 1.9 %collective-permute-done.4.refs_5_ = f32[200,256]{1,0:T(8,128)S(1)} collective-permute-done((f32[200,256]{1,0:T(8,128)S(1)}, f32[200,256]{1,0:T(8,128)S(1)}, u32[]{:S(2)}, u32[]{:S(2)}) %collective-permute-start.4) | collective-permute-done | bytes 204832 | tf_op jit(solution)/shard_map/ppermute | solution.py:671
  26.6 4.3 %shard_map.160 = (f32[8,72,256]{2,1,0:T(8,128)S(1)}, f32[8,64,256]{2,1,0:T(8,128)S(1)}, f32[8,64,256]{2,1,0:T(8,128)S(1)}, f32[8,72,256]{2,1,0:T(8,128)S(1)}, f3...) custom-call(s32[2]{0:T(128)S(1)} %get-tuple-element.101.core_ref.spot_ref, s32[2,256]{1,0:T(2,128)S(1)} %copy-done.7, ...), custom_call_target="tpu_custom_call" | custom-call | flops 10000 | bytes 10000 | tf_op jit(solution)/shard_map/pallas_call | solution.py:280
  32.8 1.8 %collective-permute-start.8 = (f32[8,64,256]{2,1,0:T(8,128)S(1)}, f32[8,64,256]{2,1,0:T(8,128)S(1)}, u32[]{:S(2)}, u32[]{:S(2)}) collective-permute-start(f32[8,64,256]{2,1,0:T(8,128)S(1)} %get-tuple-element.131), channel_id=1, source_target_pairs={{0,1},{1,0},{2,3},{3,2},{4,5},{5,4},{6,7},{7,6},{8,9},{9,8},{10,11... | collective-permute-start | bytes 1572872 | tf_op jit(solution)/shard_map/ppermute | solution.py:671
  34.6 5.4 %shard_map.159 = (f32[400,512]{1,0:T(8,128)}, f32[400,512]{1,0:T(8,128)}, f32[200,512]{1,0:T(8,128)S(1)}, f32[200,512]{1,0:T(8,128)S(1)}) custom-call(s32[2]{0:T(128)S(1)} %get-tuple-element.101.core_ref.spot_ref, s32[2,512]{1,0:T(2,128)S(1)} %copy-done.2, s32[2,512]{1,0:T(2,128)S(1)} %copy-done.4, s32[2,1024]{1,0:T(2,128)S(1)} %copy-done.3, ...), custom_call_target="tpu_custom_call" | custom-call | flops 10000 | bytes 10000 | tf_op jit(solution)/shard_map/pallas_call | solution.py:654
  40.0 1.7 %collective-permute-done.5.refs_5_ = f32[200,512]{1,0:T(8,128)S(1)} collective-permute-done((f32[200,512]{1,0:T(8,128)S(1)}, f32[200,512]{1,0:T(8,128)S(1)}, u32[]{:S(2)}, u32[]{:S(2)}) %collective-permute-start.5) | collective-permute-done | bytes 409632 | tf_op jit(solution)/shard_map/ppermute | solution.py:671
  41.8 3.7 %shard_map.161 = (f32[8,32,256]{2,1,0:T(8,128)S(1)}, f32[8,32,256]{2,1,0:T(8,128)S(1)}, f32[8,32,256]{2,1,0:T(8,128)S(1)}, f32[8,32,256]{2,1,0:T(8,128)S(1)}) custom-call(s32[2]{0:T(128)S(1)} %get-tuple-element.101.core_ref.spot_ref, s32[2,512]{1,0:T(2,128)S(1)} %copy-done.5, s32[2,512]{1,0:T(2,128)S(1)} %collective-permute-done.1.refs_1_, ...), custom_call_target="tpu_custom_call" | custom-call | flops 10000 | bytes 10000 | tf_op jit(solution)/shard_map/pallas_call | solution.py:280
  46.8 1.6 %collective-permute-start.11 = (f32[4,72,256]{2,1,0:T(8,128)S(1)}, f32[4,72,256]{2,1,0:T(8,128)S(1)}, u32[]{:S(2)}, u32[]{:S(2)}) collective-permute-start(f32[4,72,256]{2,1,0:T(8,128)S(1)} %get-tuple-element.149), channel_id=1, source_target_pairs={{0,16},{4,20},{8,24},{12,28},{16,0},{20,4},{24,8},{28,12},{1,17},{... | collective-permute-start | bytes 884744 | tf_op jit(solution)/shard_map/ppermute | solution.py:671
  48.9 1.5 %collective-permute-start.10 = (f32[8,32,256]{2,1,0:T(8,128)S(1)}, f32[8,32,256]{2,1,0:T(8,128)S(1)}, u32[]{:S(2)}, u32[]{:S(2)}) collective-permute-start(f32[8,32,256]{2,1,0:T(8,128)S(1)} %get-tuple-element.139), channel_id=1, source_target_pairs={{0,16},{4,20},{8,24},{12,28},{16,0},{20,4},{24,8},{28,12},{1,17},{... | collective-permute-start | bytes 786440 | tf_op jit(solution)/shard_map/ppermute | solution.py:671
  50.4 1.6 %collective-permute-start.12 = (f32[4,64,256]{2,1,0:T(8,128)S(1)}, f32[4,64,256]{2,1,0:T(8,128)S(1)}, u32[]{:S(2)}, u32[]{:S(2)}) collective-permute-start(f32[4,64,256]{2,1,0:T(8,128)S(1)} %get-tuple-element.150), channel_id=1, source_target_pairs={{0,1},{1,0},{2,3},{3,2},{4,5},{5,4},{6,7},{7,6},{8,9},{9,8},{10,11... | collective-permute-start | bytes 786440 | tf_op jit(solution)/shard_map/ppermute | solution.py:671
  52.6 5.0 %collective-permute-done.9.refs_2_ = f32[8,32,256]{2,1,0:T(8,128)S(1)} collective-permute-done((f32[8,32,256]{2,1,0:T(8,128)S(1)}, f32[8,32,256]{2,1,0:T(8,128)S(1)}, u32[]{:S(2)}, u32[]{:S(2)}) %collective-permute-start.9) | collective-permute-done | bytes 262176 | tf_op jit(solution)/shard_map/ppermute | solution.py:671
  57.6 3.3 %collective-permute-done.10.refs_3_ = f32[8,32,256]{2,1,0:T(8,128)S(1)} collective-permute-done((f32[8,32,256]{2,1,0:T(8,128)S(1)}, f32[8,32,256]{2,1,0:T(8,128)S(1)}, u32[]{:S(2)}, u32[]{:S(2)}) %collective-permute-start.10) | collective-permute-done | bytes 262176 | tf_op jit(solution)/shard_map/ppermute | solution.py:671
  61.5 1.6 %collective-permute-start.14 = (f32[2,72,256]{2,1,0:T(8,128)S(1)}, f32[2,72,256]{2,1,0:T(8,128)S(1)}, u32[]{:S(2)}, u32[]{:S(2)}) collective-permute-start(f32[2,72,256]{2,1,0:T(8,128)S(1)} %get-tuple-element.158), channel_id=1, source_target_pairs={{0,1},{1,0},{2,3},{3,2},{4,5},{5,4},{6,7},{7,6},{8,9},{9,8},{10,11... | collective-permute-start | bytes 442376 | tf_op jit(solution)/shard_map/ppermute | solution.py:671
  66.3 2.6 %collective-permute-start.16 = (f32[2,64,256]{2,1,0:T(8,128)S(1)}, f32[2,64,256]{2,1,0:T(8,128)S(1)}, u32[]{:S(2)}, u32[]{:S(2)}) collective-permute-start(f32[2,64,256]{2,1,0:T(8,128)S(1)} %get-tuple-element.160), channel_id=1, source_target_pairs={{0,2},{1,3},{2,0},{3,1},{4,6},{5,7},{6,4},{7,5},{8,10},{9,11},{10,... | collective-permute-start | bytes 393224 | tf_op jit(solution)/shard_map/ppermute | solution.py:671
  70.6 2.8 %collective-permute-done.16.refs_5_ = f32[2,64,256]{2,1,0:T(8,128)S(1)} collective-permute-done((f32[2,64,256]{2,1,0:T(8,128)S(1)}, f32[2,64,256]{2,1,0:T(8,128)S(1)}, u32[]{:S(2)}, u32[]{:S(2)}) %collective-permute-start.16) | collective-permute-done | bytes 131104 | tf_op jit(solution)/shard_map/ppermute | solution.py:671
  76.4 3.0 %collective-permute-start.21 = (f32[1,64,256]{2,1,0:T(8,128)S(1)}, f32[1,64,256]{2,1,0:T(8,128)S(1)}, u32[]{:S(2)}, u32[]{:S(2)}) collective-permute-start(f32[1,64,256]{2,1,0:T(8,128)S(1)} %get-tuple-element.171), channel_id=1, source_target_pairs={{0,1},{1,0},{2,3},{3,2},{4,5},{5,4},{6,7},{7,6},{8,9},{9,8},{10,11... | collective-permute-start | bytes 196616 | tf_op jit(solution)/shard_map/ppermute | solution.py:675
  79.5 2.3 %collective-permute-start.23 = (f32[1,64,256]{2,1,0:T(8,128)S(1)}, f32[1,64,256]{2,1,0:T(8,128)S(1)}, u32[]{:S(2)}, u32[]{:S(2)}) collective-permute-start(f32[1,64,256]{2,1,0:T(8,128)S(1)} %get-tuple-element.173), channel_id=1, source_target_pairs={{0,3},{1,2},{2,1},{3,0},{4,7},{5,6},{6,5},{7,4},{8,11},{9,10},{10,... | collective-permute-start | bytes 196616 | tf_op jit(solution)/shard_map/ppermute | solution.py:675
  82.5 2.2 %collective-permute-done.22.refs_7_ = f32[1,64,256]{2,1,0:T(8,128)S(1)} collective-permute-done((f32[1,64,256]{2,1,0:T(8,128)S(1)}, f32[1,64,256]{2,1,0:T(8,128)S(1)}, u32[]{:S(2)}, u32[]{:S(2)}) %collective-permute-start.22) | collective-permute-done | bytes 65568 | tf_op jit(solution)/shard_map/ppermute | solution.py:675
  88.3 1.7 %collective-permute-start.25 = (f32[1,264,256]{2,1,0:T(8,128)S(1)}, f32[1,264,256]{2,1,0:T(8,128)S(1)}, u32[]{:S(2)}, u32[]{:S(2)}) collective-permute-start(f32[1,264,256]{2,1,0:T(8,128)S(1)} %shard_map.167.refs_0_), channel_id=1, source_target_pairs={{0,2},{1,3},{2,0},{3,1},{4,6},{5,7},{6,4},{7,5},{8,10},{9,11},{10,... | collective-permute-start | bytes 811016 | tf_op jit(solution)/shard_map/ppermute | solution.py:671
  93.2 10.6 %collective-permute-done.25.refs_0_.refs_1_.refs_2_ = f32[1,264,256]{2,1,0:T(8,128)S(1)} collective-permute-done((f32[1,264,256]{2,1,0:T(8,128)S(1)}, f32[1,264,256]{2,1,0:T(8,128)S(1)}, u32[]{:S(2)}, u32[]{:S(2)}) %collective-permute-start.25) | collective-permute-done | bytes 270368 | tf_op jit(solution)/shard_map/ppermute | solution.py:671
  105.8 2.5 %collective-permute-done.29.refs_6_ = f32[1,88,256]{2,1,0:T(8,128)S(1)} collective-permute-done((f32[1,88,256]{2,1,0:T(8,128)S(1)}, f32[1,88,256]{2,1,0:T(8,128)S(1)}, u32[]{:S(2)}, u32[]{:S(2)}) %collective-permute-start.29) | collective-permute-done | bytes 90144 | tf_op jit(solution)/shard_map/ppermute | solution.py:671
  110.5 1.9 %collective-permute-start.33 = (f32[3,88,256]{2,1,0:T(8,128)S(1)}, f32[3,88,256]{2,1,0:T(8,128)S(1)}, u32[]{:S(2)}, u32[]{:S(2)}) collective-permute-start(f32[3,88,256]{2,1,0:T(8,128)S(1)} %get-tuple-element.185.refs_1_), channel_id=1, source_target_pairs={{0,1},{1,0},{2,3},{3,2},{4,5},{5,4},{6,7},{7,6},{8,9},{9,8},{10,11... | collective-permute-start | bytes 811016 | tf_op jit(solution)/shard_map/ppermute | solution.py:671
  113.7 2.7 %collective-permute-done.32.refs_6_ = f32[3,88,256]{2,1,0:T(8,128)S(1)} collective-permute-done((f32[3,88,256]{2,1,0:T(8,128)S(1)}, f32[3,88,256]{2,1,0:T(8,128)S(1)}, u32[]{:S(2)}, u32[]{:S(2)}) %collective-permute-start.32) | collective-permute-done | bytes 270368 | tf_op jit(solution)/shard_map/ppermute | solution.py:671
  117.0 1.9 %collective-permute-done.34.refs_8_ = f32[3,88,256]{2,1,0:T(8,128)S(1)} collective-permute-done((f32[3,88,256]{2,1,0:T(8,128)S(1)}, f32[3,88,256]{2,1,0:T(8,128)S(1)}, u32[]{:S(2)}, u32[]{:S(2)}) %collective-permute-start.34) | collective-permute-done | bytes 270368 | tf_op jit(solution)/shard_map/ppermute | solution.py:671
  121.6 2.0 %shard_map.172.refs_0_ = f32[2,200,4096]{2,1,0:T(8,128)} custom-call(s32[2]{0:T(128)S(1)} %get-tuple-element.101.core_ref.spot_ref, f32[9,264,256]{2,1,0:T(8,128)S(1)} %shard_map.171.near_ref), custom_call_target="tpu_custom_call" | custom-call | bytes 3276800 | tf_op jit(solution)/shard_map/pallas_call | solution.py:474
  123.9 2.0 %shard_map.173.refs_3_ = f32[2,200,4096]{2,1,0:T(8,128)} custom-call(s32[2]{0:T(128)S(1)} %get-tuple-element.101.core_ref.spot_ref, f32[9,264,256]{2,1,0:T(8,128)S(1)} %collective-permute-done.35.near_ref, f32[2,200,4096]{2,1,0:T(8,128)} %shard_map.172.refs_0_), custom_call_target="tpu_custom_call", output_to_operand_aliasing={{}: (2, {})} | custom-call | bytes 3276800 | tf_op jit(solution)/shard_map/pallas_call | solution.py:474
  125.9 10.0 %collective-permute-done.36.refs_0_ = f32[7,88,256]{2,1,0:T(8,128)S(1)} collective-permute-done((f32[7,88,256]{2,1,0:T(8,128)S(1)}, f32[7,88,256]{2,1,0:T(8,128)S(1)}, u32[]{:S(2)}, u32[]{:S(2)}) %collective-permute-start.36) | collective-permute-done | bytes 630816 | tf_op jit(solution)/shard_map/ppermute | solution.py:671
  138.0 2.8 %shard_map.174 = (f32[2,200,4096]{2,1,0:T(8,128)}, f32[2,200,1280]{2,1,0:T(8,128)}) custom-call(s32[2]{0:T(128)S(1)} %get-tuple-element.101.core_ref.spot_ref, f32[9,264,256]{2,1,0:T(8,128)S(1)} %shard_map.171.near_ref, f32[7,88,256]{2,1,0:T(8,128)S(1)} %collective-permute-done.36.refs_0_, ...), custom_call_target="tpu_custom_call", output_to_operand_aliasing={{0}: (5, {})} | custom-call | bytes 3276800 | tf_op jit(solution)/shard_map/pallas_call | solution.py:474
  141.4 2.8 %shard_map.175 = (f32[2,200,4096]{2,1,0:T(8,128)}, f32[2,200,1280]{2,1,0:T(8,128)}) custom-call(s32[2]{0:T(128)S(1)} %get-tuple-element.101.core_ref.spot_ref, f32[9,264,256]{2,1,0:T(8,128)S(1)} %collective-permute-done.35.near_ref, f32[7,88,256]{2,1,0:T(8,128)S(1)} %collective-permute-done.39.refs_0_, ...), custom_call_target="tpu_custom_call", output_to_operand_aliasing={{0}: (5, {}), {1}: (6, {})} | custom-call | bytes 3276800 | tf_op jit(solution)/shard_map/pallas_call | solution.py:474
  (96 shorter events, 34.8 us)
Async XLA Ops:
  0.7 12.1 %collective-permute-start = (s32[2,256]{1,0:T(2,128)}, s32[2,256]{1,0:T(2,128)S(1)}, u32[]{:S(2)}, u32[]{:S(2)}) collective-permute-start(s32[2,256]{1,0:T(2,128)} %refs_0_.2), channel_id=1, source_target_pairs={{0,4},{4,0},{8,12},{12,8},{16,20},{20,16},{24,28},{28,24},{1,5},{5... | collective-permute-start | bytes 6152 | tf_op jit(solution)/shard_map/ppermute | solution.py:671
  1.2 11.6 %collective-permute-start.1 = (s32[2,512]{1,0:T(2,128)}, s32[2,512]{1,0:T(2,128)S(1)}, u32[]{:S(2)}, u32[]{:S(2)}) collective-permute-start(s32[2,512]{1,0:T(2,128)} %refs_0_.3), channel_id=1, source_target_pairs={{0,4},{4,0},{8,12},{12,8},{16,20},{20,16},{24,28},{28,24},{1,5},{5... | collective-permute-start | bytes 12296 | tf_op jit(solution)/shard_map/ppermute | solution.py:671
  18.5 16.2 %collective-permute-start.2 = (f32[408,512]{1,0:T(8,128)S(1)}, f32[408,512]{1,0:T(8,128)S(1)}, u32[]{:S(2)}, u32[]{:S(2)}) collective-permute-start(f32[408,512]{1,0:T(8,128)S(1)} %get-tuple-element.111), channel_id=1, source_target_pairs={{0,4},{4,8},{8,12},{12,16},{16,20},{20,24},{24,28},{28,0},{1,5},{5... | collective-permute-start | bytes 2506760 | tf_op jit(solution)/shard_map/ppermute | solution.py:667
  21.8 4.7 %collective-permute-start.3 = (f32[200,768]{1,0:T(8,128)S(1)}, f32[200,768]{1,0:T(8,128)S(1)}, u32[]{:S(2)}, u32[]{:S(2)}) collective-permute-start(f32[200,768]{1,0:T(8,128)S(1)} %get-tuple-element.119), channel_id=1, source_target_pairs={{0,4},{4,0},{8,12},{12,8},{16,20},{20,16},{24,28},{28,24},{1,5},{5... | collective-permute-start | bytes 1843208 | tf_op jit(solution)/shard_map/ppermute | solution.py:671
  30.9 15.7 %collective-permute-start.6 = (f32[8,72,256]{2,1,0:T(8,128)S(1)}, f32[8,72,256]{2,1,0:T(8,128)S(1)}, u32[]{:S(2)}, u32[]{:S(2)}) collective-permute-start(f32[8,72,256]{2,1,0:T(8,128)S(1)} %get-tuple-element.129), channel_id=1, source_target_pairs={{0,8},{4,12},{8,0},{12,4},{16,24},{20,28},{24,16},{28,20},{1,9},{5... | collective-permute-start | bytes 1769480 | tf_op jit(solution)/shard_map/ppermute | solution.py:671
  32.4 13.9 %collective-permute-start.7 = (f32[8,64,256]{2,1,0:T(8,128)S(1)}, f32[8,64,256]{2,1,0:T(8,128)S(1)}, u32[]{:S(2)}, u32[]{:S(2)}) collective-permute-start(f32[8,64,256]{2,1,0:T(8,128)S(1)} %get-tuple-element.130), channel_id=1, source_target_pairs={{0,16},{4,20},{8,24},{12,28},{16,0},{20,4},{24,8},{28,12},{1,17},{... | collective-permute-start | bytes 1572872 | tf_op jit(solution)/shard_map/ppermute | solution.py:671
  32.8 13.7 %collective-permute-start.8 = (f32[8,64,256]{2,1,0:T(8,128)S(1)}, f32[8,64,256]{2,1,0:T(8,128)S(1)}, u32[]{:S(2)}, u32[]{:S(2)}) collective-permute-start(f32[8,64,256]{2,1,0:T(8,128)S(1)} %get-tuple-element.131), channel_id=1, source_target_pairs={{0,1},{1,0},{2,3},{3,2},{4,5},{5,4},{6,7},{7,6},{8,9},{9,8},{10,11... | collective-permute-start | bytes 1572872 | tf_op jit(solution)/shard_map/ppermute | solution.py:671
  46.8 14.7 %collective-permute-start.11 = (f32[4,72,256]{2,1,0:T(8,128)S(1)}, f32[4,72,256]{2,1,0:T(8,128)S(1)}, u32[]{:S(2)}, u32[]{:S(2)}) collective-permute-start(f32[4,72,256]{2,1,0:T(8,128)S(1)} %get-tuple-element.149), channel_id=1, source_target_pairs={{0,16},{4,20},{8,24},{12,28},{16,0},{20,4},{24,8},{28,12},{1,17},{... | collective-permute-start | bytes 884744 | tf_op jit(solution)/shard_map/ppermute | solution.py:671
  48.3 9.2 %collective-permute-start.9 = (f32[8,32,256]{2,1,0:T(8,128)S(1)}, f32[8,32,256]{2,1,0:T(8,128)S(1)}, u32[]{:S(2)}, u32[]{:S(2)}) collective-permute-start(f32[8,32,256]{2,1,0:T(8,128)S(1)} %get-tuple-element.138), channel_id=1, source_target_pairs={{0,8},{4,12},{8,0},{12,4},{16,24},{20,28},{24,16},{28,20},{1,9},{5... | collective-permute-start | bytes 786440 | tf_op jit(solution)/shard_map/ppermute | solution.py:671
  48.9 12.0 %collective-permute-start.10 = (f32[8,32,256]{2,1,0:T(8,128)S(1)}, f32[8,32,256]{2,1,0:T(8,128)S(1)}, u32[]{:S(2)}, u32[]{:S(2)}) collective-permute-start(f32[8,32,256]{2,1,0:T(8,128)S(1)} %get-tuple-element.139), channel_id=1, source_target_pairs={{0,16},{4,20},{8,24},{12,28},{16,0},{20,4},{24,8},{28,12},{1,17},{... | collective-permute-start | bytes 786440 | tf_op jit(solution)/shard_map/ppermute | solution.py:671
  50.4 10.6 %collective-permute-start.12 = (f32[4,64,256]{2,1,0:T(8,128)S(1)}, f32[4,64,256]{2,1,0:T(8,128)S(1)}, u32[]{:S(2)}, u32[]{:S(2)}) collective-permute-start(f32[4,64,256]{2,1,0:T(8,128)S(1)} %get-tuple-element.150), channel_id=1, source_target_pairs={{0,1},{1,0},{2,3},{3,2},{4,5},{5,4},{6,7},{7,6},{8,9},{9,8},{10,11... | collective-permute-start | bytes 786440 | tf_op jit(solution)/shard_map/ppermute | solution.py:671
  52.0 9.5 %collective-permute-start.13 = (f32[4,64,256]{2,1,0:T(8,128)S(1)}, f32[4,64,256]{2,1,0:T(8,128)S(1)}, u32[]{:S(2)}, u32[]{:S(2)}) collective-permute-start(f32[4,64,256]{2,1,0:T(8,128)S(1)} %get-tuple-element.151), channel_id=1, source_target_pairs={{0,8},{4,12},{8,0},{12,4},{16,24},{20,28},{24,16},{28,20},{1,9},{5... | collective-permute-start | bytes 786440 | tf_op jit(solution)/shard_map/ppermute | solution.py:671
  61.5 11.9 %collective-permute-start.14 = (f32[2,72,256]{2,1,0:T(8,128)S(1)}, f32[2,72,256]{2,1,0:T(8,128)S(1)}, u32[]{:S(2)}, u32[]{:S(2)}) collective-permute-start(f32[2,72,256]{2,1,0:T(8,128)S(1)} %get-tuple-element.158), channel_id=1, source_target_pairs={{0,1},{1,0},{2,3},{3,2},{4,5},{5,4},{6,7},{7,6},{8,9},{9,8},{10,11... | collective-permute-start | bytes 442376 | tf_op jit(solution)/shard_map/ppermute | solution.py:671
  63.2 5.7 %collective-permute-start.17 = (f32[4,32,256]{2,1,0:T(8,128)S(1)}, f32[4,32,256]{2,1,0:T(8,128)S(1)}, u32[]{:S(2)}, u32[]{:S(2)}) collective-permute-start(f32[4,32,256]{2,1,0:T(8,128)S(1)} %get-tuple-element.163), channel_id=1, source_target_pairs={{0,16},{4,20},{8,24},{12,28},{16,0},{20,4},{24,8},{28,12},{1,17},{... | collective-permute-start | bytes 393224 | tf_op jit(solution)/shard_map/ppermute | solution.py:671
  64.3 5.0 %collective-permute-start.18 = (f32[4,32,256]{2,1,0:T(8,128)S(1)}, f32[4,32,256]{2,1,0:T(8,128)S(1)}, u32[]{:S(2)}, u32[]{:S(2)}) collective-permute-start(f32[4,32,256]{2,1,0:T(8,128)S(1)} %get-tuple-element.164), channel_id=1, source_target_pairs={{0,8},{4,12},{8,0},{12,4},{16,24},{20,28},{24,16},{28,20},{1,9},{5... | collective-permute-start | bytes 393224 | tf_op jit(solution)/shard_map/ppermute | solution.py:671
  65.2 5.4 %collective-permute-start.15 = (f32[2,64,256]{2,1,0:T(8,128)S(1)}, f32[2,64,256]{2,1,0:T(8,128)S(1)}, u32[]{:S(2)}, u32[]{:S(2)}) collective-permute-start(f32[2,64,256]{2,1,0:T(8,128)S(1)} %get-tuple-element.159), channel_id=1, source_target_pairs={{0,8},{4,12},{8,0},{12,4},{16,24},{20,28},{24,16},{28,20},{1,9},{5... | collective-permute-start | bytes 393224 | tf_op jit(solution)/shard_map/ppermute | solution.py:671
  66.3 7.2 %collective-permute-start.16 = (f32[2,64,256]{2,1,0:T(8,128)S(1)}, f32[2,64,256]{2,1,0:T(8,128)S(1)}, u32[]{:S(2)}, u32[]{:S(2)}) collective-permute-start(f32[2,64,256]{2,1,0:T(8,128)S(1)} %get-tuple-element.160), channel_id=1, source_target_pairs={{0,2},{1,3},{2,0},{3,1},{4,6},{5,7},{6,4},{7,5},{8,10},{9,11},{10,... | collective-permute-start | bytes 393224 | tf_op jit(solution)/shard_map/ppermute | solution.py:671
  73.5 12.1 %collective-permute-start.19 = (f32[1,136,256]{2,1,0:T(8,128)S(1)}, f32[1,136,256]{2,1,0:T(8,128)S(1)}, u32[]{:S(2)}, u32[]{:S(2)}) collective-permute-start(f32[1,136,256]{2,1,0:T(8,128)S(1)} %get-tuple-element.168), channel_id=1, source_target_pairs={{0,2},{1,3},{2,0},{3,1},{4,6},{5,7},{6,4},{7,5},{8,10},{9,11},{10,... | collective-permute-start | bytes 417800 | tf_op jit(solution)/shard_map/ppermute | solution.py:671
  75.0 6.8 %collective-permute-start.20 = (f32[1,64,256]{2,1,0:T(8,128)S(1)}, f32[1,64,256]{2,1,0:T(8,128)S(1)}, u32[]{:S(2)}, u32[]{:S(2)}) collective-permute-start(f32[1,64,256]{2,1,0:T(8,128)S(1)} %get-tuple-element.169), channel_id=1, source_target_pairs={{0,16},{4,20},{8,24},{12,28},{16,0},{20,4},{24,8},{28,12},{1,17},{... | collective-permute-start | bytes 196616 | tf_op jit(solution)/shard_map/ppermute | solution.py:671
  76.4 6.1 %collective-permute-start.21 = (f32[1,64,256]{2,1,0:T(8,128)S(1)}, f32[1,64,256]{2,1,0:T(8,128)S(1)}, u32[]{:S(2)}, u32[]{:S(2)}) collective-permute-start(f32[1,64,256]{2,1,0:T(8,128)S(1)} %get-tuple-element.171), channel_id=1, source_target_pairs={{0,1},{1,0},{2,3},{3,2},{4,5},{5,4},{6,7},{7,6},{8,9},{9,8},{10,11... | collective-permute-start | bytes 196616 | tf_op jit(solution)/shard_map/ppermute | solution.py:675
  79.4 5.3 %collective-permute-start.22 = (f32[1,64,256]{2,1,0:T(8,128)S(1)}, f32[1,64,256]{2,1,0:T(8,128)S(1)}, u32[]{:S(2)}, u32[]{:S(2)}) collective-permute-start(f32[1,64,256]{2,1,0:T(8,128)S(1)} %get-tuple-element.172), channel_id=1, source_target_pairs={{0,2},{1,3},{2,0},{3,1},{4,6},{5,7},{6,4},{7,5},{8,10},{9,11},{10,... | collective-permute-start | bytes 196616 | tf_op jit(solution)/shard_map/ppermute | solution.py:675
  79.5 6.2 %collective-permute-start.23 = (f32[1,64,256]{2,1,0:T(8,128)S(1)}, f32[1,64,256]{2,1,0:T(8,128)S(1)}, u32[]{:S(2)}, u32[]{:S(2)}) collective-permute-start(f32[1,64,256]{2,1,0:T(8,128)S(1)} %get-tuple-element.173), channel_id=1, source_target_pairs={{0,3},{1,2},{2,1},{3,0},{4,7},{5,6},{6,5},{7,4},{8,11},{9,10},{10,... | collective-permute-start | bytes 196616 | tf_op jit(solution)/shard_map/ppermute | solution.py:675
  88.3 15.4 %collective-permute-start.25 = (f32[1,264,256]{2,1,0:T(8,128)S(1)}, f32[1,264,256]{2,1,0:T(8,128)S(1)}, u32[]{:S(2)}, u32[]{:S(2)}) collective-permute-start(f32[1,264,256]{2,1,0:T(8,128)S(1)} %shard_map.167.refs_0_), channel_id=1, source_target_pairs={{0,2},{1,3},{2,0},{3,1},{4,6},{5,7},{6,4},{7,5},{8,10},{9,11},{10,... | collective-permute-start | bytes 811016 | tf_op jit(solution)/shard_map/ppermute | solution.py:671
  90.1 14.9 %collective-permute-start.28 = (f32[1,264,256]{2,1,0:T(8,128)S(1)}, f32[1,264,256]{2,1,0:T(8,128)S(1)}, u32[]{:S(2)}, u32[]{:S(2)}) collective-permute-start(f32[1,264,256]{2,1,0:T(8,128)S(1)} %shard_map.167.refs_0_), channel_id=1, source_target_pairs={{0,16},{4,20},{8,24},{12,28},{16,0},{20,4},{24,8},{28,12},{1,17},{... | collective-permute-start | bytes 811016 | tf_op jit(solution)/shard_map/ppermute | solution.py:671
  91.1 14.7 %collective-permute-start.27 = (f32[1,264,256]{2,1,0:T(8,128)S(1)}, f32[1,264,256]{2,1,0:T(8,128)S(1)}, u32[]{:S(2)}, u32[]{:S(2)}) collective-permute-start(f32[1,264,256]{2,1,0:T(8,128)S(1)} %shard_map.167.refs_0_), channel_id=1, source_target_pairs={{0,8},{4,12},{8,0},{12,4},{16,24},{20,28},{24,16},{28,20},{1,9},{5... | collective-permute-start | bytes 811016 | tf_op jit(solution)/shard_map/ppermute | solution.py:671
  92.0 13.9 %collective-permute-start.26 = (f32[1,264,256]{2,1,0:T(8,128)S(1)}, f32[1,264,256]{2,1,0:T(8,128)S(1)}, u32[]{:S(2)}, u32[]{:S(2)}) collective-permute-start(f32[1,264,256]{2,1,0:T(8,128)S(1)} %shard_map.167.refs_0_), channel_id=1, source_target_pairs={{0,1},{1,0},{2,3},{3,2},{4,5},{5,4},{6,7},{7,6},{8,9},{9,8},{10,11... | collective-permute-start | bytes 811016 | tf_op jit(solution)/shard_map/ppermute | solution.py:671
  109.5 6.8 %collective-permute-start.32 = (f32[3,88,256]{2,1,0:T(8,128)S(1)}, f32[3,88,256]{2,1,0:T(8,128)S(1)}, u32[]{:S(2)}, u32[]{:S(2)}) collective-permute-start(f32[3,88,256]{2,1,0:T(8,128)S(1)} %get-tuple-element.184.refs_0_), channel_id=1, source_target_pairs={{0,16},{4,20},{8,24},{12,28},{16,0},{20,4},{24,8},{28,12},{1,17},{... | collective-permute-start | bytes 811016 | tf_op jit(solution)/shard_map/ppermute | solution.py:671
  110.5 6.5 %collective-permute-start.33 = (f32[3,88,256]{2,1,0:T(8,128)S(1)}, f32[3,88,256]{2,1,0:T(8,128)S(1)}, u32[]{:S(2)}, u32[]{:S(2)}) collective-permute-start(f32[3,88,256]{2,1,0:T(8,128)S(1)} %get-tuple-element.185.refs_1_), channel_id=1, source_target_pairs={{0,1},{1,0},{2,3},{3,2},{4,5},{5,4},{6,7},{7,6},{8,9},{9,8},{10,11... | collective-permute-start | bytes 811016 | tf_op jit(solution)/shard_map/ppermute | solution.py:671
  112.4 6.5 %collective-permute-start.34 = (f32[3,88,256]{2,1,0:T(8,128)S(1)}, f32[3,88,256]{2,1,0:T(8,128)S(1)}, u32[]{:S(2)}, u32[]{:S(2)}) collective-permute-start(f32[3,88,256]{2,1,0:T(8,128)S(1)} %get-tuple-element.186.refs_2_), channel_id=1, source_target_pairs={{0,8},{4,12},{8,0},{12,4},{16,24},{20,28},{24,16},{28,20},{1,9},{5... | collective-permute-start | bytes 811016 | tf_op jit(solution)/shard_map/ppermute | solution.py:671
  119.3 16.6 %collective-permute-start.36 = (f32[7,88,256]{2,1,0:T(8,128)S(1)}, f32[7,88,256]{2,1,0:T(8,128)S(1)}, u32[]{:S(2)}, u32[]{:S(2)}) collective-permute-start(f32[7,88,256]{2,1,0:T(8,128)S(1)} %get-tuple-element.187.refs_1_), channel_id=1, source_target_pairs={{0,8},{4,12},{8,0},{12,4},{16,24},{20,28},{24,16},{28,20},{1,9},{5... | collective-permute-start | bytes 1892360 | tf_op jit(solution)/shard_map/ppermute | solution.py:671
  120.6 16.3 %collective-permute-start.37 = (f32[7,88,256]{2,1,0:T(8,128)S(1)}, f32[7,88,256]{2,1,0:T(8,128)S(1)}, u32[]{:S(2)}, u32[]{:S(2)}) collective-permute-start(f32[7,88,256]{2,1,0:T(8,128)S(1)} %get-tuple-element.188.refs_2_), channel_id=1, source_target_pairs={{0,16},{4,20},{8,24},{12,28},{16,0},{20,4},{24,8},{28,12},{1,17},{... | collective-permute-start | bytes 1892360 | tf_op jit(solution)/shard_map/ppermute | solution.py:671
  121.5 16.0 %collective-permute-start.38 = (f32[7,88,256]{2,1,0:T(8,128)S(1)}, f32[7,88,256]{2,1,0:T(8,128)S(1)}, u32[]{:S(2)}, u32[]{:S(2)}) collective-permute-start(f32[7,88,256]{2,1,0:T(8,128)S(1)} %get-tuple-element.189.refs_3_), channel_id=1, source_target_pairs={{0,1},{1,0},{2,3},{3,2},{4,5},{5,4},{6,7},{7,6},{8,9},{9,8},{10,11... | collective-permute-start | bytes 1892360 | tf_op jit(solution)/shard_map/ppermute | solution.py:671
  (21 other events, 219.4 us)

commit v13 on v12

--- a/solution.py
+++ b/solution.py
@@ -90,8 +90,8 @@
     hub_tile, rel_tile = hub_buf.shape[2], rel_buf.shape[2]
     chunks = hub_ref.shape[1] // hub_own.shape[1]
     half = hub_own.shape[0]
-    steps = [(hub_ref, hub_buf, hub_tile, k) for k in range(hub_steps)]
-    steps += [(rel_ref, rel_buf, rel_tile, k) for k in range(rel_steps)]
+    steps = [(rel_ref, rel_buf, rel_tile, k) for k in range(rel_steps)]
+    steps += [(hub_ref, hub_buf, hub_tile, k) for k in range(hub_steps)]
     copies = [
         pltpu.make_async_copy(table.at[:, pl.ds(k * tile, tile)], buf.at[k % 2], sems.at[i])
         for i, (table, buf, tile, k) in enumerate(steps)
@@ -100,7 +100,8 @@
         pltpu.make_async_copy(ids, out, sems.at[len(copies) + i])
         for i, (ids, out) in enumerate([(hub_ids, hub_idx), (rel_ids, rel_idx)])
     ]
-    for copy in [*id_copies, copies[0]]:
+    ahead = rel_steps + 2
+    for copy in [*id_copies, *copies[:ahead]]:
         copy.start()
     spot_out[0] = spot_ref[0]
     spot_out[1] = spot_ref[1]
@@ -108,8 +109,6 @@
         copy.wait()
     rows = pl.ds(pl.multiple_of(spot_ref[1] * half, 8), half)
     for i, (table, buf, tile, k) in enumerate(steps):
-        if i + 1 < len(steps):
-            copies[i + 1].start()
         idx, outs, own = (hub_idx, hub_outs, hub_own) if table is hub_ref else (rel_idx, rel_outs, rel_own)
         count = idx.shape[1]
         hot = onehot(k * tile, tile, laid_out(idx[...]))
@@ -120,6 +119,8 @@
             here = part[:, b * count : (b + 1) * count]
             out[...] = here if k == 0 else out[...] + here
         take_owned(spot_ref, chunks, tile, k * tile, lambda lanes: buf[k % 2, rows, lanes], own)
+        if i >= rel_steps and i + 2 < len(steps):
+            copies[i + 2].start()
 
 
 def gather_rows(spot, hub_table, hub_idx, rel_table, rel_idx, chunks):
@@ -291,14 +292,14 @@
     )(spot, *ids, *[g for g, unused in grads])
 
 
-def call(kernel, ins, shapes):
+def call(kernel, ins, shapes, cost=None):
     return pl.pallas_call(
         kernel,
         in_specs=[VMEM] * len(ins),
         out_specs=[VMEM] * len(shapes),
         out_shape=[jax.ShapeDtypeStruct(shape, F32) for shape in shapes],
         compiler_params=PARAMS,
-        cost_estimate=COST,
+        cost_estimate=cost or COST,
     )(*ins)
 
 
@@ -615,51 +616,61 @@
     )(core, heads, left, rel_rows, hub_rows)
 
 
-def tables_kernel(
-    bucket, hubs, core_ref, heads_ref, tails_ref, negs_ref, query_grad,
-    left_ref, left_sums_ref, right_ref, rel_ref,
-    left_out, right_out, rel_keep, rel_send,
+def relations_kernel(
+    bucket, hubs, core_ref, heads_ref, tails_ref, negs_ref, query_grad, left_ref, right_ref, rel_ref,
+    rel_keep, rel_send, query_out, coef_out, head_grad,
     left_parts, right_parts,
 ):
     features, rows = left_ref.shape
     half = features // 2
     edges = heads_ref.shape[1]
     at = slice(bucket, bucket + 1)
-    core = core_ref[1]
     counts = table_counts(rows, negs_ref[at], 1.0 / (negs_ref.shape[1] + hubs))
     stack_into(left_parts, left_ref[...])
     stack_into(right_parts, right_ref[:features])
-
     tail_here = lax.broadcasted_iota(jnp.int32, (rows, edges), 0) == tails_ref[at]
-    head_hot = onehot(0, rows, heads_ref[at])
-    h = dot2(left_parts[...], head_hot, NN)
+    h = dot2(left_parts[...], onehot(0, rows, heads_ref[at]), NN)
     r = rel_ref[...]
     q = split(turned(h, r, half))
     chance = jax.nn.sigmoid(dot3((right_parts[:features], right_parts[features:]), q, TN))
     coef = split(counts * chance + jnp.where(tail_here, chance - 1.0, 0.0))
     dq = dot3_stacked(right_parts[...], coef, NN) + query_grad[...]
-    right_grad = dot3_stacked(stack(q), coef, NT)
-    rel_keep[...], rel_send[...] = keep_and_send(core, *turned_back(dq, h, half))
-    dh = jnp.concatenate(turned_back(dq, r, half), axis=0)
-    left_grad = dot2(stack(split(dh)), head_hot, NT)
-
-    left_out[...], unused = adagrad(left_ref[...], left_sums_ref[...], left_grad)
-    right_out[...], unused = adagrad(right_ref[:features], right_ref[features : features + 1], right_grad)
-
-
-def tables_step(bucket, hubs, core, heads, tails, negs, query_grad, left, left_sums, right, rel_rows):
+    rel_keep[...], rel_send[...] = keep_and_send(core_ref[1], *turned_back(dq, h, half))
+    query_out[...] = stack(q)
+    coef_out[0], coef_out[1] = coef
+    head_grad[:half], head_grad[half:] = turned_back(dq, r, half)
+
+
+def relations_step(bucket, hubs, core, heads, tails, negs, query_grad, left, right, rel_rows):
     features, rows = left.shape
     edges = heads.shape[1]
-    shapes = [(features, rows)] * 2 + [(features // 2, edges)] * 2
+    half = jax.ShapeDtypeStruct((features // 2, edges), F32)
     return pl.pallas_call(
-        functools.partial(tables_kernel, bucket, hubs),
-        in_specs=[SMEM] + [VMEM] * 8,
-        out_specs=[VMEM] * 4,
-        out_shape=[jax.ShapeDtypeStruct(shape, F32) for shape in shapes],
+        functools.partial(relations_kernel, bucket, hubs),
+        in_specs=[SMEM] + [VMEM] * 7,
+        out_specs=[VMEM] * 5,
+        out_shape=[
+            half,
+            half,
+            jax.ShapeDtypeStruct((2 * features, edges), BF16),
+            jax.ShapeDtypeStruct((2, rows, edges), BF16),
+            jax.ShapeDtypeStruct((features, edges), F32),
+        ],
         scratch_shapes=[pltpu.VMEM((2 * features, rows), BF16)] * 2,
         compiler_params=PARAMS,
         cost_estimate=COST,
-    )(core, heads, tails, negs, query_grad, left, left_sums, right, rel_rows)
+    )(core, heads, tails, negs, query_grad, left, right, rel_rows)
+
+
+def tables_kernel(
+    bucket, heads_ref, left_ref, left_sums_ref, right_ref, query_ref, coef_ref, head_grad, left_out, right_out
+):
+    features, rows = left_ref.shape
+    head_hot = onehot(0, rows, heads_ref[bucket : bucket + 1])
+    left_grad = dot2(stack(split(head_grad[...])), head_hot, NT)
+    left_out[...], unused = adagrad(left_ref[...], left_sums_ref[...], left_grad)
+    right_grad = dot3_stacked(query_ref[...], (coef_ref[0], coef_ref[1]), NT)
+    right_out[...], unused = adagrad(right_ref[:features], right_ref[features : features + 1], right_grad)
 
 
 def from_behind(x, axis, by):
@@ -777,9 +788,10 @@
     )
     send, own = parts[: len(groups)], parts[len(groups) :]
     got = exchanged(send, 0)
-    left, right, rel_keep, rel_send = tables_step(
-        last, hubs, spot, heads, tails, negatives, query_grad, left, left_sums, right, rel_rows[last]
-    )
+    rel_keep, rel_send, *parts = relations_step(
+        last, hubs, spot, heads, tails, negatives, query_grad, left, right, rel_rows[last]
+    )
+    later = [heads, left, left_sums, right, *parts]
     rel_far = other_core(rel_send)
 
     parts = chunk_columns(
@@ -850,8 +862,15 @@
     if by_copy:
         near_step = functools.partial(near_kernel, back_orders, spans, bases)
         hub_new = placed(functools.partial(near_step, True), [], spot, near, [], shapes[:1], [])
+        later, hub_new = in_turn(later, hub_new)
+        left, right = call(
+            functools.partial(tables_kernel, last), later, [left.shape] * 2,
+            pl.CostEstimate(flops=3 * 10**9, bytes_accessed=10**7, transcendentals=0),
+        )
         hub_new = placed(functools.partial(near_step, False), [], spot, far_near, [], shapes[:1], hub_new)
-        got, hub_new = in_turn(got, hub_new)
+        got, hub_new, left, right = lax.optimization_barrier((got, hub_new, left, right))
+    else:
+        left, right = call(functools.partial(tables_kernel, last), later, [left.shape] * 2)
     far_step = functools.partial(far_kernel, back_orders, spans, bases, joint_pieces, by_copy)
     scratch = [
         pltpu.VMEM((8, 128) if by_copy else (half_width, hub_count), F32),

time: 145 us -> 145 us (level)
  waiting for transfers between devices: 55.1 us -> 58.1 us
  starting transfers between devices: 43.1 us -> 40.5 us
    pallas_call x9 -> x10, Pallas kernels: 0.92 us -> 3.37 us  [call(): pl.pallas_call(kernel, in_specs=[VMEM] * len(ins), out_specs=[VMEM] * len...]
    ppermute x38, waiting for transfers between devices: 51.2 us -> 53.5 us  [flipped(): lax.ppermute(x, axis, [(i, i ^ 1 << bit) for i in range(lax.axis_size(axi...]
    pallas_call x1, Pallas kernels: 5.42 us -> 3.47 us  [relations_step(): pl.pallas_call(functools.partial(relations_kernel, bucket, hubs), in_spec...]
    ppermute x38, starting transfers between devices: 37.1 us -> 35.5 us  [flipped(): lax.ppermute(x, axis, [(i, i ^ 1 << bit) for i in range(lax.axis_size(axi...]
  transfers between devices with their start and end apart: 42 -> 42, of which waited for: 27 -> 25; matrix products, arithmetic and copies ran while one was open for 0% -> 0% of each run, Pallas kernels for 23% -> 23%
where the time goes in v13:
time: 145 us
  waiting for transfers between devices  58.1 us (40%)
  Pallas kernels  43.8 us (30%)
  starting transfers between devices  40.5 us (28%)
    ppermute x38, waiting for transfers between devices, flipped(): lax.ppermute(x, axis, [(i, i ^ 1 << bit) for i in range(lax.axis_size(axi...  53.5 us
    ppermute x38, starting transfers between devices, flipped(): lax.ppermute(x, axis, [(i, i ^ 1 << bit) for i in range(lax.axis_size(axi...  35.5 us
    pallas_call x1, Pallas kernels, gather_rows(): pl.pallas_call(functools.partial(gather_kernel, hub_steps, rel_steps), in...  9.82 us
    pallas_call x4, Pallas kernels, placed(): pl.pallas_call(kernel, in_specs=[SMEM] + [VMEM] * (1 + len(fars)) + [HBM]...  9.53 us
    pallas_call x2, Pallas kernels, chunk_columns(): pl.pallas_call(functools.partial(kernel, grad_lanes), in_specs=[SMEM] + [...  7.99 us
    pallas_call x1, Pallas kernels, bucket_step(): pl.pallas_call(functools.partial(bucket_kernel, bucket), in_specs=[SMEM]...  5.58 us
    ppermute x3, waiting for transfers between devices, flipped_by(): lax.ppermute(x, axis, [(i, i ^ offset) for i in range(lax.axis_size(axis))])  4.63 us
    ppermute x3, starting transfers between devices, flipped_by(): lax.ppermute(x, axis, [(i, i ^ offset) for i in range(lax.axis_size(axis))])  4.39 us
  transfers between devices with their start and end apart: 42, of which 25 were waited for; matrix products, arithmetic and copies ran while one was open for 0% of the time, Pallas kernels for 23%

profile of v13, /device:TPU:0, one launch (start us, length us, event | category | flops | bytes accessed | tf_op | source)
XLA Modules:
  0.0 145.1 jit_solution(386067990805372011)
XLA Ops:
  2.7 9.8 %shard_map.156 = (f32[400,256]{1,0:T(8,128)S(1)}, f32[400,256]{1,0:T(8,128)S(1)}, f32[400,512]{1,0:T(8,128)S(1)}, f32[400,512]{1,0:T(8,128)S(1)}, s32[2]{0:T(128...) custom-call(s32[2]{0:T(128)S(1)} %pad_add_fusion.spot_ref, s32[2,256]{1,0:T(2,128)S(1)} %copy-done.7, ...), custom_call_target="tpu_custom_call" | custom-call | flops 10000 | bytes 10000 | tf_op jit(solution)/shard_map/pallas_call | solution.py:136
  12.7 5.6 %shard_map.157 = (f32[400,512]{1,0:T(8,128)S(1)}, f32[1,512]{1,0:T(1,128)S(1)}, f32[408,512]{1,0:T(8,128)S(1)}, f32[200,768]{1,0:T(8,128)S(1)}, f32[200,768]{1,0:T(8,128)S(1)}) custom-call(s32[2]{0:T(128)S(1)} %get-tuple-element.114.core_ref.spot_ref, s32[2,512]{1,0:T(2,128)S(1)} %copy-done.2, s32[2,512]{1,0:T(2,128)S(1)} %copy-done.4, ...), custom_call_target="tpu_custom_call" | custom-call | flops 10000 | bytes 10000 | tf_op jit(solution)/shard_map/pallas_call | solution.py:564
  18.9 2.7 %shard_map.158 = (f32[400,512]{1,0:T(8,128)S(1)}, f32[200,256]{1,0:T(8,128)S(1)}, f32[200,256]{1,0:T(8,128)S(1)}) custom-call(s32[2]{0:T(128)S(1)} %get-tuple-element.114.core_ref.spot_ref, s32[2,512]{1,0:T(2,128)S(1)} %copy-done.2, f32[400,512]{1,0:T(8,128)S(1)} %get-tuple-element.206.left_ref, f32[400,512]{1,0:T(8,128)S(1)} %get-tuple-element.122.rel_ref, ...), custom_call_target="tpu_custom_call" | custom-call | flops 10000 | bytes 10000 | tf_op jit(solution)/shard_map/pallas_call | solution.py:605
  21.6 2.8 %collective-permute-start.2 = (f32[200,768]{1,0:T(8,128)S(1)}, f32[200,768]{1,0:T(8,128)S(1)}, u32[]{:S(2)}, u32[]{:S(2)}) collective-permute-start(f32[200,768]{1,0:T(8,128)S(1)} %get-tuple-element.127), channel_id=1, source_target_pairs={{0,4},{4,0},{8,12},{12,8},{16,20},{20,16},{24,28},{28,24},{1,5},{5... | collective-permute-start | bytes 1843208 | tf_op jit(solution)/shard_map/ppermute | solution.py:682
  24.5 1.9 %collective-permute-done.3.refs_5_ = f32[200,256]{1,0:T(8,128)S(1)} collective-permute-done((f32[200,256]{1,0:T(8,128)S(1)}, f32[200,256]{1,0:T(8,128)S(1)}, u32[]{:S(2)}, u32[]{:S(2)}) %collective-permute-start.3) | collective-permute-done | bytes 204832 | tf_op jit(solution)/shard_map/ppermute | solution.py:682
  26.4 4.3 %shard_map.159 = (f32[8,72,256]{2,1,0:T(8,128)S(1)}, f32[8,64,256]{2,1,0:T(8,128)S(1)}, f32[8,64,256]{2,1,0:T(8,128)S(1)}, f32[8,72,256]{2,1,0:T(8,128)S(1)}, f3...) custom-call(s32[2]{0:T(128)S(1)} %get-tuple-element.114.core_ref.spot_ref, s32[2,256]{1,0:T(2,128)S(1)} %copy-done.7, ...), custom_call_target="tpu_custom_call" | custom-call | flops 10000 | bytes 10000 | tf_op jit(solution)/shard_map/pallas_call | solution.py:281
  32.6 1.8 %collective-permute-start.8 = (f32[8,64,256]{2,1,0:T(8,128)S(1)}, f32[8,64,256]{2,1,0:T(8,128)S(1)}, u32[]{:S(2)}, u32[]{:S(2)}) collective-permute-start(f32[8,64,256]{2,1,0:T(8,128)S(1)} %get-tuple-element.141), channel_id=1, source_target_pairs={{0,1},{1,0},{2,3},{3,2},{4,5},{5,4},{6,7},{7,6},{8,9},{9,8},{10,11... | collective-permute-start | bytes 1572872 | tf_op jit(solution)/shard_map/ppermute | solution.py:682
  34.4 3.5 %shard_map.160 = (f32[200,512]{1,0:T(8,128)S(1)}, f32[200,512]{1,0:T(8,128)S(1)}, bf16[800,512]{1,0:T(8,128)(2,1)S(1)}, bf16[2,512,512]{2,1,0:T(8,128)(2,1)S(1)}, f32[400,512]{1,0:T(8,128)S(1)}) custom-call(s32[2]{0:T(128)S(1)} %get-tuple-element.114.core_ref.spot_ref, s32[2,512]{1,0:T(2,128)S(1)} %copy-done.2, s32[2,512]{1,0:T(2,128)S(1)} %copy-done.4, ...), custom_call_target="tpu_custom_call" | custom-call | flops 10000 | bytes 10000 | tf_op jit(solution)/shard_map/pallas_call | solution.py:648
  38.0 1.7 %collective-permute-done.5.refs_5_ = f32[200,512]{1,0:T(8,128)S(1)} collective-permute-done((f32[200,512]{1,0:T(8,128)S(1)}, f32[200,512]{1,0:T(8,128)S(1)}, u32[]{:S(2)}, u32[]{:S(2)}) %collective-permute-start.5) | collective-permute-done | bytes 409632 | tf_op jit(solution)/shard_map/ppermute | solution.py:682
  39.7 3.7 %shard_map.161 = (f32[8,32,256]{2,1,0:T(8,128)S(1)}, f32[8,32,256]{2,1,0:T(8,128)S(1)}, f32[8,32,256]{2,1,0:T(8,128)S(1)}, f32[8,32,256]{2,1,0:T(8,128)S(1)}) custom-call(s32[2]{0:T(128)S(1)} %get-tuple-element.114.core_ref.spot_ref, s32[2,512]{1,0:T(2,128)S(1)} %copy-done.5, s32[2,512]{1,0:T(2,128)S(1)} %collective-permute-done.1.refs_1_, ...), custom_call_target="tpu_custom_call" | custom-call | flops 10000 | bytes 10000 | tf_op jit(solution)/shard_map/pallas_call | solution.py:281
  43.3 2.7 %collective-permute-done.7.refs_4_ = f32[8,64,256]{2,1,0:T(8,128)S(1)} collective-permute-done((f32[8,64,256]{2,1,0:T(8,128)S(1)}, f32[8,64,256]{2,1,0:T(8,128)S(1)}, u32[]{:S(2)}, u32[]{:S(2)}) %collective-permute-start.7) | collective-permute-done | bytes 524320 | tf_op jit(solution)/shard_map/ppermute | solution.py:682
  46.6 1.6 %collective-permute-start.11 = (f32[4,72,256]{2,1,0:T(8,128)S(1)}, f32[4,72,256]{2,1,0:T(8,128)S(1)}, u32[]{:S(2)}, u32[]{:S(2)}) collective-permute-start(f32[4,72,256]{2,1,0:T(8,128)S(1)} %get-tuple-element.159), channel_id=1, source_target_pairs={{0,16},{4,20},{8,24},{12,28},{16,0},{20,4},{24,8},{28,12},{1,17},{... | collective-permute-start | bytes 884744 | tf_op jit(solution)/shard_map/ppermute | solution.py:682
  48.7 1.6 %collective-permute-start.9 = (f32[8,32,256]{2,1,0:T(8,128)S(1)}, f32[8,32,256]{2,1,0:T(8,128)S(1)}, u32[]{:S(2)}, u32[]{:S(2)}) collective-permute-start(f32[8,32,256]{2,1,0:T(8,128)S(1)} %get-tuple-element.148), channel_id=1, source_target_pairs={{0,8},{4,12},{8,0},{12,4},{16,24},{20,28},{24,16},{28,20},{1,9},{5... | collective-permute-start | bytes 786440 | tf_op jit(solution)/shard_map/ppermute | solution.py:682
  50.2 1.6 %collective-permute-start.12 = (f32[4,64,256]{2,1,0:T(8,128)S(1)}, f32[4,64,256]{2,1,0:T(8,128)S(1)}, u32[]{:S(2)}, u32[]{:S(2)}) collective-permute-start(f32[4,64,256]{2,1,0:T(8,128)S(1)} %get-tuple-element.160), channel_id=1, source_target_pairs={{0,1},{1,0},{2,3},{3,2},{4,5},{5,4},{6,7},{7,6},{8,9},{9,8},{10,11... | collective-permute-start | bytes 786440 | tf_op jit(solution)/shard_map/ppermute | solution.py:682
  52.3 8.4 %collective-permute-done.10.refs_3_ = f32[8,32,256]{2,1,0:T(8,128)S(1)} collective-permute-done((f32[8,32,256]{2,1,0:T(8,128)S(1)}, f32[8,32,256]{2,1,0:T(8,128)S(1)}, u32[]{:S(2)}, u32[]{:S(2)}) %collective-permute-start.10) | collective-permute-done | bytes 262176 | tf_op jit(solution)/shard_map/ppermute | solution.py:682
  61.6 1.6 %collective-permute-start.14 = (f32[2,72,256]{2,1,0:T(8,128)S(1)}, f32[2,72,256]{2,1,0:T(8,128)S(1)}, u32[]{:S(2)}, u32[]{:S(2)}) collective-permute-start(f32[2,72,256]{2,1,0:T(8,128)S(1)} %get-tuple-element.168), channel_id=1, source_target_pairs={{0,1},{1,0},{2,3},{3,2},{4,5},{5,4},{6,7},{7,6},{8,9},{9,8},{10,11... | collective-permute-start | bytes 442376 | tf_op jit(solution)/shard_map/ppermute | solution.py:682
  66.7 2.6 %collective-permute-start.16 = (f32[2,64,256]{2,1,0:T(8,128)S(1)}, f32[2,64,256]{2,1,0:T(8,128)S(1)}, u32[]{:S(2)}, u32[]{:S(2)}) collective-permute-start(f32[2,64,256]{2,1,0:T(8,128)S(1)} %get-tuple-element.170), channel_id=1, source_target_pairs={{0,2},{1,3},{2,0},{3,1},{4,6},{5,7},{6,4},{7,5},{8,10},{9,11},{10,... | collective-permute-start | bytes 393224 | tf_op jit(solution)/shard_map/ppermute | solution.py:682
  71.1 4.8 %collective-permute-done.16.refs_5_ = f32[2,64,256]{2,1,0:T(8,128)S(1)} collective-permute-done((f32[2,64,256]{2,1,0:T(8,128)S(1)}, f32[2,64,256]{2,1,0:T(8,128)S(1)}, u32[]{:S(2)}, u32[]{:S(2)}) %collective-permute-start.16) | collective-permute-done | bytes 131104 | tf_op jit(solution)/shard_map/ppermute | solution.py:682
  77.6 2.0 %collective-permute-start.21 = (f32[1,64,256]{2,1,0:T(8,128)S(1)}, f32[1,64,256]{2,1,0:T(8,128)S(1)}, u32[]{:S(2)}, u32[]{:S(2)}) collective-permute-start(f32[1,64,256]{2,1,0:T(8,128)S(1)} %get-tuple-element.181), channel_id=1, source_target_pairs={{0,1},{1,0},{2,3},{3,2},{4,5},{5,4},{6,7},{7,6},{8,9},{9,8},{10,11... | collective-permute-start | bytes 196616 | tf_op jit(solution)/shard_map/ppermute | solution.py:686
  80.4 1.5 %collective-permute-start.23 = (f32[1,64,256]{2,1,0:T(8,128)S(1)}, f32[1,64,256]{2,1,0:T(8,128)S(1)}, u32[]{:S(2)}, u32[]{:S(2)}) collective-permute-start(f32[1,64,256]{2,1,0:T(8,128)S(1)} %get-tuple-element.183), channel_id=1, source_target_pairs={{0,3},{1,2},{2,1},{3,0},{4,7},{5,6},{6,5},{7,4},{8,11},{9,10},{10,... | collective-permute-start | bytes 196616 | tf_op jit(solution)/shard_map/ppermute | solution.py:686
  83.3 2.1 %collective-permute-done.22.refs_7_ = f32[1,64,256]{2,1,0:T(8,128)S(1)} collective-permute-done((f32[1,64,256]{2,1,0:T(8,128)S(1)}, f32[1,64,256]{2,1,0:T(8,128)S(1)}, u32[]{:S(2)}, u32[]{:S(2)}) %collective-permute-start.22) | collective-permute-done | bytes 65568 | tf_op jit(solution)/shard_map/ppermute | solution.py:686
  93.4 11.1 %collective-permute-done.25.refs_0_.refs_1_.refs_2_ = f32[1,264,256]{2,1,0:T(8,128)S(1)} collective-permute-done((f32[1,264,256]{2,1,0:T(8,128)S(1)}, f32[1,264,256]{2,1,0:T(8,128)S(1)}, u32[]{:S(2)}, u32[]{:S(2)}) %collective-permute-start.25) | collective-permute-done | bytes 270368 | tf_op jit(solution)/shard_map/ppermute | solution.py:682
  106.5 2.6 %collective-permute-done.29.refs_6_ = f32[1,88,256]{2,1,0:T(8,128)S(1)} collective-permute-done((f32[1,88,256]{2,1,0:T(8,128)S(1)}, f32[1,88,256]{2,1,0:T(8,128)S(1)}, u32[]{:S(2)}, u32[]{:S(2)}) %collective-permute-start.29) | collective-permute-done | bytes 90144 | tf_op jit(solution)/shard_map/ppermute | solution.py:682
  111.2 1.9 %collective-permute-start.33 = (f32[3,88,256]{2,1,0:T(8,128)S(1)}, f32[3,88,256]{2,1,0:T(8,128)S(1)}, u32[]{:S(2)}, u32[]{:S(2)}) collective-permute-start(f32[3,88,256]{2,1,0:T(8,128)S(1)} %get-tuple-element.195.refs_1_), channel_id=1, source_target_pairs={{0,1},{1,0},{2,3},{3,2},{4,5},{5,4},{6,7},{7,6},{8,9},{9,8},{10,11... | collective-permute-start | bytes 811016 | tf_op jit(solution)/shard_map/ppermute | solution.py:682
  114.0 3.0 %collective-permute-done.32.refs_6_ = f32[3,88,256]{2,1,0:T(8,128)S(1)} collective-permute-done((f32[3,88,256]{2,1,0:T(8,128)S(1)}, f32[3,88,256]{2,1,0:T(8,128)S(1)}, u32[]{:S(2)}, u32[]{:S(2)}) %collective-permute-start.32) | collective-permute-done | bytes 270368 | tf_op jit(solution)/shard_map/ppermute | solution.py:682
  117.9 1.7 %collective-permute-done.34.refs_8_ = f32[3,88,256]{2,1,0:T(8,128)S(1)} collective-permute-done((f32[3,88,256]{2,1,0:T(8,128)S(1)}, f32[3,88,256]{2,1,0:T(8,128)S(1)}, u32[]{:S(2)}, u32[]{:S(2)}) %collective-permute-start.34) | collective-permute-done | bytes 270368 | tf_op jit(solution)/shard_map/ppermute | solution.py:682
  122.4 2.0 %shard_map.172.refs_0_ = f32[2,200,4096]{2,1,0:T(8,128)} custom-call(s32[2]{0:T(128)S(1)} %get-tuple-element.114.core_ref.spot_ref, f32[9,264,256]{2,1,0:T(8,128)S(1)} %shard_map.171.near_ref), custom_call_target="tpu_custom_call" | custom-call | bytes 3276800 | tf_op jit(solution)/shard_map/pallas_call | solution.py:475
  124.4 2.4 %shard_map.174 = (f32[400,512]{1,0:T(8,128)}, f32[400,512]{1,0:T(8,128)}) custom-call(s32[2,512]{1,0:T(2,128)S(1)} %copy-done.2, f32[400,512]{1,0:T(8,128)S(1)} %get-tuple-element.206.left_ref, f32[1,512]{1,0:T(1,128)S(1)} %get-tuple-element.207.left_sums_ref, f32[408,512]{1,0:T(8,128)S(1)} %collective-permute-done.4.right_ref, ...), custom_call_target="tpu_custom_call" | custom-call | flops 3000000000 | bytes 10000000 | tf_op jit(solution)/shard_map/pallas_call | solution.py:296
  126.8 2.0 %shard_map.173.refs_3_ = f32[2,200,4096]{2,1,0:T(8,128)} custom-call(s32[2]{0:T(128)S(1)} %get-tuple-element.114.core_ref.spot_ref, f32[9,264,256]{2,1,0:T(8,128)S(1)} %collective-permute-done.38.near_ref, f32[2,200,4096]{2,1,0:T(8,128)} %shard_map.172.refs_0_), custom_call_target="tpu_custom_call", output_to_operand_aliasing={{}: (2, {})} | custom-call | bytes 3276800 | tf_op jit(solution)/shard_map/pallas_call | solution.py:475
  128.8 7.7 %collective-permute-done.35.refs_0_ = f32[7,88,256]{2,1,0:T(8,128)S(1)} collective-permute-done((f32[7,88,256]{2,1,0:T(8,128)S(1)}, f32[7,88,256]{2,1,0:T(8,128)S(1)}, u32[]{:S(2)}, u32[]{:S(2)}) %collective-permute-start.35) | collective-permute-done | bytes 630816 | tf_op jit(solution)/shard_map/ppermute | solution.py:682
  138.8 2.8 %shard_map.175 = (f32[2,200,4096]{2,1,0:T(8,128)}, f32[2,200,1280]{2,1,0:T(8,128)}) custom-call(s32[2]{0:T(128)S(1)} %get-tuple-element.114.core_ref.spot_ref, f32[9,264,256]{2,1,0:T(8,128)S(1)} %shard_map.171.near_ref, f32[7,88,256]{2,1,0:T(8,128)S(1)} %collective-permute-done.35.refs_0_, ...), custom_call_target="tpu_custom_call", output_to_operand_aliasing={{0}: (5, {})} | custom-call | bytes 3276800 | tf_op jit(solution)/shard_map/pallas_call | solution.py:475
  142.1 2.8 %shard_map.176 = (f32[2,200,4096]{2,1,0:T(8,128)}, f32[2,200,1280]{2,1,0:T(8,128)}) custom-call(s32[2]{0:T(128)S(1)} %get-tuple-element.114.core_ref.spot_ref, f32[9,264,256]{2,1,0:T(8,128)S(1)} %collective-permute-done.38.near_ref, f32[7,88,256]{2,1,0:T(8,128)S(1)} %collective-permute-done.39.refs_0_, ...), custom_call_target="tpu_custom_call", output_to_operand_aliasing={{0}: (5, {}), {1}: (6, {})} | custom-call | bytes 3276800 | tf_op jit(solution)/shard_map/pallas_call | solution.py:475
  (97 shorter events, 35.6 us)
Async XLA Ops:
  0.7 11.9 %collective-permute-start.1 = (s32[2,512]{1,0:T(2,128)}, s32[2,512]{1,0:T(2,128)S(1)}, u32[]{:S(2)}, u32[]{:S(2)}) collective-permute-start(s32[2,512]{1,0:T(2,128)} %refs_0_.3), channel_id=1, source_target_pairs={{0,4},{4,0},{8,12},{12,8},{16,20},{20,16},{24,28},{28,24},{1,5},{5... | collective-permute-start | bytes 12296 | tf_op jit(solution)/shard_map/ppermute | solution.py:682
  1.2 11.4 %collective-permute-start = (s32[2,256]{1,0:T(2,128)}, s32[2,256]{1,0:T(2,128)S(1)}, u32[]{:S(2)}, u32[]{:S(2)}) collective-permute-start(s32[2,256]{1,0:T(2,128)} %refs_0_.2), channel_id=1, source_target_pairs={{0,4},{4,0},{8,12},{12,8},{16,20},{20,16},{24,28},{28,24},{1,5},{5... | collective-permute-start | bytes 6152 | tf_op jit(solution)/shard_map/ppermute | solution.py:682
  18.2 16.2 %collective-permute-start.4 = (f32[408,512]{1,0:T(8,128)S(1)}, f32[408,512]{1,0:T(8,128)S(1)}, u32[]{:S(2)}, u32[]{:S(2)}) collective-permute-start(f32[408,512]{1,0:T(8,128)S(1)} %get-tuple-element.134), channel_id=1, source_target_pairs={{0,4},{4,8},{8,12},{12,16},{16,20},{20,24},{24,28},{28,0},{1,5},{5... | collective-permute-start | bytes 2506760 | tf_op jit(solution)/shard_map/ppermute | solution.py:678
  30.7 15.7 %collective-permute-start.6 = (f32[8,72,256]{2,1,0:T(8,128)S(1)}, f32[8,72,256]{2,1,0:T(8,128)S(1)}, u32[]{:S(2)}, u32[]{:S(2)}) collective-permute-start(f32[8,72,256]{2,1,0:T(8,128)S(1)} %get-tuple-element.139), channel_id=1, source_target_pairs={{0,8},{4,12},{8,0},{12,4},{16,24},{20,28},{24,16},{28,20},{1,9},{5... | collective-permute-start | bytes 1769480 | tf_op jit(solution)/shard_map/ppermute | solution.py:682
  32.2 13.9 %collective-permute-start.7 = (f32[8,64,256]{2,1,0:T(8,128)S(1)}, f32[8,64,256]{2,1,0:T(8,128)S(1)}, u32[]{:S(2)}, u32[]{:S(2)}) collective-permute-start(f32[8,64,256]{2,1,0:T(8,128)S(1)} %get-tuple-element.140), channel_id=1, source_target_pairs={{0,16},{4,20},{8,24},{12,28},{16,0},{20,4},{24,8},{28,12},{1,17},{... | collective-permute-start | bytes 1572872 | tf_op jit(solution)/shard_map/ppermute | solution.py:682
  32.6 13.7 %collective-permute-start.8 = (f32[8,64,256]{2,1,0:T(8,128)S(1)}, f32[8,64,256]{2,1,0:T(8,128)S(1)}, u32[]{:S(2)}, u32[]{:S(2)}) collective-permute-start(f32[8,64,256]{2,1,0:T(8,128)S(1)} %get-tuple-element.141), channel_id=1, source_target_pairs={{0,1},{1,0},{2,3},{3,2},{4,5},{5,4},{6,7},{7,6},{8,9},{9,8},{10,11... | collective-permute-start | bytes 1572872 | tf_op jit(solution)/shard_map/ppermute | solution.py:682
  46.6 14.9 %collective-permute-start.11 = (f32[4,72,256]{2,1,0:T(8,128)S(1)}, f32[4,72,256]{2,1,0:T(8,128)S(1)}, u32[]{:S(2)}, u32[]{:S(2)}) collective-permute-start(f32[4,72,256]{2,1,0:T(8,128)S(1)} %get-tuple-element.159), channel_id=1, source_target_pairs={{0,16},{4,20},{8,24},{12,28},{16,0},{20,4},{24,8},{28,12},{1,17},{... | collective-permute-start | bytes 884744 | tf_op jit(solution)/shard_map/ppermute | solution.py:682
  48.1 12.6 %collective-permute-start.10 = (f32[8,32,256]{2,1,0:T(8,128)S(1)}, f32[8,32,256]{2,1,0:T(8,128)S(1)}, u32[]{:S(2)}, u32[]{:S(2)}) collective-permute-start(f32[8,32,256]{2,1,0:T(8,128)S(1)} %get-tuple-element.149), channel_id=1, source_target_pairs={{0,16},{4,20},{8,24},{12,28},{16,0},{20,4},{24,8},{28,12},{1,17},{... | collective-permute-start | bytes 786440 | tf_op jit(solution)/shard_map/ppermute | solution.py:682
  48.7 12.1 %collective-permute-start.9 = (f32[8,32,256]{2,1,0:T(8,128)S(1)}, f32[8,32,256]{2,1,0:T(8,128)S(1)}, u32[]{:S(2)}, u32[]{:S(2)}) collective-permute-start(f32[8,32,256]{2,1,0:T(8,128)S(1)} %get-tuple-element.148), channel_id=1, source_target_pairs={{0,8},{4,12},{8,0},{12,4},{16,24},{20,28},{24,16},{28,20},{1,9},{5... | collective-permute-start | bytes 786440 | tf_op jit(solution)/shard_map/ppermute | solution.py:682
  50.2 10.6 %collective-permute-start.12 = (f32[4,64,256]{2,1,0:T(8,128)S(1)}, f32[4,64,256]{2,1,0:T(8,128)S(1)}, u32[]{:S(2)}, u32[]{:S(2)}) collective-permute-start(f32[4,64,256]{2,1,0:T(8,128)S(1)} %get-tuple-element.160), channel_id=1, source_target_pairs={{0,1},{1,0},{2,3},{3,2},{4,5},{5,4},{6,7},{7,6},{8,9},{9,8},{10,11... | collective-permute-start | bytes 786440 | tf_op jit(solution)/shard_map/ppermute | solution.py:682
  51.8 9.7 %collective-permute-start.13 = (f32[4,64,256]{2,1,0:T(8,128)S(1)}, f32[4,64,256]{2,1,0:T(8,128)S(1)}, u32[]{:S(2)}, u32[]{:S(2)}) collective-permute-start(f32[4,64,256]{2,1,0:T(8,128)S(1)} %get-tuple-element.161), channel_id=1, source_target_pairs={{0,8},{4,12},{8,0},{12,4},{16,24},{20,28},{24,16},{28,20},{1,9},{5... | collective-permute-start | bytes 786440 | tf_op jit(solution)/shard_map/ppermute | solution.py:682
  61.6 14.3 %collective-permute-start.14 = (f32[2,72,256]{2,1,0:T(8,128)S(1)}, f32[2,72,256]{2,1,0:T(8,128)S(1)}, u32[]{:S(2)}, u32[]{:S(2)}) collective-permute-start(f32[2,72,256]{2,1,0:T(8,128)S(1)} %get-tuple-element.168), channel_id=1, source_target_pairs={{0,1},{1,0},{2,3},{3,2},{4,5},{5,4},{6,7},{7,6},{8,9},{9,8},{10,11... | collective-permute-start | bytes 442376 | tf_op jit(solution)/shard_map/ppermute | solution.py:682
  63.2 6.2 %collective-permute-start.17 = (f32[4,32,256]{2,1,0:T(8,128)S(1)}, f32[4,32,256]{2,1,0:T(8,128)S(1)}, u32[]{:S(2)}, u32[]{:S(2)}) collective-permute-start(f32[4,32,256]{2,1,0:T(8,128)S(1)} %get-tuple-element.173), channel_id=1, source_target_pairs={{0,16},{4,20},{8,24},{12,28},{16,0},{20,4},{24,8},{28,12},{1,17},{... | collective-permute-start | bytes 393224 | tf_op jit(solution)/shard_map/ppermute | solution.py:682
  64.7 5.0 %collective-permute-start.18 = (f32[4,32,256]{2,1,0:T(8,128)S(1)}, f32[4,32,256]{2,1,0:T(8,128)S(1)}, u32[]{:S(2)}, u32[]{:S(2)}) collective-permute-start(f32[4,32,256]{2,1,0:T(8,128)S(1)} %get-tuple-element.174), channel_id=1, source_target_pairs={{0,8},{4,12},{8,0},{12,4},{16,24},{20,28},{24,16},{28,20},{1,9},{5... | collective-permute-start | bytes 393224 | tf_op jit(solution)/shard_map/ppermute | solution.py:682
  65.3 5.8 %collective-permute-start.15 = (f32[2,64,256]{2,1,0:T(8,128)S(1)}, f32[2,64,256]{2,1,0:T(8,128)S(1)}, u32[]{:S(2)}, u32[]{:S(2)}) collective-permute-start(f32[2,64,256]{2,1,0:T(8,128)S(1)} %get-tuple-element.169), channel_id=1, source_target_pairs={{0,8},{4,12},{8,0},{12,4},{16,24},{20,28},{24,16},{28,20},{1,9},{5... | collective-permute-start | bytes 393224 | tf_op jit(solution)/shard_map/ppermute | solution.py:682
  66.7 9.2 %collective-permute-start.16 = (f32[2,64,256]{2,1,0:T(8,128)S(1)}, f32[2,64,256]{2,1,0:T(8,128)S(1)}, u32[]{:S(2)}, u32[]{:S(2)}) collective-permute-start(f32[2,64,256]{2,1,0:T(8,128)S(1)} %get-tuple-element.170), channel_id=1, source_target_pairs={{0,2},{1,3},{2,0},{3,1},{4,6},{5,7},{6,4},{7,5},{8,10},{9,11},{10,... | collective-permute-start | bytes 393224 | tf_op jit(solution)/shard_map/ppermute | solution.py:682
  76.0 10.6 %collective-permute-start.19 = (f32[1,136,256]{2,1,0:T(8,128)S(1)}, f32[1,136,256]{2,1,0:T(8,128)S(1)}, u32[]{:S(2)}, u32[]{:S(2)}) collective-permute-start(f32[1,136,256]{2,1,0:T(8,128)S(1)} %get-tuple-element.178), channel_id=1, source_target_pairs={{0,2},{1,3},{2,0},{3,1},{4,6},{5,7},{6,4},{7,5},{8,10},{9,11},{10,... | collective-permute-start | bytes 417800 | tf_op jit(solution)/shard_map/ppermute | solution.py:682
  76.1 5.9 %collective-permute-start.20 = (f32[1,64,256]{2,1,0:T(8,128)S(1)}, f32[1,64,256]{2,1,0:T(8,128)S(1)}, u32[]{:S(2)}, u32[]{:S(2)}) collective-permute-start(f32[1,64,256]{2,1,0:T(8,128)S(1)} %get-tuple-element.179), channel_id=1, source_target_pairs={{0,16},{4,20},{8,24},{12,28},{16,0},{20,4},{24,8},{28,12},{1,17},{... | collective-permute-start | bytes 196616 | tf_op jit(solution)/shard_map/ppermute | solution.py:682
  77.6 5.7 %collective-permute-start.21 = (f32[1,64,256]{2,1,0:T(8,128)S(1)}, f32[1,64,256]{2,1,0:T(8,128)S(1)}, u32[]{:S(2)}, u32[]{:S(2)}) collective-permute-start(f32[1,64,256]{2,1,0:T(8,128)S(1)} %get-tuple-element.181), channel_id=1, source_target_pairs={{0,1},{1,0},{2,3},{3,2},{4,5},{5,4},{6,7},{7,6},{8,9},{9,8},{10,11... | collective-permute-start | bytes 196616 | tf_op jit(solution)/shard_map/ppermute | solution.py:686
  79.5 5.9 %collective-permute-start.22 = (f32[1,64,256]{2,1,0:T(8,128)S(1)}, f32[1,64,256]{2,1,0:T(8,128)S(1)}, u32[]{:S(2)}, u32[]{:S(2)}) collective-permute-start(f32[1,64,256]{2,1,0:T(8,128)S(1)} %get-tuple-element.182), channel_id=1, source_target_pairs={{0,2},{1,3},{2,0},{3,1},{4,6},{5,7},{6,4},{7,5},{8,10},{9,11},{10,... | collective-permute-start | bytes 196616 | tf_op jit(solution)/shard_map/ppermute | solution.py:686
  80.4 6.2 %collective-permute-start.23 = (f32[1,64,256]{2,1,0:T(8,128)S(1)}, f32[1,64,256]{2,1,0:T(8,128)S(1)}, u32[]{:S(2)}, u32[]{:S(2)}) collective-permute-start(f32[1,64,256]{2,1,0:T(8,128)S(1)} %get-tuple-element.183), channel_id=1, source_target_pairs={{0,3},{1,2},{2,1},{3,0},{4,7},{5,6},{6,5},{7,4},{8,11},{9,10},{10,... | collective-permute-start | bytes 196616 | tf_op jit(solution)/shard_map/ppermute | solution.py:686
  89.2 15.3 %collective-permute-start.25 = (f32[1,264,256]{2,1,0:T(8,128)S(1)}, f32[1,264,256]{2,1,0:T(8,128)S(1)}, u32[]{:S(2)}, u32[]{:S(2)}) collective-permute-start(f32[1,264,256]{2,1,0:T(8,128)S(1)} %shard_map.167.refs_0_), channel_id=1, source_target_pairs={{0,2},{1,3},{2,0},{3,1},{4,6},{5,7},{6,4},{7,5},{8,10},{9,11},{10,... | collective-permute-start | bytes 811016 | tf_op jit(solution)/shard_map/ppermute | solution.py:682
  90.4 15.0 %collective-permute-start.26 = (f32[1,264,256]{2,1,0:T(8,128)S(1)}, f32[1,264,256]{2,1,0:T(8,128)S(1)}, u32[]{:S(2)}, u32[]{:S(2)}) collective-permute-start(f32[1,264,256]{2,1,0:T(8,128)S(1)} %shard_map.167.refs_0_), channel_id=1, source_target_pairs={{0,1},{1,0},{2,3},{3,2},{4,5},{5,4},{6,7},{7,6},{8,9},{9,8},{10,11... | collective-permute-start | bytes 811016 | tf_op jit(solution)/shard_map/ppermute | solution.py:682
  91.4 15.1 %collective-permute-start.27 = (f32[1,264,256]{2,1,0:T(8,128)S(1)}, f32[1,264,256]{2,1,0:T(8,128)S(1)}, u32[]{:S(2)}, u32[]{:S(2)}) collective-permute-start(f32[1,264,256]{2,1,0:T(8,128)S(1)} %shard_map.167.refs_0_), channel_id=1, source_target_pairs={{0,8},{4,12},{8,0},{12,4},{16,24},{20,28},{24,16},{28,20},{1,9},{5... | collective-permute-start | bytes 811016 | tf_op jit(solution)/shard_map/ppermute | solution.py:682
  92.7 13.9 %collective-permute-start.28 = (f32[1,264,256]{2,1,0:T(8,128)S(1)}, f32[1,264,256]{2,1,0:T(8,128)S(1)}, u32[]{:S(2)}, u32[]{:S(2)}) collective-permute-start(f32[1,264,256]{2,1,0:T(8,128)S(1)} %shard_map.167.refs_0_), channel_id=1, source_target_pairs={{0,16},{4,20},{8,24},{12,28},{16,0},{20,4},{24,8},{28,12},{1,17},{... | collective-permute-start | bytes 811016 | tf_op jit(solution)/shard_map/ppermute | solution.py:682
  110.0 7.0 %collective-permute-start.32 = (f32[3,88,256]{2,1,0:T(8,128)S(1)}, f32[3,88,256]{2,1,0:T(8,128)S(1)}, u32[]{:S(2)}, u32[]{:S(2)}) collective-permute-start(f32[3,88,256]{2,1,0:T(8,128)S(1)} %get-tuple-element.194.refs_0_), channel_id=1, source_target_pairs={{0,16},{4,20},{8,24},{12,28},{16,0},{20,4},{24,8},{28,12},{1,17},{... | collective-permute-start | bytes 811016 | tf_op jit(solution)/shard_map/ppermute | solution.py:682
  111.2 6.7 %collective-permute-start.33 = (f32[3,88,256]{2,1,0:T(8,128)S(1)}, f32[3,88,256]{2,1,0:T(8,128)S(1)}, u32[]{:S(2)}, u32[]{:S(2)}) collective-permute-start(f32[3,88,256]{2,1,0:T(8,128)S(1)} %get-tuple-element.195.refs_1_), channel_id=1, source_target_pairs={{0,1},{1,0},{2,3},{3,2},{4,5},{5,4},{6,7},{7,6},{8,9},{9,8},{10,11... | collective-permute-start | bytes 811016 | tf_op jit(solution)/shard_map/ppermute | solution.py:682
  113.1 6.5 %collective-permute-start.34 = (f32[3,88,256]{2,1,0:T(8,128)S(1)}, f32[3,88,256]{2,1,0:T(8,128)S(1)}, u32[]{:S(2)}, u32[]{:S(2)}) collective-permute-start(f32[3,88,256]{2,1,0:T(8,128)S(1)} %get-tuple-element.196.refs_2_), channel_id=1, source_target_pairs={{0,8},{4,12},{8,0},{12,4},{16,24},{20,28},{24,16},{28,20},{1,9},{5... | collective-permute-start | bytes 811016 | tf_op jit(solution)/shard_map/ppermute | solution.py:682
  119.9 7.0 %collective-permute-start.38 = (f32[9,264,256]{2,1,0:T(8,128)S(1)}, f32[9,264,256]{2,1,0:T(8,128)S(1)}, u32[]{:S(2)}, u32[]{:S(2)}) collective-permute-start(f32[9,264,256]{2,1,0:T(8,128)S(1)} %shard_map.171.near_ref), channel_id=1, source_target_pairs={{0,4},{4,0},{8,12},{12,8},{16,20},{20,16},{24,28},{28,24},{1,5},{5... | collective-permute-start | bytes 7299080 | tf_op jit(solution)/shard_map/ppermute | solution.py:682
  120.0 16.6 %collective-permute-start.35 = (f32[7,88,256]{2,1,0:T(8,128)S(1)}, f32[7,88,256]{2,1,0:T(8,128)S(1)}, u32[]{:S(2)}, u32[]{:S(2)}) collective-permute-start(f32[7,88,256]{2,1,0:T(8,128)S(1)} %get-tuple-element.197.refs_1_), channel_id=1, source_target_pairs={{0,8},{4,12},{8,0},{12,4},{16,24},{20,28},{24,16},{28,20},{1,9},{5... | collective-permute-start | bytes 1892360 | tf_op jit(solution)/shard_map/ppermute | solution.py:682
  120.9 16.3 %collective-permute-start.36 = (f32[7,88,256]{2,1,0:T(8,128)S(1)}, f32[7,88,256]{2,1,0:T(8,128)S(1)}, u32[]{:S(2)}, u32[]{:S(2)}) collective-permute-start(f32[7,88,256]{2,1,0:T(8,128)S(1)} %get-tuple-element.198.refs_2_), channel_id=1, source_target_pairs={{0,16},{4,20},{8,24},{12,28},{16,0},{20,4},{24,8},{28,12},{1,17},{... | collective-permute-start | bytes 1892360 | tf_op jit(solution)/shard_map/ppermute | solution.py:682
  122.3 16.0 %collective-permute-start.37 = (f32[7,88,256]{2,1,0:T(8,128)S(1)}, f32[7,88,256]{2,1,0:T(8,128)S(1)}, u32[]{:S(2)}, u32[]{:S(2)}) collective-permute-start(f32[7,88,256]{2,1,0:T(8,128)S(1)} %get-tuple-element.199.refs_3_), channel_id=1, source_target_pairs={{0,1},{1,0},{2,3},{3,2},{4,5},{5,4},{6,7},{7,6},{8,9},{9,8},{10,11... | collective-permute-start | bytes 1892360 | tf_op jit(solution)/shard_map/ppermute | solution.py:682
  (21 other events, 220.3 us)

commit v14 on v12

--- a/solution.py
+++ b/solution.py
@@ -667,12 +667,18 @@
     return lax.ppermute(x, axis, [(i, (i + by) % size) for i in range(size)])
 
 
+def line_label(i):
+    return i ^ (i >> 1)
+
+
+def flipped_by(x, axis, offset):
+    size = lax.axis_size(axis)
+    labels = [line_label(i) if axis == "sub" else i for i in range(size)]
+    return lax.ppermute(x, axis, [(i, labels.index(labels[i] ^ offset)) for i in range(size)])
+
+
 def flipped(x, axis, bit):
-    return lax.ppermute(x, axis, [(i, i ^ (1 << bit)) for i in range(lax.axis_size(axis))])
-
-
-def flipped_by(x, axis, offset):
-    return lax.ppermute(x, axis, [(i, i ^ offset) for i in range(lax.axis_size(axis))])
+    return flipped_by(x, axis, 1 << bit)
 
 
 def other_core(x):
@@ -745,7 +751,7 @@
         return lax.optimization_barrier((first, then))
 
     blk = lax.axis_index("blk")
-    spot = jnp.stack([(blk >> 1) * depth + lax.axis_index("sub"), blk & 1]).astype(jnp.int32)
+    spot = jnp.stack([(blk >> 1) * depth + line_label(lax.axis_index("sub")), blk & 1]).astype(jnp.int32)
     far_ids = other_core((hub_ids, relations))
     hub_rows, rel_rows, spot, owned = gather_rows(
         spot, hub_emb.reshape(features, hub_count), hub_ids, relation_emb.reshape(features, rel_count), relations, chunks

time: 145 us -> 142 us (0.979)
  waiting for transfers between devices: 55.1 us -> 51.5 us
  starting transfers between devices: 43.1 us -> 44.6 us
    ppermute x41, waiting for transfers between devices: 55.1 us -> 51.5 us  [flipped_by(): lax.ppermute(x, axis, [(i, labels.index(labels[i] ^ offset)) for i in ran...]
    ppermute x41, starting transfers between devices: 42.5 us -> 44 us  [flipped_by(): lax.ppermute(x, axis, [(i, labels.index(labels[i] ^ offset)) for i in ran...]
  transfers between devices with their start and end apart: 42 -> 42, of which waited for: 27 -> 24; matrix products, arithmetic and copies ran while one was open for 0% -> 0% of each run, Pallas kernels for 23% -> 23%
where the time goes in v14:
time: 142 us
  waiting for transfers between devices  51.5 us (36%)
  starting transfers between devices  44.6 us (31%)
  Pallas kernels  43.5 us (31%)
    ppermute x41, waiting for transfers between devices, flipped_by(): lax.ppermute(x, axis, [(i, labels.index(labels[i] ^ offset)) for i in ran...  51.5 us
    ppermute x41, starting transfers between devices, flipped_by(): lax.ppermute(x, axis, [(i, labels.index(labels[i] ^ offset)) for i in ran...  44 us
    pallas_call x1, Pallas kernels, gather_rows(): pl.pallas_call(functools.partial(gather_kernel, hub_steps, rel_steps), in...  10 us
    pallas_call x4, Pallas kernels, placed(): pl.pallas_call(kernel, in_specs=[SMEM] + [VMEM] * (1 + len(fars)) + [HBM]...  9.53 us
    pallas_call x2, Pallas kernels, chunk_columns(): pl.pallas_call(functools.partial(kernel, grad_lanes), in_specs=[SMEM] + [...  8 us
    pallas_call x1, Pallas kernels, bucket_step(): pl.pallas_call(functools.partial(bucket_kernel, bucket), in_specs=[SMEM]...  5.58 us
    pallas_call x1, Pallas kernels, tables_step(): pl.pallas_call(functools.partial(tables_kernel, bucket, hubs), in_specs=[...  5.42 us
  transfers between devices with their start and end apart: 42, of which 24 were waited for; matrix products, arithmetic and copies ran while one was open for 0% of the time, Pallas kernels for 23%

profile of v14, /device:TPU:0, one launch (start us, length us, event | category | flops | bytes accessed | tf_op | source)
XLA Modules:
  0.0 142.2 jit_solution(8658212896692951709)
XLA Ops:
  2.7 10.0 %shard_map.156 = (f32[400,256]{1,0:T(8,128)S(1)}, f32[400,256]{1,0:T(8,128)S(1)}, f32[400,512]{1,0:T(8,128)S(1)}, f32[400,512]{1,0:T(8,128)S(1)}, s32[2]{0:T(128...) custom-call(s32[2]{0:T(128)S(1)} %pad_add_fusion.spot_ref, s32[2,256]{1,0:T(2,128)S(1)} %copy-done.7, ...), custom_call_target="tpu_custom_call" | custom-call | flops 10000 | bytes 10000 | tf_op jit(solution)/shard_map/pallas_call | solution.py:135
  12.9 5.6 %shard_map.157 = (f32[400,512]{1,0:T(8,128)S(1)}, f32[1,512]{1,0:T(1,128)S(1)}, f32[408,512]{1,0:T(8,128)S(1)}, f32[200,768]{1,0:T(8,128)S(1)}, f32[200,768]{1,0:T(8,128)S(1)}) custom-call(s32[2]{0:T(128)S(1)} %get-tuple-element.101.core_ref.spot_ref, s32[2,512]{1,0:T(2,128)S(1)} %copy-done.2, s32[2,512]{1,0:T(2,128)S(1)} %copy-done.4, ...), custom_call_target="tpu_custom_call" | custom-call | flops 10000 | bytes 10000 | tf_op jit(solution)/shard_map/pallas_call | solution.py:563
  19.1 2.7 %shard_map.158 = (f32[400,512]{1,0:T(8,128)S(1)}, f32[200,256]{1,0:T(8,128)S(1)}, f32[200,256]{1,0:T(8,128)S(1)}) custom-call(s32[2]{0:T(128)S(1)} %get-tuple-element.101.core_ref.spot_ref, s32[2,512]{1,0:T(2,128)S(1)} %copy-done.2, f32[400,512]{1,0:T(8,128)S(1)} %get-tuple-element.106.left_ref, f32[400,512]{1,0:T(8,128)S(1)} %get-tuple-element.107.rel_ref, ...), custom_call_target="tpu_custom_call" | custom-call | flops 10000 | bytes 10000 | tf_op jit(solution)/shard_map/pallas_call | solution.py:604
  21.8 2.8 %collective-permute-start.3 = (f32[200,768]{1,0:T(8,128)S(1)}, f32[200,768]{1,0:T(8,128)S(1)}, u32[]{:S(2)}, u32[]{:S(2)}) collective-permute-start(f32[200,768]{1,0:T(8,128)S(1)} %get-tuple-element.119), channel_id=1, source_target_pairs={{0,4},{4,0},{8,12},{12,8},{16,20},{20,16},{24,28},{28,24},{1,5},{5... | collective-permute-start | bytes 1843208 | tf_op jit(solution)/shard_map/ppermute | solution.py:677
  24.7 1.9 %collective-permute-done.4.refs_5_ = f32[200,256]{1,0:T(8,128)S(1)} collective-permute-done((f32[200,256]{1,0:T(8,128)S(1)}, f32[200,256]{1,0:T(8,128)S(1)}, u32[]{:S(2)}, u32[]{:S(2)}) %collective-permute-start.4) | collective-permute-done | bytes 204832 | tf_op jit(solution)/shard_map/ppermute | solution.py:677
  26.6 4.3 %shard_map.160 = (f32[8,72,256]{2,1,0:T(8,128)S(1)}, f32[8,64,256]{2,1,0:T(8,128)S(1)}, f32[8,64,256]{2,1,0:T(8,128)S(1)}, f32[8,72,256]{2,1,0:T(8,128)S(1)}, f3...) custom-call(s32[2]{0:T(128)S(1)} %get-tuple-element.101.core_ref.spot_ref, s32[2,256]{1,0:T(2,128)S(1)} %copy-done.7, ...), custom_call_target="tpu_custom_call" | custom-call | flops 10000 | bytes 10000 | tf_op jit(solution)/shard_map/pallas_call | solution.py:280
  32.8 1.8 %collective-permute-start.8 = (f32[8,64,256]{2,1,0:T(8,128)S(1)}, f32[8,64,256]{2,1,0:T(8,128)S(1)}, u32[]{:S(2)}, u32[]{:S(2)}) collective-permute-start(f32[8,64,256]{2,1,0:T(8,128)S(1)} %get-tuple-element.131), channel_id=1, source_target_pairs={{0,1},{1,0},{2,3},{3,2},{4,5},{5,4},{6,7},{7,6},{8,9},{9,8},{10,11... | collective-permute-start | bytes 1572872 | tf_op jit(solution)/shard_map/ppermute | solution.py:677
  34.6 5.4 %shard_map.159 = (f32[400,512]{1,0:T(8,128)}, f32[400,512]{1,0:T(8,128)}, f32[200,512]{1,0:T(8,128)S(1)}, f32[200,512]{1,0:T(8,128)S(1)}) custom-call(s32[2]{0:T(128)S(1)} %get-tuple-element.101.core_ref.spot_ref, s32[2,512]{1,0:T(2,128)S(1)} %copy-done.2, s32[2,512]{1,0:T(2,128)S(1)} %copy-done.4, s32[2,1024]{1,0:T(2,128)S(1)} %copy-done.3, ...), custom_call_target="tpu_custom_call" | custom-call | flops 10000 | bytes 10000 | tf_op jit(solution)/shard_map/pallas_call | solution.py:654
  40.0 1.7 %collective-permute-done.5.refs_5_ = f32[200,512]{1,0:T(8,128)S(1)} collective-permute-done((f32[200,512]{1,0:T(8,128)S(1)}, f32[200,512]{1,0:T(8,128)S(1)}, u32[]{:S(2)}, u32[]{:S(2)}) %collective-permute-start.5) | collective-permute-done | bytes 409632 | tf_op jit(solution)/shard_map/ppermute | solution.py:677
  41.8 3.7 %shard_map.161 = (f32[8,32,256]{2,1,0:T(8,128)S(1)}, f32[8,32,256]{2,1,0:T(8,128)S(1)}, f32[8,32,256]{2,1,0:T(8,128)S(1)}, f32[8,32,256]{2,1,0:T(8,128)S(1)}) custom-call(s32[2]{0:T(128)S(1)} %get-tuple-element.101.core_ref.spot_ref, s32[2,512]{1,0:T(2,128)S(1)} %copy-done.5, s32[2,512]{1,0:T(2,128)S(1)} %collective-permute-done.1.refs_1_, ...), custom_call_target="tpu_custom_call" | custom-call | flops 10000 | bytes 10000 | tf_op jit(solution)/shard_map/pallas_call | solution.py:280
  46.8 1.6 %collective-permute-start.11 = (f32[4,72,256]{2,1,0:T(8,128)S(1)}, f32[4,72,256]{2,1,0:T(8,128)S(1)}, u32[]{:S(2)}, u32[]{:S(2)}) collective-permute-start(f32[4,72,256]{2,1,0:T(8,128)S(1)} %get-tuple-element.149), channel_id=1, source_target_pairs={{0,16},{4,20},{8,24},{12,28},{16,0},{20,4},{24,8},{28,12},{1,17},{... | collective-permute-start | bytes 884744 | tf_op jit(solution)/shard_map/ppermute | solution.py:677
  52.6 5.0 %collective-permute-done.9.refs_2_ = f32[8,32,256]{2,1,0:T(8,128)S(1)} collective-permute-done((f32[8,32,256]{2,1,0:T(8,128)S(1)}, f32[8,32,256]{2,1,0:T(8,128)S(1)}, u32[]{:S(2)}, u32[]{:S(2)}) %collective-permute-start.9) | collective-permute-done | bytes 262176 | tf_op jit(solution)/shard_map/ppermute | solution.py:677
  57.6 3.3 %collective-permute-done.10.refs_3_ = f32[8,32,256]{2,1,0:T(8,128)S(1)} collective-permute-done((f32[8,32,256]{2,1,0:T(8,128)S(1)}, f32[8,32,256]{2,1,0:T(8,128)S(1)}, u32[]{:S(2)}, u32[]{:S(2)}) %collective-permute-start.10) | collective-permute-done | bytes 262176 | tf_op jit(solution)/shard_map/ppermute | solution.py:677
  61.5 1.6 %collective-permute-start.14 = (f32[2,72,256]{2,1,0:T(8,128)S(1)}, f32[2,72,256]{2,1,0:T(8,128)S(1)}, u32[]{:S(2)}, u32[]{:S(2)}) collective-permute-start(f32[2,72,256]{2,1,0:T(8,128)S(1)} %get-tuple-element.158), channel_id=1, source_target_pairs={{0,1},{1,0},{2,3},{3,2},{4,5},{5,4},{6,7},{7,6},{8,9},{9,8},{10,11... | collective-permute-start | bytes 442376 | tf_op jit(solution)/shard_map/ppermute | solution.py:677
  66.3 2.5 %collective-permute-start.16 = (f32[2,64,256]{2,1,0:T(8,128)S(1)}, f32[2,64,256]{2,1,0:T(8,128)S(1)}, u32[]{:S(2)}, u32[]{:S(2)}) collective-permute-start(f32[2,64,256]{2,1,0:T(8,128)S(1)} %get-tuple-element.160), channel_id=1, source_target_pairs={{0,3},{1,2},{2,1},{3,0},{4,7},{5,6},{6,5},{7,4},{8,11},{9,10},{10,... | collective-permute-start | bytes 393224 | tf_op jit(solution)/shard_map/ppermute | solution.py:677
  70.6 2.5 %collective-permute-done.16.refs_5_ = f32[2,64,256]{2,1,0:T(8,128)S(1)} collective-permute-done((f32[2,64,256]{2,1,0:T(8,128)S(1)}, f32[2,64,256]{2,1,0:T(8,128)S(1)}, u32[]{:S(2)}, u32[]{:S(2)}) %collective-permute-start.16) | collective-permute-done | bytes 131104 | tf_op jit(solution)/shard_map/ppermute | solution.py:677
  73.2 2.5 %collective-permute-start.19 = (f32[1,136,256]{2,1,0:T(8,128)S(1)}, f32[1,136,256]{2,1,0:T(8,128)S(1)}, u32[]{:S(2)}, u32[]{:S(2)}) collective-permute-start(f32[1,136,256]{2,1,0:T(8,128)S(1)} %get-tuple-element.168), channel_id=1, source_target_pairs={{0,3},{1,2},{2,1},{3,0},{4,7},{5,6},{6,5},{7,4},{8,11},{9,10},{10,... | collective-permute-start | bytes 417800 | tf_op jit(solution)/shard_map/ppermute | solution.py:677
  76.7 2.2 %collective-permute-start.21 = (f32[1,64,256]{2,1,0:T(8,128)S(1)}, f32[1,64,256]{2,1,0:T(8,128)S(1)}, u32[]{:S(2)}, u32[]{:S(2)}) collective-permute-start(f32[1,64,256]{2,1,0:T(8,128)S(1)} %get-tuple-element.171), channel_id=1, source_target_pairs={{0,1},{1,0},{2,3},{3,2},{4,5},{5,4},{6,7},{7,6},{8,9},{9,8},{10,11... | collective-permute-start | bytes 196616 | tf_op jit(solution)/shard_map/ppermute | solution.py:677
  81.4 3.6 %collective-permute-done.22.refs_7_ = f32[1,64,256]{2,1,0:T(8,128)S(1)} collective-permute-done((f32[1,64,256]{2,1,0:T(8,128)S(1)}, f32[1,64,256]{2,1,0:T(8,128)S(1)}, u32[]{:S(2)}, u32[]{:S(2)}) %collective-permute-start.22) | collective-permute-done | bytes 65568 | tf_op jit(solution)/shard_map/ppermute | solution.py:677
  89.0 1.6 %collective-permute-start.25 = (f32[1,264,256]{2,1,0:T(8,128)S(1)}, f32[1,264,256]{2,1,0:T(8,128)S(1)}, u32[]{:S(2)}, u32[]{:S(2)}) collective-permute-start(f32[1,264,256]{2,1,0:T(8,128)S(1)} %shard_map.167.refs_0_), channel_id=1, source_target_pairs={{0,3},{1,2},{2,1},{3,0},{4,7},{5,6},{6,5},{7,4},{8,11},{9,10},{10,... | collective-permute-start | bytes 811016 | tf_op jit(solution)/shard_map/ppermute | solution.py:677
  92.6 7.7 %collective-permute-done.25.refs_0_.refs_1_.refs_2_ = f32[1,264,256]{2,1,0:T(8,128)S(1)} collective-permute-done((f32[1,264,256]{2,1,0:T(8,128)S(1)}, f32[1,264,256]{2,1,0:T(8,128)S(1)}, u32[]{:S(2)}, u32[]{:S(2)}) %collective-permute-start.25) | collective-permute-done | bytes 270368 | tf_op jit(solution)/shard_map/ppermute | solution.py:677
  100.3 3.2 %collective-permute-start.29 = (f32[1,88,256]{2,1,0:T(8,128)S(1)}, f32[1,88,256]{2,1,0:T(8,128)S(1)}, u32[]{:S(2)}, u32[]{:S(2)}) collective-permute-start(f32[1,88,256]{2,1,0:T(8,128)S(1)} %get-tuple-element.181.refs_0_), channel_id=1, source_target_pairs={{0,1},{1,0},{2,3},{3,2},{4,5},{5,4},{6,7},{7,6},{8,9},{9,8},{10,11... | collective-permute-start | bytes 270344 | tf_op jit(solution)/shard_map/ppermute | solution.py:677
  103.5 2.0 %collective-permute-start.31 = (f32[1,88,256]{2,1,0:T(8,128)S(1)}, f32[1,88,256]{2,1,0:T(8,128)S(1)}, u32[]{:S(2)}, u32[]{:S(2)}) collective-permute-start(f32[1,88,256]{2,1,0:T(8,128)S(1)} %get-tuple-element.183.refs_2_), channel_id=1, source_target_pairs={{0,16},{4,20},{8,24},{12,28},{16,0},{20,4},{24,8},{28,12},{1,17},{... | collective-permute-start | bytes 270344 | tf_op jit(solution)/shard_map/ppermute | solution.py:677
  105.4 1.8 %collective-permute-done.29.refs_6_ = f32[1,88,256]{2,1,0:T(8,128)S(1)} collective-permute-done((f32[1,88,256]{2,1,0:T(8,128)S(1)}, f32[1,88,256]{2,1,0:T(8,128)S(1)}, u32[]{:S(2)}, u32[]{:S(2)}) %collective-permute-start.29) | collective-permute-done | bytes 90144 | tf_op jit(solution)/shard_map/ppermute | solution.py:677
  108.1 2.0 %collective-permute-start.32 = (f32[3,88,256]{2,1,0:T(8,128)S(1)}, f32[3,88,256]{2,1,0:T(8,128)S(1)}, u32[]{:S(2)}, u32[]{:S(2)}) collective-permute-start(f32[3,88,256]{2,1,0:T(8,128)S(1)} %get-tuple-element.184.refs_0_), channel_id=1, source_target_pairs={{0,16},{4,20},{8,24},{12,28},{16,0},{20,4},{24,8},{28,12},{1,17},{... | collective-permute-start | bytes 811016 | tf_op jit(solution)/shard_map/ppermute | solution.py:677
  111.3 4.5 %collective-permute-done.32.refs_6_ = f32[3,88,256]{2,1,0:T(8,128)S(1)} collective-permute-done((f32[3,88,256]{2,1,0:T(8,128)S(1)}, f32[3,88,256]{2,1,0:T(8,128)S(1)}, u32[]{:S(2)}, u32[]{:S(2)}) %collective-permute-start.32) | collective-permute-done | bytes 270368 | tf_op jit(solution)/shard_map/ppermute | solution.py:677
  119.2 1.9 %collective-permute-start.38 = (f32[7,88,256]{2,1,0:T(8,128)S(1)}, f32[7,88,256]{2,1,0:T(8,128)S(1)}, u32[]{:S(2)}, u32[]{:S(2)}) collective-permute-start(f32[7,88,256]{2,1,0:T(8,128)S(1)} %get-tuple-element.189.refs_3_), channel_id=1, source_target_pairs={{0,1},{1,0},{2,3},{3,2},{4,5},{5,4},{6,7},{7,6},{8,9},{9,8},{10,11... | collective-permute-start | bytes 1892360 | tf_op jit(solution)/shard_map/ppermute | solution.py:677
  121.1 2.0 %shard_map.172.refs_0_ = f32[2,200,4096]{2,1,0:T(8,128)} custom-call(s32[2]{0:T(128)S(1)} %get-tuple-element.101.core_ref.spot_ref, f32[9,264,256]{2,1,0:T(8,128)S(1)} %shard_map.171.near_ref), custom_call_target="tpu_custom_call" | custom-call | bytes 3276800 | tf_op jit(solution)/shard_map/pallas_call | solution.py:474
  123.1 2.0 %shard_map.173.refs_3_ = f32[2,200,4096]{2,1,0:T(8,128)} custom-call(s32[2]{0:T(128)S(1)} %get-tuple-element.101.core_ref.spot_ref, f32[9,264,256]{2,1,0:T(8,128)S(1)} %collective-permute-done.35.near_ref, f32[2,200,4096]{2,1,0:T(8,128)} %shard_map.172.refs_0_), custom_call_target="tpu_custom_call", output_to_operand_aliasing={{}: (2, {})} | custom-call | bytes 3276800 | tf_op jit(solution)/shard_map/pallas_call | solution.py:474
  125.2 8.5 %collective-permute-done.36.refs_0_ = f32[7,88,256]{2,1,0:T(8,128)S(1)} collective-permute-done((f32[7,88,256]{2,1,0:T(8,128)S(1)}, f32[7,88,256]{2,1,0:T(8,128)S(1)}, u32[]{:S(2)}, u32[]{:S(2)}) %collective-permute-start.36) | collective-permute-done | bytes 630816 | tf_op jit(solution)/shard_map/ppermute | solution.py:677
  135.9 2.8 %shard_map.174 = (f32[2,200,4096]{2,1,0:T(8,128)}, f32[2,200,1280]{2,1,0:T(8,128)}) custom-call(s32[2]{0:T(128)S(1)} %get-tuple-element.101.core_ref.spot_ref, f32[9,264,256]{2,1,0:T(8,128)S(1)} %shard_map.171.near_ref, f32[7,88,256]{2,1,0:T(8,128)S(1)} %collective-permute-done.36.refs_0_, ...), custom_call_target="tpu_custom_call", output_to_operand_aliasing={{0}: (5, {})} | custom-call | bytes 3276800 | tf_op jit(solution)/shard_map/pallas_call | solution.py:474
  139.2 2.8 %shard_map.175 = (f32[2,200,4096]{2,1,0:T(8,128)}, f32[2,200,1280]{2,1,0:T(8,128)}) custom-call(s32[2]{0:T(128)S(1)} %get-tuple-element.101.core_ref.spot_ref, f32[9,264,256]{2,1,0:T(8,128)S(1)} %collective-permute-done.35.near_ref, f32[7,88,256]{2,1,0:T(8,128)S(1)} %collective-permute-done.39.refs_0_, ...), custom_call_target="tpu_custom_call", output_to_operand_aliasing={{0}: (5, {}), {1}: (6, {})} | custom-call | bytes 3276800 | tf_op jit(solution)/shard_map/pallas_call | solution.py:474
  (96 shorter events, 33.6 us)
Async XLA Ops:
  0.7 12.1 %collective-permute-start = (s32[2,256]{1,0:T(2,128)}, s32[2,256]{1,0:T(2,128)S(1)}, u32[]{:S(2)}, u32[]{:S(2)}) collective-permute-start(s32[2,256]{1,0:T(2,128)} %refs_0_.2), channel_id=1, source_target_pairs={{0,4},{4,0},{8,12},{12,8},{16,20},{20,16},{24,28},{28,24},{1,5},{5... | collective-permute-start | bytes 6152 | tf_op jit(solution)/shard_map/ppermute | solution.py:677
  1.2 11.6 %collective-permute-start.1 = (s32[2,512]{1,0:T(2,128)}, s32[2,512]{1,0:T(2,128)S(1)}, u32[]{:S(2)}, u32[]{:S(2)}) collective-permute-start(s32[2,512]{1,0:T(2,128)} %refs_0_.3), channel_id=1, source_target_pairs={{0,4},{4,0},{8,12},{12,8},{16,20},{20,16},{24,28},{28,24},{1,5},{5... | collective-permute-start | bytes 12296 | tf_op jit(solution)/shard_map/ppermute | solution.py:677
  18.5 16.2 %collective-permute-start.2 = (f32[408,512]{1,0:T(8,128)S(1)}, f32[408,512]{1,0:T(8,128)S(1)}, u32[]{:S(2)}, u32[]{:S(2)}) collective-permute-start(f32[408,512]{1,0:T(8,128)S(1)} %get-tuple-element.111), channel_id=1, source_target_pairs={{0,4},{4,8},{8,12},{12,16},{16,20},{20,24},{24,28},{28,0},{1,5},{5... | collective-permute-start | bytes 2506760 | tf_op jit(solution)/shard_map/ppermute | solution.py:667
  21.8 4.7 %collective-permute-start.3 = (f32[200,768]{1,0:T(8,128)S(1)}, f32[200,768]{1,0:T(8,128)S(1)}, u32[]{:S(2)}, u32[]{:S(2)}) collective-permute-start(f32[200,768]{1,0:T(8,128)S(1)} %get-tuple-element.119), channel_id=1, source_target_pairs={{0,4},{4,0},{8,12},{12,8},{16,20},{20,16},{24,28},{28,24},{1,5},{5... | collective-permute-start | bytes 1843208 | tf_op jit(solution)/shard_map/ppermute | solution.py:677
  30.9 15.7 %collective-permute-start.6 = (f32[8,72,256]{2,1,0:T(8,128)S(1)}, f32[8,72,256]{2,1,0:T(8,128)S(1)}, u32[]{:S(2)}, u32[]{:S(2)}) collective-permute-start(f32[8,72,256]{2,1,0:T(8,128)S(1)} %get-tuple-element.129), channel_id=1, source_target_pairs={{0,8},{4,12},{8,0},{12,4},{16,24},{20,28},{24,16},{28,20},{1,9},{5... | collective-permute-start | bytes 1769480 | tf_op jit(solution)/shard_map/ppermute | solution.py:677
  32.4 13.9 %collective-permute-start.7 = (f32[8,64,256]{2,1,0:T(8,128)S(1)}, f32[8,64,256]{2,1,0:T(8,128)S(1)}, u32[]{:S(2)}, u32[]{:S(2)}) collective-permute-start(f32[8,64,256]{2,1,0:T(8,128)S(1)} %get-tuple-element.130), channel_id=1, source_target_pairs={{0,16},{4,20},{8,24},{12,28},{16,0},{20,4},{24,8},{28,12},{1,17},{... | collective-permute-start | bytes 1572872 | tf_op jit(solution)/shard_map/ppermute | solution.py:677
  32.8 13.7 %collective-permute-start.8 = (f32[8,64,256]{2,1,0:T(8,128)S(1)}, f32[8,64,256]{2,1,0:T(8,128)S(1)}, u32[]{:S(2)}, u32[]{:S(2)}) collective-permute-start(f32[8,64,256]{2,1,0:T(8,128)S(1)} %get-tuple-element.131), channel_id=1, source_target_pairs={{0,1},{1,0},{2,3},{3,2},{4,5},{5,4},{6,7},{7,6},{8,9},{9,8},{10,11... | collective-permute-start | bytes 1572872 | tf_op jit(solution)/shard_map/ppermute | solution.py:677
  46.8 14.7 %collective-permute-start.11 = (f32[4,72,256]{2,1,0:T(8,128)S(1)}, f32[4,72,256]{2,1,0:T(8,128)S(1)}, u32[]{:S(2)}, u32[]{:S(2)}) collective-permute-start(f32[4,72,256]{2,1,0:T(8,128)S(1)} %get-tuple-element.149), channel_id=1, source_target_pairs={{0,16},{4,20},{8,24},{12,28},{16,0},{20,4},{24,8},{28,12},{1,17},{... | collective-permute-start | bytes 884744 | tf_op jit(solution)/shard_map/ppermute | solution.py:677
  48.3 9.2 %collective-permute-start.9 = (f32[8,32,256]{2,1,0:T(8,128)S(1)}, f32[8,32,256]{2,1,0:T(8,128)S(1)}, u32[]{:S(2)}, u32[]{:S(2)}) collective-permute-start(f32[8,32,256]{2,1,0:T(8,128)S(1)} %get-tuple-element.138), channel_id=1, source_target_pairs={{0,8},{4,12},{8,0},{12,4},{16,24},{20,28},{24,16},{28,20},{1,9},{5... | collective-permute-start | bytes 786440 | tf_op jit(solution)/shard_map/ppermute | solution.py:677
  48.9 12.0 %collective-permute-start.10 = (f32[8,32,256]{2,1,0:T(8,128)S(1)}, f32[8,32,256]{2,1,0:T(8,128)S(1)}, u32[]{:S(2)}, u32[]{:S(2)}) collective-permute-start(f32[8,32,256]{2,1,0:T(8,128)S(1)} %get-tuple-element.139), channel_id=1, source_target_pairs={{0,16},{4,20},{8,24},{12,28},{16,0},{20,4},{24,8},{28,12},{1,17},{... | collective-permute-start | bytes 786440 | tf_op jit(solution)/shard_map/ppermute | solution.py:677
  50.4 10.6 %collective-permute-start.12 = (f32[4,64,256]{2,1,0:T(8,128)S(1)}, f32[4,64,256]{2,1,0:T(8,128)S(1)}, u32[]{:S(2)}, u32[]{:S(2)}) collective-permute-start(f32[4,64,256]{2,1,0:T(8,128)S(1)} %get-tuple-element.150), channel_id=1, source_target_pairs={{0,1},{1,0},{2,3},{3,2},{4,5},{5,4},{6,7},{7,6},{8,9},{9,8},{10,11... | collective-permute-start | bytes 786440 | tf_op jit(solution)/shard_map/ppermute | solution.py:677
  52.0 9.5 %collective-permute-start.13 = (f32[4,64,256]{2,1,0:T(8,128)S(1)}, f32[4,64,256]{2,1,0:T(8,128)S(1)}, u32[]{:S(2)}, u32[]{:S(2)}) collective-permute-start(f32[4,64,256]{2,1,0:T(8,128)S(1)} %get-tuple-element.151), channel_id=1, source_target_pairs={{0,8},{4,12},{8,0},{12,4},{16,24},{20,28},{24,16},{28,20},{1,9},{5... | collective-permute-start | bytes 786440 | tf_op jit(solution)/shard_map/ppermute | solution.py:677
  61.5 11.6 %collective-permute-start.14 = (f32[2,72,256]{2,1,0:T(8,128)S(1)}, f32[2,72,256]{2,1,0:T(8,128)S(1)}, u32[]{:S(2)}, u32[]{:S(2)}) collective-permute-start(f32[2,72,256]{2,1,0:T(8,128)S(1)} %get-tuple-element.158), channel_id=1, source_target_pairs={{0,1},{1,0},{2,3},{3,2},{4,5},{5,4},{6,7},{7,6},{8,9},{9,8},{10,11... | collective-permute-start | bytes 442376 | tf_op jit(solution)/shard_map/ppermute | solution.py:677
  63.2 5.6 %collective-permute-start.17 = (f32[4,32,256]{2,1,0:T(8,128)S(1)}, f32[4,32,256]{2,1,0:T(8,128)S(1)}, u32[]{:S(2)}, u32[]{:S(2)}) collective-permute-start(f32[4,32,256]{2,1,0:T(8,128)S(1)} %get-tuple-element.163), channel_id=1, source_target_pairs={{0,16},{4,20},{8,24},{12,28},{16,0},{20,4},{24,8},{28,12},{1,17},{... | collective-permute-start | bytes 393224 | tf_op jit(solution)/shard_map/ppermute | solution.py:677
  64.3 5.0 %collective-permute-start.18 = (f32[4,32,256]{2,1,0:T(8,128)S(1)}, f32[4,32,256]{2,1,0:T(8,128)S(1)}, u32[]{:S(2)}, u32[]{:S(2)}) collective-permute-start(f32[4,32,256]{2,1,0:T(8,128)S(1)} %get-tuple-element.164), channel_id=1, source_target_pairs={{0,8},{4,12},{8,0},{12,4},{16,24},{20,28},{24,16},{28,20},{1,9},{5... | collective-permute-start | bytes 393224 | tf_op jit(solution)/shard_map/ppermute | solution.py:677
  65.2 5.4 %collective-permute-start.15 = (f32[2,64,256]{2,1,0:T(8,128)S(1)}, f32[2,64,256]{2,1,0:T(8,128)S(1)}, u32[]{:S(2)}, u32[]{:S(2)}) collective-permute-start(f32[2,64,256]{2,1,0:T(8,128)S(1)} %get-tuple-element.159), channel_id=1, source_target_pairs={{0,8},{4,12},{8,0},{12,4},{16,24},{20,28},{24,16},{28,20},{1,9},{5... | collective-permute-start | bytes 393224 | tf_op jit(solution)/shard_map/ppermute | solution.py:677
  66.3 6.9 %collective-permute-start.16 = (f32[2,64,256]{2,1,0:T(8,128)S(1)}, f32[2,64,256]{2,1,0:T(8,128)S(1)}, u32[]{:S(2)}, u32[]{:S(2)}) collective-permute-start(f32[2,64,256]{2,1,0:T(8,128)S(1)} %get-tuple-element.160), channel_id=1, source_target_pairs={{0,3},{1,2},{2,1},{3,0},{4,7},{5,6},{6,5},{7,4},{8,11},{9,10},{10,... | collective-permute-start | bytes 393224 | tf_op jit(solution)/shard_map/ppermute | solution.py:677
  73.2 13.1 %collective-permute-start.19 = (f32[1,136,256]{2,1,0:T(8,128)S(1)}, f32[1,136,256]{2,1,0:T(8,128)S(1)}, u32[]{:S(2)}, u32[]{:S(2)}) collective-permute-start(f32[1,136,256]{2,1,0:T(8,128)S(1)} %get-tuple-element.168), channel_id=1, source_target_pairs={{0,3},{1,2},{2,1},{3,0},{4,7},{5,6},{6,5},{7,4},{8,11},{9,10},{10,... | collective-permute-start | bytes 417800 | tf_op jit(solution)/shard_map/ppermute | solution.py:677
  78.9 6.1 %collective-permute-start.22 = (f32[1,64,256]{2,1,0:T(8,128)S(1)}, f32[1,64,256]{2,1,0:T(8,128)S(1)}, u32[]{:S(2)}, u32[]{:S(2)}) collective-permute-start(f32[1,64,256]{2,1,0:T(8,128)S(1)} %get-tuple-element.172), channel_id=1, source_target_pairs={{0,3},{1,2},{2,1},{3,0},{4,7},{5,6},{6,5},{7,4},{8,11},{9,10},{10,... | collective-permute-start | bytes 196616 | tf_op jit(solution)/shard_map/ppermute | solution.py:677
  79.9 6.5 %collective-permute-start.23 = (f32[1,64,256]{2,1,0:T(8,128)S(1)}, f32[1,64,256]{2,1,0:T(8,128)S(1)}, u32[]{:S(2)}, u32[]{:S(2)}) collective-permute-start(f32[1,64,256]{2,1,0:T(8,128)S(1)} %get-tuple-element.173), channel_id=1, source_target_pairs={{0,2},{1,3},{2,0},{3,1},{4,6},{5,7},{6,4},{7,5},{8,10},{9,11},{10,... | collective-permute-start | bytes 196616 | tf_op jit(solution)/shard_map/ppermute | solution.py:677
  89.0 11.3 %collective-permute-start.25 = (f32[1,264,256]{2,1,0:T(8,128)S(1)}, f32[1,264,256]{2,1,0:T(8,128)S(1)}, u32[]{:S(2)}, u32[]{:S(2)}) collective-permute-start(f32[1,264,256]{2,1,0:T(8,128)S(1)} %shard_map.167.refs_0_), channel_id=1, source_target_pairs={{0,3},{1,2},{2,1},{3,0},{4,7},{5,6},{6,5},{7,4},{8,11},{9,10},{10,... | collective-permute-start | bytes 811016 | tf_op jit(solution)/shard_map/ppermute | solution.py:677
  90.6 12.9 %collective-permute-start.28 = (f32[1,264,256]{2,1,0:T(8,128)S(1)}, f32[1,264,256]{2,1,0:T(8,128)S(1)}, u32[]{:S(2)}, u32[]{:S(2)}) collective-permute-start(f32[1,264,256]{2,1,0:T(8,128)S(1)} %shard_map.167.refs_0_), channel_id=1, source_target_pairs={{0,16},{4,20},{8,24},{12,28},{16,0},{20,4},{24,8},{28,12},{1,17},{... | collective-permute-start | bytes 811016 | tf_op jit(solution)/shard_map/ppermute | solution.py:677
  91.7 13.8 %collective-permute-start.27 = (f32[1,264,256]{2,1,0:T(8,128)S(1)}, f32[1,264,256]{2,1,0:T(8,128)S(1)}, u32[]{:S(2)}, u32[]{:S(2)}) collective-permute-start(f32[1,264,256]{2,1,0:T(8,128)S(1)} %shard_map.167.refs_0_), channel_id=1, source_target_pairs={{0,8},{4,12},{8,0},{12,4},{16,24},{20,28},{24,16},{28,20},{1,9},{5... | collective-permute-start | bytes 811016 | tf_op jit(solution)/shard_map/ppermute | solution.py:677
  92.6 12.9 %collective-permute-start.26 = (f32[1,264,256]{2,1,0:T(8,128)S(1)}, f32[1,264,256]{2,1,0:T(8,128)S(1)}, u32[]{:S(2)}, u32[]{:S(2)}) collective-permute-start(f32[1,264,256]{2,1,0:T(8,128)S(1)} %shard_map.167.refs_0_), channel_id=1, source_target_pairs={{0,1},{1,0},{2,3},{3,2},{4,5},{5,4},{6,7},{7,6},{8,9},{9,8},{10,11... | collective-permute-start | bytes 811016 | tf_op jit(solution)/shard_map/ppermute | solution.py:677
  100.3 7.0 %collective-permute-start.29 = (f32[1,88,256]{2,1,0:T(8,128)S(1)}, f32[1,88,256]{2,1,0:T(8,128)S(1)}, u32[]{:S(2)}, u32[]{:S(2)}) collective-permute-start(f32[1,88,256]{2,1,0:T(8,128)S(1)} %get-tuple-element.181.refs_0_), channel_id=1, source_target_pairs={{0,1},{1,0},{2,3},{3,2},{4,5},{5,4},{6,7},{7,6},{8,9},{9,8},{10,11... | collective-permute-start | bytes 270344 | tf_op jit(solution)/shard_map/ppermute | solution.py:677
  108.1 7.7 %collective-permute-start.32 = (f32[3,88,256]{2,1,0:T(8,128)S(1)}, f32[3,88,256]{2,1,0:T(8,128)S(1)}, u32[]{:S(2)}, u32[]{:S(2)}) collective-permute-start(f32[3,88,256]{2,1,0:T(8,128)S(1)} %get-tuple-element.184.refs_0_), channel_id=1, source_target_pairs={{0,16},{4,20},{8,24},{12,28},{16,0},{20,4},{24,8},{28,12},{1,17},{... | collective-permute-start | bytes 811016 | tf_op jit(solution)/shard_map/ppermute | solution.py:677
  110.1 6.5 %collective-permute-start.33 = (f32[3,88,256]{2,1,0:T(8,128)S(1)}, f32[3,88,256]{2,1,0:T(8,128)S(1)}, u32[]{:S(2)}, u32[]{:S(2)}) collective-permute-start(f32[3,88,256]{2,1,0:T(8,128)S(1)} %get-tuple-element.185.refs_1_), channel_id=1, source_target_pairs={{0,1},{1,0},{2,3},{3,2},{4,5},{5,4},{6,7},{7,6},{8,9},{9,8},{10,11... | collective-permute-start | bytes 811016 | tf_op jit(solution)/shard_map/ppermute | solution.py:677
  110.2 6.5 %collective-permute-start.34 = (f32[3,88,256]{2,1,0:T(8,128)S(1)}, f32[3,88,256]{2,1,0:T(8,128)S(1)}, u32[]{:S(2)}, u32[]{:S(2)}) collective-permute-start(f32[3,88,256]{2,1,0:T(8,128)S(1)} %get-tuple-element.186.refs_2_), channel_id=1, source_target_pairs={{0,8},{4,12},{8,0},{12,4},{16,24},{20,28},{24,16},{28,20},{1,9},{5... | collective-permute-start | bytes 811016 | tf_op jit(solution)/shard_map/ppermute | solution.py:677
  116.9 6.2 %collective-permute-start.35 = (f32[9,264,256]{2,1,0:T(8,128)S(1)}, f32[9,264,256]{2,1,0:T(8,128)S(1)}, u32[]{:S(2)}, u32[]{:S(2)}) collective-permute-start(f32[9,264,256]{2,1,0:T(8,128)S(1)} %shard_map.171.near_ref), channel_id=1, source_target_pairs={{0,4},{4,0},{8,12},{12,8},{16,20},{20,16},{24,28},{28,24},{1,5},{5... | collective-permute-start | bytes 7299080 | tf_op jit(solution)/shard_map/ppermute | solution.py:677
  117.0 16.6 %collective-permute-start.36 = (f32[7,88,256]{2,1,0:T(8,128)S(1)}, f32[7,88,256]{2,1,0:T(8,128)S(1)}, u32[]{:S(2)}, u32[]{:S(2)}) collective-permute-start(f32[7,88,256]{2,1,0:T(8,128)S(1)} %get-tuple-element.187.refs_1_), channel_id=1, source_target_pairs={{0,8},{4,12},{8,0},{12,4},{16,24},{20,28},{24,16},{28,20},{1,9},{5... | collective-permute-start | bytes 1892360 | tf_op jit(solution)/shard_map/ppermute | solution.py:677
  118.2 16.3 %collective-permute-start.37 = (f32[7,88,256]{2,1,0:T(8,128)S(1)}, f32[7,88,256]{2,1,0:T(8,128)S(1)}, u32[]{:S(2)}, u32[]{:S(2)}) collective-permute-start(f32[7,88,256]{2,1,0:T(8,128)S(1)} %get-tuple-element.188.refs_2_), channel_id=1, source_target_pairs={{0,16},{4,20},{8,24},{12,28},{16,0},{20,4},{24,8},{28,12},{1,17},{... | collective-permute-start | bytes 1892360 | tf_op jit(solution)/shard_map/ppermute | solution.py:677
  119.2 16.2 %collective-permute-start.38 = (f32[7,88,256]{2,1,0:T(8,128)S(1)}, f32[7,88,256]{2,1,0:T(8,128)S(1)}, u32[]{:S(2)}, u32[]{:S(2)}) collective-permute-start(f32[7,88,256]{2,1,0:T(8,128)S(1)} %get-tuple-element.189.refs_3_), channel_id=1, source_target_pairs={{0,1},{1,0},{2,3},{3,2},{4,5},{5,4},{6,7},{7,6},{8,9},{9,8},{10,11... | collective-permute-start | bytes 1892360 | tf_op jit(solution)/shard_map/ppermute | solution.py:677
  (21 other events, 220.7 us)
